TPU v7x, 32 devices: a whole 2x2x4 slice. The times are simulated.
32 devices in a mesh: group: 16 (over z, y, core), head: 2 (over x).
Axes of the slice: x: 2, y: 2, z: 4, core: 2. Of those that a mesh axis runs over, the one named last changes fastest.
Arguments:
- kv_pool: bfloat16 [512, 128, 2048], P('group', None, 'head'), may hold values from -6 to 6
- lengths: int32 [256], replicated, may hold values from 1 to 256, as said below
- prefill_of: int32 [256], replicated, may hold values from 0 to 15, as said below
- decode_of: int32 [256], replicated, may hold values from 0 to 15, as said below
- row_request: int32 [256], replicated, may hold values from 0 to 255, as said below
- queries: bfloat16 [256, 8192], P('group', 'head'), may hold values from -6 to 6
- out_weight: bfloat16 [8192, 8192], P('head', 'group'), may hold values from -0.0625 to 0.0625
Outputs:
- received: bfloat16 [512, 128, 2048], P('group', None, 'head')
- output: bfloat16 [256, 8192], P('head', 'group')
Inputs may be any that keep to these rules, and one draw needn't show every extreme that they name: `lengths`: every prefill group has a request of 256 tokens. `prefill_of`: each prefill group holds exactly 16 requests. `decode_of`: no two requests of one prefill group have the same decode group; every decode group receives at least one request. `row_request`: row b's request has decode group b // 16.
All inputs are finite; a program needn't handle non-finite values.
Results may differ from a plain program's by a relative error of at most 0.009.
Values may be sent and summed in bfloat16 or wider, within the bound.
No kernel may reach another device: no remote copies, remote signals or barrier semaphores. Data moves between devices by JAX's collectives and lax.ppermute only.
A program may use at most 128 MiB of HBM per device.

v0:
```python
import math

import jax
import jax.numpy as jnp
from jax import lax
from jax.sharding import PartitionSpec as P

HD = 128
MAX_PAGES = 2


def page_tables(lengths, prefill_of, page_size):
    counts = (lengths + page_size - 1) // page_size
    ordinal = jnp.arange(lengths.shape[0], dtype=jnp.int32)
    same_group = (prefill_of[None, :] == prefill_of[:, None]) & (
        ordinal[None, :] < ordinal[:, None]
    )
    starts = jnp.sum(jnp.where(same_group, counts[None, :], 0), axis=1)
    return (counts, starts)


def pair_lookup(fixed_of, fixed_value, peer_of, groups):
    ordinal = jnp.arange(fixed_of.shape[0], dtype=jnp.int32)
    member = (fixed_of[None, :] == fixed_value) & (
        peer_of[None, :] == jnp.arange(groups, dtype=jnp.int32)[:, None]
    )
    present = jnp.any(member, axis=1)
    request_id = jnp.sum(jnp.where(member, ordinal[None, :], 0), axis=1)
    return (present, request_id)


def slot_tags(present, request_id, counts, lengths, page_size):
    slot_index = jnp.arange(MAX_PAGES, dtype=jnp.int32)[None, :]
    filled = present[:, None] & (slot_index < counts[request_id][:, None])
    owner = jnp.where(filled, request_id[:, None], -1)
    limit = jnp.where(
        filled, jnp.clip(lengths[request_id][:, None] - slot_index * page_size, 0, page_size), 0
    )
    return (filled, owner, limit)


def attend_all(query_heads, incoming, owner, limit, row_requests, scaling):
    groups, slot_total, page_size, feature_width = incoming.shape
    local_heads = feature_width // (2 * HD)
    cache_heads = incoming.reshape(groups * slot_total * page_size, local_heads, 2, HD)
    scores = (
        jnp.einsum(
            "bhjd,thd->bhjt",
            query_heads,
            cache_heads[:, :, 0, :],
            preferred_element_type=jnp.float32,
        )
        * scaling
    )
    token_owner = jnp.repeat(owner.reshape(-1), page_size)
    token_limit = jnp.repeat(limit.reshape(-1), page_size)
    position = jnp.arange(token_owner.shape[0], dtype=jnp.int32) % page_size
    token_mask = (
        (token_owner[None, :] == row_requests[:, None]) & (position < token_limit)[None, :]
    )[:, None, None, :]
    masked = jnp.where(token_mask, scores, -1e30)
    highest = jnp.max(masked, axis=-1, keepdims=True)
    weights = jnp.where(token_mask, jnp.exp(masked - highest), 0.0)
    totals = jnp.sum(weights, axis=-1)
    mixture = jnp.einsum(
        "bhjt,thd->bhjd",
        weights.astype(jnp.bfloat16),
        cache_heads[:, :, 1, :],
        preferred_element_type=jnp.float32,
    )
    return mixture / totals[..., None]


def local(kv_pool, lengths, prefill_of, decode_of, row_request, queries, out_weight):
    groups = lax.axis_size("group")
    group_index = lax.axis_index("group")
    page_size = kv_pool.shape[1]
    feature_width = kv_pool.shape[2]
    local_heads = feature_width // (2 * HD)
    scaling = 1.0 / math.sqrt(HD)
    counts, starts = page_tables(lengths, prefill_of, page_size)
    sent_present, sent_request = pair_lookup(prefill_of, group_index, decode_of, groups)
    sent_filled, sent_owner, sent_limit = slot_tags(
        sent_present, sent_request, counts, lengths, page_size
    )
    page_index = starts[sent_request][:, None] + jnp.arange(MAX_PAGES, dtype=jnp.int32)[None, :]
    page_index = jnp.clip(page_index, 0, kv_pool.shape[0] - 1)
    outgoing = jnp.where(
        sent_filled[:, :, None, None],
        jnp.take(kv_pool, page_index, axis=0),
        jnp.zeros((), jnp.bfloat16),
    )
    row_local = queries.shape[0]
    row_requests = lax.dynamic_slice_in_dim(row_request, group_index * row_local, row_local)
    query_heads = queries.reshape(row_local, local_heads, -1, HD)
    incoming = lax.all_to_all(outgoing, "group", split_axis=0, concat_axis=0, tiled=True)
    recv_present, recv_request = pair_lookup(decode_of, group_index, prefill_of, groups)
    recv_filled, recv_owner, recv_limit = slot_tags(
        recv_present, recv_request, counts, lengths, page_size
    )
    mixture = attend_all(query_heads, incoming, recv_owner, recv_limit, row_requests, scaling)
    received = incoming.reshape(groups * MAX_PAGES, page_size, feature_width)
    attended = mixture.reshape(row_local, -1).astype(jnp.bfloat16)
    gathered = lax.all_gather(attended, "group", axis=0, tiled=True)
    row_share = gathered.shape[0] // lax.axis_size("head")
    summed = lax.psum(
        jnp.dot(gathered, out_weight, preferred_element_type=jnp.float32).astype(jnp.bfloat16),
        "head",
    ).astype(jnp.float32)
    summed_rows = lax.dynamic_slice_in_dim(summed, lax.axis_index("head") * row_share, row_share, 0)
    return (received, summed_rows.astype(jnp.bfloat16))


def solution(mesh):
    in_specs = (
        P("group", None, "head"),
        P(),
        P(),
        P(),
        P(),
        P("group", "head"),
        P("head", "group"),
    )
    out_specs = (P("group", None, "head"), P("head", "group"))
    return jax.shard_map(local, mesh=mesh, in_specs=in_specs, out_specs=out_specs, check_vma=False)
```

profile of v0, /device:TPU:0, one launch (start us, length us, event | category | flops | bytes accessed | tf_op | source)
XLA Modules:
  0.0 352.0 jit_solution(9327768008494436841)
XLA Ops:
  7.2 0.7 broadcast_compare_fusion.1
  7.9 0.8 select_reduce_fusion.2
  8.7 0.8 fusion.23
  9.5 0.7 and_select_fusion
  10.2 0.9 select_reduce_fusion
  11.1 0.7 gather_fusion
  11.8 0.7 gather_fusion.1
  12.4 0.1 compare_select_fusion
  12.5 0.1 reshape.254
  12.6 0.1 fusion.29
  12.7 8.6 %gather_fusion.2 = bf16[32,128,1024]{2,1,0:T(8,128)(2,1)} fusion(bf16[32,128,1024]{2,1,0:T(8,128)(2,1)} %param.7, s32[1024]{0:T(1024)S(1)} %pad_clamp_fusion.1), kind=kCustom, calls=%fused_computation.2 | custom fusion | bytes 16777344 | tf_op jit(solution)/shard_map/jit(_take)/gather | solution.py:90
  21.3 7.8 %select_select_fusion = bf16[16,2,128,1024]{3,2,1,0:T(8,128)(2,1)} fusion(bf16[16,2,128,1024]{3,2,1,0:T(8,128)(2,1)} %bitcast.64, pred[16,2]{1,0:T(8,128)(4,1)S(1)} %get-tuple-element.8, pred[16,2]{1,0:T(8,128)(4,1)S(1)} %get-tuple-element.9), kind=kLoop, calls=%fused_computation.8 | loop fusion | flops 8388608 | bytes 16777280 | tf_op jit(solution)/shard_map/jit(_where)/select_n | solution.py:88
  29.0 0.0 copy-start.3
  29.0 0.0 copy-start.2
  29.0 0.0 copy-start
  29.0 0.0 copy-start.4
  29.1 7.6 %all-to-all-start = ((bf16[16,2,128,1024]{3,2,1,0:T(8,128)(2,1)}), bf16[16,2,128,1024]{3,2,1,0:T(8,128)(2,1)}, u32[]{:S(2)}, u32[]{:S(2)}) async-start(bf16[16,2,128,1024]{3,2,1,0:T(8,128)(2,1)} %select_select_fusion), calls=%async_computation | async-start | bytes 16777216 | tf_op jit(solution)/shard_map/all_to_all | solution.py:96
  36.6 0.0 all-gather.2.cloned.1.call-start
  36.7 0.0 copy-done.3
  36.7 0.0 copy-done.2
  36.7 0.1 select_reduce_fusion.1
  36.9 0.7 gather_fusion.3
  37.5 0.0 copy-done
  37.5 0.7 gather_fusion.4
  38.2 0.1 fusion.25
  38.3 0.1 clamp_select_fusion
  38.4 0.1 select_n.113
  38.5 0.1 select_n.117
  38.6 0.0 copy-done.1
  38.6 0.0 copy-done.4
  38.6 0.1 dynamic_slice.6
  38.7 0.1 fusion.19
  38.8 0.1 broadcast_bitcast_fusion
  38.9 0.1 compare_and_fusion
  39.0 148.4 %all-to-all-done = bf16[16,2,128,1024]{3,2,1,0:T(8,128)(2,1)} async-done(((bf16[16,2,128,1024]{3,2,1,0:T(8,128)(2,1)}), bf16[16,2,128,1024]{3,2,1,0:T(8,128)(2,1)}, u32[]{:S(2)}, u32[]{:S(2)}) %all-to-all-start) | async-done | bytes 8388640 | tf_op jit(solution)/shard_map/all_to_all | solution.py:96
  187.4 14.2 %reshape.233 = bf16[4096,4,2,128]{3,2,1,0:T(2,128)(2,1)} reshape(bf16[16,2,128,1024]{3,2,1,0:T(8,128)(2,1)} %all-to-all-done) | data formatting | bytes 16777216 | tf_op jit(solution)/shard_map/reshape | solution.py:45
  201.6 17.2 %fusion.37 = (bf16[4096,4,1,128]{3,2,1,0:T(2,128)(2,1)}, bf16[4096,4,1,128]{3,2,1,0:T(2,128)(2,1)}) fusion(bf16[4096,4,2,128]{3,2,1,0:T(2,128)(2,1)} %reshape.233), kind=kLoop, calls=%fused_computation.71 | loop fusion | bytes 16777216 | tf_op jit(solution)/shard_map/slice | solution.py:68
  218.8 9.2 %fusion.38 = (f32[16,4,8]{0,2,1:T(8,128)S(1)}, bf16[16,4,8,4096]{3,0,2,1:T(8,128)(2,1)}) fusion(pred[16,4096]{1,0:T(8,128)(4,1)S(1)} %compare_and_fusion, bf16[4096,4,1,128]{3,2,1,0:T(2,128)(2,1)} %get-tuple-element.3, bf16[16,4,8,128]{3,2,1,0:T(8,128)(2,1)S(1)} %bitcast.68), kind=kOutput, calls=%fused_computation.72 | convolution fusion | flops 549457920 | bytes 8587264 | tf_op jit(solution)/shard_map/sub | solution.py:63
  228.0 6.1 %fusion.14 = bf16[16,4,8,128]{3,0,2,1:T(8,128)(2,1)S(1)} fusion(bf16[16,4,8,4096]{3,0,2,1:T(8,128)(2,1)} %get-tuple-element.7, bf16[4096,4,1,128]{3,2,1,0:T(2,128)(2,1)} %get-tuple-element.2, f32[16,4,8]{0,2,1:T(8,128)S(1)} %get-tuple-element.6), kind=kOutput, calls=%fused_computation.21 | convolution fusion | flops 537001984 | bytes 8521728 | tf_op jit(solution)/shard_map/bhjt,thd->bhjd/dot_general | solution.py:65
  234.2 0.7 copy.45
  234.9 0.0 all-gather.2.cloned.1.call-update
  234.9 0.0 all-reduce.2.cloned.1.call-start
  235.0 73.3 %all-gather.2.cloned.1.call-done = bf16[256,4096]{1,0:T(8,128)(2,1)} async-done(((bf16[16,4096]{1,0:T(8,128)(2,1)}), bf16[256,4096]{1,0:T(8,128)(2,1)}) %all-gather.2.cloned.1.call-update) | async-done | bytes 2097168 | tf_op jit(solution)/shard_map/all_gather | solution.py:104
  308.3 4.8 %convolution_convert_fusion = bf16[256,512]{1,0:T(8,128)(2,1)} fusion(bf16[256,4096]{1,0:T(8,128)(2,1)} %all-gather.2.cloned.1.call-done, bf16[4096,512]{1,0:T(8,128)(2,1)} %param.13), kind=kOutput, calls=%fused_computation.18 | convolution fusion | flops 1073872896 | bytes 6553600 | tf_op jit(solution)/shard_map/dot_general | solution.py:107
  313.0 0.0 all-reduce.2.cloned.1.call-update
  313.1 22.1 %all-reduce.2.cloned.1.call-done = bf16[256,512]{1,0:T(8,128)(2,1)} async-done(((bf16[256,512]{1,0:T(8,128)(2,1)}), bf16[256,512]{1,0:T(8,128)(2,1)}) %all-reduce.2.cloned.1.call-update) | async-done | bytes 262160 | tf_op jit(solution)/shard_map/psum | solution.py:106
  335.2 1.6 convert_convert_fusion
  336.8 8.4 %copy.48 = bf16[32,128,1024]{2,1,0:T(8,128)(2,1)} copy(bf16[32,128,1024]{2,1,0:T(8,128)(2,1)} %bitcast.3) | data formatting | bytes 16777216
  (10 shorter events, 0.1 us)
Async XLA Ops:
  29.0 7.7 %copy-start.3 = (s32[256]{0:T(256)S(1)}, s32[256]{0:T(256)}, u32[]{:S(2)}) copy-start(s32[256]{0:T(256)} %param.10) | copy-start | bytes 3076
  29.0 7.7 %copy-start.2 = (s32[256]{0:T(256)S(1)}, s32[256]{0:T(256)}, u32[]{:S(2)}) copy-start(s32[256]{0:T(256)} %param.9) | copy-start | bytes 3076
  29.0 8.5 %copy-start = (s32[256]{0:T(256)S(1)}, s32[256]{0:T(256)}, u32[]{:S(2)}) copy-start(s32[256]{0:T(256)} %param.8) | copy-start | bytes 3076
  29.0 9.6 %copy-start.1 = (bf16[16,4096]{1,0:T(8,128)(2,1)S(1)}, bf16[16,4096]{1,0:T(8,128)(2,1)}, u32[]{:S(2)}) copy-start(bf16[16,4096]{1,0:T(8,128)(2,1)} %param.12) | copy-start | bytes 393220
  29.0 9.6 %copy-start.4 = (s32[256]{0:T(256)S(1)}, s32[256]{0:T(256)}, u32[]{:S(2)}) copy-start(s32[256]{0:T(256)} %param.11) | copy-start | bytes 3076
  29.1 158.3 %all-to-all-start = ((bf16[16,2,128,1024]{3,2,1,0:T(8,128)(2,1)}), bf16[16,2,128,1024]{3,2,1,0:T(8,128)(2,1)}, u32[]{:S(2)}, u32[]{:S(2)}) async-start(bf16[16,2,128,1024]{3,2,1,0:T(8,128)(2,1)} %select_select_fusion), calls=%async_computation | async-start | bytes 16777216 | tf_op jit(solution)/shard_map/all_to_all | solution.py:96
  36.6 271.6 %all-gather.2.cloned.1.call-start = ((), (), s32[]{:S(2)}) async-start(), calls=%async_computation.1 | async-start | bytes 2228224 | tf_op jit(solution)/shard_map/all_gather | solution.py:104
  234.9 100.3 %all-reduce.2.cloned.1.call-start = ((), (), s32[]{:S(2)}) async-start(), calls=%async_computation.2 | async-start | bytes 524288 | tf_op jit(solution)/shard_map/psum | solution.py:106
Sparse Core Ops, SparseCore 0:
  235.0 73.1 all-gather.1
  313.2 21.9 all-reduce.1
where the time goes:
time: 353 us; the launch traced here: 352 us
  waiting for transfers between devices  244 us (69%)
  local copies, waits for them, and re-layouts  52.3 us (15%)
  matrix products  20.1 us (6%)
  between operations  14.2 us (4%)
  other arithmetic  13.9 us (4%)
  starting transfers between devices  7.66 us (2%)
    all_to_all x1, waiting for transfers between devices, local(): lax.all_to_all(outgoing, 'group', split_axis=0, concat_axis=0, tiled=True)  148 us
    all_gather x1, waiting for transfers between devices, local(): gathered = lax.all_gather(attended, 'group', axis=0, tiled=True)  73.3 us
    psum x1, waiting for transfers between devices, local(): lax.psum(jnp.dot(gathered, out_weight, preferred_element_type=jnp.float32...  22.1 us
    slice x1, local copies, waits for them, and re-layouts, attend_all(): cache_heads[:, :, 1, :]  17.2 us
    reshape x1, local copies, waits for them, and re-layouts, attend_all(): incoming.reshape(groups * slot_total * page_size, local_heads, 2, HD)  14.2 us
    sub x1, matrix products, attend_all(): weights = jnp.where(token_mask, jnp.exp(masked - highest), 0.0)  9.2 us
    unnamed x13, local copies, waits for them, and re-layouts  9.12 us
    gather x1, local copies, waits for them, and re-layouts, local(): jnp.take(kv_pool, page_index, axis=0)  8.57 us
  transfers between devices with their start and end apart: 3, of which 3 were waited for; matrix products, arithmetic and copies ran while one was open for 1% of the time, Pallas kernels for 0%

commit v1 on v0

v1 whole, which is shorter than its diff:
```python
import functools
import itertools
import math

import jax
import jax.numpy as jnp
from jax import lax
from jax.experimental import pallas as pl
from jax.experimental.pallas import tpu as pltpu
from jax.sharding import PartitionSpec as P

HD = 128
MAX_PAGES = 2
CAPACITY = 32
ROW_UNROLL = 4
VMEM_LIMIT = 48 * 1024 * 1024


def factors(groups):
    if groups % 4 == 0:
        return (groups // 4, 2, 2)
    return (groups,)


def strides(dims):
    return tuple(math.prod(dims[i + 1 :]) for i in range(len(dims)))


def shifted(index, offset, dims):
    result = 0
    for size, stride, ahead in zip(dims, strides(dims), offset):
        result = result + lax.rem(index // stride % size + ahead + size, size) * stride
    return result


def shifted_static(index, offset, dims):
    result = 0
    for size, stride, ahead in zip(dims, strides(dims), offset):
        result += (index // stride % size + ahead) % size * stride
    return result


def send_by(array, offset, dims):
    groups = math.prod(dims)
    pairs = [(s, shifted_static(s, offset, dims)) for s in range(groups)]
    return lax.ppermute(array, "group", pairs)


def gather_shards(shard, dims):
    held = {(0,) * len(dims): shard}
    for axis, size in enumerate(dims):
        incoming = {}
        for ahead in range(1, size):
            step = tuple(ahead if i == axis else 0 for i in range(len(dims)))
            for offset, array in held.items():
                place = tuple(a + b for a, b in zip(offset, step))
                incoming[place] = send_by(array, step, dims)
        held.update(incoming)
    return held


def offset_rank(offset, dims):
    return sum(o * s for o, s in zip(offset, strides(dims)))


def behind_rank(me, other, dims):
    rank = 0
    for size, stride in zip(dims, strides(dims)):
        rank = rank + lax.rem(me // stride % size - other // stride % size + size, size) * stride
    return rank


def prepare_kernel(dims, offsets, lengths, prefill_of, decode_of, pool, received, *rest):
    sends = rest[: len(offsets)]
    zero_page, start_of, count_of, zero_sem, sems = rest[len(offsets) :]
    me = lax.axis_index("group")
    page_size = pool.shape[1]
    for d in range(math.prod(dims)):
        start_of[d] = 0
        count_of[d] = 0
    start_of[math.prod(dims)] = 0
    count_of[math.prod(dims)] = 0
    zero_page[...] = jnp.zeros_like(zero_page)

    def visit(r, running):
        mine = prefill_of[r] == me
        count = (lengths[r] + page_size - 1) // page_size
        place = jnp.where(mine, decode_of[r], math.prod(dims))
        start_of[place] = running
        count_of[place] = count
        return running + jnp.where(mine, count, 0)

    lax.fori_loop(0, lengths.shape[0], visit, jnp.int32(0), unroll=8)

    def fill(target, page, start, count, sem):
        @pl.when(page < count)
        def _():
            pltpu.make_async_copy(pool.at[start + page], target, sem).start()

        @pl.when(page >= count)
        def _():
            pltpu.make_async_copy(zero_page, target, sem).start()

    own = start_of[me], count_of[me]
    for page in range(MAX_PAGES):
        fill(received.at[me * MAX_PAGES + page], page, *own, zero_sem.at[page])
    for i, offset in enumerate(offsets):
        to = shifted(me, offset, dims)
        start, count = start_of[to], count_of[to]
        for page in range(MAX_PAGES):
            fill(sends[i].at[page], page, start, count, sems.at[i, page])
    for page in range(MAX_PAGES):
        pltpu.make_async_copy(zero_page, received.at[page], zero_sem.at[page]).wait()
    for i in range(len(offsets)):
        for page in range(MAX_PAGES):
            pltpu.make_async_copy(zero_page, sends[i].at[page], sems.at[i, page]).wait()


def prepare(dims, offsets, lengths, prefill_of, decode_of, pool):
    groups = math.prod(dims)
    page = pool.shape[1:]
    block = jax.ShapeDtypeStruct((MAX_PAGES,) + page, pool.dtype)
    outs = [jax.ShapeDtypeStruct((groups * MAX_PAGES,) + page, pool.dtype)] + [block] * len(offsets)
    smem = pl.BlockSpec(memory_space=pltpu.SMEM)
    hbm = pl.BlockSpec(memory_space=pl.ANY)
    return pl.pallas_call(
        functools.partial(prepare_kernel, dims, offsets),
        out_shape=outs,
        in_specs=[smem, smem, smem, hbm],
        out_specs=[hbm] * len(outs),
        scratch_shapes=[
            pltpu.VMEM(page, pool.dtype),
            pltpu.SMEM((groups + 1,), jnp.int32),
            pltpu.SMEM((groups + 1,), jnp.int32),
            pltpu.SemaphoreType.DMA((MAX_PAGES,)),
            pltpu.SemaphoreType.DMA((len(offsets), MAX_PAGES)),
        ],
        compiler_params=pltpu.CompilerParams(vmem_limit_bytes=VMEM_LIMIT),
        cost_estimate=pl.CostEstimate(flops=0, bytes_accessed=4 * pool.size, transcendentals=0),
        name="outgoing_pages",
    )(lengths, prefill_of, decode_of, pool)


def place_kernel(dims, offsets, received_in, *rest):
    blocks = rest[: len(offsets)]
    received, sems = rest[len(offsets) :]
    me = lax.axis_index("group")
    copies = []
    for i, offset in enumerate(offsets):
        source = shifted(me, tuple(-o for o in offset), dims)
        copies.append(
            pltpu.make_async_copy(
                blocks[i], received.at[pl.ds(source * MAX_PAGES, MAX_PAGES)], sems.at[i]
            )
        )
        copies[-1].start()
    for copy in copies:
        copy.wait()


def place(dims, offsets, received, blocks):
    hbm = pl.BlockSpec(memory_space=pl.ANY)
    return pl.pallas_call(
        functools.partial(place_kernel, dims, offsets),
        out_shape=jax.ShapeDtypeStruct(received.shape, received.dtype),
        in_specs=[hbm] * (1 + len(blocks)),
        out_specs=hbm,
        scratch_shapes=[pltpu.SemaphoreType.DMA((len(blocks),))],
        input_output_aliases={0: 0},
        compiler_params=pltpu.CompilerParams(vmem_limit_bytes=VMEM_LIMIT),
        cost_estimate=pl.CostEstimate(
            flops=0, bytes_accessed=4 * sum(b.size for b in blocks), transcendentals=0
        ),
        name="place_pages",
    )(received, *blocks)


def attend_kernel(dims, offsets, lengths, prefill_of, row_request, pool, *rest):
    shards = rest[: len(offsets)]
    out, queries, start_of, mine_rows, sems = rest[len(offsets) :]
    me = lax.axis_index("group")
    page_total, page_size, width = pool.shape
    row_local, query_heads = queries.shape[1:3]
    row_total = row_request.shape[0]
    kv_heads = width // (2 * HD)
    share = query_heads // kv_heads
    copies = []
    for i, offset in enumerate(offsets):
        copies.append(
            pltpu.make_async_copy(shards[i], queries.at[offset_rank(offset, dims)], sems.at[i])
        )
        copies[-1].start()
    out[...] = jnp.zeros_like(out)

    def visit(r, running):
        start_of[r] = running
        count = (lengths[r] + page_size - 1) // page_size
        return running + jnp.where(prefill_of[r] == me, count, 0)

    lax.fori_loop(0, lengths.shape[0], visit, jnp.int32(0), unroll=8)
    for i in range(ROW_UNROLL):
        mine_rows[i] = 0

    def collect(b, held):
        mine_rows[held] = b
        return held + jnp.where(prefill_of[row_request[b]] == me, 1, 0)

    row_count = lax.fori_loop(0, row_total, collect, jnp.int32(0), unroll=8)
    for i in range(ROW_UNROLL):
        mine_rows[row_count + i] = 0
    for copy in copies:
        copy.wait()
    scaling = 1.0 / math.sqrt(HD)

    def one_row(place):
        row = mine_rows[place]
        request = row_request[row]
        first = jnp.minimum(start_of[request], page_total - 1)
        second = jnp.minimum(first + 1, page_total - 1)
        length = lengths[request]
        from_rank = behind_rank(me, row // row_local, dims)
        query = queries[from_rank, lax.rem(row, row_local)]
        scores = []
        for h in range(kv_heads):
            columns = slice(2 * h * HD, (2 * h + 1) * HD)
            keys = jnp.concatenate([pool[first, :, columns], pool[second, :, columns]], axis=0)
            every = lax.dot_general(
                query, keys, (((1,), (1,)), ((), ())), preferred_element_type=jnp.float32
            )
            scores.append(every[h * share : (h + 1) * share])
        score = jnp.concatenate(scores, axis=0) * scaling
        token = lax.broadcasted_iota(jnp.int32, score.shape, 1)
        live = token < length
        masked = jnp.where(live, score, -1e30)
        highest = jnp.max(masked, axis=1, keepdims=True)
        weights = jnp.where(live, jnp.exp(masked - highest), 0.0)
        totals = jnp.sum(weights, axis=1, keepdims=True)
        rounded = weights.astype(jnp.bfloat16)
        mixtures = []
        for h in range(kv_heads):
            columns = slice((2 * h + 1) * HD, (2 * h + 2) * HD)
            values = jnp.concatenate([pool[first, :, columns], pool[second, :, columns]], axis=0)
            every = jnp.dot(rounded, values, preferred_element_type=jnp.float32)
            mixtures.append(every[h * share : (h + 1) * share])
        mixture = jnp.concatenate(mixtures, axis=0) / totals
        return mixture.astype(jnp.bfloat16)

    @pl.loop(0, (row_count + ROW_UNROLL - 1) // ROW_UNROLL)
    def _(step):
        for i in range(ROW_UNROLL):
            out[step * ROW_UNROLL + i] = one_row(step * ROW_UNROLL + i)


def attend(dims, shards, lengths, prefill_of, row_request, pool):
    offsets = list(shards)
    row_local, query_heads, _ = shards[offsets[0]].shape
    row_total = row_request.shape[0]
    smem = pl.BlockSpec(memory_space=pltpu.SMEM)
    vmem = pl.BlockSpec(memory_space=pltpu.VMEM)
    hbm = pl.BlockSpec(memory_space=pl.ANY)
    return pl.pallas_call(
        functools.partial(attend_kernel, dims, offsets),
        out_shape=jax.ShapeDtypeStruct((row_total + ROW_UNROLL, query_heads, HD), jnp.bfloat16),
        in_specs=[smem, smem, smem, vmem] + [hbm] * len(offsets),
        out_specs=vmem,
        scratch_shapes=[
            pltpu.VMEM((len(offsets), row_local, query_heads, HD), jnp.bfloat16),
            pltpu.SMEM((lengths.shape[0],), jnp.int32),
            pltpu.SMEM((row_total + ROW_UNROLL,), jnp.int32),
            pltpu.SemaphoreType.DMA((len(offsets),)),
        ],
        compiler_params=pltpu.CompilerParams(vmem_limit_bytes=VMEM_LIMIT),
        cost_estimate=pl.CostEstimate(
            flops=1 << 33, bytes_accessed=2 * pool.size, transcendentals=1 << 20
        ),
        name="attend_local_rows",
    )(lengths, prefill_of, row_request, pool, *(shards[o] for o in offsets))


def local(dims, kv_pool, lengths, prefill_of, decode_of, row_request, queries, out_weight):
    groups = math.prod(dims)
    me = lax.axis_index("group")
    row_local, query_width = queries.shape
    row_total = row_request.shape[0]
    query_heads = query_width // HD
    offsets = [o for o in itertools.product(*(range(n) for n in dims)) if any(o)]

    received, *sends = prepare(dims, offsets, lengths, prefill_of, decode_of, kv_pool)
    arrived = [send_by(block, offset, dims) for block, offset in zip(sends, offsets)]

    shards = gather_shards(queries.reshape(row_local, query_heads, HD), dims)
    rows = attend(dims, shards, lengths, prefill_of, row_request, kv_pool)
    rows = rows.reshape(rows.shape[0], query_width)

    row_home = prefill_of[row_request]
    ordinal = jnp.arange(row_total, dtype=jnp.int32)
    earlier = (row_home[None, :] == row_home[:, None]) & (ordinal[None, :] < ordinal[:, None])
    row_rank = jnp.sum(earlier.astype(jnp.int32), axis=1)
    home_slot = behind_rank(me, row_home, dims) * CAPACITY

    def gather_round(done):
        gathered = gather_shards(lax.dynamic_slice_in_dim(rows, done, CAPACITY), dims)
        stacked = jnp.concatenate(
            [gathered[o] for o in sorted(gathered, key=lambda o: offset_rank(o, dims))], axis=0
        )
        inside = (row_rank >= done) & (row_rank < done + CAPACITY)
        slot = jnp.where(inside, home_slot + row_rank - done, -1)
        chosen = slot[:, None] == jnp.arange(stacked.shape[0], dtype=jnp.int32)[None, :]
        return jnp.dot(
            chosen.astype(jnp.bfloat16), stacked, preferred_element_type=jnp.float32
        ).astype(jnp.bfloat16)

    most = jnp.max(row_rank) + 1
    attended = gather_round(jnp.int32(0))
    _, attended = lax.while_loop(
        lambda state: state[0] < most,
        lambda state: (state[0] + CAPACITY, state[1] + gather_round(state[0])),
        (jnp.int32(CAPACITY), attended),
    )
    product = jnp.dot(attended, out_weight, preferred_element_type=jnp.float32)

    heads = lax.axis_size("head")
    my_head = lax.axis_index("head")
    share = row_total // heads
    output = lax.dynamic_slice_in_dim(product, my_head * share, share)
    for ahead in range(1, heads):
        theirs = lax.dynamic_slice_in_dim(product, lax.rem(my_head + ahead, heads) * share, share)
        pairs = [(h, (h + ahead) % heads) for h in range(heads)]
        output = output + lax.ppermute(theirs.astype(jnp.bfloat16), "head", pairs).astype(jnp.float32)

    received = place(dims, offsets, received, arrived)
    return (received, output.astype(jnp.bfloat16))


def solution(mesh):
    in_specs = (
        P("group", None, "head"),
        P(),
        P(),
        P(),
        P(),
        P("group", "head"),
        P("head", "group"),
    )
    out_specs = (P("group", None, "head"), P("head", "group"))
    body = functools.partial(local, factors(mesh.shape["group"]))
    return jax.shard_map(body, mesh=mesh, in_specs=in_specs, out_specs=out_specs, check_vma=False)
```

time: 353 us -> 541 us (1.53)
  Pallas kernels: 0 us -> 251 us
  starting transfers between devices: 7.66 us -> 138 us
  waiting for transfers between devices: 244 us -> 122 us
  local copies, waits for them, and re-layouts: 52.3 us -> 14.6 us
  matrix products: 20.1 us -> 5.4 us
  between operations: 14.2 us -> 1.75 us
  other arithmetic: 13.9 us -> 2.22 us
    pallas_call x0 -> x3, Pallas kernels: none -> 251 us  [the longest x1 128 us: place(): pl.pallas_call(functools.partial(place_kernel, dims, offsets), out_shape=...]
    all_to_all x1 -> x0, waiting for transfers between devices: 148 us -> none  [local(): lax.all_to_all(outgoing, 'group', split_axis=0, concat_axis=0, tiled=True)]
    ppermute x0 -> x46, starting transfers between devices: none -> 138 us  [the longest x45 136 us: send_by(): return lax.ppermute(array, 'group', pairs)]
    ppermute x0 -> x46, waiting for transfers between devices: none -> 122 us  [the longest x45 122 us: send_by(): return lax.ppermute(array, 'group', pairs)]
    all_gather x1 -> x0, waiting for transfers between devices: 73.3 us -> none  [local(): gathered = lax.all_gather(attended, 'group', axis=0, tiled=True)]
    psum x1 -> x0, waiting for transfers between devices: 22.1 us -> none  [local(): lax.psum(jnp.dot(gathered, out_weight, preferred_element_type=jnp.float32...]
    slice x1 -> x0, local copies, waits for them, and re-layouts: 17.2 us -> none  [attend_all(): cache_heads[:, :, 1, :]]
    reshape x1 -> x0, local copies, waits for them, and re-layouts: 14.2 us -> none  [attend_all(): incoming.reshape(groups * slot_total * page_size, local_heads, 2, HD)]
  transfers between devices with their start and end apart: 3 -> 46, of which waited for: 3 -> 19; matrix products, arithmetic and copies ran while one was open for 1% -> 2% of each run, Pallas kernels for 0% -> 44%
where the time goes in v1:
time: 541 us; the launch traced here: 535 us
  Pallas kernels  251 us (46%)
  starting transfers between devices  138 us (26%)
  waiting for transfers between devices  122 us (23%)
  local copies, waits for them, and re-layouts  14.6 us (3%)
    ppermute x45, starting transfers between devices, send_by(): return lax.ppermute(array, 'group', pairs)  136 us
    pallas_call x1, Pallas kernels, place(): pl.pallas_call(functools.partial(place_kernel, dims, offsets), out_shape=...  128 us
    ppermute x45, waiting for transfers between devices, send_by(): return lax.ppermute(array, 'group', pairs)  122 us
    pallas_call x1, Pallas kernels, prepare(): pl.pallas_call(functools.partial(prepare_kernel, dims, offsets), out_shap...  107 us
    pallas_call x1, Pallas kernels, attend(): pl.pallas_call(functools.partial(attend_kernel, dims, offsets), out_shape...  15.7 us
    unnamed x49, local copies, waits for them, and re-layouts  12.6 us
  transfers between devices with their start and end apart: 46, of which 19 were waited for; matrix products, arithmetic and copies ran while one was open for 2% of the time, Pallas kernels for 44%

profile of v1, /device:TPU:0, one launch (start us, length us, event | category | flops | bytes accessed | tf_op | source)
XLA Modules:
  0.0 534.8 jit_solution(2935001902520744502)
XLA Ops:
  0.6 0.9 copy.10
  1.6 3.1 collective-permute-start.30
  4.6 2.6 collective-permute-start.31
  7.2 1.3 collective-permute-start.32
  8.6 1.5 collective-permute-start.33
  10.8 2.0 gather_fusion
  13.6 2.3 collective-permute-done.31.rest_2_
  15.9 1.5 collective-permute-start.35
  21.5 107.3 %outgoing_pages.1 = (bf16[32,128,1024]{2,1,0:T(8,128)(2,1)}, bf16[2,128,1024]{2,1,0:T(8,128)(2,1)S(1)}, bf16[2,128,1024]{2,1,0:T(8,128)(2,1)}, bf16[2,128,1024]{...) custom-call(s32[256]{0:T(256)S(1)} %copy-done.4, ...), custom_call_target="tpu_custom_call" | custom-call | bytes 16777216 | tf_op jit(solution)/shard_map/outgoing_pages/pallas_call | solution.py:126
  128.8 0.8 copy-done.9
  129.6 0.8 copy-done.10
  130.4 0.8 copy-done.11
  131.2 16.0 %collective-permute-start.40 = (bf16[16,32,128]{2,1,0:T(8,128)(2,1)S(1)}, bf16[16,32,128]{2,1,0:T(8,128)(2,1)S(1)}, u32[]{:S(2)}, u32[]{:S(2)}) collective-permute-start(bf16[16,32,128]{2,1,0:T(8,128)(2,1)S(1)} %collective-permute-done.32.rest_3_), channel_id=1, source_target_pairs={{0,2},{2,0},{4,6},{6,4},{8,10},{10,8},{12,14},{14,12},{16,18},{18,... | collective-permute-start | bytes 393224 | tf_op jit(solution)/shard_map/ppermute | solution.py:46
  149.2 15.7 %attend_local_rows.1 = bf16[260,32,128]{2,1,0:T(8,128)(2,1)S(1)} custom-call(s32[256]{0:T(256)S(1)} %copy-done.4, s32[256]{0:T(256)S(1)} %copy-done, s32[256]{0:T(256)S(1)} %copy-done.5, bf16[32,128,1024]{2,1,0:T(8,128)(2,1)} %pool.3, bf16[16,32,128]{2,1,0:T(8,128)(2,1)S(1)} %bitcast.27, bf16[16,32,128]{2,1,0:T(8,128)(2,1)S(1)} %collective-permute-done.30.rest_1_, ...), custom_call_target="tpu_custom_call" | custom-call | flops 8589934592 | bytes 8388608 | tf_op jit(solution)/shard_map/attend_local_rows/pallas_call | solution.py:261
  165.2 22.2 %collective-permute-start.48 = (bf16[32,4096]{1,0:T(8,128)(2,1)S(1)}, bf16[32,4096]{1,0:T(8,128)(2,1)S(1)}, u32[]{:S(2)}, u32[]{:S(2)}) collective-permute-start(bf16[32,4096]{1,0:T(8,128)(2,1)S(1)} %bitcast.34), channel_id=1, source_target_pairs={{0,8},{2,10},{4,12},{6,14},{8,16},{10,18},{12,20},{14,22},{16,24},... | collective-permute-start | bytes 786440 | tf_op jit(solution)/shard_map/ppermute | solution.py:46
  188.0 2.4 copy.12
  190.4 2.3 collective-permute-start.56
  192.8 1.4 collective-permute-done.48
  194.3 7.4 %collective-permute-done.52 = bf16[32,4096]{1,0:T(8,128)(2,1)S(1)} collective-permute-done((bf16[32,4096]{1,0:T(8,128)(2,1)S(1)}, bf16[32,4096]{1,0:T(8,128)(2,1)S(1)}, u32[]{:S(2)}, u32[]{:S(2)}) %collective-permute-start.52) | collective-permute-done | bytes 262176 | tf_op jit(solution)/shard_map/ppermute | solution.py:46
  202.2 2.1 collective-permute-done.56
  205.2 5.7 %collective-permute-done.54 = bf16[32,4096]{1,0:T(8,128)(2,1)S(1)} collective-permute-done((bf16[32,4096]{1,0:T(8,128)(2,1)S(1)}, bf16[32,4096]{1,0:T(8,128)(2,1)S(1)}, u32[]{:S(2)}, u32[]{:S(2)}) %collective-permute-start.54) | collective-permute-done | bytes 262176 | tf_op jit(solution)/shard_map/ppermute | solution.py:46
  210.9 5.2 collective-permute-done.58
  216.4 1.3 collective-permute-done.59
  217.7 1.3 convolution_convert_fusion.1
  219.1 1.3 copy-done.12
  220.9 1.3 collective-permute-start.17
  222.3 8.4 %collective-permute-start.18 = (bf16[2,128,1024]{2,1,0:T(8,128)(2,1)}, bf16[2,128,1024]{2,1,0:T(8,128)(2,1)S(1)}, u32[]{:S(2)}, u32[]{:S(2)}) collective-permute-start(bf16[2,128,1024]{2,1,0:T(8,128)(2,1)} %get-tuple-element.98), channel_id=1, source_target_pairs={{0,8},{2,10},{4,12},{6,14},{8,16},{10,18},{12,20},{14,22},{16,24},... | collective-permute-start | bytes 1572872 | tf_op jit(solution)/shard_map/ppermute | solution.py:46
  230.8 3.4 collective-permute-start.20
  234.2 1.3 collective-permute-done.16.rest_1_
  235.5 6.8 %collective-permute-start.21 = (bf16[2,128,1024]{2,1,0:T(8,128)(2,1)}, bf16[2,128,1024]{2,1,0:T(8,128)(2,1)}, u32[]{:S(2)}, u32[]{:S(2)}) collective-permute-start(bf16[2,128,1024]{2,1,0:T(8,128)(2,1)} %copy-done.10), channel_id=1, source_target_pairs={{0,14},{2,12},{4,10},{6,8},{8,22},{10,20},{12,18},{14,16},{16,30},... | collective-permute-start | bytes 1572872 | tf_op jit(solution)/shard_map/ppermute | solution.py:46
  242.3 3.3 collective-permute-done.17.rest_2_
  245.6 1.5 collective-permute-start.22
  247.2 1.4 collective-permute-start.23
  248.6 8.7 %collective-permute-done.19.rest_4_ = bf16[2,128,1024]{2,1,0:T(8,128)(2,1)S(1)} collective-permute-done((bf16[2,128,1024]{2,1,0:T(8,128)(2,1)}, bf16[2,128,1024]{2,1,0:T(8,128)(2,1)S(1)}, u32[]{:S(2)}, u32[]{:S(2)}) %collective-permute-start.19) | collective-permute-done | bytes 524320 | tf_op jit(solution)/shard_map/ppermute | solution.py:46
  257.6 11.2 %collective-permute-done.20.rest_5_ = bf16[2,128,1024]{2,1,0:T(8,128)(2,1)S(1)} collective-permute-done((bf16[2,128,1024]{2,1,0:T(8,128)(2,1)}, bf16[2,128,1024]{2,1,0:T(8,128)(2,1)S(1)}, u32[]{:S(2)}, u32[]{:S(2)}) %collective-permute-start.20) | collective-permute-done | bytes 524320 | tf_op jit(solution)/shard_map/ppermute | solution.py:46
  268.8 10.8 %collective-permute-done.21.rest_6_ = bf16[2,128,1024]{2,1,0:T(8,128)(2,1)} collective-permute-done((bf16[2,128,1024]{2,1,0:T(8,128)(2,1)}, bf16[2,128,1024]{2,1,0:T(8,128)(2,1)}, u32[]{:S(2)}, u32[]{:S(2)}) %collective-permute-start.21) | collective-permute-done | bytes 524320 | tf_op jit(solution)/shard_map/ppermute | solution.py:46
  279.7 2.8 collective-permute-start.26
  282.4 53.8 %collective-permute-done.22.rest_7_ = bf16[2,128,1024]{2,1,0:T(8,128)(2,1)} collective-permute-done((bf16[2,128,1024]{2,1,0:T(8,128)(2,1)}, bf16[2,128,1024]{2,1,0:T(8,128)(2,1)}, u32[]{:S(2)}, u32[]{:S(2)}) %collective-permute-start.22) | collective-permute-done | bytes 524320 | tf_op jit(solution)/shard_map/ppermute | solution.py:46
  336.2 10.2 %collective-permute-start.27 = (bf16[2,128,1024]{2,1,0:T(8,128)(2,1)}, bf16[2,128,1024]{2,1,0:T(8,128)(2,1)}, u32[]{:S(2)}, u32[]{:S(2)}) collective-permute-start(bf16[2,128,1024]{2,1,0:T(8,128)(2,1)} %get-tuple-element.107), channel_id=1, source_target_pairs={{0,26},{2,24},{4,30},{6,28},{8,2},{10,0},{12,6},{14,4},{16,10},{18... | collective-permute-start | bytes 1572872 | tf_op jit(solution)/shard_map/ppermute | solution.py:46
  346.4 1.1 collective-permute-done.23.rest_8_
  347.5 21.5 %collective-permute-start.28 = (bf16[2,128,1024]{2,1,0:T(8,128)(2,1)}, bf16[2,128,1024]{2,1,0:T(8,128)(2,1)}, u32[]{:S(2)}, u32[]{:S(2)}) collective-permute-start(bf16[2,128,1024]{2,1,0:T(8,128)(2,1)} %get-tuple-element.108), channel_id=1, source_target_pairs={{0,28},{2,30},{4,24},{6,26},{8,4},{10,6},{12,0},{14,2},{16,12},{18... | collective-permute-start | bytes 1572872 | tf_op jit(solution)/shard_map/ppermute | solution.py:46
  369.0 23.3 %collective-permute-start.29 = (bf16[2,128,1024]{2,1,0:T(8,128)(2,1)}, bf16[2,128,1024]{2,1,0:T(8,128)(2,1)}, u32[]{:S(2)}, u32[]{:S(2)}) collective-permute-start(bf16[2,128,1024]{2,1,0:T(8,128)(2,1)} %get-tuple-element.109), channel_id=1, source_target_pairs={{0,30},{2,28},{4,26},{6,24},{8,6},{10,4},{12,2},{14,0},{16,14},{18... | collective-permute-start | bytes 1572872 | tf_op jit(solution)/shard_map/ppermute | solution.py:46
  392.3 4.1 fusion.34
  397.2 0.8 copy-done.1
  398.0 1.5 collective-permute-start.60
  399.5 5.2 collective-permute-done.29.rest_14_
  404.7 1.0 copy-done.2
  405.8 128.3 %place_pages.1 = bf16[32,128,1024]{2,1,0:T(8,128)(2,1)} custom-call(bf16[32,128,1024]{2,1,0:T(8,128)(2,1)} %get-tuple-element.94.received_in, bf16[2,128,1024]{2,1,0:T(8,128)(2,1)S(1)} %collective-permute-done.15.rest_0_, bf16[2,128,1024]{2,1,0:T(8,128)(2,1)S(1)} %collective-permute-done.16.rest_1_, ...), custom_call_target="tpu_custom_call", output_to_operand_aliasing={{}: (0, {})} | custom-call | bytes 15728640 | tf_op jit(solution)/shard_map/place_pages/pallas_call | solution.py:163
  (109 shorter events, 11.9 us)
Async XLA Ops:
  1.6 11.5 %collective-permute-start.30 = (bf16[16,32,128]{2,1,0:T(8,128)(2,1)S(1)}, bf16[16,32,128]{2,1,0:T(8,128)(2,1)S(1)}, u32[]{:S(2)}, u32[]{:S(2)}) collective-permute-start(bf16[16,32,128]{2,1,0:T(8,128)(2,1)S(1)} %bitcast.22), channel_id=1, source_target_pairs={{0,8},{2,10},{4,12},{6,14},{8,16},{10,18},{12,20},{14,22},{16,24},... | collective-permute-start | bytes 393224 | tf_op jit(solution)/shard_map/ppermute | solution.py:46
  4.6 11.2 %collective-permute-start.31 = (bf16[16,32,128]{2,1,0:T(8,128)(2,1)S(1)}, bf16[16,32,128]{2,1,0:T(8,128)(2,1)S(1)}, u32[]{:S(2)}, u32[]{:S(2)}) collective-permute-start(bf16[16,32,128]{2,1,0:T(8,128)(2,1)S(1)} %bitcast.23), channel_id=1, source_target_pairs={{0,16},{2,18},{4,20},{6,22},{8,24},{10,26},{12,28},{14,30},{16,0},... | collective-permute-start | bytes 393224 | tf_op jit(solution)/shard_map/ppermute | solution.py:46
  7.2 8.6 %collective-permute-start.32 = (bf16[16,32,128]{2,1,0:T(8,128)(2,1)S(1)}, bf16[16,32,128]{2,1,0:T(8,128)(2,1)S(1)}, u32[]{:S(2)}, u32[]{:S(2)}) collective-permute-start(bf16[16,32,128]{2,1,0:T(8,128)(2,1)S(1)} %bitcast.24), channel_id=1, source_target_pairs={{0,24},{2,26},{4,28},{6,30},{8,0},{10,2},{12,4},{14,6},{16,8},{18,... | collective-permute-start | bytes 393224 | tf_op jit(solution)/shard_map/ppermute | solution.py:46
  8.6 8.8 %collective-permute-start.33 = (bf16[16,32,128]{2,1,0:T(8,128)(2,1)S(1)}, bf16[16,32,128]{2,1,0:T(8,128)(2,1)S(1)}, u32[]{:S(2)}, u32[]{:S(2)}) collective-permute-start(bf16[16,32,128]{2,1,0:T(8,128)(2,1)S(1)} %bitcast.25), channel_id=1, source_target_pairs={{0,4},{2,6},{4,0},{6,2},{8,12},{10,14},{12,8},{14,10},{16,20},{18,... | collective-permute-start | bytes 393224 | tf_op jit(solution)/shard_map/ppermute | solution.py:46
  10.8 6.9 %collective-permute-start.37 = (bf16[16,32,128]{2,1,0:T(8,128)(2,1)S(1)}, bf16[16,32,128]{2,1,0:T(8,128)(2,1)S(1)}, u32[]{:S(2)}, u32[]{:S(2)}) collective-permute-start(bf16[16,32,128]{2,1,0:T(8,128)(2,1)S(1)} %bitcast.26), channel_id=1, source_target_pairs={{0,2},{2,0},{4,6},{6,4},{8,10},{10,8},{12,14},{14,12},{16,18},{18,... | collective-permute-start | bytes 393224 | tf_op jit(solution)/shard_map/ppermute | solution.py:46
  13.0 118.2 %collective-permute-start.34 = (bf16[16,32,128]{2,1,0:T(8,128)(2,1)S(1)}, bf16[16,32,128]{2,1,0:T(8,128)(2,1)S(1)}, u32[]{:S(2)}, u32[]{:S(2)}) collective-permute-start(bf16[16,32,128]{2,1,0:T(8,128)(2,1)S(1)} %collective-permute-done.30.rest_1_), channel_id=1, source_target_pairs={{0,4},{2,6},{4,0},{6,2},{8,12},{10,14},{12,8},{14,10},{16,20},{18,... | collective-permute-start | bytes 393224 | tf_op jit(solution)/shard_map/ppermute | solution.py:46
  15.9 131.8 %collective-permute-start.38 = (bf16[16,32,128]{2,1,0:T(8,128)(2,1)S(1)}, bf16[16,32,128]{2,1,0:T(8,128)(2,1)S(1)}, u32[]{:S(2)}, u32[]{:S(2)}) collective-permute-start(bf16[16,32,128]{2,1,0:T(8,128)(2,1)S(1)} %collective-permute-done.30.rest_1_), channel_id=1, source_target_pairs={{0,2},{2,0},{4,6},{6,4},{8,10},{10,8},{12,14},{14,12},{16,18},{18,... | collective-permute-start | bytes 393224 | tf_op jit(solution)/shard_map/ppermute | solution.py:46
  15.9 131.3 %collective-permute-start.35 = (bf16[16,32,128]{2,1,0:T(8,128)(2,1)S(1)}, bf16[16,32,128]{2,1,0:T(8,128)(2,1)S(1)}, u32[]{:S(2)}, u32[]{:S(2)}) collective-permute-start(bf16[16,32,128]{2,1,0:T(8,128)(2,1)S(1)} %collective-permute-done.31.rest_2_), channel_id=1, source_target_pairs={{0,4},{2,6},{4,0},{6,2},{8,12},{10,14},{12,8},{14,10},{16,20},{18,... | collective-permute-start | bytes 393224 | tf_op jit(solution)/shard_map/ppermute | solution.py:46
  17.4 130.4 %collective-permute-start.39 = (bf16[16,32,128]{2,1,0:T(8,128)(2,1)S(1)}, bf16[16,32,128]{2,1,0:T(8,128)(2,1)S(1)}, u32[]{:S(2)}, u32[]{:S(2)}) collective-permute-start(bf16[16,32,128]{2,1,0:T(8,128)(2,1)S(1)} %collective-permute-done.31.rest_2_), channel_id=1, source_target_pairs={{0,2},{2,0},{4,6},{6,4},{8,10},{10,8},{12,14},{14,12},{16,18},{18,... | collective-permute-start | bytes 393224 | tf_op jit(solution)/shard_map/ppermute | solution.py:46
  17.6 129.6 %collective-permute-start.36 = (bf16[16,32,128]{2,1,0:T(8,128)(2,1)S(1)}, bf16[16,32,128]{2,1,0:T(8,128)(2,1)S(1)}, u32[]{:S(2)}, u32[]{:S(2)}) collective-permute-start(bf16[16,32,128]{2,1,0:T(8,128)(2,1)S(1)} %collective-permute-done.32.rest_3_), channel_id=1, source_target_pairs={{0,4},{2,6},{4,0},{6,2},{8,12},{10,14},{12,8},{14,10},{16,20},{18,... | collective-permute-start | bytes 393224 | tf_op jit(solution)/shard_map/ppermute | solution.py:46
  21.5 127.8 %copy-start.5 = (s32[256]{0:T(256)S(1)}, s32[256]{0:T(256)}, u32[]{:S(2)}) copy-start(s32[256]{0:T(256)} %row_request.1) | copy-start | bytes 3076
  131.2 17.0 %collective-permute-start.40 = (bf16[16,32,128]{2,1,0:T(8,128)(2,1)S(1)}, bf16[16,32,128]{2,1,0:T(8,128)(2,1)S(1)}, u32[]{:S(2)}, u32[]{:S(2)}) collective-permute-start(bf16[16,32,128]{2,1,0:T(8,128)(2,1)S(1)} %collective-permute-done.32.rest_3_), channel_id=1, source_target_pairs={{0,2},{2,0},{4,6},{6,4},{8,10},{10,8},{12,14},{14,12},{16,18},{18,... | collective-permute-start | bytes 393224 | tf_op jit(solution)/shard_map/ppermute | solution.py:46
  147.2 1.3 collective-permute-start.41
  147.3 1.4 collective-permute-start.42
  147.7 1.3 collective-permute-start.43
  147.8 1.4 collective-permute-start.44
  165.1 29.1 %collective-permute-start.45 = (bf16[32,4096]{1,0:T(8,128)(2,1)S(1)}, bf16[32,4096]{1,0:T(8,128)(2,1)S(1)}, u32[]{:S(2)}, u32[]{:S(2)}) collective-permute-start(bf16[32,4096]{1,0:T(8,128)(2,1)S(1)} %bitcast.32), channel_id=1, source_target_pairs={{0,2},{2,0},{4,6},{6,4},{8,10},{10,8},{12,14},{14,12},{16,18},{18,... | collective-permute-start | bytes 786440 | tf_op jit(solution)/shard_map/ppermute | solution.py:46
  165.1 27.6 %collective-permute-start.46 = (bf16[32,4096]{1,0:T(8,128)(2,1)S(1)}, bf16[32,4096]{1,0:T(8,128)(2,1)S(1)}, u32[]{:S(2)}, u32[]{:S(2)}) collective-permute-start(bf16[32,4096]{1,0:T(8,128)(2,1)S(1)} %bitcast.33), channel_id=1, source_target_pairs={{0,4},{2,6},{4,0},{6,2},{8,12},{10,14},{12,8},{14,10},{16,20},{18,... | collective-permute-start | bytes 786440 | tf_op jit(solution)/shard_map/ppermute | solution.py:46
  165.2 28.9 %collective-permute-start.48 = (bf16[32,4096]{1,0:T(8,128)(2,1)S(1)}, bf16[32,4096]{1,0:T(8,128)(2,1)S(1)}, u32[]{:S(2)}, u32[]{:S(2)}) collective-permute-start(bf16[32,4096]{1,0:T(8,128)(2,1)S(1)} %bitcast.34), channel_id=1, source_target_pairs={{0,8},{2,10},{4,12},{6,14},{8,16},{10,18},{12,20},{14,22},{16,24},... | collective-permute-start | bytes 786440 | tf_op jit(solution)/shard_map/ppermute | solution.py:46
  187.5 14.2 %collective-permute-start.52 = (bf16[32,4096]{1,0:T(8,128)(2,1)S(1)}, bf16[32,4096]{1,0:T(8,128)(2,1)S(1)}, u32[]{:S(2)}, u32[]{:S(2)}) collective-permute-start(bf16[32,4096]{1,0:T(8,128)(2,1)S(1)} %bitcast.35), channel_id=1, source_target_pairs={{0,16},{2,18},{4,20},{6,22},{8,24},{10,26},{12,28},{14,30},{16,0},... | collective-permute-start | bytes 786440 | tf_op jit(solution)/shard_map/ppermute | solution.py:46
  190.4 13.8 %collective-permute-start.56 = (bf16[32,4096]{1,0:T(8,128)(2,1)S(1)}, bf16[32,4096]{1,0:T(8,128)(2,1)S(1)}, u32[]{:S(2)}, u32[]{:S(2)}) collective-permute-start(bf16[32,4096]{1,0:T(8,128)(2,1)S(1)} %bitcast.36), channel_id=1, source_target_pairs={{0,24},{2,26},{4,28},{6,30},{8,0},{10,2},{12,4},{14,6},{16,8},{18,... | collective-permute-start | bytes 786440 | tf_op jit(solution)/shard_map/ppermute | solution.py:46
  192.8 9.0 %collective-permute-start.47 = (bf16[32,4096]{1,0:T(8,128)(2,1)S(1)}, bf16[32,4096]{1,0:T(8,128)(2,1)S(1)}, u32[]{:S(2)}, u32[]{:S(2)}) collective-permute-start(bf16[32,4096]{1,0:T(8,128)(2,1)S(1)} %collective-permute-done.46), channel_id=1, source_target_pairs={{0,2},{2,0},{4,6},{6,4},{8,10},{10,8},{12,14},{14,12},{16,18},{18,... | collective-permute-start | bytes 786440 | tf_op jit(solution)/shard_map/ppermute | solution.py:46
  194.2 10.4 %collective-permute-start.49 = (bf16[32,4096]{1,0:T(8,128)(2,1)S(1)}, bf16[32,4096]{1,0:T(8,128)(2,1)S(1)}, u32[]{:S(2)}, u32[]{:S(2)}) collective-permute-start(bf16[32,4096]{1,0:T(8,128)(2,1)S(1)} %collective-permute-done.48), channel_id=1, source_target_pairs={{0,2},{2,0},{4,6},{6,4},{8,10},{10,8},{12,14},{14,12},{16,18},{18,... | collective-permute-start | bytes 786440 | tf_op jit(solution)/shard_map/ppermute | solution.py:46
  194.2 10.4 %collective-permute-start.50 = (bf16[32,4096]{1,0:T(8,128)(2,1)S(1)}, bf16[32,4096]{1,0:T(8,128)(2,1)S(1)}, u32[]{:S(2)}, u32[]{:S(2)}) collective-permute-start(bf16[32,4096]{1,0:T(8,128)(2,1)S(1)} %collective-permute-done.48), channel_id=1, source_target_pairs={{0,4},{2,6},{4,0},{6,2},{8,12},{10,14},{12,8},{14,10},{16,20},{18,... | collective-permute-start | bytes 786440 | tf_op jit(solution)/shard_map/ppermute | solution.py:46
  201.7 14.5 %collective-permute-start.53 = (bf16[32,4096]{1,0:T(8,128)(2,1)S(1)}, bf16[32,4096]{1,0:T(8,128)(2,1)S(1)}, u32[]{:S(2)}, u32[]{:S(2)}) collective-permute-start(bf16[32,4096]{1,0:T(8,128)(2,1)S(1)} %collective-permute-done.52), channel_id=1, source_target_pairs={{0,2},{2,0},{4,6},{6,4},{8,10},{10,8},{12,14},{14,12},{16,18},{18,... | collective-permute-start | bytes 786440 | tf_op jit(solution)/shard_map/ppermute | solution.py:46
  201.8 9.2 %collective-permute-start.54 = (bf16[32,4096]{1,0:T(8,128)(2,1)S(1)}, bf16[32,4096]{1,0:T(8,128)(2,1)S(1)}, u32[]{:S(2)}, u32[]{:S(2)}) collective-permute-start(bf16[32,4096]{1,0:T(8,128)(2,1)S(1)} %collective-permute-done.52), channel_id=1, source_target_pairs={{0,4},{2,6},{4,0},{6,2},{8,12},{10,14},{12,8},{14,10},{16,20},{18,... | collective-permute-start | bytes 786440 | tf_op jit(solution)/shard_map/ppermute | solution.py:46
  204.3 11.9 %collective-permute-start.58 = (bf16[32,4096]{1,0:T(8,128)(2,1)S(1)}, bf16[32,4096]{1,0:T(8,128)(2,1)S(1)}, u32[]{:S(2)}, u32[]{:S(2)}) collective-permute-start(bf16[32,4096]{1,0:T(8,128)(2,1)S(1)} %collective-permute-done.56), channel_id=1, source_target_pairs={{0,4},{2,6},{4,0},{6,2},{8,12},{10,14},{12,8},{14,10},{16,20},{18,... | collective-permute-start | bytes 786440 | tf_op jit(solution)/shard_map/ppermute | solution.py:46
  204.6 11.6 %collective-permute-start.51 = (bf16[32,4096]{1,0:T(8,128)(2,1)S(1)}, bf16[32,4096]{1,0:T(8,128)(2,1)S(1)}, u32[]{:S(2)}, u32[]{:S(2)}) collective-permute-start(bf16[32,4096]{1,0:T(8,128)(2,1)S(1)} %collective-permute-done.50), channel_id=1, source_target_pairs={{0,2},{2,0},{4,6},{6,4},{8,10},{10,8},{12,14},{14,12},{16,18},{18,... | collective-permute-start | bytes 786440 | tf_op jit(solution)/shard_map/ppermute | solution.py:46
  204.7 11.7 %collective-permute-start.57 = (bf16[32,4096]{1,0:T(8,128)(2,1)S(1)}, bf16[32,4096]{1,0:T(8,128)(2,1)S(1)}, u32[]{:S(2)}, u32[]{:S(2)}) collective-permute-start(bf16[32,4096]{1,0:T(8,128)(2,1)S(1)} %collective-permute-done.56), channel_id=1, source_target_pairs={{0,2},{2,0},{4,6},{6,4},{8,10},{10,8},{12,14},{14,12},{16,18},{18,... | collective-permute-start | bytes 786440 | tf_op jit(solution)/shard_map/ppermute | solution.py:46
  210.9 5.4 %collective-permute-start.55 = (bf16[32,4096]{1,0:T(8,128)(2,1)S(1)}, bf16[32,4096]{1,0:T(8,128)(2,1)S(1)}, u32[]{:S(2)}, u32[]{:S(2)}) collective-permute-start(bf16[32,4096]{1,0:T(8,128)(2,1)S(1)} %collective-permute-done.54), channel_id=1, source_target_pairs={{0,2},{2,0},{4,6},{6,4},{8,10},{10,8},{12,14},{14,12},{16,18},{18,... | collective-permute-start | bytes 786440 | tf_op jit(solution)/shard_map/ppermute | solution.py:46
  216.2 1.5 collective-permute-start.59
  220.4 10.3 %collective-permute-start.15 = (bf16[2,128,1024]{2,1,0:T(8,128)(2,1)S(1)}, bf16[2,128,1024]{2,1,0:T(8,128)(2,1)S(1)}, u32[]{:S(2)}, u32[]{:S(2)}) collective-permute-start(bf16[2,128,1024]{2,1,0:T(8,128)(2,1)S(1)} %get-tuple-element.95), channel_id=1, source_target_pairs={{0,2},{2,0},{4,6},{6,4},{8,10},{10,8},{12,14},{14,12},{16,18},{18,... | collective-permute-start | bytes 1572872 | tf_op jit(solution)/shard_map/ppermute | solution.py:46
  220.5 15.0 %collective-permute-start.16 = (bf16[2,128,1024]{2,1,0:T(8,128)(2,1)}, bf16[2,128,1024]{2,1,0:T(8,128)(2,1)S(1)}, u32[]{:S(2)}, u32[]{:S(2)}) collective-permute-start(bf16[2,128,1024]{2,1,0:T(8,128)(2,1)} %get-tuple-element.96), channel_id=1, source_target_pairs={{0,4},{2,6},{4,0},{6,2},{8,12},{10,14},{12,8},{14,10},{16,20},{18,... | collective-permute-start | bytes 1572872 | tf_op jit(solution)/shard_map/ppermute | solution.py:46
  220.9 24.7 %collective-permute-start.17 = (bf16[2,128,1024]{2,1,0:T(8,128)(2,1)}, bf16[2,128,1024]{2,1,0:T(8,128)(2,1)S(1)}, u32[]{:S(2)}, u32[]{:S(2)}) collective-permute-start(bf16[2,128,1024]{2,1,0:T(8,128)(2,1)} %get-tuple-element.97), channel_id=1, source_target_pairs={{0,6},{2,4},{4,2},{6,0},{8,14},{10,12},{12,10},{14,8},{16,22},{18,... | collective-permute-start | bytes 1572872 | tf_op jit(solution)/shard_map/ppermute | solution.py:46
  222.3 24.9 %collective-permute-start.18 = (bf16[2,128,1024]{2,1,0:T(8,128)(2,1)}, bf16[2,128,1024]{2,1,0:T(8,128)(2,1)S(1)}, u32[]{:S(2)}, u32[]{:S(2)}) collective-permute-start(bf16[2,128,1024]{2,1,0:T(8,128)(2,1)} %get-tuple-element.98), channel_id=1, source_target_pairs={{0,8},{2,10},{4,12},{6,14},{8,16},{10,18},{12,20},{14,22},{16,24},... | collective-permute-start | bytes 1572872 | tf_op jit(solution)/shard_map/ppermute | solution.py:46
  230.7 26.6 %collective-permute-start.19 = (bf16[2,128,1024]{2,1,0:T(8,128)(2,1)}, bf16[2,128,1024]{2,1,0:T(8,128)(2,1)S(1)}, u32[]{:S(2)}, u32[]{:S(2)}) collective-permute-start(bf16[2,128,1024]{2,1,0:T(8,128)(2,1)} %get-tuple-element.99), channel_id=1, source_target_pairs={{0,10},{2,8},{4,14},{6,12},{8,18},{10,16},{12,22},{14,20},{16,26},... | collective-permute-start | bytes 1572872 | tf_op jit(solution)/shard_map/ppermute | solution.py:46
  230.8 38.1 %collective-permute-start.20 = (bf16[2,128,1024]{2,1,0:T(8,128)(2,1)}, bf16[2,128,1024]{2,1,0:T(8,128)(2,1)S(1)}, u32[]{:S(2)}, u32[]{:S(2)}) collective-permute-start(bf16[2,128,1024]{2,1,0:T(8,128)(2,1)} %copy-done.11), channel_id=1, source_target_pairs={{0,12},{2,14},{4,8},{6,10},{8,20},{10,22},{12,16},{14,18},{16,28},... | collective-permute-start | bytes 1572872 | tf_op jit(solution)/shard_map/ppermute | solution.py:46
  235.5 44.1 %collective-permute-start.21 = (bf16[2,128,1024]{2,1,0:T(8,128)(2,1)}, bf16[2,128,1024]{2,1,0:T(8,128)(2,1)}, u32[]{:S(2)}, u32[]{:S(2)}) collective-permute-start(bf16[2,128,1024]{2,1,0:T(8,128)(2,1)} %copy-done.10), channel_id=1, source_target_pairs={{0,14},{2,12},{4,10},{6,8},{8,22},{10,20},{12,18},{14,16},{16,30},... | collective-permute-start | bytes 1572872 | tf_op jit(solution)/shard_map/ppermute | solution.py:46
  245.6 90.6 %collective-permute-start.22 = (bf16[2,128,1024]{2,1,0:T(8,128)(2,1)}, bf16[2,128,1024]{2,1,0:T(8,128)(2,1)}, u32[]{:S(2)}, u32[]{:S(2)}) collective-permute-start(bf16[2,128,1024]{2,1,0:T(8,128)(2,1)} %copy-done.9), channel_id=1, source_target_pairs={{0,16},{2,18},{4,20},{6,22},{8,24},{10,26},{12,28},{14,30},{16,0},... | collective-permute-start | bytes 1572872 | tf_op jit(solution)/shard_map/ppermute | solution.py:46
  247.2 100.3 %collective-permute-start.23 = (bf16[2,128,1024]{2,1,0:T(8,128)(2,1)}, bf16[2,128,1024]{2,1,0:T(8,128)(2,1)}, u32[]{:S(2)}, u32[]{:S(2)}) collective-permute-start(bf16[2,128,1024]{2,1,0:T(8,128)(2,1)} %copy-done.8), channel_id=1, source_target_pairs={{0,18},{2,16},{4,22},{6,20},{8,26},{10,24},{12,30},{14,28},{16,2},... | collective-permute-start | bytes 1572872 | tf_op jit(solution)/shard_map/ppermute | solution.py:46
  257.3 111.7 %collective-permute-start.24 = (bf16[2,128,1024]{2,1,0:T(8,128)(2,1)}, bf16[2,128,1024]{2,1,0:T(8,128)(2,1)}, u32[]{:S(2)}, u32[]{:S(2)}) collective-permute-start(bf16[2,128,1024]{2,1,0:T(8,128)(2,1)} %copy-done.7), channel_id=1, source_target_pairs={{0,20},{2,22},{4,16},{6,18},{8,28},{10,30},{12,24},{14,26},{16,4},... | collective-permute-start | bytes 1572872 | tf_op jit(solution)/shard_map/ppermute | solution.py:46
  268.8 127.6 %collective-permute-start.25 = (bf16[2,128,1024]{2,1,0:T(8,128)(2,1)}, bf16[2,128,1024]{2,1,0:T(8,128)(2,1)S(1)}, u32[]{:S(2)}, u32[]{:S(2)}) collective-permute-start(bf16[2,128,1024]{2,1,0:T(8,128)(2,1)} %copy-done.6), channel_id=1, source_target_pairs={{0,22},{2,20},{4,18},{6,16},{8,30},{10,28},{12,26},{14,24},{16,6},... | collective-permute-start | bytes 1572872 | tf_op jit(solution)/shard_map/ppermute | solution.py:46
  279.7 119.8 %collective-permute-start.26 = (bf16[2,128,1024]{2,1,0:T(8,128)(2,1)}, bf16[2,128,1024]{2,1,0:T(8,128)(2,1)}, u32[]{:S(2)}, u32[]{:S(2)}) collective-permute-start(bf16[2,128,1024]{2,1,0:T(8,128)(2,1)} %get-tuple-element.106), channel_id=1, source_target_pairs={{0,24},{2,26},{4,28},{6,30},{8,0},{10,2},{12,4},{14,6},{16,8},{18,... | collective-permute-start | bytes 1572872 | tf_op jit(solution)/shard_map/ppermute | solution.py:46
  336.2 63.3 %collective-permute-start.27 = (bf16[2,128,1024]{2,1,0:T(8,128)(2,1)}, bf16[2,128,1024]{2,1,0:T(8,128)(2,1)}, u32[]{:S(2)}, u32[]{:S(2)}) collective-permute-start(bf16[2,128,1024]{2,1,0:T(8,128)(2,1)} %get-tuple-element.107), channel_id=1, source_target_pairs={{0,26},{2,24},{4,30},{6,28},{8,2},{10,0},{12,6},{14,4},{16,10},{18... | collective-permute-start | bytes 1572872 | tf_op jit(solution)/shard_map/ppermute | solution.py:46
  347.5 52.0 %collective-permute-start.28 = (bf16[2,128,1024]{2,1,0:T(8,128)(2,1)}, bf16[2,128,1024]{2,1,0:T(8,128)(2,1)}, u32[]{:S(2)}, u32[]{:S(2)}) collective-permute-start(bf16[2,128,1024]{2,1,0:T(8,128)(2,1)} %get-tuple-element.108), channel_id=1, source_target_pairs={{0,28},{2,30},{4,24},{6,26},{8,4},{10,6},{12,0},{14,2},{16,12},{18... | collective-permute-start | bytes 1572872 | tf_op jit(solution)/shard_map/ppermute | solution.py:46
  369.0 35.7 %collective-permute-start.29 = (bf16[2,128,1024]{2,1,0:T(8,128)(2,1)}, bf16[2,128,1024]{2,1,0:T(8,128)(2,1)}, u32[]{:S(2)}, u32[]{:S(2)}) collective-permute-start(bf16[2,128,1024]{2,1,0:T(8,128)(2,1)} %get-tuple-element.109), channel_id=1, source_target_pairs={{0,30},{2,28},{4,26},{6,24},{8,6},{10,4},{12,2},{14,0},{16,14},{18... | collective-permute-start | bytes 1572872 | tf_op jit(solution)/shard_map/ppermute | solution.py:46
  398.0 136.1 %collective-permute-start.60 = (bf16[128,512]{1,0:T(8,128)(2,1)S(1)}, bf16[128,512]{1,0:T(8,128)(2,1)S(1)}, u32[]{:S(2)}, u32[]{:S(2)}) collective-permute-start(bf16[128,512]{1,0:T(8,128)(2,1)S(1)} %dynamic-slice_convert_fusion), channel_id=1, source_target_pairs={{0,1},{1,0},{2,3},{3,2},{4,5},{5,4},{6,7},{7,6},{8,9},{9,8},{10,11... | collective-permute-start | bytes 393224 | tf_op jit(solution)/shard_map/ppermute | solution.py:329
  405.8 128.3 %copy-start.14 = (f32[256,512]{1,0:T(8,128)S(1)}, f32[256,512]{1,0:T(8,128)}, u32[]{:S(2)}) copy-start(f32[256,512]{1,0:T(8,128)} %copy-done.13) | copy-start | bytes 1572868
  (13 other events, 109.6 us)

commit v2 on v1

--- a/solution.py
+++ b/solution.py
@@ -46,15 +46,33 @@
     return lax.ppermute(array, "group", pairs)
 
 
+def along(axis, step, dims):
+    return tuple(step if i == axis else 0 for i in range(len(dims)))
+
+
+def relay(array, axis, step, dims):
+    groups, size, stride = math.prod(dims), dims[axis], strides(dims)[axis]
+    pairs = [(s, s + step * stride) for s in range(groups) if 0 <= s // stride % size + step < size]
+    return lax.ppermute(array, "group", pairs)
+
+
 def gather_shards(shard, dims):
     held = {(0,) * len(dims): shard}
+    me = lax.axis_index("group")
     for axis, size in enumerate(dims):
+        digit = me // strides(dims)[axis] % size
         incoming = {}
-        for ahead in range(1, size):
-            step = tuple(ahead if i == axis else 0 for i in range(len(dims)))
-            for offset, array in held.items():
-                place = tuple(a + b for a, b in zip(offset, step))
-                incoming[place] = send_by(array, step, dims)
+        for offset, array in held.items():
+            if size == 2:
+                passed = {1: send_by(array, along(axis, 1, dims), dims)}
+            else:
+                up, down = [array], [array]
+                for _ in range(1, size):
+                    up.append(relay(up[-1], axis, 1, dims))
+                    down.append(relay(down[-1], axis, -1, dims))
+                passed = {k: jnp.where(digit >= k, up[k], down[size - k]) for k in range(1, size)}
+            for k, moved in passed.items():
+                incoming[tuple(a + b for a, b in zip(offset, along(axis, k, dims)))] = moved
         held.update(incoming)
     return held
 
@@ -70,70 +88,64 @@
     return rank
 
 
-def prepare_kernel(dims, offsets, lengths, prefill_of, decode_of, pool, received, *rest):
-    sends = rest[: len(offsets)]
-    zero_page, start_of, count_of, zero_sem, sems = rest[len(offsets) :]
+def prepare_kernel(groups, lengths, prefill_of, decode_of, pool, sends, held, zero_page, start_of, count_of, in_sems, out_sem):
     me = lax.axis_index("group")
-    page_size = pool.shape[1]
-    for d in range(math.prod(dims)):
+    page_total, page_size, _ = pool.shape
+    loads = [pltpu.make_async_copy(pool.at[p], held.at[p], in_sems.at[p]) for p in range(page_total)]
+    for load in loads:
+        load.start()
+    for d in range(groups + 1):
         start_of[d] = 0
         count_of[d] = 0
-    start_of[math.prod(dims)] = 0
-    count_of[math.prod(dims)] = 0
     zero_page[...] = jnp.zeros_like(zero_page)
 
     def visit(r, running):
         mine = prefill_of[r] == me
         count = (lengths[r] + page_size - 1) // page_size
-        place = jnp.where(mine, decode_of[r], math.prod(dims))
-        start_of[place] = running
-        count_of[place] = count
+        to = jnp.where(mine, decode_of[r], groups)
+        start_of[to] = running
+        count_of[to] = count
         return running + jnp.where(mine, count, 0)
 
     lax.fori_loop(0, lengths.shape[0], visit, jnp.int32(0), unroll=8)
-
-    def fill(target, page, start, count, sem):
-        @pl.when(page < count)
+    for load in loads:
+        load.wait()
+
+    def store(d, page, do):
+        target = sends.at[d, page]
+
+        @pl.when(page < count_of[d])
         def _():
-            pltpu.make_async_copy(pool.at[start + page], target, sem).start()
-
-        @pl.when(page >= count)
+            do(pltpu.make_async_copy(held.at[start_of[d] + page], target, out_sem))
+
+        @pl.when(page >= count_of[d])
         def _():
-            pltpu.make_async_copy(zero_page, target, sem).start()
-
-    own = start_of[me], count_of[me]
-    for page in range(MAX_PAGES):
-        fill(received.at[me * MAX_PAGES + page], page, *own, zero_sem.at[page])
-    for i, offset in enumerate(offsets):
-        to = shifted(me, offset, dims)
-        start, count = start_of[to], count_of[to]
+            do(pltpu.make_async_copy(zero_page, target, out_sem))
+
+    for d in range(groups):
         for page in range(MAX_PAGES):
-            fill(sends[i].at[page], page, start, count, sems.at[i, page])
-    for page in range(MAX_PAGES):
-        pltpu.make_async_copy(zero_page, received.at[page], zero_sem.at[page]).wait()
-    for i in range(len(offsets)):
+            store(d, page, lambda copy: copy.start())
+    for d in range(groups):
         for page in range(MAX_PAGES):
-            pltpu.make_async_copy(zero_page, sends[i].at[page], sems.at[i, page]).wait()
-
-
-def prepare(dims, offsets, lengths, prefill_of, decode_of, pool):
-    groups = math.prod(dims)
+            store(d, page, lambda copy: copy.wait())
+
+
+def prepare(groups, lengths, prefill_of, decode_of, pool):
     page = pool.shape[1:]
-    block = jax.ShapeDtypeStruct((MAX_PAGES,) + page, pool.dtype)
-    outs = [jax.ShapeDtypeStruct((groups * MAX_PAGES,) + page, pool.dtype)] + [block] * len(offsets)
     smem = pl.BlockSpec(memory_space=pltpu.SMEM)
     hbm = pl.BlockSpec(memory_space=pl.ANY)
     return pl.pallas_call(
-        functools.partial(prepare_kernel, dims, offsets),
-        out_shape=outs,
+        functools.partial(prepare_kernel, groups),
+        out_shape=jax.ShapeDtypeStruct((groups, MAX_PAGES) + page, pool.dtype),
         in_specs=[smem, smem, smem, hbm],
-        out_specs=[hbm] * len(outs),
+        out_specs=hbm,
         scratch_shapes=[
+            pltpu.VMEM(pool.shape, pool.dtype),
             pltpu.VMEM(page, pool.dtype),
             pltpu.SMEM((groups + 1,), jnp.int32),
             pltpu.SMEM((groups + 1,), jnp.int32),
-            pltpu.SemaphoreType.DMA((MAX_PAGES,)),
-            pltpu.SemaphoreType.DMA((len(offsets), MAX_PAGES)),
+            pltpu.SemaphoreType.DMA((pool.shape[0],)),
+            pltpu.SemaphoreType.DMA,
         ],
         compiler_params=pltpu.CompilerParams(vmem_limit_bytes=VMEM_LIMIT),
         cost_estimate=pl.CostEstimate(flops=0, bytes_accessed=4 * pool.size, transcendentals=0),
@@ -141,41 +153,41 @@
     )(lengths, prefill_of, decode_of, pool)
 
 
-def place_kernel(dims, offsets, received_in, *rest):
-    blocks = rest[: len(offsets)]
-    received, sems = rest[len(offsets) :]
-    me = lax.axis_index("group")
-    copies = []
-    for i, offset in enumerate(offsets):
-        source = shifted(me, tuple(-o for o in offset), dims)
-        copies.append(
-            pltpu.make_async_copy(
-                blocks[i], received.at[pl.ds(source * MAX_PAGES, MAX_PAGES)], sems.at[i]
-            )
-        )
-        copies[-1].start()
-    for copy in copies:
-        copy.wait()
-
-
-def place(dims, offsets, received, blocks):
+def hand_on_kernel(blocks, arrived, after, received, held, in_sems, out_sems):
+    step = arrived.shape[0] // blocks
+    loads, stores = [], []
+    for i in range(blocks):
+        part = pl.ds(i * step, step)
+        loads.append(pltpu.make_async_copy(arrived.at[part], held.at[part], in_sems.at[i]))
+        stores.append(pltpu.make_async_copy(held.at[part], received.at[part], out_sems.at[i]))
+        loads[-1].start()
+    for load, store in zip(loads, stores):
+        load.wait()
+        store.start()
+    for store in stores:
+        store.wait()
+
+
+def hand_on(arrived, after):
     hbm = pl.BlockSpec(memory_space=pl.ANY)
+    blocks = math.gcd(arrived.shape[0], 16)
     return pl.pallas_call(
-        functools.partial(place_kernel, dims, offsets),
-        out_shape=jax.ShapeDtypeStruct(received.shape, received.dtype),
-        in_specs=[hbm] * (1 + len(blocks)),
+        functools.partial(hand_on_kernel, blocks),
+        out_shape=jax.ShapeDtypeStruct(arrived.shape, arrived.dtype),
+        in_specs=[hbm, hbm],
         out_specs=hbm,
-        scratch_shapes=[pltpu.SemaphoreType.DMA((len(blocks),))],
-        input_output_aliases={0: 0},
+        scratch_shapes=[
+            pltpu.VMEM(arrived.shape, arrived.dtype),
+            pltpu.SemaphoreType.DMA((blocks,)),
+            pltpu.SemaphoreType.DMA((blocks,)),
+        ],
         compiler_params=pltpu.CompilerParams(vmem_limit_bytes=VMEM_LIMIT),
-        cost_estimate=pl.CostEstimate(
-            flops=0, bytes_accessed=4 * sum(b.size for b in blocks), transcendentals=0
-        ),
+        cost_estimate=pl.CostEstimate(flops=0, bytes_accessed=4 * arrived.size, transcendentals=0),
         name="place_pages",
-    )(received, *blocks)
-
-
-def attend_kernel(dims, offsets, lengths, prefill_of, row_request, pool, *rest):
+    )(arrived, after)
+
+
+def attend_kernel(dims, offsets, lengths, prefill_of, row_request, pool, after, *rest):
     shards = rest[: len(offsets)]
     out, queries, start_of, mine_rows, sems = rest[len(offsets) :]
     me = lax.axis_index("group")
@@ -251,7 +263,7 @@
             out[step * ROW_UNROLL + i] = one_row(step * ROW_UNROLL + i)
 
 
-def attend(dims, shards, lengths, prefill_of, row_request, pool):
+def attend(dims, shards, lengths, prefill_of, row_request, pool, after):
     offsets = list(shards)
     row_local, query_heads, _ = shards[offsets[0]].shape
     row_total = row_request.shape[0]
@@ -261,7 +273,7 @@
     return pl.pallas_call(
         functools.partial(attend_kernel, dims, offsets),
         out_shape=jax.ShapeDtypeStruct((row_total + ROW_UNROLL, query_heads, HD), jnp.bfloat16),
-        in_specs=[smem, smem, smem, vmem] + [hbm] * len(offsets),
+        in_specs=[smem, smem, smem, vmem, hbm] + [hbm] * len(offsets),
         out_specs=vmem,
         scratch_shapes=[
             pltpu.VMEM((len(offsets), row_local, query_heads, HD), jnp.bfloat16),
@@ -274,7 +286,20 @@
             flops=1 << 33, bytes_accessed=2 * pool.size, transcendentals=1 << 20
         ),
         name="attend_local_rows",
-    )(lengths, prefill_of, row_request, pool, *(shards[o] for o in offsets))
+    )(lengths, prefill_of, row_request, pool, after, *(shards[o] for o in offsets))
+
+
+def project(attended, out_weight):
+    product = jnp.dot(attended, out_weight, preferred_element_type=jnp.float32)
+    heads = lax.axis_size("head")
+    my_head = lax.axis_index("head")
+    share = attended.shape[0] // heads
+    output = lax.dynamic_slice_in_dim(product, my_head * share, share)
+    for ahead in range(1, heads):
+        theirs = lax.dynamic_slice_in_dim(product, lax.rem(my_head + ahead, heads) * share, share)
+        pairs = [(h, (h + ahead) % heads) for h in range(heads)]
+        output = output + lax.ppermute(theirs.astype(jnp.bfloat16), "head", pairs).astype(jnp.float32)
+    return output.astype(jnp.bfloat16)
 
 
 def local(dims, kv_pool, lengths, prefill_of, decode_of, row_request, queries, out_weight):
@@ -282,15 +307,12 @@
     me = lax.axis_index("group")
     row_local, query_width = queries.shape
     row_total = row_request.shape[0]
-    query_heads = query_width // HD
-    offsets = [o for o in itertools.product(*(range(n) for n in dims)) if any(o)]
-
-    received, *sends = prepare(dims, offsets, lengths, prefill_of, decode_of, kv_pool)
-    arrived = [send_by(block, offset, dims) for block, offset in zip(sends, offsets)]
-
-    shards = gather_shards(queries.reshape(row_local, query_heads, HD), dims)
-    rows = attend(dims, shards, lengths, prefill_of, row_request, kv_pool)
-    rows = rows.reshape(rows.shape[0], query_width)
+
+    outgoing = prepare(groups, lengths, prefill_of, decode_of, kv_pool)
+    incoming = lax.all_to_all(outgoing, "group", split_axis=0, concat_axis=0, tiled=True)
+
+    shards = gather_shards(queries.reshape(row_local, query_width // HD, HD), dims)
+    rows = attend(dims, shards, lengths, prefill_of, row_request, kv_pool, outgoing)
 
     row_home = prefill_of[row_request]
     ordinal = jnp.arange(row_total, dtype=jnp.int32)
@@ -299,7 +321,8 @@
     home_slot = behind_rank(me, row_home, dims) * CAPACITY
 
     def gather_round(done):
-        gathered = gather_shards(lax.dynamic_slice_in_dim(rows, done, CAPACITY), dims)
+        part = lax.dynamic_slice_in_dim(rows, done, CAPACITY).reshape(CAPACITY, query_width)
+        gathered = gather_shards(part, dims)
         stacked = jnp.concatenate(
             [gathered[o] for o in sorted(gathered, key=lambda o: offset_rank(o, dims))], axis=0
         )
@@ -312,24 +335,19 @@
 
     most = jnp.max(row_rank) + 1
     attended = gather_round(jnp.int32(0))
-    _, attended = lax.while_loop(
-        lambda state: state[0] < most,
-        lambda state: (state[0] + CAPACITY, state[1] + gather_round(state[0])),
-        (jnp.int32(CAPACITY), attended),
-    )
-    product = jnp.dot(attended, out_weight, preferred_element_type=jnp.float32)
-
-    heads = lax.axis_size("head")
-    my_head = lax.axis_index("head")
-    share = row_total // heads
-    output = lax.dynamic_slice_in_dim(product, my_head * share, share)
-    for ahead in range(1, heads):
-        theirs = lax.dynamic_slice_in_dim(product, lax.rem(my_head + ahead, heads) * share, share)
-        pairs = [(h, (h + ahead) % heads) for h in range(heads)]
-        output = output + lax.ppermute(theirs.astype(jnp.bfloat16), "head", pairs).astype(jnp.float32)
-
-    received = place(dims, offsets, received, arrived)
-    return (received, output.astype(jnp.bfloat16))
+    output = project(attended, out_weight)
+
+    def further_rounds(attended, output):
+        _, attended = lax.while_loop(
+            lambda state: state[0] < most,
+            lambda state: (state[0] + CAPACITY, state[1] + gather_round(state[0])),
+            (jnp.int32(CAPACITY), attended),
+        )
+        return project(attended, out_weight)
+
+    received = hand_on(incoming.reshape((groups * MAX_PAGES,) + kv_pool.shape[1:]), output)
+    output = lax.cond(most > CAPACITY, further_rounds, lambda attended, output: output, attended, output)
+    return (received, output)
 
 
 def solution(mesh):

time: 541 us -> 334 us (0.62); the launches traced: 535 us -> 334 us
  Pallas kernels: 251 us -> 29.7 us
  waiting for transfers between devices: 122 us -> 183 us
  starting transfers between devices: 138 us -> 102 us
    pallas_call x2, Pallas kernels: 236 us -> 14 us  [the longest x1 7.47 us: prepare(): pl.pallas_call(functools.partial(prepare_kernel, groups), out_shape=jax.S...]
    ppermute x1 -> x13, waiting for transfers between devices: 0.01 us -> 166 us  [the longest x12 162 us: relay(): return lax.ppermute(array, 'group', pairs)]
    ppermute x45 -> x24, starting transfers between devices: 136 us -> 9.78 us  [send_by(): return lax.ppermute(array, 'group', pairs)]
    ppermute x45 -> x24, waiting for transfers between devices: 122 us -> 16.4 us  [send_by(): return lax.ppermute(array, 'group', pairs)]
    ppermute x1 -> x13, starting transfers between devices: 1.5 us -> 84.9 us  [the longest x12 83.4 us: relay(): return lax.ppermute(array, 'group', pairs)]
    all_to_all x0 -> x1, starting transfers between devices: none -> 7.58 us  [local(): lax.all_to_all(outgoing, 'group', split_axis=0, concat_axis=0, tiled=True)]
    unnamed x49 -> x34, local copies, waits for them, and re-layouts: 12.6 us -> 7.13 us
  transfers between devices with their start and end apart: 46 -> 38, of which waited for: 19 -> 20; matrix products, arithmetic and copies ran while one was open for 2% -> 4% of each run, Pallas kernels for 44% -> 5%
where the time goes in v2:
time: 334 us
  waiting for transfers between devices  183 us (55%)
  starting transfers between devices  102 us (31%)
  Pallas kernels  29.7 us (9%)
  local copies, waits for them, and re-layouts  10.5 us (3%)
  matrix products  4.87 us (1%)
    ppermute x12, waiting for transfers between devices, relay(): return lax.ppermute(array, 'group', pairs)  162 us
    ppermute x12, starting transfers between devices, relay(): return lax.ppermute(array, 'group', pairs)  83.4 us
    ppermute x24, waiting for transfers between devices, send_by(): return lax.ppermute(array, 'group', pairs)  16.4 us
    pallas_call x1, Pallas kernels, attend(): pl.pallas_call(functools.partial(attend_kernel, dims, offsets), out_shape...  15.7 us
    ppermute x24, starting transfers between devices, send_by(): return lax.ppermute(array, 'group', pairs)  9.78 us
    all_to_all x1, starting transfers between devices, local(): lax.all_to_all(outgoing, 'group', split_axis=0, concat_axis=0, tiled=True)  7.58 us
    pallas_call x1, Pallas kernels, prepare(): pl.pallas_call(functools.partial(prepare_kernel, groups), out_shape=jax.S...  7.47 us
    unnamed x34, local copies, waits for them, and re-layouts  7.13 us
  transfers between devices with their start and end apart: 38, of which 20 were waited for; matrix products, arithmetic and copies ran while one was open for 4% of the time, Pallas kernels for 5%

profile of v2, /device:TPU:0, one launch (start us, length us, event | category | flops | bytes accessed | tf_op | source)
XLA Modules:
  0.0 333.8 jit_solution(3728307768641817397)
XLA Ops:
  2.7 7.5 %outgoing_pages.1.after = bf16[16,2,128,1024]{3,2,1,0:T(8,128)(2,1)} custom-call(s32[256]{0:T(256)S(1)} %copy-done.3, s32[256]{0:T(256)S(1)} %copy-done, s32[256]{0:T(256)S(1)} %copy-done.2, bf16[32,128,1024]{2,1,0:T(8,128)(2,1)} %pool.3), custom_call_target="tpu_custom_call" | custom-call | bytes 16777216 | tf_op jit(solution)/shard_map/outgoing_pages/pallas_call | solution.py:137
  10.2 7.6 %all-to-all-start = ((bf16[16,2,128,1024]{3,2,1,0:T(8,128)(2,1)}), bf16[16,2,128,1024]{3,2,1,0:T(8,128)(2,1)}, u32[]{:S(2)}, u32[]{:S(2)}) async-start(bf16[16,2,128,1024]{3,2,1,0:T(8,128)(2,1)} %outgoing_pages.1.after), calls=%async_computation | async-start | bytes 16777216 | tf_op jit(solution)/shard_map/all_to_all | solution.py:312
  17.8 1.3 collective-permute-start.20
  19.1 4.6 %collective-permute-start.19 = (bf16[16,32,128]{2,1,0:T(8,128)(2,1)S(1)}, bf16[16,32,128]{2,1,0:T(8,128)(2,1)S(1)}, u32[]{:S(2)}, u32[]{:S(2)}) collective-permute-start(bf16[16,32,128]{2,1,0:T(8,128)(2,1)S(1)} %bitcast.34), channel_id=1, source_target_pairs={{0,8},{2,10},{4,12},{6,14},{8,16},{10,18},{12,20},{14,22},{16,24},... | collective-permute-start | bytes 393224 | tf_op jit(solution)/shard_map/ppermute | solution.py:56
  23.7 1.9 collective-permute-start.25
  25.6 110.4 %collective-permute-done.20 = bf16[16,32,128]{2,1,0:T(8,128)(2,1)S(1)} collective-permute-done((bf16[16,32,128]{2,1,0:T(8,128)(2,1)S(1)}, bf16[16,32,128]{2,1,0:T(8,128)(2,1)S(1)}, u32[]{:S(2)}, u32[]{:S(2)}) %collective-permute-start.20) | collective-permute-done | bytes 131104 | tf_op jit(solution)/shard_map/ppermute | solution.py:56
  136.1 1.3 collective-permute-start.21
  137.4 19.2 %collective-permute-done.19 = bf16[16,32,128]{2,1,0:T(8,128)(2,1)S(1)} collective-permute-done((bf16[16,32,128]{2,1,0:T(8,128)(2,1)S(1)}, bf16[16,32,128]{2,1,0:T(8,128)(2,1)S(1)}, u32[]{:S(2)}, u32[]{:S(2)}) %collective-permute-start.19) | collective-permute-done | bytes 131104 | tf_op jit(solution)/shard_map/ppermute | solution.py:56
  156.6 52.3 %collective-permute-start.23 = (bf16[16,32,128]{2,1,0:T(8,128)(2,1)S(1)}, bf16[16,32,128]{2,1,0:T(8,128)(2,1)S(1)}, u32[]{:S(2)}, u32[]{:S(2)}) collective-permute-start(bf16[16,32,128]{2,1,0:T(8,128)(2,1)S(1)} %collective-permute-done.19), channel_id=1, source_target_pairs={{0,8},{2,10},{4,12},{6,14},{8,16},{10,18},{12,20},{14,22},{16,24},... | collective-permute-start | bytes 393224 | tf_op jit(solution)/shard_map/ppermute | solution.py:56
  209.5 0.8 collective-permute-done.21
  210.2 1.3 collective-permute-start.22
  211.6 1.6 collective-permute-start.27
  213.1 4.0 %collective-permute-done.22 = bf16[16,32,128]{2,1,0:T(8,128)(2,1)S(1)} collective-permute-done((bf16[16,32,128]{2,1,0:T(8,128)(2,1)S(1)}, bf16[16,32,128]{2,1,0:T(8,128)(2,1)S(1)}, u32[]{:S(2)}, u32[]{:S(2)}) %collective-permute-start.22) | collective-permute-done | bytes 131104 | tf_op jit(solution)/shard_map/ppermute | solution.py:56
  217.2 3.6 %collective-permute-start.24 = (bf16[16,32,128]{2,1,0:T(8,128)(2,1)S(1)}, bf16[16,32,128]{2,1,0:T(8,128)(2,1)S(1)}, u32[]{:S(2)}, u32[]{:S(2)}) collective-permute-start(bf16[16,32,128]{2,1,0:T(8,128)(2,1)S(1)} %collective-permute-done.23), channel_id=1, source_target_pairs={{0,8},{2,10},{4,12},{6,14},{8,16},{10,18},{12,20},{14,22},{16,24},... | collective-permute-start | bytes 393224 | tf_op jit(solution)/shard_map/ppermute | solution.py:56
  220.8 2.5 collective-permute-done.24
  223.3 1.5 collective-permute-start.26
  226.0 2.3 collective-permute-done.26.rest_5_
  228.3 1.6 collective-permute-done.28.rest_7_
  229.9 1.3 collective-permute-done.36.rest_15_
  231.2 15.7 %attend_local_rows.1 = bf16[260,32,128]{2,1,0:T(8,128)(2,1)S(1)} custom-call(s32[256]{0:T(256)S(1)} %copy-done.4, s32[256]{0:T(256)S(1)} %copy-done.1, s32[256]{0:T(256)S(1)} %copy-done.5, bf16[32,128,1024]{2,1,0:T(8,128)(2,1)} %pool.3, bf16[16,2,128,1024]{3,2,1,0:T(8,128)(2,1)} %outgoing_pages.1.after, bf16[16,32,128]{2,1,0:T(8,128)(2,1)S(1)} %bitcast.37, ...), custom_call_target="tpu_custom_call" | custom-call | flops 8589934592 | bytes 8388608 | tf_op jit(solution)/shard_map/attend_local_rows/pallas_call | solution.py:273
  247.2 1.3 collective-permute-start.41
  248.6 7.6 %collective-permute-start.40 = (bf16[32,4096]{1,0:T(8,128)(2,1)S(1)}, bf16[32,4096]{1,0:T(8,128)(2,1)S(1)}, u32[]{:S(2)}, u32[]{:S(2)}) collective-permute-start(bf16[32,4096]{1,0:T(8,128)(2,1)S(1)} %bitcast.49), channel_id=1, source_target_pairs={{0,8},{2,10},{4,12},{6,14},{8,16},{10,18},{12,20},{14,22},{16,24},... | collective-permute-start | bytes 786440 | tf_op jit(solution)/shard_map/ppermute | solution.py:56
  256.3 4.4 %collective-permute-done.41 = bf16[32,4096]{1,0:T(8,128)(2,1)S(1)} collective-permute-done((bf16[32,4096]{1,0:T(8,128)(2,1)S(1)}, bf16[32,4096]{1,0:T(8,128)(2,1)S(1)}, u32[]{:S(2)}, u32[]{:S(2)}) %collective-permute-start.41) | collective-permute-done | bytes 262176 | tf_op jit(solution)/shard_map/ppermute | solution.py:56
  260.8 1.3 collective-permute-start.42
  262.1 8.3 %collective-permute-done.42 = bf16[32,4096]{1,0:T(8,128)(2,1)S(1)} collective-permute-done((bf16[32,4096]{1,0:T(8,128)(2,1)S(1)}, bf16[32,4096]{1,0:T(8,128)(2,1)S(1)}, u32[]{:S(2)}, u32[]{:S(2)}) %collective-permute-start.42) | collective-permute-done | bytes 262176 | tf_op jit(solution)/shard_map/ppermute | solution.py:56
  270.4 1.3 collective-permute-start.43
  271.8 7.4 %collective-permute-done.43 = bf16[32,4096]{1,0:T(8,128)(2,1)S(1)} collective-permute-done((bf16[32,4096]{1,0:T(8,128)(2,1)S(1)}, bf16[32,4096]{1,0:T(8,128)(2,1)S(1)}, u32[]{:S(2)}, u32[]{:S(2)}) %collective-permute-start.43) | collective-permute-done | bytes 262176 | tf_op jit(solution)/shard_map/ppermute | solution.py:56
  279.3 1.1 collective-permute-start.45
  280.4 3.2 collective-permute-start.47
  283.6 2.1 collective-permute-done.45
  285.8 1.5 collective-permute-done.46
  287.3 2.5 collective-permute-done.47
  289.9 0.9 collective-permute-start.49
  290.8 1.1 copy-done.9
  291.9 1.9 gather_fusion
  293.9 4.4 %collective-permute-start.51 = (bf16[32,4096]{1,0:T(8,128)(2,1)S(1)}, bf16[32,4096]{1,0:T(8,128)(2,1)S(1)}, u32[]{:S(2)}, u32[]{:S(2)}) collective-permute-start(bf16[32,4096]{1,0:T(8,128)(2,1)S(1)} %collective-permute-done.47), channel_id=1, source_target_pairs={{0,8},{2,10},{4,12},{6,14},{8,16},{10,18},{12,20},{14,22},{16,24},... | collective-permute-start | bytes 786440 | tf_op jit(solution)/shard_map/ppermute | solution.py:56
  300.2 0.7 constant_dynamic-update-slice_fusion.20
  300.9 2.8 collective-permute-done.51
  303.7 0.8 constant_dynamic-update-slice_fusion.19
  304.5 0.8 collective-permute-start.53
  306.1 7.1 %collective-permute-done.53 = bf16[32,4096]{1,0:T(8,128)(2,1)S(1)} collective-permute-done((bf16[32,4096]{1,0:T(8,128)(2,1)S(1)}, bf16[32,4096]{1,0:T(8,128)(2,1)S(1)}, u32[]{:S(2)}, u32[]{:S(2)}) %collective-permute-start.53) | collective-permute-done | bytes 262176 | tf_op jit(solution)/shard_map/ppermute | solution.py:46
  313.2 0.7 constant_dynamic-update-slice_fusion.18
  313.9 0.7 constant_dynamic-update-slice_fusion.17
  315.5 3.6 %convolution_convert_fusion.1 = bf16[256,4096]{1,0:T(8,128)(2,1)S(1)} fusion(bf16[512,4096]{1,0:T(8,128)(2,1)} %constant_dynamic-update-slice_fusion.16, s32[256]{0:T(256)S(1)} %get-tuple-element.178), kind=kOutput, calls=%fused_computation.38 | convolution fusion | flops 1074921472 | bytes 6292480 | tf_op jit(solution)/shard_map/dot_general | solution.py:332
  319.1 1.2 fusion.27
  320.4 1.6 collective-permute-start.55
  322.6 3.7 %collective-permute-done.55 = bf16[128,512]{1,0:T(8,128)(2,1)S(1)} collective-permute-done((bf16[128,512]{1,0:T(8,128)(2,1)S(1)}, bf16[128,512]{1,0:T(8,128)(2,1)S(1)}, u32[]{:S(2)}, u32[]{:S(2)}) %collective-permute-start.55) | collective-permute-done | bytes 131104 | tf_op jit(solution)/shard_map/ppermute | solution.py:301
  327.0 6.6 %place_pages.1 = bf16[32,128,1024]{2,1,0:T(8,128)(2,1)} custom-call(bf16[32,128,1024]{2,1,0:T(8,128)(2,1)} %bitcast.2.arrived, bf16[128,512]{1,0:T(8,128)(2,1)S(1)} %add_convert_fusion.1.after), custom_call_target="tpu_custom_call" | custom-call | bytes 16777216 | tf_op jit(solution)/shard_map/place_pages/pallas_call | solution.py:174
  (87 shorter events, 9.5 us)
Async XLA Ops:
  0.6 0.7 copy-start
  1.3 0.7 copy-start.2
  2.0 0.7 copy-start.3
  10.2 7.6 %copy-start.8 = (bf16[16,4096]{1,0:T(8,128)(2,1)S(1)}, bf16[16,4096]{1,0:T(8,128)(2,1)}, u32[]{:S(2)}) copy-start(bf16[16,4096]{1,0:T(8,128)(2,1)} %param.16) | copy-start | bytes 393220
  10.2 221.1 %copy-start.1 = (s32[256]{0:T(256)S(1)}, s32[256]{0:T(256)}, u32[]{:S(2)}) copy-start(s32[256]{0:T(256)} %prefill_of.3) | copy-start | bytes 3076
  10.2 221.0 %copy-start.4 = (s32[256]{0:T(256)S(1)}, s32[256]{0:T(256)}, u32[]{:S(2)}) copy-start(s32[256]{0:T(256)} %lengths.3) | copy-start | bytes 3076
  10.2 221.0 %copy-start.5 = (s32[256]{0:T(256)S(1)}, s32[256]{0:T(256)}, u32[]{:S(2)}) copy-start(s32[256]{0:T(256)} %row_request.1) | copy-start | bytes 3076
  10.2 316.8 %all-to-all-start = ((bf16[16,2,128,1024]{3,2,1,0:T(8,128)(2,1)}), bf16[16,2,128,1024]{3,2,1,0:T(8,128)(2,1)}, u32[]{:S(2)}, u32[]{:S(2)}) async-start(bf16[16,2,128,1024]{3,2,1,0:T(8,128)(2,1)} %outgoing_pages.1.after), calls=%async_computation | async-start | bytes 16777216 | tf_op jit(solution)/shard_map/all_to_all | solution.py:312
  17.8 118.2 %collective-permute-start.20 = (bf16[16,32,128]{2,1,0:T(8,128)(2,1)S(1)}, bf16[16,32,128]{2,1,0:T(8,128)(2,1)S(1)}, u32[]{:S(2)}, u32[]{:S(2)}) collective-permute-start(bf16[16,32,128]{2,1,0:T(8,128)(2,1)S(1)} %bitcast.33), channel_id=1, source_target_pairs={{8,0},{10,2},{12,4},{14,6},{16,8},{18,10},{20,12},{22,14},{24,16},... | collective-permute-start | bytes 393224 | tf_op jit(solution)/shard_map/ppermute | solution.py:56
  19.1 137.5 %collective-permute-start.19 = (bf16[16,32,128]{2,1,0:T(8,128)(2,1)S(1)}, bf16[16,32,128]{2,1,0:T(8,128)(2,1)S(1)}, u32[]{:S(2)}, u32[]{:S(2)}) collective-permute-start(bf16[16,32,128]{2,1,0:T(8,128)(2,1)S(1)} %bitcast.34), channel_id=1, source_target_pairs={{0,8},{2,10},{4,12},{6,14},{8,16},{10,18},{12,20},{14,22},{16,24},... | collective-permute-start | bytes 393224 | tf_op jit(solution)/shard_map/ppermute | solution.py:56
  23.7 185.3 %collective-permute-start.25 = (bf16[16,32,128]{2,1,0:T(8,128)(2,1)S(1)}, bf16[16,32,128]{2,1,0:T(8,128)(2,1)S(1)}, u32[]{:S(2)}, u32[]{:S(2)}) collective-permute-start(bf16[16,32,128]{2,1,0:T(8,128)(2,1)S(1)} %bitcast.35), channel_id=1, source_target_pairs={{0,4},{2,6},{4,0},{6,2},{8,12},{10,14},{12,8},{14,10},{16,20},{18,... | collective-permute-start | bytes 393224 | tf_op jit(solution)/shard_map/ppermute | solution.py:46
  136.1 74.2 %collective-permute-start.21 = (bf16[16,32,128]{2,1,0:T(8,128)(2,1)S(1)}, bf16[16,32,128]{2,1,0:T(8,128)(2,1)S(1)}, u32[]{:S(2)}, u32[]{:S(2)}) collective-permute-start(bf16[16,32,128]{2,1,0:T(8,128)(2,1)S(1)} %collective-permute-done.20), channel_id=1, source_target_pairs={{8,0},{10,2},{12,4},{14,6},{16,8},{18,10},{20,12},{22,14},{24,16},... | collective-permute-start | bytes 393224 | tf_op jit(solution)/shard_map/ppermute | solution.py:56
  156.6 54.9 %collective-permute-start.23 = (bf16[16,32,128]{2,1,0:T(8,128)(2,1)S(1)}, bf16[16,32,128]{2,1,0:T(8,128)(2,1)S(1)}, u32[]{:S(2)}, u32[]{:S(2)}) collective-permute-start(bf16[16,32,128]{2,1,0:T(8,128)(2,1)S(1)} %collective-permute-done.19), channel_id=1, source_target_pairs={{0,8},{2,10},{4,12},{6,14},{8,16},{10,18},{12,20},{14,22},{16,24},... | collective-permute-start | bytes 393224 | tf_op jit(solution)/shard_map/ppermute | solution.py:56
  208.9 15.9 %collective-permute-start.29 = (bf16[16,32,128]{2,1,0:T(8,128)(2,1)S(1)}, bf16[16,32,128]{2,1,0:T(8,128)(2,1)S(1)}, u32[]{:S(2)}, u32[]{:S(2)}) collective-permute-start(bf16[16,32,128]{2,1,0:T(8,128)(2,1)S(1)} %bitcast.36), channel_id=1, source_target_pairs={{0,2},{2,0},{4,6},{6,4},{8,10},{10,8},{12,14},{14,12},{16,18},{18,... | collective-permute-start | bytes 393224 | tf_op jit(solution)/shard_map/ppermute | solution.py:46
  209.0 16.4 %collective-permute-start.33 = (bf16[16,32,128]{2,1,0:T(8,128)(2,1)S(1)}, bf16[16,32,128]{2,1,0:T(8,128)(2,1)S(1)}, u32[]{:S(2)}, u32[]{:S(2)}) collective-permute-start(bf16[16,32,128]{2,1,0:T(8,128)(2,1)S(1)} %collective-permute-done.25.rest_4_), channel_id=1, source_target_pairs={{0,2},{2,0},{4,6},{6,4},{8,10},{10,8},{12,14},{14,12},{16,18},{18,... | collective-permute-start | bytes 393224 | tf_op jit(solution)/shard_map/ppermute | solution.py:46
  210.2 6.9 %collective-permute-start.22 = (bf16[16,32,128]{2,1,0:T(8,128)(2,1)S(1)}, bf16[16,32,128]{2,1,0:T(8,128)(2,1)S(1)}, u32[]{:S(2)}, u32[]{:S(2)}) collective-permute-start(bf16[16,32,128]{2,1,0:T(8,128)(2,1)S(1)} %collective-permute-done.21), channel_id=1, source_target_pairs={{8,0},{10,2},{12,4},{14,6},{16,8},{18,10},{20,12},{22,14},{24,16},... | collective-permute-start | bytes 393224 | tf_op jit(solution)/shard_map/ppermute | solution.py:56
  211.6 13.9 %collective-permute-start.27 = (bf16[16,32,128]{2,1,0:T(8,128)(2,1)S(1)}, bf16[16,32,128]{2,1,0:T(8,128)(2,1)S(1)}, u32[]{:S(2)}, u32[]{:S(2)}) collective-permute-start(bf16[16,32,128]{2,1,0:T(8,128)(2,1)S(1)} %broadcast_select_fusion.7.rest_2_), channel_id=1, source_target_pairs={{0,4},{2,6},{4,0},{6,2},{8,12},{10,14},{12,8},{14,10},{16,20},{18,... | collective-permute-start | bytes 393224 | tf_op jit(solution)/shard_map/ppermute | solution.py:46
  213.1 12.8 %collective-permute-start.31 = (bf16[16,32,128]{2,1,0:T(8,128)(2,1)S(1)}, bf16[16,32,128]{2,1,0:T(8,128)(2,1)S(1)}, u32[]{:S(2)}, u32[]{:S(2)}) collective-permute-start(bf16[16,32,128]{2,1,0:T(8,128)(2,1)S(1)} %broadcast_select_fusion.7.rest_2_), channel_id=1, source_target_pairs={{0,2},{2,0},{4,6},{6,4},{8,10},{10,8},{12,14},{14,12},{16,18},{18,... | collective-permute-start | bytes 393224 | tf_op jit(solution)/shard_map/ppermute | solution.py:46
  217.2 6.1 %collective-permute-start.24 = (bf16[16,32,128]{2,1,0:T(8,128)(2,1)S(1)}, bf16[16,32,128]{2,1,0:T(8,128)(2,1)S(1)}, u32[]{:S(2)}, u32[]{:S(2)}) collective-permute-start(bf16[16,32,128]{2,1,0:T(8,128)(2,1)S(1)} %collective-permute-done.23), channel_id=1, source_target_pairs={{0,8},{2,10},{4,12},{6,14},{8,16},{10,18},{12,20},{14,22},{16,24},... | collective-permute-start | bytes 393224 | tf_op jit(solution)/shard_map/ppermute | solution.py:56
  223.3 5.0 %collective-permute-start.26 = (bf16[16,32,128]{2,1,0:T(8,128)(2,1)S(1)}, bf16[16,32,128]{2,1,0:T(8,128)(2,1)S(1)}, u32[]{:S(2)}, u32[]{:S(2)}) collective-permute-start(bf16[16,32,128]{2,1,0:T(8,128)(2,1)S(1)} %broadcast_select_fusion.8.rest_1_), channel_id=1, source_target_pairs={{0,4},{2,6},{4,0},{6,2},{8,12},{10,14},{12,8},{14,10},{16,20},{18,... | collective-permute-start | bytes 393224 | tf_op jit(solution)/shard_map/ppermute | solution.py:46
  224.8 5.0 %collective-permute-start.28 = (bf16[16,32,128]{2,1,0:T(8,128)(2,1)S(1)}, bf16[16,32,128]{2,1,0:T(8,128)(2,1)S(1)}, u32[]{:S(2)}, u32[]{:S(2)}) collective-permute-start(bf16[16,32,128]{2,1,0:T(8,128)(2,1)S(1)} %broadcast_select_fusion.6.rest_3_), channel_id=1, source_target_pairs={{0,4},{2,6},{4,0},{6,2},{8,12},{10,14},{12,8},{14,10},{16,20},{18,... | collective-permute-start | bytes 393224 | tf_op jit(solution)/shard_map/ppermute | solution.py:46
  225.4 4.5 %collective-permute-start.30 = (bf16[16,32,128]{2,1,0:T(8,128)(2,1)S(1)}, bf16[16,32,128]{2,1,0:T(8,128)(2,1)S(1)}, u32[]{:S(2)}, u32[]{:S(2)}) collective-permute-start(bf16[16,32,128]{2,1,0:T(8,128)(2,1)S(1)} %broadcast_select_fusion.8.rest_1_), channel_id=1, source_target_pairs={{0,2},{2,0},{4,6},{6,4},{8,10},{10,8},{12,14},{14,12},{16,18},{18,... | collective-permute-start | bytes 393224 | tf_op jit(solution)/shard_map/ppermute | solution.py:46
  225.4 4.5 %collective-permute-start.32 = (bf16[16,32,128]{2,1,0:T(8,128)(2,1)S(1)}, bf16[16,32,128]{2,1,0:T(8,128)(2,1)S(1)}, u32[]{:S(2)}, u32[]{:S(2)}) collective-permute-start(bf16[16,32,128]{2,1,0:T(8,128)(2,1)S(1)} %broadcast_select_fusion.6.rest_3_), channel_id=1, source_target_pairs={{0,2},{2,0},{4,6},{6,4},{8,10},{10,8},{12,14},{14,12},{16,18},{18,... | collective-permute-start | bytes 393224 | tf_op jit(solution)/shard_map/ppermute | solution.py:46
  225.9 3.9 %collective-permute-start.35 = (bf16[16,32,128]{2,1,0:T(8,128)(2,1)S(1)}, bf16[16,32,128]{2,1,0:T(8,128)(2,1)S(1)}, u32[]{:S(2)}, u32[]{:S(2)}) collective-permute-start(bf16[16,32,128]{2,1,0:T(8,128)(2,1)S(1)} %collective-permute-done.27.rest_6_), channel_id=1, source_target_pairs={{0,2},{2,0},{4,6},{6,4},{8,10},{10,8},{12,14},{14,12},{16,18},{18,... | collective-permute-start | bytes 393224 | tf_op jit(solution)/shard_map/ppermute | solution.py:46
  228.3 1.6 collective-permute-start.34
  229.9 1.3 collective-permute-start.36
  246.9 33.5 %copy-start.7 = (bf16[260,32,128]{2,1,0:T(8,128)(2,1)}, bf16[260,32,128]{2,1,0:T(8,128)(2,1)S(1)}, u32[]{:S(2)}) copy-start(bf16[260,32,128]{2,1,0:T(8,128)(2,1)S(1)} %attend_local_rows.1) | copy-start | bytes 6389764
  247.1 15.0 %collective-permute-start.37 = (bf16[32,4096]{1,0:T(8,128)(2,1)S(1)}, bf16[32,4096]{1,0:T(8,128)(2,1)S(1)}, u32[]{:S(2)}, u32[]{:S(2)}) collective-permute-start(bf16[32,4096]{1,0:T(8,128)(2,1)S(1)} %bitcast.46), channel_id=1, source_target_pairs={{0,2},{2,0},{4,6},{6,4},{8,10},{10,8},{12,14},{14,12},{16,18},{18,... | collective-permute-start | bytes 786440 | tf_op jit(solution)/shard_map/ppermute | solution.py:46
  247.1 9.1 %collective-permute-start.38 = (bf16[32,4096]{1,0:T(8,128)(2,1)S(1)}, bf16[32,4096]{1,0:T(8,128)(2,1)S(1)}, u32[]{:S(2)}, u32[]{:S(2)}) collective-permute-start(bf16[32,4096]{1,0:T(8,128)(2,1)S(1)} %bitcast.47), channel_id=1, source_target_pairs={{0,4},{2,6},{4,0},{6,2},{8,12},{10,14},{12,8},{14,10},{16,20},{18,... | collective-permute-start | bytes 786440 | tf_op jit(solution)/shard_map/ppermute | solution.py:46
  247.2 13.5 %collective-permute-start.41 = (bf16[32,4096]{1,0:T(8,128)(2,1)S(1)}, bf16[32,4096]{1,0:T(8,128)(2,1)S(1)}, u32[]{:S(2)}, u32[]{:S(2)}) collective-permute-start(bf16[32,4096]{1,0:T(8,128)(2,1)S(1)} %bitcast.48), channel_id=1, source_target_pairs={{8,0},{10,2},{12,4},{14,6},{16,8},{18,10},{20,12},{22,14},{24,16},... | collective-permute-start | bytes 786440 | tf_op jit(solution)/shard_map/ppermute | solution.py:56
  248.6 23.1 %collective-permute-start.40 = (bf16[32,4096]{1,0:T(8,128)(2,1)S(1)}, bf16[32,4096]{1,0:T(8,128)(2,1)S(1)}, u32[]{:S(2)}, u32[]{:S(2)}) collective-permute-start(bf16[32,4096]{1,0:T(8,128)(2,1)S(1)} %bitcast.49), channel_id=1, source_target_pairs={{0,8},{2,10},{4,12},{6,14},{8,16},{10,18},{12,20},{14,22},{16,24},... | collective-permute-start | bytes 786440 | tf_op jit(solution)/shard_map/ppermute | solution.py:56
  256.3 15.5 %collective-permute-start.39 = (bf16[32,4096]{1,0:T(8,128)(2,1)S(1)}, bf16[32,4096]{1,0:T(8,128)(2,1)S(1)}, u32[]{:S(2)}, u32[]{:S(2)}) collective-permute-start(bf16[32,4096]{1,0:T(8,128)(2,1)S(1)} %collective-permute-done.38), channel_id=1, source_target_pairs={{0,2},{2,0},{4,6},{6,4},{8,10},{10,8},{12,14},{14,12},{16,18},{18,... | collective-permute-start | bytes 786440 | tf_op jit(solution)/shard_map/ppermute | solution.py:46
  260.8 9.7 %collective-permute-start.42 = (bf16[32,4096]{1,0:T(8,128)(2,1)S(1)}, bf16[32,4096]{1,0:T(8,128)(2,1)S(1)}, u32[]{:S(2)}, u32[]{:S(2)}) collective-permute-start(bf16[32,4096]{1,0:T(8,128)(2,1)S(1)} %collective-permute-done.41), channel_id=1, source_target_pairs={{8,0},{10,2},{12,4},{14,6},{16,8},{18,10},{20,12},{22,14},{24,16},... | collective-permute-start | bytes 786440 | tf_op jit(solution)/shard_map/ppermute | solution.py:56
  270.4 8.8 %collective-permute-start.43 = (bf16[32,4096]{1,0:T(8,128)(2,1)S(1)}, bf16[32,4096]{1,0:T(8,128)(2,1)S(1)}, u32[]{:S(2)}, u32[]{:S(2)}) collective-permute-start(bf16[32,4096]{1,0:T(8,128)(2,1)S(1)} %collective-permute-done.42), channel_id=1, source_target_pairs={{8,0},{10,2},{12,4},{14,6},{16,8},{18,10},{20,12},{22,14},{24,16},... | collective-permute-start | bytes 786440 | tf_op jit(solution)/shard_map/ppermute | solution.py:56
  279.3 6.4 %collective-permute-start.45 = (bf16[32,4096]{1,0:T(8,128)(2,1)S(1)}, bf16[32,4096]{1,0:T(8,128)(2,1)S(1)}, u32[]{:S(2)}, u32[]{:S(2)}) collective-permute-start(bf16[32,4096]{1,0:T(8,128)(2,1)S(1)} %get-tuple-element.176), channel_id=1, source_target_pairs={{0,4},{2,6},{4,0},{6,2},{8,12},{10,14},{12,8},{14,10},{16,20},{18,... | collective-permute-start | bytes 786440 | tf_op jit(solution)/shard_map/ppermute | solution.py:46
  280.4 5.3 %collective-permute-start.44 = (bf16[32,4096]{1,0:T(8,128)(2,1)S(1)}, bf16[32,4096]{1,0:T(8,128)(2,1)S(1)}, u32[]{:S(2)}, u32[]{:S(2)}) collective-permute-start(bf16[32,4096]{1,0:T(8,128)(2,1)S(1)} %get-tuple-element.176), channel_id=1, source_target_pairs={{0,2},{2,0},{4,6},{6,4},{8,10},{10,8},{12,14},{14,12},{16,18},{18,... | collective-permute-start | bytes 786440 | tf_op jit(solution)/shard_map/ppermute | solution.py:46
  280.4 9.4 %collective-permute-start.47 = (bf16[32,4096]{1,0:T(8,128)(2,1)S(1)}, bf16[32,4096]{1,0:T(8,128)(2,1)S(1)}, u32[]{:S(2)}, u32[]{:S(2)}) collective-permute-start(bf16[32,4096]{1,0:T(8,128)(2,1)S(1)} %collective-permute-done.40), channel_id=1, source_target_pairs={{0,8},{2,10},{4,12},{6,14},{8,16},{10,18},{12,20},{14,22},{16,24},... | collective-permute-start | bytes 786440 | tf_op jit(solution)/shard_map/ppermute | solution.py:56
  285.7 1.5 collective-permute-start.46
  289.8 2.1 copy-start.9
  289.8 8.8 %collective-permute-start.48 = (bf16[32,4096]{1,0:T(8,128)(2,1)S(1)}, bf16[32,4096]{1,0:T(8,128)(2,1)S(1)}, u32[]{:S(2)}, u32[]{:S(2)}) collective-permute-start(bf16[32,4096]{1,0:T(8,128)(2,1)S(1)} %get-tuple-element.174), channel_id=1, source_target_pairs={{0,2},{2,0},{4,6},{6,4},{8,10},{10,8},{12,14},{14,12},{16,18},{18,... | collective-permute-start | bytes 786440 | tf_op jit(solution)/shard_map/ppermute | solution.py:46
  289.9 8.7 %collective-permute-start.49 = (bf16[32,4096]{1,0:T(8,128)(2,1)S(1)}, bf16[32,4096]{1,0:T(8,128)(2,1)S(1)}, u32[]{:S(2)}, u32[]{:S(2)}) collective-permute-start(bf16[32,4096]{1,0:T(8,128)(2,1)S(1)} %get-tuple-element.174), channel_id=1, source_target_pairs={{0,4},{2,6},{4,0},{6,2},{8,12},{10,14},{12,8},{14,10},{16,20},{18,... | collective-permute-start | bytes 786440 | tf_op jit(solution)/shard_map/ppermute | solution.py:46
  293.9 9.8 %collective-permute-start.51 = (bf16[32,4096]{1,0:T(8,128)(2,1)S(1)}, bf16[32,4096]{1,0:T(8,128)(2,1)S(1)}, u32[]{:S(2)}, u32[]{:S(2)}) collective-permute-start(bf16[32,4096]{1,0:T(8,128)(2,1)S(1)} %collective-permute-done.47), channel_id=1, source_target_pairs={{0,8},{2,10},{4,12},{6,14},{8,16},{10,18},{12,20},{14,22},{16,24},... | collective-permute-start | bytes 786440 | tf_op jit(solution)/shard_map/ppermute | solution.py:56
  298.6 1.5 collective-permute-start.50
  304.5 8.7 %collective-permute-start.52 = (bf16[32,4096]{1,0:T(8,128)(2,1)S(1)}, bf16[32,4096]{1,0:T(8,128)(2,1)S(1)}, u32[]{:S(2)}, u32[]{:S(2)}) collective-permute-start(bf16[32,4096]{1,0:T(8,128)(2,1)S(1)} %get-tuple-element.172), channel_id=1, source_target_pairs={{0,2},{2,0},{4,6},{6,4},{8,10},{10,8},{12,14},{14,12},{16,18},{18,... | collective-permute-start | bytes 786440 | tf_op jit(solution)/shard_map/ppermute | solution.py:46
  304.5 8.7 %collective-permute-start.53 = (bf16[32,4096]{1,0:T(8,128)(2,1)S(1)}, bf16[32,4096]{1,0:T(8,128)(2,1)S(1)}, u32[]{:S(2)}, u32[]{:S(2)}) collective-permute-start(bf16[32,4096]{1,0:T(8,128)(2,1)S(1)} %get-tuple-element.172), channel_id=1, source_target_pairs={{0,4},{2,6},{4,0},{6,2},{8,12},{10,14},{12,8},{14,10},{16,20},{18,... | collective-permute-start | bytes 786440 | tf_op jit(solution)/shard_map/ppermute | solution.py:46
  313.2 1.5 collective-permute-start.54
  315.4 3.6 %copy-start.10 = (bf16[4096,512]{1,0:T(8,128)(2,1)S(1)}, bf16[4096,512]{1,0:T(8,128)(2,1)}, u32[]{:S(2)}) copy-start(bf16[4096,512]{1,0:T(8,128)(2,1)} %param.17) | copy-start | bytes 12582916
  320.4 5.9 %collective-permute-start.55 = (bf16[128,512]{1,0:T(8,128)(2,1)S(1)}, bf16[128,512]{1,0:T(8,128)(2,1)S(1)}, u32[]{:S(2)}, u32[]{:S(2)}) collective-permute-start(bf16[128,512]{1,0:T(8,128)(2,1)S(1)} %dynamic-slice_convert_fusion.1), channel_id=1, source_target_pairs={{0,1},{1,0},{2,3},{3,2},{4,5},{5,4},{6,7},{7,6},{8,9},{9,8},{10,11... | collective-permute-start | bytes 393224 | tf_op jit(solution)/shard_map/ppermute | solution.py:301

commit v3 on v0

v3 whole, which is shorter than its diff:
```python
import functools
import itertools
import math

import jax
import jax.numpy as jnp
from jax import lax
from jax.experimental import pallas as pl
from jax.experimental.pallas import tpu as pltpu
from jax.sharding import PartitionSpec as P

HD = 128
MAX_PAGES = 2
WAVE = 3
ROW_UNROLL = 4
VMEM_LIMIT = 48 * 1024 * 1024


def factors(groups):
    if groups % 4 == 0:
        return (groups // 4, 2, 2)
    return (groups,)


def strides(dims):
    return tuple(math.prod(dims[i + 1 :]) for i in range(len(dims)))


def shifted(index, offset, dims):
    result = 0
    for size, stride, ahead in zip(dims, strides(dims), offset):
        result = result + lax.rem(index // stride % size + ahead + size, size) * stride
    return result


def shifted_static(index, offset, dims):
    result = 0
    for size, stride, ahead in zip(dims, strides(dims), offset):
        result += (index // stride % size + ahead) % size * stride
    return result


def send_by(array, offset, dims):
    groups = math.prod(dims)
    pairs = [(s, shifted_static(s, offset, dims)) for s in range(groups)]
    return lax.ppermute(array, "group", pairs)


def offset_rank(offset, dims):
    return sum(o * s for o, s in zip(offset, strides(dims)))


def behind_rank(me, other, dims):
    rank = 0
    for size, stride in zip(dims, strides(dims)):
        rank = rank + lax.rem(me // stride % size - other // stride % size + size, size) * stride
    return rank


def behind(me, offset, dims):
    return shifted(me, tuple(-o for o in offset), dims)


def gather_shards(shard, dims):
    held = {(0,) * len(dims): shard}
    for axis, size in enumerate(dims):
        incoming = {}
        for ahead in range(1, size):
            step = tuple(ahead if i == axis else 0 for i in range(len(dims)))
            for offset, array in held.items():
                incoming[tuple(a + b for a, b in zip(offset, step))] = send_by(array, step, dims)
        held.update(incoming)
    return held


def prepare_kernel(dims, offsets, lengths, prefill_of, decode_of, pool, received, *rest):
    sends = rest[: len(offsets)]
    held, zero_page, start_of, count_of, in_sems, out_sem = rest[len(offsets) :]
    groups = math.prod(dims)
    me = lax.axis_index("group")
    page_total, page_size, _ = pool.shape
    loads = [pltpu.make_async_copy(pool.at[p], held.at[p], in_sems.at[p]) for p in range(page_total)]
    for load in loads:
        load.start()
    for d in range(groups + 1):
        start_of[d] = 0
        count_of[d] = 0
    zero_page[...] = jnp.zeros_like(zero_page)

    def visit(r, running):
        mine = prefill_of[r] == me
        count = (lengths[r] + page_size - 1) // page_size
        to = jnp.where(mine, decode_of[r], groups)
        start_of[to] = running
        count_of[to] = count
        return running + jnp.where(mine, count, 0)

    lax.fori_loop(0, lengths.shape[0], visit, jnp.int32(0), unroll=8)
    for load in loads:
        load.wait()

    def store(start, count, page, target, do):
        @pl.when(page < count)
        def _():
            do(pltpu.make_async_copy(held.at[start + page], target, out_sem))

        @pl.when(page >= count)
        def _():
            do(pltpu.make_async_copy(zero_page, target, out_sem))

    def every(do):
        for send, offset in zip(sends, offsets):
            to = shifted(me, offset, dims)
            for page in range(MAX_PAGES):
                store(start_of[to], count_of[to], page, send.at[page], do)
        for page in range(MAX_PAGES):
            store(start_of[me], count_of[me], page, received.at[me * MAX_PAGES + page], do)

    every(lambda copy: copy.start())
    every(lambda copy: copy.wait())


def prepare(dims, offsets, lengths, prefill_of, decode_of, pool):
    groups = math.prod(dims)
    page = pool.shape[1:]
    smem = pl.BlockSpec(memory_space=pltpu.SMEM)
    hbm = pl.BlockSpec(memory_space=pl.ANY)
    block = jax.ShapeDtypeStruct((MAX_PAGES,) + page, pool.dtype)
    outs = [jax.ShapeDtypeStruct((groups * MAX_PAGES,) + page, pool.dtype)] + [block] * len(offsets)
    return pl.pallas_call(
        functools.partial(prepare_kernel, dims, offsets),
        out_shape=outs,
        in_specs=[smem, smem, smem, hbm],
        out_specs=[hbm] * len(outs),
        scratch_shapes=[
            pltpu.VMEM(pool.shape, pool.dtype),
            pltpu.VMEM(page, pool.dtype),
            pltpu.SMEM((groups + 1,), jnp.int32),
            pltpu.SMEM((groups + 1,), jnp.int32),
            pltpu.SemaphoreType.DMA((pool.shape[0],)),
            pltpu.SemaphoreType.DMA,
        ],
        compiler_params=pltpu.CompilerParams(vmem_limit_bytes=VMEM_LIMIT),
        cost_estimate=pl.CostEstimate(flops=0, bytes_accessed=4 * pool.size, transcendentals=0),
        name="outgoing_pages",
    )(lengths, prefill_of, decode_of, pool)


def attend_row(query, pages, length):
    first, second = pages
    kv_heads = first.shape[1] // (2 * HD)
    share = query.shape[0] // kv_heads
    scores = []
    for h in range(kv_heads):
        columns = slice(2 * h * HD, (2 * h + 1) * HD)
        keys = jnp.concatenate([first[:, columns], second[:, columns]], axis=0)
        every = lax.dot_general(
            query, keys, (((1,), (1,)), ((), ())), preferred_element_type=jnp.float32
        )
        scores.append(every[h * share : (h + 1) * share])
    score = jnp.concatenate(scores, axis=0) * (1.0 / math.sqrt(HD))
    live = lax.broadcasted_iota(jnp.int32, score.shape, 1) < length
    masked = jnp.where(live, score, -1e30)
    highest = jnp.max(masked, axis=1, keepdims=True)
    weights = jnp.where(live, jnp.exp(masked - highest), 0.0)
    totals = jnp.sum(weights, axis=1, keepdims=True)
    rounded = weights.astype(jnp.bfloat16)
    mixtures = []
    for h in range(kv_heads):
        columns = slice((2 * h + 1) * HD, (2 * h + 2) * HD)
        values = jnp.concatenate([first[:, columns], second[:, columns]], axis=0)
        every = jnp.dot(rounded, values, preferred_element_type=jnp.float32)
        mixtures.append(every[h * share : (h + 1) * share])
    return jnp.concatenate(mixtures, axis=0) / totals


def settle_kernel(dims, offsets, own, last, lengths, prefill_of, row_request, queries, rows_in, received_in, *rest):
    blocks = rest[: len(offsets)]
    received, out, rows, held, list_row, list_block, list_length, in_sems, out_sems = rest[len(offsets) :]
    me = lax.axis_index("group")
    row_local, query_heads, _ = queries.shape
    mine = pl.ds(me * MAX_PAGES, MAX_PAGES)
    places = [pl.ds(behind(me, offset, dims) * MAX_PAGES, MAX_PAGES) for offset in offsets]
    sources = list(blocks) + ([received_in.at[mine]] if own else [])
    ranks = [offset_rank(offset, dims) for offset in offsets] + ([0] if own else [])
    loads = [pltpu.make_async_copy(s, held.at[i], in_sems.at[i]) for i, s in enumerate(sources)]
    stores = [
        pltpu.make_async_copy(held.at[i], received.at[place], out_sems.at[i]) for i, place in enumerate(places)
    ]
    for load in loads:
        load.start()

    found = jnp.int32(0)
    for b in range(row_local):
        request = row_request[me * row_local + b]
        rank = behind_rank(me, prefill_of[request], dims)
        block, match = jnp.int32(0), jnp.int32(0)
        for i, here in enumerate(ranks):
            block = jnp.where(rank == here, i, block)
            match = jnp.where(rank == here, 1, match)
        list_row[found] = b
        list_block[found] = block
        list_length[found] = lengths[request]
        found = found + match
    for i in range(ROW_UNROLL):
        list_row[found + i] = row_local
        list_block[found + i] = 0
        list_length[found + i] = 1
    rows[:row_local] = rows_in[...]
    for load in loads:
        load.wait()
    for store in stores:
        store.start()

    @pl.loop(0, (found + ROW_UNROLL - 1) // ROW_UNROLL)
    def _(step):
        results = []
        for i in range(ROW_UNROLL):
            at = step * ROW_UNROLL + i
            query = queries[jnp.minimum(list_row[at], row_local - 1)]
            pages = [held[list_block[at], page] for page in range(MAX_PAGES)]
            results.append(attend_row(query, pages, list_length[at]))
        for i, result in enumerate(results):
            rows[list_row[step * ROW_UNROLL + i]] = result

    if last:
        for h in range(query_heads):
            out[:, h * HD : (h + 1) * HD] = rows[:row_local, h, :].astype(out.dtype)
    else:
        out[...] = rows[:row_local]
    for store in stores:
        store.wait()


def settle(dims, offsets, own, last, tables, queries, rows, received, blocks):
    row_local, query_heads, _ = queries.shape
    smem = pl.BlockSpec(memory_space=pltpu.SMEM)
    vmem = pl.BlockSpec(memory_space=pltpu.VMEM)
    hbm = pl.BlockSpec(memory_space=pl.ANY)
    count = len(blocks) + (1 if own else 0)
    if last:
        out = jax.ShapeDtypeStruct((row_local, query_heads * HD), jnp.bfloat16)
    else:
        out = jax.ShapeDtypeStruct(rows.shape, rows.dtype)
    return pl.pallas_call(
        functools.partial(settle_kernel, dims, offsets, own, last),
        out_shape=[jax.ShapeDtypeStruct(received.shape, received.dtype), out],
        in_specs=[smem, smem, smem, vmem, vmem, hbm] + [hbm] * len(blocks),
        out_specs=[hbm, vmem],
        scratch_shapes=[
            pltpu.VMEM((row_local + 1, query_heads, HD), jnp.float32),
            pltpu.VMEM((count, MAX_PAGES) + received.shape[1:], received.dtype),
            pltpu.SMEM((row_local + ROW_UNROLL,), jnp.int32),
            pltpu.SMEM((row_local + ROW_UNROLL,), jnp.int32),
            pltpu.SMEM((row_local + ROW_UNROLL,), jnp.int32),
            pltpu.SemaphoreType.DMA((count,)),
            pltpu.SemaphoreType.DMA((count,)),
        ],
        input_output_aliases={5: 0},
        compiler_params=pltpu.CompilerParams(vmem_limit_bytes=VMEM_LIMIT),
        cost_estimate=pl.CostEstimate(
            flops=1 << 30, bytes_accessed=4 * sum(b.size for b in blocks), transcendentals=1 << 18
        ),
        name="settle_pages",
    )(*tables, queries, rows, received, *blocks)


def project_kernel(dims, offsets, out_weight, *rest):
    shards = rest[: len(offsets)]
    own, *theirs = rest[len(offsets) : -3]
    attended, product, sems = rest[-3:]
    me = lax.axis_index("group")
    heads = lax.axis_size("head")
    my_head = lax.axis_index("head")
    row_local = shards[0].shape[0]
    share = own.shape[0]
    copies = []
    for i, offset in enumerate(offsets):
        place = pl.ds(behind(me, offset, dims) * row_local, row_local)
        copies.append(pltpu.make_async_copy(shards[i], attended.at[place], sems.at[i]))
        copies[-1].start()
    for copy in copies:
        copy.wait()
    product[...] = jnp.dot(attended[...], out_weight[...], preferred_element_type=jnp.float32)
    own[...] = product[pl.ds(pl.multiple_of(my_head * share, share), share)]
    for ahead, target in enumerate(theirs, 1):
        start = pl.multiple_of(lax.rem(my_head + ahead, heads) * share, share)
        target[...] = product[pl.ds(start, share)].astype(target.dtype)


def project(dims, gathered, out_weight, heads):
    offsets = list(gathered)
    shards = [gathered[o] for o in offsets]
    row_local, width = shards[0].shape
    row_total = row_local * len(shards)
    share, columns = row_total // heads, out_weight.shape[1]
    vmem = pl.BlockSpec(memory_space=pltpu.VMEM)
    hbm = pl.BlockSpec(memory_space=pl.ANY)
    theirs = jax.ShapeDtypeStruct((share, columns), jnp.bfloat16)
    return pl.pallas_call(
        functools.partial(project_kernel, dims, offsets),
        out_shape=[jax.ShapeDtypeStruct((share, columns), jnp.float32)] + [theirs] * (heads - 1),
        in_specs=[vmem] + [hbm] * len(shards),
        out_specs=[vmem] * heads,
        scratch_shapes=[
            pltpu.VMEM((row_total, width), jnp.bfloat16),
            pltpu.VMEM((row_total, columns), jnp.float32),
            pltpu.SemaphoreType.DMA((len(shards),)),
        ],
        compiler_params=pltpu.CompilerParams(vmem_limit_bytes=VMEM_LIMIT),
        cost_estimate=pl.CostEstimate(
            flops=2 * row_total * width * columns, bytes_accessed=2 * out_weight.size, transcendentals=0
        ),
        name="project_rows",
    )(out_weight, *shards)


def local(dims, kv_pool, lengths, prefill_of, decode_of, row_request, queries, out_weight):
    row_local, query_width = queries.shape
    query_heads = queries.reshape(row_local, query_width // HD, HD)
    heads = lax.axis_size("head")

    far, near = range(dims[0]), list(itertools.product(*(range(n) for n in dims[1:])))
    offsets = [(z,) + n for n in near for z in far if z or any(n)]
    received, *sends = prepare(dims, offsets, lengths, prefill_of, decode_of, kv_pool)
    arrived = [send_by(block, offset, dims) for block, offset in zip(sends, offsets)]
    rows = jnp.zeros(query_heads.shape, jnp.float32)
    tables = (lengths, prefill_of, row_request)
    for first in range(0, len(offsets), WAVE):
        wave = slice(first, first + WAVE)
        last = first + WAVE >= len(offsets)
        received, rows = settle(
            dims, offsets[wave], first == 0, last, tables, query_heads, rows, received, arrived[wave]
        )

    own, *theirs = project(dims, gather_shards(rows, dims), out_weight, heads)
    for ahead, part in enumerate(theirs, 1):
        pairs = [(h, (h + ahead) % heads) for h in range(heads)]
        own = own + lax.ppermute(part, "head", pairs).astype(jnp.float32)
    return (received, own.astype(jnp.bfloat16))


def solution(mesh):
    in_specs = (
        P("group", None, "head"),
        P(),
        P(),
        P(),
        P(),
        P("group", "head"),
        P("head", "group"),
    )
    out_specs = (P("group", None, "head"), P("head", "group"))
    body = functools.partial(local, factors(mesh.shape["group"]))
    return jax.shard_map(body, mesh=mesh, in_specs=in_specs, out_specs=out_specs, check_vma=False)
```

time: 353 us -> 236 us (0.67)
  waiting for transfers between devices: 244 us -> 111 us
  starting transfers between devices: 7.66 us -> 92 us
  local copies, waits for them, and re-layouts: 52.3 us -> 2.07 us
  Pallas kernels: 0 us -> 29.2 us
  matrix products: 20.1 us -> 0 us
  between operations: 14.2 us -> 0.8 us
  other arithmetic: 13.9 us -> 0.68 us
    all_to_all x1 -> x0, waiting for transfers between devices: 148 us -> none  [local(): lax.all_to_all(outgoing, 'group', split_axis=0, concat_axis=0, tiled=True)]
    ppermute x0 -> x31, waiting for transfers between devices: none -> 111 us  [the longest x30 107 us: send_by(): return lax.ppermute(array, 'group', pairs)]
    ppermute x0 -> x31, starting transfers between devices: none -> 92 us  [the longest x30 90.4 us: send_by(): return lax.ppermute(array, 'group', pairs)]
    all_gather x1 -> x0, waiting for transfers between devices: 73.3 us -> none  [local(): gathered = lax.all_gather(attended, 'group', axis=0, tiled=True)]
    pallas_call x0 -> x7, Pallas kernels: none -> 29.2 us  [the longest x5 16.1 us: settle(): pl.pallas_call(functools.partial(settle_kernel, dims, offsets, own, last)...]
    psum x1 -> x0, waiting for transfers between devices: 22.1 us -> none  [local(): lax.psum(jnp.dot(gathered, out_weight, preferred_element_type=jnp.float32...]
    slice x1 -> x0, local copies, waits for them, and re-layouts: 17.2 us -> none  [attend_all(): cache_heads[:, :, 1, :]]
    reshape x1 -> x0, local copies, waits for them, and re-layouts: 14.2 us -> none  [attend_all(): incoming.reshape(groups * slot_total * page_size, local_heads, 2, HD)]
  transfers between devices with their start and end apart: 3 -> 31, of which waited for: 3 -> 12; matrix products, arithmetic and copies ran while one was open for 1% -> 0% of each run, Pallas kernels for 0% -> 5%
where the time goes in v3:
time: 236 us
  waiting for transfers between devices  111 us (47%)
  starting transfers between devices  92 us (39%)
  Pallas kernels  29.2 us (12%)
    ppermute x30, waiting for transfers between devices, send_by(): return lax.ppermute(array, 'group', pairs)  107 us
    ppermute x30, starting transfers between devices, send_by(): return lax.ppermute(array, 'group', pairs)  90.4 us
    pallas_call x5, Pallas kernels, settle(): pl.pallas_call(functools.partial(settle_kernel, dims, offsets, own, last)...  16.1 us
    pallas_call x1, Pallas kernels, project(): pl.pallas_call(functools.partial(project_kernel, dims, offsets), out_shap...  6.68 us
    pallas_call x1, Pallas kernels, prepare(): pl.pallas_call(functools.partial(prepare_kernel, dims, offsets), out_shap...  6.39 us
  transfers between devices with their start and end apart: 31, of which 12 were waited for; matrix products, arithmetic and copies ran while one was open for 0% of the time, Pallas kernels for 5%

profile of v3, /device:TPU:0, one launch (start us, length us, event | category | flops | bytes accessed | tf_op | source)
XLA Modules:
  0.0 235.8 jit_solution(8249148440524714233)
XLA Ops:
  0.6 0.7 copy-done
  1.3 0.7 copy-done.1
  2.0 0.7 copy-done.3
  2.7 6.4 %outgoing_pages.1 = (bf16[32,128,1024]{2,1,0:T(8,128)(2,1)}, bf16[2,128,1024]{2,1,0:T(8,128)(2,1)S(1)}, bf16[2,128,1024]{2,1,0:T(8,128)(2,1)S(1)}, bf16[2,128,10...) custom-call(s32[256]{0:T(256)S(1)} %copy-done, ...), custom_call_target="tpu_custom_call" | custom-call | bytes 16777216 | tf_op jit(solution)/shard_map/outgoing_pages/pallas_call | solution.py:130
  9.1 3.1 %collective-permute-start = (bf16[2,128,1024]{2,1,0:T(8,128)(2,1)S(1)}, bf16[2,128,1024]{2,1,0:T(8,128)(2,1)S(1)}, u32[]{:S(2)}, u32[]{:S(2)}) collective-permute-start(bf16[2,128,1024]{2,1,0:T(8,128)(2,1)S(1)} %get-tuple-element.31), channel_id=1, source_target_pairs={{0,8},{2,10},{4,12},{6,14},{8,16},{10,18},{12,20},{14,22},{16,24},... | collective-permute-start | bytes 1572872 | tf_op jit(solution)/shard_map/ppermute | solution.py:46
  12.2 2.6 %collective-permute-start.1 = (bf16[2,128,1024]{2,1,0:T(8,128)(2,1)S(1)}, bf16[2,128,1024]{2,1,0:T(8,128)(2,1)S(1)}, u32[]{:S(2)}, u32[]{:S(2)}) collective-permute-start(bf16[2,128,1024]{2,1,0:T(8,128)(2,1)S(1)} %get-tuple-element.32), channel_id=1, source_target_pairs={{0,16},{2,18},{4,20},{6,22},{8,24},{10,26},{12,28},{14,30},{16,0},... | collective-permute-start | bytes 1572872 | tf_op jit(solution)/shard_map/ppermute | solution.py:46
  14.7 1.4 collective-permute-start.2
  16.1 0.8 collective-permute-start.4
  16.9 10.2 %collective-permute-done.rest_0_ = bf16[2,128,1024]{2,1,0:T(8,128)(2,1)S(1)} collective-permute-done((bf16[2,128,1024]{2,1,0:T(8,128)(2,1)S(1)}, bf16[2,128,1024]{2,1,0:T(8,128)(2,1)S(1)}, u32[]{:S(2)}, u32[]{:S(2)}) %collective-permute-start) | collective-permute-done | bytes 524320 | tf_op jit(solution)/shard_map/ppermute | solution.py:46
  27.1 22.5 %collective-permute-done.1.rest_1_ = bf16[2,128,1024]{2,1,0:T(8,128)(2,1)S(1)} collective-permute-done((bf16[2,128,1024]{2,1,0:T(8,128)(2,1)S(1)}, bf16[2,128,1024]{2,1,0:T(8,128)(2,1)S(1)}, u32[]{:S(2)}, u32[]{:S(2)}) %collective-permute-start.1) | collective-permute-done | bytes 524320 | tf_op jit(solution)/shard_map/ppermute | solution.py:46
  49.5 10.6 %collective-permute-start.6 = (bf16[2,128,1024]{2,1,0:T(8,128)(2,1)S(1)}, bf16[2,128,1024]{2,1,0:T(8,128)(2,1)S(1)}, u32[]{:S(2)}, u32[]{:S(2)}) collective-permute-start(bf16[2,128,1024]{2,1,0:T(8,128)(2,1)S(1)} %get-tuple-element.41), channel_id=1, source_target_pairs={{0,26},{2,24},{4,30},{6,28},{8,2},{10,0},{12,6},{14,4},{16,10},{18... | collective-permute-start | bytes 1572872 | tf_op jit(solution)/shard_map/ppermute | solution.py:46
  60.1 0.0 collective-permute-done.2.rest_2_
  60.1 1.5 collective-permute-start.7
  61.6 22.8 %collective-permute-start.8 = (bf16[2,128,1024]{2,1,0:T(8,128)(2,1)S(1)}, bf16[2,128,1024]{2,1,0:T(8,128)(2,1)S(1)}, u32[]{:S(2)}, u32[]{:S(2)}) collective-permute-start(bf16[2,128,1024]{2,1,0:T(8,128)(2,1)S(1)} %get-tuple-element.43), channel_id=1, source_target_pairs={{0,12},{2,14},{4,8},{6,10},{8,20},{10,22},{12,16},{14,18},{16,28},... | collective-permute-start | bytes 1572872 | tf_op jit(solution)/shard_map/ppermute | solution.py:46
  84.4 9.6 %collective-permute-start.9 = (bf16[2,128,1024]{2,1,0:T(8,128)(2,1)S(1)}, bf16[2,128,1024]{2,1,0:T(8,128)(2,1)S(1)}, u32[]{:S(2)}, u32[]{:S(2)}) collective-permute-start(bf16[2,128,1024]{2,1,0:T(8,128)(2,1)S(1)} %get-tuple-element.46), channel_id=1, source_target_pairs={{0,20},{2,22},{4,16},{6,18},{8,28},{10,30},{12,24},{14,26},{16,4},... | collective-permute-start | bytes 1572872 | tf_op jit(solution)/shard_map/ppermute | solution.py:46
  94.1 21.9 %collective-permute-done.5.rest_2_ = bf16[2,128,1024]{2,1,0:T(8,128)(2,1)S(1)} collective-permute-done((bf16[2,128,1024]{2,1,0:T(8,128)(2,1)S(1)}, bf16[2,128,1024]{2,1,0:T(8,128)(2,1)S(1)}, u32[]{:S(2)}, u32[]{:S(2)}) %collective-permute-start.5) | collective-permute-done | bytes 524320 | tf_op jit(solution)/shard_map/ppermute | solution.py:46
  116.0 1.5 collective-permute-start.10
  117.5 2.0 collective-permute-start.11
  119.5 9.5 %collective-permute-start.12 = (bf16[2,128,1024]{2,1,0:T(8,128)(2,1)}, bf16[2,128,1024]{2,1,0:T(8,128)(2,1)S(1)}, u32[]{:S(2)}, u32[]{:S(2)}) collective-permute-start(bf16[2,128,1024]{2,1,0:T(8,128)(2,1)} %get-tuple-element.51), channel_id=1, source_target_pairs={{0,14},{2,12},{4,10},{6,8},{8,22},{10,20},{12,18},{14,16},{16,30},... | collective-permute-start | bytes 1572872 | tf_op jit(solution)/shard_map/ppermute | solution.py:46
  129.0 10.2 %collective-permute-start.13 = (bf16[2,128,1024]{2,1,0:T(8,128)(2,1)}, bf16[2,128,1024]{2,1,0:T(8,128)(2,1)S(1)}, u32[]{:S(2)}, u32[]{:S(2)}) collective-permute-start(bf16[2,128,1024]{2,1,0:T(8,128)(2,1)} %get-tuple-element.52), channel_id=1, source_target_pairs={{0,22},{2,20},{4,18},{6,16},{8,30},{10,28},{12,26},{14,24},{16,6},... | collective-permute-start | bytes 1572872 | tf_op jit(solution)/shard_map/ppermute | solution.py:46
  139.2 23.0 %collective-permute-done.9.rest_0_ = bf16[2,128,1024]{2,1,0:T(8,128)(2,1)S(1)} collective-permute-done((bf16[2,128,1024]{2,1,0:T(8,128)(2,1)S(1)}, bf16[2,128,1024]{2,1,0:T(8,128)(2,1)S(1)}, u32[]{:S(2)}, u32[]{:S(2)}) %collective-permute-start.9) | collective-permute-done | bytes 524320 | tf_op jit(solution)/shard_map/ppermute | solution.py:46
  162.1 0.5 collective-permute-start.14
  162.6 4.5 %settle_pages.5 = (bf16[32,128,1024]{2,1,0:T(8,128)(2,1)}, f32[16,32,128]{2,1,0:T(8,128)S(1)}) custom-call(s32[256]{0:T(256)S(1)} %copy-done, s32[256]{0:T(256)S(1)} %copy-done.1, s32[256]{0:T(256)S(1)} %copy-done.2, bf16[16,32,128]{2,1,0:T(8,128)(2,1)S(1)} %bitcast.2, f32[16,32,128]{2,1,0:T(8,128)S(1)} %broadcast_in_dim.3.rows_in, ...), custom_call_target="tpu_custom_call", output_to_operand_aliasing={{0}: (5, {})} | custom-call | flops 1073741824 | bytes 3145728 | tf_op jit(solution)/shard_map/settle_pages/pallas_call | solution.py:245
  167.1 2.5 %settle_pages.6 = (bf16[32,128,1024]{2,1,0:T(8,128)(2,1)}, f32[16,32,128]{2,1,0:T(8,128)S(1)}) custom-call(s32[256]{0:T(256)S(1)} %copy-done, s32[256]{0:T(256)S(1)} %copy-done.1, s32[256]{0:T(256)S(1)} %copy-done.2, bf16[16,32,128]{2,1,0:T(8,128)(2,1)S(1)} %bitcast.3, ...), custom_call_target="tpu_custom_call", output_to_operand_aliasing={{0}: (5, {})} | custom-call | flops 1073741824 | bytes 3145728 | tf_op jit(solution)/shard_map/settle_pages/pallas_call | solution.py:245
  169.6 2.5 %settle_pages.7 = (bf16[32,128,1024]{2,1,0:T(8,128)(2,1)}, f32[16,32,128]{2,1,0:T(8,128)S(1)}) custom-call(s32[256]{0:T(256)S(1)} %copy-done, s32[256]{0:T(256)S(1)} %copy-done.1, s32[256]{0:T(256)S(1)} %copy-done.2, bf16[16,32,128]{2,1,0:T(8,128)(2,1)S(1)} %bitcast.4, ...), custom_call_target="tpu_custom_call", output_to_operand_aliasing={{0}: (5, {})} | custom-call | flops 1073741824 | bytes 3145728 | tf_op jit(solution)/shard_map/settle_pages/pallas_call | solution.py:245
  172.2 2.5 %settle_pages.8 = (bf16[32,128,1024]{2,1,0:T(8,128)(2,1)}, f32[16,32,128]{2,1,0:T(8,128)S(1)}) custom-call(s32[256]{0:T(256)S(1)} %copy-done, s32[256]{0:T(256)S(1)} %copy-done.1, s32[256]{0:T(256)S(1)} %copy-done.2, bf16[16,32,128]{2,1,0:T(8,128)(2,1)S(1)} %bitcast.5, ...), custom_call_target="tpu_custom_call", output_to_operand_aliasing={{0}: (5, {})} | custom-call | flops 1073741824 | bytes 3145728 | tf_op jit(solution)/shard_map/settle_pages/pallas_call | solution.py:245
  174.8 9.8 %collective-permute-done.13.rest_1_ = bf16[2,128,1024]{2,1,0:T(8,128)(2,1)S(1)} collective-permute-done((bf16[2,128,1024]{2,1,0:T(8,128)(2,1)}, bf16[2,128,1024]{2,1,0:T(8,128)(2,1)S(1)}, u32[]{:S(2)}, u32[]{:S(2)}) %collective-permute-start.13) | collective-permute-done | bytes 524320 | tf_op jit(solution)/shard_map/ppermute | solution.py:46
  184.5 4.1 %collective-permute-done.14.rest_2_ = bf16[2,128,1024]{2,1,0:T(8,128)(2,1)S(1)} collective-permute-done((bf16[2,128,1024]{2,1,0:T(8,128)(2,1)}, bf16[2,128,1024]{2,1,0:T(8,128)(2,1)S(1)}, u32[]{:S(2)}, u32[]{:S(2)}) %collective-permute-start.14) | collective-permute-done | bytes 524320 | tf_op jit(solution)/shard_map/ppermute | solution.py:46
  188.6 4.1 %settle_pages.9 = (bf16[32,128,1024]{2,1,0:T(8,128)(2,1)}, bf16[16,4096]{1,0:T(8,128)(2,1)S(1)}) custom-call(s32[256]{0:T(256)S(1)} %copy-done, s32[256]{0:T(256)S(1)} %copy-done.1, s32[256]{0:T(256)S(1)} %copy-done.2, bf16[16,32,128]{2,1,0:T(8,128)(2,1)S(1)} %bitcast.6, ...), custom_call_target="tpu_custom_call", output_to_operand_aliasing={{0}: (5, {})} | custom-call | flops 1073741824 | bytes 3145728 | tf_op jit(solution)/shard_map/settle_pages/pallas_call | solution.py:245
  192.7 0.1 collective-permute-start.18
  192.8 8.2 %collective-permute-start.17 = (bf16[16,4096]{1,0:T(8,128)(2,1)S(1)}, bf16[16,4096]{1,0:T(8,128)(2,1)S(1)}, u32[]{:S(2)}, u32[]{:S(2)}) collective-permute-start(bf16[16,4096]{1,0:T(8,128)(2,1)S(1)} %get-tuple-element.55.rest_0_), channel_id=1, source_target_pairs={{0,24},{2,26},{4,28},{6,30},{8,0},{10,2},{12,4},{14,6},{16,8},{18,... | collective-permute-start | bytes 393224 | tf_op jit(solution)/shard_map/ppermute | solution.py:46
  200.9 0.7 collective-permute-start.22
  201.6 0.9 collective-permute-start.15
  202.6 2.3 collective-permute-done.17.rest_3_
  204.9 0.1 collective-permute-start.25
  205.0 1.9 collective-permute-start.21
  206.9 6.6 %collective-permute-done.16.rest_2_ = bf16[16,4096]{1,0:T(8,128)(2,1)S(1)} collective-permute-done((bf16[16,4096]{1,0:T(8,128)(2,1)S(1)}, bf16[16,4096]{1,0:T(8,128)(2,1)S(1)}, u32[]{:S(2)}, u32[]{:S(2)}) %collective-permute-start.16) | collective-permute-done | bytes 131104 | tf_op jit(solution)/shard_map/ppermute | solution.py:46
  213.5 1.8 collective-permute-start.20
  215.3 0.2 collective-permute-start.19
  215.5 0.5 collective-permute-start.23
  216.0 0.1 collective-permute-start.29
  216.1 3.8 %collective-permute-done.20.rest_6_ = bf16[16,4096]{1,0:T(8,128)(2,1)S(1)} collective-permute-done((bf16[16,4096]{1,0:T(8,128)(2,1)S(1)}, bf16[16,4096]{1,0:T(8,128)(2,1)S(1)}, u32[]{:S(2)}, u32[]{:S(2)}) %collective-permute-start.20) | collective-permute-done | bytes 131104 | tf_op jit(solution)/shard_map/ppermute | solution.py:46
  219.9 1.6 collective-permute-done.19.rest_5_
  221.5 1.3 collective-permute-done.27.rest_13_
  222.8 6.7 %project_rows.1 = (f32[128,512]{1,0:T(8,128)S(1)}, bf16[128,512]{1,0:T(8,128)(2,1)S(1)}) custom-call(bf16[4096,512]{1,0:T(8,128)(2,1)} %out_weight.1, bf16[16,4096]{1,0:T(8,128)(2,1)S(1)} %get-tuple-element.55.rest_0_, bf16[16,4096]{1,0:T(8,128)(2,1)S(1)} %collective-permute-done.15.rest_1_, bf16[16,4096]{1,0:T(8,128)(2,1)S(1)} %collective-permute-done.16.rest_2_, ...), custom_call_target="tpu_custom_call" | custom-call | flops 1073741824 | bytes 4194304 | tf_op jit(solution)/shard_map/project_rows/pallas_call | solution.py:300
  229.5 1.6 collective-permute-start.30
  231.1 4.1 %collective-permute-done.30 = bf16[128,512]{1,0:T(8,128)(2,1)S(1)} collective-permute-done((bf16[128,512]{1,0:T(8,128)(2,1)S(1)}, bf16[128,512]{1,0:T(8,128)(2,1)S(1)}, u32[]{:S(2)}, u32[]{:S(2)}) %collective-permute-start.30) | collective-permute-done | bytes 131104 | tf_op jit(solution)/shard_map/ppermute | solution.py:339
  235.1 0.7 add_convert_fusion
  (34 shorter events, 0.1 us)
Async XLA Ops:
  0.6 0.7 copy-start
  1.3 0.7 copy-start.1
  2.0 0.7 copy-start.3
  2.7 159.9 %copy-start.4 = (bf16[16,4096]{1,0:T(8,128)(2,1)S(1)}, bf16[16,4096]{1,0:T(8,128)(2,1)}, u32[]{:S(2)}) copy-start(bf16[16,4096]{1,0:T(8,128)(2,1)} %param.12) | copy-start | bytes 393220
  2.7 160.0 %copy-start.2 = (s32[256]{0:T(256)S(1)}, s32[256]{0:T(256)}, u32[]{:S(2)}) copy-start(s32[256]{0:T(256)} %row_request.9) | copy-start | bytes 3076
  9.1 18.0 %collective-permute-start = (bf16[2,128,1024]{2,1,0:T(8,128)(2,1)S(1)}, bf16[2,128,1024]{2,1,0:T(8,128)(2,1)S(1)}, u32[]{:S(2)}, u32[]{:S(2)}) collective-permute-start(bf16[2,128,1024]{2,1,0:T(8,128)(2,1)S(1)} %get-tuple-element.31), channel_id=1, source_target_pairs={{0,8},{2,10},{4,12},{6,14},{8,16},{10,18},{12,20},{14,22},{16,24},... | collective-permute-start | bytes 1572872 | tf_op jit(solution)/shard_map/ppermute | solution.py:46
  12.2 37.4 %collective-permute-start.1 = (bf16[2,128,1024]{2,1,0:T(8,128)(2,1)S(1)}, bf16[2,128,1024]{2,1,0:T(8,128)(2,1)S(1)}, u32[]{:S(2)}, u32[]{:S(2)}) collective-permute-start(bf16[2,128,1024]{2,1,0:T(8,128)(2,1)S(1)} %get-tuple-element.32), channel_id=1, source_target_pairs={{0,16},{2,18},{4,20},{6,22},{8,24},{10,26},{12,28},{14,30},{16,0},... | collective-permute-start | bytes 1572872 | tf_op jit(solution)/shard_map/ppermute | solution.py:46
  14.7 45.4 %collective-permute-start.2 = (bf16[2,128,1024]{2,1,0:T(8,128)(2,1)S(1)}, bf16[2,128,1024]{2,1,0:T(8,128)(2,1)S(1)}, u32[]{:S(2)}, u32[]{:S(2)}) collective-permute-start(bf16[2,128,1024]{2,1,0:T(8,128)(2,1)S(1)} %get-tuple-element.33), channel_id=1, source_target_pairs={{0,24},{2,26},{4,28},{6,30},{8,0},{10,2},{12,4},{14,6},{16,8},{18,... | collective-permute-start | bytes 1572872 | tf_op jit(solution)/shard_map/ppermute | solution.py:46
  16.1 45.5 %collective-permute-start.3 = (bf16[2,128,1024]{2,1,0:T(8,128)(2,1)S(1)}, bf16[2,128,1024]{2,1,0:T(8,128)(2,1)S(1)}, u32[]{:S(2)}, u32[]{:S(2)}) collective-permute-start(bf16[2,128,1024]{2,1,0:T(8,128)(2,1)S(1)} %get-tuple-element.36), channel_id=1, source_target_pairs={{0,2},{2,0},{4,6},{6,4},{8,10},{10,8},{12,14},{14,12},{16,18},{18,... | collective-permute-start | bytes 1572872 | tf_op jit(solution)/shard_map/ppermute | solution.py:46
  16.1 68.4 %collective-permute-start.4 = (bf16[2,128,1024]{2,1,0:T(8,128)(2,1)S(1)}, bf16[2,128,1024]{2,1,0:T(8,128)(2,1)S(1)}, u32[]{:S(2)}, u32[]{:S(2)}) collective-permute-start(bf16[2,128,1024]{2,1,0:T(8,128)(2,1)S(1)} %get-tuple-element.37), channel_id=1, source_target_pairs={{0,10},{2,8},{4,14},{6,12},{8,18},{10,16},{12,22},{14,20},{16,26},... | collective-permute-start | bytes 1572872 | tf_op jit(solution)/shard_map/ppermute | solution.py:46
  27.1 88.9 %collective-permute-start.5 = (bf16[2,128,1024]{2,1,0:T(8,128)(2,1)S(1)}, bf16[2,128,1024]{2,1,0:T(8,128)(2,1)S(1)}, u32[]{:S(2)}, u32[]{:S(2)}) collective-permute-start(bf16[2,128,1024]{2,1,0:T(8,128)(2,1)S(1)} %get-tuple-element.38), channel_id=1, source_target_pairs={{0,18},{2,16},{4,22},{6,20},{8,26},{10,24},{12,30},{14,28},{16,2},... | collective-permute-start | bytes 1572872 | tf_op jit(solution)/shard_map/ppermute | solution.py:46
  49.5 68.0 %collective-permute-start.6 = (bf16[2,128,1024]{2,1,0:T(8,128)(2,1)S(1)}, bf16[2,128,1024]{2,1,0:T(8,128)(2,1)S(1)}, u32[]{:S(2)}, u32[]{:S(2)}) collective-permute-start(bf16[2,128,1024]{2,1,0:T(8,128)(2,1)S(1)} %get-tuple-element.41), channel_id=1, source_target_pairs={{0,26},{2,24},{4,30},{6,28},{8,2},{10,0},{12,6},{14,4},{16,10},{18... | collective-permute-start | bytes 1572872 | tf_op jit(solution)/shard_map/ppermute | solution.py:46
  60.1 59.4 %collective-permute-start.7 = (bf16[2,128,1024]{2,1,0:T(8,128)(2,1)S(1)}, bf16[2,128,1024]{2,1,0:T(8,128)(2,1)S(1)}, u32[]{:S(2)}, u32[]{:S(2)}) collective-permute-start(bf16[2,128,1024]{2,1,0:T(8,128)(2,1)S(1)} %get-tuple-element.42), channel_id=1, source_target_pairs={{0,4},{2,6},{4,0},{6,2},{8,12},{10,14},{12,8},{14,10},{16,20},{18,... | collective-permute-start | bytes 1572872 | tf_op jit(solution)/shard_map/ppermute | solution.py:46
  61.6 67.4 %collective-permute-start.8 = (bf16[2,128,1024]{2,1,0:T(8,128)(2,1)S(1)}, bf16[2,128,1024]{2,1,0:T(8,128)(2,1)S(1)}, u32[]{:S(2)}, u32[]{:S(2)}) collective-permute-start(bf16[2,128,1024]{2,1,0:T(8,128)(2,1)S(1)} %get-tuple-element.43), channel_id=1, source_target_pairs={{0,12},{2,14},{4,8},{6,10},{8,20},{10,22},{12,16},{14,18},{16,28},... | collective-permute-start | bytes 1572872 | tf_op jit(solution)/shard_map/ppermute | solution.py:46
  84.4 77.7 %collective-permute-start.9 = (bf16[2,128,1024]{2,1,0:T(8,128)(2,1)S(1)}, bf16[2,128,1024]{2,1,0:T(8,128)(2,1)S(1)}, u32[]{:S(2)}, u32[]{:S(2)}) collective-permute-start(bf16[2,128,1024]{2,1,0:T(8,128)(2,1)S(1)} %get-tuple-element.46), channel_id=1, source_target_pairs={{0,20},{2,22},{4,16},{6,18},{8,28},{10,30},{12,24},{14,26},{16,4},... | collective-permute-start | bytes 1572872 | tf_op jit(solution)/shard_map/ppermute | solution.py:46
  116.0 56.2 %collective-permute-start.10 = (bf16[2,128,1024]{2,1,0:T(8,128)(2,1)S(1)}, bf16[2,128,1024]{2,1,0:T(8,128)(2,1)S(1)}, u32[]{:S(2)}, u32[]{:S(2)}) collective-permute-start(bf16[2,128,1024]{2,1,0:T(8,128)(2,1)S(1)} %get-tuple-element.47), channel_id=1, source_target_pairs={{0,28},{2,30},{4,24},{6,26},{8,4},{10,6},{12,0},{14,2},{16,12},{18... | collective-permute-start | bytes 1572872 | tf_op jit(solution)/shard_map/ppermute | solution.py:46
  117.5 54.7 %collective-permute-start.11 = (bf16[2,128,1024]{2,1,0:T(8,128)(2,1)}, bf16[2,128,1024]{2,1,0:T(8,128)(2,1)S(1)}, u32[]{:S(2)}, u32[]{:S(2)}) collective-permute-start(bf16[2,128,1024]{2,1,0:T(8,128)(2,1)} %get-tuple-element.48), channel_id=1, source_target_pairs={{0,6},{2,4},{4,2},{6,0},{8,14},{10,12},{12,10},{14,8},{16,22},{18,... | collective-permute-start | bytes 1572872 | tf_op jit(solution)/shard_map/ppermute | solution.py:46
  119.5 55.3 %collective-permute-start.12 = (bf16[2,128,1024]{2,1,0:T(8,128)(2,1)}, bf16[2,128,1024]{2,1,0:T(8,128)(2,1)S(1)}, u32[]{:S(2)}, u32[]{:S(2)}) collective-permute-start(bf16[2,128,1024]{2,1,0:T(8,128)(2,1)} %get-tuple-element.51), channel_id=1, source_target_pairs={{0,14},{2,12},{4,10},{6,8},{8,22},{10,20},{12,18},{14,16},{16,30},... | collective-permute-start | bytes 1572872 | tf_op jit(solution)/shard_map/ppermute | solution.py:46
  129.0 55.5 %collective-permute-start.13 = (bf16[2,128,1024]{2,1,0:T(8,128)(2,1)}, bf16[2,128,1024]{2,1,0:T(8,128)(2,1)S(1)}, u32[]{:S(2)}, u32[]{:S(2)}) collective-permute-start(bf16[2,128,1024]{2,1,0:T(8,128)(2,1)} %get-tuple-element.52), channel_id=1, source_target_pairs={{0,22},{2,20},{4,18},{6,16},{8,30},{10,28},{12,26},{14,24},{16,6},... | collective-permute-start | bytes 1572872 | tf_op jit(solution)/shard_map/ppermute | solution.py:46
  162.1 26.5 %collective-permute-start.14 = (bf16[2,128,1024]{2,1,0:T(8,128)(2,1)}, bf16[2,128,1024]{2,1,0:T(8,128)(2,1)S(1)}, u32[]{:S(2)}, u32[]{:S(2)}) collective-permute-start(bf16[2,128,1024]{2,1,0:T(8,128)(2,1)} %get-tuple-element.53), channel_id=1, source_target_pairs={{0,30},{2,28},{4,26},{6,24},{8,6},{10,4},{12,2},{14,0},{16,14},{18... | collective-permute-start | bytes 1572872 | tf_op jit(solution)/shard_map/ppermute | solution.py:46
  192.7 9.9 %collective-permute-start.18 = (bf16[16,4096]{1,0:T(8,128)(2,1)S(1)}, bf16[16,4096]{1,0:T(8,128)(2,1)S(1)}, u32[]{:S(2)}, u32[]{:S(2)}) collective-permute-start(bf16[16,4096]{1,0:T(8,128)(2,1)S(1)} %get-tuple-element.55.rest_0_), channel_id=1, source_target_pairs={{0,4},{2,6},{4,0},{6,2},{8,12},{10,14},{12,8},{14,10},{16,20},{18,... | collective-permute-start | bytes 393224 | tf_op jit(solution)/shard_map/ppermute | solution.py:46
  192.8 12.1 %collective-permute-start.17 = (bf16[16,4096]{1,0:T(8,128)(2,1)S(1)}, bf16[16,4096]{1,0:T(8,128)(2,1)S(1)}, u32[]{:S(2)}, u32[]{:S(2)}) collective-permute-start(bf16[16,4096]{1,0:T(8,128)(2,1)S(1)} %get-tuple-element.55.rest_0_), channel_id=1, source_target_pairs={{0,24},{2,26},{4,28},{6,30},{8,0},{10,2},{12,4},{14,6},{16,8},{18,... | collective-permute-start | bytes 393224 | tf_op jit(solution)/shard_map/ppermute | solution.py:46
  200.9 4.1 %collective-permute-start.22 = (bf16[16,4096]{1,0:T(8,128)(2,1)S(1)}, bf16[16,4096]{1,0:T(8,128)(2,1)S(1)}, u32[]{:S(2)}, u32[]{:S(2)}) collective-permute-start(bf16[16,4096]{1,0:T(8,128)(2,1)S(1)} %get-tuple-element.55.rest_0_), channel_id=1, source_target_pairs={{0,2},{2,0},{4,6},{6,4},{8,10},{10,8},{12,14},{14,12},{16,18},{18,... | collective-permute-start | bytes 393224 | tf_op jit(solution)/shard_map/ppermute | solution.py:46
  201.6 11.9 %collective-permute-start.16 = (bf16[16,4096]{1,0:T(8,128)(2,1)S(1)}, bf16[16,4096]{1,0:T(8,128)(2,1)S(1)}, u32[]{:S(2)}, u32[]{:S(2)}) collective-permute-start(bf16[16,4096]{1,0:T(8,128)(2,1)S(1)} %get-tuple-element.55.rest_0_), channel_id=1, source_target_pairs={{0,16},{2,18},{4,20},{6,22},{8,24},{10,26},{12,28},{14,30},{16,0},... | collective-permute-start | bytes 393224 | tf_op jit(solution)/shard_map/ppermute | solution.py:46
  201.6 13.7 %collective-permute-start.15 = (bf16[16,4096]{1,0:T(8,128)(2,1)S(1)}, bf16[16,4096]{1,0:T(8,128)(2,1)S(1)}, u32[]{:S(2)}, u32[]{:S(2)}) collective-permute-start(bf16[16,4096]{1,0:T(8,128)(2,1)S(1)} %get-tuple-element.55.rest_0_), channel_id=1, source_target_pairs={{0,8},{2,10},{4,12},{6,14},{8,16},{10,18},{12,20},{14,22},{16,24},... | collective-permute-start | bytes 393224 | tf_op jit(solution)/shard_map/ppermute | solution.py:46
  202.6 13.0 %collective-permute-start.26 = (bf16[16,4096]{1,0:T(8,128)(2,1)S(1)}, bf16[16,4096]{1,0:T(8,128)(2,1)S(1)}, u32[]{:S(2)}, u32[]{:S(2)}) collective-permute-start(bf16[16,4096]{1,0:T(8,128)(2,1)S(1)} %collective-permute-done.18.rest_4_), channel_id=1, source_target_pairs={{0,2},{2,0},{4,6},{6,4},{8,10},{10,8},{12,14},{14,12},{16,18},{18,... | collective-permute-start | bytes 393224 | tf_op jit(solution)/shard_map/ppermute | solution.py:46
  204.9 10.7 %collective-permute-start.25 = (bf16[16,4096]{1,0:T(8,128)(2,1)S(1)}, bf16[16,4096]{1,0:T(8,128)(2,1)S(1)}, u32[]{:S(2)}, u32[]{:S(2)}) collective-permute-start(bf16[16,4096]{1,0:T(8,128)(2,1)S(1)} %collective-permute-done.17.rest_3_), channel_id=1, source_target_pairs={{0,2},{2,0},{4,6},{6,4},{8,10},{10,8},{12,14},{14,12},{16,18},{18,... | collective-permute-start | bytes 393224 | tf_op jit(solution)/shard_map/ppermute | solution.py:46
  205.0 11.0 %collective-permute-start.21 = (bf16[16,4096]{1,0:T(8,128)(2,1)S(1)}, bf16[16,4096]{1,0:T(8,128)(2,1)S(1)}, u32[]{:S(2)}, u32[]{:S(2)}) collective-permute-start(bf16[16,4096]{1,0:T(8,128)(2,1)S(1)} %collective-permute-done.17.rest_3_), channel_id=1, source_target_pairs={{0,4},{2,6},{4,0},{6,2},{8,12},{10,14},{12,8},{14,10},{16,20},{18,... | collective-permute-start | bytes 393224 | tf_op jit(solution)/shard_map/ppermute | solution.py:46
  213.5 6.4 %collective-permute-start.20 = (bf16[16,4096]{1,0:T(8,128)(2,1)S(1)}, bf16[16,4096]{1,0:T(8,128)(2,1)S(1)}, u32[]{:S(2)}, u32[]{:S(2)}) collective-permute-start(bf16[16,4096]{1,0:T(8,128)(2,1)S(1)} %collective-permute-done.16.rest_2_), channel_id=1, source_target_pairs={{0,4},{2,6},{4,0},{6,2},{8,12},{10,14},{12,8},{14,10},{16,20},{18,... | collective-permute-start | bytes 393224 | tf_op jit(solution)/shard_map/ppermute | solution.py:46
  215.3 6.2 %collective-permute-start.19 = (bf16[16,4096]{1,0:T(8,128)(2,1)S(1)}, bf16[16,4096]{1,0:T(8,128)(2,1)S(1)}, u32[]{:S(2)}, u32[]{:S(2)}) collective-permute-start(bf16[16,4096]{1,0:T(8,128)(2,1)S(1)} %collective-permute-done.15.rest_1_), channel_id=1, source_target_pairs={{0,4},{2,6},{4,0},{6,2},{8,12},{10,14},{12,8},{14,10},{16,20},{18,... | collective-permute-start | bytes 393224 | tf_op jit(solution)/shard_map/ppermute | solution.py:46
  215.5 6.0 %collective-permute-start.24 = (bf16[16,4096]{1,0:T(8,128)(2,1)S(1)}, bf16[16,4096]{1,0:T(8,128)(2,1)S(1)}, u32[]{:S(2)}, u32[]{:S(2)}) collective-permute-start(bf16[16,4096]{1,0:T(8,128)(2,1)S(1)} %collective-permute-done.16.rest_2_), channel_id=1, source_target_pairs={{0,2},{2,0},{4,6},{6,4},{8,10},{10,8},{12,14},{14,12},{16,18},{18,... | collective-permute-start | bytes 393224 | tf_op jit(solution)/shard_map/ppermute | solution.py:46
  215.5 6.0 %collective-permute-start.23 = (bf16[16,4096]{1,0:T(8,128)(2,1)S(1)}, bf16[16,4096]{1,0:T(8,128)(2,1)S(1)}, u32[]{:S(2)}, u32[]{:S(2)}) collective-permute-start(bf16[16,4096]{1,0:T(8,128)(2,1)S(1)} %collective-permute-done.15.rest_1_), channel_id=1, source_target_pairs={{0,2},{2,0},{4,6},{6,4},{8,10},{10,8},{12,14},{14,12},{16,18},{18,... | collective-permute-start | bytes 393224 | tf_op jit(solution)/shard_map/ppermute | solution.py:46
  216.0 5.5 %collective-permute-start.29 = (bf16[16,4096]{1,0:T(8,128)(2,1)S(1)}, bf16[16,4096]{1,0:T(8,128)(2,1)S(1)}, u32[]{:S(2)}, u32[]{:S(2)}) collective-permute-start(bf16[16,4096]{1,0:T(8,128)(2,1)S(1)} %collective-permute-done.21.rest_7_), channel_id=1, source_target_pairs={{0,2},{2,0},{4,6},{6,4},{8,10},{10,8},{12,14},{14,12},{16,18},{18,... | collective-permute-start | bytes 393224 | tf_op jit(solution)/shard_map/ppermute | solution.py:46
  219.9 1.6 collective-permute-start.28
  221.5 1.3 collective-permute-start.27
  229.5 5.6 %collective-permute-start.30 = (bf16[128,512]{1,0:T(8,128)(2,1)S(1)}, bf16[128,512]{1,0:T(8,128)(2,1)S(1)}, u32[]{:S(2)}, u32[]{:S(2)}) collective-permute-start(bf16[128,512]{1,0:T(8,128)(2,1)S(1)} %get-tuple-element.57), channel_id=1, source_target_pairs={{0,1},{1,0},{2,3},{3,2},{4,5},{5,4},{6,7},{7,6},{8,9},{9,8},{10,11... | collective-permute-start | bytes 393224 | tf_op jit(solution)/shard_map/ppermute | solution.py:339

commit v4 on v3

v4 whole, which is shorter than its diff:
```python
import functools
import math

import jax
import jax.numpy as jnp
from jax import lax
from jax.experimental import pallas as pl
from jax.experimental.pallas import tpu as pltpu
from jax.sharding import PartitionSpec as P

HD = 128
MAX_PAGES = 2
WAVE = 3
ROW_UNROLL = 4
EARLY = 4
DEPTH = 512
VMEM_LIMIT = 48 * 1024 * 1024


def partner(me, code):
    return me ^ code


def send_by(array, code):
    groups = lax.axis_size("group")
    return lax.ppermute(array, "group", [(s, partner(s, code)) for s in range(groups)])


def page_codes(groups):
    near = min(4, groups)
    far = groups // near
    order = [z * near + n for n in range(near) for z in list(range(far // 2, far)) + list(range(far // 2)) if z * near + n]
    tail = order[-far:]
    return order[:-far] + tail[far // 2 :] + tail[: far // 2]


def gather_shards(shard):
    groups = lax.axis_size("group")
    held = {0: shard}
    near = min(4, groups)
    for codes in (range(groups - near, 0, -near), (2,), (1,)):
        incoming = {}
        for step in codes:
            for code, array in held.items():
                incoming[code | step] = send_by(array, step)
        held.update(incoming)
    return held


def prepare_kernel(codes, own, lengths_hbm, prefill_hbm, decode_hbm, pool, *rest):
    aliased = 0 if own else 1
    received, *sends = rest[aliased : aliased + 1 + len(codes)]
    lengths, prefill_of, decode_of, held, zero_page, start_of, count_of, table_sem, in_sems, out_sem = rest[
        aliased + 1 + len(codes) :
    ]
    me = lax.axis_index("group")
    groups = lax.axis_size("group")
    page_size = pool.shape[1]
    tables = [
        pltpu.make_async_copy(source, target, table_sem.at[i])
        for i, (source, target) in enumerate(
            [(lengths_hbm, lengths), (prefill_hbm, prefill_of), (decode_hbm, decode_of)]
        )
    ]
    for table in tables:
        table.start()
    for d in range(groups + 1):
        start_of[d] = 0
        count_of[d] = 0
    zero_page[...] = jnp.zeros_like(zero_page)
    for table in tables:
        table.wait()

    def visit(r, running):
        mine = prefill_of[r] == me
        count = (lengths[r] + page_size - 1) // page_size
        to = jnp.where(mine, decode_of[r], groups)
        start_of[to] = running
        count_of[to] = count
        return running + jnp.where(mine, count, 0)

    lax.fori_loop(0, lengths.shape[0], visit, jnp.int32(0), unroll=8)
    targets = [(partner(me, code), send, 0) for code, send in zip(codes, sends)]
    if own:
        targets.append((me, received, me * MAX_PAGES))

    def each(do):
        for i, (to, target, base) in enumerate(targets):
            for page in range(MAX_PAGES):
                there = page < count_of[to]
                source = pool.at[jnp.where(there, start_of[to] + page, 0)]
                buffer, place = held.at[i, page], target.at[base + page]
                do(there, (source, buffer, in_sems.at[i, page]), (buffer, place, out_sem), (zero_page, place, out_sem))

    def fetch(there, load, store, blank):
        @pl.when(there)
        def _():
            pltpu.make_async_copy(*load).start()

        @pl.when(jnp.logical_not(there))
        def _():
            pltpu.make_async_copy(*blank).start()

    def forward(there, load, store, blank):
        @pl.when(there)
        def _():
            pltpu.make_async_copy(*load).wait()
            pltpu.make_async_copy(*store).start()

    def finish(there, load, store, blank):
        pltpu.make_async_copy(*blank).wait()

    each(fetch)
    each(forward)
    each(finish)


def prepare(codes, lengths, prefill_of, decode_of, pool, received=None):
    own = received is None
    groups = lax.axis_size("group")
    page = pool.shape[1:]
    blocks = len(codes) + (1 if own else 0)
    hbm = pl.BlockSpec(memory_space=pl.ANY)
    block = jax.ShapeDtypeStruct((MAX_PAGES,) + page, pool.dtype)
    outs = [jax.ShapeDtypeStruct((groups * MAX_PAGES,) + page, pool.dtype)] + [block] * len(codes)
    operands = [lengths, prefill_of, decode_of, pool] + ([] if own else [received])
    table = pltpu.SMEM(lengths.shape, jnp.int32)
    return pl.pallas_call(
        functools.partial(prepare_kernel, codes, own),
        out_shape=outs,
        in_specs=[hbm] * len(operands),
        out_specs=[hbm] * len(outs),
        scratch_shapes=[
            table,
            table,
            table,
            pltpu.VMEM((blocks, MAX_PAGES) + page, pool.dtype),
            pltpu.VMEM(page, pool.dtype),
            pltpu.SMEM((groups + 1,), jnp.int32),
            pltpu.SMEM((groups + 1,), jnp.int32),
            pltpu.SemaphoreType.DMA((3,)),
            pltpu.SemaphoreType.DMA((blocks, MAX_PAGES)),
            pltpu.SemaphoreType.DMA,
        ],
        input_output_aliases={} if own else {4: 0},
        compiler_params=pltpu.CompilerParams(vmem_limit_bytes=VMEM_LIMIT),
        cost_estimate=pl.CostEstimate(
            flops=0, bytes_accessed=4 * blocks * MAX_PAGES * math.prod(page), transcendentals=0
        ),
        name="outgoing_pages",
    )(*operands)


def attend_row(query, pages, length):
    first, second = pages
    kv_heads = first.shape[1] // (2 * HD)
    share = query.shape[0] // kv_heads
    scores = []
    for h in range(kv_heads):
        columns = slice(2 * h * HD, (2 * h + 1) * HD)
        keys = jnp.concatenate([first[:, columns], second[:, columns]], axis=0)
        every = lax.dot_general(
            query, keys, (((1,), (1,)), ((), ())), preferred_element_type=jnp.float32
        )
        scores.append(every[h * share : (h + 1) * share])
    score = jnp.concatenate(scores, axis=0) * (1.0 / math.sqrt(HD))
    live = lax.broadcasted_iota(jnp.int32, score.shape, 1) < length
    masked = jnp.where(live, score, -1e30)
    highest = jnp.max(masked, axis=1, keepdims=True)
    weights = jnp.where(live, jnp.exp(masked - highest), 0.0)
    totals = jnp.sum(weights, axis=1, keepdims=True)
    rounded = weights.astype(jnp.bfloat16)
    mixtures = []
    for h in range(kv_heads):
        columns = slice((2 * h + 1) * HD, (2 * h + 2) * HD)
        values = jnp.concatenate([first[:, columns], second[:, columns]], axis=0)
        every = jnp.dot(rounded, values, preferred_element_type=jnp.float32)
        mixtures.append(every[h * share : (h + 1) * share])
    return jnp.concatenate(mixtures, axis=0) / totals


def settle_kernel(codes, own, last, lengths, prefill_of, row_request, queries, rows_in, received_in, *rest):
    blocks = rest[: len(codes)]
    received, out, rows, held, list_row, list_block, list_length, in_sems, out_sems = rest[len(codes) :]
    me = lax.axis_index("group")
    row_local, query_heads, _ = queries.shape
    mine = pl.ds(me * MAX_PAGES, MAX_PAGES)
    places = [pl.ds(partner(me, code) * MAX_PAGES, MAX_PAGES) for code in codes]
    sources = list(blocks) + ([received_in.at[mine]] if own else [])
    kinds = list(codes) + ([0] if own else [])
    loads = [pltpu.make_async_copy(s, held.at[i], in_sems.at[i]) for i, s in enumerate(sources)]
    stores = [
        pltpu.make_async_copy(held.at[i], received.at[place], out_sems.at[i]) for i, place in enumerate(places)
    ]
    for load in loads:
        load.start()

    found = jnp.int32(0)
    for b in range(row_local):
        request = row_request[me * row_local + b]
        kind = partner(me, prefill_of[request])
        block, match = jnp.int32(0), jnp.int32(0)
        for i, here in enumerate(kinds):
            block = jnp.where(kind == here, i, block)
            match = jnp.where(kind == here, 1, match)
        list_row[found] = b
        list_block[found] = block
        list_length[found] = lengths[request]
        found = found + match
    for i in range(ROW_UNROLL):
        list_row[found + i] = row_local
        list_block[found + i] = 0
        list_length[found + i] = 1
    rows[:row_local] = rows_in[...]
    for load in loads:
        load.wait()
    for store in stores:
        store.start()

    @pl.loop(0, (found + ROW_UNROLL - 1) // ROW_UNROLL)
    def _(step):
        results = []
        for i in range(ROW_UNROLL):
            at = step * ROW_UNROLL + i
            query = queries[jnp.minimum(list_row[at], row_local - 1)]
            pages = [held[list_block[at], page] for page in range(MAX_PAGES)]
            results.append(attend_row(query, pages, list_length[at]))
        for i, result in enumerate(results):
            rows[list_row[step * ROW_UNROLL + i]] = result

    if last:
        for h in range(query_heads):
            out[:, h * HD : (h + 1) * HD] = rows[:row_local, h, :].astype(out.dtype)
    else:
        out[...] = rows[:row_local]
    for store in stores:
        store.wait()


def settle(codes, own, last, tables, queries, rows, received, blocks):
    row_local, query_heads, _ = queries.shape
    smem = pl.BlockSpec(memory_space=pltpu.SMEM)
    vmem = pl.BlockSpec(memory_space=pltpu.VMEM)
    hbm = pl.BlockSpec(memory_space=pl.ANY)
    count = len(blocks) + (1 if own else 0)
    if last:
        out = jax.ShapeDtypeStruct((row_local, query_heads * HD), jnp.bfloat16)
    else:
        out = jax.ShapeDtypeStruct(rows.shape, rows.dtype)
    return pl.pallas_call(
        functools.partial(settle_kernel, codes, own, last),
        out_shape=[jax.ShapeDtypeStruct(received.shape, received.dtype), out],
        in_specs=[smem, smem, smem, vmem, vmem, hbm] + [hbm] * len(blocks),
        out_specs=[hbm, vmem],
        scratch_shapes=[
            pltpu.VMEM((row_local + 1, query_heads, HD), jnp.float32),
            pltpu.VMEM((count, MAX_PAGES) + received.shape[1:], received.dtype),
            pltpu.SMEM((row_local + ROW_UNROLL,), jnp.int32),
            pltpu.SMEM((row_local + ROW_UNROLL,), jnp.int32),
            pltpu.SMEM((row_local + ROW_UNROLL,), jnp.int32),
            pltpu.SemaphoreType.DMA((count,)),
            pltpu.SemaphoreType.DMA((count,)),
        ],
        input_output_aliases={5: 0},
        compiler_params=pltpu.CompilerParams(vmem_limit_bytes=VMEM_LIMIT),
        cost_estimate=pl.CostEstimate(
            flops=1 << 30, bytes_accessed=4 * sum(b.size for b in blocks), transcendentals=1 << 18
        ),
        name="settle_pages",
    )(*tables, queries, rows, received, *blocks)


def project_kernel(codes, out_weight, *rest):
    shards = rest[: len(codes)]
    own, *theirs = rest[len(codes) : -5]
    attended, weight, product, sems, weight_sems = rest[-5:]
    me = lax.axis_index("group")
    heads = lax.axis_size("head")
    my_head = lax.axis_index("head")
    row_local, width = shards[0].shape
    share = own.shape[0]
    copies = []
    for i, code in enumerate(codes):
        place = pl.ds(partner(me, code) * row_local, row_local)
        copies.append(pltpu.make_async_copy(shards[i], attended.at[place], sems.at[i]))
    loads = []
    for k in range(0, width, DEPTH):
        part = pl.ds(k, DEPTH)
        loads.append(pltpu.make_async_copy(out_weight.at[part], weight.at[part], weight_sems.at[k // DEPTH]))
    for copy in copies + loads:
        copy.start()
    for copy in copies:
        copy.wait()
    for k, load in zip(range(0, width, DEPTH), loads):
        load.wait()
        part = jnp.dot(
            attended[:, k : k + DEPTH], weight[k : k + DEPTH], preferred_element_type=jnp.float32
        )
        product[...] = part if k == 0 else product[...] + part
    own[...] = product[pl.ds(pl.multiple_of(my_head * share, share), share)]
    for ahead, target in enumerate(theirs, 1):
        start = pl.multiple_of(lax.rem(my_head + ahead, heads) * share, share)
        target[...] = product[pl.ds(start, share)].astype(target.dtype)


def project(gathered, out_weight, heads):
    codes = list(gathered)
    shards = [gathered[code] for code in codes]
    row_local, width = shards[0].shape
    row_total = row_local * len(shards)
    share, columns = row_total // heads, out_weight.shape[1]
    vmem = pl.BlockSpec(memory_space=pltpu.VMEM)
    hbm = pl.BlockSpec(memory_space=pl.ANY)
    theirs = jax.ShapeDtypeStruct((share, columns), jnp.bfloat16)
    return pl.pallas_call(
        functools.partial(project_kernel, codes),
        out_shape=[jax.ShapeDtypeStruct((share, columns), jnp.float32)] + [theirs] * (heads - 1),
        in_specs=[hbm] + [hbm] * len(shards),
        out_specs=[vmem] * heads,
        scratch_shapes=[
            pltpu.VMEM((row_total, width), jnp.bfloat16),
            pltpu.VMEM(out_weight.shape, jnp.bfloat16),
            pltpu.VMEM((row_total, columns), jnp.float32),
            pltpu.SemaphoreType.DMA((len(shards),)),
            pltpu.SemaphoreType.DMA((width // DEPTH,)),
        ],
        compiler_params=pltpu.CompilerParams(vmem_limit_bytes=VMEM_LIMIT),
        cost_estimate=pl.CostEstimate(
            flops=2 * row_total * width * columns, bytes_accessed=2 * out_weight.size, transcendentals=0
        ),
        name="project_rows",
    )(out_weight, *shards)


def local(kv_pool, lengths, prefill_of, decode_of, row_request, queries, out_weight):
    row_local, query_width = queries.shape
    query_heads = queries.reshape(row_local, query_width // HD, HD)
    heads = lax.axis_size("head")

    codes = page_codes(lax.axis_size("group"))
    pages = (lengths, prefill_of, decode_of, kv_pool)
    received, *early = prepare(codes[:EARLY], *pages)
    received, *late = prepare(codes[EARLY:], *pages, received)
    arrived = [send_by(block, code) for block, code in zip(early + late, codes)]
    rows = jnp.zeros(query_heads.shape, jnp.float32)
    tables = (lengths, prefill_of, row_request)
    for first in range(0, len(codes), WAVE):
        wave = slice(first, first + WAVE)
        last = first + WAVE >= len(codes)
        received, rows = settle(
            codes[wave], first == 0, last, tables, query_heads, rows, received, arrived[wave]
        )

    own, *theirs = project(gather_shards(rows), out_weight, heads)
    for ahead, part in enumerate(theirs, 1):
        pairs = [(h, (h + ahead) % heads) for h in range(heads)]
        own = own + lax.ppermute(part, "head", pairs).astype(jnp.float32)
    return (received, own.astype(jnp.bfloat16))


def solution(mesh):
    in_specs = (
        P("group", None, "head"),
        P(),
        P(),
        P(),
        P(),
        P("group", "head"),
        P("head", "group"),
    )
    out_specs = (P("group", None, "head"), P("head", "group"))
    assert mesh.shape["group"] & (mesh.shape["group"] - 1) == 0
    return jax.shard_map(local, mesh=mesh, in_specs=in_specs, out_specs=out_specs, check_vma=False)
```

time: 236 us -> 245 us (1.038)
  starting transfers between devices: 92 us -> 134 us
  waiting for transfers between devices: 111 us -> 77.7 us
    ppermute x30, starting transfers between devices: 90.4 us -> 133 us  [send_by(): lax.ppermute(array, 'group', [(s, partner(s, code)) for s in range(groups)])]
    ppermute x30, waiting for transfers between devices: 107 us -> 73.6 us  [send_by(): lax.ppermute(array, 'group', [(s, partner(s, code)) for s in range(groups)])]
    pallas_call x7 -> x8, Pallas kernels: 29.2 us -> 29.7 us  [the longest x5 13.5 us: settle(): pl.pallas_call(functools.partial(settle_kernel, codes, own, last), out_sh...]
  transfers between devices with their start and end apart: 31 -> 31, of which waited for: 12 -> 10; matrix products, arithmetic and copies ran while one was open for 0% -> 0% of each run, Pallas kernels for 5% -> 6%
where the time goes in v4:
time: 245 us
  starting transfers between devices  134 us (55%)
  waiting for transfers between devices  77.7 us (32%)
  Pallas kernels  29.7 us (12%)
    ppermute x30, starting transfers between devices, send_by(): lax.ppermute(array, 'group', [(s, partner(s, code)) for s in range(groups)])  133 us
    ppermute x30, waiting for transfers between devices, send_by(): lax.ppermute(array, 'group', [(s, partner(s, code)) for s in range(groups)])  73.6 us
    pallas_call x5, Pallas kernels, settle(): pl.pallas_call(functools.partial(settle_kernel, codes, own, last), out_sh...  13.5 us
    pallas_call x2, Pallas kernels, prepare(): pl.pallas_call(functools.partial(prepare_kernel, codes, own), out_shape=o...  10.3 us
    pallas_call x1, Pallas kernels, project(): pl.pallas_call(functools.partial(project_kernel, codes), out_shape=[jax.S...  5.95 us
  transfers between devices with their start and end apart: 31, of which 10 were waited for; matrix products, arithmetic and copies ran while one was open for 0% of the time, Pallas kernels for 6%

profile of v4, /device:TPU:0, one launch (start us, length us, event | category | flops | bytes accessed | tf_op | source)
XLA Modules:
  0.0 245.1 jit_solution(14160656163652728174)
XLA Ops:
  0.6 0.7 copy-done
  1.3 0.7 copy-done.1
  2.0 0.7 copy-done.3
  2.7 5.0 %outgoing_pages.2 = (bf16[32,128,1024]{2,1,0:T(8,128)(2,1)}, bf16[2,128,1024]{2,1,0:T(8,128)(2,1)S(1)}, bf16[2,128,1024]{2,1,0:T(8,128)(2,1)S(1)}, bf16[2,128,10...) custom-call(s32[256]{0:T(256)S(1)} %copy-done, s32[256]{0:T(256)S(1)} %copy-done.1, s32[256]{0:T(256)S(1)} %copy-done.3, ...), custom_call_target="tpu_custom_call" | custom-call | bytes 5242880 | tf_op jit(solution)/shard_map/outgoing_pages/pallas_call | solution.py:128
  7.6 4.2 %collective-permute-start = (bf16[2,128,1024]{2,1,0:T(8,128)(2,1)S(1)}, bf16[2,128,1024]{2,1,0:T(8,128)(2,1)S(1)}, u32[]{:S(2)}, u32[]{:S(2)}) collective-permute-start(bf16[2,128,1024]{2,1,0:T(8,128)(2,1)S(1)} %get-tuple-element.33), channel_id=1, source_target_pairs={{0,16},{2,18},{4,20},{6,22},{8,24},{10,26},{12,28},{14,30},{16,0},... | collective-permute-start | bytes 1572872 | tf_op jit(solution)/shard_map/ppermute | solution.py:26
  11.8 1.3 collective-permute-start.1
  13.1 0.2 collective-permute-start.2
  13.3 1.6 collective-permute-start.3
  15.0 5.3 %outgoing_pages.3 = (bf16[32,128,1024]{2,1,0:T(8,128)(2,1)}, bf16[2,128,1024]{2,1,0:T(8,128)(2,1)S(1)}, bf16[2,128,1024]{2,1,0:T(8,128)(2,1)S(1)}, bf16[2,128,10...) custom-call(s32[256]{0:T(256)S(1)} %copy-done, ...), custom_call_target="tpu_custom_call", output_to_operand_aliasing={{0}: (4, {})} | custom-call | bytes 11534336 | tf_op jit(solution)/shard_map/outgoing_pages/pallas_call | solution.py:128
  20.3 2.0 collective-permute-start.4
  22.3 25.6 %collective-permute-done.rest_0_ = bf16[2,128,1024]{2,1,0:T(8,128)(2,1)S(1)} collective-permute-done((bf16[2,128,1024]{2,1,0:T(8,128)(2,1)S(1)}, bf16[2,128,1024]{2,1,0:T(8,128)(2,1)S(1)}, u32[]{:S(2)}, u32[]{:S(2)}) %collective-permute-start) | collective-permute-done | bytes 524320 | tf_op jit(solution)/shard_map/ppermute | solution.py:26
  47.9 32.5 %collective-permute-start.6 = (bf16[2,128,1024]{2,1,0:T(8,128)(2,1)S(1)}, bf16[2,128,1024]{2,1,0:T(8,128)(2,1)S(1)}, u32[]{:S(2)}, u32[]{:S(2)}) collective-permute-start(bf16[2,128,1024]{2,1,0:T(8,128)(2,1)S(1)} %get-tuple-element.43), channel_id=1, source_target_pairs={{0,10},{2,8},{4,14},{6,12},{8,2},{10,0},{12,6},{14,4},{16,26},{18,... | collective-permute-start | bytes 1572872 | tf_op jit(solution)/shard_map/ppermute | solution.py:26
  80.4 3.3 %collective-permute-start.7 = (bf16[2,128,1024]{2,1,0:T(8,128)(2,1)S(1)}, bf16[2,128,1024]{2,1,0:T(8,128)(2,1)S(1)}, u32[]{:S(2)}, u32[]{:S(2)}) collective-permute-start(bf16[2,128,1024]{2,1,0:T(8,128)(2,1)S(1)} %get-tuple-element.44), channel_id=1, source_target_pairs={{0,20},{2,22},{4,16},{6,18},{8,28},{10,30},{12,24},{14,26},{16,4},... | collective-permute-start | bytes 1572872 | tf_op jit(solution)/shard_map/ppermute | solution.py:26
  83.7 7.1 %collective-permute-done.3.rest_0_ = bf16[2,128,1024]{2,1,0:T(8,128)(2,1)S(1)} collective-permute-done((bf16[2,128,1024]{2,1,0:T(8,128)(2,1)S(1)}, bf16[2,128,1024]{2,1,0:T(8,128)(2,1)S(1)}, u32[]{:S(2)}, u32[]{:S(2)}) %collective-permute-start.3) | collective-permute-done | bytes 524320 | tf_op jit(solution)/shard_map/ppermute | solution.py:26
  90.8 4.9 %collective-permute-start.8 = (bf16[2,128,1024]{2,1,0:T(8,128)(2,1)S(1)}, bf16[2,128,1024]{2,1,0:T(8,128)(2,1)S(1)}, u32[]{:S(2)}, u32[]{:S(2)}) collective-permute-start(bf16[2,128,1024]{2,1,0:T(8,128)(2,1)S(1)} %get-tuple-element.45), channel_id=1, source_target_pairs={{0,28},{2,30},{4,24},{6,26},{8,20},{10,22},{12,16},{14,18},{16,12}... | collective-permute-start | bytes 1572872 | tf_op jit(solution)/shard_map/ppermute | solution.py:26
  95.7 0.6 collective-permute-start.9
  96.3 31.1 %collective-permute-start.10 = (bf16[2,128,1024]{2,1,0:T(8,128)(2,1)S(1)}, bf16[2,128,1024]{2,1,0:T(8,128)(2,1)S(1)}, u32[]{:S(2)}, u32[]{:S(2)}) collective-permute-start(bf16[2,128,1024]{2,1,0:T(8,128)(2,1)S(1)} %get-tuple-element.49), channel_id=1, source_target_pairs={{0,12},{2,14},{4,8},{6,10},{8,4},{10,6},{12,0},{14,2},{16,28},{18,... | collective-permute-start | bytes 1572872 | tf_op jit(solution)/shard_map/ppermute | solution.py:26
  127.4 1.2 collective-permute-start.11
  128.6 9.9 %collective-permute-done.7.rest_1_ = bf16[2,128,1024]{2,1,0:T(8,128)(2,1)S(1)} collective-permute-done((bf16[2,128,1024]{2,1,0:T(8,128)(2,1)S(1)}, bf16[2,128,1024]{2,1,0:T(8,128)(2,1)S(1)}, u32[]{:S(2)}, u32[]{:S(2)}) %collective-permute-start.7) | collective-permute-done | bytes 524320 | tf_op jit(solution)/shard_map/ppermute | solution.py:26
  138.5 23.1 %collective-permute-start.13 = (bf16[2,128,1024]{2,1,0:T(8,128)(2,1)S(1)}, bf16[2,128,1024]{2,1,0:T(8,128)(2,1)S(1)}, u32[]{:S(2)}, u32[]{:S(2)}) collective-permute-start(bf16[2,128,1024]{2,1,0:T(8,128)(2,1)S(1)} %get-tuple-element.54), channel_id=1, source_target_pairs={{0,22},{2,20},{4,18},{6,16},{8,30},{10,28},{12,26},{14,24},{16,6},... | collective-permute-start | bytes 1572872 | tf_op jit(solution)/shard_map/ppermute | solution.py:26
  161.6 1.1 collective-permute-start.14
  162.7 3.1 %settle_pages.5 = (bf16[32,128,1024]{2,1,0:T(8,128)(2,1)}, f32[16,32,128]{2,1,0:T(8,128)S(1)}) custom-call(s32[256]{0:T(256)S(1)} %copy-done, s32[256]{0:T(256)S(1)} %copy-done.1, s32[256]{0:T(256)S(1)} %copy-done.2, bf16[16,32,128]{2,1,0:T(8,128)(2,1)S(1)} %bitcast.2, f32[16,32,128]{2,1,0:T(8,128)S(1)} %broadcast_in_dim.3.rows_in, ...), custom_call_target="tpu_custom_call", output_to_operand_aliasing={{0}: (5, {})} | custom-call | flops 1073741824 | bytes 3145728 | tf_op jit(solution)/shard_map/settle_pages/pallas_call | solution.py:250
  165.9 2.2 settle_pages.6
  168.1 2.2 settle_pages.7
  170.3 3.3 %collective-permute-done.11.rest_2_ = bf16[2,128,1024]{2,1,0:T(8,128)(2,1)S(1)} collective-permute-done((bf16[2,128,1024]{2,1,0:T(8,128)(2,1)S(1)}, bf16[2,128,1024]{2,1,0:T(8,128)(2,1)S(1)}, u32[]{:S(2)}, u32[]{:S(2)}) %collective-permute-start.11) | collective-permute-done | bytes 524320 | tf_op jit(solution)/shard_map/ppermute | solution.py:26
  173.6 2.2 settle_pages.8
  175.8 19.6 %collective-permute-done.13.rest_1_ = bf16[2,128,1024]{2,1,0:T(8,128)(2,1)S(1)} collective-permute-done((bf16[2,128,1024]{2,1,0:T(8,128)(2,1)S(1)}, bf16[2,128,1024]{2,1,0:T(8,128)(2,1)S(1)}, u32[]{:S(2)}, u32[]{:S(2)}) %collective-permute-start.13) | collective-permute-done | bytes 524320 | tf_op jit(solution)/shard_map/ppermute | solution.py:26
  195.4 3.7 %settle_pages.9 = (bf16[32,128,1024]{2,1,0:T(8,128)(2,1)}, bf16[16,4096]{1,0:T(8,128)(2,1)S(1)}) custom-call(s32[256]{0:T(256)S(1)} %copy-done, s32[256]{0:T(256)S(1)} %copy-done.1, s32[256]{0:T(256)S(1)} %copy-done.2, bf16[16,32,128]{2,1,0:T(8,128)(2,1)S(1)} %bitcast.6, ...), custom_call_target="tpu_custom_call", output_to_operand_aliasing={{0}: (5, {})} | custom-call | flops 1073741824 | bytes 3145728 | tf_op jit(solution)/shard_map/settle_pages/pallas_call | solution.py:250
  199.2 0.5 collective-permute-start.18
  199.6 11.8 %collective-permute-start.17 = (bf16[16,4096]{1,0:T(8,128)(2,1)S(1)}, bf16[16,4096]{1,0:T(8,128)(2,1)S(1)}, u32[]{:S(2)}, u32[]{:S(2)}) collective-permute-start(bf16[16,4096]{1,0:T(8,128)(2,1)S(1)} %get-tuple-element.57.rest_0_), channel_id=1, source_target_pairs={{0,8},{2,10},{4,12},{6,14},{8,0},{10,2},{12,4},{14,6},{16,24},{18,... | collective-permute-start | bytes 393224 | tf_op jit(solution)/shard_map/ppermute | solution.py:26
  211.4 0.2 collective-permute-start.22
  211.6 3.0 %collective-permute-start.16 = (bf16[16,4096]{1,0:T(8,128)(2,1)S(1)}, bf16[16,4096]{1,0:T(8,128)(2,1)S(1)}, u32[]{:S(2)}, u32[]{:S(2)}) collective-permute-start(bf16[16,4096]{1,0:T(8,128)(2,1)S(1)} %get-tuple-element.57.rest_0_), channel_id=1, source_target_pairs={{0,16},{2,18},{4,20},{6,22},{8,24},{10,26},{12,28},{14,30},{16,0},... | collective-permute-start | bytes 393224 | tf_op jit(solution)/shard_map/ppermute | solution.py:26
  214.7 1.2 collective-permute-start.15
  215.8 0.2 collective-permute-start.26
  216.0 0.3 collective-permute-start.25
  216.4 0.5 collective-permute-start.21
  216.9 1.7 collective-permute-done.16.rest_2_
  218.6 7.3 %collective-permute-start.20 = (bf16[16,4096]{1,0:T(8,128)(2,1)S(1)}, bf16[16,4096]{1,0:T(8,128)(2,1)S(1)}, u32[]{:S(2)}, u32[]{:S(2)}) collective-permute-start(bf16[16,4096]{1,0:T(8,128)(2,1)S(1)} %collective-permute-done.16.rest_2_), channel_id=1, source_target_pairs={{0,4},{2,6},{4,0},{6,2},{8,12},{10,14},{12,8},{14,10},{16,20},{18,... | collective-permute-start | bytes 393224 | tf_op jit(solution)/shard_map/ppermute | solution.py:26
  225.9 0.0 collective-permute-start.24
  226.0 0.5 collective-permute-start.23
  226.5 0.1 collective-permute-start.29
  226.5 3.6 %collective-permute-done.20.rest_6_ = bf16[16,4096]{1,0:T(8,128)(2,1)S(1)} collective-permute-done((bf16[16,4096]{1,0:T(8,128)(2,1)S(1)}, bf16[16,4096]{1,0:T(8,128)(2,1)S(1)}, u32[]{:S(2)}, u32[]{:S(2)}) %collective-permute-start.20) | collective-permute-done | bytes 131104 | tf_op jit(solution)/shard_map/ppermute | solution.py:26
  230.1 1.4 collective-permute-done.19.rest_5_
  231.6 1.3 collective-permute-done.27.rest_13_
  232.9 6.0 %project_rows.1 = (f32[128,512]{1,0:T(8,128)S(1)}, bf16[128,512]{1,0:T(8,128)(2,1)S(1)}) custom-call(bf16[4096,512]{1,0:T(8,128)(2,1)} %out_weight.1, bf16[16,4096]{1,0:T(8,128)(2,1)S(1)} %get-tuple-element.57.rest_0_, bf16[16,4096]{1,0:T(8,128)(2,1)S(1)} %collective-permute-done.15.rest_1_, bf16[16,4096]{1,0:T(8,128)(2,1)S(1)} %collective-permute-done.16.rest_2_, ...), custom_call_target="tpu_custom_call" | custom-call | flops 1073741824 | bytes 4194304 | tf_op jit(solution)/shard_map/project_rows/pallas_call | solution.py:315
  238.8 1.6 collective-permute-start.30
  240.4 4.1 %collective-permute-done.30 = bf16[128,512]{1,0:T(8,128)(2,1)S(1)} collective-permute-done((bf16[128,512]{1,0:T(8,128)(2,1)S(1)}, bf16[128,512]{1,0:T(8,128)(2,1)S(1)}, u32[]{:S(2)}, u32[]{:S(2)}) %collective-permute-start.30) | collective-permute-done | bytes 131104 | tf_op jit(solution)/shard_map/ppermute | solution.py:357
  244.4 0.7 add_convert_fusion
  (35 shorter events, 0.1 us)
Async XLA Ops:
  0.6 0.7 copy-start
  1.3 0.7 copy-start.1
  2.0 0.7 copy-start.3
  7.6 40.3 %collective-permute-start = (bf16[2,128,1024]{2,1,0:T(8,128)(2,1)S(1)}, bf16[2,128,1024]{2,1,0:T(8,128)(2,1)S(1)}, u32[]{:S(2)}, u32[]{:S(2)}) collective-permute-start(bf16[2,128,1024]{2,1,0:T(8,128)(2,1)S(1)} %get-tuple-element.33), channel_id=1, source_target_pairs={{0,16},{2,18},{4,20},{6,22},{8,24},{10,26},{12,28},{14,30},{16,0},... | collective-permute-start | bytes 1572872 | tf_op jit(solution)/shard_map/ppermute | solution.py:26
  11.8 36.1 %collective-permute-start.1 = (bf16[2,128,1024]{2,1,0:T(8,128)(2,1)S(1)}, bf16[2,128,1024]{2,1,0:T(8,128)(2,1)S(1)}, u32[]{:S(2)}, u32[]{:S(2)}) collective-permute-start(bf16[2,128,1024]{2,1,0:T(8,128)(2,1)S(1)} %get-tuple-element.34), channel_id=1, source_target_pairs={{0,24},{2,26},{4,28},{6,30},{8,16},{10,18},{12,20},{14,22},{16,8},... | collective-permute-start | bytes 1572872 | tf_op jit(solution)/shard_map/ppermute | solution.py:26
  13.1 67.3 %collective-permute-start.2 = (bf16[2,128,1024]{2,1,0:T(8,128)(2,1)S(1)}, bf16[2,128,1024]{2,1,0:T(8,128)(2,1)S(1)}, u32[]{:S(2)}, u32[]{:S(2)}) collective-permute-start(bf16[2,128,1024]{2,1,0:T(8,128)(2,1)S(1)} %get-tuple-element.35), channel_id=1, source_target_pairs={{0,8},{2,10},{4,12},{6,14},{8,0},{10,2},{12,4},{14,6},{16,24},{18,... | collective-permute-start | bytes 1572872 | tf_op jit(solution)/shard_map/ppermute | solution.py:26
  13.3 77.4 %collective-permute-start.3 = (bf16[2,128,1024]{2,1,0:T(8,128)(2,1)S(1)}, bf16[2,128,1024]{2,1,0:T(8,128)(2,1)S(1)}, u32[]{:S(2)}, u32[]{:S(2)}) collective-permute-start(bf16[2,128,1024]{2,1,0:T(8,128)(2,1)S(1)} %get-tuple-element.38), channel_id=1, source_target_pairs={{0,18},{2,16},{4,22},{6,20},{8,26},{10,24},{12,30},{14,28},{16,2},... | collective-permute-start | bytes 1572872 | tf_op jit(solution)/shard_map/ppermute | solution.py:26
  15.0 147.7 %copy-start.4 = (bf16[16,4096]{1,0:T(8,128)(2,1)S(1)}, bf16[16,4096]{1,0:T(8,128)(2,1)}, u32[]{:S(2)}) copy-start(bf16[16,4096]{1,0:T(8,128)(2,1)} %param.12) | copy-start | bytes 393220
  15.0 147.8 %copy-start.2 = (s32[256]{0:T(256)S(1)}, s32[256]{0:T(256)}, u32[]{:S(2)}) copy-start(s32[256]{0:T(256)} %row_request.9) | copy-start | bytes 3076
  20.3 75.4 %collective-permute-start.4 = (bf16[2,128,1024]{2,1,0:T(8,128)(2,1)S(1)}, bf16[2,128,1024]{2,1,0:T(8,128)(2,1)S(1)}, u32[]{:S(2)}, u32[]{:S(2)}) collective-permute-start(bf16[2,128,1024]{2,1,0:T(8,128)(2,1)S(1)} %get-tuple-element.39), channel_id=1, source_target_pairs={{0,26},{2,24},{4,30},{6,28},{8,18},{10,16},{12,22},{14,20},{16,10}... | collective-permute-start | bytes 1572872 | tf_op jit(solution)/shard_map/ppermute | solution.py:26
  47.9 48.4 %collective-permute-start.5 = (bf16[2,128,1024]{2,1,0:T(8,128)(2,1)S(1)}, bf16[2,128,1024]{2,1,0:T(8,128)(2,1)S(1)}, u32[]{:S(2)}, u32[]{:S(2)}) collective-permute-start(bf16[2,128,1024]{2,1,0:T(8,128)(2,1)S(1)} %get-tuple-element.40), channel_id=1, source_target_pairs={{0,2},{2,0},{4,6},{6,4},{8,10},{10,8},{12,14},{14,12},{16,18},{18,... | collective-permute-start | bytes 1572872 | tf_op jit(solution)/shard_map/ppermute | solution.py:26
  47.9 79.5 %collective-permute-start.6 = (bf16[2,128,1024]{2,1,0:T(8,128)(2,1)S(1)}, bf16[2,128,1024]{2,1,0:T(8,128)(2,1)S(1)}, u32[]{:S(2)}, u32[]{:S(2)}) collective-permute-start(bf16[2,128,1024]{2,1,0:T(8,128)(2,1)S(1)} %get-tuple-element.43), channel_id=1, source_target_pairs={{0,10},{2,8},{4,14},{6,12},{8,2},{10,0},{12,6},{14,4},{16,26},{18,... | collective-permute-start | bytes 1572872 | tf_op jit(solution)/shard_map/ppermute | solution.py:26
  80.4 58.1 %collective-permute-start.7 = (bf16[2,128,1024]{2,1,0:T(8,128)(2,1)S(1)}, bf16[2,128,1024]{2,1,0:T(8,128)(2,1)S(1)}, u32[]{:S(2)}, u32[]{:S(2)}) collective-permute-start(bf16[2,128,1024]{2,1,0:T(8,128)(2,1)S(1)} %get-tuple-element.44), channel_id=1, source_target_pairs={{0,20},{2,22},{4,16},{6,18},{8,28},{10,30},{12,24},{14,26},{16,4},... | collective-permute-start | bytes 1572872 | tf_op jit(solution)/shard_map/ppermute | solution.py:26
  90.8 47.7 %collective-permute-start.8 = (bf16[2,128,1024]{2,1,0:T(8,128)(2,1)S(1)}, bf16[2,128,1024]{2,1,0:T(8,128)(2,1)S(1)}, u32[]{:S(2)}, u32[]{:S(2)}) collective-permute-start(bf16[2,128,1024]{2,1,0:T(8,128)(2,1)S(1)} %get-tuple-element.45), channel_id=1, source_target_pairs={{0,28},{2,30},{4,24},{6,26},{8,20},{10,22},{12,16},{14,18},{16,12}... | collective-permute-start | bytes 1572872 | tf_op jit(solution)/shard_map/ppermute | solution.py:26
  95.7 65.9 %collective-permute-start.9 = (bf16[2,128,1024]{2,1,0:T(8,128)(2,1)S(1)}, bf16[2,128,1024]{2,1,0:T(8,128)(2,1)S(1)}, u32[]{:S(2)}, u32[]{:S(2)}) collective-permute-start(bf16[2,128,1024]{2,1,0:T(8,128)(2,1)S(1)} %get-tuple-element.48), channel_id=1, source_target_pairs={{0,4},{2,6},{4,0},{6,2},{8,12},{10,14},{12,8},{14,10},{16,20},{18,... | collective-permute-start | bytes 1572872 | tf_op jit(solution)/shard_map/ppermute | solution.py:26
  96.3 74.0 %collective-permute-start.10 = (bf16[2,128,1024]{2,1,0:T(8,128)(2,1)S(1)}, bf16[2,128,1024]{2,1,0:T(8,128)(2,1)S(1)}, u32[]{:S(2)}, u32[]{:S(2)}) collective-permute-start(bf16[2,128,1024]{2,1,0:T(8,128)(2,1)S(1)} %get-tuple-element.49), channel_id=1, source_target_pairs={{0,12},{2,14},{4,8},{6,10},{8,4},{10,6},{12,0},{14,2},{16,28},{18,... | collective-permute-start | bytes 1572872 | tf_op jit(solution)/shard_map/ppermute | solution.py:26
  127.4 46.2 %collective-permute-start.11 = (bf16[2,128,1024]{2,1,0:T(8,128)(2,1)S(1)}, bf16[2,128,1024]{2,1,0:T(8,128)(2,1)S(1)}, u32[]{:S(2)}, u32[]{:S(2)}) collective-permute-start(bf16[2,128,1024]{2,1,0:T(8,128)(2,1)S(1)} %get-tuple-element.50), channel_id=1, source_target_pairs={{0,6},{2,4},{4,2},{6,0},{8,14},{10,12},{12,10},{14,8},{16,22},{18,... | collective-permute-start | bytes 1572872 | tf_op jit(solution)/shard_map/ppermute | solution.py:26
  138.5 37.3 %collective-permute-start.12 = (bf16[2,128,1024]{2,1,0:T(8,128)(2,1)S(1)}, bf16[2,128,1024]{2,1,0:T(8,128)(2,1)S(1)}, u32[]{:S(2)}, u32[]{:S(2)}) collective-permute-start(bf16[2,128,1024]{2,1,0:T(8,128)(2,1)S(1)} %get-tuple-element.53), channel_id=1, source_target_pairs={{0,14},{2,12},{4,10},{6,8},{8,6},{10,4},{12,2},{14,0},{16,30},{18,... | collective-permute-start | bytes 1572872 | tf_op jit(solution)/shard_map/ppermute | solution.py:26
  138.5 56.9 %collective-permute-start.13 = (bf16[2,128,1024]{2,1,0:T(8,128)(2,1)S(1)}, bf16[2,128,1024]{2,1,0:T(8,128)(2,1)S(1)}, u32[]{:S(2)}, u32[]{:S(2)}) collective-permute-start(bf16[2,128,1024]{2,1,0:T(8,128)(2,1)S(1)} %get-tuple-element.54), channel_id=1, source_target_pairs={{0,22},{2,20},{4,18},{6,16},{8,30},{10,28},{12,26},{14,24},{16,6},... | collective-permute-start | bytes 1572872 | tf_op jit(solution)/shard_map/ppermute | solution.py:26
  161.6 33.8 %collective-permute-start.14 = (bf16[2,128,1024]{2,1,0:T(8,128)(2,1)S(1)}, bf16[2,128,1024]{2,1,0:T(8,128)(2,1)S(1)}, u32[]{:S(2)}, u32[]{:S(2)}) collective-permute-start(bf16[2,128,1024]{2,1,0:T(8,128)(2,1)S(1)} %get-tuple-element.55), channel_id=1, source_target_pairs={{0,30},{2,28},{4,26},{6,24},{8,22},{10,20},{12,18},{14,16},{16,14}... | collective-permute-start | bytes 1572872 | tf_op jit(solution)/shard_map/ppermute | solution.py:26
  199.2 16.7 %collective-permute-start.18 = (bf16[16,4096]{1,0:T(8,128)(2,1)S(1)}, bf16[16,4096]{1,0:T(8,128)(2,1)S(1)}, u32[]{:S(2)}, u32[]{:S(2)}) collective-permute-start(bf16[16,4096]{1,0:T(8,128)(2,1)S(1)} %get-tuple-element.57.rest_0_), channel_id=1, source_target_pairs={{0,4},{2,6},{4,0},{6,2},{8,12},{10,14},{12,8},{14,10},{16,20},{18,... | collective-permute-start | bytes 393224 | tf_op jit(solution)/shard_map/ppermute | solution.py:26
  199.6 16.4 %collective-permute-start.17 = (bf16[16,4096]{1,0:T(8,128)(2,1)S(1)}, bf16[16,4096]{1,0:T(8,128)(2,1)S(1)}, u32[]{:S(2)}, u32[]{:S(2)}) collective-permute-start(bf16[16,4096]{1,0:T(8,128)(2,1)S(1)} %get-tuple-element.57.rest_0_), channel_id=1, source_target_pairs={{0,8},{2,10},{4,12},{6,14},{8,0},{10,2},{12,4},{14,6},{16,24},{18,... | collective-permute-start | bytes 393224 | tf_op jit(solution)/shard_map/ppermute | solution.py:26
  211.4 4.9 %collective-permute-start.22 = (bf16[16,4096]{1,0:T(8,128)(2,1)S(1)}, bf16[16,4096]{1,0:T(8,128)(2,1)S(1)}, u32[]{:S(2)}, u32[]{:S(2)}) collective-permute-start(bf16[16,4096]{1,0:T(8,128)(2,1)S(1)} %get-tuple-element.57.rest_0_), channel_id=1, source_target_pairs={{0,2},{2,0},{4,6},{6,4},{8,10},{10,8},{12,14},{14,12},{16,18},{18,... | collective-permute-start | bytes 393224 | tf_op jit(solution)/shard_map/ppermute | solution.py:26
  211.6 7.0 %collective-permute-start.16 = (bf16[16,4096]{1,0:T(8,128)(2,1)S(1)}, bf16[16,4096]{1,0:T(8,128)(2,1)S(1)}, u32[]{:S(2)}, u32[]{:S(2)}) collective-permute-start(bf16[16,4096]{1,0:T(8,128)(2,1)S(1)} %get-tuple-element.57.rest_0_), channel_id=1, source_target_pairs={{0,16},{2,18},{4,20},{6,22},{8,24},{10,26},{12,28},{14,30},{16,0},... | collective-permute-start | bytes 393224 | tf_op jit(solution)/shard_map/ppermute | solution.py:26
  214.7 11.2 %collective-permute-start.15 = (bf16[16,4096]{1,0:T(8,128)(2,1)S(1)}, bf16[16,4096]{1,0:T(8,128)(2,1)S(1)}, u32[]{:S(2)}, u32[]{:S(2)}) collective-permute-start(bf16[16,4096]{1,0:T(8,128)(2,1)S(1)} %get-tuple-element.57.rest_0_), channel_id=1, source_target_pairs={{0,24},{2,26},{4,28},{6,30},{8,16},{10,18},{12,20},{14,22},{16,8},... | collective-permute-start | bytes 393224 | tf_op jit(solution)/shard_map/ppermute | solution.py:26
  215.8 10.1 %collective-permute-start.26 = (bf16[16,4096]{1,0:T(8,128)(2,1)S(1)}, bf16[16,4096]{1,0:T(8,128)(2,1)S(1)}, u32[]{:S(2)}, u32[]{:S(2)}) collective-permute-start(bf16[16,4096]{1,0:T(8,128)(2,1)S(1)} %collective-permute-done.18.rest_4_), channel_id=1, source_target_pairs={{0,2},{2,0},{4,6},{6,4},{8,10},{10,8},{12,14},{14,12},{16,18},{18,... | collective-permute-start | bytes 393224 | tf_op jit(solution)/shard_map/ppermute | solution.py:26
  216.0 9.9 %collective-permute-start.25 = (bf16[16,4096]{1,0:T(8,128)(2,1)S(1)}, bf16[16,4096]{1,0:T(8,128)(2,1)S(1)}, u32[]{:S(2)}, u32[]{:S(2)}) collective-permute-start(bf16[16,4096]{1,0:T(8,128)(2,1)S(1)} %collective-permute-done.17.rest_3_), channel_id=1, source_target_pairs={{0,2},{2,0},{4,6},{6,4},{8,10},{10,8},{12,14},{14,12},{16,18},{18,... | collective-permute-start | bytes 393224 | tf_op jit(solution)/shard_map/ppermute | solution.py:26
  216.4 10.1 %collective-permute-start.21 = (bf16[16,4096]{1,0:T(8,128)(2,1)S(1)}, bf16[16,4096]{1,0:T(8,128)(2,1)S(1)}, u32[]{:S(2)}, u32[]{:S(2)}) collective-permute-start(bf16[16,4096]{1,0:T(8,128)(2,1)S(1)} %collective-permute-done.17.rest_3_), channel_id=1, source_target_pairs={{0,4},{2,6},{4,0},{6,2},{8,12},{10,14},{12,8},{14,10},{16,20},{18,... | collective-permute-start | bytes 393224 | tf_op jit(solution)/shard_map/ppermute | solution.py:26
  218.6 11.6 %collective-permute-start.20 = (bf16[16,4096]{1,0:T(8,128)(2,1)S(1)}, bf16[16,4096]{1,0:T(8,128)(2,1)S(1)}, u32[]{:S(2)}, u32[]{:S(2)}) collective-permute-start(bf16[16,4096]{1,0:T(8,128)(2,1)S(1)} %collective-permute-done.16.rest_2_), channel_id=1, source_target_pairs={{0,4},{2,6},{4,0},{6,2},{8,12},{10,14},{12,8},{14,10},{16,20},{18,... | collective-permute-start | bytes 393224 | tf_op jit(solution)/shard_map/ppermute | solution.py:26
  225.9 5.7 %collective-permute-start.19 = (bf16[16,4096]{1,0:T(8,128)(2,1)S(1)}, bf16[16,4096]{1,0:T(8,128)(2,1)S(1)}, u32[]{:S(2)}, u32[]{:S(2)}) collective-permute-start(bf16[16,4096]{1,0:T(8,128)(2,1)S(1)} %collective-permute-done.15.rest_1_), channel_id=1, source_target_pairs={{0,4},{2,6},{4,0},{6,2},{8,12},{10,14},{12,8},{14,10},{16,20},{18,... | collective-permute-start | bytes 393224 | tf_op jit(solution)/shard_map/ppermute | solution.py:26
  225.9 5.6 %collective-permute-start.24 = (bf16[16,4096]{1,0:T(8,128)(2,1)S(1)}, bf16[16,4096]{1,0:T(8,128)(2,1)S(1)}, u32[]{:S(2)}, u32[]{:S(2)}) collective-permute-start(bf16[16,4096]{1,0:T(8,128)(2,1)S(1)} %collective-permute-done.16.rest_2_), channel_id=1, source_target_pairs={{0,2},{2,0},{4,6},{6,4},{8,10},{10,8},{12,14},{14,12},{16,18},{18,... | collective-permute-start | bytes 393224 | tf_op jit(solution)/shard_map/ppermute | solution.py:26
  226.0 5.6 %collective-permute-start.23 = (bf16[16,4096]{1,0:T(8,128)(2,1)S(1)}, bf16[16,4096]{1,0:T(8,128)(2,1)S(1)}, u32[]{:S(2)}, u32[]{:S(2)}) collective-permute-start(bf16[16,4096]{1,0:T(8,128)(2,1)S(1)} %collective-permute-done.15.rest_1_), channel_id=1, source_target_pairs={{0,2},{2,0},{4,6},{6,4},{8,10},{10,8},{12,14},{14,12},{16,18},{18,... | collective-permute-start | bytes 393224 | tf_op jit(solution)/shard_map/ppermute | solution.py:26
  226.5 5.1 %collective-permute-start.29 = (bf16[16,4096]{1,0:T(8,128)(2,1)S(1)}, bf16[16,4096]{1,0:T(8,128)(2,1)S(1)}, u32[]{:S(2)}, u32[]{:S(2)}) collective-permute-start(bf16[16,4096]{1,0:T(8,128)(2,1)S(1)} %collective-permute-done.21.rest_7_), channel_id=1, source_target_pairs={{0,2},{2,0},{4,6},{6,4},{8,10},{10,8},{12,14},{14,12},{16,18},{18,... | collective-permute-start | bytes 393224 | tf_op jit(solution)/shard_map/ppermute | solution.py:26
  230.1 1.4 collective-permute-start.28
  231.5 1.3 collective-permute-start.27
  238.8 5.6 %collective-permute-start.30 = (bf16[128,512]{1,0:T(8,128)(2,1)S(1)}, bf16[128,512]{1,0:T(8,128)(2,1)S(1)}, u32[]{:S(2)}, u32[]{:S(2)}) collective-permute-start(bf16[128,512]{1,0:T(8,128)(2,1)S(1)} %get-tuple-element.59), channel_id=1, source_target_pairs={{0,1},{1,0},{2,3},{3,2},{4,5},{5,4},{6,7},{7,6},{8,9},{9,8},{10,11... | collective-permute-start | bytes 393224 | tf_op jit(solution)/shard_map/ppermute | solution.py:357

commit v5 on v4

--- a/solution.py
+++ b/solution.py
@@ -17,41 +17,64 @@
 VMEM_LIMIT = 48 * 1024 * 1024
 
 
-def partner(me, code):
-    return me ^ code
-
-
-def send_by(array, code):
-    groups = lax.axis_size("group")
-    return lax.ppermute(array, "group", [(s, partner(s, code)) for s in range(groups)])
-
-
-def page_codes(groups):
-    near = min(4, groups)
-    far = groups // near
-    order = [z * near + n for n in range(near) for z in list(range(far // 2, far)) + list(range(far // 2)) if z * near + n]
-    tail = order[-far:]
-    return order[:-far] + tail[far // 2 :] + tail[: far // 2]
-
-
-def gather_shards(shard):
-    groups = lax.axis_size("group")
-    held = {0: shard}
-    near = min(4, groups)
-    for codes in (range(groups - near, 0, -near), (2,), (1,)):
+def factors(groups):
+    near = math.gcd(groups, 4)
+    return groups // near, near
+
+
+def ahead(me, offset, dims, sign=1):
+    far, near = dims
+    return lax.rem(me // near + sign * offset[0] + far, far) * near + (me % near ^ offset[1])
+
+
+def behind(me, offset, dims):
+    return ahead(me, offset, dims, -1)
+
+
+def kind_of(offset, dims):
+    return offset[0] * dims[1] + offset[1]
+
+
+def kind_behind(me, other, dims):
+    far, near = dims
+    return lax.rem(me // near - other // near + far, far) * near + (me % near ^ other % near)
+
+
+def send_by(array, offset, dims):
+    far, near = dims
+    pairs = [
+        (s, (s // near + offset[0]) % far * near + (s % near ^ offset[1])) for s in range(far * near)
+    ]
+    return lax.ppermute(array, "group", pairs)
+
+
+def page_offsets(dims):
+    far, near = dims
+    steps = sorted(range(1, far), key=lambda z: (min(z, far - z), z))
+    order = [(z, n) for z in steps for n in range(near)]
+    for n in range(1, near):
+        order.insert(min(2 * n, len(order)), (0, n))
+    return order
+
+
+def gather_shards(shard, dims):
+    far, near = dims
+    held = {(0, 0): shard}
+    swaps = [1 << i for i in reversed(range(near.bit_length() - 1))]
+    for stage in [[(z, 0) for z in range(1, far)]] + [[(0, n)] for n in swaps]:
         incoming = {}
-        for step in codes:
-            for code, array in held.items():
-                incoming[code | step] = send_by(array, step)
+        for step in stage:
+            for offset, array in held.items():
+                incoming[offset[0] + step[0], offset[1] | step[1]] = send_by(array, step, dims)
         held.update(incoming)
     return held
 
 
-def prepare_kernel(codes, own, lengths_hbm, prefill_hbm, decode_hbm, pool, *rest):
+def prepare_kernel(dims, offsets, own, lengths_hbm, prefill_hbm, decode_hbm, pool, *rest):
     aliased = 0 if own else 1
-    received, *sends = rest[aliased : aliased + 1 + len(codes)]
+    received, *sends = rest[aliased : aliased + 1 + len(offsets)]
     lengths, prefill_of, decode_of, held, zero_page, start_of, count_of, table_sem, in_sems, out_sem = rest[
-        aliased + 1 + len(codes) :
+        aliased + 1 + len(offsets) :
     ]
     me = lax.axis_index("group")
     groups = lax.axis_size("group")
@@ -80,7 +103,7 @@
         return running + jnp.where(mine, count, 0)
 
     lax.fori_loop(0, lengths.shape[0], visit, jnp.int32(0), unroll=8)
-    targets = [(partner(me, code), send, 0) for code, send in zip(codes, sends)]
+    targets = [(ahead(me, offset, dims), send, 0) for offset, send in zip(offsets, sends)]
     if own:
         targets.append((me, received, me * MAX_PAGES))
 
@@ -115,18 +138,18 @@
     each(finish)
 
 
-def prepare(codes, lengths, prefill_of, decode_of, pool, received=None):
+def prepare(dims, offsets, lengths, prefill_of, decode_of, pool, received=None):
     own = received is None
     groups = lax.axis_size("group")
     page = pool.shape[1:]
-    blocks = len(codes) + (1 if own else 0)
+    blocks = len(offsets) + (1 if own else 0)
     hbm = pl.BlockSpec(memory_space=pl.ANY)
     block = jax.ShapeDtypeStruct((MAX_PAGES,) + page, pool.dtype)
-    outs = [jax.ShapeDtypeStruct((groups * MAX_PAGES,) + page, pool.dtype)] + [block] * len(codes)
+    outs = [jax.ShapeDtypeStruct((groups * MAX_PAGES,) + page, pool.dtype)] + [block] * len(offsets)
     operands = [lengths, prefill_of, decode_of, pool] + ([] if own else [received])
     table = pltpu.SMEM(lengths.shape, jnp.int32)
     return pl.pallas_call(
-        functools.partial(prepare_kernel, codes, own),
+        functools.partial(prepare_kernel, dims, offsets, own),
         out_shape=outs,
         in_specs=[hbm] * len(operands),
         out_specs=[hbm] * len(outs),
@@ -179,15 +202,15 @@
     return jnp.concatenate(mixtures, axis=0) / totals
 
 
-def settle_kernel(codes, own, last, lengths, prefill_of, row_request, queries, rows_in, received_in, *rest):
-    blocks = rest[: len(codes)]
-    received, out, rows, held, list_row, list_block, list_length, in_sems, out_sems = rest[len(codes) :]
+def settle_kernel(dims, offsets, own, last, lengths, prefill_of, row_request, queries, rows_in, received_in, *rest):
+    blocks = rest[: len(offsets)]
+    received, out, rows, held, list_row, list_block, list_length, in_sems, out_sems = rest[len(offsets) :]
     me = lax.axis_index("group")
     row_local, query_heads, _ = queries.shape
     mine = pl.ds(me * MAX_PAGES, MAX_PAGES)
-    places = [pl.ds(partner(me, code) * MAX_PAGES, MAX_PAGES) for code in codes]
+    places = [pl.ds(behind(me, offset, dims) * MAX_PAGES, MAX_PAGES) for offset in offsets]
     sources = list(blocks) + ([received_in.at[mine]] if own else [])
-    kinds = list(codes) + ([0] if own else [])
+    kinds = [kind_of(offset, dims) for offset in offsets] + ([0] if own else [])
     loads = [pltpu.make_async_copy(s, held.at[i], in_sems.at[i]) for i, s in enumerate(sources)]
     stores = [
         pltpu.make_async_copy(held.at[i], received.at[place], out_sems.at[i]) for i, place in enumerate(places)
@@ -198,7 +221,7 @@
     found = jnp.int32(0)
     for b in range(row_local):
         request = row_request[me * row_local + b]
-        kind = partner(me, prefill_of[request])
+        kind = kind_behind(me, prefill_of[request], dims)
         block, match = jnp.int32(0), jnp.int32(0)
         for i, here in enumerate(kinds):
             block = jnp.where(kind == here, i, block)
@@ -237,7 +260,7 @@
         store.wait()
 
 
-def settle(codes, own, last, tables, queries, rows, received, blocks):
+def settle(dims, offsets, own, last, tables, queries, rows, received, blocks):
     row_local, query_heads, _ = queries.shape
     smem = pl.BlockSpec(memory_space=pltpu.SMEM)
     vmem = pl.BlockSpec(memory_space=pltpu.VMEM)
@@ -248,7 +271,7 @@
     else:
         out = jax.ShapeDtypeStruct(rows.shape, rows.dtype)
     return pl.pallas_call(
-        functools.partial(settle_kernel, codes, own, last),
+        functools.partial(settle_kernel, dims, offsets, own, last),
         out_shape=[jax.ShapeDtypeStruct(received.shape, received.dtype), out],
         in_specs=[smem, smem, smem, vmem, vmem, hbm] + [hbm] * len(blocks),
         out_specs=[hbm, vmem],
@@ -270,9 +293,9 @@
     )(*tables, queries, rows, received, *blocks)
 
 
-def project_kernel(codes, out_weight, *rest):
-    shards = rest[: len(codes)]
-    own, *theirs = rest[len(codes) : -5]
+def project_kernel(dims, offsets, out_weight, *rest):
+    shards = rest[: len(offsets)]
+    own, *theirs = rest[len(offsets) : -5]
     attended, weight, product, sems, weight_sems = rest[-5:]
     me = lax.axis_index("group")
     heads = lax.axis_size("head")
@@ -280,8 +303,8 @@
     row_local, width = shards[0].shape
     share = own.shape[0]
     copies = []
-    for i, code in enumerate(codes):
-        place = pl.ds(partner(me, code) * row_local, row_local)
+    for i, offset in enumerate(offsets):
+        place = pl.ds(behind(me, offset, dims) * row_local, row_local)
         copies.append(pltpu.make_async_copy(shards[i], attended.at[place], sems.at[i]))
     loads = []
     for k in range(0, width, DEPTH):
@@ -303,9 +326,9 @@
         target[...] = product[pl.ds(start, share)].astype(target.dtype)
 
 
-def project(gathered, out_weight, heads):
-    codes = list(gathered)
-    shards = [gathered[code] for code in codes]
+def project(dims, gathered, out_weight, heads):
+    offsets = list(gathered)
+    shards = [gathered[offset] for offset in offsets]
     row_local, width = shards[0].shape
     row_total = row_local * len(shards)
     share, columns = row_total // heads, out_weight.shape[1]
@@ -313,7 +336,7 @@
     hbm = pl.BlockSpec(memory_space=pl.ANY)
     theirs = jax.ShapeDtypeStruct((share, columns), jnp.bfloat16)
     return pl.pallas_call(
-        functools.partial(project_kernel, codes),
+        functools.partial(project_kernel, dims, offsets),
         out_shape=[jax.ShapeDtypeStruct((share, columns), jnp.float32)] + [theirs] * (heads - 1),
         in_specs=[hbm] + [hbm] * len(shards),
         out_specs=[vmem] * heads,
@@ -337,21 +360,22 @@
     query_heads = queries.reshape(row_local, query_width // HD, HD)
     heads = lax.axis_size("head")
 
-    codes = page_codes(lax.axis_size("group"))
+    dims = factors(lax.axis_size("group"))
+    offsets = page_offsets(dims)
     pages = (lengths, prefill_of, decode_of, kv_pool)
-    received, *early = prepare(codes[:EARLY], *pages)
-    received, *late = prepare(codes[EARLY:], *pages, received)
-    arrived = [send_by(block, code) for block, code in zip(early + late, codes)]
+    received, *early = prepare(dims, offsets[:EARLY], *pages)
+    received, *late = prepare(dims, offsets[EARLY:], *pages, received)
+    arrived = [send_by(block, offset, dims) for block, offset in zip(early + late, offsets)]
     rows = jnp.zeros(query_heads.shape, jnp.float32)
     tables = (lengths, prefill_of, row_request)
-    for first in range(0, len(codes), WAVE):
+    for first in range(0, len(offsets), WAVE):
         wave = slice(first, first + WAVE)
-        last = first + WAVE >= len(codes)
+        last = first + WAVE >= len(offsets)
         received, rows = settle(
-            codes[wave], first == 0, last, tables, query_heads, rows, received, arrived[wave]
+            dims, offsets[wave], first == 0, last, tables, query_heads, rows, received, arrived[wave]
         )
 
-    own, *theirs = project(gather_shards(rows), out_weight, heads)
+    own, *theirs = project(dims, gather_shards(rows, dims), out_weight, heads)
     for ahead, part in enumerate(theirs, 1):
         pairs = [(h, (h + ahead) % heads) for h in range(heads)]
         own = own + lax.ppermute(part, "head", pairs).astype(jnp.float32)
@@ -369,5 +393,4 @@
         P("head", "group"),
     )
     out_specs = (P("group", None, "head"), P("head", "group"))
-    assert mesh.shape["group"] & (mesh.shape["group"] - 1) == 0
     return jax.shard_map(local, mesh=mesh, in_specs=in_specs, out_specs=out_specs, check_vma=False)

time: 245 us -> 238 us (0.971)
  starting transfers between devices: 134 us -> 80.7 us
  waiting for transfers between devices: 77.7 us -> 124 us
    ppermute x30, starting transfers between devices: 133 us -> 79.1 us  [send_by(): return lax.ppermute(array, 'group', pairs)]
    ppermute x30, waiting for transfers between devices: 73.6 us -> 119 us  [send_by(): return lax.ppermute(array, 'group', pairs)]
  transfers between devices with their start and end apart: 31 -> 31, of which waited for: 10 -> 14; matrix products, arithmetic and copies ran while one was open for 0% -> 0% of each run, Pallas kernels for 6% -> 7%
where the time goes in v5:
time: 238 us
  waiting for transfers between devices  124 us (52%)
  starting transfers between devices  80.7 us (34%)
  Pallas kernels  30.1 us (13%)
    ppermute x30, waiting for transfers between devices, send_by(): return lax.ppermute(array, 'group', pairs)  119 us
    ppermute x30, starting transfers between devices, send_by(): return lax.ppermute(array, 'group', pairs)  79.1 us
    pallas_call x5, Pallas kernels, settle(): pl.pallas_call(functools.partial(settle_kernel, dims, offsets, own, last)...  14 us
    pallas_call x2, Pallas kernels, prepare(): pl.pallas_call(functools.partial(prepare_kernel, dims, offsets, own), out...  10.1 us
    pallas_call x1, Pallas kernels, project(): pl.pallas_call(functools.partial(project_kernel, dims, offsets), out_shap...  6.02 us
  transfers between devices with their start and end apart: 31, of which 14 were waited for; matrix products, arithmetic and copies ran while one was open for 0% of the time, Pallas kernels for 7%

profile of v5, /device:TPU:0, one launch (start us, length us, event | category | flops | bytes accessed | tf_op | source)
XLA Modules:
  0.0 237.9 jit_solution(8316984111482646486)
XLA Ops:
  0.6 0.7 copy-done
  1.3 0.7 copy-done.1
  2.0 0.7 copy-done.3
  2.7 5.0 %outgoing_pages.2 = (bf16[32,128,1024]{2,1,0:T(8,128)(2,1)}, bf16[2,128,1024]{2,1,0:T(8,128)(2,1)S(1)}, bf16[2,128,1024]{2,1,0:T(8,128)(2,1)S(1)}, bf16[2,128,10...) custom-call(s32[256]{0:T(256)S(1)} %copy-done, s32[256]{0:T(256)S(1)} %copy-done.1, s32[256]{0:T(256)S(1)} %copy-done.3, ...), custom_call_target="tpu_custom_call" | custom-call | bytes 5242880 | tf_op jit(solution)/shard_map/outgoing_pages/pallas_call | solution.py:151
  7.7 3.2 %collective-permute-start = (bf16[2,128,1024]{2,1,0:T(8,128)(2,1)S(1)}, bf16[2,128,1024]{2,1,0:T(8,128)(2,1)S(1)}, u32[]{:S(2)}, u32[]{:S(2)}) collective-permute-start(bf16[2,128,1024]{2,1,0:T(8,128)(2,1)S(1)} %get-tuple-element.33), channel_id=1, source_target_pairs={{0,8},{2,10},{4,12},{6,14},{8,16},{10,18},{12,20},{14,22},{16,24},... | collective-permute-start | bytes 1572872 | tf_op jit(solution)/shard_map/ppermute | solution.py:48
  10.8 0.9 collective-permute-start.1
  11.7 0.9 collective-permute-start.2
  12.6 2.5 %collective-permute-start.3 = (bf16[2,128,1024]{2,1,0:T(8,128)(2,1)S(1)}, bf16[2,128,1024]{2,1,0:T(8,128)(2,1)S(1)}, u32[]{:S(2)}, u32[]{:S(2)}) collective-permute-start(bf16[2,128,1024]{2,1,0:T(8,128)(2,1)S(1)} %get-tuple-element.38), channel_id=1, source_target_pairs={{0,12},{2,14},{4,8},{6,10},{8,20},{10,22},{12,16},{14,18},{16,28},... | collective-permute-start | bytes 1572872 | tf_op jit(solution)/shard_map/ppermute | solution.py:48
  15.1 5.1 %outgoing_pages.3 = (bf16[32,128,1024]{2,1,0:T(8,128)(2,1)}, bf16[2,128,1024]{2,1,0:T(8,128)(2,1)S(1)}, bf16[2,128,1024]{2,1,0:T(8,128)(2,1)S(1)}, bf16[2,128,10...) custom-call(s32[256]{0:T(256)S(1)} %copy-done, ...), custom_call_target="tpu_custom_call", output_to_operand_aliasing={{0}: (4, {})} | custom-call | bytes 11534336 | tf_op jit(solution)/shard_map/outgoing_pages/pallas_call | solution.py:151
  20.3 0.6 collective-permute-start.4
  20.9 4.7 %collective-permute-done.rest_0_ = bf16[2,128,1024]{2,1,0:T(8,128)(2,1)S(1)} collective-permute-done((bf16[2,128,1024]{2,1,0:T(8,128)(2,1)S(1)}, bf16[2,128,1024]{2,1,0:T(8,128)(2,1)S(1)}, u32[]{:S(2)}, u32[]{:S(2)}) %collective-permute-start) | collective-permute-done | bytes 524320 | tf_op jit(solution)/shard_map/ppermute | solution.py:48
  25.7 9.7 %collective-permute-done.1.rest_1_ = bf16[2,128,1024]{2,1,0:T(8,128)(2,1)S(1)} collective-permute-done((bf16[2,128,1024]{2,1,0:T(8,128)(2,1)S(1)}, bf16[2,128,1024]{2,1,0:T(8,128)(2,1)S(1)}, u32[]{:S(2)}, u32[]{:S(2)}) %collective-permute-start.1) | collective-permute-done | bytes 524320 | tf_op jit(solution)/shard_map/ppermute | solution.py:48
  35.4 2.9 %collective-permute-start.6 = (bf16[2,128,1024]{2,1,0:T(8,128)(2,1)S(1)}, bf16[2,128,1024]{2,1,0:T(8,128)(2,1)S(1)}, u32[]{:S(2)}, u32[]{:S(2)}) collective-permute-start(bf16[2,128,1024]{2,1,0:T(8,128)(2,1)S(1)} %get-tuple-element.43), channel_id=1, source_target_pairs={{0,6},{2,4},{4,2},{6,0},{8,14},{10,12},{12,10},{14,8},{16,22},{18,... | collective-permute-start | bytes 1572872 | tf_op jit(solution)/shard_map/ppermute | solution.py:48
  38.3 1.9 collective-permute-start.7
  40.2 9.3 %collective-permute-done.3.rest_0_ = bf16[2,128,1024]{2,1,0:T(8,128)(2,1)S(1)} collective-permute-done((bf16[2,128,1024]{2,1,0:T(8,128)(2,1)S(1)}, bf16[2,128,1024]{2,1,0:T(8,128)(2,1)S(1)}, u32[]{:S(2)}, u32[]{:S(2)}) %collective-permute-start.3) | collective-permute-done | bytes 524320 | tf_op jit(solution)/shard_map/ppermute | solution.py:48
  49.5 1.7 collective-permute-start.9
  51.2 7.6 %collective-permute-done.5.rest_2_ = bf16[2,128,1024]{2,1,0:T(8,128)(2,1)S(1)} collective-permute-done((bf16[2,128,1024]{2,1,0:T(8,128)(2,1)S(1)}, bf16[2,128,1024]{2,1,0:T(8,128)(2,1)S(1)}, u32[]{:S(2)}, u32[]{:S(2)}) %collective-permute-start.5) | collective-permute-done | bytes 524320 | tf_op jit(solution)/shard_map/ppermute | solution.py:48
  58.8 41.6 %collective-permute-start.10 = (bf16[2,128,1024]{2,1,0:T(8,128)(2,1)S(1)}, bf16[2,128,1024]{2,1,0:T(8,128)(2,1)S(1)}, u32[]{:S(2)}, u32[]{:S(2)}) collective-permute-start(bf16[2,128,1024]{2,1,0:T(8,128)(2,1)S(1)} %get-tuple-element.49), channel_id=1, source_target_pairs={{0,30},{2,28},{4,26},{6,24},{8,6},{10,4},{12,2},{14,0},{16,14},{18... | collective-permute-start | bytes 1572872 | tf_op jit(solution)/shard_map/ppermute | solution.py:48
  100.3 0.1 collective-permute-start.12
  100.4 12.6 %collective-permute-start.13 = (bf16[2,128,1024]{2,1,0:T(8,128)(2,1)S(1)}, bf16[2,128,1024]{2,1,0:T(8,128)(2,1)S(1)}, u32[]{:S(2)}, u32[]{:S(2)}) collective-permute-start(bf16[2,128,1024]{2,1,0:T(8,128)(2,1)S(1)} %get-tuple-element.54), channel_id=1, source_target_pairs={{0,20},{2,22},{4,16},{6,18},{8,28},{10,30},{12,24},{14,26},{16,4},... | collective-permute-start | bytes 1572872 | tf_op jit(solution)/shard_map/ppermute | solution.py:48
  113.2 4.4 %settle_pages.5 = (bf16[32,128,1024]{2,1,0:T(8,128)(2,1)}, f32[16,32,128]{2,1,0:T(8,128)S(1)}) custom-call(s32[256]{0:T(256)S(1)} %copy-done, s32[256]{0:T(256)S(1)} %copy-done.1, s32[256]{0:T(256)S(1)} %copy-done.2, bf16[16,32,128]{2,1,0:T(8,128)(2,1)S(1)} %bitcast.2, f32[16,32,128]{2,1,0:T(8,128)S(1)} %broadcast_in_dim.3.rows_in, ...), custom_call_target="tpu_custom_call", output_to_operand_aliasing={{0}: (5, {})} | custom-call | flops 1073741824 | bytes 3145728 | tf_op jit(solution)/shard_map/settle_pages/pallas_call | solution.py:273
  117.6 2.3 settle_pages.6
  119.9 2.3 settle_pages.7
  122.3 44.6 %collective-permute-done.11.rest_2_ = bf16[2,128,1024]{2,1,0:T(8,128)(2,1)S(1)} collective-permute-done((bf16[2,128,1024]{2,1,0:T(8,128)(2,1)S(1)}, bf16[2,128,1024]{2,1,0:T(8,128)(2,1)S(1)}, u32[]{:S(2)}, u32[]{:S(2)}) %collective-permute-start.11) | collective-permute-done | bytes 524320 | tf_op jit(solution)/shard_map/ppermute | solution.py:48
  166.9 2.3 settle_pages.8
  169.2 23.5 %collective-permute-done.13.rest_1_ = bf16[2,128,1024]{2,1,0:T(8,128)(2,1)S(1)} collective-permute-done((bf16[2,128,1024]{2,1,0:T(8,128)(2,1)S(1)}, bf16[2,128,1024]{2,1,0:T(8,128)(2,1)S(1)}, u32[]{:S(2)}, u32[]{:S(2)}) %collective-permute-start.13) | collective-permute-done | bytes 524320 | tf_op jit(solution)/shard_map/ppermute | solution.py:48
  192.7 7.6 %collective-permute-done.14.rest_2_ = bf16[2,128,1024]{2,1,0:T(8,128)(2,1)S(1)} collective-permute-done((bf16[2,128,1024]{2,1,0:T(8,128)(2,1)S(1)}, bf16[2,128,1024]{2,1,0:T(8,128)(2,1)S(1)}, u32[]{:S(2)}, u32[]{:S(2)}) %collective-permute-start.14) | collective-permute-done | bytes 524320 | tf_op jit(solution)/shard_map/ppermute | solution.py:48
  200.3 2.6 %settle_pages.9 = (bf16[32,128,1024]{2,1,0:T(8,128)(2,1)}, bf16[16,4096]{1,0:T(8,128)(2,1)S(1)}) custom-call(s32[256]{0:T(256)S(1)} %copy-done, s32[256]{0:T(256)S(1)} %copy-done.1, s32[256]{0:T(256)S(1)} %copy-done.2, bf16[16,32,128]{2,1,0:T(8,128)(2,1)S(1)} %bitcast.6, ...), custom_call_target="tpu_custom_call", output_to_operand_aliasing={{0}: (5, {})} | custom-call | flops 1073741824 | bytes 3145728 | tf_op jit(solution)/shard_map/settle_pages/pallas_call | solution.py:273
  202.9 0.1 collective-permute-start.18
  203.1 1.7 collective-permute-start.22
  204.8 0.2 collective-permute-start.16
  204.9 2.0 collective-permute-start.15
  206.9 1.8 collective-permute-done.18.rest_4_
  208.7 0.7 collective-permute-start.26
  209.5 0.4 collective-permute-done.17.rest_3_
  209.9 0.7 collective-permute-start.25
  210.6 2.1 collective-permute-start.21
  212.7 4.1 %collective-permute-done.16.rest_2_ = bf16[16,4096]{1,0:T(8,128)(2,1)S(1)} collective-permute-done((bf16[16,4096]{1,0:T(8,128)(2,1)S(1)}, bf16[16,4096]{1,0:T(8,128)(2,1)S(1)}, u32[]{:S(2)}, u32[]{:S(2)}) %collective-permute-start.16) | collective-permute-done | bytes 131104 | tf_op jit(solution)/shard_map/ppermute | solution.py:48
  216.8 1.5 collective-permute-start.20
  218.3 0.5 collective-permute-start.19
  218.9 0.5 collective-permute-start.23
  219.4 3.4 %collective-permute-done.20.rest_6_ = bf16[16,4096]{1,0:T(8,128)(2,1)S(1)} collective-permute-done((bf16[16,4096]{1,0:T(8,128)(2,1)S(1)}, bf16[16,4096]{1,0:T(8,128)(2,1)S(1)}, u32[]{:S(2)}, u32[]{:S(2)}) %collective-permute-start.20) | collective-permute-done | bytes 131104 | tf_op jit(solution)/shard_map/ppermute | solution.py:48
  222.9 1.4 collective-permute-done.19.rest_5_
  224.3 1.3 collective-permute-done.27.rest_13_
  225.6 6.0 %project_rows.1 = (f32[128,512]{1,0:T(8,128)S(1)}, bf16[128,512]{1,0:T(8,128)(2,1)S(1)}) custom-call(bf16[4096,512]{1,0:T(8,128)(2,1)} %out_weight.1, bf16[16,4096]{1,0:T(8,128)(2,1)S(1)} %get-tuple-element.57.rest_0_, bf16[16,4096]{1,0:T(8,128)(2,1)S(1)} %collective-permute-done.15.rest_1_, bf16[16,4096]{1,0:T(8,128)(2,1)S(1)} %collective-permute-done.16.rest_2_, ...), custom_call_target="tpu_custom_call" | custom-call | flops 1073741824 | bytes 4194304 | tf_op jit(solution)/shard_map/project_rows/pallas_call | solution.py:338
  231.6 1.6 collective-permute-start.30
  233.2 4.1 %collective-permute-done.30 = bf16[128,512]{1,0:T(8,128)(2,1)S(1)} collective-permute-done((bf16[128,512]{1,0:T(8,128)(2,1)S(1)}, bf16[128,512]{1,0:T(8,128)(2,1)S(1)}, u32[]{:S(2)}, u32[]{:S(2)}) %collective-permute-start.30) | collective-permute-done | bytes 131104 | tf_op jit(solution)/shard_map/ppermute | solution.py:381
  237.2 0.7 add_convert_fusion
  (35 shorter events, 0.2 us)
Async XLA Ops:
  0.6 0.7 copy-start
  1.3 0.7 copy-start.1
  2.0 0.7 copy-start.3
  7.7 18.0 %collective-permute-start = (bf16[2,128,1024]{2,1,0:T(8,128)(2,1)S(1)}, bf16[2,128,1024]{2,1,0:T(8,128)(2,1)S(1)}, u32[]{:S(2)}, u32[]{:S(2)}) collective-permute-start(bf16[2,128,1024]{2,1,0:T(8,128)(2,1)S(1)} %get-tuple-element.33), channel_id=1, source_target_pairs={{0,8},{2,10},{4,12},{6,14},{8,16},{10,18},{12,20},{14,22},{16,24},... | collective-permute-start | bytes 1572872 | tf_op jit(solution)/shard_map/ppermute | solution.py:48
  10.8 24.6 %collective-permute-start.1 = (bf16[2,128,1024]{2,1,0:T(8,128)(2,1)S(1)}, bf16[2,128,1024]{2,1,0:T(8,128)(2,1)S(1)}, u32[]{:S(2)}, u32[]{:S(2)}) collective-permute-start(bf16[2,128,1024]{2,1,0:T(8,128)(2,1)S(1)} %get-tuple-element.34), channel_id=1, source_target_pairs={{0,10},{2,8},{4,14},{6,12},{8,18},{10,16},{12,22},{14,20},{16,26},... | collective-permute-start | bytes 1572872 | tf_op jit(solution)/shard_map/ppermute | solution.py:48
  11.7 26.6 %collective-permute-start.2 = (bf16[2,128,1024]{2,1,0:T(8,128)(2,1)S(1)}, bf16[2,128,1024]{2,1,0:T(8,128)(2,1)S(1)}, u32[]{:S(2)}, u32[]{:S(2)}) collective-permute-start(bf16[2,128,1024]{2,1,0:T(8,128)(2,1)S(1)} %get-tuple-element.35), channel_id=1, source_target_pairs={{0,2},{2,0},{4,6},{6,4},{8,10},{10,8},{12,14},{14,12},{16,18},{18,... | collective-permute-start | bytes 1572872 | tf_op jit(solution)/shard_map/ppermute | solution.py:48
  12.6 36.9 %collective-permute-start.3 = (bf16[2,128,1024]{2,1,0:T(8,128)(2,1)S(1)}, bf16[2,128,1024]{2,1,0:T(8,128)(2,1)S(1)}, u32[]{:S(2)}, u32[]{:S(2)}) collective-permute-start(bf16[2,128,1024]{2,1,0:T(8,128)(2,1)S(1)} %get-tuple-element.38), channel_id=1, source_target_pairs={{0,12},{2,14},{4,8},{6,10},{8,20},{10,22},{12,16},{14,18},{16,28},... | collective-permute-start | bytes 1572872 | tf_op jit(solution)/shard_map/ppermute | solution.py:48
  15.1 98.0 %copy-start.4 = (bf16[16,4096]{1,0:T(8,128)(2,1)S(1)}, bf16[16,4096]{1,0:T(8,128)(2,1)}, u32[]{:S(2)}) copy-start(bf16[16,4096]{1,0:T(8,128)(2,1)} %param.12) | copy-start | bytes 393220
  15.1 98.0 %copy-start.2 = (s32[256]{0:T(256)S(1)}, s32[256]{0:T(256)}, u32[]{:S(2)}) copy-start(s32[256]{0:T(256)} %row_request.9) | copy-start | bytes 3076
  20.3 29.2 %collective-permute-start.4 = (bf16[2,128,1024]{2,1,0:T(8,128)(2,1)S(1)}, bf16[2,128,1024]{2,1,0:T(8,128)(2,1)S(1)}, u32[]{:S(2)}, u32[]{:S(2)}) collective-permute-start(bf16[2,128,1024]{2,1,0:T(8,128)(2,1)S(1)} %get-tuple-element.39), channel_id=1, source_target_pairs={{0,4},{2,6},{4,0},{6,2},{8,12},{10,14},{12,8},{14,10},{16,20},{18,... | collective-permute-start | bytes 1572872 | tf_op jit(solution)/shard_map/ppermute | solution.py:48
  25.6 33.1 %collective-permute-start.5 = (bf16[2,128,1024]{2,1,0:T(8,128)(2,1)S(1)}, bf16[2,128,1024]{2,1,0:T(8,128)(2,1)S(1)}, u32[]{:S(2)}, u32[]{:S(2)}) collective-permute-start(bf16[2,128,1024]{2,1,0:T(8,128)(2,1)S(1)} %get-tuple-element.40), channel_id=1, source_target_pairs={{0,14},{2,12},{4,10},{6,8},{8,22},{10,20},{12,18},{14,16},{16,30},... | collective-permute-start | bytes 1572872 | tf_op jit(solution)/shard_map/ppermute | solution.py:48
  35.4 65.0 %collective-permute-start.6 = (bf16[2,128,1024]{2,1,0:T(8,128)(2,1)S(1)}, bf16[2,128,1024]{2,1,0:T(8,128)(2,1)S(1)}, u32[]{:S(2)}, u32[]{:S(2)}) collective-permute-start(bf16[2,128,1024]{2,1,0:T(8,128)(2,1)S(1)} %get-tuple-element.43), channel_id=1, source_target_pairs={{0,6},{2,4},{4,2},{6,0},{8,14},{10,12},{12,10},{14,8},{16,22},{18,... | collective-permute-start | bytes 1572872 | tf_op jit(solution)/shard_map/ppermute | solution.py:48
  38.3 62.0 %collective-permute-start.7 = (bf16[2,128,1024]{2,1,0:T(8,128)(2,1)S(1)}, bf16[2,128,1024]{2,1,0:T(8,128)(2,1)S(1)}, u32[]{:S(2)}, u32[]{:S(2)}) collective-permute-start(bf16[2,128,1024]{2,1,0:T(8,128)(2,1)S(1)} %get-tuple-element.44), channel_id=1, source_target_pairs={{0,24},{2,26},{4,28},{6,30},{8,0},{10,2},{12,4},{14,6},{16,8},{18,... | collective-permute-start | bytes 1572872 | tf_op jit(solution)/shard_map/ppermute | solution.py:48
  49.5 50.9 %collective-permute-start.8 = (bf16[2,128,1024]{2,1,0:T(8,128)(2,1)S(1)}, bf16[2,128,1024]{2,1,0:T(8,128)(2,1)S(1)}, u32[]{:S(2)}, u32[]{:S(2)}) collective-permute-start(bf16[2,128,1024]{2,1,0:T(8,128)(2,1)S(1)} %get-tuple-element.45), channel_id=1, source_target_pairs={{0,26},{2,24},{4,30},{6,28},{8,2},{10,0},{12,6},{14,4},{16,10},{18... | collective-permute-start | bytes 1572872 | tf_op jit(solution)/shard_map/ppermute | solution.py:48
  49.5 63.6 %collective-permute-start.9 = (bf16[2,128,1024]{2,1,0:T(8,128)(2,1)S(1)}, bf16[2,128,1024]{2,1,0:T(8,128)(2,1)S(1)}, u32[]{:S(2)}, u32[]{:S(2)}) collective-permute-start(bf16[2,128,1024]{2,1,0:T(8,128)(2,1)S(1)} %get-tuple-element.48), channel_id=1, source_target_pairs={{0,28},{2,30},{4,24},{6,26},{8,4},{10,6},{12,0},{14,2},{16,12},{18... | collective-permute-start | bytes 1572872 | tf_op jit(solution)/shard_map/ppermute | solution.py:48
  58.8 63.5 %collective-permute-start.10 = (bf16[2,128,1024]{2,1,0:T(8,128)(2,1)S(1)}, bf16[2,128,1024]{2,1,0:T(8,128)(2,1)S(1)}, u32[]{:S(2)}, u32[]{:S(2)}) collective-permute-start(bf16[2,128,1024]{2,1,0:T(8,128)(2,1)S(1)} %get-tuple-element.49), channel_id=1, source_target_pairs={{0,30},{2,28},{4,26},{6,24},{8,6},{10,4},{12,2},{14,0},{16,14},{18... | collective-permute-start | bytes 1572872 | tf_op jit(solution)/shard_map/ppermute | solution.py:48
  100.3 66.6 %collective-permute-start.11 = (bf16[2,128,1024]{2,1,0:T(8,128)(2,1)S(1)}, bf16[2,128,1024]{2,1,0:T(8,128)(2,1)S(1)}, u32[]{:S(2)}, u32[]{:S(2)}) collective-permute-start(bf16[2,128,1024]{2,1,0:T(8,128)(2,1)S(1)} %get-tuple-element.50), channel_id=1, source_target_pairs={{0,16},{2,18},{4,20},{6,22},{8,24},{10,26},{12,28},{14,30},{16,0},... | collective-permute-start | bytes 1572872 | tf_op jit(solution)/shard_map/ppermute | solution.py:48
  100.3 68.9 %collective-permute-start.12 = (bf16[2,128,1024]{2,1,0:T(8,128)(2,1)S(1)}, bf16[2,128,1024]{2,1,0:T(8,128)(2,1)S(1)}, u32[]{:S(2)}, u32[]{:S(2)}) collective-permute-start(bf16[2,128,1024]{2,1,0:T(8,128)(2,1)S(1)} %get-tuple-element.53), channel_id=1, source_target_pairs={{0,18},{2,16},{4,22},{6,20},{8,26},{10,24},{12,30},{14,28},{16,2},... | collective-permute-start | bytes 1572872 | tf_op jit(solution)/shard_map/ppermute | solution.py:48
  100.4 92.3 %collective-permute-start.13 = (bf16[2,128,1024]{2,1,0:T(8,128)(2,1)S(1)}, bf16[2,128,1024]{2,1,0:T(8,128)(2,1)S(1)}, u32[]{:S(2)}, u32[]{:S(2)}) collective-permute-start(bf16[2,128,1024]{2,1,0:T(8,128)(2,1)S(1)} %get-tuple-element.54), channel_id=1, source_target_pairs={{0,20},{2,22},{4,16},{6,18},{8,28},{10,30},{12,24},{14,26},{16,4},... | collective-permute-start | bytes 1572872 | tf_op jit(solution)/shard_map/ppermute | solution.py:48
  113.1 87.3 %collective-permute-start.14 = (bf16[2,128,1024]{2,1,0:T(8,128)(2,1)S(1)}, bf16[2,128,1024]{2,1,0:T(8,128)(2,1)S(1)}, u32[]{:S(2)}, u32[]{:S(2)}) collective-permute-start(bf16[2,128,1024]{2,1,0:T(8,128)(2,1)S(1)} %get-tuple-element.55), channel_id=1, source_target_pairs={{0,22},{2,20},{4,18},{6,16},{8,30},{10,28},{12,26},{14,24},{16,6},... | collective-permute-start | bytes 1572872 | tf_op jit(solution)/shard_map/ppermute | solution.py:48
  202.9 5.8 %collective-permute-start.18 = (bf16[16,4096]{1,0:T(8,128)(2,1)S(1)}, bf16[16,4096]{1,0:T(8,128)(2,1)S(1)}, u32[]{:S(2)}, u32[]{:S(2)}) collective-permute-start(bf16[16,4096]{1,0:T(8,128)(2,1)S(1)} %get-tuple-element.57.rest_0_), channel_id=1, source_target_pairs={{0,4},{2,6},{4,0},{6,2},{8,12},{10,14},{12,8},{14,10},{16,20},{18,... | collective-permute-start | bytes 393224 | tf_op jit(solution)/shard_map/ppermute | solution.py:48
  203.0 6.9 %collective-permute-start.17 = (bf16[16,4096]{1,0:T(8,128)(2,1)S(1)}, bf16[16,4096]{1,0:T(8,128)(2,1)S(1)}, u32[]{:S(2)}, u32[]{:S(2)}) collective-permute-start(bf16[16,4096]{1,0:T(8,128)(2,1)S(1)} %get-tuple-element.57.rest_0_), channel_id=1, source_target_pairs={{0,24},{2,26},{4,28},{6,30},{8,0},{10,2},{12,4},{14,6},{16,8},{18,... | collective-permute-start | bytes 393224 | tf_op jit(solution)/shard_map/ppermute | solution.py:48
  203.1 7.6 %collective-permute-start.22 = (bf16[16,4096]{1,0:T(8,128)(2,1)S(1)}, bf16[16,4096]{1,0:T(8,128)(2,1)S(1)}, u32[]{:S(2)}, u32[]{:S(2)}) collective-permute-start(bf16[16,4096]{1,0:T(8,128)(2,1)S(1)} %get-tuple-element.57.rest_0_), channel_id=1, source_target_pairs={{0,2},{2,0},{4,6},{6,4},{8,10},{10,8},{12,14},{14,12},{16,18},{18,... | collective-permute-start | bytes 393224 | tf_op jit(solution)/shard_map/ppermute | solution.py:48
  204.8 12.0 %collective-permute-start.16 = (bf16[16,4096]{1,0:T(8,128)(2,1)S(1)}, bf16[16,4096]{1,0:T(8,128)(2,1)S(1)}, u32[]{:S(2)}, u32[]{:S(2)}) collective-permute-start(bf16[16,4096]{1,0:T(8,128)(2,1)S(1)} %get-tuple-element.57.rest_0_), channel_id=1, source_target_pairs={{0,16},{2,18},{4,20},{6,22},{8,24},{10,26},{12,28},{14,30},{16,0},... | collective-permute-start | bytes 393224 | tf_op jit(solution)/shard_map/ppermute | solution.py:48
  204.9 13.4 %collective-permute-start.15 = (bf16[16,4096]{1,0:T(8,128)(2,1)S(1)}, bf16[16,4096]{1,0:T(8,128)(2,1)S(1)}, u32[]{:S(2)}, u32[]{:S(2)}) collective-permute-start(bf16[16,4096]{1,0:T(8,128)(2,1)S(1)} %get-tuple-element.57.rest_0_), channel_id=1, source_target_pairs={{0,8},{2,10},{4,12},{6,14},{8,16},{10,18},{12,20},{14,22},{16,24},... | collective-permute-start | bytes 393224 | tf_op jit(solution)/shard_map/ppermute | solution.py:48
  208.7 10.1 %collective-permute-start.26 = (bf16[16,4096]{1,0:T(8,128)(2,1)S(1)}, bf16[16,4096]{1,0:T(8,128)(2,1)S(1)}, u32[]{:S(2)}, u32[]{:S(2)}) collective-permute-start(bf16[16,4096]{1,0:T(8,128)(2,1)S(1)} %collective-permute-done.18.rest_4_), channel_id=1, source_target_pairs={{0,2},{2,0},{4,6},{6,4},{8,10},{10,8},{12,14},{14,12},{16,18},{18,... | collective-permute-start | bytes 393224 | tf_op jit(solution)/shard_map/ppermute | solution.py:48
  209.9 9.0 %collective-permute-start.25 = (bf16[16,4096]{1,0:T(8,128)(2,1)S(1)}, bf16[16,4096]{1,0:T(8,128)(2,1)S(1)}, u32[]{:S(2)}, u32[]{:S(2)}) collective-permute-start(bf16[16,4096]{1,0:T(8,128)(2,1)S(1)} %collective-permute-done.17.rest_3_), channel_id=1, source_target_pairs={{0,2},{2,0},{4,6},{6,4},{8,10},{10,8},{12,14},{14,12},{16,18},{18,... | collective-permute-start | bytes 393224 | tf_op jit(solution)/shard_map/ppermute | solution.py:48
  210.6 8.8 %collective-permute-start.21 = (bf16[16,4096]{1,0:T(8,128)(2,1)S(1)}, bf16[16,4096]{1,0:T(8,128)(2,1)S(1)}, u32[]{:S(2)}, u32[]{:S(2)}) collective-permute-start(bf16[16,4096]{1,0:T(8,128)(2,1)S(1)} %collective-permute-done.17.rest_3_), channel_id=1, source_target_pairs={{0,4},{2,6},{4,0},{6,2},{8,12},{10,14},{12,8},{14,10},{16,20},{18,... | collective-permute-start | bytes 393224 | tf_op jit(solution)/shard_map/ppermute | solution.py:48
  216.8 6.0 %collective-permute-start.20 = (bf16[16,4096]{1,0:T(8,128)(2,1)S(1)}, bf16[16,4096]{1,0:T(8,128)(2,1)S(1)}, u32[]{:S(2)}, u32[]{:S(2)}) collective-permute-start(bf16[16,4096]{1,0:T(8,128)(2,1)S(1)} %collective-permute-done.16.rest_2_), channel_id=1, source_target_pairs={{0,4},{2,6},{4,0},{6,2},{8,12},{10,14},{12,8},{14,10},{16,20},{18,... | collective-permute-start | bytes 393224 | tf_op jit(solution)/shard_map/ppermute | solution.py:48
  218.3 5.9 %collective-permute-start.19 = (bf16[16,4096]{1,0:T(8,128)(2,1)S(1)}, bf16[16,4096]{1,0:T(8,128)(2,1)S(1)}, u32[]{:S(2)}, u32[]{:S(2)}) collective-permute-start(bf16[16,4096]{1,0:T(8,128)(2,1)S(1)} %collective-permute-done.15.rest_1_), channel_id=1, source_target_pairs={{0,4},{2,6},{4,0},{6,2},{8,12},{10,14},{12,8},{14,10},{16,20},{18,... | collective-permute-start | bytes 393224 | tf_op jit(solution)/shard_map/ppermute | solution.py:48
  218.8 5.4 %collective-permute-start.24 = (bf16[16,4096]{1,0:T(8,128)(2,1)S(1)}, bf16[16,4096]{1,0:T(8,128)(2,1)S(1)}, u32[]{:S(2)}, u32[]{:S(2)}) collective-permute-start(bf16[16,4096]{1,0:T(8,128)(2,1)S(1)} %collective-permute-done.16.rest_2_), channel_id=1, source_target_pairs={{0,2},{2,0},{4,6},{6,4},{8,10},{10,8},{12,14},{14,12},{16,18},{18,... | collective-permute-start | bytes 393224 | tf_op jit(solution)/shard_map/ppermute | solution.py:48
  218.9 5.4 %collective-permute-start.23 = (bf16[16,4096]{1,0:T(8,128)(2,1)S(1)}, bf16[16,4096]{1,0:T(8,128)(2,1)S(1)}, u32[]{:S(2)}, u32[]{:S(2)}) collective-permute-start(bf16[16,4096]{1,0:T(8,128)(2,1)S(1)} %collective-permute-done.15.rest_1_), channel_id=1, source_target_pairs={{0,2},{2,0},{4,6},{6,4},{8,10},{10,8},{12,14},{14,12},{16,18},{18,... | collective-permute-start | bytes 393224 | tf_op jit(solution)/shard_map/ppermute | solution.py:48
  219.4 4.9 %collective-permute-start.29 = (bf16[16,4096]{1,0:T(8,128)(2,1)S(1)}, bf16[16,4096]{1,0:T(8,128)(2,1)S(1)}, u32[]{:S(2)}, u32[]{:S(2)}) collective-permute-start(bf16[16,4096]{1,0:T(8,128)(2,1)S(1)} %collective-permute-done.21.rest_7_), channel_id=1, source_target_pairs={{0,2},{2,0},{4,6},{6,4},{8,10},{10,8},{12,14},{14,12},{16,18},{18,... | collective-permute-start | bytes 393224 | tf_op jit(solution)/shard_map/ppermute | solution.py:48
  222.9 1.4 collective-permute-start.28
  224.3 1.3 collective-permute-start.27
  231.6 5.6 %collective-permute-start.30 = (bf16[128,512]{1,0:T(8,128)(2,1)S(1)}, bf16[128,512]{1,0:T(8,128)(2,1)S(1)}, u32[]{:S(2)}, u32[]{:S(2)}) collective-permute-start(bf16[128,512]{1,0:T(8,128)(2,1)S(1)} %get-tuple-element.59), channel_id=1, source_target_pairs={{0,1},{1,0},{2,3},{3,2},{4,5},{5,4},{6,7},{7,6},{8,9},{9,8},{10,11... | collective-permute-start | bytes 393224 | tf_op jit(solution)/shard_map/ppermute | solution.py:381

commit v6 on v3

v6 whole, which is shorter than its diff:
```python
import functools
import math

import jax
import jax.numpy as jnp
from jax import lax
from jax.experimental import pallas as pl
from jax.experimental.pallas import tpu as pltpu
from jax.sharding import PartitionSpec as P

HD = 128
MAX_PAGES = 2
ROW_UNROLL = 4
VMEM_LIMIT = 40 * 1024 * 1024


def factors(groups):
    near = math.gcd(groups, 4)
    return groups // near, near


def ahead(me, offset, dims, sign=1):
    far, near = dims
    return lax.rem(me // near + sign * offset[0] + far, far) * near + (me % near ^ offset[1])


def behind(me, offset, dims):
    return ahead(me, offset, dims, -1)


def send_by(array, offset, dims):
    far, near = dims
    pairs = [
        (s, (s // near + offset[0]) % far * near + (s % near ^ offset[1])) for s in range(far * near)
    ]
    return lax.ppermute(array, "group", pairs)


def gather_shards(shard, dims):
    far, near = dims
    held = {(0, 0): shard}
    swaps = [1 << i for i in reversed(range(near.bit_length() - 1))]
    for stage in [[(z, 0) for z in range(1, far)]] + [[(0, n)] for n in swaps]:
        incoming = {}
        for step in stage:
            for offset, array in held.items():
                incoming[offset[0] + step[0], offset[1] | step[1]] = send_by(array, step, dims)
        held.update(incoming)
    return held


def prepare_kernel(lengths_hbm, prefill_hbm, decode_hbm, pool, sends, *scratch):
    lengths, prefill_of, decode_of, held, zero_page, start_of, count_of, table_sem, in_sems, out_sem = scratch
    me = lax.axis_index("group")
    groups = sends.shape[0]
    page_total, page_size, _ = pool.shape
    sources = (lengths_hbm, prefill_hbm, decode_hbm)
    tables = [
        pltpu.make_async_copy(source, target, table_sem.at[i])
        for i, (source, target) in enumerate(zip(sources, (lengths, prefill_of, decode_of)))
    ]
    loads = [pltpu.make_async_copy(pool.at[p], held.at[p], in_sems.at[p]) for p in range(page_total)]
    for copy in tables + loads:
        copy.start()
    for d in range(groups + 1):
        start_of[d] = 0
        count_of[d] = 0
    zero_page[...] = jnp.zeros_like(zero_page)
    for table in tables:
        table.wait()

    def visit(r, running):
        mine = prefill_of[r] == me
        count = (lengths[r] + page_size - 1) // page_size
        to = jnp.where(mine, decode_of[r], groups)
        start_of[to] = running
        count_of[to] = count
        return running + jnp.where(mine, count, 0)

    lax.fori_loop(0, lengths.shape[0], visit, jnp.int32(0), unroll=8)
    for load in loads:
        load.wait()

    for d in range(groups):
        for page in range(MAX_PAGES):
            there = page < count_of[d]

            @pl.when(there)
            def _():
                pltpu.make_async_copy(held.at[start_of[d] + page], sends.at[d, page], out_sem).start()

            @pl.when(jnp.logical_not(there))
            def _():
                pltpu.make_async_copy(zero_page, sends.at[d, page], out_sem).start()

    for d in range(groups):
        for page in range(MAX_PAGES):
            pltpu.make_async_copy(zero_page, sends.at[d, page], out_sem).wait()


def prepare(groups, lengths, prefill_of, decode_of, pool):
    page = pool.shape[1:]
    hbm = pl.BlockSpec(memory_space=pl.ANY)
    table = pltpu.SMEM(lengths.shape, jnp.int32)
    return pl.pallas_call(
        prepare_kernel,
        out_shape=jax.ShapeDtypeStruct((groups, MAX_PAGES) + page, pool.dtype),
        in_specs=[hbm] * 4,
        out_specs=hbm,
        scratch_shapes=[
            table,
            table,
            table,
            pltpu.VMEM(pool.shape, pool.dtype),
            pltpu.VMEM(page, pool.dtype),
            pltpu.SMEM((groups + 1,), jnp.int32),
            pltpu.SMEM((groups + 1,), jnp.int32),
            pltpu.SemaphoreType.DMA((3,)),
            pltpu.SemaphoreType.DMA((pool.shape[0],)),
            pltpu.SemaphoreType.DMA,
        ],
        compiler_params=pltpu.CompilerParams(vmem_limit_bytes=VMEM_LIMIT),
        cost_estimate=pl.CostEstimate(flops=0, bytes_accessed=4 * pool.size, transcendentals=0),
        name="outgoing_pages",
    )(lengths, prefill_of, decode_of, pool)


def hand_on_kernel(blocks, arrived, received, held, in_sems, out_sems):
    step = arrived.shape[0] // blocks
    loads, stores = [], []
    for i in range(blocks):
        part = pl.ds(i * step, step)
        loads.append(pltpu.make_async_copy(arrived.at[part], held.at[part], in_sems.at[i]))
        stores.append(pltpu.make_async_copy(held.at[part], received.at[part], out_sems.at[i]))
        loads[-1].start()
    for load, store in zip(loads, stores):
        load.wait()
        store.start()
    for store in stores:
        store.wait()


def hand_on(arrived):
    hbm = pl.BlockSpec(memory_space=pl.ANY)
    blocks = math.gcd(arrived.shape[0], 16)
    return pl.pallas_call(
        functools.partial(hand_on_kernel, blocks),
        out_shape=jax.ShapeDtypeStruct(arrived.shape, arrived.dtype),
        in_specs=[hbm],
        out_specs=hbm,
        scratch_shapes=[
            pltpu.VMEM(arrived.shape, arrived.dtype),
            pltpu.SemaphoreType.DMA((blocks,)),
            pltpu.SemaphoreType.DMA((blocks,)),
        ],
        compiler_params=pltpu.CompilerParams(vmem_limit_bytes=VMEM_LIMIT),
        cost_estimate=pl.CostEstimate(flops=0, bytes_accessed=4 * arrived.size, transcendentals=0),
        name="place_pages",
    )(arrived)


def attend_row(query, pages, length):
    first, second = pages
    kv_heads = first.shape[1] // (2 * HD)
    share = query.shape[0] // kv_heads
    scores = []
    for h in range(kv_heads):
        columns = slice(2 * h * HD, (2 * h + 1) * HD)
        keys = jnp.concatenate([first[:, columns], second[:, columns]], axis=0)
        every = lax.dot_general(
            query, keys, (((1,), (1,)), ((), ())), preferred_element_type=jnp.float32
        )
        scores.append(every[h * share : (h + 1) * share])
    score = jnp.concatenate(scores, axis=0) * (1.0 / math.sqrt(HD))
    live = lax.broadcasted_iota(jnp.int32, score.shape, 1) < length
    masked = jnp.where(live, score, -1e30)
    highest = jnp.max(masked, axis=1, keepdims=True)
    weights = jnp.where(live, jnp.exp(masked - highest), 0.0)
    totals = jnp.sum(weights, axis=1, keepdims=True)
    rounded = weights.astype(jnp.bfloat16)
    mixtures = []
    for h in range(kv_heads):
        columns = slice((2 * h + 1) * HD, (2 * h + 2) * HD)
        values = jnp.concatenate([first[:, columns], second[:, columns]], axis=0)
        every = jnp.dot(rounded, values, preferred_element_type=jnp.float32)
        mixtures.append(every[h * share : (h + 1) * share])
    return jnp.concatenate(mixtures, axis=0) / totals


def attend_kernel(lengths, prefill_of, row_request, queries, incoming, out, rows, held, sems):
    me = lax.axis_index("group")
    row_local, query_heads, _ = queries.shape

    def request_of(b):
        return row_request[me * row_local + b]

    for b in range(row_local):
        pltpu.make_async_copy(incoming.at[prefill_of[request_of(b)]], held.at[b], sems.at[b]).start()
    for first in range(0, row_local, ROW_UNROLL):
        several = range(first, min(first + ROW_UNROLL, row_local))
        for b in several:
            pltpu.make_async_copy(incoming.at[0], held.at[b], sems.at[b]).wait()
        results = []
        for b in several:
            pages = [held[b, page] for page in range(MAX_PAGES)]
            results.append(attend_row(queries[b], pages, lengths[request_of(b)]))
        for b, result in zip(several, results):
            rows[b] = result
    for h in range(query_heads):
        out[:, h * HD : (h + 1) * HD] = rows[:, h, :].astype(out.dtype)


def attend(lengths, prefill_of, row_request, queries, incoming):
    row_local, query_heads, _ = queries.shape
    smem = pl.BlockSpec(memory_space=pltpu.SMEM)
    vmem = pl.BlockSpec(memory_space=pltpu.VMEM)
    hbm = pl.BlockSpec(memory_space=pl.ANY)
    return pl.pallas_call(
        attend_kernel,
        out_shape=jax.ShapeDtypeStruct((row_local, query_heads * HD), jnp.bfloat16),
        in_specs=[smem, smem, smem, vmem, hbm],
        out_specs=vmem,
        scratch_shapes=[
            pltpu.VMEM(queries.shape, jnp.float32),
            pltpu.VMEM((row_local,) + incoming.shape[1:], incoming.dtype),
            pltpu.SemaphoreType.DMA((row_local,)),
        ],
        compiler_params=pltpu.CompilerParams(vmem_limit_bytes=VMEM_LIMIT),
        cost_estimate=pl.CostEstimate(
            flops=1 << 32, bytes_accessed=2 * incoming.size, transcendentals=1 << 20
        ),
        name="attend_rows",
    )(lengths, prefill_of, row_request, queries, incoming)


def project_kernel(dims, offsets, out_weight, *rest):
    shards = rest[: len(offsets)]
    own, *theirs = rest[len(offsets) : -3]
    attended, product, sems = rest[-3:]
    me = lax.axis_index("group")
    heads = lax.axis_size("head")
    my_head = lax.axis_index("head")
    row_local = shards[0].shape[0]
    share = own.shape[0]
    copies = []
    for i, offset in enumerate(offsets):
        place = pl.ds(behind(me, offset, dims) * row_local, row_local)
        copies.append(pltpu.make_async_copy(shards[i], attended.at[place], sems.at[i]))
        copies[-1].start()
    for copy in copies:
        copy.wait()
    product[...] = jnp.dot(attended[...], out_weight[...], preferred_element_type=jnp.float32)
    own[...] = product[pl.ds(pl.multiple_of(my_head * share, share), share)]
    for ahead_by, target in enumerate(theirs, 1):
        start = pl.multiple_of(lax.rem(my_head + ahead_by, heads) * share, share)
        target[...] = product[pl.ds(start, share)].astype(target.dtype)


def project(dims, gathered, out_weight, heads):
    offsets = list(gathered)
    shards = [gathered[offset] for offset in offsets]
    row_local, width = shards[0].shape
    row_total = row_local * len(shards)
    share, columns = row_total // heads, out_weight.shape[1]
    vmem = pl.BlockSpec(memory_space=pltpu.VMEM)
    hbm = pl.BlockSpec(memory_space=pl.ANY)
    theirs = jax.ShapeDtypeStruct((share, columns), jnp.bfloat16)
    return pl.pallas_call(
        functools.partial(project_kernel, dims, offsets),
        out_shape=[jax.ShapeDtypeStruct((share, columns), jnp.float32)] + [theirs] * (heads - 1),
        in_specs=[vmem] + [hbm] * len(shards),
        out_specs=[vmem] * heads,
        scratch_shapes=[
            pltpu.VMEM((row_total, width), jnp.bfloat16),
            pltpu.VMEM((row_total, columns), jnp.float32),
            pltpu.SemaphoreType.DMA((len(shards),)),
        ],
        compiler_params=pltpu.CompilerParams(vmem_limit_bytes=VMEM_LIMIT),
        cost_estimate=pl.CostEstimate(
            flops=2 * row_total * width * columns, bytes_accessed=2 * out_weight.size, transcendentals=0
        ),
        name="project_rows",
    )(pltpu.with_memory_space_constraint(out_weight, pltpu.VMEM), *shards)


def local(kv_pool, lengths, prefill_of, decode_of, row_request, queries, out_weight):
    row_local, query_width = queries.shape
    query_heads = queries.reshape(row_local, query_width // HD, HD)
    dims = factors(lax.axis_size("group"))
    groups = math.prod(dims)
    heads = lax.axis_size("head")

    outgoing = prepare(groups, lengths, prefill_of, decode_of, kv_pool)
    incoming = lax.all_to_all(outgoing, "group", split_axis=0, concat_axis=0, tiled=True)
    rows = attend(lengths, prefill_of, row_request, query_heads, incoming)
    received = hand_on(incoming.reshape((groups * MAX_PAGES,) + kv_pool.shape[1:]))

    own, *theirs = project(dims, gather_shards(rows, dims), out_weight, heads)
    for ahead_by, part in enumerate(theirs, 1):
        pairs = [(h, (h + ahead_by) % heads) for h in range(heads)]
        own = own + lax.ppermute(part, "head", pairs).astype(jnp.float32)
    return (received, own.astype(jnp.bfloat16))


def solution(mesh):
    in_specs = (
        P("group", None, "head"),
        P(),
        P(),
        P(),
        P(),
        P("group", "head"),
        P("head", "group"),
    )
    out_specs = (P("group", None, "head"), P("head", "group"))
    return jax.shard_map(local, mesh=mesh, in_specs=in_specs, out_specs=out_specs, check_vma=False)
```

time: 236 us -> 246 us (1.042)
  waiting for transfers between devices: 111 us -> 160 us
  starting transfers between devices: 92 us -> 53.9 us
  Pallas kernels: 29.2 us -> 23.7 us
  local copies, waits for them, and re-layouts: 2.07 us -> 5.46 us
    all_to_all x0 -> x1, waiting for transfers between devices: none -> 151 us  [local(): lax.all_to_all(outgoing, 'group', split_axis=0, concat_axis=0, tiled=True)]
    ppermute x30 -> x15, waiting for transfers between devices: 107 us -> 8.96 us  [send_by(): return lax.ppermute(array, 'group', pairs)]
    ppermute x30 -> x15, starting transfers between devices: 90.4 us -> 44.7 us  [send_by(): return lax.ppermute(array, 'group', pairs)]
    all_to_all x0 -> x1, starting transfers between devices: none -> 7.59 us  [local(): lax.all_to_all(outgoing, 'group', split_axis=0, concat_axis=0, tiled=True)]
    ppermute x1, waiting for transfers between devices: 4.06 us -> 0.01 us  [local(): own = own + lax.ppermute(part, 'head', pairs).astype(jnp.float32)]
    unnamed x11 -> x19, local copies, waits for them, and re-layouts: 2.06 us -> 5.46 us
    pallas_call x6 -> x3, Pallas kernels: 22.5 us -> 19.3 us  [the longest x1 8.09 us: attend(): pl.pallas_call(attend_kernel, out_shape=jax.ShapeDtypeStruct((row_local,...]
  transfers between devices with their start and end apart: 31 -> 17, of which waited for: 12 -> 8; matrix products, arithmetic and copies ran while one was open for 0% -> 0% of each run, Pallas kernels for 5% -> 3%
where the time goes in v6:
time: 246 us; the launch traced here: 244 us
  waiting for transfers between devices  160 us (65%)
  starting transfers between devices  53.9 us (22%)
  Pallas kernels  23.7 us (10%)
  local copies, waits for them, and re-layouts  5.46 us (2%)
    all_to_all x1, waiting for transfers between devices, local(): lax.all_to_all(outgoing, 'group', split_axis=0, concat_axis=0, tiled=True)  151 us
    ppermute x15, starting transfers between devices, send_by(): return lax.ppermute(array, 'group', pairs)  44.7 us
    ppermute x15, waiting for transfers between devices, send_by(): return lax.ppermute(array, 'group', pairs)  8.96 us
    pallas_call x1, Pallas kernels, attend(): pl.pallas_call(attend_kernel, out_shape=jax.ShapeDtypeStruct((row_local,...  8.09 us
    all_to_all x1, starting transfers between devices, local(): lax.all_to_all(outgoing, 'group', split_axis=0, concat_axis=0, tiled=True)  7.59 us
    pallas_call x1, Pallas kernels, hand_on(): pl.pallas_call(functools.partial(hand_on_kernel, blocks), out_shape=jax.S...  6.57 us
    unnamed x19, local copies, waits for them, and re-layouts  5.46 us
  transfers between devices with their start and end apart: 17, of which 8 were waited for; matrix products, arithmetic and copies ran while one was open for 0% of the time, Pallas kernels for 3%

profile of v6, /device:TPU:0, one launch (start us, length us, event | category | flops | bytes accessed | tf_op | source)
XLA Modules:
  0.0 244.1 jit_solution(4667691412242419961)
XLA Ops:
  0.6 0.0 copy-start.2
  0.6 0.7 copy-done.2
  1.3 0.7 copy-done.3
  2.0 0.7 copy-done.5
  2.7 4.7 %outgoing_pages.1 = bf16[16,2,128,1024]{3,2,1,0:T(8,128)(2,1)S(1)} custom-call(s32[256]{0:T(256)S(1)} %copy-done.3, s32[256]{0:T(256)S(1)} %copy-done.5, s32[256]{0:T(256)S(1)} %copy-done.2, bf16[32,128,1024]{2,1,0:T(8,128)(2,1)} %pool.1), custom_call_target="tpu_custom_call" | custom-call | bytes 16777216 | tf_op jit(solution)/shard_map/outgoing_pages/pallas_call | solution.py:105
  7.3 0.0 copy-start
  7.4 3.4 %copy-done = bf16[16,2,128,1024]{3,2,1,0:T(8,128)(2,1)} copy-done((bf16[16,2,128,1024]{3,2,1,0:T(8,128)(2,1)}, bf16[16,2,128,1024]{3,2,1,0:T(8,128)(2,1)S(1)}, u32[]{:S(2)}) %copy-start) | copy-done | bytes 8388632
  10.8 7.6 %all-to-all-start = ((bf16[16,2,128,1024]{3,2,1,0:T(8,128)(2,1)}), bf16[16,2,128,1024]{3,2,1,0:T(8,128)(2,1)}, u32[]{:S(2)}, u32[]{:S(2)}) async-start(bf16[16,2,128,1024]{3,2,1,0:T(8,128)(2,1)} %copy-done), calls=%async_computation | async-start | bytes 16777216 | tf_op jit(solution)/shard_map/all_to_all | solution.py:294
  18.4 0.0 copy-done.8
  18.4 150.7 %all-to-all-done.incoming = bf16[16,2,128,1024]{3,2,1,0:T(8,128)(2,1)} async-done(((bf16[16,2,128,1024]{3,2,1,0:T(8,128)(2,1)}), bf16[16,2,128,1024]{3,2,1,0:T(8,128)(2,1)}, u32[]{:S(2)}, u32[]{:S(2)}) %all-to-all-start) | async-done | bytes 8388640 | tf_op jit(solution)/shard_map/all_to_all | solution.py:294
  169.1 0.0 copy-done.4
  169.1 0.0 copy-done.7
  169.1 8.1 %attend_rows.1.rest_0_ = bf16[16,4096]{1,0:T(8,128)(2,1)S(1)} custom-call(s32[256]{0:T(256)S(1)} %copy-done.4, s32[256]{0:T(256)S(1)} %copy-done.6, s32[256]{0:T(256)S(1)} %copy-done.7, bf16[16,32,128]{2,1,0:T(8,128)(2,1)S(1)} %bitcast.3, bf16[16,2,128,1024]{3,2,1,0:T(8,128)(2,1)} %all-to-all-done.incoming), custom_call_target="tpu_custom_call" | custom-call | flops 4294967296 | bytes 8388608 | tf_op jit(solution)/shard_map/attend_rows/pallas_call | solution.py:218
  177.2 32.2 %collective-permute-start = (bf16[16,4096]{1,0:T(8,128)(2,1)S(1)}, bf16[16,4096]{1,0:T(8,128)(2,1)S(1)}, u32[]{:S(2)}, u32[]{:S(2)}) collective-permute-start(bf16[16,4096]{1,0:T(8,128)(2,1)S(1)} %attend_rows.1.rest_0_), channel_id=1, source_target_pairs={{0,8},{2,10},{4,12},{6,14},{8,16},{10,18},{12,20},{14,22},{16,24},... | collective-permute-start | bytes 393224 | tf_op jit(solution)/shard_map/ppermute | solution.py:36
  209.3 3.5 %collective-permute-start.1 = (bf16[16,4096]{1,0:T(8,128)(2,1)S(1)}, bf16[16,4096]{1,0:T(8,128)(2,1)S(1)}, u32[]{:S(2)}, u32[]{:S(2)}) collective-permute-start(bf16[16,4096]{1,0:T(8,128)(2,1)S(1)} %attend_rows.1.rest_0_), channel_id=1, source_target_pairs={{0,16},{2,18},{4,20},{6,22},{8,24},{10,26},{12,28},{14,30},{16,0},... | collective-permute-start | bytes 393224 | tf_op jit(solution)/shard_map/ppermute | solution.py:36
  212.8 2.8 %collective-permute-start.2 = (bf16[16,4096]{1,0:T(8,128)(2,1)S(1)}, bf16[16,4096]{1,0:T(8,128)(2,1)S(1)}, u32[]{:S(2)}, u32[]{:S(2)}) collective-permute-start(bf16[16,4096]{1,0:T(8,128)(2,1)S(1)} %attend_rows.1.rest_0_), channel_id=1, source_target_pairs={{0,24},{2,26},{4,28},{6,30},{8,0},{10,2},{12,4},{14,6},{16,8},{18,... | collective-permute-start | bytes 393224 | tf_op jit(solution)/shard_map/ppermute | solution.py:36
  215.6 0.0 collective-permute-start.3
  215.7 0.9 collective-permute-start.7
  216.6 0.0 collective-permute-done.rest_1_
  216.6 1.1 collective-permute-start.4
  217.7 1.6 collective-permute-done.1.rest_2_
  219.3 3.1 %collective-permute-start.5 = (bf16[16,4096]{1,0:T(8,128)(2,1)S(1)}, bf16[16,4096]{1,0:T(8,128)(2,1)S(1)}, u32[]{:S(2)}, u32[]{:S(2)}) collective-permute-start(bf16[16,4096]{1,0:T(8,128)(2,1)S(1)} %collective-permute-done.1.rest_2_), channel_id=1, source_target_pairs={{0,4},{2,6},{4,0},{6,2},{8,12},{10,14},{12,8},{14,10},{16,20},{18,... | collective-permute-start | bytes 393224 | tf_op jit(solution)/shard_map/ppermute | solution.py:36
  222.4 0.0 collective-permute-done.2.rest_3_
  222.4 0.0 collective-permute-start.6
  222.4 0.0 collective-permute-done.3.rest_4_
  222.4 0.0 collective-permute-start.10
  222.5 0.0 collective-permute-done.7.rest_8_
  222.5 0.5 collective-permute-start.8
  223.0 0.5 collective-permute-done.4.rest_5_
  223.5 0.0 collective-permute-start.9
  223.5 3.2 %collective-permute-done.5.rest_6_ = bf16[16,4096]{1,0:T(8,128)(2,1)S(1)} collective-permute-done((bf16[16,4096]{1,0:T(8,128)(2,1)S(1)}, bf16[16,4096]{1,0:T(8,128)(2,1)S(1)}, u32[]{:S(2)}, u32[]{:S(2)}) %collective-permute-start.5) | collective-permute-done | bytes 131104 | tf_op jit(solution)/shard_map/ppermute | solution.py:36
  226.7 0.0 collective-permute-start.11
  226.7 2.4 collective-permute-done.6.rest_7_
  229.0 0.0 collective-permute-start.12
  229.0 0.0 collective-permute-done.10.rest_11_
  229.0 0.5 collective-permute-start.13
  229.5 0.0 collective-permute-done.8.rest_9_
  229.5 0.1 collective-permute-start.14
  229.6 0.0 collective-permute-done.9.rest_10_
  229.6 0.0 collective-permute-done.11.rest_12_
  229.6 0.8 collective-permute-done.12.rest_13_
  230.4 0.2 collective-permute-done.13.rest_14_
  230.6 0.3 collective-permute-done.14.rest_15_
  230.9 4.4 %project_rows.1 = (f32[128,512]{1,0:T(8,128)S(1)}, bf16[128,512]{1,0:T(8,128)(2,1)S(1)}) custom-call(bf16[4096,512]{1,0:T(8,128)(2,1)S(1)} %copy-done.1, bf16[16,4096]{1,0:T(8,128)(2,1)S(1)} %attend_rows.1.rest_0_, bf16[16,4096]{1,0:T(8,128)(2,1)S(1)} %collective-permute-done.rest_1_, bf16[16,4096]{1,0:T(8,128)(2,1)S(1)} %collective-permute-done.1.rest_2_, ...), custom_call_target="tpu_custom_call" | custom-call | flops 1073741824 | bytes 4194304 | tf_op jit(solution)/shard_map/project_rows/pallas_call | solution.py:268
  235.3 1.6 collective-permute-start.15
  236.9 6.6 %place_pages.1 = bf16[32,128,1024]{2,1,0:T(8,128)(2,1)} custom-call(bf16[32,128,1024]{2,1,0:T(8,128)(2,1)} %bitcast.arrived), custom_call_target="tpu_custom_call" | custom-call | bytes 16777216 | tf_op jit(solution)/shard_map/place_pages/pallas_call | solution.py:146
  243.4 0.0 collective-permute-done.15
  243.5 0.7 add_convert_fusion
  (10 shorter events, 0.0 us)
Async XLA Ops:
  0.6 0.7 copy-start.2
  1.3 0.7 copy-start.3
  2.0 0.7 copy-start.5
  7.3 3.4 %copy-start = (bf16[16,2,128,1024]{3,2,1,0:T(8,128)(2,1)}, bf16[16,2,128,1024]{3,2,1,0:T(8,128)(2,1)S(1)}, u32[]{:S(2)}) copy-start(bf16[16,2,128,1024]{3,2,1,0:T(8,128)(2,1)S(1)} %outgoing_pages.1) | copy-start | bytes 25165828
  10.7 7.6 %copy-start.8 = (bf16[16,4096]{1,0:T(8,128)(2,1)S(1)}, bf16[16,4096]{1,0:T(8,128)(2,1)}, u32[]{:S(2)}) copy-start(bf16[16,4096]{1,0:T(8,128)(2,1)} %param.12) | copy-start | bytes 393220
  10.7 158.3 %copy-start.4 = (s32[256]{0:T(256)S(1)}, s32[256]{0:T(256)}, u32[]{:S(2)}) copy-start(s32[256]{0:T(256)} %lengths.1) | copy-start | bytes 3076
  10.8 158.3 %copy-start.6 = (s32[256]{0:T(256)S(1)}, s32[256]{0:T(256)}, u32[]{:S(2)}) copy-start(s32[256]{0:T(256)} %prefill_of.1) | copy-start | bytes 3076
  10.8 158.3 %copy-start.7 = (s32[256]{0:T(256)S(1)}, s32[256]{0:T(256)}, u32[]{:S(2)}) copy-start(s32[256]{0:T(256)} %row_request.1) | copy-start | bytes 3076
  10.8 158.3 %all-to-all-start = ((bf16[16,2,128,1024]{3,2,1,0:T(8,128)(2,1)}), bf16[16,2,128,1024]{3,2,1,0:T(8,128)(2,1)}, u32[]{:S(2)}, u32[]{:S(2)}) async-start(bf16[16,2,128,1024]{3,2,1,0:T(8,128)(2,1)} %copy-done), calls=%async_computation | async-start | bytes 16777216 | tf_op jit(solution)/shard_map/all_to_all | solution.py:294
  169.1 61.8 %copy-start.1 = (bf16[4096,512]{1,0:T(8,128)(2,1)S(1)}, bf16[4096,512]{1,0:T(8,128)(2,1)}, u32[]{:S(2)}) copy-start(bf16[4096,512]{1,0:T(8,128)(2,1)} %out_weight.1) | copy-start | bytes 12582916
  177.2 39.4 %collective-permute-start = (bf16[16,4096]{1,0:T(8,128)(2,1)S(1)}, bf16[16,4096]{1,0:T(8,128)(2,1)S(1)}, u32[]{:S(2)}, u32[]{:S(2)}) collective-permute-start(bf16[16,4096]{1,0:T(8,128)(2,1)S(1)} %attend_rows.1.rest_0_), channel_id=1, source_target_pairs={{0,8},{2,10},{4,12},{6,14},{8,16},{10,18},{12,20},{14,22},{16,24},... | collective-permute-start | bytes 393224 | tf_op jit(solution)/shard_map/ppermute | solution.py:36
  209.3 9.9 %collective-permute-start.1 = (bf16[16,4096]{1,0:T(8,128)(2,1)S(1)}, bf16[16,4096]{1,0:T(8,128)(2,1)S(1)}, u32[]{:S(2)}, u32[]{:S(2)}) collective-permute-start(bf16[16,4096]{1,0:T(8,128)(2,1)S(1)} %attend_rows.1.rest_0_), channel_id=1, source_target_pairs={{0,16},{2,18},{4,20},{6,22},{8,24},{10,26},{12,28},{14,30},{16,0},... | collective-permute-start | bytes 393224 | tf_op jit(solution)/shard_map/ppermute | solution.py:36
  212.8 9.6 %collective-permute-start.2 = (bf16[16,4096]{1,0:T(8,128)(2,1)S(1)}, bf16[16,4096]{1,0:T(8,128)(2,1)S(1)}, u32[]{:S(2)}, u32[]{:S(2)}) collective-permute-start(bf16[16,4096]{1,0:T(8,128)(2,1)S(1)} %attend_rows.1.rest_0_), channel_id=1, source_target_pairs={{0,24},{2,26},{4,28},{6,30},{8,0},{10,2},{12,4},{14,6},{16,8},{18,... | collective-permute-start | bytes 393224 | tf_op jit(solution)/shard_map/ppermute | solution.py:36
  215.6 6.8 %collective-permute-start.3 = (bf16[16,4096]{1,0:T(8,128)(2,1)S(1)}, bf16[16,4096]{1,0:T(8,128)(2,1)S(1)}, u32[]{:S(2)}, u32[]{:S(2)}) collective-permute-start(bf16[16,4096]{1,0:T(8,128)(2,1)S(1)} %attend_rows.1.rest_0_), channel_id=1, source_target_pairs={{0,4},{2,6},{4,0},{6,2},{8,12},{10,14},{12,8},{14,10},{16,20},{18,... | collective-permute-start | bytes 393224 | tf_op jit(solution)/shard_map/ppermute | solution.py:36
  215.7 6.8 %collective-permute-start.7 = (bf16[16,4096]{1,0:T(8,128)(2,1)S(1)}, bf16[16,4096]{1,0:T(8,128)(2,1)S(1)}, u32[]{:S(2)}, u32[]{:S(2)}) collective-permute-start(bf16[16,4096]{1,0:T(8,128)(2,1)S(1)} %attend_rows.1.rest_0_), channel_id=1, source_target_pairs={{0,2},{2,0},{4,6},{6,4},{8,10},{10,8},{12,14},{14,12},{16,18},{18,... | collective-permute-start | bytes 393224 | tf_op jit(solution)/shard_map/ppermute | solution.py:36
  216.6 6.9 %collective-permute-start.4 = (bf16[16,4096]{1,0:T(8,128)(2,1)S(1)}, bf16[16,4096]{1,0:T(8,128)(2,1)S(1)}, u32[]{:S(2)}, u32[]{:S(2)}) collective-permute-start(bf16[16,4096]{1,0:T(8,128)(2,1)S(1)} %collective-permute-done.rest_1_), channel_id=1, source_target_pairs={{0,4},{2,6},{4,0},{6,2},{8,12},{10,14},{12,8},{14,10},{16,20},{18,... | collective-permute-start | bytes 393224 | tf_op jit(solution)/shard_map/ppermute | solution.py:36
  219.3 7.4 %collective-permute-start.5 = (bf16[16,4096]{1,0:T(8,128)(2,1)S(1)}, bf16[16,4096]{1,0:T(8,128)(2,1)S(1)}, u32[]{:S(2)}, u32[]{:S(2)}) collective-permute-start(bf16[16,4096]{1,0:T(8,128)(2,1)S(1)} %collective-permute-done.1.rest_2_), channel_id=1, source_target_pairs={{0,4},{2,6},{4,0},{6,2},{8,12},{10,14},{12,8},{14,10},{16,20},{18,... | collective-permute-start | bytes 393224 | tf_op jit(solution)/shard_map/ppermute | solution.py:36
  222.4 6.7 %collective-permute-start.6 = (bf16[16,4096]{1,0:T(8,128)(2,1)S(1)}, bf16[16,4096]{1,0:T(8,128)(2,1)S(1)}, u32[]{:S(2)}, u32[]{:S(2)}) collective-permute-start(bf16[16,4096]{1,0:T(8,128)(2,1)S(1)} %collective-permute-done.2.rest_3_), channel_id=1, source_target_pairs={{0,4},{2,6},{4,0},{6,2},{8,12},{10,14},{12,8},{14,10},{16,20},{18,... | collective-permute-start | bytes 393224 | tf_op jit(solution)/shard_map/ppermute | solution.py:36
  222.4 6.6 %collective-permute-start.10 = (bf16[16,4096]{1,0:T(8,128)(2,1)S(1)}, bf16[16,4096]{1,0:T(8,128)(2,1)S(1)}, u32[]{:S(2)}, u32[]{:S(2)}) collective-permute-start(bf16[16,4096]{1,0:T(8,128)(2,1)S(1)} %collective-permute-done.2.rest_3_), channel_id=1, source_target_pairs={{0,2},{2,0},{4,6},{6,4},{8,10},{10,8},{12,14},{14,12},{16,18},{18,... | collective-permute-start | bytes 393224 | tf_op jit(solution)/shard_map/ppermute | solution.py:36
  222.5 7.1 %collective-permute-start.8 = (bf16[16,4096]{1,0:T(8,128)(2,1)S(1)}, bf16[16,4096]{1,0:T(8,128)(2,1)S(1)}, u32[]{:S(2)}, u32[]{:S(2)}) collective-permute-start(bf16[16,4096]{1,0:T(8,128)(2,1)S(1)} %collective-permute-done.rest_1_), channel_id=1, source_target_pairs={{0,2},{2,0},{4,6},{6,4},{8,10},{10,8},{12,14},{14,12},{16,18},{18,... | collective-permute-start | bytes 393224 | tf_op jit(solution)/shard_map/ppermute | solution.py:36
  223.5 6.1 %collective-permute-start.9 = (bf16[16,4096]{1,0:T(8,128)(2,1)S(1)}, bf16[16,4096]{1,0:T(8,128)(2,1)S(1)}, u32[]{:S(2)}, u32[]{:S(2)}) collective-permute-start(bf16[16,4096]{1,0:T(8,128)(2,1)S(1)} %collective-permute-done.1.rest_2_), channel_id=1, source_target_pairs={{0,2},{2,0},{4,6},{6,4},{8,10},{10,8},{12,14},{14,12},{16,18},{18,... | collective-permute-start | bytes 393224 | tf_op jit(solution)/shard_map/ppermute | solution.py:36
  226.7 3.0 %collective-permute-start.11 = (bf16[16,4096]{1,0:T(8,128)(2,1)S(1)}, bf16[16,4096]{1,0:T(8,128)(2,1)S(1)}, u32[]{:S(2)}, u32[]{:S(2)}) collective-permute-start(bf16[16,4096]{1,0:T(8,128)(2,1)S(1)} %collective-permute-done.3.rest_4_), channel_id=1, source_target_pairs={{0,2},{2,0},{4,6},{6,4},{8,10},{10,8},{12,14},{14,12},{16,18},{18,... | collective-permute-start | bytes 393224 | tf_op jit(solution)/shard_map/ppermute | solution.py:36
  229.0 1.3 collective-permute-start.12
  229.0 1.5 collective-permute-start.13
  229.5 1.3 collective-permute-start.14
  235.3 8.1 %collective-permute-start.15 = (bf16[128,512]{1,0:T(8,128)(2,1)S(1)}, bf16[128,512]{1,0:T(8,128)(2,1)S(1)}, u32[]{:S(2)}, u32[]{:S(2)}) collective-permute-start(bf16[128,512]{1,0:T(8,128)(2,1)S(1)} %get-tuple-element.5), channel_id=1, source_target_pairs={{0,1},{1,0},{2,3},{3,2},{4,5},{5,4},{6,7},{7,6},{8,9},{9,8},{10,11... | collective-permute-start | bytes 393224 | tf_op jit(solution)/shard_map/ppermute | solution.py:301

commit v7 on v5

v7 whole, which is shorter than its diff:
```python
import functools
import math

import jax
import jax.numpy as jnp
from jax import lax
from jax.experimental import pallas as pl
from jax.experimental.pallas import tpu as pltpu
from jax.sharding import PartitionSpec as P

HD = 128
MAX_PAGES = 2
WAVE = 3
ROW_UNROLL = 4
EARLY = 4
VMEM_LIMIT = 40 * 1024 * 1024


def factors(groups):
    near = math.gcd(groups, 4)
    return groups // near, near


def uniform(step, swap, dims):
    return tuple(((z + step) % dims[0], swap) for z in range(dims[0]))


def page_rounds(dims):
    far, near = dims
    if far != 4:
        near_rounds = [uniform(0, n, dims) for n in range(1, near)]
        return near_rounds + [uniform(z, n, dims) for z in range(1, far) for n in range(near)]
    outer = [((2, n), (0, n), (3, n), (1, n)) for n in range(near)]
    inner = [((1, n), (3, n), (0, n), (2, n)) for n in range(near)]
    outer += [((3, n), (1, n), (2, n), (0, n)) for n in range(1, near)]
    inner += [((0, n), (2, n), (1, n), (3, n)) for n in range(1, near)]
    return outer + [((3, 0), (2, 0), (1, 0), (0, 0))] + inner


def reverse(route):
    sources = {to: (z, swap) for z, (to, swap) in enumerate(route)}
    return tuple(sources[z] for z in range(len(route)))


def routed(me, route, dims):
    near = dims[1]
    z = me // near
    to, swap = jnp.int32(route[0][0]), jnp.int32(route[0][1])
    for place in range(1, dims[0]):
        to = jnp.where(z == place, route[place][0], to)
        swap = jnp.where(z == place, route[place][1], swap)
    return to * near + (me % near ^ swap)


def send_by(array, route, dims):
    far, near = dims
    pairs = [
        (z * near + n, route[z][0] * near + (n ^ route[z][1])) for z in range(far) for n in range(near)
    ]
    return lax.ppermute(array, "group", pairs)


def gather_shards(shard, dims):
    far, near = dims
    held = {(0, 0): shard}
    swaps = [1 << i for i in reversed(range(near.bit_length() - 1))]
    for stage in [[(z, 0) for z in range(1, far)]] + [[(0, n)] for n in swaps]:
        incoming = {}
        for step in stage:
            for offset, array in held.items():
                moved = send_by(array, uniform(*step, dims), dims)
                incoming[offset[0] + step[0], offset[1] | step[1]] = moved
        held.update(incoming)
    return held


def packed(lengths, prefill_of, decode_of, groups):
    bits = (groups - 1).bit_length()
    return (lengths << 2 * bits) | (prefill_of << bits) | decode_of


def unpacked(entry, groups):
    bits = (groups - 1).bit_length()
    mask = (1 << bits) - 1
    return entry >> 2 * bits, (entry >> bits) & mask, entry & mask


def prepare_kernel(dims, routes, own, table_hbm, pool, *rest):
    aliased = 0 if own else 1
    received, *sends = rest[aliased : aliased + 1 + len(routes)]
    table, held, zero_page, start_of, count_of, table_sem, in_sems, out_sem = rest[aliased + 1 + len(routes) :]
    me = lax.axis_index("group")
    groups = lax.axis_size("group")
    page_size = pool.shape[1]
    copy = pltpu.make_async_copy(table_hbm, table, table_sem)
    copy.start()
    for d in range(groups + 1):
        start_of[d] = 0
        count_of[d] = 0
    zero_page[...] = jnp.zeros_like(zero_page)
    copy.wait()

    def visit(r, running):
        length, home, destination = unpacked(table[r], groups)
        mine = home == me
        count = (length + page_size - 1) // page_size
        to = jnp.where(mine, destination, groups)
        start_of[to] = running
        count_of[to] = count
        return running + jnp.where(mine, count, 0)

    lax.fori_loop(0, table.shape[0], visit, jnp.int32(0), unroll=8)
    targets = [(routed(me, route, dims), send, 0) for route, send in zip(routes, sends)]
    if own:
        targets.append((me, received, me * MAX_PAGES))

    def each(do):
        for i, (to, target, base) in enumerate(targets):
            for page in range(MAX_PAGES):
                there = page < count_of[to]
                source = pool.at[jnp.where(there, start_of[to] + page, 0)]
                buffer, place = held.at[i, page], target.at[base + page]
                do(there, (source, buffer, in_sems.at[i, page]), (buffer, place, out_sem), (zero_page, place, out_sem))

    def fetch(there, load, store, blank):
        @pl.when(there)
        def _():
            pltpu.make_async_copy(*load).start()

        @pl.when(jnp.logical_not(there))
        def _():
            pltpu.make_async_copy(*blank).start()

    def forward(there, load, store, blank):
        @pl.when(there)
        def _():
            pltpu.make_async_copy(*load).wait()
            pltpu.make_async_copy(*store).start()

    def finish(there, load, store, blank):
        pltpu.make_async_copy(*blank).wait()

    each(fetch)
    each(forward)
    each(finish)


def prepare(dims, routes, table, pool, received=None):
    own = received is None
    groups = lax.axis_size("group")
    page = pool.shape[1:]
    blocks = len(routes) + (1 if own else 0)
    hbm = pl.BlockSpec(memory_space=pl.ANY)
    block = jax.ShapeDtypeStruct((MAX_PAGES,) + page, pool.dtype)
    outs = [jax.ShapeDtypeStruct((groups * MAX_PAGES,) + page, pool.dtype)] + [block] * len(routes)
    operands = [table, pool] + ([] if own else [received])
    return pl.pallas_call(
        functools.partial(prepare_kernel, dims, routes, own),
        out_shape=outs,
        in_specs=[hbm] * len(operands),
        out_specs=[hbm] * len(outs),
        scratch_shapes=[
            pltpu.SMEM(table.shape, jnp.int32),
            pltpu.VMEM((blocks, MAX_PAGES) + page, pool.dtype),
            pltpu.VMEM(page, pool.dtype),
            pltpu.SMEM((groups + 1,), jnp.int32),
            pltpu.SMEM((groups + 1,), jnp.int32),
            pltpu.SemaphoreType.DMA,
            pltpu.SemaphoreType.DMA((blocks, MAX_PAGES)),
            pltpu.SemaphoreType.DMA,
        ],
        input_output_aliases={} if own else {2: 0},
        compiler_params=pltpu.CompilerParams(vmem_limit_bytes=VMEM_LIMIT),
        cost_estimate=pl.CostEstimate(
            flops=0, bytes_accessed=4 * blocks * MAX_PAGES * math.prod(page), transcendentals=0
        ),
        name="outgoing_pages",
    )(*operands)


def attend_row(query, pages, length):
    first, second = pages
    kv_heads = first.shape[1] // (2 * HD)
    share = query.shape[0] // kv_heads
    scores = []
    for h in range(kv_heads):
        columns = slice(2 * h * HD, (2 * h + 1) * HD)
        keys = jnp.concatenate([first[:, columns], second[:, columns]], axis=0)
        every = lax.dot_general(
            query, keys, (((1,), (1,)), ((), ())), preferred_element_type=jnp.float32
        )
        scores.append(every[h * share : (h + 1) * share])
    score = jnp.concatenate(scores, axis=0) * (1.0 / math.sqrt(HD))
    live = lax.broadcasted_iota(jnp.int32, score.shape, 1) < length
    masked = jnp.where(live, score, -1e30)
    highest = jnp.max(masked, axis=1, keepdims=True)
    weights = jnp.where(live, jnp.exp(masked - highest), 0.0)
    totals = jnp.sum(weights, axis=1, keepdims=True)
    rounded = weights.astype(jnp.bfloat16)
    mixtures = []
    for h in range(kv_heads):
        columns = slice((2 * h + 1) * HD, (2 * h + 2) * HD)
        values = jnp.concatenate([first[:, columns], second[:, columns]], axis=0)
        every = jnp.dot(rounded, values, preferred_element_type=jnp.float32)
        mixtures.append(every[h * share : (h + 1) * share])
    return jnp.concatenate(mixtures, axis=0) / totals


def settle_kernel(dims, routes, own, last, table, row_request, queries, rows_in, received_in, *rest):
    blocks = rest[: len(routes)]
    received, out, rows, held, list_row, list_block, list_length, in_sems, out_sems = rest[len(routes) :]
    me = lax.axis_index("group")
    row_local, query_heads, _ = queries.shape
    mine = pl.ds(me * MAX_PAGES, MAX_PAGES)
    origins = [routed(me, reverse(route), dims) for route in routes]
    places = [pl.ds(origin * MAX_PAGES, MAX_PAGES) for origin in origins]
    sources = list(blocks) + ([received_in.at[mine]] if own else [])
    origins += [me] if own else []
    loads = [pltpu.make_async_copy(s, held.at[i], in_sems.at[i]) for i, s in enumerate(sources)]
    stores = [
        pltpu.make_async_copy(held.at[i], received.at[place], out_sems.at[i]) for i, place in enumerate(places)
    ]
    for load in loads:
        load.start()

    found = jnp.int32(0)
    for b in range(row_local):
        length, home, _ = unpacked(table[row_request[me * row_local + b]], math.prod(dims))
        block, match = jnp.int32(0), jnp.int32(0)
        for i, origin in enumerate(origins):
            block = jnp.where(home == origin, i, block)
            match = jnp.where(home == origin, 1, match)
        list_row[found] = b
        list_block[found] = block
        list_length[found] = length
        found = found + match
    for i in range(ROW_UNROLL):
        list_row[found + i] = row_local
        list_block[found + i] = 0
        list_length[found + i] = 1
    rows[:row_local] = rows_in[...]
    for load in loads:
        load.wait()
    for store in stores:
        store.start()

    @pl.loop(0, (found + ROW_UNROLL - 1) // ROW_UNROLL)
    def _(step):
        results = []
        for i in range(ROW_UNROLL):
            at = step * ROW_UNROLL + i
            query = queries[jnp.minimum(list_row[at], row_local - 1)]
            pages = [held[list_block[at], page] for page in range(MAX_PAGES)]
            results.append(attend_row(query, pages, list_length[at]))
        for i, result in enumerate(results):
            rows[list_row[step * ROW_UNROLL + i]] = result

    if last:
        for h in range(query_heads):
            out[:, h * HD : (h + 1) * HD] = rows[:row_local, h, :].astype(out.dtype)
    else:
        out[...] = rows[:row_local]
    for store in stores:
        store.wait()


def settle(dims, routes, own, last, table, row_request, queries, rows, received, blocks):
    row_local, query_heads, _ = queries.shape
    smem = pl.BlockSpec(memory_space=pltpu.SMEM)
    vmem = pl.BlockSpec(memory_space=pltpu.VMEM)
    hbm = pl.BlockSpec(memory_space=pl.ANY)
    count = len(blocks) + (1 if own else 0)
    if last:
        out = jax.ShapeDtypeStruct((row_local, query_heads * HD), jnp.bfloat16)
    else:
        out = jax.ShapeDtypeStruct(rows.shape, rows.dtype)
    return pl.pallas_call(
        functools.partial(settle_kernel, dims, routes, own, last),
        out_shape=[jax.ShapeDtypeStruct(received.shape, received.dtype), out],
        in_specs=[smem, smem, vmem, vmem, hbm] + [hbm] * len(blocks),
        out_specs=[hbm, vmem],
        scratch_shapes=[
            pltpu.VMEM((row_local + 1, query_heads, HD), jnp.float32),
            pltpu.VMEM((count, MAX_PAGES) + received.shape[1:], received.dtype),
            pltpu.SMEM((row_local + ROW_UNROLL,), jnp.int32),
            pltpu.SMEM((row_local + ROW_UNROLL,), jnp.int32),
            pltpu.SMEM((row_local + ROW_UNROLL,), jnp.int32),
            pltpu.SemaphoreType.DMA((count,)),
            pltpu.SemaphoreType.DMA((count,)),
        ],
        input_output_aliases={4: 0},
        compiler_params=pltpu.CompilerParams(vmem_limit_bytes=VMEM_LIMIT),
        cost_estimate=pl.CostEstimate(
            flops=1 << 30, bytes_accessed=4 * sum(b.size for b in blocks), transcendentals=1 << 18
        ),
        name="settle_pages",
    )(table, row_request, queries, rows, received, *blocks)


def project_kernel(dims, offsets, out_weight, *rest):
    shards = rest[: len(offsets)]
    own, *theirs = rest[len(offsets) : -3]
    attended, product, sems = rest[-3:]
    me = lax.axis_index("group")
    heads = lax.axis_size("head")
    my_head = lax.axis_index("head")
    row_local = shards[0].shape[0]
    share = own.shape[0]
    copies = []
    for i, offset in enumerate(offsets):
        place = pl.ds(routed(me, reverse(uniform(*offset, dims)), dims) * row_local, row_local)
        copies.append(pltpu.make_async_copy(shards[i], attended.at[place], sems.at[i]))
        copies[-1].start()
    for copy in copies:
        copy.wait()
    product[...] = jnp.dot(attended[...], out_weight[...], preferred_element_type=jnp.float32)
    own[...] = product[pl.ds(pl.multiple_of(my_head * share, share), share)]
    for ahead_by, target in enumerate(theirs, 1):
        start = pl.multiple_of(lax.rem(my_head + ahead_by, heads) * share, share)
        target[...] = product[pl.ds(start, share)].astype(target.dtype)


def project(dims, gathered, out_weight, heads):
    offsets = list(gathered)
    shards = [gathered[offset] for offset in offsets]
    row_local, width = shards[0].shape
    row_total = row_local * len(shards)
    share, columns = row_total // heads, out_weight.shape[1]
    vmem = pl.BlockSpec(memory_space=pltpu.VMEM)
    hbm = pl.BlockSpec(memory_space=pl.ANY)
    theirs = jax.ShapeDtypeStruct((share, columns), jnp.bfloat16)
    return pl.pallas_call(
        functools.partial(project_kernel, dims, offsets),
        out_shape=[jax.ShapeDtypeStruct((share, columns), jnp.float32)] + [theirs] * (heads - 1),
        in_specs=[vmem] + [hbm] * len(shards),
        out_specs=[vmem] * heads,
        scratch_shapes=[
            pltpu.VMEM((row_total, width), jnp.bfloat16),
            pltpu.VMEM((row_total, columns), jnp.float32),
            pltpu.SemaphoreType.DMA((len(shards),)),
        ],
        compiler_params=pltpu.CompilerParams(vmem_limit_bytes=VMEM_LIMIT),
        cost_estimate=pl.CostEstimate(
            flops=2 * row_total * width * columns, bytes_accessed=2 * out_weight.size, transcendentals=0
        ),
        name="project_rows",
    )(pltpu.with_memory_space_constraint(out_weight, pltpu.VMEM), *shards)


def local(kv_pool, lengths, prefill_of, decode_of, row_request, queries, out_weight):
    row_local, query_width = queries.shape
    query_heads = queries.reshape(row_local, query_width // HD, HD)
    heads = lax.axis_size("head")

    dims = factors(lax.axis_size("group"))
    routes = page_rounds(dims)
    table = packed(lengths, prefill_of, decode_of, math.prod(dims))
    received, *early = prepare(dims, routes[:EARLY], table, kv_pool)
    received, *late = prepare(dims, routes[EARLY:], table, kv_pool, received)
    arrived = [send_by(block, route, dims) for block, route in zip(early + late, routes)]
    rows = jnp.zeros(query_heads.shape, jnp.float32)
    for first in range(0, len(routes), WAVE):
        wave = slice(first, first + WAVE)
        last = first + WAVE >= len(routes)
        received, rows = settle(
            dims, routes[wave], first == 0, last, table, row_request, query_heads, rows, received, arrived[wave]
        )

    own, *theirs = project(dims, gather_shards(rows, dims), out_weight, heads)
    for ahead_by, part in enumerate(theirs, 1):
        pairs = [(h, (h + ahead_by) % heads) for h in range(heads)]
        own = own + lax.ppermute(part, "head", pairs).astype(jnp.float32)
    return (received, own.astype(jnp.bfloat16))


def solution(mesh):
    in_specs = (
        P("group", None, "head"),
        P(),
        P(),
        P(),
        P(),
        P("group", "head"),
        P("head", "group"),
    )
    out_specs = (P("group", None, "head"), P("head", "group"))
    return jax.shard_map(local, mesh=mesh, in_specs=in_specs, out_specs=out_specs, check_vma=False)
```

time: 238 us -> 235 us (0.987)
  starting transfers between devices: 80.7 us -> 60.5 us
  waiting for transfers between devices: 124 us -> 142 us
  Pallas kernels: 30.1 us -> 25.9 us
    ppermute x30, starting transfers between devices: 79.1 us -> 58.9 us  [send_by(): return lax.ppermute(array, 'group', pairs)]
    ppermute x30, waiting for transfers between devices: 119 us -> 138 us  [send_by(): return lax.ppermute(array, 'group', pairs)]
    pallas_call x7, Pallas kernels: 24.1 us -> 21.5 us  [the longest x5 13.4 us: settle(): pl.pallas_call(functools.partial(settle_kernel, dims, routes, own, last),...]
  transfers between devices with their start and end apart: 31 -> 31, of which waited for: 14 -> 20; matrix products, arithmetic and copies ran while one was open for 0% -> 0% of each run, Pallas kernels for 7% -> 6%
where the time goes in v7:
time: 235 us; the launch traced here: 234 us
  waiting for transfers between devices  142 us (60%)
  starting transfers between devices  60.5 us (26%)
  Pallas kernels  25.9 us (11%)
  local copies, waits for them, and re-layouts  3.43 us (1%)
    ppermute x30, waiting for transfers between devices, send_by(): return lax.ppermute(array, 'group', pairs)  138 us
    ppermute x30, starting transfers between devices, send_by(): return lax.ppermute(array, 'group', pairs)  58.9 us
    pallas_call x5, Pallas kernels, settle(): pl.pallas_call(functools.partial(settle_kernel, dims, routes, own, last),...  13.4 us
    pallas_call x2, Pallas kernels, prepare(): pl.pallas_call(functools.partial(prepare_kernel, dims, routes, own), out_...  8.09 us
  transfers between devices with their start and end apart: 31, of which 20 were waited for; matrix products, arithmetic and copies ran while one was open for 0% of the time, Pallas kernels for 6%

profile of v7, /device:TPU:0, one launch (start us, length us, event | category | flops | bytes accessed | tf_op | source)
XLA Modules:
  0.0 234.0 jit_solution(3772969831435475365)
XLA Ops:
  0.6 0.7 or_or_fusion.table_hbm.table
  1.3 3.4 %copy-done = bf16[32,128,1024]{2,1,0:T(8,128)(2,1)S(1)} copy-done((bf16[32,128,1024]{2,1,0:T(8,128)(2,1)S(1)}, bf16[32,128,1024]{2,1,0:T(8,128)(2,1)}, u32[]{:S(2)}) %copy-start) | copy-done | bytes 8388632
  4.7 4.0 %outgoing_pages.2 = (bf16[32,128,1024]{2,1,0:T(8,128)(2,1)}, bf16[2,128,1024]{2,1,0:T(8,128)(2,1)S(1)}, bf16[2,128,1024]{2,1,0:T(8,128)(2,1)S(1)}, bf16[2,128,10...) custom-call(s32[256]{0:T(256)S(1)} %or_or_fusion.table_hbm.table, bf16[32,128,1024]{2,1,0:T(8,128)(2,1)S(1)} %copy-done), custom_call_target="tpu_custom_call" | custom-call | bytes 5242880 | tf_op jit(solution)/shard_map/outgoing_pages/pallas_call | solution.py:157
  8.7 4.3 %collective-permute-start = (bf16[2,128,1024]{2,1,0:T(8,128)(2,1)S(1)}, bf16[2,128,1024]{2,1,0:T(8,128)(2,1)S(1)}, u32[]{:S(2)}, u32[]{:S(2)}) collective-permute-start(bf16[2,128,1024]{2,1,0:T(8,128)(2,1)S(1)} %get-tuple-element.33), channel_id=1, source_target_pairs={{0,16},{2,18},{4,20},{6,22},{8,0},{10,2},{12,4},{14,6},{16,24},{18... | collective-permute-start | bytes 1572872 | tf_op jit(solution)/shard_map/ppermute | solution.py:60
  13.0 0.7 collective-permute-start.1
  13.7 1.8 collective-permute-start.2
  15.5 4.1 %outgoing_pages.3 = (bf16[32,128,1024]{2,1,0:T(8,128)(2,1)}, bf16[2,128,1024]{2,1,0:T(8,128)(2,1)S(1)}, bf16[2,128,1024]{2,1,0:T(8,128)(2,1)S(1)}, bf16[2,128,10...) custom-call(s32[256]{0:T(256)S(1)} %or_or_fusion.table_hbm.table, ...), custom_call_target="tpu_custom_call", output_to_operand_aliasing={{0}: (2, {})} | custom-call | bytes 11534336 | tf_op jit(solution)/shard_map/outgoing_pages/pallas_call | solution.py:157
  19.6 3.3 %collective-permute-start.4 = (bf16[2,128,1024]{2,1,0:T(8,128)(2,1)S(1)}, bf16[2,128,1024]{2,1,0:T(8,128)(2,1)S(1)}, u32[]{:S(2)}, u32[]{:S(2)}) collective-permute-start(bf16[2,128,1024]{2,1,0:T(8,128)(2,1)S(1)} %get-tuple-element.39), channel_id=1, source_target_pairs={{0,26},{2,24},{4,30},{6,28},{8,10},{10,8},{12,14},{14,12},{16,18},... | collective-permute-start | bytes 1572872 | tf_op jit(solution)/shard_map/ppermute | solution.py:60
  22.9 2.4 %collective-permute-done.rest_0_ = bf16[2,128,1024]{2,1,0:T(8,128)(2,1)S(1)} collective-permute-done((bf16[2,128,1024]{2,1,0:T(8,128)(2,1)S(1)}, bf16[2,128,1024]{2,1,0:T(8,128)(2,1)S(1)}, u32[]{:S(2)}, u32[]{:S(2)}) %collective-permute-start) | collective-permute-done | bytes 524320 | tf_op jit(solution)/shard_map/ppermute | solution.py:60
  25.3 4.4 %collective-permute-start.5 = (bf16[2,128,1024]{2,1,0:T(8,128)(2,1)S(1)}, bf16[2,128,1024]{2,1,0:T(8,128)(2,1)S(1)}, u32[]{:S(2)}, u32[]{:S(2)}) collective-permute-start(bf16[2,128,1024]{2,1,0:T(8,128)(2,1)S(1)} %get-tuple-element.40), channel_id=1, source_target_pairs={{0,28},{2,30},{4,24},{6,26},{8,12},{10,14},{12,8},{14,10},{16,20},... | collective-permute-start | bytes 1572872 | tf_op jit(solution)/shard_map/ppermute | solution.py:60
  29.7 6.8 %collective-permute-done.1.rest_1_ = bf16[2,128,1024]{2,1,0:T(8,128)(2,1)S(1)} collective-permute-done((bf16[2,128,1024]{2,1,0:T(8,128)(2,1)S(1)}, bf16[2,128,1024]{2,1,0:T(8,128)(2,1)S(1)}, u32[]{:S(2)}, u32[]{:S(2)}) %collective-permute-start.1) | collective-permute-done | bytes 524320 | tf_op jit(solution)/shard_map/ppermute | solution.py:60
  36.6 4.1 %collective-permute-start.6 = (bf16[2,128,1024]{2,1,0:T(8,128)(2,1)S(1)}, bf16[2,128,1024]{2,1,0:T(8,128)(2,1)S(1)}, u32[]{:S(2)}, u32[]{:S(2)}) collective-permute-start(bf16[2,128,1024]{2,1,0:T(8,128)(2,1)S(1)} %get-tuple-element.43), channel_id=1, source_target_pairs={{0,30},{2,28},{4,26},{6,24},{8,14},{10,12},{12,10},{14,8},{16,22},... | collective-permute-start | bytes 1572872 | tf_op jit(solution)/shard_map/ppermute | solution.py:60
  40.7 7.8 %collective-permute-done.2.rest_2_ = bf16[2,128,1024]{2,1,0:T(8,128)(2,1)S(1)} collective-permute-done((bf16[2,128,1024]{2,1,0:T(8,128)(2,1)S(1)}, bf16[2,128,1024]{2,1,0:T(8,128)(2,1)S(1)}, u32[]{:S(2)}, u32[]{:S(2)}) %collective-permute-start.2) | collective-permute-done | bytes 524320 | tf_op jit(solution)/shard_map/ppermute | solution.py:60
  48.5 3.7 %collective-permute-start.7 = (bf16[2,128,1024]{2,1,0:T(8,128)(2,1)S(1)}, bf16[2,128,1024]{2,1,0:T(8,128)(2,1)S(1)}, u32[]{:S(2)}, u32[]{:S(2)}) collective-permute-start(bf16[2,128,1024]{2,1,0:T(8,128)(2,1)S(1)} %get-tuple-element.44), channel_id=1, source_target_pairs={{0,24},{2,26},{4,28},{6,30},{8,16},{10,18},{12,20},{14,22},{16,8},... | collective-permute-start | bytes 1572872 | tf_op jit(solution)/shard_map/ppermute | solution.py:60
  52.2 6.9 %collective-permute-done.3.rest_0_ = bf16[2,128,1024]{2,1,0:T(8,128)(2,1)S(1)} collective-permute-done((bf16[2,128,1024]{2,1,0:T(8,128)(2,1)S(1)}, bf16[2,128,1024]{2,1,0:T(8,128)(2,1)S(1)}, u32[]{:S(2)}, u32[]{:S(2)}) %collective-permute-start.3) | collective-permute-done | bytes 524320 | tf_op jit(solution)/shard_map/ppermute | solution.py:60
  59.1 1.1 collective-permute-start.8
  60.3 10.1 %collective-permute-done.4.rest_1_ = bf16[2,128,1024]{2,1,0:T(8,128)(2,1)S(1)} collective-permute-done((bf16[2,128,1024]{2,1,0:T(8,128)(2,1)S(1)}, bf16[2,128,1024]{2,1,0:T(8,128)(2,1)S(1)}, u32[]{:S(2)}, u32[]{:S(2)}) %collective-permute-start.4) | collective-permute-done | bytes 524320 | tf_op jit(solution)/shard_map/ppermute | solution.py:60
  70.4 13.9 %collective-permute-done.5.rest_2_ = bf16[2,128,1024]{2,1,0:T(8,128)(2,1)S(1)} collective-permute-done((bf16[2,128,1024]{2,1,0:T(8,128)(2,1)S(1)}, bf16[2,128,1024]{2,1,0:T(8,128)(2,1)S(1)}, u32[]{:S(2)}, u32[]{:S(2)}) %collective-permute-start.5) | collective-permute-done | bytes 524320 | tf_op jit(solution)/shard_map/ppermute | solution.py:60
  84.2 9.1 %collective-permute-done.6.rest_0_ = bf16[2,128,1024]{2,1,0:T(8,128)(2,1)S(1)} collective-permute-done((bf16[2,128,1024]{2,1,0:T(8,128)(2,1)S(1)}, bf16[2,128,1024]{2,1,0:T(8,128)(2,1)S(1)}, u32[]{:S(2)}, u32[]{:S(2)}) %collective-permute-start.6) | collective-permute-done | bytes 524320 | tf_op jit(solution)/shard_map/ppermute | solution.py:60
  93.4 12.4 %collective-permute-done.7.rest_1_ = bf16[2,128,1024]{2,1,0:T(8,128)(2,1)S(1)} collective-permute-done((bf16[2,128,1024]{2,1,0:T(8,128)(2,1)S(1)}, bf16[2,128,1024]{2,1,0:T(8,128)(2,1)S(1)}, u32[]{:S(2)}, u32[]{:S(2)}) %collective-permute-start.7) | collective-permute-done | bytes 524320 | tf_op jit(solution)/shard_map/ppermute | solution.py:60
  105.7 21.5 %collective-permute-done.8.rest_2_ = bf16[2,128,1024]{2,1,0:T(8,128)(2,1)S(1)} collective-permute-done((bf16[2,128,1024]{2,1,0:T(8,128)(2,1)S(1)}, bf16[2,128,1024]{2,1,0:T(8,128)(2,1)S(1)}, u32[]{:S(2)}, u32[]{:S(2)}) %collective-permute-start.8) | collective-permute-done | bytes 524320 | tf_op jit(solution)/shard_map/ppermute | solution.py:60
  127.2 1.5 collective-permute-start.13
  128.7 9.5 %collective-permute-done.9.rest_0_ = bf16[2,128,1024]{2,1,0:T(8,128)(2,1)S(1)} collective-permute-done((bf16[2,128,1024]{2,1,0:T(8,128)(2,1)S(1)}, bf16[2,128,1024]{2,1,0:T(8,128)(2,1)S(1)}, u32[]{:S(2)}, u32[]{:S(2)}) %collective-permute-start.9) | collective-permute-done | bytes 524320 | tf_op jit(solution)/shard_map/ppermute | solution.py:60
  138.2 1.4 collective-permute-start.14
  139.7 3.1 %settle_pages.5 = (bf16[32,128,1024]{2,1,0:T(8,128)(2,1)}, f32[16,32,128]{2,1,0:T(8,128)S(1)}) custom-call(s32[256]{0:T(256)S(1)} %or_or_fusion.table_hbm.table, s32[256]{0:T(256)S(1)} %copy-done.2, bf16[16,32,128]{2,1,0:T(8,128)(2,1)S(1)} %bitcast.2, f32[16,32,128]{2,1,0:T(8,128)S(1)} %broadcast_in_dim.3.rows_in, ...), custom_call_target="tpu_custom_call", output_to_operand_aliasing={{0}: (4, {})} | custom-call | flops 1073741824 | bytes 3145728 | tf_op jit(solution)/shard_map/settle_pages/pallas_call | solution.py:277
  142.8 2.2 settle_pages.6
  145.0 3.5 %settle_pages.7 = (bf16[32,128,1024]{2,1,0:T(8,128)(2,1)}, f32[16,32,128]{2,1,0:T(8,128)S(1)}) custom-call(s32[256]{0:T(256)S(1)} %or_or_fusion.table_hbm.table, s32[256]{0:T(256)S(1)} %copy-done.2, bf16[16,32,128]{2,1,0:T(8,128)(2,1)S(1)} %bitcast.4, f32[16,32,128]{2,1,0:T(8,128)S(1)} %get-tuple-element.41.rows_in, ...), custom_call_target="tpu_custom_call", output_to_operand_aliasing={{0}: (4, {})} | custom-call | flops 1073741824 | bytes 3145728 | tf_op jit(solution)/shard_map/settle_pages/pallas_call | solution.py:277
  148.5 2.2 collective-permute-done.10.rest_1_
  150.7 11.0 %collective-permute-done.11.rest_2_ = bf16[2,128,1024]{2,1,0:T(8,128)(2,1)S(1)} collective-permute-done((bf16[2,128,1024]{2,1,0:T(8,128)(2,1)S(1)}, bf16[2,128,1024]{2,1,0:T(8,128)(2,1)S(1)}, u32[]{:S(2)}, u32[]{:S(2)}) %collective-permute-start.11) | collective-permute-done | bytes 524320 | tf_op jit(solution)/shard_map/ppermute | solution.py:60
  161.7 2.2 settle_pages.8
  164.5 9.2 %collective-permute-done.14.rest_2_ = bf16[2,128,1024]{2,1,0:T(8,128)(2,1)S(1)} collective-permute-done((bf16[2,128,1024]{2,1,0:T(8,128)(2,1)S(1)}, bf16[2,128,1024]{2,1,0:T(8,128)(2,1)S(1)}, u32[]{:S(2)}, u32[]{:S(2)}) %collective-permute-start.14) | collective-permute-done | bytes 524320 | tf_op jit(solution)/shard_map/ppermute | solution.py:60
  173.7 2.4 %settle_pages.9 = (bf16[32,128,1024]{2,1,0:T(8,128)(2,1)}, bf16[16,4096]{1,0:T(8,128)(2,1)S(1)}) custom-call(s32[256]{0:T(256)S(1)} %or_or_fusion.table_hbm.table, s32[256]{0:T(256)S(1)} %copy-done.2, bf16[16,32,128]{2,1,0:T(8,128)(2,1)S(1)} %bitcast.6, f32[16,32,128]{2,1,0:T(8,128)S(1)} %get-tuple-element.51.rows_in, ...), custom_call_target="tpu_custom_call", output_to_operand_aliasing={{0}: (4, {})} | custom-call | flops 1073741824 | bytes 3145728 | tf_op jit(solution)/shard_map/settle_pages/pallas_call | solution.py:277
  176.1 1.5 collective-permute-start.18
  177.6 2.5 %collective-permute-start.17 = (bf16[16,4096]{1,0:T(8,128)(2,1)S(1)}, bf16[16,4096]{1,0:T(8,128)(2,1)S(1)}, u32[]{:S(2)}, u32[]{:S(2)}) collective-permute-start(bf16[16,4096]{1,0:T(8,128)(2,1)S(1)} %get-tuple-element.57.rest_0_), channel_id=1, source_target_pairs={{0,24},{2,26},{4,28},{6,30},{8,0},{10,2},{12,4},{14,6},{16,8},{18,... | collective-permute-start | bytes 393224 | tf_op jit(solution)/shard_map/ppermute | solution.py:60
  180.1 1.6 collective-permute-start.22
  181.7 22.1 %collective-permute-start.16 = (bf16[16,4096]{1,0:T(8,128)(2,1)S(1)}, bf16[16,4096]{1,0:T(8,128)(2,1)S(1)}, u32[]{:S(2)}, u32[]{:S(2)}) collective-permute-start(bf16[16,4096]{1,0:T(8,128)(2,1)S(1)} %get-tuple-element.57.rest_0_), channel_id=1, source_target_pairs={{0,16},{2,18},{4,20},{6,22},{8,24},{10,26},{12,28},{14,30},{16,0},... | collective-permute-start | bytes 393224 | tf_op jit(solution)/shard_map/ppermute | solution.py:60
  203.8 0.9 collective-permute-start.15
  204.7 0.8 collective-permute-done.17.rest_3_
  205.6 1.3 collective-permute-start.21
  206.9 8.1 %collective-permute-done.16.rest_2_ = bf16[16,4096]{1,0:T(8,128)(2,1)S(1)} collective-permute-done((bf16[16,4096]{1,0:T(8,128)(2,1)S(1)}, bf16[16,4096]{1,0:T(8,128)(2,1)S(1)}, u32[]{:S(2)}, u32[]{:S(2)}) %collective-permute-start.16) | collective-permute-done | bytes 131104 | tf_op jit(solution)/shard_map/ppermute | solution.py:60
  215.0 1.2 collective-permute-start.20
  216.2 0.8 collective-permute-start.19
  217.6 3.0 %collective-permute-done.20.rest_6_ = bf16[16,4096]{1,0:T(8,128)(2,1)S(1)} collective-permute-done((bf16[16,4096]{1,0:T(8,128)(2,1)S(1)}, bf16[16,4096]{1,0:T(8,128)(2,1)S(1)}, u32[]{:S(2)}, u32[]{:S(2)}) %collective-permute-start.20) | collective-permute-done | bytes 131104 | tf_op jit(solution)/shard_map/ppermute | solution.py:60
  220.6 1.4 collective-permute-done.19.rest_5_
  222.1 1.3 collective-permute-done.27.rest_13_
  223.4 4.3 %project_rows.1 = (f32[128,512]{1,0:T(8,128)S(1)}, bf16[128,512]{1,0:T(8,128)(2,1)S(1)}) custom-call(bf16[4096,512]{1,0:T(8,128)(2,1)S(1)} %copy-done.1, bf16[16,4096]{1,0:T(8,128)(2,1)S(1)} %get-tuple-element.57.rest_0_, bf16[16,4096]{1,0:T(8,128)(2,1)S(1)} %collective-permute-done.15.rest_1_, bf16[16,4096]{1,0:T(8,128)(2,1)S(1)} %collective-permute-done.16.rest_2_, ...), custom_call_target="tpu_custom_call" | custom-call | flops 1073741824 | bytes 4194304 | tf_op jit(solution)/shard_map/project_rows/pallas_call | solution.py:332
  227.7 1.6 collective-permute-start.30
  229.3 4.1 %collective-permute-done.30 = bf16[128,512]{1,0:T(8,128)(2,1)S(1)} collective-permute-done((bf16[128,512]{1,0:T(8,128)(2,1)S(1)}, bf16[128,512]{1,0:T(8,128)(2,1)S(1)}, u32[]{:S(2)}, u32[]{:S(2)}) %collective-permute-start.30) | collective-permute-done | bytes 131104 | tf_op jit(solution)/shard_map/ppermute | solution.py:372
  (34 shorter events, 1.9 us)
Async XLA Ops:
  1.3 3.4 %copy-start = (bf16[32,128,1024]{2,1,0:T(8,128)(2,1)S(1)}, bf16[32,128,1024]{2,1,0:T(8,128)(2,1)}, u32[]{:S(2)}) copy-start(bf16[32,128,1024]{2,1,0:T(8,128)(2,1)} %pool.3) | copy-start | bytes 25165828
  8.7 16.6 %collective-permute-start = (bf16[2,128,1024]{2,1,0:T(8,128)(2,1)S(1)}, bf16[2,128,1024]{2,1,0:T(8,128)(2,1)S(1)}, u32[]{:S(2)}, u32[]{:S(2)}) collective-permute-start(bf16[2,128,1024]{2,1,0:T(8,128)(2,1)S(1)} %get-tuple-element.33), channel_id=1, source_target_pairs={{0,16},{2,18},{4,20},{6,22},{8,0},{10,2},{12,4},{14,6},{16,24},{18... | collective-permute-start | bytes 1572872 | tf_op jit(solution)/shard_map/ppermute | solution.py:60
  13.0 23.6 %collective-permute-start.1 = (bf16[2,128,1024]{2,1,0:T(8,128)(2,1)S(1)}, bf16[2,128,1024]{2,1,0:T(8,128)(2,1)S(1)}, u32[]{:S(2)}, u32[]{:S(2)}) collective-permute-start(bf16[2,128,1024]{2,1,0:T(8,128)(2,1)S(1)} %get-tuple-element.34), channel_id=1, source_target_pairs={{0,18},{2,16},{4,22},{6,20},{8,2},{10,0},{12,6},{14,4},{16,26},{18... | collective-permute-start | bytes 1572872 | tf_op jit(solution)/shard_map/ppermute | solution.py:60
  13.7 34.8 %collective-permute-start.2 = (bf16[2,128,1024]{2,1,0:T(8,128)(2,1)S(1)}, bf16[2,128,1024]{2,1,0:T(8,128)(2,1)S(1)}, u32[]{:S(2)}, u32[]{:S(2)}) collective-permute-start(bf16[2,128,1024]{2,1,0:T(8,128)(2,1)S(1)} %get-tuple-element.35), channel_id=1, source_target_pairs={{0,20},{2,22},{4,16},{6,18},{8,4},{10,6},{12,0},{14,2},{16,28},{18... | collective-permute-start | bytes 1572872 | tf_op jit(solution)/shard_map/ppermute | solution.py:60
  15.5 43.6 %collective-permute-start.3 = (bf16[2,128,1024]{2,1,0:T(8,128)(2,1)S(1)}, bf16[2,128,1024]{2,1,0:T(8,128)(2,1)S(1)}, u32[]{:S(2)}, u32[]{:S(2)}) collective-permute-start(bf16[2,128,1024]{2,1,0:T(8,128)(2,1)S(1)} %get-tuple-element.38), channel_id=1, source_target_pairs={{0,22},{2,20},{4,18},{6,16},{8,6},{10,4},{12,2},{14,0},{16,30},{18... | collective-permute-start | bytes 1572872 | tf_op jit(solution)/shard_map/ppermute | solution.py:60
  15.5 124.1 %copy-start.3 = (bf16[16,4096]{1,0:T(8,128)(2,1)S(1)}, bf16[16,4096]{1,0:T(8,128)(2,1)}, u32[]{:S(2)}) copy-start(bf16[16,4096]{1,0:T(8,128)(2,1)} %param.12) | copy-start | bytes 393220
  15.5 124.2 %copy-start.2 = (s32[256]{0:T(256)S(1)}, s32[256]{0:T(256)}, u32[]{:S(2)}) copy-start(s32[256]{0:T(256)} %row_request.9) | copy-start | bytes 3076
  19.6 50.8 %collective-permute-start.4 = (bf16[2,128,1024]{2,1,0:T(8,128)(2,1)S(1)}, bf16[2,128,1024]{2,1,0:T(8,128)(2,1)S(1)}, u32[]{:S(2)}, u32[]{:S(2)}) collective-permute-start(bf16[2,128,1024]{2,1,0:T(8,128)(2,1)S(1)} %get-tuple-element.39), channel_id=1, source_target_pairs={{0,26},{2,24},{4,30},{6,28},{8,10},{10,8},{12,14},{14,12},{16,18},... | collective-permute-start | bytes 1572872 | tf_op jit(solution)/shard_map/ppermute | solution.py:60
  25.3 58.9 %collective-permute-start.5 = (bf16[2,128,1024]{2,1,0:T(8,128)(2,1)S(1)}, bf16[2,128,1024]{2,1,0:T(8,128)(2,1)S(1)}, u32[]{:S(2)}, u32[]{:S(2)}) collective-permute-start(bf16[2,128,1024]{2,1,0:T(8,128)(2,1)S(1)} %get-tuple-element.40), channel_id=1, source_target_pairs={{0,28},{2,30},{4,24},{6,26},{8,12},{10,14},{12,8},{14,10},{16,20},... | collective-permute-start | bytes 1572872 | tf_op jit(solution)/shard_map/ppermute | solution.py:60
  36.6 56.8 %collective-permute-start.6 = (bf16[2,128,1024]{2,1,0:T(8,128)(2,1)S(1)}, bf16[2,128,1024]{2,1,0:T(8,128)(2,1)S(1)}, u32[]{:S(2)}, u32[]{:S(2)}) collective-permute-start(bf16[2,128,1024]{2,1,0:T(8,128)(2,1)S(1)} %get-tuple-element.43), channel_id=1, source_target_pairs={{0,30},{2,28},{4,26},{6,24},{8,14},{10,12},{12,10},{14,8},{16,22},... | collective-permute-start | bytes 1572872 | tf_op jit(solution)/shard_map/ppermute | solution.py:60
  48.5 57.2 %collective-permute-start.7 = (bf16[2,128,1024]{2,1,0:T(8,128)(2,1)S(1)}, bf16[2,128,1024]{2,1,0:T(8,128)(2,1)S(1)}, u32[]{:S(2)}, u32[]{:S(2)}) collective-permute-start(bf16[2,128,1024]{2,1,0:T(8,128)(2,1)S(1)} %get-tuple-element.44), channel_id=1, source_target_pairs={{0,24},{2,26},{4,28},{6,30},{8,16},{10,18},{12,20},{14,22},{16,8},... | collective-permute-start | bytes 1572872 | tf_op jit(solution)/shard_map/ppermute | solution.py:60
  59.1 68.1 %collective-permute-start.8 = (bf16[2,128,1024]{2,1,0:T(8,128)(2,1)S(1)}, bf16[2,128,1024]{2,1,0:T(8,128)(2,1)S(1)}, u32[]{:S(2)}, u32[]{:S(2)}) collective-permute-start(bf16[2,128,1024]{2,1,0:T(8,128)(2,1)S(1)} %get-tuple-element.45), channel_id=1, source_target_pairs={{0,8},{2,10},{4,12},{6,14},{8,24},{10,26},{12,28},{14,30},{16,0},{... | collective-permute-start | bytes 1572872 | tf_op jit(solution)/shard_map/ppermute | solution.py:60
  70.4 67.9 %collective-permute-start.9 = (bf16[2,128,1024]{2,1,0:T(8,128)(2,1)S(1)}, bf16[2,128,1024]{2,1,0:T(8,128)(2,1)S(1)}, u32[]{:S(2)}, u32[]{:S(2)}) collective-permute-start(bf16[2,128,1024]{2,1,0:T(8,128)(2,1)S(1)} %get-tuple-element.48), channel_id=1, source_target_pairs={{0,10},{2,8},{4,14},{6,12},{8,26},{10,24},{12,30},{14,28},{16,2},{... | collective-permute-start | bytes 1572872 | tf_op jit(solution)/shard_map/ppermute | solution.py:60
  84.2 66.5 %collective-permute-start.10 = (bf16[2,128,1024]{2,1,0:T(8,128)(2,1)S(1)}, bf16[2,128,1024]{2,1,0:T(8,128)(2,1)S(1)}, u32[]{:S(2)}, u32[]{:S(2)}) collective-permute-start(bf16[2,128,1024]{2,1,0:T(8,128)(2,1)S(1)} %get-tuple-element.49), channel_id=1, source_target_pairs={{0,12},{2,14},{4,8},{6,10},{8,28},{10,30},{12,24},{14,26},{16,4},{... | collective-permute-start | bytes 1572872 | tf_op jit(solution)/shard_map/ppermute | solution.py:60
  93.4 68.4 %collective-permute-start.11 = (bf16[2,128,1024]{2,1,0:T(8,128)(2,1)S(1)}, bf16[2,128,1024]{2,1,0:T(8,128)(2,1)S(1)}, u32[]{:S(2)}, u32[]{:S(2)}) collective-permute-start(bf16[2,128,1024]{2,1,0:T(8,128)(2,1)S(1)} %get-tuple-element.50), channel_id=1, source_target_pairs={{0,14},{2,12},{4,10},{6,8},{8,30},{10,28},{12,26},{14,24},{16,6},{... | collective-permute-start | bytes 1572872 | tf_op jit(solution)/shard_map/ppermute | solution.py:60
  105.7 58.2 %collective-permute-start.12 = (bf16[2,128,1024]{2,1,0:T(8,128)(2,1)S(1)}, bf16[2,128,1024]{2,1,0:T(8,128)(2,1)S(1)}, u32[]{:S(2)}, u32[]{:S(2)}) collective-permute-start(bf16[2,128,1024]{2,1,0:T(8,128)(2,1)S(1)} %get-tuple-element.53), channel_id=1, source_target_pairs={{0,2},{2,0},{4,6},{6,4},{8,18},{10,16},{12,22},{14,20},{16,10},{18... | collective-permute-start | bytes 1572872 | tf_op jit(solution)/shard_map/ppermute | solution.py:60
  127.2 37.3 %collective-permute-start.13 = (bf16[2,128,1024]{2,1,0:T(8,128)(2,1)S(1)}, bf16[2,128,1024]{2,1,0:T(8,128)(2,1)S(1)}, u32[]{:S(2)}, u32[]{:S(2)}) collective-permute-start(bf16[2,128,1024]{2,1,0:T(8,128)(2,1)S(1)} %get-tuple-element.54), channel_id=1, source_target_pairs={{0,4},{2,6},{4,0},{6,2},{8,20},{10,22},{12,16},{14,18},{16,12},{18... | collective-permute-start | bytes 1572872 | tf_op jit(solution)/shard_map/ppermute | solution.py:60
  138.2 35.4 %collective-permute-start.14 = (bf16[2,128,1024]{2,1,0:T(8,128)(2,1)S(1)}, bf16[2,128,1024]{2,1,0:T(8,128)(2,1)S(1)}, u32[]{:S(2)}, u32[]{:S(2)}) collective-permute-start(bf16[2,128,1024]{2,1,0:T(8,128)(2,1)S(1)} %get-tuple-element.55), channel_id=1, source_target_pairs={{0,6},{2,4},{4,2},{6,0},{8,22},{10,20},{12,18},{14,16},{16,14},{18... | collective-permute-start | bytes 1572872 | tf_op jit(solution)/shard_map/ppermute | solution.py:60
  161.7 61.7 %copy-start.1 = (bf16[4096,512]{1,0:T(8,128)(2,1)S(1)}, bf16[4096,512]{1,0:T(8,128)(2,1)}, u32[]{:S(2)}) copy-start(bf16[4096,512]{1,0:T(8,128)(2,1)} %out_weight.1) | copy-start | bytes 12582916
  176.1 28.6 %collective-permute-start.18 = (bf16[16,4096]{1,0:T(8,128)(2,1)S(1)}, bf16[16,4096]{1,0:T(8,128)(2,1)S(1)}, u32[]{:S(2)}, u32[]{:S(2)}) collective-permute-start(bf16[16,4096]{1,0:T(8,128)(2,1)S(1)} %get-tuple-element.57.rest_0_), channel_id=1, source_target_pairs={{0,4},{2,6},{4,0},{6,2},{8,12},{10,14},{12,8},{14,10},{16,20},{18,... | collective-permute-start | bytes 393224 | tf_op jit(solution)/shard_map/ppermute | solution.py:60
  177.6 28.0 %collective-permute-start.17 = (bf16[16,4096]{1,0:T(8,128)(2,1)S(1)}, bf16[16,4096]{1,0:T(8,128)(2,1)S(1)}, u32[]{:S(2)}, u32[]{:S(2)}) collective-permute-start(bf16[16,4096]{1,0:T(8,128)(2,1)S(1)} %get-tuple-element.57.rest_0_), channel_id=1, source_target_pairs={{0,24},{2,26},{4,28},{6,30},{8,0},{10,2},{12,4},{14,6},{16,8},{18,... | collective-permute-start | bytes 393224 | tf_op jit(solution)/shard_map/ppermute | solution.py:60
  180.1 25.4 %collective-permute-start.22 = (bf16[16,4096]{1,0:T(8,128)(2,1)S(1)}, bf16[16,4096]{1,0:T(8,128)(2,1)S(1)}, u32[]{:S(2)}, u32[]{:S(2)}) collective-permute-start(bf16[16,4096]{1,0:T(8,128)(2,1)S(1)} %get-tuple-element.57.rest_0_), channel_id=1, source_target_pairs={{0,2},{2,0},{4,6},{6,4},{8,10},{10,8},{12,14},{14,12},{16,18},{18,... | collective-permute-start | bytes 393224 | tf_op jit(solution)/shard_map/ppermute | solution.py:60
  181.7 33.2 %collective-permute-start.16 = (bf16[16,4096]{1,0:T(8,128)(2,1)S(1)}, bf16[16,4096]{1,0:T(8,128)(2,1)S(1)}, u32[]{:S(2)}, u32[]{:S(2)}) collective-permute-start(bf16[16,4096]{1,0:T(8,128)(2,1)S(1)} %get-tuple-element.57.rest_0_), channel_id=1, source_target_pairs={{0,16},{2,18},{4,20},{6,22},{8,24},{10,26},{12,28},{14,30},{16,0},... | collective-permute-start | bytes 393224 | tf_op jit(solution)/shard_map/ppermute | solution.py:60
  203.8 12.4 %collective-permute-start.15 = (bf16[16,4096]{1,0:T(8,128)(2,1)S(1)}, bf16[16,4096]{1,0:T(8,128)(2,1)S(1)}, u32[]{:S(2)}, u32[]{:S(2)}) collective-permute-start(bf16[16,4096]{1,0:T(8,128)(2,1)S(1)} %get-tuple-element.57.rest_0_), channel_id=1, source_target_pairs={{0,8},{2,10},{4,12},{6,14},{8,16},{10,18},{12,20},{14,22},{16,24},... | collective-permute-start | bytes 393224 | tf_op jit(solution)/shard_map/ppermute | solution.py:60
  204.7 12.3 %collective-permute-start.26 = (bf16[16,4096]{1,0:T(8,128)(2,1)S(1)}, bf16[16,4096]{1,0:T(8,128)(2,1)S(1)}, u32[]{:S(2)}, u32[]{:S(2)}) collective-permute-start(bf16[16,4096]{1,0:T(8,128)(2,1)S(1)} %collective-permute-done.18.rest_4_), channel_id=1, source_target_pairs={{0,2},{2,0},{4,6},{6,4},{8,10},{10,8},{12,14},{14,12},{16,18},{18,... | collective-permute-start | bytes 393224 | tf_op jit(solution)/shard_map/ppermute | solution.py:60
  205.6 11.5 %collective-permute-start.25 = (bf16[16,4096]{1,0:T(8,128)(2,1)S(1)}, bf16[16,4096]{1,0:T(8,128)(2,1)S(1)}, u32[]{:S(2)}, u32[]{:S(2)}) collective-permute-start(bf16[16,4096]{1,0:T(8,128)(2,1)S(1)} %collective-permute-done.17.rest_3_), channel_id=1, source_target_pairs={{0,2},{2,0},{4,6},{6,4},{8,10},{10,8},{12,14},{14,12},{16,18},{18,... | collective-permute-start | bytes 393224 | tf_op jit(solution)/shard_map/ppermute | solution.py:60
  205.6 12.0 %collective-permute-start.21 = (bf16[16,4096]{1,0:T(8,128)(2,1)S(1)}, bf16[16,4096]{1,0:T(8,128)(2,1)S(1)}, u32[]{:S(2)}, u32[]{:S(2)}) collective-permute-start(bf16[16,4096]{1,0:T(8,128)(2,1)S(1)} %collective-permute-done.17.rest_3_), channel_id=1, source_target_pairs={{0,4},{2,6},{4,0},{6,2},{8,12},{10,14},{12,8},{14,10},{16,20},{18,... | collective-permute-start | bytes 393224 | tf_op jit(solution)/shard_map/ppermute | solution.py:60
  215.0 5.7 %collective-permute-start.20 = (bf16[16,4096]{1,0:T(8,128)(2,1)S(1)}, bf16[16,4096]{1,0:T(8,128)(2,1)S(1)}, u32[]{:S(2)}, u32[]{:S(2)}) collective-permute-start(bf16[16,4096]{1,0:T(8,128)(2,1)S(1)} %collective-permute-done.16.rest_2_), channel_id=1, source_target_pairs={{0,4},{2,6},{4,0},{6,2},{8,12},{10,14},{12,8},{14,10},{16,20},{18,... | collective-permute-start | bytes 393224 | tf_op jit(solution)/shard_map/ppermute | solution.py:60
  216.2 5.8 %collective-permute-start.19 = (bf16[16,4096]{1,0:T(8,128)(2,1)S(1)}, bf16[16,4096]{1,0:T(8,128)(2,1)S(1)}, u32[]{:S(2)}, u32[]{:S(2)}) collective-permute-start(bf16[16,4096]{1,0:T(8,128)(2,1)S(1)} %collective-permute-done.15.rest_1_), channel_id=1, source_target_pairs={{0,4},{2,6},{4,0},{6,2},{8,12},{10,14},{12,8},{14,10},{16,20},{18,... | collective-permute-start | bytes 393224 | tf_op jit(solution)/shard_map/ppermute | solution.py:60
  217.0 5.0 %collective-permute-start.24 = (bf16[16,4096]{1,0:T(8,128)(2,1)S(1)}, bf16[16,4096]{1,0:T(8,128)(2,1)S(1)}, u32[]{:S(2)}, u32[]{:S(2)}) collective-permute-start(bf16[16,4096]{1,0:T(8,128)(2,1)S(1)} %collective-permute-done.16.rest_2_), channel_id=1, source_target_pairs={{0,2},{2,0},{4,6},{6,4},{8,10},{10,8},{12,14},{14,12},{16,18},{18,... | collective-permute-start | bytes 393224 | tf_op jit(solution)/shard_map/ppermute | solution.py:60
  217.0 5.0 %collective-permute-start.23 = (bf16[16,4096]{1,0:T(8,128)(2,1)S(1)}, bf16[16,4096]{1,0:T(8,128)(2,1)S(1)}, u32[]{:S(2)}, u32[]{:S(2)}) collective-permute-start(bf16[16,4096]{1,0:T(8,128)(2,1)S(1)} %collective-permute-done.15.rest_1_), channel_id=1, source_target_pairs={{0,2},{2,0},{4,6},{6,4},{8,10},{10,8},{12,14},{14,12},{16,18},{18,... | collective-permute-start | bytes 393224 | tf_op jit(solution)/shard_map/ppermute | solution.py:60
  217.5 4.5 %collective-permute-start.29 = (bf16[16,4096]{1,0:T(8,128)(2,1)S(1)}, bf16[16,4096]{1,0:T(8,128)(2,1)S(1)}, u32[]{:S(2)}, u32[]{:S(2)}) collective-permute-start(bf16[16,4096]{1,0:T(8,128)(2,1)S(1)} %collective-permute-done.21.rest_7_), channel_id=1, source_target_pairs={{0,2},{2,0},{4,6},{6,4},{8,10},{10,8},{12,14},{14,12},{16,18},{18,... | collective-permute-start | bytes 393224 | tf_op jit(solution)/shard_map/ppermute | solution.py:60
  220.6 1.4 collective-permute-start.28
  222.0 1.3 collective-permute-start.27
  227.7 5.6 %collective-permute-start.30 = (bf16[128,512]{1,0:T(8,128)(2,1)S(1)}, bf16[128,512]{1,0:T(8,128)(2,1)S(1)}, u32[]{:S(2)}, u32[]{:S(2)}) collective-permute-start(bf16[128,512]{1,0:T(8,128)(2,1)S(1)} %get-tuple-element.59), channel_id=1, source_target_pairs={{0,1},{1,0},{2,3},{3,2},{4,5},{5,4},{6,7},{7,6},{8,9},{9,8},{10,11... | collective-permute-start | bytes 393224 | tf_op jit(solution)/shard_map/ppermute | solution.py:372

commit v8 on v7

v8 whole, which is shorter than its diff:
```python
import functools
import math

import jax
import jax.numpy as jnp
from jax import lax
from jax.experimental import pallas as pl
from jax.experimental.pallas import tpu as pltpu
from jax.sharding import PartitionSpec as P

HD = 128
MAX_PAGES = 2
ROW_UNROLL = 4
EARLY = 4
VMEM_LIMIT = 57 * 1024 * 1024


def factors(groups):
    near = math.gcd(groups, 4)
    return groups // near, near


def uniform(step, swap, dims):
    return tuple(((z + step) % dims[0], swap) for z in range(dims[0]))


def page_rounds(dims):
    far, near = dims
    steps = sorted(range(1, far), key=lambda z: (min(z, far - z), z))
    order = [(z, n) for z in steps for n in range(near)]
    for n in range(1, near):
        order.insert(min(2 * n, len(order)), (0, n))
    return [uniform(z, n, dims) for z, n in order]


def reverse(route):
    sources = {to: (z, swap) for z, (to, swap) in enumerate(route)}
    return tuple(sources[z] for z in range(len(route)))


def routed(me, route, dims):
    near = dims[1]
    z = me // near
    to, swap = jnp.int32(route[0][0]), jnp.int32(route[0][1])
    for place in range(1, dims[0]):
        to = jnp.where(z == place, route[place][0], to)
        swap = jnp.where(z == place, route[place][1], swap)
    return to * near + (me % near ^ swap)


def send_by(array, route, dims):
    far, near = dims
    pairs = [
        (z * near + n, route[z][0] * near + (n ^ route[z][1])) for z in range(far) for n in range(near)
    ]
    return lax.ppermute(array, "group", pairs)


def gather_stages(dims):
    far, near = dims
    swaps = [1 << i for i in reversed(range(near.bit_length() - 1))]
    return [[(z, 0) for z in range(1, far)]] + [[(0, n)] for n in swaps]


def gather_shards(shard, dims):
    held = {(0, 0): shard}
    for stage in gather_stages(dims):
        incoming = {}
        for step in stage:
            for offset, array in held.items():
                moved = send_by(array, uniform(*step, dims), dims)
                incoming[offset[0] + step[0], offset[1] | step[1]] = moved
        held.update(incoming)
    return {offset: (array, 0) for offset, array in held.items()}


def gather_stacked(shard, dims):
    rows = shard.shape[0]
    held, whole = {(0, 0): (shard, 0)}, shard
    for stage in gather_stages(dims):
        arrays, offsets = [whole], list(held)
        before = dict(held)
        for step in stage:
            moved = send_by(whole, uniform(*step, dims), dims)
            arrays.append(moved)
            for offset, (_, row) in before.items():
                held[offset[0] + step[0], offset[1] | step[1]] = (moved, row)
        yield arrays[1:], held
        whole = jnp.concatenate(arrays, axis=0)
        held = {}
        for i, step in enumerate([(0, 0)] + stage):
            for offset, (_, row) in before.items():
                held[offset[0] + step[0], offset[1] | step[1]] = (whole, i * len(offsets) * rows + row)


def packed(lengths, prefill_of, decode_of, groups):
    bits = (groups - 1).bit_length()
    return (lengths << 2 * bits) | (prefill_of << bits) | decode_of


def unpacked(entry, groups):
    bits = (groups - 1).bit_length()
    mask = (1 << bits) - 1
    return entry >> 2 * bits, (entry >> bits) & mask, entry & mask


def prepare_kernel(dims, sendings, columns, own, table_hbm, pool, *rest):
    table, held, zero_page, start_of, count_of, table_sem, in_sems, out_sem = rest[-8:]
    received, *sends = rest[-9 - len(sendings) : -8]
    me = lax.axis_index("group")
    groups = lax.axis_size("group")
    page_size = pool.shape[1]
    copy = pltpu.make_async_copy(table_hbm, table, table_sem)
    copy.start()
    for d in range(groups + 1):
        start_of[d] = 0
        count_of[d] = 0
    zero_page[...] = jnp.zeros_like(zero_page)
    copy.wait()

    def visit(r, running):
        length, home, destination = unpacked(table[r], groups)
        mine = home == me
        count = (length + page_size - 1) // page_size
        to = jnp.where(mine, destination, groups)
        start_of[to] = running
        count_of[to] = count
        return running + jnp.where(mine, count, 0)

    lax.fori_loop(0, table.shape[0], visit, jnp.int32(0), unroll=8)
    targets = [
        (routed(me, route, dims), send, 0, columns[part]) for (route, part), send in zip(sendings, sends)
    ]
    if own:
        targets.append((me, received, me * MAX_PAGES, (0, pool.shape[2])))

    def each(do):
        for i, (to, target, base, (first, width)) in enumerate(targets):
            for page in range(MAX_PAGES):
                there = page < count_of[to]
                lanes = pl.ds(first, width)
                source = pool.at[jnp.where(there, start_of[to] + page, 0), :, lanes]
                buffer, place = held.at[i, page, :, pl.ds(0, width)], target.at[base + page]
                blank = zero_page.at[:, pl.ds(0, width)]
                do(there, (source, buffer, in_sems.at[i, page]), (buffer, place, out_sem), (blank, place, out_sem))

    def fetch(there, load, store, blank):
        @pl.when(there)
        def _():
            pltpu.make_async_copy(*load).start()

        @pl.when(jnp.logical_not(there))
        def _():
            pltpu.make_async_copy(*blank).start()

    def forward(there, load, store, blank):
        @pl.when(there)
        def _():
            pltpu.make_async_copy(*load).wait()
            pltpu.make_async_copy(*store).start()

    def finish(there, load, store, blank):
        pltpu.make_async_copy(*blank).wait()

    each(fetch)
    each(forward)
    each(finish)


def prepare(dims, sendings, columns, table, pool, received=None, after=()):
    own = received is None
    groups = math.prod(dims)
    page_size, width = pool.shape[1:]
    count = len(sendings) + (1 if own else 0)
    widest = width if own else max(w for _, w in columns)
    hbm = pl.BlockSpec(memory_space=pl.ANY)
    outs = [jax.ShapeDtypeStruct((groups * MAX_PAGES, page_size, width), pool.dtype)]
    outs += [jax.ShapeDtypeStruct((MAX_PAGES, page_size, columns[part][1]), pool.dtype) for _, part in sendings]
    operands = [table, pool] + ([] if own else [received]) + list(after)
    return pl.pallas_call(
        functools.partial(prepare_kernel, dims, sendings, columns, own),
        out_shape=outs,
        in_specs=[hbm] * len(operands),
        out_specs=[hbm] * len(outs),
        scratch_shapes=[
            pltpu.SMEM(table.shape, jnp.int32),
            pltpu.VMEM((count, MAX_PAGES, page_size, widest), pool.dtype),
            pltpu.VMEM((page_size, widest), pool.dtype),
            pltpu.SMEM((groups + 1,), jnp.int32),
            pltpu.SMEM((groups + 1,), jnp.int32),
            pltpu.SemaphoreType.DMA,
            pltpu.SemaphoreType.DMA((count, MAX_PAGES)),
            pltpu.SemaphoreType.DMA,
        ],
        input_output_aliases={} if own else {2: 0},
        compiler_params=pltpu.CompilerParams(vmem_limit_bytes=VMEM_LIMIT),
        cost_estimate=pl.CostEstimate(
            flops=0, bytes_accessed=4 * sum(math.prod(o.shape) for o in outs[1:]), transcendentals=0
        ),
        name="outgoing_pages",
    )(*operands)


def attend_row(query, pages, length):
    first, second = pages
    kv_heads = first.shape[1] // (2 * HD)
    share = query.shape[0] // kv_heads
    scores = []
    for h in range(kv_heads):
        columns = slice(2 * h * HD, (2 * h + 1) * HD)
        keys = jnp.concatenate([first[:, columns], second[:, columns]], axis=0)
        every = lax.dot_general(
            query, keys, (((1,), (1,)), ((), ())), preferred_element_type=jnp.float32
        )
        scores.append(every[h * share : (h + 1) * share])
    score = jnp.concatenate(scores, axis=0) * (1.0 / math.sqrt(HD))
    live = lax.broadcasted_iota(jnp.int32, score.shape, 1) < length
    masked = jnp.where(live, score, -1e30)
    highest = jnp.max(masked, axis=1, keepdims=True)
    weights = jnp.where(live, jnp.exp(masked - highest), 0.0)
    totals = jnp.sum(weights, axis=1, keepdims=True)
    rounded = weights.astype(jnp.bfloat16)
    mixtures = []
    for h in range(kv_heads):
        columns = slice((2 * h + 1) * HD, (2 * h + 2) * HD)
        values = jnp.concatenate([first[:, columns], second[:, columns]], axis=0)
        every = jnp.dot(rounded, values, preferred_element_type=jnp.float32)
        mixtures.append(every[h * share : (h + 1) * share])
    return jnp.concatenate(mixtures, axis=0) / totals


def settle_kernel(dims, routes, lanes, heads_here, own, last, table, row_request, queries, rows_in, received_in, *rest):
    blocks = rest[: len(routes)]
    received, out, rows, held, list_row, list_block, list_length, in_sems, out_sems = rest[-9:]
    me = lax.axis_index("group")
    row_local = queries.shape[0]
    first_head, head_count = heads_here
    mine = pl.ds(me * MAX_PAGES, MAX_PAGES)
    lanes = pl.ds(*lanes)
    origins = [routed(me, reverse(route), dims) for route in routes]
    places = [pl.ds(origin * MAX_PAGES, MAX_PAGES) for origin in origins]
    sources = list(blocks) + ([received_in.at[mine, :, lanes]] if own else [])
    origins += [me] if own else []
    loads = [pltpu.make_async_copy(s, held.at[i], in_sems.at[i]) for i, s in enumerate(sources)]
    stores = [
        pltpu.make_async_copy(held.at[i], received.at[place, :, lanes], out_sems.at[i])
        for i, place in enumerate(places)
    ]
    for load in loads:
        load.start()

    found = jnp.int32(0)
    for b in range(row_local):
        length, home, _ = unpacked(table[row_request[me * row_local + b]], math.prod(dims))
        block, match = jnp.int32(0), jnp.int32(0)
        for i, origin in enumerate(origins):
            block = jnp.where(home == origin, i, block)
            match = jnp.where(home == origin, 1, match)
        list_row[found] = b
        list_block[found] = block
        list_length[found] = length
        found = found + match
    for i in range(ROW_UNROLL):
        list_row[found + i] = row_local
        list_block[found + i] = 0
        list_length[found + i] = 1
    rows[:row_local] = rows_in[...]
    for load in loads:
        load.wait()
    for store in stores:
        store.start()

    @pl.loop(0, (found + ROW_UNROLL - 1) // ROW_UNROLL)
    def _(step):
        results = []
        for i in range(ROW_UNROLL):
            at = step * ROW_UNROLL + i
            query = queries[jnp.minimum(list_row[at], row_local - 1), first_head : first_head + head_count]
            pages = [held[list_block[at], page] for page in range(MAX_PAGES)]
            results.append(attend_row(query, pages, list_length[at]))
        for i, result in enumerate(results):
            rows[list_row[step * ROW_UNROLL + i]] = result

    if last:
        for h in range(head_count):
            out[:, h * HD : (h + 1) * HD] = rows[:row_local, h, :].astype(out.dtype)
    else:
        out[...] = rows[:row_local]
    for store in stores:
        store.wait()


def settle(dims, routes, lanes, heads_here, own, last, table, row_request, queries, rows, received, blocks, after):
    row_local = queries.shape[0]
    smem = pl.BlockSpec(memory_space=pltpu.SMEM)
    vmem = pl.BlockSpec(memory_space=pltpu.VMEM)
    hbm = pl.BlockSpec(memory_space=pl.ANY)
    count = len(blocks) + (1 if own else 0)
    if last:
        out = jax.ShapeDtypeStruct((row_local, heads_here[1] * HD), jnp.bfloat16)
    else:
        out = jax.ShapeDtypeStruct(rows.shape, rows.dtype)
    return pl.pallas_call(
        functools.partial(settle_kernel, dims, routes, lanes, heads_here, own, last),
        out_shape=[jax.ShapeDtypeStruct(received.shape, received.dtype), out],
        in_specs=[smem, smem, vmem, vmem, hbm] + [hbm] * (len(blocks) + len(after)),
        out_specs=[hbm, vmem],
        scratch_shapes=[
            pltpu.VMEM((row_local + 1,) + rows.shape[1:], jnp.float32),
            pltpu.VMEM((count, MAX_PAGES, received.shape[1], lanes[1]), received.dtype),
            pltpu.SMEM((row_local + ROW_UNROLL,), jnp.int32),
            pltpu.SMEM((row_local + ROW_UNROLL,), jnp.int32),
            pltpu.SMEM((row_local + ROW_UNROLL,), jnp.int32),
            pltpu.SemaphoreType.DMA((count,)),
            pltpu.SemaphoreType.DMA((count,)),
        ],
        input_output_aliases={4: 0},
        compiler_params=pltpu.CompilerParams(vmem_limit_bytes=VMEM_LIMIT),
        cost_estimate=pl.CostEstimate(
            flops=1 << 30, bytes_accessed=4 * sum(b.size for b in blocks), transcendentals=1 << 18
        ),
        name="settle_pages",
    )(table, row_request, queries, rows, received, *blocks, *after)


def project_kernel(dims, pieces, arrays, row_local, aheads, inputs, added, out_weight, *rest):
    stacks = rest[:arrays]
    partials = rest[arrays : arrays + added]
    outs = rest[arrays + added : -2]
    attended, sems = rest[-2:]
    me = lax.axis_index("group")
    heads = lax.axis_size("head")
    my_head = lax.axis_index("head")
    share = outs[0].shape[0]

    def each(do):
        for i, (offset, stack, first) in enumerate(pieces):
            row = routed(me, reverse(uniform(*offset, dims)), dims) * row_local
            ahead = lax.rem(row // share - my_head + heads, heads)
            for at, wanted in enumerate(aheads):

                @pl.when(ahead == wanted)
                def _():
                    place = attended.at[pl.ds(pl.multiple_of(at * share + lax.rem(row, share), row_local), row_local)]
                    do(pltpu.make_async_copy(stacks[stack].at[pl.ds(first, row_local)], place, sems.at[i]))

    each(lambda copy: copy.start())
    each(lambda copy: copy.wait())
    product = jnp.dot(attended[...], out_weight[pl.ds(*inputs)], preferred_element_type=jnp.float32)
    for at, (ahead, out) in enumerate(zip(aheads, outs)):
        block = product[at * share : (at + 1) * share]
        if added:
            block = block + partials[ahead][...]
        out[...] = block.astype(out.dtype)


def project(dims, gathered, row_local, out_weight, inputs, heads, aheads, dtype, added=()):
    stacks = list({id(array): array for array, _ in gathered.values()}.values())
    places = {id(array): i for i, array in enumerate(stacks)}
    pieces = [(offset, places[id(array)], first) for offset, (array, first) in gathered.items()]
    width, columns = stacks[0].shape[1], out_weight.shape[1]
    share = row_local * len(pieces) // heads
    vmem = pl.BlockSpec(memory_space=pltpu.VMEM)
    hbm = pl.BlockSpec(memory_space=pl.ANY)
    return pl.pallas_call(
        functools.partial(project_kernel, dims, pieces, len(stacks), row_local, aheads, inputs, len(added)),
        out_shape=[jax.ShapeDtypeStruct((share, columns), dtype)] * len(aheads),
        in_specs=[vmem] + [hbm] * len(stacks) + [vmem] * len(added),
        out_specs=[vmem] * len(aheads),
        scratch_shapes=[
            pltpu.VMEM((len(aheads) * share, width), jnp.bfloat16),
            pltpu.SemaphoreType.DMA((len(pieces),)),
        ],
        compiler_params=pltpu.CompilerParams(vmem_limit_bytes=VMEM_LIMIT),
        cost_estimate=pl.CostEstimate(
            flops=2 * len(aheads) * share * width * columns, bytes_accessed=2 * width * columns, transcendentals=0
        ),
        name="project_rows",
    )(out_weight, *stacks, *added)


def local(kv_pool, lengths, prefill_of, decode_of, row_request, queries, out_weight):
    row_local, query_width = queries.shape
    query_heads = query_width // HD
    queries = queries.reshape(row_local, query_heads, HD)
    kv_heads = kv_pool.shape[2] // (2 * HD)
    share = query_heads // kv_heads
    dims = factors(lax.axis_size("group"))
    heads = lax.axis_size("head")

    cut = kv_heads // 2
    parts = [(first, last - first) for first, last in ((0, cut), (cut, kv_heads)) if last > first]
    columns = [(first * 2 * HD, count * 2 * HD) for first, count in parts]

    routes = page_rounds(dims)
    total = len(routes)
    table = packed(lengths, prefill_of, decode_of, math.prod(dims))
    received, arrived = None, {}

    def send(*several, after=()):
        nonlocal received
        chosen = [(part, i) for part, first, last in several for i in range(first, last)]
        sendings = [(routes[i], part) for part, i in chosen]
        received, *blocks = prepare(dims, sendings, columns, table, kv_pool, received, after)
        for (part, i), block in zip(chosen, blocks):
            arrived[part, i] = send_by(block, routes[i], dims)

    def take(part, first, last, rows, after=()):
        nonlocal received
        head_first, head_count = parts[part][0] * share, parts[part][1] * share
        if rows is None:
            rows = jnp.zeros((row_local, head_count, HD), jnp.float32)
        blocks = [arrived[part, i] for i in range(first, last)]
        received, rows = settle(
            dims, routes[first:last], columns[part], (head_first, head_count), first == 0, last == total,
            table, row_request, queries, rows, received, blocks, list(after),
        )
        return rows

    weight = pltpu.with_memory_space_constraint(out_weight, pltpu.VMEM)
    inputs = [(first * share * HD, count * share * HD) for first, count in parts]
    fifth = total // 5
    send((0, 0, EARLY))
    if len(parts) == 1:
        send((0, EARLY, total))
        rows = take(0, 0, 2 * fifth, None)
        rows = take(0, 2 * fifth, 4 * fifth, rows)
        rows = take(0, 4 * fifth, total, rows)
        done = []
    else:
        send((0, EARLY, total), (1, 0, fifth))
        rows = take(0, 0, 2 * fifth, None)
        rows = take(0, 2 * fifth, 4 * fifth, rows)
        send((1, fifth, 5 * fifth // 2 + 1))
        rows = take(0, 4 * fifth, total, rows)
        stages = gather_stacked(rows, dims)
        landed, _ = next(stages)
        send((1, 5 * fifth // 2 + 1, 7 * fifth // 2 + 1), after=landed)
        landed, _ = next(stages)
        rows = take(1, 0, fifth, None)
        send((1, 7 * fifth // 2 + 1, total), after=landed)
        for landed, gathered in stages:
            pass
        rows = take(1, fifth, 2 * fifth, rows)
        rows = take(1, 2 * fifth, 4 * fifth, rows, after=landed)
        done = project(dims, gathered, row_local, weight, inputs[0], heads, range(heads), jnp.float32)
        rows = take(1, 4 * fifth, total, rows, after=done)
    gathered = gather_shards(rows, dims)

    theirs = project(dims, gathered, row_local, weight, inputs[-1], heads, range(1, heads), jnp.bfloat16, done)
    (own,) = project(dims, gathered, row_local, weight, inputs[-1], heads, range(1), jnp.float32, done)
    for ahead, part in enumerate(theirs, 1):
        pairs = [(h, (h + ahead) % heads) for h in range(heads)]
        own = own + lax.ppermute(part, "head", pairs).astype(jnp.float32)
    return (received, own.astype(jnp.bfloat16))


def solution(mesh):
    in_specs = (
        P("group", None, "head"),
        P(),
        P(),
        P(),
        P(),
        P("group", "head"),
        P("head", "group"),
    )
    out_specs = (P("group", None, "head"), P("head", "group"))
    return jax.shard_map(local, mesh=mesh, in_specs=in_specs, out_specs=out_specs, check_vma=False)
```

time: 235 us -> 256 us (1.089)
  Pallas kernels: 25.9 us -> 69.8 us
  waiting for transfers between devices: 142 us -> 107 us
  starting transfers between devices: 60.5 us -> 68.5 us
    pallas_call x8 -> x15, Pallas kernels: 25.9 us -> 69.8 us  [the longest x7 33.8 us: settle(): pl.pallas_call(functools.partial(settle_kernel, dims, routes, lanes, head...]
    ppermute x30 -> x50, waiting for transfers between devices: 138 us -> 106 us  [send_by(): return lax.ppermute(array, 'group', pairs)]
    ppermute x30 -> x50, starting transfers between devices: 58.9 us -> 66.9 us  [send_by(): return lax.ppermute(array, 'group', pairs)]
    ppermute x1, waiting for transfers between devices: 4.05 us -> 0.86 us  [local(): own = own + lax.ppermute(part, 'head', pairs).astype(jnp.float32)]
  transfers between devices with their start and end apart: 31 -> 51, of which waited for: 20 -> 20; matrix products, arithmetic and copies ran while one was open for 0% -> 1% of each run, Pallas kernels for 6% -> 22%
where the time goes in v8:
time: 256 us
  waiting for transfers between devices  107 us (42%)
  Pallas kernels  69.8 us (27%)
  starting transfers between devices  68.5 us (27%)
  local copies, waits for them, and re-layouts  5.12 us (2%)
  other arithmetic  3.8 us (1%)
    ppermute x50, waiting for transfers between devices, send_by(): return lax.ppermute(array, 'group', pairs)  106 us
    ppermute x50, starting transfers between devices, send_by(): return lax.ppermute(array, 'group', pairs)  66.9 us
    pallas_call x7, Pallas kernels, settle(): pl.pallas_call(functools.partial(settle_kernel, dims, routes, lanes, head...  33.8 us
    pallas_call x5, Pallas kernels, prepare(): pl.pallas_call(functools.partial(prepare_kernel, dims, sendings, columns,...  26.4 us
    pallas_call x3, Pallas kernels, project(): pl.pallas_call(functools.partial(project_kernel, dims, pieces, len(stacks...  9.65 us
  transfers between devices with their start and end apart: 51, of which 20 were waited for; matrix products, arithmetic and copies ran while one was open for 1% of the time, Pallas kernels for 22%

profile of v8, /device:TPU:0, one launch (start us, length us, event | category | flops | bytes accessed | tf_op | source)
XLA Modules:
  0.0 255.6 jit_solution(1093696465949413055)
XLA Ops:
  0.6 1.3 or_or_fusion.table_hbm.table
  1.9 5.2 %outgoing_pages.5 = (bf16[32,128,1024]{2,1,0:T(8,128)(2,1)}, bf16[2,128,512]{2,1,0:T(8,128)(2,1)}, bf16[2,128,512]{2,1,0:T(8,128)(2,1)}, bf16[2,128,512]{2,1,0:T(8,128)(2,1)}, bf16[2,128,512]{2,1,0:T(8,128)(2,1)}) custom-call(s32[256]{0:T(256)} %or_or_fusion.table_hbm.table, bf16[32,128,1024]{2,1,0:T(8,128)(2,1)} %pool.9), custom_call_target="tpu_custom_call" | custom-call | bytes 2097152 | tf_op jit(solution)/shard_map/outgoing_pages/pallas_call | solution.py:180
  7.1 3.1 %collective-permute-start = (bf16[2,128,512]{2,1,0:T(8,128)(2,1)}, bf16[2,128,512]{2,1,0:T(8,128)(2,1)S(1)}, u32[]{:S(2)}, u32[]{:S(2)}) collective-permute-start(bf16[2,128,512]{2,1,0:T(8,128)(2,1)} %get-tuple-element.55), channel_id=1, source_target_pairs={{0,8},{2,10},{4,12},{6,14},{8,16},{10,18},{12,20},{14,22},{16,24},... | collective-permute-start | bytes 786440 | tf_op jit(solution)/shard_map/ppermute | solution.py:56
  11.9 2.5 collective-permute-start.3
  14.4 6.2 %outgoing_pages.6 = (bf16[32,128,1024]{2,1,0:T(8,128)(2,1)}, bf16[2,128,512]{2,1,0:T(8,128)(2,1)}, bf16[2,128,512]{2,1,0:T(8,128)(2,1)}, bf16[2,128,512]{2,1,0:T...) custom-call(s32[256]{0:T(256)} %or_or_fusion.table_hbm.table, ...), custom_call_target="tpu_custom_call", output_to_operand_aliasing={{0}: (2, {})} | custom-call | bytes 7340032 | tf_op jit(solution)/shard_map/outgoing_pages/pallas_call | solution.py:180
  21.6 1.9 collective-permute-done.1.rest_1_
  23.5 3.1 %collective-permute-start.6 = (bf16[2,128,512]{2,1,0:T(8,128)(2,1)}, bf16[2,128,512]{2,1,0:T(8,128)(2,1)S(1)}, u32[]{:S(2)}, u32[]{:S(2)}) collective-permute-start(bf16[2,128,512]{2,1,0:T(8,128)(2,1)} %get-tuple-element.63), channel_id=1, source_target_pairs={{0,6},{2,4},{4,2},{6,0},{8,14},{10,12},{12,10},{14,8},{16,22},{18,... | collective-permute-start | bytes 786440 | tf_op jit(solution)/shard_map/ppermute | solution.py:56
  26.7 1.8 collective-permute-start.7
  28.5 3.7 %collective-permute-done.3.rest_3_ = bf16[2,128,512]{2,1,0:T(8,128)(2,1)S(1)} collective-permute-done((bf16[2,128,512]{2,1,0:T(8,128)(2,1)}, bf16[2,128,512]{2,1,0:T(8,128)(2,1)S(1)}, u32[]{:S(2)}, u32[]{:S(2)}) %collective-permute-start.3) | collective-permute-done | bytes 262176 | tf_op jit(solution)/shard_map/ppermute | solution.py:56
  32.2 9.0 %collective-permute-done.4.rest_4_ = bf16[2,128,512]{2,1,0:T(8,128)(2,1)S(1)} collective-permute-done((bf16[2,128,512]{2,1,0:T(8,128)(2,1)}, bf16[2,128,512]{2,1,0:T(8,128)(2,1)S(1)}, u32[]{:S(2)}, u32[]{:S(2)}) %collective-permute-start.4) | collective-permute-done | bytes 262176 | tf_op jit(solution)/shard_map/ppermute | solution.py:56
  41.3 1.7 collective-permute-start.9
  43.0 14.5 %collective-permute-start.10 = (bf16[2,128,512]{2,1,0:T(8,128)(2,1)}, bf16[2,128,512]{2,1,0:T(8,128)(2,1)S(1)}, u32[]{:S(2)}, u32[]{:S(2)}) collective-permute-start(bf16[2,128,512]{2,1,0:T(8,128)(2,1)} %get-tuple-element.67), channel_id=1, source_target_pairs={{0,30},{2,28},{4,26},{6,24},{8,6},{10,4},{12,2},{14,0},{16,14},{18... | collective-permute-start | bytes 786440 | tf_op jit(solution)/shard_map/ppermute | solution.py:56
  57.6 3.9 %collective-permute-start.13 = (bf16[2,128,512]{2,1,0:T(8,128)(2,1)}, bf16[2,128,512]{2,1,0:T(8,128)(2,1)S(1)}, u32[]{:S(2)}, u32[]{:S(2)}) collective-permute-start(bf16[2,128,512]{2,1,0:T(8,128)(2,1)} %get-tuple-element.73), channel_id=1, source_target_pairs={{0,20},{2,22},{4,16},{6,18},{8,28},{10,30},{12,24},{14,26},{16,4},... | collective-permute-start | bytes 786440 | tf_op jit(solution)/shard_map/ppermute | solution.py:56
  61.5 2.2 collective-permute-start.14
  65.1 5.4 %settle_pages.7 = (bf16[32,128,1024]{2,1,0:T(8,128)(2,1)}, f32[16,16,128]{2,1,0:T(8,128)}) custom-call(s32[256]{0:T(256)} %or_or_fusion.table_hbm.table, s32[256]{0:T(256)} %row_request.13, bf16[16,32,128]{2,1,0:T(8,128)(2,1)} %bitcast.2, f32[16,16,128]{2,1,0:T(8,128)} %broadcast_1_rows_in.2.rows_in, ...), custom_call_target="tpu_custom_call", output_to_operand_aliasing={{0}: (4, {})} | custom-call | flops 1073741824 | bytes 3145728 | tf_op jit(solution)/shard_map/settle_pages/pallas_call | solution.py:303
  70.5 25.4 %collective-permute-done.11.rest_5_ = bf16[2,128,512]{2,1,0:T(8,128)(2,1)S(1)} collective-permute-done((bf16[2,128,512]{2,1,0:T(8,128)(2,1)}, bf16[2,128,512]{2,1,0:T(8,128)(2,1)S(1)}, u32[]{:S(2)}, u32[]{:S(2)}) %collective-permute-start.11) | collective-permute-done | bytes 262176 | tf_op jit(solution)/shard_map/ppermute | solution.py:56
  96.6 5.2 %settle_pages.8 = (bf16[32,128,1024]{2,1,0:T(8,128)(2,1)}, f32[16,16,128]{2,1,0:T(8,128)}) custom-call(s32[256]{0:T(256)} %or_or_fusion.table_hbm.table, s32[256]{0:T(256)} %row_request.13, bf16[16,32,128]{2,1,0:T(8,128)(2,1)} %bitcast.3, f32[16,16,128]{2,1,0:T(8,128)} %get-tuple-element.61.rows_in, ...), custom_call_target="tpu_custom_call", output_to_operand_aliasing={{0}: (4, {})} | custom-call | flops 1073741824 | bytes 3145728 | tf_op jit(solution)/shard_map/settle_pages/pallas_call | solution.py:303
  101.9 5.1 %outgoing_pages.7 = (bf16[32,128,1024]{2,1,0:T(8,128)(2,1)}, bf16[2,128,512]{2,1,0:T(8,128)(2,1)}, bf16[2,128,512]{2,1,0:T(8,128)(2,1)}, bf16[2,128,512]{2,1,0:T...) custom-call(s32[256]{0:T(256)} %or_or_fusion.table_hbm.table, ...), custom_call_target="tpu_custom_call", output_to_operand_aliasing={{0}: (2, {})} | custom-call | bytes 2621440 | tf_op jit(solution)/shard_map/outgoing_pages/pallas_call | solution.py:180
  107.1 6.6 %collective-permute-done.13.rest_1_ = bf16[2,128,512]{2,1,0:T(8,128)(2,1)S(1)} collective-permute-done((bf16[2,128,512]{2,1,0:T(8,128)(2,1)}, bf16[2,128,512]{2,1,0:T(8,128)(2,1)S(1)}, u32[]{:S(2)}, u32[]{:S(2)}) %collective-permute-start.13) | collective-permute-done | bytes 262176 | tf_op jit(solution)/shard_map/ppermute | solution.py:56
  115.0 5.0 %settle_pages.9 = (bf16[32,128,1024]{2,1,0:T(8,128)(2,1)}, bf16[16,2048]{1,0:T(8,128)(2,1)}) custom-call(s32[256]{0:T(256)} %or_or_fusion.table_hbm.table, s32[256]{0:T(256)} %row_request.13, bf16[16,32,128]{2,1,0:T(8,128)(2,1)} %bitcast.4, f32[16,16,128]{2,1,0:T(8,128)} %get-tuple-element.69.rows_in, ...), custom_call_target="tpu_custom_call", output_to_operand_aliasing={{0}: (4, {})} | custom-call | flops 1073741824 | bytes 1572864 | tf_op jit(solution)/shard_map/settle_pages/pallas_call | solution.py:303
  121.3 1.9 collective-permute-start.15
  124.6 1.5 collective-permute-start.20
  126.2 2.8 %collective-permute-start.22 = (bf16[2,128,512]{2,1,0:T(8,128)(2,1)S(1)}, bf16[2,128,512]{2,1,0:T(8,128)(2,1)S(1)}, u32[]{:S(2)}, u32[]{:S(2)}) collective-permute-start(bf16[2,128,512]{2,1,0:T(8,128)(2,1)S(1)} %copy-done.58), channel_id=1, source_target_pairs={{0,12},{2,14},{4,8},{6,10},{8,20},{10,22},{12,16},{14,18},{16,28},... | collective-permute-start | bytes 786440 | tf_op jit(solution)/shard_map/ppermute | solution.py:56
  129.9 1.5 collective-permute-start.21
  132.1 11.6 %collective-permute-done.21.rest_1_ = bf16[64,2048]{1,0:T(8,128)(2,1)S(1)} collective-permute-done((bf16[64,2048]{1,0:T(8,128)(2,1)S(1)}, bf16[64,2048]{1,0:T(8,128)(2,1)S(1)}, u32[]{:S(2)}, u32[]{:S(2)}) %collective-permute-start.21) | collective-permute-done | bytes 262176 | tf_op jit(solution)/shard_map/ppermute | solution.py:56
  145.1 3.9 %collective-permute-start.26 = (bf16[2,128,512]{2,1,0:T(8,128)(2,1)S(1)}, bf16[2,128,512]{2,1,0:T(8,128)(2,1)S(1)}, u32[]{:S(2)}, u32[]{:S(2)}) collective-permute-start(bf16[2,128,512]{2,1,0:T(8,128)(2,1)S(1)} %copy-done.55), channel_id=1, source_target_pairs={{0,24},{2,26},{4,28},{6,30},{8,0},{10,2},{12,4},{14,6},{16,8},{18,... | collective-permute-start | bytes 786440 | tf_op jit(solution)/shard_map/ppermute | solution.py:56
  149.0 4.9 %outgoing_pages.8 = (bf16[32,128,1024]{2,1,0:T(8,128)(2,1)}, bf16[2,128,512]{2,1,0:T(8,128)(2,1)}, bf16[2,128,512]{2,1,0:T(8,128)(2,1)}, bf16[2,128,512]{2,1,0:T(8,128)(2,1)}) custom-call(s32[256]{0:T(256)} %or_or_fusion.table_hbm.table, bf16[32,128,1024]{2,1,0:T(8,128)(2,1)} %pool.9, ...), custom_call_target="tpu_custom_call", output_to_operand_aliasing={{0}: (2, {})} | custom-call | bytes 1572864 | tf_op jit(solution)/shard_map/outgoing_pages/pallas_call | solution.py:180
  154.0 2.3 collective-permute-start.27
  156.7 4.0 %settle_pages.10 = (bf16[32,128,1024]{2,1,0:T(8,128)(2,1)}, f32[16,16,128]{2,1,0:T(8,128)}) custom-call(s32[256]{0:T(256)} %or_or_fusion.table_hbm.table, s32[256]{0:T(256)} %row_request.13, bf16[16,32,128]{2,1,0:T(8,128)(2,1)} %bitcast.5, f32[16,16,128]{2,1,0:T(8,128)} %broadcast_1_rows_in.2.rows_in, ...), custom_call_target="tpu_custom_call", output_to_operand_aliasing={{0}: (4, {})} | custom-call | flops 1073741824 | bytes 1572864 | tf_op jit(solution)/shard_map/settle_pages/pallas_call | solution.py:303
  160.7 4.9 %outgoing_pages.9 = (bf16[32,128,1024]{2,1,0:T(8,128)(2,1)}, bf16[2,128,512]{2,1,0:T(8,128)(2,1)}, bf16[2,128,512]{2,1,0:T(8,128)(2,1)}, bf16[2,128,512]{2,1,0:T(8,128)(2,1)}, bf16[2,128,512]{2,1,0:T(8,128)(2,1)}) custom-call(s32[256]{0:T(256)} %or_or_fusion.table_hbm.table, bf16[32,128,1024]{2,1,0:T(8,128)(2,1)} %pool.9, ...), custom_call_target="tpu_custom_call", output_to_operand_aliasing={{0}: (2, {})} | custom-call | bytes 2097152 | tf_op jit(solution)/shard_map/outgoing_pages/pallas_call | solution.py:180
  167.0 2.3 collective-permute-start.30
  169.6 2.4 collective-permute-done.28.rest_3_
  174.3 3.9 %settle_pages.11 = (bf16[32,128,1024]{2,1,0:T(8,128)(2,1)}, f32[16,16,128]{2,1,0:T(8,128)}) custom-call(s32[256]{0:T(256)} %or_or_fusion.table_hbm.table, s32[256]{0:T(256)} %row_request.13, bf16[16,32,128]{2,1,0:T(8,128)(2,1)} %bitcast.6, f32[16,16,128]{2,1,0:T(8,128)} %get-tuple-element.81.rows_in, ...), custom_call_target="tpu_custom_call", output_to_operand_aliasing={{0}: (4, {})} | custom-call | flops 1073741824 | bytes 1572864 | tf_op jit(solution)/shard_map/settle_pages/pallas_call | solution.py:303
  178.2 2.9 %project_rows.3 = (f32[128,512]{1,0:T(8,128)}, f32[128,512]{1,0:T(8,128)}) custom-call(bf16[4096,512]{1,0:T(8,128)(2,1)S(1)} %copy-done, bf16[128,2048]{1,0:T(8,128)(2,1)} %copy-done.3, bf16[128,2048]{1,0:T(8,128)(2,1)} %copy-done.1), custom_call_target="tpu_custom_call" | custom-call | flops 536870912 | bytes 2097152 | tf_op jit(solution)/shard_map/project_rows/pallas_call | solution.py:365
  181.1 23.8 %collective-permute-done.30.rest_5_ = bf16[2,128,512]{2,1,0:T(8,128)(2,1)} collective-permute-done((bf16[2,128,512]{2,1,0:T(8,128)(2,1)}, bf16[2,128,512]{2,1,0:T(8,128)(2,1)}, u32[]{:S(2)}, u32[]{:S(2)}) %collective-permute-start.30) | collective-permute-done | bytes 262176 | tf_op jit(solution)/shard_map/ppermute | solution.py:56
  204.9 5.3 %settle_pages.12 = (bf16[32,128,1024]{2,1,0:T(8,128)(2,1)}, f32[16,16,128]{2,1,0:T(8,128)}) custom-call(s32[256]{0:T(256)} %or_or_fusion.table_hbm.table, s32[256]{0:T(256)} %row_request.13, bf16[16,32,128]{2,1,0:T(8,128)(2,1)} %bitcast.7, f32[16,16,128]{2,1,0:T(8,128)} %get-tuple-element.87.rows_in, ...), custom_call_target="tpu_custom_call", output_to_operand_aliasing={{0}: (4, {})} | custom-call | flops 1073741824 | bytes 3145728 | tf_op jit(solution)/shard_map/settle_pages/pallas_call | solution.py:303
  210.2 7.1 %collective-permute-done.33.rest_1_ = bf16[2,128,512]{2,1,0:T(8,128)(2,1)S(1)} collective-permute-done((bf16[2,128,512]{2,1,0:T(8,128)(2,1)}, bf16[2,128,512]{2,1,0:T(8,128)(2,1)S(1)}, u32[]{:S(2)}, u32[]{:S(2)}) %collective-permute-start.33) | collective-permute-done | bytes 262176 | tf_op jit(solution)/shard_map/ppermute | solution.py:56
  217.3 3.3 %collective-permute-done.34.rest_2_ = bf16[2,128,512]{2,1,0:T(8,128)(2,1)S(1)} collective-permute-done((bf16[2,128,512]{2,1,0:T(8,128)(2,1)}, bf16[2,128,512]{2,1,0:T(8,128)(2,1)S(1)}, u32[]{:S(2)}, u32[]{:S(2)}) %collective-permute-start.34) | collective-permute-done | bytes 262176 | tf_op jit(solution)/shard_map/ppermute | solution.py:56
  221.3 5.0 %settle_pages.13 = (bf16[32,128,1024]{2,1,0:T(8,128)(2,1)}, bf16[16,2048]{1,0:T(8,128)(2,1)}) custom-call(s32[256]{0:T(256)} %or_or_fusion.table_hbm.table, s32[256]{0:T(256)} %row_request.13, bf16[16,32,128]{2,1,0:T(8,128)(2,1)} %bitcast.8, f32[16,16,128]{2,1,0:T(8,128)} %get-tuple-element.95.rows_in, ...), custom_call_target="tpu_custom_call", output_to_operand_aliasing={{0}: (4, {})} | custom-call | flops 1073741824 | bytes 1572864 | tf_op jit(solution)/shard_map/settle_pages/pallas_call | solution.py:303
  226.3 1.3 collective-permute-start.38
  227.7 2.8 %collective-permute-start.37 = (bf16[16,2048]{1,0:T(8,128)(2,1)}, bf16[16,2048]{1,0:T(8,128)(2,1)S(1)}, u32[]{:S(2)}, u32[]{:S(2)}) collective-permute-start(bf16[16,2048]{1,0:T(8,128)(2,1)} %get-tuple-element.103.rest_0_), channel_id=1, source_target_pairs={{0,24},{2,26},{4,28},{6,30},{8,0},{10,2},{12,4},{14,6},{16,8},{18,... | collective-permute-start | bytes 196616 | tf_op jit(solution)/shard_map/ppermute | solution.py:56
  231.7 1.6 collective-permute-done.37.rest_3_
  233.4 4.1 %collective-permute-done.36.rest_2_ = bf16[16,2048]{1,0:T(8,128)(2,1)S(1)} collective-permute-done((bf16[16,2048]{1,0:T(8,128)(2,1)}, bf16[16,2048]{1,0:T(8,128)(2,1)S(1)}, u32[]{:S(2)}, u32[]{:S(2)}) %collective-permute-start.36) | collective-permute-done | bytes 65568 | tf_op jit(solution)/shard_map/ppermute | solution.py:56
  240.2 1.9 collective-permute-done.40.rest_6_
  244.8 3.3 %project_rows.5 = bf16[128,512]{1,0:T(8,128)(2,1)} custom-call(bf16[4096,512]{1,0:T(8,128)(2,1)S(1)} %copy-done, bf16[16,2048]{1,0:T(8,128)(2,1)} %get-tuple-element.103.rest_0_, bf16[16,2048]{1,0:T(8,128)(2,1)} %copy-done.11, bf16[16,2048]{1,0:T(8,128)(2,1)} %copy-done.10, bf16[16,2048]{1,0:T(8,128)(2,1)} %copy-done.8, bf16[16,2048]{1,0:T(8,128)(2,1)} %copy-done.7, ...), custom_call_target="tpu_custom_call" | custom-call | flops 268435456 | bytes 2097152 | tf_op jit(solution)/shard_map/project_rows/pallas_call | solution.py:365
  248.1 1.6 collective-permute-start.50
  249.7 3.4 %project_rows.4 = f32[128,512]{1,0:T(8,128)} custom-call(bf16[4096,512]{1,0:T(8,128)(2,1)S(1)} %copy-done, bf16[16,2048]{1,0:T(8,128)(2,1)} %get-tuple-element.103.rest_0_, bf16[16,2048]{1,0:T(8,128)(2,1)} %copy-done.11, bf16[16,2048]{1,0:T(8,128)(2,1)} %copy-done.10, bf16[16,2048]{1,0:T(8,128)(2,1)} %copy-done.8, bf16[16,2048]{1,0:T(8,128)(2,1)} %copy-done.7, ...), custom_call_target="tpu_custom_call" | custom-call | flops 268435456 | bytes 2097152 | tf_op jit(solution)/shard_map/project_rows/pallas_call | solution.py:365
  253.9 1.6 add_convert_fusion
  (197 shorter events, 24.3 us)
Async XLA Ops:
  7.1 14.2 %collective-permute-start = (bf16[2,128,512]{2,1,0:T(8,128)(2,1)}, bf16[2,128,512]{2,1,0:T(8,128)(2,1)S(1)}, u32[]{:S(2)}, u32[]{:S(2)}) collective-permute-start(bf16[2,128,512]{2,1,0:T(8,128)(2,1)} %get-tuple-element.55), channel_id=1, source_target_pairs={{0,8},{2,10},{4,12},{6,14},{8,16},{10,18},{12,20},{14,22},{16,24},... | collective-permute-start | bytes 786440 | tf_op jit(solution)/shard_map/ppermute | solution.py:56
  10.2 13.3 %collective-permute-start.1 = (bf16[2,128,512]{2,1,0:T(8,128)(2,1)}, bf16[2,128,512]{2,1,0:T(8,128)(2,1)S(1)}, u32[]{:S(2)}, u32[]{:S(2)}) collective-permute-start(bf16[2,128,512]{2,1,0:T(8,128)(2,1)} %get-tuple-element.56), channel_id=1, source_target_pairs={{0,10},{2,8},{4,14},{6,12},{8,18},{10,16},{12,22},{14,20},{16,26},... | collective-permute-start | bytes 786440 | tf_op jit(solution)/shard_map/ppermute | solution.py:56
  10.9 15.7 %collective-permute-start.2 = (bf16[2,128,512]{2,1,0:T(8,128)(2,1)}, bf16[2,128,512]{2,1,0:T(8,128)(2,1)S(1)}, u32[]{:S(2)}, u32[]{:S(2)}) collective-permute-start(bf16[2,128,512]{2,1,0:T(8,128)(2,1)} %get-tuple-element.57), channel_id=1, source_target_pairs={{0,2},{2,0},{4,6},{6,4},{8,10},{10,8},{12,14},{14,12},{16,18},{18,... | collective-permute-start | bytes 786440 | tf_op jit(solution)/shard_map/ppermute | solution.py:56
  11.9 20.3 %collective-permute-start.3 = (bf16[2,128,512]{2,1,0:T(8,128)(2,1)}, bf16[2,128,512]{2,1,0:T(8,128)(2,1)S(1)}, u32[]{:S(2)}, u32[]{:S(2)}) collective-permute-start(bf16[2,128,512]{2,1,0:T(8,128)(2,1)} %get-tuple-element.58), channel_id=1, source_target_pairs={{0,12},{2,14},{4,8},{6,10},{8,20},{10,22},{12,16},{14,18},{16,28},... | collective-permute-start | bytes 786440 | tf_op jit(solution)/shard_map/ppermute | solution.py:56
  20.7 20.6 %collective-permute-start.4 = (bf16[2,128,512]{2,1,0:T(8,128)(2,1)}, bf16[2,128,512]{2,1,0:T(8,128)(2,1)S(1)}, u32[]{:S(2)}, u32[]{:S(2)}) collective-permute-start(bf16[2,128,512]{2,1,0:T(8,128)(2,1)} %get-tuple-element.59), channel_id=1, source_target_pairs={{0,4},{2,6},{4,0},{6,2},{8,12},{10,14},{12,8},{14,10},{16,20},{18,... | collective-permute-start | bytes 786440 | tf_op jit(solution)/shard_map/ppermute | solution.py:56
  21.4 21.6 %collective-permute-start.5 = (bf16[2,128,512]{2,1,0:T(8,128)(2,1)}, bf16[2,128,512]{2,1,0:T(8,128)(2,1)S(1)}, u32[]{:S(2)}, u32[]{:S(2)}) collective-permute-start(bf16[2,128,512]{2,1,0:T(8,128)(2,1)} %get-tuple-element.60), channel_id=1, source_target_pairs={{0,14},{2,12},{4,10},{6,8},{8,22},{10,20},{12,18},{14,16},{16,30},... | collective-permute-start | bytes 786440 | tf_op jit(solution)/shard_map/ppermute | solution.py:56
  23.5 34.0 %collective-permute-start.6 = (bf16[2,128,512]{2,1,0:T(8,128)(2,1)}, bf16[2,128,512]{2,1,0:T(8,128)(2,1)S(1)}, u32[]{:S(2)}, u32[]{:S(2)}) collective-permute-start(bf16[2,128,512]{2,1,0:T(8,128)(2,1)} %get-tuple-element.63), channel_id=1, source_target_pairs={{0,6},{2,4},{4,2},{6,0},{8,14},{10,12},{12,10},{14,8},{16,22},{18,... | collective-permute-start | bytes 786440 | tf_op jit(solution)/shard_map/ppermute | solution.py:56
  26.7 30.8 %collective-permute-start.7 = (bf16[2,128,512]{2,1,0:T(8,128)(2,1)}, bf16[2,128,512]{2,1,0:T(8,128)(2,1)S(1)}, u32[]{:S(2)}, u32[]{:S(2)}) collective-permute-start(bf16[2,128,512]{2,1,0:T(8,128)(2,1)} %get-tuple-element.64), channel_id=1, source_target_pairs={{0,24},{2,26},{4,28},{6,30},{8,0},{10,2},{12,4},{14,6},{16,8},{18,... | collective-permute-start | bytes 786440 | tf_op jit(solution)/shard_map/ppermute | solution.py:56
  32.2 25.4 %collective-permute-start.8 = (bf16[2,128,512]{2,1,0:T(8,128)(2,1)}, bf16[2,128,512]{2,1,0:T(8,128)(2,1)S(1)}, u32[]{:S(2)}, u32[]{:S(2)}) collective-permute-start(bf16[2,128,512]{2,1,0:T(8,128)(2,1)} %get-tuple-element.65), channel_id=1, source_target_pairs={{0,26},{2,24},{4,30},{6,28},{8,2},{10,0},{12,6},{14,4},{16,10},{18... | collective-permute-start | bytes 786440 | tf_op jit(solution)/shard_map/ppermute | solution.py:56
  41.3 20.2 %collective-permute-start.9 = (bf16[2,128,512]{2,1,0:T(8,128)(2,1)}, bf16[2,128,512]{2,1,0:T(8,128)(2,1)S(1)}, u32[]{:S(2)}, u32[]{:S(2)}) collective-permute-start(bf16[2,128,512]{2,1,0:T(8,128)(2,1)} %get-tuple-element.66), channel_id=1, source_target_pairs={{0,28},{2,30},{4,24},{6,26},{8,4},{10,6},{12,0},{14,2},{16,12},{18... | collective-permute-start | bytes 786440 | tf_op jit(solution)/shard_map/ppermute | solution.py:56
  43.0 27.4 %collective-permute-start.10 = (bf16[2,128,512]{2,1,0:T(8,128)(2,1)}, bf16[2,128,512]{2,1,0:T(8,128)(2,1)S(1)}, u32[]{:S(2)}, u32[]{:S(2)}) collective-permute-start(bf16[2,128,512]{2,1,0:T(8,128)(2,1)} %get-tuple-element.67), channel_id=1, source_target_pairs={{0,30},{2,28},{4,26},{6,24},{8,6},{10,4},{12,2},{14,0},{16,14},{18... | collective-permute-start | bytes 786440 | tf_op jit(solution)/shard_map/ppermute | solution.py:56
  57.5 38.4 %collective-permute-start.11 = (bf16[2,128,512]{2,1,0:T(8,128)(2,1)}, bf16[2,128,512]{2,1,0:T(8,128)(2,1)S(1)}, u32[]{:S(2)}, u32[]{:S(2)}) collective-permute-start(bf16[2,128,512]{2,1,0:T(8,128)(2,1)} %get-tuple-element.68), channel_id=1, source_target_pairs={{0,16},{2,18},{4,20},{6,22},{8,24},{10,26},{12,28},{14,30},{16,0},... | collective-permute-start | bytes 786440 | tf_op jit(solution)/shard_map/ppermute | solution.py:56
  57.5 49.5 %collective-permute-start.12 = (bf16[2,128,512]{2,1,0:T(8,128)(2,1)}, bf16[2,128,512]{2,1,0:T(8,128)(2,1)S(1)}, u32[]{:S(2)}, u32[]{:S(2)}) collective-permute-start(bf16[2,128,512]{2,1,0:T(8,128)(2,1)} %get-tuple-element.72), channel_id=1, source_target_pairs={{0,18},{2,16},{4,22},{6,20},{8,26},{10,24},{12,30},{14,28},{16,2},... | collective-permute-start | bytes 786440 | tf_op jit(solution)/shard_map/ppermute | solution.py:56
  57.6 56.0 %collective-permute-start.13 = (bf16[2,128,512]{2,1,0:T(8,128)(2,1)}, bf16[2,128,512]{2,1,0:T(8,128)(2,1)S(1)}, u32[]{:S(2)}, u32[]{:S(2)}) collective-permute-start(bf16[2,128,512]{2,1,0:T(8,128)(2,1)} %get-tuple-element.73), channel_id=1, source_target_pairs={{0,20},{2,22},{4,16},{6,18},{8,28},{10,30},{12,24},{14,26},{16,4},... | collective-permute-start | bytes 786440 | tf_op jit(solution)/shard_map/ppermute | solution.py:56
  61.5 52.9 %collective-permute-start.14 = (bf16[2,128,512]{2,1,0:T(8,128)(2,1)}, bf16[2,128,512]{2,1,0:T(8,128)(2,1)S(1)}, u32[]{:S(2)}, u32[]{:S(2)}) collective-permute-start(bf16[2,128,512]{2,1,0:T(8,128)(2,1)} %get-tuple-element.74), channel_id=1, source_target_pairs={{0,22},{2,20},{4,18},{6,16},{8,30},{10,28},{12,26},{14,24},{16,6},... | collective-permute-start | bytes 786440 | tf_op jit(solution)/shard_map/ppermute | solution.py:56
  70.5 60.9 %collective-permute-start.18 = (bf16[2,128,512]{2,1,0:T(8,128)(2,1)S(1)}, bf16[2,128,512]{2,1,0:T(8,128)(2,1)S(1)}, u32[]{:S(2)}, u32[]{:S(2)}) collective-permute-start(bf16[2,128,512]{2,1,0:T(8,128)(2,1)S(1)} %copy-done.54), channel_id=1, source_target_pairs={{0,8},{2,10},{4,12},{6,14},{8,16},{10,18},{12,20},{14,22},{16,24},... | collective-permute-start | bytes 786440 | tf_op jit(solution)/shard_map/ppermute | solution.py:56
  95.9 48.4 %collective-permute-start.19 = (bf16[2,128,512]{2,1,0:T(8,128)(2,1)S(1)}, bf16[2,128,512]{2,1,0:T(8,128)(2,1)S(1)}, u32[]{:S(2)}, u32[]{:S(2)}) collective-permute-start(bf16[2,128,512]{2,1,0:T(8,128)(2,1)S(1)} %copy-done.53), channel_id=1, source_target_pairs={{0,10},{2,8},{4,14},{6,12},{8,18},{10,16},{12,22},{14,20},{16,26},... | collective-permute-start | bytes 786440 | tf_op jit(solution)/shard_map/ppermute | solution.py:56
  120.1 4.5 %collective-permute-start.17 = (bf16[16,2048]{1,0:T(8,128)(2,1)}, bf16[16,2048]{1,0:T(8,128)(2,1)S(1)}, u32[]{:S(2)}, u32[]{:S(2)}) collective-permute-start(bf16[16,2048]{1,0:T(8,128)(2,1)} %get-tuple-element.76), channel_id=1, source_target_pairs={{0,24},{2,26},{4,28},{6,30},{8,0},{10,2},{12,4},{14,6},{16,8},{18,... | collective-permute-start | bytes 196616 | tf_op jit(solution)/shard_map/ppermute | solution.py:56
  120.2 6.0 %collective-permute-start.16 = (bf16[16,2048]{1,0:T(8,128)(2,1)}, bf16[16,2048]{1,0:T(8,128)(2,1)S(1)}, u32[]{:S(2)}, u32[]{:S(2)}) collective-permute-start(bf16[16,2048]{1,0:T(8,128)(2,1)} %get-tuple-element.76), channel_id=1, source_target_pairs={{0,16},{2,18},{4,20},{6,22},{8,24},{10,26},{12,28},{14,30},{16,0},... | collective-permute-start | bytes 196616 | tf_op jit(solution)/shard_map/ppermute | solution.py:56
  121.3 7.7 %collective-permute-start.15 = (bf16[16,2048]{1,0:T(8,128)(2,1)}, bf16[16,2048]{1,0:T(8,128)(2,1)S(1)}, u32[]{:S(2)}, u32[]{:S(2)}) collective-permute-start(bf16[16,2048]{1,0:T(8,128)(2,1)} %get-tuple-element.76), channel_id=1, source_target_pairs={{0,8},{2,10},{4,12},{6,14},{8,16},{10,18},{12,20},{14,22},{16,24},... | collective-permute-start | bytes 196616 | tf_op jit(solution)/shard_map/ppermute | solution.py:56
  124.6 20.1 %collective-permute-start.20 = (bf16[2,128,512]{2,1,0:T(8,128)(2,1)S(1)}, bf16[2,128,512]{2,1,0:T(8,128)(2,1)S(1)}, u32[]{:S(2)}, u32[]{:S(2)}) collective-permute-start(bf16[2,128,512]{2,1,0:T(8,128)(2,1)S(1)} %copy-done.52), channel_id=1, source_target_pairs={{0,2},{2,0},{4,6},{6,4},{8,10},{10,8},{12,14},{14,12},{16,18},{18,... | collective-permute-start | bytes 786440 | tf_op jit(solution)/shard_map/ppermute | solution.py:56
  126.2 19.0 %collective-permute-start.22 = (bf16[2,128,512]{2,1,0:T(8,128)(2,1)S(1)}, bf16[2,128,512]{2,1,0:T(8,128)(2,1)S(1)}, u32[]{:S(2)}, u32[]{:S(2)}) collective-permute-start(bf16[2,128,512]{2,1,0:T(8,128)(2,1)S(1)} %copy-done.58), channel_id=1, source_target_pairs={{0,12},{2,14},{4,8},{6,10},{8,20},{10,22},{12,16},{14,18},{16,28},... | collective-permute-start | bytes 786440 | tf_op jit(solution)/shard_map/ppermute | solution.py:56
  129.9 13.9 %collective-permute-start.21 = (bf16[64,2048]{1,0:T(8,128)(2,1)S(1)}, bf16[64,2048]{1,0:T(8,128)(2,1)S(1)}, u32[]{:S(2)}, u32[]{:S(2)}) collective-permute-start(bf16[64,2048]{1,0:T(8,128)(2,1)S(1)} %pad_maximum_fusion), channel_id=1, source_target_pairs={{0,4},{2,6},{4,0},{6,2},{8,12},{10,14},{12,8},{14,10},{16,20},{18,... | collective-permute-start | bytes 786440 | tf_op jit(solution)/shard_map/ppermute | solution.py:56
  131.4 22.6 %collective-permute-start.23 = (bf16[2,128,512]{2,1,0:T(8,128)(2,1)S(1)}, bf16[2,128,512]{2,1,0:T(8,128)(2,1)S(1)}, u32[]{:S(2)}, u32[]{:S(2)}) collective-permute-start(bf16[2,128,512]{2,1,0:T(8,128)(2,1)S(1)} %copy-done.57), channel_id=1, source_target_pairs={{0,4},{2,6},{4,0},{6,2},{8,12},{10,14},{12,8},{14,10},{16,20},{18,... | collective-permute-start | bytes 786440 | tf_op jit(solution)/shard_map/ppermute | solution.py:56
  143.7 12.6 %collective-permute-start.24 = (bf16[2,128,512]{2,1,0:T(8,128)(2,1)S(1)}, bf16[2,128,512]{2,1,0:T(8,128)(2,1)S(1)}, u32[]{:S(2)}, u32[]{:S(2)}) collective-permute-start(bf16[2,128,512]{2,1,0:T(8,128)(2,1)S(1)} %copy-done.56), channel_id=1, source_target_pairs={{0,14},{2,12},{4,10},{6,8},{8,22},{10,20},{12,18},{14,16},{16,30},... | collective-permute-start | bytes 786440 | tf_op jit(solution)/shard_map/ppermute | solution.py:56
  144.4 28.8 %collective-permute-start.31 = (bf16[128,2048]{1,0:T(8,128)(2,1)S(1)}, bf16[128,2048]{1,0:T(8,128)(2,1)S(1)}, u32[]{:S(2)}, u32[]{:S(2)}) collective-permute-start(bf16[128,2048]{1,0:T(8,128)(2,1)S(1)} %constant_dynamic-update-slice_fusion.rest_0_), channel_id=1, source_target_pairs={{0,2},{2,0},{4,6},{6,4},{8,10},{10,8},{12,14},{14,12},{16,18},{18,... | collective-permute-start | bytes 1572872 | tf_op jit(solution)/shard_map/ppermute | solution.py:56
  144.8 20.9 %collective-permute-start.25 = (bf16[2,128,512]{2,1,0:T(8,128)(2,1)}, bf16[2,128,512]{2,1,0:T(8,128)(2,1)S(1)}, u32[]{:S(2)}, u32[]{:S(2)}) collective-permute-start(bf16[2,128,512]{2,1,0:T(8,128)(2,1)} %get-tuple-element.89), channel_id=1, source_target_pairs={{0,6},{2,4},{4,2},{6,0},{8,14},{10,12},{12,10},{14,8},{16,22},{18,... | collective-permute-start | bytes 786440 | tf_op jit(solution)/shard_map/ppermute | solution.py:56
  145.1 21.9 %collective-permute-start.26 = (bf16[2,128,512]{2,1,0:T(8,128)(2,1)S(1)}, bf16[2,128,512]{2,1,0:T(8,128)(2,1)S(1)}, u32[]{:S(2)}, u32[]{:S(2)}) collective-permute-start(bf16[2,128,512]{2,1,0:T(8,128)(2,1)S(1)} %copy-done.55), channel_id=1, source_target_pairs={{0,24},{2,26},{4,28},{6,30},{8,0},{10,2},{12,4},{14,6},{16,8},{18,... | collective-permute-start | bytes 786440 | tf_op jit(solution)/shard_map/ppermute | solution.py:56
  154.0 15.4 %collective-permute-start.27 = (bf16[2,128,512]{2,1,0:T(8,128)(2,1)}, bf16[2,128,512]{2,1,0:T(8,128)(2,1)S(1)}, u32[]{:S(2)}, u32[]{:S(2)}) collective-permute-start(bf16[2,128,512]{2,1,0:T(8,128)(2,1)} %get-tuple-element.91), channel_id=1, source_target_pairs={{0,26},{2,24},{4,30},{6,28},{8,2},{10,0},{12,6},{14,4},{16,10},{18... | collective-permute-start | bytes 786440 | tf_op jit(solution)/shard_map/ppermute | solution.py:56
  156.3 15.7 %collective-permute-start.28 = (bf16[2,128,512]{2,1,0:T(8,128)(2,1)}, bf16[2,128,512]{2,1,0:T(8,128)(2,1)S(1)}, u32[]{:S(2)}, u32[]{:S(2)}) collective-permute-start(bf16[2,128,512]{2,1,0:T(8,128)(2,1)} %get-tuple-element.92), channel_id=1, source_target_pairs={{0,28},{2,30},{4,24},{6,26},{8,4},{10,6},{12,0},{14,2},{16,12},{18... | collective-permute-start | bytes 786440 | tf_op jit(solution)/shard_map/ppermute | solution.py:56
  165.7 15.4 %collective-permute-start.29 = (bf16[2,128,512]{2,1,0:T(8,128)(2,1)}, bf16[2,128,512]{2,1,0:T(8,128)(2,1)S(1)}, u32[]{:S(2)}, u32[]{:S(2)}) collective-permute-start(bf16[2,128,512]{2,1,0:T(8,128)(2,1)} %get-tuple-element.93), channel_id=1, source_target_pairs={{0,30},{2,28},{4,26},{6,24},{8,6},{10,4},{12,2},{14,0},{16,14},{18... | collective-permute-start | bytes 786440 | tf_op jit(solution)/shard_map/ppermute | solution.py:56
  167.0 37.9 %collective-permute-start.30 = (bf16[2,128,512]{2,1,0:T(8,128)(2,1)}, bf16[2,128,512]{2,1,0:T(8,128)(2,1)}, u32[]{:S(2)}, u32[]{:S(2)}) collective-permute-start(bf16[2,128,512]{2,1,0:T(8,128)(2,1)} %get-tuple-element.94), channel_id=1, source_target_pairs={{0,16},{2,18},{4,20},{6,22},{8,24},{10,26},{12,28},{14,30},{16,0},... | collective-permute-start | bytes 786440 | tf_op jit(solution)/shard_map/ppermute | solution.py:56
  169.3 40.9 %collective-permute-start.32 = (bf16[2,128,512]{2,1,0:T(8,128)(2,1)}, bf16[2,128,512]{2,1,0:T(8,128)(2,1)S(1)}, u32[]{:S(2)}, u32[]{:S(2)}) collective-permute-start(bf16[2,128,512]{2,1,0:T(8,128)(2,1)} %get-tuple-element.97), channel_id=1, source_target_pairs={{0,18},{2,16},{4,22},{6,20},{8,26},{10,24},{12,30},{14,28},{16,2},... | collective-permute-start | bytes 786440 | tf_op jit(solution)/shard_map/ppermute | solution.py:56
  171.9 45.4 %collective-permute-start.33 = (bf16[2,128,512]{2,1,0:T(8,128)(2,1)}, bf16[2,128,512]{2,1,0:T(8,128)(2,1)S(1)}, u32[]{:S(2)}, u32[]{:S(2)}) collective-permute-start(bf16[2,128,512]{2,1,0:T(8,128)(2,1)} %get-tuple-element.98), channel_id=1, source_target_pairs={{0,20},{2,22},{4,16},{6,18},{8,28},{10,30},{12,24},{14,26},{16,4},... | collective-permute-start | bytes 786440 | tf_op jit(solution)/shard_map/ppermute | solution.py:56
  173.2 47.4 %collective-permute-start.34 = (bf16[2,128,512]{2,1,0:T(8,128)(2,1)}, bf16[2,128,512]{2,1,0:T(8,128)(2,1)S(1)}, u32[]{:S(2)}, u32[]{:S(2)}) collective-permute-start(bf16[2,128,512]{2,1,0:T(8,128)(2,1)} %get-tuple-element.99), channel_id=1, source_target_pairs={{0,22},{2,20},{4,18},{6,16},{8,30},{10,28},{12,26},{14,24},{16,6},... | collective-permute-start | bytes 786440 | tf_op jit(solution)/shard_map/ppermute | solution.py:56
  226.3 5.2 %collective-permute-start.38 = (bf16[16,2048]{1,0:T(8,128)(2,1)}, bf16[16,2048]{1,0:T(8,128)(2,1)S(1)}, u32[]{:S(2)}, u32[]{:S(2)}) collective-permute-start(bf16[16,2048]{1,0:T(8,128)(2,1)} %get-tuple-element.103.rest_0_), channel_id=1, source_target_pairs={{0,4},{2,6},{4,0},{6,2},{8,12},{10,14},{12,8},{14,10},{16,20},{18,... | collective-permute-start | bytes 196616 | tf_op jit(solution)/shard_map/ppermute | solution.py:56
  227.7 5.6 %collective-permute-start.37 = (bf16[16,2048]{1,0:T(8,128)(2,1)}, bf16[16,2048]{1,0:T(8,128)(2,1)S(1)}, u32[]{:S(2)}, u32[]{:S(2)}) collective-permute-start(bf16[16,2048]{1,0:T(8,128)(2,1)} %get-tuple-element.103.rest_0_), channel_id=1, source_target_pairs={{0,24},{2,26},{4,28},{6,30},{8,0},{10,2},{12,4},{14,6},{16,8},{18,... | collective-permute-start | bytes 196616 | tf_op jit(solution)/shard_map/ppermute | solution.py:56
  230.4 2.9 %collective-permute-start.42 = (bf16[16,2048]{1,0:T(8,128)(2,1)}, bf16[16,2048]{1,0:T(8,128)(2,1)S(1)}, u32[]{:S(2)}, u32[]{:S(2)}) collective-permute-start(bf16[16,2048]{1,0:T(8,128)(2,1)} %get-tuple-element.103.rest_0_), channel_id=1, source_target_pairs={{0,2},{2,0},{4,6},{6,4},{8,10},{10,8},{12,14},{14,12},{16,18},{18,... | collective-permute-start | bytes 196616 | tf_op jit(solution)/shard_map/ppermute | solution.py:56
  230.4 7.1 %collective-permute-start.36 = (bf16[16,2048]{1,0:T(8,128)(2,1)}, bf16[16,2048]{1,0:T(8,128)(2,1)S(1)}, u32[]{:S(2)}, u32[]{:S(2)}) collective-permute-start(bf16[16,2048]{1,0:T(8,128)(2,1)} %get-tuple-element.103.rest_0_), channel_id=1, source_target_pairs={{0,16},{2,18},{4,20},{6,22},{8,24},{10,26},{12,28},{14,30},{16,0},... | collective-permute-start | bytes 196616 | tf_op jit(solution)/shard_map/ppermute | solution.py:56
  230.4 7.9 %collective-permute-start.35 = (bf16[16,2048]{1,0:T(8,128)(2,1)}, bf16[16,2048]{1,0:T(8,128)(2,1)S(1)}, u32[]{:S(2)}, u32[]{:S(2)}) collective-permute-start(bf16[16,2048]{1,0:T(8,128)(2,1)} %get-tuple-element.103.rest_0_), channel_id=1, source_target_pairs={{0,8},{2,10},{4,12},{6,14},{8,16},{10,18},{12,20},{14,22},{16,24},... | collective-permute-start | bytes 196616 | tf_op jit(solution)/shard_map/ppermute | solution.py:56
  231.5 8.0 %collective-permute-start.46 = (bf16[16,2048]{1,0:T(8,128)(2,1)S(1)}, bf16[16,2048]{1,0:T(8,128)(2,1)S(1)}, u32[]{:S(2)}, u32[]{:S(2)}) collective-permute-start(bf16[16,2048]{1,0:T(8,128)(2,1)S(1)} %collective-permute-done.38.rest_4_), channel_id=1, source_target_pairs={{0,2},{2,0},{4,6},{6,4},{8,10},{10,8},{12,14},{14,12},{16,18},{18,... | collective-permute-start | bytes 196616 | tf_op jit(solution)/shard_map/ppermute | solution.py:56
  233.3 6.3 %collective-permute-start.45 = (bf16[16,2048]{1,0:T(8,128)(2,1)S(1)}, bf16[16,2048]{1,0:T(8,128)(2,1)S(1)}, u32[]{:S(2)}, u32[]{:S(2)}) collective-permute-start(bf16[16,2048]{1,0:T(8,128)(2,1)S(1)} %collective-permute-done.37.rest_3_), channel_id=1, source_target_pairs={{0,2},{2,0},{4,6},{6,4},{8,10},{10,8},{12,14},{14,12},{16,18},{18,... | collective-permute-start | bytes 196616 | tf_op jit(solution)/shard_map/ppermute | solution.py:56
  233.3 6.8 %collective-permute-start.41 = (bf16[16,2048]{1,0:T(8,128)(2,1)S(1)}, bf16[16,2048]{1,0:T(8,128)(2,1)S(1)}, u32[]{:S(2)}, u32[]{:S(2)}) collective-permute-start(bf16[16,2048]{1,0:T(8,128)(2,1)S(1)} %collective-permute-done.37.rest_3_), channel_id=1, source_target_pairs={{0,4},{2,6},{4,0},{6,2},{8,12},{10,14},{12,8},{14,10},{16,20},{18,... | collective-permute-start | bytes 196616 | tf_op jit(solution)/shard_map/ppermute | solution.py:56
  237.5 4.5 %collective-permute-start.40 = (bf16[16,2048]{1,0:T(8,128)(2,1)S(1)}, bf16[16,2048]{1,0:T(8,128)(2,1)S(1)}, u32[]{:S(2)}, u32[]{:S(2)}) collective-permute-start(bf16[16,2048]{1,0:T(8,128)(2,1)S(1)} %collective-permute-done.36.rest_2_), channel_id=1, source_target_pairs={{0,4},{2,6},{4,0},{6,2},{8,12},{10,14},{12,8},{14,10},{16,20},{18,... | collective-permute-start | bytes 196616 | tf_op jit(solution)/shard_map/ppermute | solution.py:56
  238.3 4.4 %collective-permute-start.39 = (bf16[16,2048]{1,0:T(8,128)(2,1)S(1)}, bf16[16,2048]{1,0:T(8,128)(2,1)S(1)}, u32[]{:S(2)}, u32[]{:S(2)}) collective-permute-start(bf16[16,2048]{1,0:T(8,128)(2,1)S(1)} %collective-permute-done.35.rest_1_), channel_id=1, source_target_pairs={{0,4},{2,6},{4,0},{6,2},{8,12},{10,14},{12,8},{14,10},{16,20},{18,... | collective-permute-start | bytes 196616 | tf_op jit(solution)/shard_map/ppermute | solution.py:56
  239.6 3.2 %collective-permute-start.44 = (bf16[16,2048]{1,0:T(8,128)(2,1)S(1)}, bf16[16,2048]{1,0:T(8,128)(2,1)S(1)}, u32[]{:S(2)}, u32[]{:S(2)}) collective-permute-start(bf16[16,2048]{1,0:T(8,128)(2,1)S(1)} %collective-permute-done.36.rest_2_), channel_id=1, source_target_pairs={{0,2},{2,0},{4,6},{6,4},{8,10},{10,8},{12,14},{14,12},{16,18},{18,... | collective-permute-start | bytes 196616 | tf_op jit(solution)/shard_map/ppermute | solution.py:56
  239.6 3.2 %collective-permute-start.43 = (bf16[16,2048]{1,0:T(8,128)(2,1)S(1)}, bf16[16,2048]{1,0:T(8,128)(2,1)S(1)}, u32[]{:S(2)}, u32[]{:S(2)}) collective-permute-start(bf16[16,2048]{1,0:T(8,128)(2,1)S(1)} %collective-permute-done.35.rest_1_), channel_id=1, source_target_pairs={{0,2},{2,0},{4,6},{6,4},{8,10},{10,8},{12,14},{14,12},{16,18},{18,... | collective-permute-start | bytes 196616 | tf_op jit(solution)/shard_map/ppermute | solution.py:56
  248.1 5.8 %collective-permute-start.50 = (bf16[128,512]{1,0:T(8,128)(2,1)}, bf16[128,512]{1,0:T(8,128)(2,1)S(1)}, u32[]{:S(2)}, u32[]{:S(2)}) collective-permute-start(bf16[128,512]{1,0:T(8,128)(2,1)} %project_rows.5), channel_id=1, source_target_pairs={{0,1},{1,0},{2,3},{3,2},{4,5},{5,4},{6,7},{7,6},{8,9},{9,8},{10,11... | collective-permute-start | bytes 393224 | tf_op jit(solution)/shard_map/ppermute | solution.py:454
  (62 other events, 1129.6 us)

commit v9 on v7

--- a/solution.py
+++ b/solution.py
@@ -13,7 +13,7 @@
 WAVE = 3
 ROW_UNROLL = 4
 EARLY = 4
-VMEM_LIMIT = 40 * 1024 * 1024
+VMEM_LIMIT = 57 * 1024 * 1024
 
 
 def factors(groups):
@@ -27,14 +27,11 @@
 
 def page_rounds(dims):
     far, near = dims
-    if far != 4:
-        near_rounds = [uniform(0, n, dims) for n in range(1, near)]
-        return near_rounds + [uniform(z, n, dims) for z in range(1, far) for n in range(near)]
-    outer = [((2, n), (0, n), (3, n), (1, n)) for n in range(near)]
-    inner = [((1, n), (3, n), (0, n), (2, n)) for n in range(near)]
-    outer += [((3, n), (1, n), (2, n), (0, n)) for n in range(1, near)]
-    inner += [((0, n), (2, n), (1, n), (3, n)) for n in range(1, near)]
-    return outer + [((3, 0), (2, 0), (1, 0), (0, 0))] + inner
+    steps = sorted(range(1, far), key=lambda z: (min(z, far - z), z))
+    order = [(z, n) for z in steps for n in range(near)]
+    for n in range(1, near):
+        order.insert(min(2 * n, len(order)), (0, n))
+    return [uniform(z, n, dims) for z, n in order]
 
 
 def reverse(route):

time: 235 us -> 238 us (1.013)
  waiting for transfers between devices: 142 us -> 108 us
  starting transfers between devices: 60.5 us -> 79.2 us
  Pallas kernels: 25.9 us -> 41.6 us
    ppermute x30, waiting for transfers between devices: 138 us -> 104 us  [send_by(): return lax.ppermute(array, 'group', pairs)]
    ppermute x30, starting transfers between devices: 58.9 us -> 77.6 us  [send_by(): return lax.ppermute(array, 'group', pairs)]
    pallas_call x5, Pallas kernels: 13.4 us -> 24.4 us  [settle(): pl.pallas_call(functools.partial(settle_kernel, dims, routes, own, last),...]
    pallas_call x2, Pallas kernels: 8.09 us -> 13.4 us  [prepare(): pl.pallas_call(functools.partial(prepare_kernel, dims, routes, own), out_...]
  transfers between devices with their start and end apart: 31 -> 31, of which waited for: 20 -> 14; matrix products, arithmetic and copies ran while one was open for 0% -> 1% of each run, Pallas kernels for 6% -> 12%
where the time goes in v9:
time: 238 us; the launch traced here: 236 us
  waiting for transfers between devices  108 us (45%)
  starting transfers between devices  79.2 us (33%)
  Pallas kernels  41.6 us (17%)
  local copies, waits for them, and re-layouts  2.99 us (1%)
  other arithmetic  2.89 us (1%)
    ppermute x30, waiting for transfers between devices, send_by(): return lax.ppermute(array, 'group', pairs)  104 us
    ppermute x30, starting transfers between devices, send_by(): return lax.ppermute(array, 'group', pairs)  77.6 us
    pallas_call x5, Pallas kernels, settle(): pl.pallas_call(functools.partial(settle_kernel, dims, routes, own, last),...  24.4 us
    pallas_call x2, Pallas kernels, prepare(): pl.pallas_call(functools.partial(prepare_kernel, dims, routes, own), out_...  13.4 us
  transfers between devices with their start and end apart: 31, of which 14 were waited for; matrix products, arithmetic and copies ran while one was open for 1% of the time, Pallas kernels for 12%

profile of v9, /device:TPU:0, one launch (start us, length us, event | category | flops | bytes accessed | tf_op | source)
XLA Modules:
  0.0 236.0 jit_solution(11080642218595056350)
XLA Ops:
  0.6 1.2 or_or_fusion.table_hbm.table
  1.9 5.5 %outgoing_pages.2 = (bf16[32,128,1024]{2,1,0:T(8,128)(2,1)}, bf16[2,128,1024]{2,1,0:T(8,128)(2,1)}, bf16[2,128,1024]{2,1,0:T(8,128)(2,1)}, bf16[2,128,1024]{2,1,0:T(8,128)(2,1)}, bf16[2,128,1024]{2,1,0:T(8,128)(2,1)}) custom-call(s32[256]{0:T(256)} %or_or_fusion.table_hbm.table, bf16[32,128,1024]{2,1,0:T(8,128)(2,1)} %pool.3), custom_call_target="tpu_custom_call" | custom-call | bytes 5242880 | tf_op jit(solution)/shard_map/outgoing_pages/pallas_call | solution.py:154
  7.4 3.1 %collective-permute-start = (bf16[2,128,1024]{2,1,0:T(8,128)(2,1)}, bf16[2,128,1024]{2,1,0:T(8,128)(2,1)S(1)}, u32[]{:S(2)}, u32[]{:S(2)}) collective-permute-start(bf16[2,128,1024]{2,1,0:T(8,128)(2,1)} %get-tuple-element.33), channel_id=1, source_target_pairs={{0,8},{2,10},{4,12},{6,14},{8,16},{10,18},{12,20},{14,22},{16,24},... | collective-permute-start | bytes 1572872 | tf_op jit(solution)/shard_map/ppermute | solution.py:57
  10.4 0.7 collective-permute-start.1
  11.2 1.0 collective-permute-start.2
  12.1 2.5 %collective-permute-start.3 = (bf16[2,128,1024]{2,1,0:T(8,128)(2,1)}, bf16[2,128,1024]{2,1,0:T(8,128)(2,1)S(1)}, u32[]{:S(2)}, u32[]{:S(2)}) collective-permute-start(bf16[2,128,1024]{2,1,0:T(8,128)(2,1)} %get-tuple-element.38), channel_id=1, source_target_pairs={{0,12},{2,14},{4,8},{6,10},{8,20},{10,22},{12,16},{14,18},{16,28},... | collective-permute-start | bytes 1572872 | tf_op jit(solution)/shard_map/ppermute | solution.py:57
  14.7 7.9 %outgoing_pages.3 = (bf16[32,128,1024]{2,1,0:T(8,128)(2,1)}, bf16[2,128,1024]{2,1,0:T(8,128)(2,1)}, bf16[2,128,1024]{2,1,0:T(8,128)(2,1)}, bf16[2,128,1024]{2,1,...) custom-call(s32[256]{0:T(256)} %or_or_fusion.table_hbm.table, ...), custom_call_target="tpu_custom_call", output_to_operand_aliasing={{0}: (2, {})} | custom-call | bytes 11534336 | tf_op jit(solution)/shard_map/outgoing_pages/pallas_call | solution.py:154
  22.6 0.5 collective-permute-start.4
  23.0 2.4 %collective-permute-done.rest_0_ = bf16[2,128,1024]{2,1,0:T(8,128)(2,1)S(1)} collective-permute-done((bf16[2,128,1024]{2,1,0:T(8,128)(2,1)}, bf16[2,128,1024]{2,1,0:T(8,128)(2,1)S(1)}, u32[]{:S(2)}, u32[]{:S(2)}) %collective-permute-start) | collective-permute-done | bytes 524320 | tf_op jit(solution)/shard_map/ppermute | solution.py:57
  25.4 9.6 %collective-permute-done.1.rest_1_ = bf16[2,128,1024]{2,1,0:T(8,128)(2,1)S(1)} collective-permute-done((bf16[2,128,1024]{2,1,0:T(8,128)(2,1)}, bf16[2,128,1024]{2,1,0:T(8,128)(2,1)S(1)}, u32[]{:S(2)}, u32[]{:S(2)}) %collective-permute-start.1) | collective-permute-done | bytes 524320 | tf_op jit(solution)/shard_map/ppermute | solution.py:57
  35.0 3.1 %collective-permute-start.6 = (bf16[2,128,1024]{2,1,0:T(8,128)(2,1)}, bf16[2,128,1024]{2,1,0:T(8,128)(2,1)S(1)}, u32[]{:S(2)}, u32[]{:S(2)}) collective-permute-start(bf16[2,128,1024]{2,1,0:T(8,128)(2,1)} %get-tuple-element.43), channel_id=1, source_target_pairs={{0,6},{2,4},{4,2},{6,0},{8,14},{10,12},{12,10},{14,8},{16,22},{18,... | collective-permute-start | bytes 1572872 | tf_op jit(solution)/shard_map/ppermute | solution.py:57
  38.1 1.8 collective-permute-start.7
  40.0 9.3 %collective-permute-done.3.rest_0_ = bf16[2,128,1024]{2,1,0:T(8,128)(2,1)S(1)} collective-permute-done((bf16[2,128,1024]{2,1,0:T(8,128)(2,1)}, bf16[2,128,1024]{2,1,0:T(8,128)(2,1)S(1)}, u32[]{:S(2)}, u32[]{:S(2)}) %collective-permute-start.3) | collective-permute-done | bytes 524320 | tf_op jit(solution)/shard_map/ppermute | solution.py:57
  49.3 1.7 collective-permute-start.9
  51.0 7.4 %collective-permute-done.5.rest_2_ = bf16[2,128,1024]{2,1,0:T(8,128)(2,1)S(1)} collective-permute-done((bf16[2,128,1024]{2,1,0:T(8,128)(2,1)}, bf16[2,128,1024]{2,1,0:T(8,128)(2,1)S(1)}, u32[]{:S(2)}, u32[]{:S(2)}) %collective-permute-start.5) | collective-permute-done | bytes 524320 | tf_op jit(solution)/shard_map/ppermute | solution.py:57
  58.4 41.7 %collective-permute-start.10 = (bf16[2,128,1024]{2,1,0:T(8,128)(2,1)}, bf16[2,128,1024]{2,1,0:T(8,128)(2,1)S(1)}, u32[]{:S(2)}, u32[]{:S(2)}) collective-permute-start(bf16[2,128,1024]{2,1,0:T(8,128)(2,1)} %get-tuple-element.49), channel_id=1, source_target_pairs={{0,30},{2,28},{4,26},{6,24},{8,6},{10,4},{12,2},{14,0},{16,14},{18... | collective-permute-start | bytes 1572872 | tf_op jit(solution)/shard_map/ppermute | solution.py:57
  100.2 0.1 collective-permute-start.12
  100.3 12.7 %collective-permute-start.13 = (bf16[2,128,1024]{2,1,0:T(8,128)(2,1)}, bf16[2,128,1024]{2,1,0:T(8,128)(2,1)S(1)}, u32[]{:S(2)}, u32[]{:S(2)}) collective-permute-start(bf16[2,128,1024]{2,1,0:T(8,128)(2,1)} %get-tuple-element.54), channel_id=1, source_target_pairs={{0,20},{2,22},{4,16},{6,18},{8,28},{10,30},{12,24},{14,26},{16,4},... | collective-permute-start | bytes 1572872 | tf_op jit(solution)/shard_map/ppermute | solution.py:57
  113.0 0.7 copy.15
  113.8 0.7 broadcast_in_dim.3.rows_in
  114.5 5.9 %settle_pages.5 = (bf16[32,128,1024]{2,1,0:T(8,128)(2,1)}, f32[16,32,128]{2,1,0:T(8,128)}) custom-call(s32[256]{0:T(256)} %or_or_fusion.table_hbm.table, s32[256]{0:T(256)} %row_request.9, bf16[16,32,128]{2,1,0:T(8,128)(2,1)} %bitcast.2, f32[16,32,128]{2,1,0:T(8,128)} %broadcast_in_dim.3.rows_in, ...), custom_call_target="tpu_custom_call", output_to_operand_aliasing={{0}: (4, {})} | custom-call | flops 1073741824 | bytes 3145728 | tf_op jit(solution)/shard_map/settle_pages/pallas_call | solution.py:274
  120.5 4.5 %settle_pages.6 = (bf16[32,128,1024]{2,1,0:T(8,128)(2,1)}, f32[16,32,128]{2,1,0:T(8,128)}) custom-call(s32[256]{0:T(256)} %or_or_fusion.table_hbm.table, s32[256]{0:T(256)} %row_request.9, bf16[16,32,128]{2,1,0:T(8,128)(2,1)} %bitcast.3, f32[16,32,128]{2,1,0:T(8,128)} %get-tuple-element.36.rows_in, ...), custom_call_target="tpu_custom_call", output_to_operand_aliasing={{0}: (4, {})} | custom-call | flops 1073741824 | bytes 3145728 | tf_op jit(solution)/shard_map/settle_pages/pallas_call | solution.py:274
  125.0 4.5 %settle_pages.7 = (bf16[32,128,1024]{2,1,0:T(8,128)(2,1)}, f32[16,32,128]{2,1,0:T(8,128)}) custom-call(s32[256]{0:T(256)} %or_or_fusion.table_hbm.table, s32[256]{0:T(256)} %row_request.9, bf16[16,32,128]{2,1,0:T(8,128)(2,1)} %bitcast.4, f32[16,32,128]{2,1,0:T(8,128)} %get-tuple-element.41.rows_in, ...), custom_call_target="tpu_custom_call", output_to_operand_aliasing={{0}: (4, {})} | custom-call | flops 1073741824 | bytes 3145728 | tf_op jit(solution)/shard_map/settle_pages/pallas_call | solution.py:274
  129.5 0.8 copy-done.12
  130.3 4.8 %settle_pages.8 = (bf16[32,128,1024]{2,1,0:T(8,128)(2,1)}, f32[16,32,128]{2,1,0:T(8,128)}) custom-call(s32[256]{0:T(256)} %or_or_fusion.table_hbm.table, s32[256]{0:T(256)} %row_request.9, bf16[16,32,128]{2,1,0:T(8,128)(2,1)} %bitcast.5, f32[16,32,128]{2,1,0:T(8,128)} %get-tuple-element.46.rows_in, ...), custom_call_target="tpu_custom_call", output_to_operand_aliasing={{0}: (4, {})} | custom-call | flops 1073741824 | bytes 3145728 | tf_op jit(solution)/shard_map/settle_pages/pallas_call | solution.py:274
  135.1 33.9 %collective-permute-done.12.rest_0_ = bf16[2,128,1024]{2,1,0:T(8,128)(2,1)S(1)} collective-permute-done((bf16[2,128,1024]{2,1,0:T(8,128)(2,1)}, bf16[2,128,1024]{2,1,0:T(8,128)(2,1)S(1)}, u32[]{:S(2)}, u32[]{:S(2)}) %collective-permute-start.12) | collective-permute-done | bytes 524320 | tf_op jit(solution)/shard_map/ppermute | solution.py:57
  169.0 14.1 %collective-permute-done.13.rest_1_ = bf16[2,128,1024]{2,1,0:T(8,128)(2,1)S(1)} collective-permute-done((bf16[2,128,1024]{2,1,0:T(8,128)(2,1)}, bf16[2,128,1024]{2,1,0:T(8,128)(2,1)S(1)}, u32[]{:S(2)}, u32[]{:S(2)}) %collective-permute-start.13) | collective-permute-done | bytes 524320 | tf_op jit(solution)/shard_map/ppermute | solution.py:57
  183.1 13.2 %collective-permute-done.14.rest_2_ = bf16[2,128,1024]{2,1,0:T(8,128)(2,1)} collective-permute-done((bf16[2,128,1024]{2,1,0:T(8,128)(2,1)}, bf16[2,128,1024]{2,1,0:T(8,128)(2,1)}, u32[]{:S(2)}, u32[]{:S(2)}) %collective-permute-start.14) | collective-permute-done | bytes 524320 | tf_op jit(solution)/shard_map/ppermute | solution.py:57
  196.3 4.7 %settle_pages.9 = (bf16[32,128,1024]{2,1,0:T(8,128)(2,1)}, bf16[16,4096]{1,0:T(8,128)(2,1)}) custom-call(s32[256]{0:T(256)} %or_or_fusion.table_hbm.table, s32[256]{0:T(256)} %row_request.9, bf16[16,32,128]{2,1,0:T(8,128)(2,1)} %bitcast.6, f32[16,32,128]{2,1,0:T(8,128)} %get-tuple-element.51.rows_in, ...), custom_call_target="tpu_custom_call", output_to_operand_aliasing={{0}: (4, {})} | custom-call | flops 1073741824 | bytes 3145728 | tf_op jit(solution)/shard_map/settle_pages/pallas_call | solution.py:274
  201.1 0.8 collective-permute-start.17
  201.9 0.8 collective-permute-start.22
  202.7 0.8 collective-permute-start.15
  203.5 2.7 %collective-permute-done.18.rest_4_ = bf16[16,4096]{1,0:T(8,128)(2,1)S(1)} collective-permute-done((bf16[16,4096]{1,0:T(8,128)(2,1)}, bf16[16,4096]{1,0:T(8,128)(2,1)S(1)}, u32[]{:S(2)}, u32[]{:S(2)}) %collective-permute-start.18) | collective-permute-done | bytes 131104 | tf_op jit(solution)/shard_map/ppermute | solution.py:57
  206.3 0.5 collective-permute-start.25
  206.8 3.1 %collective-permute-start.21 = (bf16[16,4096]{1,0:T(8,128)(2,1)S(1)}, bf16[16,4096]{1,0:T(8,128)(2,1)S(1)}, u32[]{:S(2)}, u32[]{:S(2)}) collective-permute-start(bf16[16,4096]{1,0:T(8,128)(2,1)S(1)} %collective-permute-done.17.rest_3_), channel_id=1, source_target_pairs={{0,4},{2,6},{4,0},{6,2},{8,12},{10,14},{12,8},{14,10},{16,20},{18,... | collective-permute-start | bytes 393224 | tf_op jit(solution)/shard_map/ppermute | solution.py:57
  209.9 4.9 %collective-permute-done.16.rest_2_ = bf16[16,4096]{1,0:T(8,128)(2,1)S(1)} collective-permute-done((bf16[16,4096]{1,0:T(8,128)(2,1)}, bf16[16,4096]{1,0:T(8,128)(2,1)S(1)}, u32[]{:S(2)}, u32[]{:S(2)}) %collective-permute-start.16) | collective-permute-done | bytes 131104 | tf_op jit(solution)/shard_map/ppermute | solution.py:57
  214.8 1.0 collective-permute-start.20
  215.8 1.0 collective-permute-start.19
  216.9 0.5 collective-permute-start.23
  217.4 0.1 collective-permute-start.29
  217.4 3.7 %collective-permute-done.20.rest_6_ = bf16[16,4096]{1,0:T(8,128)(2,1)S(1)} collective-permute-done((bf16[16,4096]{1,0:T(8,128)(2,1)S(1)}, bf16[16,4096]{1,0:T(8,128)(2,1)S(1)}, u32[]{:S(2)}, u32[]{:S(2)}) %collective-permute-start.20) | collective-permute-done | bytes 131104 | tf_op jit(solution)/shard_map/ppermute | solution.py:57
  221.2 1.4 collective-permute-done.19.rest_5_
  222.7 1.3 collective-permute-done.27.rest_13_
  224.1 0.6 copy-done.28
  224.7 3.8 %project_rows.1 = (f32[128,512]{1,0:T(8,128)}, bf16[128,512]{1,0:T(8,128)(2,1)}) custom-call(bf16[4096,512]{1,0:T(8,128)(2,1)S(1)} %copy-done, bf16[16,4096]{1,0:T(8,128)(2,1)} %get-tuple-element.57.rest_0_, bf16[16,4096]{1,0:T(8,128)(2,1)} %copy-done.18, bf16[16,4096]{1,0:T(8,128)(2,1)} %copy-done.17, bf16[16,4096]{1,0:T(8,128)(2,1)} %copy-done.15, ...), custom_call_target="tpu_custom_call" | custom-call | flops 1073741824 | bytes 4194304 | tf_op jit(solution)/shard_map/project_rows/pallas_call | solution.py:329
  228.5 1.6 collective-permute-start.30
  230.1 4.3 %collective-permute-done.30 = bf16[128,512]{1,0:T(8,128)(2,1)S(1)} collective-permute-done((bf16[128,512]{1,0:T(8,128)(2,1)}, bf16[128,512]{1,0:T(8,128)(2,1)S(1)}, u32[]{:S(2)}, u32[]{:S(2)}) %collective-permute-start.30) | collective-permute-done | bytes 131104 | tf_op jit(solution)/shard_map/ppermute | solution.py:369
  234.4 1.6 add_convert_fusion
  (86 shorter events, 0.3 us)
Async XLA Ops:
  7.4 18.1 %collective-permute-start = (bf16[2,128,1024]{2,1,0:T(8,128)(2,1)}, bf16[2,128,1024]{2,1,0:T(8,128)(2,1)S(1)}, u32[]{:S(2)}, u32[]{:S(2)}) collective-permute-start(bf16[2,128,1024]{2,1,0:T(8,128)(2,1)} %get-tuple-element.33), channel_id=1, source_target_pairs={{0,8},{2,10},{4,12},{6,14},{8,16},{10,18},{12,20},{14,22},{16,24},... | collective-permute-start | bytes 1572872 | tf_op jit(solution)/shard_map/ppermute | solution.py:57
  10.4 24.6 %collective-permute-start.1 = (bf16[2,128,1024]{2,1,0:T(8,128)(2,1)}, bf16[2,128,1024]{2,1,0:T(8,128)(2,1)S(1)}, u32[]{:S(2)}, u32[]{:S(2)}) collective-permute-start(bf16[2,128,1024]{2,1,0:T(8,128)(2,1)} %get-tuple-element.34), channel_id=1, source_target_pairs={{0,10},{2,8},{4,14},{6,12},{8,18},{10,16},{12,22},{14,20},{16,26},... | collective-permute-start | bytes 1572872 | tf_op jit(solution)/shard_map/ppermute | solution.py:57
  11.2 27.0 %collective-permute-start.2 = (bf16[2,128,1024]{2,1,0:T(8,128)(2,1)}, bf16[2,128,1024]{2,1,0:T(8,128)(2,1)S(1)}, u32[]{:S(2)}, u32[]{:S(2)}) collective-permute-start(bf16[2,128,1024]{2,1,0:T(8,128)(2,1)} %get-tuple-element.35), channel_id=1, source_target_pairs={{0,2},{2,0},{4,6},{6,4},{8,10},{10,8},{12,14},{14,12},{16,18},{18,... | collective-permute-start | bytes 1572872 | tf_op jit(solution)/shard_map/ppermute | solution.py:57
  12.1 37.2 %collective-permute-start.3 = (bf16[2,128,1024]{2,1,0:T(8,128)(2,1)}, bf16[2,128,1024]{2,1,0:T(8,128)(2,1)S(1)}, u32[]{:S(2)}, u32[]{:S(2)}) collective-permute-start(bf16[2,128,1024]{2,1,0:T(8,128)(2,1)} %get-tuple-element.38), channel_id=1, source_target_pairs={{0,12},{2,14},{4,8},{6,10},{8,20},{10,22},{12,16},{14,18},{16,28},... | collective-permute-start | bytes 1572872 | tf_op jit(solution)/shard_map/ppermute | solution.py:57
  14.7 98.4 %copy-start.29 = (bf16[16,4096]{1,0:T(8,128)(2,1)S(1)}, bf16[16,4096]{1,0:T(8,128)(2,1)}, u32[]{:S(2)}) copy-start(bf16[16,4096]{1,0:T(8,128)(2,1)} %param.12) | copy-start | bytes 393220
  22.6 26.7 %collective-permute-start.4 = (bf16[2,128,1024]{2,1,0:T(8,128)(2,1)}, bf16[2,128,1024]{2,1,0:T(8,128)(2,1)S(1)}, u32[]{:S(2)}, u32[]{:S(2)}) collective-permute-start(bf16[2,128,1024]{2,1,0:T(8,128)(2,1)} %get-tuple-element.39), channel_id=1, source_target_pairs={{0,4},{2,6},{4,0},{6,2},{8,12},{10,14},{12,8},{14,10},{16,20},{18,... | collective-permute-start | bytes 1572872 | tf_op jit(solution)/shard_map/ppermute | solution.py:57
  25.4 89.1 %copy-start.1 = (bf16[2,128,1024]{2,1,0:T(8,128)(2,1)}, bf16[2,128,1024]{2,1,0:T(8,128)(2,1)S(1)}, u32[]{:S(2)}) copy-start(bf16[2,128,1024]{2,1,0:T(8,128)(2,1)S(1)} %collective-permute-done.rest_0_) | copy-start | bytes 1572868
  25.4 33.0 %collective-permute-start.5 = (bf16[2,128,1024]{2,1,0:T(8,128)(2,1)}, bf16[2,128,1024]{2,1,0:T(8,128)(2,1)S(1)}, u32[]{:S(2)}, u32[]{:S(2)}) collective-permute-start(bf16[2,128,1024]{2,1,0:T(8,128)(2,1)} %get-tuple-element.40), channel_id=1, source_target_pairs={{0,14},{2,12},{4,10},{6,8},{8,22},{10,20},{12,18},{14,16},{16,30},... | collective-permute-start | bytes 1572872 | tf_op jit(solution)/shard_map/ppermute | solution.py:57
  35.0 79.5 %copy-start.2 = (bf16[2,128,1024]{2,1,0:T(8,128)(2,1)}, bf16[2,128,1024]{2,1,0:T(8,128)(2,1)S(1)}, u32[]{:S(2)}) copy-start(bf16[2,128,1024]{2,1,0:T(8,128)(2,1)S(1)} %collective-permute-done.1.rest_1_) | copy-start | bytes 1572868
  35.0 65.1 %collective-permute-start.6 = (bf16[2,128,1024]{2,1,0:T(8,128)(2,1)}, bf16[2,128,1024]{2,1,0:T(8,128)(2,1)S(1)}, u32[]{:S(2)}, u32[]{:S(2)}) collective-permute-start(bf16[2,128,1024]{2,1,0:T(8,128)(2,1)} %get-tuple-element.43), channel_id=1, source_target_pairs={{0,6},{2,4},{4,2},{6,0},{8,14},{10,12},{12,10},{14,8},{16,22},{18,... | collective-permute-start | bytes 1572872 | tf_op jit(solution)/shard_map/ppermute | solution.py:57
  38.1 76.4 %copy-start.4 = (bf16[2,128,1024]{2,1,0:T(8,128)(2,1)}, bf16[2,128,1024]{2,1,0:T(8,128)(2,1)S(1)}, u32[]{:S(2)}) copy-start(bf16[2,128,1024]{2,1,0:T(8,128)(2,1)S(1)} %collective-permute-done.2.rest_2_) | copy-start | bytes 1572868
  38.1 62.0 %collective-permute-start.7 = (bf16[2,128,1024]{2,1,0:T(8,128)(2,1)}, bf16[2,128,1024]{2,1,0:T(8,128)(2,1)S(1)}, u32[]{:S(2)}, u32[]{:S(2)}) collective-permute-start(bf16[2,128,1024]{2,1,0:T(8,128)(2,1)} %get-tuple-element.44), channel_id=1, source_target_pairs={{0,24},{2,26},{4,28},{6,30},{8,0},{10,2},{12,4},{14,6},{16,8},{18,... | collective-permute-start | bytes 1572872 | tf_op jit(solution)/shard_map/ppermute | solution.py:57
  49.3 71.1 %copy-start.3 = (bf16[2,128,1024]{2,1,0:T(8,128)(2,1)}, bf16[2,128,1024]{2,1,0:T(8,128)(2,1)S(1)}, u32[]{:S(2)}) copy-start(bf16[2,128,1024]{2,1,0:T(8,128)(2,1)S(1)} %collective-permute-done.3.rest_0_) | copy-start | bytes 1572868
  49.3 50.9 %collective-permute-start.8 = (bf16[2,128,1024]{2,1,0:T(8,128)(2,1)}, bf16[2,128,1024]{2,1,0:T(8,128)(2,1)S(1)}, u32[]{:S(2)}, u32[]{:S(2)}) collective-permute-start(bf16[2,128,1024]{2,1,0:T(8,128)(2,1)} %get-tuple-element.45), channel_id=1, source_target_pairs={{0,26},{2,24},{4,30},{6,28},{8,2},{10,0},{12,6},{14,4},{16,10},{18... | collective-permute-start | bytes 1572872 | tf_op jit(solution)/shard_map/ppermute | solution.py:57
  49.3 71.1 %copy-start.5 = (bf16[2,128,1024]{2,1,0:T(8,128)(2,1)}, bf16[2,128,1024]{2,1,0:T(8,128)(2,1)S(1)}, u32[]{:S(2)}) copy-start(bf16[2,128,1024]{2,1,0:T(8,128)(2,1)S(1)} %collective-permute-done.4.rest_1_) | copy-start | bytes 1572868
  49.3 63.7 %collective-permute-start.9 = (bf16[2,128,1024]{2,1,0:T(8,128)(2,1)}, bf16[2,128,1024]{2,1,0:T(8,128)(2,1)S(1)}, u32[]{:S(2)}, u32[]{:S(2)}) collective-permute-start(bf16[2,128,1024]{2,1,0:T(8,128)(2,1)} %get-tuple-element.48), channel_id=1, source_target_pairs={{0,28},{2,30},{4,24},{6,26},{8,4},{10,6},{12,0},{14,2},{16,12},{18... | collective-permute-start | bytes 1572872 | tf_op jit(solution)/shard_map/ppermute | solution.py:57
  58.4 62.1 %copy-start.6 = (bf16[2,128,1024]{2,1,0:T(8,128)(2,1)}, bf16[2,128,1024]{2,1,0:T(8,128)(2,1)S(1)}, u32[]{:S(2)}) copy-start(bf16[2,128,1024]{2,1,0:T(8,128)(2,1)S(1)} %collective-permute-done.5.rest_2_) | copy-start | bytes 1572868
  58.4 71.1 %collective-permute-start.10 = (bf16[2,128,1024]{2,1,0:T(8,128)(2,1)}, bf16[2,128,1024]{2,1,0:T(8,128)(2,1)S(1)}, u32[]{:S(2)}, u32[]{:S(2)}) collective-permute-start(bf16[2,128,1024]{2,1,0:T(8,128)(2,1)} %get-tuple-element.49), channel_id=1, source_target_pairs={{0,30},{2,28},{4,26},{6,24},{8,6},{10,4},{12,2},{14,0},{16,14},{18... | collective-permute-start | bytes 1572872 | tf_op jit(solution)/shard_map/ppermute | solution.py:57
  100.1 24.8 %copy-start.7 = (bf16[2,128,1024]{2,1,0:T(8,128)(2,1)}, bf16[2,128,1024]{2,1,0:T(8,128)(2,1)S(1)}, u32[]{:S(2)}) copy-start(bf16[2,128,1024]{2,1,0:T(8,128)(2,1)S(1)} %collective-permute-done.6.rest_0_) | copy-start | bytes 1572868
  100.1 29.4 %collective-permute-start.11 = (bf16[2,128,1024]{2,1,0:T(8,128)(2,1)}, bf16[2,128,1024]{2,1,0:T(8,128)(2,1)}, u32[]{:S(2)}, u32[]{:S(2)}) collective-permute-start(bf16[2,128,1024]{2,1,0:T(8,128)(2,1)} %get-tuple-element.50), channel_id=1, source_target_pairs={{0,16},{2,18},{4,20},{6,22},{8,24},{10,26},{12,28},{14,30},{16,0},... | collective-permute-start | bytes 1572872 | tf_op jit(solution)/shard_map/ppermute | solution.py:57
  100.2 24.8 %copy-start.8 = (bf16[2,128,1024]{2,1,0:T(8,128)(2,1)}, bf16[2,128,1024]{2,1,0:T(8,128)(2,1)S(1)}, u32[]{:S(2)}) copy-start(bf16[2,128,1024]{2,1,0:T(8,128)(2,1)S(1)} %collective-permute-done.7.rest_1_) | copy-start | bytes 1572868
  100.2 68.8 %collective-permute-start.12 = (bf16[2,128,1024]{2,1,0:T(8,128)(2,1)}, bf16[2,128,1024]{2,1,0:T(8,128)(2,1)S(1)}, u32[]{:S(2)}, u32[]{:S(2)}) collective-permute-start(bf16[2,128,1024]{2,1,0:T(8,128)(2,1)} %get-tuple-element.53), channel_id=1, source_target_pairs={{0,18},{2,16},{4,22},{6,20},{8,26},{10,24},{12,30},{14,28},{16,2},... | collective-permute-start | bytes 1572872 | tf_op jit(solution)/shard_map/ppermute | solution.py:57
  100.3 24.7 %copy-start.11 = (bf16[2,128,1024]{2,1,0:T(8,128)(2,1)}, bf16[2,128,1024]{2,1,0:T(8,128)(2,1)S(1)}, u32[]{:S(2)}) copy-start(bf16[2,128,1024]{2,1,0:T(8,128)(2,1)S(1)} %collective-permute-done.8.rest_2_) | copy-start | bytes 1572868
  100.3 82.8 %collective-permute-start.13 = (bf16[2,128,1024]{2,1,0:T(8,128)(2,1)}, bf16[2,128,1024]{2,1,0:T(8,128)(2,1)S(1)}, u32[]{:S(2)}, u32[]{:S(2)}) collective-permute-start(bf16[2,128,1024]{2,1,0:T(8,128)(2,1)} %get-tuple-element.54), channel_id=1, source_target_pairs={{0,20},{2,22},{4,16},{6,18},{8,28},{10,30},{12,24},{14,26},{16,4},... | collective-permute-start | bytes 1572872 | tf_op jit(solution)/shard_map/ppermute | solution.py:57
  113.0 12.0 %copy-start.9 = (bf16[2,128,1024]{2,1,0:T(8,128)(2,1)}, bf16[2,128,1024]{2,1,0:T(8,128)(2,1)S(1)}, u32[]{:S(2)}) copy-start(bf16[2,128,1024]{2,1,0:T(8,128)(2,1)S(1)} %collective-permute-done.9.rest_0_) | copy-start | bytes 1572868
  113.0 83.3 %collective-permute-start.14 = (bf16[2,128,1024]{2,1,0:T(8,128)(2,1)}, bf16[2,128,1024]{2,1,0:T(8,128)(2,1)}, u32[]{:S(2)}, u32[]{:S(2)}) collective-permute-start(bf16[2,128,1024]{2,1,0:T(8,128)(2,1)} %get-tuple-element.55), channel_id=1, source_target_pairs={{0,22},{2,20},{4,18},{6,16},{8,30},{10,28},{12,26},{14,24},{16,6},... | collective-permute-start | bytes 1572872 | tf_op jit(solution)/shard_map/ppermute | solution.py:57
  130.3 94.4 %copy-start = (bf16[4096,512]{1,0:T(8,128)(2,1)S(1)}, bf16[4096,512]{1,0:T(8,128)(2,1)}, u32[]{:S(2)}) copy-start(bf16[4096,512]{1,0:T(8,128)(2,1)} %out_weight.1) | copy-start | bytes 12582916
  169.0 27.3 %copy-start.10 = (bf16[2,128,1024]{2,1,0:T(8,128)(2,1)}, bf16[2,128,1024]{2,1,0:T(8,128)(2,1)S(1)}, u32[]{:S(2)}) copy-start(bf16[2,128,1024]{2,1,0:T(8,128)(2,1)S(1)} %collective-permute-done.12.rest_0_) | copy-start | bytes 1572868
  183.1 13.2 %copy-start.13 = (bf16[2,128,1024]{2,1,0:T(8,128)(2,1)}, bf16[2,128,1024]{2,1,0:T(8,128)(2,1)S(1)}, u32[]{:S(2)}) copy-start(bf16[2,128,1024]{2,1,0:T(8,128)(2,1)S(1)} %collective-permute-done.13.rest_1_) | copy-start | bytes 1572868
  201.0 5.2 %collective-permute-start.18 = (bf16[16,4096]{1,0:T(8,128)(2,1)}, bf16[16,4096]{1,0:T(8,128)(2,1)S(1)}, u32[]{:S(2)}, u32[]{:S(2)}) collective-permute-start(bf16[16,4096]{1,0:T(8,128)(2,1)} %get-tuple-element.57.rest_0_), channel_id=1, source_target_pairs={{0,4},{2,6},{4,0},{6,2},{8,12},{10,14},{12,8},{14,10},{16,20},{18,... | collective-permute-start | bytes 393224 | tf_op jit(solution)/shard_map/ppermute | solution.py:57
  201.1 5.2 %collective-permute-start.17 = (bf16[16,4096]{1,0:T(8,128)(2,1)}, bf16[16,4096]{1,0:T(8,128)(2,1)S(1)}, u32[]{:S(2)}, u32[]{:S(2)}) collective-permute-start(bf16[16,4096]{1,0:T(8,128)(2,1)} %get-tuple-element.57.rest_0_), channel_id=1, source_target_pairs={{0,24},{2,26},{4,28},{6,30},{8,0},{10,2},{12,4},{14,6},{16,8},{18,... | collective-permute-start | bytes 393224 | tf_op jit(solution)/shard_map/ppermute | solution.py:57
  201.9 4.9 %collective-permute-start.22 = (bf16[16,4096]{1,0:T(8,128)(2,1)}, bf16[16,4096]{1,0:T(8,128)(2,1)S(1)}, u32[]{:S(2)}, u32[]{:S(2)}) collective-permute-start(bf16[16,4096]{1,0:T(8,128)(2,1)} %get-tuple-element.57.rest_0_), channel_id=1, source_target_pairs={{0,2},{2,0},{4,6},{6,4},{8,10},{10,8},{12,14},{14,12},{16,18},{18,... | collective-permute-start | bytes 393224 | tf_op jit(solution)/shard_map/ppermute | solution.py:57
  202.7 12.1 %collective-permute-start.16 = (bf16[16,4096]{1,0:T(8,128)(2,1)}, bf16[16,4096]{1,0:T(8,128)(2,1)S(1)}, u32[]{:S(2)}, u32[]{:S(2)}) collective-permute-start(bf16[16,4096]{1,0:T(8,128)(2,1)} %get-tuple-element.57.rest_0_), channel_id=1, source_target_pairs={{0,16},{2,18},{4,20},{6,22},{8,24},{10,26},{12,28},{14,30},{16,0},... | collective-permute-start | bytes 393224 | tf_op jit(solution)/shard_map/ppermute | solution.py:57
  202.7 13.1 %collective-permute-start.15 = (bf16[16,4096]{1,0:T(8,128)(2,1)}, bf16[16,4096]{1,0:T(8,128)(2,1)S(1)}, u32[]{:S(2)}, u32[]{:S(2)}) collective-permute-start(bf16[16,4096]{1,0:T(8,128)(2,1)} %get-tuple-element.57.rest_0_), channel_id=1, source_target_pairs={{0,8},{2,10},{4,12},{6,14},{8,16},{10,18},{12,20},{14,22},{16,24},... | collective-permute-start | bytes 393224 | tf_op jit(solution)/shard_map/ppermute | solution.py:57
  206.2 17.7 %copy-start.14 = (bf16[16,4096]{1,0:T(8,128)(2,1)}, bf16[16,4096]{1,0:T(8,128)(2,1)S(1)}, u32[]{:S(2)}) copy-start(bf16[16,4096]{1,0:T(8,128)(2,1)S(1)} %collective-permute-done.18.rest_4_) | copy-start | bytes 393220
  206.2 10.6 %collective-permute-start.26 = (bf16[16,4096]{1,0:T(8,128)(2,1)S(1)}, bf16[16,4096]{1,0:T(8,128)(2,1)S(1)}, u32[]{:S(2)}, u32[]{:S(2)}) collective-permute-start(bf16[16,4096]{1,0:T(8,128)(2,1)S(1)} %collective-permute-done.18.rest_4_), channel_id=1, source_target_pairs={{0,2},{2,0},{4,6},{6,4},{8,10},{10,8},{12,14},{14,12},{16,18},{18,... | collective-permute-start | bytes 393224 | tf_op jit(solution)/shard_map/ppermute | solution.py:57
  206.3 17.7 %copy-start.15 = (bf16[16,4096]{1,0:T(8,128)(2,1)}, bf16[16,4096]{1,0:T(8,128)(2,1)S(1)}, u32[]{:S(2)}) copy-start(bf16[16,4096]{1,0:T(8,128)(2,1)S(1)} %collective-permute-done.17.rest_3_) | copy-start | bytes 393220
  206.3 10.5 %collective-permute-start.25 = (bf16[16,4096]{1,0:T(8,128)(2,1)S(1)}, bf16[16,4096]{1,0:T(8,128)(2,1)S(1)}, u32[]{:S(2)}, u32[]{:S(2)}) collective-permute-start(bf16[16,4096]{1,0:T(8,128)(2,1)S(1)} %collective-permute-done.17.rest_3_), channel_id=1, source_target_pairs={{0,2},{2,0},{4,6},{6,4},{8,10},{10,8},{12,14},{14,12},{16,18},{18,... | collective-permute-start | bytes 393224 | tf_op jit(solution)/shard_map/ppermute | solution.py:57
  206.8 17.2 %copy-start.16 = (bf16[16,4096]{1,0:T(8,128)(2,1)}, bf16[16,4096]{1,0:T(8,128)(2,1)S(1)}, u32[]{:S(2)}) copy-start(bf16[16,4096]{1,0:T(8,128)(2,1)S(1)} %collective-permute-done.22.rest_8_) | copy-start | bytes 393220
  206.8 10.6 %collective-permute-start.21 = (bf16[16,4096]{1,0:T(8,128)(2,1)S(1)}, bf16[16,4096]{1,0:T(8,128)(2,1)S(1)}, u32[]{:S(2)}, u32[]{:S(2)}) collective-permute-start(bf16[16,4096]{1,0:T(8,128)(2,1)S(1)} %collective-permute-done.17.rest_3_), channel_id=1, source_target_pairs={{0,4},{2,6},{4,0},{6,2},{8,12},{10,14},{12,8},{14,10},{16,20},{18,... | collective-permute-start | bytes 393224 | tf_op jit(solution)/shard_map/ppermute | solution.py:57
  214.8 6.4 %collective-permute-start.20 = (bf16[16,4096]{1,0:T(8,128)(2,1)S(1)}, bf16[16,4096]{1,0:T(8,128)(2,1)S(1)}, u32[]{:S(2)}, u32[]{:S(2)}) collective-permute-start(bf16[16,4096]{1,0:T(8,128)(2,1)S(1)} %collective-permute-done.16.rest_2_), channel_id=1, source_target_pairs={{0,4},{2,6},{4,0},{6,2},{8,12},{10,14},{12,8},{14,10},{16,20},{18,... | collective-permute-start | bytes 393224 | tf_op jit(solution)/shard_map/ppermute | solution.py:57
  215.8 6.8 %collective-permute-start.19 = (bf16[16,4096]{1,0:T(8,128)(2,1)S(1)}, bf16[16,4096]{1,0:T(8,128)(2,1)S(1)}, u32[]{:S(2)}, u32[]{:S(2)}) collective-permute-start(bf16[16,4096]{1,0:T(8,128)(2,1)S(1)} %collective-permute-done.15.rest_1_), channel_id=1, source_target_pairs={{0,4},{2,6},{4,0},{6,2},{8,12},{10,14},{12,8},{14,10},{16,20},{18,... | collective-permute-start | bytes 393224 | tf_op jit(solution)/shard_map/ppermute | solution.py:57
  216.8 5.8 %collective-permute-start.24 = (bf16[16,4096]{1,0:T(8,128)(2,1)S(1)}, bf16[16,4096]{1,0:T(8,128)(2,1)S(1)}, u32[]{:S(2)}, u32[]{:S(2)}) collective-permute-start(bf16[16,4096]{1,0:T(8,128)(2,1)S(1)} %collective-permute-done.16.rest_2_), channel_id=1, source_target_pairs={{0,2},{2,0},{4,6},{6,4},{8,10},{10,8},{12,14},{14,12},{16,18},{18,... | collective-permute-start | bytes 393224 | tf_op jit(solution)/shard_map/ppermute | solution.py:57
  216.9 5.8 %collective-permute-start.23 = (bf16[16,4096]{1,0:T(8,128)(2,1)S(1)}, bf16[16,4096]{1,0:T(8,128)(2,1)S(1)}, u32[]{:S(2)}, u32[]{:S(2)}) collective-permute-start(bf16[16,4096]{1,0:T(8,128)(2,1)S(1)} %collective-permute-done.15.rest_1_), channel_id=1, source_target_pairs={{0,2},{2,0},{4,6},{6,4},{8,10},{10,8},{12,14},{14,12},{16,18},{18,... | collective-permute-start | bytes 393224 | tf_op jit(solution)/shard_map/ppermute | solution.py:57
  217.4 5.3 %collective-permute-start.29 = (bf16[16,4096]{1,0:T(8,128)(2,1)S(1)}, bf16[16,4096]{1,0:T(8,128)(2,1)S(1)}, u32[]{:S(2)}, u32[]{:S(2)}) collective-permute-start(bf16[16,4096]{1,0:T(8,128)(2,1)S(1)} %collective-permute-done.21.rest_7_), channel_id=1, source_target_pairs={{0,2},{2,0},{4,6},{6,4},{8,10},{10,8},{12,14},{14,12},{16,18},{18,... | collective-permute-start | bytes 393224 | tf_op jit(solution)/shard_map/ppermute | solution.py:57
  221.2 1.5 collective-permute-start.28
  222.6 1.3 collective-permute-start.27
  228.5 5.8 %collective-permute-start.30 = (bf16[128,512]{1,0:T(8,128)(2,1)}, bf16[128,512]{1,0:T(8,128)(2,1)S(1)}, u32[]{:S(2)}, u32[]{:S(2)}) collective-permute-start(bf16[128,512]{1,0:T(8,128)(2,1)} %get-tuple-element.59), channel_id=1, source_target_pairs={{0,1},{1,0},{2,3},{3,2},{4,5},{5,4},{6,7},{7,6},{8,9},{9,8},{10,11... | collective-permute-start | bytes 393224 | tf_op jit(solution)/shard_map/ppermute | solution.py:369
  (13 other events, 49.6 us)

commit v10 on v9

--- a/solution.py
+++ b/solution.py
@@ -13,7 +13,7 @@
 WAVE = 3
 ROW_UNROLL = 4
 EARLY = 4
-VMEM_LIMIT = 57 * 1024 * 1024
+VMEM_LIMIT = 20 * 1024 * 1024
 
 
 def factors(groups):
@@ -352,6 +352,7 @@
     dims = factors(lax.axis_size("group"))
     routes = page_rounds(dims)
     table = packed(lengths, prefill_of, decode_of, math.prod(dims))
+    kv_pool = pltpu.with_memory_space_constraint(kv_pool, pltpu.HBM)
     received, *early = prepare(dims, routes[:EARLY], table, kv_pool)
     received, *late = prepare(dims, routes[EARLY:], table, kv_pool, received)
     arrived = [send_by(block, route, dims) for block, route in zip(early + late, routes)]

time: 238 us -> 236 us (level)
  Pallas kernels: 41.6 us -> 26.8 us
  starting transfers between devices: 79.2 us -> 88.6 us
  waiting for transfers between devices: 108 us -> 117 us
  local copies, waits for them, and re-layouts: 2.99 us -> 0.05 us
    pallas_call x5, Pallas kernels: 24.4 us -> 12.1 us  [settle(): pl.pallas_call(functools.partial(settle_kernel, dims, routes, own, last),...]
    ppermute x30, starting transfers between devices: 77.6 us -> 87.1 us  [send_by(): return lax.ppermute(array, 'group', pairs)]
    ppermute x30, waiting for transfers between devices: 104 us -> 113 us  [send_by(): return lax.ppermute(array, 'group', pairs)]
    pallas_call x2, Pallas kernels: 13.4 us -> 10.3 us  [prepare(): pl.pallas_call(functools.partial(prepare_kernel, dims, routes, own), out_...]
  transfers between devices with their start and end apart: 31 -> 31, of which waited for: 14 -> 14; matrix products, arithmetic and copies ran while one was open for 1% -> 0% of each run, Pallas kernels for 12% -> 6%
where the time goes in v10:
time: 236 us; the launch traced here: 235 us
  waiting for transfers between devices  117 us (50%)
  starting transfers between devices  88.6 us (38%)
  Pallas kernels  26.8 us (11%)
    ppermute x30, waiting for transfers between devices, send_by(): return lax.ppermute(array, 'group', pairs)  113 us
    ppermute x30, starting transfers between devices, send_by(): return lax.ppermute(array, 'group', pairs)  87.1 us
    pallas_call x5, Pallas kernels, settle(): pl.pallas_call(functools.partial(settle_kernel, dims, routes, own, last),...  12.1 us
    pallas_call x2, Pallas kernels, prepare(): pl.pallas_call(functools.partial(prepare_kernel, dims, routes, own), out_...  10.3 us
  transfers between devices with their start and end apart: 31, of which 14 were waited for; matrix products, arithmetic and copies ran while one was open for 0% of the time, Pallas kernels for 6%

profile of v10, /device:TPU:0, one launch (start us, length us, event | category | flops | bytes accessed | tf_op | source)
XLA Modules:
  0.0 234.9 jit_solution(12503017420100024135)
XLA Ops:
  0.6 0.7 or_or_fusion.table_hbm.table
  1.3 5.1 %outgoing_pages.2 = (bf16[32,128,1024]{2,1,0:T(8,128)(2,1)}, bf16[2,128,1024]{2,1,0:T(8,128)(2,1)S(1)}, bf16[2,128,1024]{2,1,0:T(8,128)(2,1)S(1)}, bf16[2,128,10...) custom-call(s32[256]{0:T(256)S(1)} %or_or_fusion.table_hbm.table, bf16[32,128,1024]{2,1,0:T(8,128)(2,1)} %pool.3), custom_call_target="tpu_custom_call" | custom-call | bytes 5242880 | tf_op jit(solution)/shard_map/outgoing_pages/pallas_call | solution.py:154
  6.5 3.2 %collective-permute-start = (bf16[2,128,1024]{2,1,0:T(8,128)(2,1)S(1)}, bf16[2,128,1024]{2,1,0:T(8,128)(2,1)S(1)}, u32[]{:S(2)}, u32[]{:S(2)}) collective-permute-start(bf16[2,128,1024]{2,1,0:T(8,128)(2,1)S(1)} %get-tuple-element.33), channel_id=1, source_target_pairs={{0,8},{2,10},{4,12},{6,14},{8,16},{10,18},{12,20},{14,22},{16,24},... | collective-permute-start | bytes 1572872 | tf_op jit(solution)/shard_map/ppermute | solution.py:57
  9.7 0.5 collective-permute-start.1
  10.2 1.0 collective-permute-start.2
  11.2 2.5 %collective-permute-start.3 = (bf16[2,128,1024]{2,1,0:T(8,128)(2,1)S(1)}, bf16[2,128,1024]{2,1,0:T(8,128)(2,1)S(1)}, u32[]{:S(2)}, u32[]{:S(2)}) collective-permute-start(bf16[2,128,1024]{2,1,0:T(8,128)(2,1)S(1)} %get-tuple-element.38), channel_id=1, source_target_pairs={{0,12},{2,14},{4,8},{6,10},{8,20},{10,22},{12,16},{14,18},{16,28},... | collective-permute-start | bytes 1572872 | tf_op jit(solution)/shard_map/ppermute | solution.py:57
  13.7 5.2 %outgoing_pages.3 = (bf16[32,128,1024]{2,1,0:T(8,128)(2,1)}, bf16[2,128,1024]{2,1,0:T(8,128)(2,1)S(1)}, bf16[2,128,1024]{2,1,0:T(8,128)(2,1)S(1)}, bf16[2,128,10...) custom-call(s32[256]{0:T(256)S(1)} %or_or_fusion.table_hbm.table, ...), custom_call_target="tpu_custom_call", output_to_operand_aliasing={{0}: (2, {})} | custom-call | bytes 11534336 | tf_op jit(solution)/shard_map/outgoing_pages/pallas_call | solution.py:154
  18.9 0.7 collective-permute-start.4
  19.6 4.8 %collective-permute-done.rest_0_ = bf16[2,128,1024]{2,1,0:T(8,128)(2,1)S(1)} collective-permute-done((bf16[2,128,1024]{2,1,0:T(8,128)(2,1)S(1)}, bf16[2,128,1024]{2,1,0:T(8,128)(2,1)S(1)}, u32[]{:S(2)}, u32[]{:S(2)}) %collective-permute-start) | collective-permute-done | bytes 524320 | tf_op jit(solution)/shard_map/ppermute | solution.py:57
  24.3 0.0 collective-permute-start.5
  24.3 9.7 %collective-permute-done.1.rest_1_ = bf16[2,128,1024]{2,1,0:T(8,128)(2,1)S(1)} collective-permute-done((bf16[2,128,1024]{2,1,0:T(8,128)(2,1)S(1)}, bf16[2,128,1024]{2,1,0:T(8,128)(2,1)S(1)}, u32[]{:S(2)}, u32[]{:S(2)}) %collective-permute-start.1) | collective-permute-done | bytes 524320 | tf_op jit(solution)/shard_map/ppermute | solution.py:57
  34.1 3.0 %collective-permute-start.6 = (bf16[2,128,1024]{2,1,0:T(8,128)(2,1)S(1)}, bf16[2,128,1024]{2,1,0:T(8,128)(2,1)S(1)}, u32[]{:S(2)}, u32[]{:S(2)}) collective-permute-start(bf16[2,128,1024]{2,1,0:T(8,128)(2,1)S(1)} %get-tuple-element.43), channel_id=1, source_target_pairs={{0,6},{2,4},{4,2},{6,0},{8,14},{10,12},{12,10},{14,8},{16,22},{18,... | collective-permute-start | bytes 1572872 | tf_op jit(solution)/shard_map/ppermute | solution.py:57
  37.1 0.0 collective-permute-done.2.rest_2_
  37.1 1.4 collective-permute-start.7
  38.5 9.7 %collective-permute-done.3.rest_0_ = bf16[2,128,1024]{2,1,0:T(8,128)(2,1)S(1)} collective-permute-done((bf16[2,128,1024]{2,1,0:T(8,128)(2,1)S(1)}, bf16[2,128,1024]{2,1,0:T(8,128)(2,1)S(1)}, u32[]{:S(2)}, u32[]{:S(2)}) %collective-permute-start.3) | collective-permute-done | bytes 524320 | tf_op jit(solution)/shard_map/ppermute | solution.py:57
  48.3 1.6 collective-permute-start.9
  49.9 7.5 %collective-permute-done.5.rest_2_ = bf16[2,128,1024]{2,1,0:T(8,128)(2,1)S(1)} collective-permute-done((bf16[2,128,1024]{2,1,0:T(8,128)(2,1)S(1)}, bf16[2,128,1024]{2,1,0:T(8,128)(2,1)S(1)}, u32[]{:S(2)}, u32[]{:S(2)}) %collective-permute-start.5) | collective-permute-done | bytes 524320 | tf_op jit(solution)/shard_map/ppermute | solution.py:57
  57.4 51.6 %collective-permute-start.10 = (bf16[2,128,1024]{2,1,0:T(8,128)(2,1)S(1)}, bf16[2,128,1024]{2,1,0:T(8,128)(2,1)S(1)}, u32[]{:S(2)}, u32[]{:S(2)}) collective-permute-start(bf16[2,128,1024]{2,1,0:T(8,128)(2,1)S(1)} %get-tuple-element.49), channel_id=1, source_target_pairs={{0,30},{2,28},{4,26},{6,24},{8,6},{10,4},{12,2},{14,0},{16,14},{18... | collective-permute-start | bytes 1572872 | tf_op jit(solution)/shard_map/ppermute | solution.py:57
  108.9 0.1 collective-permute-start.12
  109.0 0.1 collective-permute-start.13
  109.1 6.0 %collective-permute-start.14 = (bf16[2,128,1024]{2,1,0:T(8,128)(2,1)S(1)}, bf16[2,128,1024]{2,1,0:T(8,128)(2,1)S(1)}, u32[]{:S(2)}, u32[]{:S(2)}) collective-permute-start(bf16[2,128,1024]{2,1,0:T(8,128)(2,1)S(1)} %get-tuple-element.55), channel_id=1, source_target_pairs={{0,22},{2,20},{4,18},{6,16},{8,30},{10,28},{12,26},{14,24},{16,6},... | collective-permute-start | bytes 1572872 | tf_op jit(solution)/shard_map/ppermute | solution.py:57
  115.2 3.1 %settle_pages.5 = (bf16[32,128,1024]{2,1,0:T(8,128)(2,1)}, f32[16,32,128]{2,1,0:T(8,128)S(1)}) custom-call(s32[256]{0:T(256)S(1)} %or_or_fusion.table_hbm.table, s32[256]{0:T(256)S(1)} %copy-done.1, bf16[16,32,128]{2,1,0:T(8,128)(2,1)S(1)} %bitcast.2, f32[16,32,128]{2,1,0:T(8,128)S(1)} %broadcast_in_dim.3.rows_in, ...), custom_call_target="tpu_custom_call", output_to_operand_aliasing={{0}: (4, {})} | custom-call | flops 1073741824 | bytes 3145728 | tf_op jit(solution)/shard_map/settle_pages/pallas_call | solution.py:274
  118.3 2.2 settle_pages.6
  120.5 2.2 settle_pages.7
  122.7 45.4 %collective-permute-done.11.rest_2_ = bf16[2,128,1024]{2,1,0:T(8,128)(2,1)S(1)} collective-permute-done((bf16[2,128,1024]{2,1,0:T(8,128)(2,1)S(1)}, bf16[2,128,1024]{2,1,0:T(8,128)(2,1)S(1)}, u32[]{:S(2)}, u32[]{:S(2)}) %collective-permute-start.11) | collective-permute-done | bytes 524320 | tf_op jit(solution)/shard_map/ppermute | solution.py:57
  168.2 2.2 settle_pages.8
  170.4 5.4 %collective-permute-done.12.rest_0_ = bf16[2,128,1024]{2,1,0:T(8,128)(2,1)S(1)} collective-permute-done((bf16[2,128,1024]{2,1,0:T(8,128)(2,1)S(1)}, bf16[2,128,1024]{2,1,0:T(8,128)(2,1)S(1)}, u32[]{:S(2)}, u32[]{:S(2)}) %collective-permute-start.12) | collective-permute-done | bytes 524320 | tf_op jit(solution)/shard_map/ppermute | solution.py:57
  175.7 7.2 %collective-permute-done.13.rest_1_ = bf16[2,128,1024]{2,1,0:T(8,128)(2,1)S(1)} collective-permute-done((bf16[2,128,1024]{2,1,0:T(8,128)(2,1)S(1)}, bf16[2,128,1024]{2,1,0:T(8,128)(2,1)S(1)}, u32[]{:S(2)}, u32[]{:S(2)}) %collective-permute-start.13) | collective-permute-done | bytes 524320 | tf_op jit(solution)/shard_map/ppermute | solution.py:57
  183.0 8.9 %collective-permute-done.14.rest_2_ = bf16[2,128,1024]{2,1,0:T(8,128)(2,1)S(1)} collective-permute-done((bf16[2,128,1024]{2,1,0:T(8,128)(2,1)S(1)}, bf16[2,128,1024]{2,1,0:T(8,128)(2,1)S(1)}, u32[]{:S(2)}, u32[]{:S(2)}) %collective-permute-start.14) | collective-permute-done | bytes 524320 | tf_op jit(solution)/shard_map/ppermute | solution.py:57
  191.9 2.4 %settle_pages.9 = (bf16[32,128,1024]{2,1,0:T(8,128)(2,1)}, bf16[16,4096]{1,0:T(8,128)(2,1)S(1)}) custom-call(s32[256]{0:T(256)S(1)} %or_or_fusion.table_hbm.table, s32[256]{0:T(256)S(1)} %copy-done.1, bf16[16,32,128]{2,1,0:T(8,128)(2,1)S(1)} %bitcast.6, f32[16,32,128]{2,1,0:T(8,128)S(1)} %get-tuple-element.51.rows_in, ...), custom_call_target="tpu_custom_call", output_to_operand_aliasing={{0}: (4, {})} | custom-call | flops 1073741824 | bytes 3145728 | tf_op jit(solution)/shard_map/settle_pages/pallas_call | solution.py:274
  194.3 7.4 %collective-permute-start.18 = (bf16[16,4096]{1,0:T(8,128)(2,1)S(1)}, bf16[16,4096]{1,0:T(8,128)(2,1)S(1)}, u32[]{:S(2)}, u32[]{:S(2)}) collective-permute-start(bf16[16,4096]{1,0:T(8,128)(2,1)S(1)} %get-tuple-element.57.rest_0_), channel_id=1, source_target_pairs={{0,4},{2,6},{4,0},{6,2},{8,12},{10,14},{12,8},{14,10},{16,20},{18,... | collective-permute-start | bytes 393224 | tf_op jit(solution)/shard_map/ppermute | solution.py:57
  201.7 1.8 collective-permute-start.22
  203.6 1.7 collective-permute-start.15
  205.3 0.9 collective-permute-start.26
  206.2 2.3 collective-permute-done.17.rest_3_
  208.5 1.0 collective-permute-start.25
  209.4 6.1 %collective-permute-done.16.rest_2_ = bf16[16,4096]{1,0:T(8,128)(2,1)S(1)} collective-permute-done((bf16[16,4096]{1,0:T(8,128)(2,1)S(1)}, bf16[16,4096]{1,0:T(8,128)(2,1)S(1)}, u32[]{:S(2)}, u32[]{:S(2)}) %collective-permute-start.16) | collective-permute-done | bytes 131104 | tf_op jit(solution)/shard_map/ppermute | solution.py:57
  215.5 0.5 collective-permute-start.20
  216.0 1.5 collective-permute-start.19
  217.6 0.5 collective-permute-start.23
  218.1 0.1 collective-permute-start.29
  218.1 3.3 %collective-permute-done.20.rest_6_ = bf16[16,4096]{1,0:T(8,128)(2,1)S(1)} collective-permute-done((bf16[16,4096]{1,0:T(8,128)(2,1)S(1)}, bf16[16,4096]{1,0:T(8,128)(2,1)S(1)}, u32[]{:S(2)}, u32[]{:S(2)}) %collective-permute-start.20) | collective-permute-done | bytes 131104 | tf_op jit(solution)/shard_map/ppermute | solution.py:57
  221.5 1.4 collective-permute-done.19.rest_5_
  222.9 1.3 collective-permute-done.27.rest_13_
  224.2 4.3 %project_rows.1 = (f32[128,512]{1,0:T(8,128)S(1)}, bf16[128,512]{1,0:T(8,128)(2,1)S(1)}) custom-call(bf16[4096,512]{1,0:T(8,128)(2,1)S(1)} %copy-done, bf16[16,4096]{1,0:T(8,128)(2,1)S(1)} %get-tuple-element.57.rest_0_, bf16[16,4096]{1,0:T(8,128)(2,1)S(1)} %collective-permute-done.15.rest_1_, bf16[16,4096]{1,0:T(8,128)(2,1)S(1)} %collective-permute-done.16.rest_2_, ...), custom_call_target="tpu_custom_call" | custom-call | flops 1073741824 | bytes 4194304 | tf_op jit(solution)/shard_map/project_rows/pallas_call | solution.py:329
  228.6 1.6 collective-permute-start.30
  230.1 4.1 %collective-permute-done.30 = bf16[128,512]{1,0:T(8,128)(2,1)S(1)} collective-permute-done((bf16[128,512]{1,0:T(8,128)(2,1)S(1)}, bf16[128,512]{1,0:T(8,128)(2,1)S(1)}, u32[]{:S(2)}, u32[]{:S(2)}) %collective-permute-start.30) | collective-permute-done | bytes 131104 | tf_op jit(solution)/shard_map/ppermute | solution.py:370
  234.2 0.7 add_convert_fusion
  (32 shorter events, 0.1 us)
Async XLA Ops:
  6.5 17.8 %collective-permute-start = (bf16[2,128,1024]{2,1,0:T(8,128)(2,1)S(1)}, bf16[2,128,1024]{2,1,0:T(8,128)(2,1)S(1)}, u32[]{:S(2)}, u32[]{:S(2)}) collective-permute-start(bf16[2,128,1024]{2,1,0:T(8,128)(2,1)S(1)} %get-tuple-element.33), channel_id=1, source_target_pairs={{0,8},{2,10},{4,12},{6,14},{8,16},{10,18},{12,20},{14,22},{16,24},... | collective-permute-start | bytes 1572872 | tf_op jit(solution)/shard_map/ppermute | solution.py:57
  9.7 24.3 %collective-permute-start.1 = (bf16[2,128,1024]{2,1,0:T(8,128)(2,1)S(1)}, bf16[2,128,1024]{2,1,0:T(8,128)(2,1)S(1)}, u32[]{:S(2)}, u32[]{:S(2)}) collective-permute-start(bf16[2,128,1024]{2,1,0:T(8,128)(2,1)S(1)} %get-tuple-element.34), channel_id=1, source_target_pairs={{0,10},{2,8},{4,14},{6,12},{8,18},{10,16},{12,22},{14,20},{16,26},... | collective-permute-start | bytes 1572872 | tf_op jit(solution)/shard_map/ppermute | solution.py:57
  10.2 26.8 %collective-permute-start.2 = (bf16[2,128,1024]{2,1,0:T(8,128)(2,1)S(1)}, bf16[2,128,1024]{2,1,0:T(8,128)(2,1)S(1)}, u32[]{:S(2)}, u32[]{:S(2)}) collective-permute-start(bf16[2,128,1024]{2,1,0:T(8,128)(2,1)S(1)} %get-tuple-element.35), channel_id=1, source_target_pairs={{0,2},{2,0},{4,6},{6,4},{8,10},{10,8},{12,14},{14,12},{16,18},{18,... | collective-permute-start | bytes 1572872 | tf_op jit(solution)/shard_map/ppermute | solution.py:57
  11.2 37.0 %collective-permute-start.3 = (bf16[2,128,1024]{2,1,0:T(8,128)(2,1)S(1)}, bf16[2,128,1024]{2,1,0:T(8,128)(2,1)S(1)}, u32[]{:S(2)}, u32[]{:S(2)}) collective-permute-start(bf16[2,128,1024]{2,1,0:T(8,128)(2,1)S(1)} %get-tuple-element.38), channel_id=1, source_target_pairs={{0,12},{2,14},{4,8},{6,10},{8,20},{10,22},{12,16},{14,18},{16,28},... | collective-permute-start | bytes 1572872 | tf_op jit(solution)/shard_map/ppermute | solution.py:57
  13.7 101.4 %copy-start.2 = (bf16[16,4096]{1,0:T(8,128)(2,1)S(1)}, bf16[16,4096]{1,0:T(8,128)(2,1)}, u32[]{:S(2)}) copy-start(bf16[16,4096]{1,0:T(8,128)(2,1)} %param.12) | copy-start | bytes 393220
  13.7 101.5 %copy-start.1 = (s32[256]{0:T(256)S(1)}, s32[256]{0:T(256)}, u32[]{:S(2)}) copy-start(s32[256]{0:T(256)} %row_request.9) | copy-start | bytes 3076
  18.9 29.4 %collective-permute-start.4 = (bf16[2,128,1024]{2,1,0:T(8,128)(2,1)S(1)}, bf16[2,128,1024]{2,1,0:T(8,128)(2,1)S(1)}, u32[]{:S(2)}, u32[]{:S(2)}) collective-permute-start(bf16[2,128,1024]{2,1,0:T(8,128)(2,1)S(1)} %get-tuple-element.39), channel_id=1, source_target_pairs={{0,4},{2,6},{4,0},{6,2},{8,12},{10,14},{12,8},{14,10},{16,20},{18,... | collective-permute-start | bytes 1572872 | tf_op jit(solution)/shard_map/ppermute | solution.py:57
  24.3 33.0 %collective-permute-start.5 = (bf16[2,128,1024]{2,1,0:T(8,128)(2,1)S(1)}, bf16[2,128,1024]{2,1,0:T(8,128)(2,1)S(1)}, u32[]{:S(2)}, u32[]{:S(2)}) collective-permute-start(bf16[2,128,1024]{2,1,0:T(8,128)(2,1)S(1)} %get-tuple-element.40), channel_id=1, source_target_pairs={{0,14},{2,12},{4,10},{6,8},{8,22},{10,20},{12,18},{14,16},{16,30},... | collective-permute-start | bytes 1572872 | tf_op jit(solution)/shard_map/ppermute | solution.py:57
  34.1 74.9 %collective-permute-start.6 = (bf16[2,128,1024]{2,1,0:T(8,128)(2,1)S(1)}, bf16[2,128,1024]{2,1,0:T(8,128)(2,1)S(1)}, u32[]{:S(2)}, u32[]{:S(2)}) collective-permute-start(bf16[2,128,1024]{2,1,0:T(8,128)(2,1)S(1)} %get-tuple-element.43), channel_id=1, source_target_pairs={{0,6},{2,4},{4,2},{6,0},{8,14},{10,12},{12,10},{14,8},{16,22},{18,... | collective-permute-start | bytes 1572872 | tf_op jit(solution)/shard_map/ppermute | solution.py:57
  37.1 71.9 %collective-permute-start.7 = (bf16[2,128,1024]{2,1,0:T(8,128)(2,1)S(1)}, bf16[2,128,1024]{2,1,0:T(8,128)(2,1)S(1)}, u32[]{:S(2)}, u32[]{:S(2)}) collective-permute-start(bf16[2,128,1024]{2,1,0:T(8,128)(2,1)S(1)} %get-tuple-element.44), channel_id=1, source_target_pairs={{0,24},{2,26},{4,28},{6,30},{8,0},{10,2},{12,4},{14,6},{16,8},{18,... | collective-permute-start | bytes 1572872 | tf_op jit(solution)/shard_map/ppermute | solution.py:57
  48.3 60.8 %collective-permute-start.8 = (bf16[2,128,1024]{2,1,0:T(8,128)(2,1)S(1)}, bf16[2,128,1024]{2,1,0:T(8,128)(2,1)S(1)}, u32[]{:S(2)}, u32[]{:S(2)}) collective-permute-start(bf16[2,128,1024]{2,1,0:T(8,128)(2,1)S(1)} %get-tuple-element.45), channel_id=1, source_target_pairs={{0,26},{2,24},{4,30},{6,28},{8,2},{10,0},{12,6},{14,4},{16,10},{18... | collective-permute-start | bytes 1572872 | tf_op jit(solution)/shard_map/ppermute | solution.py:57
  48.3 60.8 %collective-permute-start.9 = (bf16[2,128,1024]{2,1,0:T(8,128)(2,1)S(1)}, bf16[2,128,1024]{2,1,0:T(8,128)(2,1)S(1)}, u32[]{:S(2)}, u32[]{:S(2)}) collective-permute-start(bf16[2,128,1024]{2,1,0:T(8,128)(2,1)S(1)} %get-tuple-element.48), channel_id=1, source_target_pairs={{0,28},{2,30},{4,24},{6,26},{8,4},{10,6},{12,0},{14,2},{16,12},{18... | collective-permute-start | bytes 1572872 | tf_op jit(solution)/shard_map/ppermute | solution.py:57
  57.4 65.4 %collective-permute-start.10 = (bf16[2,128,1024]{2,1,0:T(8,128)(2,1)S(1)}, bf16[2,128,1024]{2,1,0:T(8,128)(2,1)S(1)}, u32[]{:S(2)}, u32[]{:S(2)}) collective-permute-start(bf16[2,128,1024]{2,1,0:T(8,128)(2,1)S(1)} %get-tuple-element.49), channel_id=1, source_target_pairs={{0,30},{2,28},{4,26},{6,24},{8,6},{10,4},{12,2},{14,0},{16,14},{18... | collective-permute-start | bytes 1572872 | tf_op jit(solution)/shard_map/ppermute | solution.py:57
  108.9 59.2 %collective-permute-start.11 = (bf16[2,128,1024]{2,1,0:T(8,128)(2,1)S(1)}, bf16[2,128,1024]{2,1,0:T(8,128)(2,1)S(1)}, u32[]{:S(2)}, u32[]{:S(2)}) collective-permute-start(bf16[2,128,1024]{2,1,0:T(8,128)(2,1)S(1)} %get-tuple-element.50), channel_id=1, source_target_pairs={{0,16},{2,18},{4,20},{6,22},{8,24},{10,26},{12,28},{14,30},{16,0},... | collective-permute-start | bytes 1572872 | tf_op jit(solution)/shard_map/ppermute | solution.py:57
  108.9 66.8 %collective-permute-start.12 = (bf16[2,128,1024]{2,1,0:T(8,128)(2,1)S(1)}, bf16[2,128,1024]{2,1,0:T(8,128)(2,1)S(1)}, u32[]{:S(2)}, u32[]{:S(2)}) collective-permute-start(bf16[2,128,1024]{2,1,0:T(8,128)(2,1)S(1)} %get-tuple-element.53), channel_id=1, source_target_pairs={{0,18},{2,16},{4,22},{6,20},{8,26},{10,24},{12,30},{14,28},{16,2},... | collective-permute-start | bytes 1572872 | tf_op jit(solution)/shard_map/ppermute | solution.py:57
  109.0 74.0 %collective-permute-start.13 = (bf16[2,128,1024]{2,1,0:T(8,128)(2,1)S(1)}, bf16[2,128,1024]{2,1,0:T(8,128)(2,1)S(1)}, u32[]{:S(2)}, u32[]{:S(2)}) collective-permute-start(bf16[2,128,1024]{2,1,0:T(8,128)(2,1)S(1)} %get-tuple-element.54), channel_id=1, source_target_pairs={{0,20},{2,22},{4,16},{6,18},{8,28},{10,30},{12,24},{14,26},{16,4},... | collective-permute-start | bytes 1572872 | tf_op jit(solution)/shard_map/ppermute | solution.py:57
  109.1 82.8 %collective-permute-start.14 = (bf16[2,128,1024]{2,1,0:T(8,128)(2,1)S(1)}, bf16[2,128,1024]{2,1,0:T(8,128)(2,1)S(1)}, u32[]{:S(2)}, u32[]{:S(2)}) collective-permute-start(bf16[2,128,1024]{2,1,0:T(8,128)(2,1)S(1)} %get-tuple-element.55), channel_id=1, source_target_pairs={{0,22},{2,20},{4,18},{6,16},{8,30},{10,28},{12,26},{14,24},{16,6},... | collective-permute-start | bytes 1572872 | tf_op jit(solution)/shard_map/ppermute | solution.py:57
  168.2 56.1 %copy-start = (bf16[4096,512]{1,0:T(8,128)(2,1)S(1)}, bf16[4096,512]{1,0:T(8,128)(2,1)}, u32[]{:S(2)}) copy-start(bf16[4096,512]{1,0:T(8,128)(2,1)} %out_weight.1) | copy-start | bytes 12582916
  194.3 11.0 %collective-permute-start.18 = (bf16[16,4096]{1,0:T(8,128)(2,1)S(1)}, bf16[16,4096]{1,0:T(8,128)(2,1)S(1)}, u32[]{:S(2)}, u32[]{:S(2)}) collective-permute-start(bf16[16,4096]{1,0:T(8,128)(2,1)S(1)} %get-tuple-element.57.rest_0_), channel_id=1, source_target_pairs={{0,4},{2,6},{4,0},{6,2},{8,12},{10,14},{12,8},{14,10},{16,20},{18,... | collective-permute-start | bytes 393224 | tf_op jit(solution)/shard_map/ppermute | solution.py:57
  201.7 6.8 %collective-permute-start.17 = (bf16[16,4096]{1,0:T(8,128)(2,1)S(1)}, bf16[16,4096]{1,0:T(8,128)(2,1)S(1)}, u32[]{:S(2)}, u32[]{:S(2)}) collective-permute-start(bf16[16,4096]{1,0:T(8,128)(2,1)S(1)} %get-tuple-element.57.rest_0_), channel_id=1, source_target_pairs={{0,24},{2,26},{4,28},{6,30},{8,0},{10,2},{12,4},{14,6},{16,8},{18,... | collective-permute-start | bytes 393224 | tf_op jit(solution)/shard_map/ppermute | solution.py:57
  201.7 7.7 %collective-permute-start.22 = (bf16[16,4096]{1,0:T(8,128)(2,1)S(1)}, bf16[16,4096]{1,0:T(8,128)(2,1)S(1)}, u32[]{:S(2)}, u32[]{:S(2)}) collective-permute-start(bf16[16,4096]{1,0:T(8,128)(2,1)S(1)} %get-tuple-element.57.rest_0_), channel_id=1, source_target_pairs={{0,2},{2,0},{4,6},{6,4},{8,10},{10,8},{12,14},{14,12},{16,18},{18,... | collective-permute-start | bytes 393224 | tf_op jit(solution)/shard_map/ppermute | solution.py:57
  203.6 12.0 %collective-permute-start.16 = (bf16[16,4096]{1,0:T(8,128)(2,1)S(1)}, bf16[16,4096]{1,0:T(8,128)(2,1)S(1)}, u32[]{:S(2)}, u32[]{:S(2)}) collective-permute-start(bf16[16,4096]{1,0:T(8,128)(2,1)S(1)} %get-tuple-element.57.rest_0_), channel_id=1, source_target_pairs={{0,16},{2,18},{4,20},{6,22},{8,24},{10,26},{12,28},{14,30},{16,0},... | collective-permute-start | bytes 393224 | tf_op jit(solution)/shard_map/ppermute | solution.py:57
  203.6 12.5 %collective-permute-start.15 = (bf16[16,4096]{1,0:T(8,128)(2,1)S(1)}, bf16[16,4096]{1,0:T(8,128)(2,1)S(1)}, u32[]{:S(2)}, u32[]{:S(2)}) collective-permute-start(bf16[16,4096]{1,0:T(8,128)(2,1)S(1)} %get-tuple-element.57.rest_0_), channel_id=1, source_target_pairs={{0,8},{2,10},{4,12},{6,14},{8,16},{10,18},{12,20},{14,22},{16,24},... | collective-permute-start | bytes 393224 | tf_op jit(solution)/shard_map/ppermute | solution.py:57
  205.3 12.2 %collective-permute-start.26 = (bf16[16,4096]{1,0:T(8,128)(2,1)S(1)}, bf16[16,4096]{1,0:T(8,128)(2,1)S(1)}, u32[]{:S(2)}, u32[]{:S(2)}) collective-permute-start(bf16[16,4096]{1,0:T(8,128)(2,1)S(1)} %collective-permute-done.18.rest_4_), channel_id=1, source_target_pairs={{0,2},{2,0},{4,6},{6,4},{8,10},{10,8},{12,14},{14,12},{16,18},{18,... | collective-permute-start | bytes 393224 | tf_op jit(solution)/shard_map/ppermute | solution.py:57
  208.5 9.1 %collective-permute-start.25 = (bf16[16,4096]{1,0:T(8,128)(2,1)S(1)}, bf16[16,4096]{1,0:T(8,128)(2,1)S(1)}, u32[]{:S(2)}, u32[]{:S(2)}) collective-permute-start(bf16[16,4096]{1,0:T(8,128)(2,1)S(1)} %collective-permute-done.17.rest_3_), channel_id=1, source_target_pairs={{0,2},{2,0},{4,6},{6,4},{8,10},{10,8},{12,14},{14,12},{16,18},{18,... | collective-permute-start | bytes 393224 | tf_op jit(solution)/shard_map/ppermute | solution.py:57
  209.4 8.6 %collective-permute-start.21 = (bf16[16,4096]{1,0:T(8,128)(2,1)S(1)}, bf16[16,4096]{1,0:T(8,128)(2,1)S(1)}, u32[]{:S(2)}, u32[]{:S(2)}) collective-permute-start(bf16[16,4096]{1,0:T(8,128)(2,1)S(1)} %collective-permute-done.17.rest_3_), channel_id=1, source_target_pairs={{0,4},{2,6},{4,0},{6,2},{8,12},{10,14},{12,8},{14,10},{16,20},{18,... | collective-permute-start | bytes 393224 | tf_op jit(solution)/shard_map/ppermute | solution.py:57
  215.5 6.0 %collective-permute-start.20 = (bf16[16,4096]{1,0:T(8,128)(2,1)S(1)}, bf16[16,4096]{1,0:T(8,128)(2,1)S(1)}, u32[]{:S(2)}, u32[]{:S(2)}) collective-permute-start(bf16[16,4096]{1,0:T(8,128)(2,1)S(1)} %collective-permute-done.16.rest_2_), channel_id=1, source_target_pairs={{0,4},{2,6},{4,0},{6,2},{8,12},{10,14},{12,8},{14,10},{16,20},{18,... | collective-permute-start | bytes 393224 | tf_op jit(solution)/shard_map/ppermute | solution.py:57
  216.0 6.9 %collective-permute-start.19 = (bf16[16,4096]{1,0:T(8,128)(2,1)S(1)}, bf16[16,4096]{1,0:T(8,128)(2,1)S(1)}, u32[]{:S(2)}, u32[]{:S(2)}) collective-permute-start(bf16[16,4096]{1,0:T(8,128)(2,1)S(1)} %collective-permute-done.15.rest_1_), channel_id=1, source_target_pairs={{0,4},{2,6},{4,0},{6,2},{8,12},{10,14},{12,8},{14,10},{16,20},{18,... | collective-permute-start | bytes 393224 | tf_op jit(solution)/shard_map/ppermute | solution.py:57
  217.6 5.3 %collective-permute-start.24 = (bf16[16,4096]{1,0:T(8,128)(2,1)S(1)}, bf16[16,4096]{1,0:T(8,128)(2,1)S(1)}, u32[]{:S(2)}, u32[]{:S(2)}) collective-permute-start(bf16[16,4096]{1,0:T(8,128)(2,1)S(1)} %collective-permute-done.16.rest_2_), channel_id=1, source_target_pairs={{0,2},{2,0},{4,6},{6,4},{8,10},{10,8},{12,14},{14,12},{16,18},{18,... | collective-permute-start | bytes 393224 | tf_op jit(solution)/shard_map/ppermute | solution.py:57
  217.6 5.3 %collective-permute-start.23 = (bf16[16,4096]{1,0:T(8,128)(2,1)S(1)}, bf16[16,4096]{1,0:T(8,128)(2,1)S(1)}, u32[]{:S(2)}, u32[]{:S(2)}) collective-permute-start(bf16[16,4096]{1,0:T(8,128)(2,1)S(1)} %collective-permute-done.15.rest_1_), channel_id=1, source_target_pairs={{0,2},{2,0},{4,6},{6,4},{8,10},{10,8},{12,14},{14,12},{16,18},{18,... | collective-permute-start | bytes 393224 | tf_op jit(solution)/shard_map/ppermute | solution.py:57
  218.1 4.8 %collective-permute-start.29 = (bf16[16,4096]{1,0:T(8,128)(2,1)S(1)}, bf16[16,4096]{1,0:T(8,128)(2,1)S(1)}, u32[]{:S(2)}, u32[]{:S(2)}) collective-permute-start(bf16[16,4096]{1,0:T(8,128)(2,1)S(1)} %collective-permute-done.21.rest_7_), channel_id=1, source_target_pairs={{0,2},{2,0},{4,6},{6,4},{8,10},{10,8},{12,14},{14,12},{16,18},{18,... | collective-permute-start | bytes 393224 | tf_op jit(solution)/shard_map/ppermute | solution.py:57
  221.5 1.4 collective-permute-start.28
  222.9 1.3 collective-permute-start.27
  228.6 5.6 %collective-permute-start.30 = (bf16[128,512]{1,0:T(8,128)(2,1)S(1)}, bf16[128,512]{1,0:T(8,128)(2,1)S(1)}, u32[]{:S(2)}, u32[]{:S(2)}) collective-permute-start(bf16[128,512]{1,0:T(8,128)(2,1)S(1)} %get-tuple-element.59), channel_id=1, source_target_pairs={{0,1},{1,0},{2,3},{3,2},{4,5},{5,4},{6,7},{7,6},{8,9},{9,8},{10,11... | collective-permute-start | bytes 393224 | tf_op jit(solution)/shard_map/ppermute | solution.py:370

commit v11 on v10

--- a/solution.py
+++ b/solution.py
@@ -27,10 +27,12 @@
 
 def page_rounds(dims):
     far, near = dims
-    steps = sorted(range(1, far), key=lambda z: (min(z, far - z), z))
-    order = [(z, n) for z in steps for n in range(near)]
-    for n in range(1, near):
-        order.insert(min(2 * n, len(order)), (0, n))
+    single, longer = [(1, n) for n in range(near)], [(z, n) for n in range(near) for z in range(2, far)]
+    order, near_left = single[:2], [(0, n) for n in range(1, near)]
+    single = single[2:]
+    while longer or single or near_left:
+        order += near_left[:1] + longer[: max(far - 2, 1)] + single[:1]
+        near_left, longer, single = near_left[1:], longer[max(far - 2, 1) :], single[1:]
     return [uniform(z, n, dims) for z, n in order]
 
 

time: 236 us -> 231 us (0.979)
  waiting for transfers between devices: 117 us -> 93.3 us
  starting transfers between devices: 88.6 us -> 107 us
    ppermute x30, waiting for transfers between devices: 113 us -> 89.3 us  [send_by(): return lax.ppermute(array, 'group', pairs)]
    ppermute x30, starting transfers between devices: 87.1 us -> 105 us  [send_by(): return lax.ppermute(array, 'group', pairs)]
  transfers between devices with their start and end apart: 31 -> 31, of which waited for: 14 -> 13; matrix products, arithmetic and copies ran while one was open for 0% -> 0% of each run, Pallas kernels for 6% -> 7%
where the time goes in v11:
time: 231 us; the launch traced here: 230 us
  starting transfers between devices  107 us (46%)
  waiting for transfers between devices  93.3 us (40%)
  Pallas kernels  28.2 us (12%)
    ppermute x30, starting transfers between devices, send_by(): return lax.ppermute(array, 'group', pairs)  105 us
    ppermute x30, waiting for transfers between devices, send_by(): return lax.ppermute(array, 'group', pairs)  89.3 us
    pallas_call x5, Pallas kernels, settle(): pl.pallas_call(functools.partial(settle_kernel, dims, routes, own, last),...  13.4 us
    pallas_call x2, Pallas kernels, prepare(): pl.pallas_call(functools.partial(prepare_kernel, dims, routes, own), out_...  10.4 us
  transfers between devices with their start and end apart: 31, of which 13 were waited for; matrix products, arithmetic and copies ran while one was open for 0% of the time, Pallas kernels for 7%

profile of v11, /device:TPU:0, one launch (start us, length us, event | category | flops | bytes accessed | tf_op | source)
XLA Modules:
  0.0 230.4 jit_solution(8065012814756035964)
XLA Ops:
  0.6 0.7 or_or_fusion.table_hbm.table
  1.3 5.1 %outgoing_pages.2 = (bf16[32,128,1024]{2,1,0:T(8,128)(2,1)}, bf16[2,128,1024]{2,1,0:T(8,128)(2,1)S(1)}, bf16[2,128,1024]{2,1,0:T(8,128)(2,1)S(1)}, bf16[2,128,10...) custom-call(s32[256]{0:T(256)S(1)} %or_or_fusion.table_hbm.table, bf16[32,128,1024]{2,1,0:T(8,128)(2,1)} %pool.3), custom_call_target="tpu_custom_call" | custom-call | bytes 5242880 | tf_op jit(solution)/shard_map/outgoing_pages/pallas_call | solution.py:156
  6.5 3.0 %collective-permute-start = (bf16[2,128,1024]{2,1,0:T(8,128)(2,1)S(1)}, bf16[2,128,1024]{2,1,0:T(8,128)(2,1)S(1)}, u32[]{:S(2)}, u32[]{:S(2)}) collective-permute-start(bf16[2,128,1024]{2,1,0:T(8,128)(2,1)S(1)} %get-tuple-element.33), channel_id=1, source_target_pairs={{0,8},{2,10},{4,12},{6,14},{8,16},{10,18},{12,20},{14,22},{16,24},... | collective-permute-start | bytes 1572872 | tf_op jit(solution)/shard_map/ppermute | solution.py:59
  9.5 0.7 collective-permute-start.1
  10.2 1.2 collective-permute-start.2
  11.4 0.9 collective-permute-start.3
  12.3 5.3 %outgoing_pages.3 = (bf16[32,128,1024]{2,1,0:T(8,128)(2,1)}, bf16[2,128,1024]{2,1,0:T(8,128)(2,1)S(1)}, bf16[2,128,1024]{2,1,0:T(8,128)(2,1)S(1)}, bf16[2,128,10...) custom-call(s32[256]{0:T(256)S(1)} %or_or_fusion.table_hbm.table, ...), custom_call_target="tpu_custom_call", output_to_operand_aliasing={{0}: (2, {})} | custom-call | bytes 11534336 | tf_op jit(solution)/shard_map/outgoing_pages/pallas_call | solution.py:156
  17.6 2.8 %collective-permute-start.4 = (bf16[2,128,1024]{2,1,0:T(8,128)(2,1)S(1)}, bf16[2,128,1024]{2,1,0:T(8,128)(2,1)S(1)}, u32[]{:S(2)}, u32[]{:S(2)}) collective-permute-start(bf16[2,128,1024]{2,1,0:T(8,128)(2,1)S(1)} %get-tuple-element.39), channel_id=1, source_target_pairs={{0,24},{2,26},{4,28},{6,30},{8,0},{10,2},{12,4},{14,6},{16,8},{18,... | collective-permute-start | bytes 1572872 | tf_op jit(solution)/shard_map/ppermute | solution.py:59
  20.4 4.2 %collective-permute-done.rest_0_ = bf16[2,128,1024]{2,1,0:T(8,128)(2,1)S(1)} collective-permute-done((bf16[2,128,1024]{2,1,0:T(8,128)(2,1)S(1)}, bf16[2,128,1024]{2,1,0:T(8,128)(2,1)S(1)}, u32[]{:S(2)}, u32[]{:S(2)}) %collective-permute-start) | collective-permute-done | bytes 524320 | tf_op jit(solution)/shard_map/ppermute | solution.py:59
  24.5 0.9 collective-permute-start.5
  25.4 8.9 %collective-permute-done.1.rest_1_ = bf16[2,128,1024]{2,1,0:T(8,128)(2,1)S(1)} collective-permute-done((bf16[2,128,1024]{2,1,0:T(8,128)(2,1)S(1)}, bf16[2,128,1024]{2,1,0:T(8,128)(2,1)S(1)}, u32[]{:S(2)}, u32[]{:S(2)}) %collective-permute-start.1) | collective-permute-done | bytes 524320 | tf_op jit(solution)/shard_map/ppermute | solution.py:59
  34.3 1.0 collective-permute-start.6
  35.2 24.7 %collective-permute-start.7 = (bf16[2,128,1024]{2,1,0:T(8,128)(2,1)S(1)}, bf16[2,128,1024]{2,1,0:T(8,128)(2,1)S(1)}, u32[]{:S(2)}, u32[]{:S(2)}) collective-permute-start(bf16[2,128,1024]{2,1,0:T(8,128)(2,1)S(1)} %get-tuple-element.44), channel_id=1, source_target_pairs={{0,18},{2,16},{4,22},{6,20},{8,26},{10,24},{12,30},{14,28},{16,2},... | collective-permute-start | bytes 1572872 | tf_op jit(solution)/shard_map/ppermute | solution.py:59
  59.9 8.4 %collective-permute-start.8 = (bf16[2,128,1024]{2,1,0:T(8,128)(2,1)S(1)}, bf16[2,128,1024]{2,1,0:T(8,128)(2,1)S(1)}, u32[]{:S(2)}, u32[]{:S(2)}) collective-permute-start(bf16[2,128,1024]{2,1,0:T(8,128)(2,1)S(1)} %get-tuple-element.45), channel_id=1, source_target_pairs={{0,26},{2,24},{4,30},{6,28},{8,2},{10,0},{12,6},{14,4},{16,10},{18... | collective-permute-start | bytes 1572872 | tf_op jit(solution)/shard_map/ppermute | solution.py:59
  68.3 29.3 %collective-permute-start.9 = (bf16[2,128,1024]{2,1,0:T(8,128)(2,1)S(1)}, bf16[2,128,1024]{2,1,0:T(8,128)(2,1)S(1)}, u32[]{:S(2)}, u32[]{:S(2)}) collective-permute-start(bf16[2,128,1024]{2,1,0:T(8,128)(2,1)S(1)} %get-tuple-element.48), channel_id=1, source_target_pairs={{0,14},{2,12},{4,10},{6,8},{8,22},{10,20},{12,18},{14,16},{16,30},... | collective-permute-start | bytes 1572872 | tf_op jit(solution)/shard_map/ppermute | solution.py:59
  97.7 0.8 collective-permute-start.10
  98.5 6.7 %collective-permute-start.11 = (bf16[2,128,1024]{2,1,0:T(8,128)(2,1)S(1)}, bf16[2,128,1024]{2,1,0:T(8,128)(2,1)S(1)}, u32[]{:S(2)}, u32[]{:S(2)}) collective-permute-start(bf16[2,128,1024]{2,1,0:T(8,128)(2,1)S(1)} %get-tuple-element.50), channel_id=1, source_target_pairs={{0,20},{2,22},{4,16},{6,18},{8,28},{10,30},{12,24},{14,26},{16,4},... | collective-permute-start | bytes 1572872 | tf_op jit(solution)/shard_map/ppermute | solution.py:59
  105.2 19.6 %collective-permute-done.7.rest_1_ = bf16[2,128,1024]{2,1,0:T(8,128)(2,1)S(1)} collective-permute-done((bf16[2,128,1024]{2,1,0:T(8,128)(2,1)S(1)}, bf16[2,128,1024]{2,1,0:T(8,128)(2,1)S(1)}, u32[]{:S(2)}, u32[]{:S(2)}) %collective-permute-start.7) | collective-permute-done | bytes 524320 | tf_op jit(solution)/shard_map/ppermute | solution.py:59
  124.7 11.3 %collective-permute-start.13 = (bf16[2,128,1024]{2,1,0:T(8,128)(2,1)S(1)}, bf16[2,128,1024]{2,1,0:T(8,128)(2,1)S(1)}, u32[]{:S(2)}, u32[]{:S(2)}) collective-permute-start(bf16[2,128,1024]{2,1,0:T(8,128)(2,1)S(1)} %get-tuple-element.54), channel_id=1, source_target_pairs={{0,22},{2,20},{4,18},{6,16},{8,30},{10,28},{12,26},{14,24},{16,6},... | collective-permute-start | bytes 1572872 | tf_op jit(solution)/shard_map/ppermute | solution.py:59
  136.1 3.5 %collective-permute-start.14 = (bf16[2,128,1024]{2,1,0:T(8,128)(2,1)S(1)}, bf16[2,128,1024]{2,1,0:T(8,128)(2,1)S(1)}, u32[]{:S(2)}, u32[]{:S(2)}) collective-permute-start(bf16[2,128,1024]{2,1,0:T(8,128)(2,1)S(1)} %get-tuple-element.55), channel_id=1, source_target_pairs={{0,30},{2,28},{4,26},{6,24},{8,6},{10,4},{12,2},{14,0},{16,14},{18... | collective-permute-start | bytes 1572872 | tf_op jit(solution)/shard_map/ppermute | solution.py:59
  139.6 3.1 %settle_pages.5 = (bf16[32,128,1024]{2,1,0:T(8,128)(2,1)}, f32[16,32,128]{2,1,0:T(8,128)S(1)}) custom-call(s32[256]{0:T(256)S(1)} %or_or_fusion.table_hbm.table, s32[256]{0:T(256)S(1)} %copy-done.1, bf16[16,32,128]{2,1,0:T(8,128)(2,1)S(1)} %bitcast.2, f32[16,32,128]{2,1,0:T(8,128)S(1)} %broadcast_in_dim.3.rows_in, ...), custom_call_target="tpu_custom_call", output_to_operand_aliasing={{0}: (4, {})} | custom-call | flops 1073741824 | bytes 3145728 | tf_op jit(solution)/shard_map/settle_pages/pallas_call | solution.py:276
  142.7 3.5 %settle_pages.6 = (bf16[32,128,1024]{2,1,0:T(8,128)(2,1)}, f32[16,32,128]{2,1,0:T(8,128)S(1)}) custom-call(s32[256]{0:T(256)S(1)} %or_or_fusion.table_hbm.table, s32[256]{0:T(256)S(1)} %copy-done.1, bf16[16,32,128]{2,1,0:T(8,128)(2,1)S(1)} %bitcast.3, f32[16,32,128]{2,1,0:T(8,128)S(1)} %get-tuple-element.36.rows_in, ...), custom_call_target="tpu_custom_call", output_to_operand_aliasing={{0}: (4, {})} | custom-call | flops 1073741824 | bytes 3145728 | tf_op jit(solution)/shard_map/settle_pages/pallas_call | solution.py:276
  146.3 2.2 settle_pages.7
  148.5 11.0 %collective-permute-done.11.rest_2_ = bf16[2,128,1024]{2,1,0:T(8,128)(2,1)S(1)} collective-permute-done((bf16[2,128,1024]{2,1,0:T(8,128)(2,1)S(1)}, bf16[2,128,1024]{2,1,0:T(8,128)(2,1)S(1)}, u32[]{:S(2)}, u32[]{:S(2)}) %collective-permute-start.11) | collective-permute-done | bytes 524320 | tf_op jit(solution)/shard_map/ppermute | solution.py:59
  159.5 2.2 settle_pages.8
  161.7 20.2 %collective-permute-done.13.rest_1_ = bf16[2,128,1024]{2,1,0:T(8,128)(2,1)S(1)} collective-permute-done((bf16[2,128,1024]{2,1,0:T(8,128)(2,1)S(1)}, bf16[2,128,1024]{2,1,0:T(8,128)(2,1)S(1)}, u32[]{:S(2)}, u32[]{:S(2)}) %collective-permute-start.13) | collective-permute-done | bytes 524320 | tf_op jit(solution)/shard_map/ppermute | solution.py:59
  181.9 9.1 %collective-permute-done.14.rest_2_ = bf16[2,128,1024]{2,1,0:T(8,128)(2,1)S(1)} collective-permute-done((bf16[2,128,1024]{2,1,0:T(8,128)(2,1)S(1)}, bf16[2,128,1024]{2,1,0:T(8,128)(2,1)S(1)}, u32[]{:S(2)}, u32[]{:S(2)}) %collective-permute-start.14) | collective-permute-done | bytes 524320 | tf_op jit(solution)/shard_map/ppermute | solution.py:59
  191.0 2.4 %settle_pages.9 = (bf16[32,128,1024]{2,1,0:T(8,128)(2,1)}, bf16[16,4096]{1,0:T(8,128)(2,1)S(1)}) custom-call(s32[256]{0:T(256)S(1)} %or_or_fusion.table_hbm.table, s32[256]{0:T(256)S(1)} %copy-done.1, bf16[16,32,128]{2,1,0:T(8,128)(2,1)S(1)} %bitcast.6, f32[16,32,128]{2,1,0:T(8,128)S(1)} %get-tuple-element.51.rows_in, ...), custom_call_target="tpu_custom_call", output_to_operand_aliasing={{0}: (4, {})} | custom-call | flops 1073741824 | bytes 3145728 | tf_op jit(solution)/shard_map/settle_pages/pallas_call | solution.py:276
  193.5 0.9 collective-permute-start.18
  194.4 2.2 collective-permute-start.17
  196.6 0.7 collective-permute-start.22
  197.3 1.7 collective-permute-start.16
  199.0 0.9 collective-permute-done.18.rest_4_
  199.9 0.1 collective-permute-start.26
  200.0 1.3 collective-permute-done.17.rest_3_
  201.3 1.7 collective-permute-start.21
  203.0 7.9 %collective-permute-done.16.rest_2_ = bf16[16,4096]{1,0:T(8,128)(2,1)S(1)} collective-permute-done((bf16[16,4096]{1,0:T(8,128)(2,1)S(1)}, bf16[16,4096]{1,0:T(8,128)(2,1)S(1)}, u32[]{:S(2)}, u32[]{:S(2)}) %collective-permute-start.16) | collective-permute-done | bytes 131104 | tf_op jit(solution)/shard_map/ppermute | solution.py:59
  210.9 1.7 collective-permute-start.20
  212.6 0.4 collective-permute-start.19
  212.9 0.5 collective-permute-start.23
  213.4 0.1 collective-permute-start.29
  213.5 3.5 %collective-permute-done.20.rest_6_ = bf16[16,4096]{1,0:T(8,128)(2,1)S(1)} collective-permute-done((bf16[16,4096]{1,0:T(8,128)(2,1)S(1)}, bf16[16,4096]{1,0:T(8,128)(2,1)S(1)}, u32[]{:S(2)}, u32[]{:S(2)}) %collective-permute-start.20) | collective-permute-done | bytes 131104 | tf_op jit(solution)/shard_map/ppermute | solution.py:59
  217.0 1.4 collective-permute-done.19.rest_5_
  218.4 1.3 collective-permute-done.27.rest_13_
  219.7 4.3 %project_rows.1 = (f32[128,512]{1,0:T(8,128)S(1)}, bf16[128,512]{1,0:T(8,128)(2,1)S(1)}) custom-call(bf16[4096,512]{1,0:T(8,128)(2,1)S(1)} %copy-done, bf16[16,4096]{1,0:T(8,128)(2,1)S(1)} %get-tuple-element.57.rest_0_, bf16[16,4096]{1,0:T(8,128)(2,1)S(1)} %collective-permute-done.15.rest_1_, bf16[16,4096]{1,0:T(8,128)(2,1)S(1)} %collective-permute-done.16.rest_2_, ...), custom_call_target="tpu_custom_call" | custom-call | flops 1073741824 | bytes 4194304 | tf_op jit(solution)/shard_map/project_rows/pallas_call | solution.py:331
  224.1 1.6 collective-permute-start.30
  225.6 4.1 %collective-permute-done.30 = bf16[128,512]{1,0:T(8,128)(2,1)S(1)} collective-permute-done((bf16[128,512]{1,0:T(8,128)(2,1)S(1)}, bf16[128,512]{1,0:T(8,128)(2,1)S(1)}, u32[]{:S(2)}, u32[]{:S(2)}) %collective-permute-start.30) | collective-permute-done | bytes 131104 | tf_op jit(solution)/shard_map/ppermute | solution.py:372
  229.7 0.7 add_convert_fusion
  (32 shorter events, 0.1 us)
Async XLA Ops:
  6.5 18.0 %collective-permute-start = (bf16[2,128,1024]{2,1,0:T(8,128)(2,1)S(1)}, bf16[2,128,1024]{2,1,0:T(8,128)(2,1)S(1)}, u32[]{:S(2)}, u32[]{:S(2)}) collective-permute-start(bf16[2,128,1024]{2,1,0:T(8,128)(2,1)S(1)} %get-tuple-element.33), channel_id=1, source_target_pairs={{0,8},{2,10},{4,12},{6,14},{8,16},{10,18},{12,20},{14,22},{16,24},... | collective-permute-start | bytes 1572872 | tf_op jit(solution)/shard_map/ppermute | solution.py:59
  9.5 24.8 %collective-permute-start.1 = (bf16[2,128,1024]{2,1,0:T(8,128)(2,1)S(1)}, bf16[2,128,1024]{2,1,0:T(8,128)(2,1)S(1)}, u32[]{:S(2)}, u32[]{:S(2)}) collective-permute-start(bf16[2,128,1024]{2,1,0:T(8,128)(2,1)S(1)} %get-tuple-element.34), channel_id=1, source_target_pairs={{0,10},{2,8},{4,14},{6,12},{8,18},{10,16},{12,22},{14,20},{16,26},... | collective-permute-start | bytes 1572872 | tf_op jit(solution)/shard_map/ppermute | solution.py:59
  10.2 25.0 %collective-permute-start.2 = (bf16[2,128,1024]{2,1,0:T(8,128)(2,1)S(1)}, bf16[2,128,1024]{2,1,0:T(8,128)(2,1)S(1)}, u32[]{:S(2)}, u32[]{:S(2)}) collective-permute-start(bf16[2,128,1024]{2,1,0:T(8,128)(2,1)S(1)} %get-tuple-element.35), channel_id=1, source_target_pairs={{0,2},{2,0},{4,6},{6,4},{8,10},{10,8},{12,14},{14,12},{16,18},{18,... | collective-permute-start | bytes 1572872 | tf_op jit(solution)/shard_map/ppermute | solution.py:59
  11.4 48.5 %collective-permute-start.3 = (bf16[2,128,1024]{2,1,0:T(8,128)(2,1)S(1)}, bf16[2,128,1024]{2,1,0:T(8,128)(2,1)S(1)}, u32[]{:S(2)}, u32[]{:S(2)}) collective-permute-start(bf16[2,128,1024]{2,1,0:T(8,128)(2,1)S(1)} %get-tuple-element.38), channel_id=1, source_target_pairs={{0,16},{2,18},{4,20},{6,22},{8,24},{10,26},{12,28},{14,30},{16,0},... | collective-permute-start | bytes 1572872 | tf_op jit(solution)/shard_map/ppermute | solution.py:59
  12.3 127.2 %copy-start.2 = (bf16[16,4096]{1,0:T(8,128)(2,1)S(1)}, bf16[16,4096]{1,0:T(8,128)(2,1)}, u32[]{:S(2)}) copy-start(bf16[16,4096]{1,0:T(8,128)(2,1)} %param.12) | copy-start | bytes 393220
  12.3 127.3 %copy-start.1 = (s32[256]{0:T(256)S(1)}, s32[256]{0:T(256)}, u32[]{:S(2)}) copy-start(s32[256]{0:T(256)} %row_request.9) | copy-start | bytes 3076
  17.6 50.7 %collective-permute-start.4 = (bf16[2,128,1024]{2,1,0:T(8,128)(2,1)S(1)}, bf16[2,128,1024]{2,1,0:T(8,128)(2,1)S(1)}, u32[]{:S(2)}, u32[]{:S(2)}) collective-permute-start(bf16[2,128,1024]{2,1,0:T(8,128)(2,1)S(1)} %get-tuple-element.39), channel_id=1, source_target_pairs={{0,24},{2,26},{4,28},{6,30},{8,0},{10,2},{12,4},{14,6},{16,8},{18,... | collective-permute-start | bytes 1572872 | tf_op jit(solution)/shard_map/ppermute | solution.py:59
  24.5 73.1 %collective-permute-start.5 = (bf16[2,128,1024]{2,1,0:T(8,128)(2,1)S(1)}, bf16[2,128,1024]{2,1,0:T(8,128)(2,1)S(1)}, u32[]{:S(2)}, u32[]{:S(2)}) collective-permute-start(bf16[2,128,1024]{2,1,0:T(8,128)(2,1)S(1)} %get-tuple-element.40), channel_id=1, source_target_pairs={{0,12},{2,14},{4,8},{6,10},{8,20},{10,22},{12,16},{14,18},{16,28},... | collective-permute-start | bytes 1572872 | tf_op jit(solution)/shard_map/ppermute | solution.py:59
  34.3 64.2 %collective-permute-start.6 = (bf16[2,128,1024]{2,1,0:T(8,128)(2,1)S(1)}, bf16[2,128,1024]{2,1,0:T(8,128)(2,1)S(1)}, u32[]{:S(2)}, u32[]{:S(2)}) collective-permute-start(bf16[2,128,1024]{2,1,0:T(8,128)(2,1)S(1)} %get-tuple-element.43), channel_id=1, source_target_pairs={{0,4},{2,6},{4,0},{6,2},{8,12},{10,14},{12,8},{14,10},{16,20},{18,... | collective-permute-start | bytes 1572872 | tf_op jit(solution)/shard_map/ppermute | solution.py:59
  35.2 89.5 %collective-permute-start.7 = (bf16[2,128,1024]{2,1,0:T(8,128)(2,1)S(1)}, bf16[2,128,1024]{2,1,0:T(8,128)(2,1)S(1)}, u32[]{:S(2)}, u32[]{:S(2)}) collective-permute-start(bf16[2,128,1024]{2,1,0:T(8,128)(2,1)S(1)} %get-tuple-element.44), channel_id=1, source_target_pairs={{0,18},{2,16},{4,22},{6,20},{8,26},{10,24},{12,30},{14,28},{16,2},... | collective-permute-start | bytes 1572872 | tf_op jit(solution)/shard_map/ppermute | solution.py:59
  59.9 64.8 %collective-permute-start.8 = (bf16[2,128,1024]{2,1,0:T(8,128)(2,1)S(1)}, bf16[2,128,1024]{2,1,0:T(8,128)(2,1)S(1)}, u32[]{:S(2)}, u32[]{:S(2)}) collective-permute-start(bf16[2,128,1024]{2,1,0:T(8,128)(2,1)S(1)} %get-tuple-element.45), channel_id=1, source_target_pairs={{0,26},{2,24},{4,30},{6,28},{8,2},{10,0},{12,6},{14,4},{16,10},{18... | collective-permute-start | bytes 1572872 | tf_op jit(solution)/shard_map/ppermute | solution.py:59
  68.3 67.7 %collective-permute-start.9 = (bf16[2,128,1024]{2,1,0:T(8,128)(2,1)S(1)}, bf16[2,128,1024]{2,1,0:T(8,128)(2,1)S(1)}, u32[]{:S(2)}, u32[]{:S(2)}) collective-permute-start(bf16[2,128,1024]{2,1,0:T(8,128)(2,1)S(1)} %get-tuple-element.48), channel_id=1, source_target_pairs={{0,14},{2,12},{4,10},{6,8},{8,22},{10,20},{12,18},{14,16},{16,30},... | collective-permute-start | bytes 1572872 | tf_op jit(solution)/shard_map/ppermute | solution.py:59
  97.7 50.8 %collective-permute-start.10 = (bf16[2,128,1024]{2,1,0:T(8,128)(2,1)S(1)}, bf16[2,128,1024]{2,1,0:T(8,128)(2,1)S(1)}, u32[]{:S(2)}, u32[]{:S(2)}) collective-permute-start(bf16[2,128,1024]{2,1,0:T(8,128)(2,1)S(1)} %get-tuple-element.49), channel_id=1, source_target_pairs={{0,6},{2,4},{4,2},{6,0},{8,14},{10,12},{12,10},{14,8},{16,22},{18,... | collective-permute-start | bytes 1572872 | tf_op jit(solution)/shard_map/ppermute | solution.py:59
  98.5 61.0 %collective-permute-start.11 = (bf16[2,128,1024]{2,1,0:T(8,128)(2,1)S(1)}, bf16[2,128,1024]{2,1,0:T(8,128)(2,1)S(1)}, u32[]{:S(2)}, u32[]{:S(2)}) collective-permute-start(bf16[2,128,1024]{2,1,0:T(8,128)(2,1)S(1)} %get-tuple-element.50), channel_id=1, source_target_pairs={{0,20},{2,22},{4,16},{6,18},{8,28},{10,30},{12,24},{14,26},{16,4},... | collective-permute-start | bytes 1572872 | tf_op jit(solution)/shard_map/ppermute | solution.py:59
  124.7 37.0 %collective-permute-start.12 = (bf16[2,128,1024]{2,1,0:T(8,128)(2,1)S(1)}, bf16[2,128,1024]{2,1,0:T(8,128)(2,1)S(1)}, u32[]{:S(2)}, u32[]{:S(2)}) collective-permute-start(bf16[2,128,1024]{2,1,0:T(8,128)(2,1)S(1)} %get-tuple-element.53), channel_id=1, source_target_pairs={{0,28},{2,30},{4,24},{6,26},{8,4},{10,6},{12,0},{14,2},{16,12},{18... | collective-permute-start | bytes 1572872 | tf_op jit(solution)/shard_map/ppermute | solution.py:59
  124.7 57.1 %collective-permute-start.13 = (bf16[2,128,1024]{2,1,0:T(8,128)(2,1)S(1)}, bf16[2,128,1024]{2,1,0:T(8,128)(2,1)S(1)}, u32[]{:S(2)}, u32[]{:S(2)}) collective-permute-start(bf16[2,128,1024]{2,1,0:T(8,128)(2,1)S(1)} %get-tuple-element.54), channel_id=1, source_target_pairs={{0,22},{2,20},{4,18},{6,16},{8,30},{10,28},{12,26},{14,24},{16,6},... | collective-permute-start | bytes 1572872 | tf_op jit(solution)/shard_map/ppermute | solution.py:59
  136.1 55.0 %collective-permute-start.14 = (bf16[2,128,1024]{2,1,0:T(8,128)(2,1)S(1)}, bf16[2,128,1024]{2,1,0:T(8,128)(2,1)S(1)}, u32[]{:S(2)}, u32[]{:S(2)}) collective-permute-start(bf16[2,128,1024]{2,1,0:T(8,128)(2,1)S(1)} %get-tuple-element.55), channel_id=1, source_target_pairs={{0,30},{2,28},{4,26},{6,24},{8,6},{10,4},{12,2},{14,0},{16,14},{18... | collective-permute-start | bytes 1572872 | tf_op jit(solution)/shard_map/ppermute | solution.py:59
  159.5 60.2 %copy-start = (bf16[4096,512]{1,0:T(8,128)(2,1)S(1)}, bf16[4096,512]{1,0:T(8,128)(2,1)}, u32[]{:S(2)}) copy-start(bf16[4096,512]{1,0:T(8,128)(2,1)} %out_weight.1) | copy-start | bytes 12582916
  193.5 6.4 %collective-permute-start.18 = (bf16[16,4096]{1,0:T(8,128)(2,1)S(1)}, bf16[16,4096]{1,0:T(8,128)(2,1)S(1)}, u32[]{:S(2)}, u32[]{:S(2)}) collective-permute-start(bf16[16,4096]{1,0:T(8,128)(2,1)S(1)} %get-tuple-element.57.rest_0_), channel_id=1, source_target_pairs={{0,4},{2,6},{4,0},{6,2},{8,12},{10,14},{12,8},{14,10},{16,20},{18,... | collective-permute-start | bytes 393224 | tf_op jit(solution)/shard_map/ppermute | solution.py:59
  194.4 6.9 %collective-permute-start.17 = (bf16[16,4096]{1,0:T(8,128)(2,1)S(1)}, bf16[16,4096]{1,0:T(8,128)(2,1)S(1)}, u32[]{:S(2)}, u32[]{:S(2)}) collective-permute-start(bf16[16,4096]{1,0:T(8,128)(2,1)S(1)} %get-tuple-element.57.rest_0_), channel_id=1, source_target_pairs={{0,24},{2,26},{4,28},{6,30},{8,0},{10,2},{12,4},{14,6},{16,8},{18,... | collective-permute-start | bytes 393224 | tf_op jit(solution)/shard_map/ppermute | solution.py:59
  196.6 4.7 %collective-permute-start.22 = (bf16[16,4096]{1,0:T(8,128)(2,1)S(1)}, bf16[16,4096]{1,0:T(8,128)(2,1)S(1)}, u32[]{:S(2)}, u32[]{:S(2)}) collective-permute-start(bf16[16,4096]{1,0:T(8,128)(2,1)S(1)} %get-tuple-element.57.rest_0_), channel_id=1, source_target_pairs={{0,2},{2,0},{4,6},{6,4},{8,10},{10,8},{12,14},{14,12},{16,18},{18,... | collective-permute-start | bytes 393224 | tf_op jit(solution)/shard_map/ppermute | solution.py:59
  197.3 13.6 %collective-permute-start.16 = (bf16[16,4096]{1,0:T(8,128)(2,1)S(1)}, bf16[16,4096]{1,0:T(8,128)(2,1)S(1)}, u32[]{:S(2)}, u32[]{:S(2)}) collective-permute-start(bf16[16,4096]{1,0:T(8,128)(2,1)S(1)} %get-tuple-element.57.rest_0_), channel_id=1, source_target_pairs={{0,16},{2,18},{4,20},{6,22},{8,24},{10,26},{12,28},{14,30},{16,0},... | collective-permute-start | bytes 393224 | tf_op jit(solution)/shard_map/ppermute | solution.py:59
  199.0 13.6 %collective-permute-start.15 = (bf16[16,4096]{1,0:T(8,128)(2,1)S(1)}, bf16[16,4096]{1,0:T(8,128)(2,1)S(1)}, u32[]{:S(2)}, u32[]{:S(2)}) collective-permute-start(bf16[16,4096]{1,0:T(8,128)(2,1)S(1)} %get-tuple-element.57.rest_0_), channel_id=1, source_target_pairs={{0,8},{2,10},{4,12},{6,14},{8,16},{10,18},{12,20},{14,22},{16,24},... | collective-permute-start | bytes 393224 | tf_op jit(solution)/shard_map/ppermute | solution.py:59
  199.9 13.1 %collective-permute-start.26 = (bf16[16,4096]{1,0:T(8,128)(2,1)S(1)}, bf16[16,4096]{1,0:T(8,128)(2,1)S(1)}, u32[]{:S(2)}, u32[]{:S(2)}) collective-permute-start(bf16[16,4096]{1,0:T(8,128)(2,1)S(1)} %collective-permute-done.18.rest_4_), channel_id=1, source_target_pairs={{0,2},{2,0},{4,6},{6,4},{8,10},{10,8},{12,14},{14,12},{16,18},{18,... | collective-permute-start | bytes 393224 | tf_op jit(solution)/shard_map/ppermute | solution.py:59
  201.3 11.7 %collective-permute-start.25 = (bf16[16,4096]{1,0:T(8,128)(2,1)S(1)}, bf16[16,4096]{1,0:T(8,128)(2,1)S(1)}, u32[]{:S(2)}, u32[]{:S(2)}) collective-permute-start(bf16[16,4096]{1,0:T(8,128)(2,1)S(1)} %collective-permute-done.17.rest_3_), channel_id=1, source_target_pairs={{0,2},{2,0},{4,6},{6,4},{8,10},{10,8},{12,14},{14,12},{16,18},{18,... | collective-permute-start | bytes 393224 | tf_op jit(solution)/shard_map/ppermute | solution.py:59
  201.3 12.2 %collective-permute-start.21 = (bf16[16,4096]{1,0:T(8,128)(2,1)S(1)}, bf16[16,4096]{1,0:T(8,128)(2,1)S(1)}, u32[]{:S(2)}, u32[]{:S(2)}) collective-permute-start(bf16[16,4096]{1,0:T(8,128)(2,1)S(1)} %collective-permute-done.17.rest_3_), channel_id=1, source_target_pairs={{0,4},{2,6},{4,0},{6,2},{8,12},{10,14},{12,8},{14,10},{16,20},{18,... | collective-permute-start | bytes 393224 | tf_op jit(solution)/shard_map/ppermute | solution.py:59
  210.9 6.1 %collective-permute-start.20 = (bf16[16,4096]{1,0:T(8,128)(2,1)S(1)}, bf16[16,4096]{1,0:T(8,128)(2,1)S(1)}, u32[]{:S(2)}, u32[]{:S(2)}) collective-permute-start(bf16[16,4096]{1,0:T(8,128)(2,1)S(1)} %collective-permute-done.16.rest_2_), channel_id=1, source_target_pairs={{0,4},{2,6},{4,0},{6,2},{8,12},{10,14},{12,8},{14,10},{16,20},{18,... | collective-permute-start | bytes 393224 | tf_op jit(solution)/shard_map/ppermute | solution.py:59
  212.6 5.8 %collective-permute-start.19 = (bf16[16,4096]{1,0:T(8,128)(2,1)S(1)}, bf16[16,4096]{1,0:T(8,128)(2,1)S(1)}, u32[]{:S(2)}, u32[]{:S(2)}) collective-permute-start(bf16[16,4096]{1,0:T(8,128)(2,1)S(1)} %collective-permute-done.15.rest_1_), channel_id=1, source_target_pairs={{0,4},{2,6},{4,0},{6,2},{8,12},{10,14},{12,8},{14,10},{16,20},{18,... | collective-permute-start | bytes 393224 | tf_op jit(solution)/shard_map/ppermute | solution.py:59
  212.9 5.5 %collective-permute-start.24 = (bf16[16,4096]{1,0:T(8,128)(2,1)S(1)}, bf16[16,4096]{1,0:T(8,128)(2,1)S(1)}, u32[]{:S(2)}, u32[]{:S(2)}) collective-permute-start(bf16[16,4096]{1,0:T(8,128)(2,1)S(1)} %collective-permute-done.16.rest_2_), channel_id=1, source_target_pairs={{0,2},{2,0},{4,6},{6,4},{8,10},{10,8},{12,14},{14,12},{16,18},{18,... | collective-permute-start | bytes 393224 | tf_op jit(solution)/shard_map/ppermute | solution.py:59
  212.9 5.4 %collective-permute-start.23 = (bf16[16,4096]{1,0:T(8,128)(2,1)S(1)}, bf16[16,4096]{1,0:T(8,128)(2,1)S(1)}, u32[]{:S(2)}, u32[]{:S(2)}) collective-permute-start(bf16[16,4096]{1,0:T(8,128)(2,1)S(1)} %collective-permute-done.15.rest_1_), channel_id=1, source_target_pairs={{0,2},{2,0},{4,6},{6,4},{8,10},{10,8},{12,14},{14,12},{16,18},{18,... | collective-permute-start | bytes 393224 | tf_op jit(solution)/shard_map/ppermute | solution.py:59
  213.4 4.9 %collective-permute-start.29 = (bf16[16,4096]{1,0:T(8,128)(2,1)S(1)}, bf16[16,4096]{1,0:T(8,128)(2,1)S(1)}, u32[]{:S(2)}, u32[]{:S(2)}) collective-permute-start(bf16[16,4096]{1,0:T(8,128)(2,1)S(1)} %collective-permute-done.21.rest_7_), channel_id=1, source_target_pairs={{0,2},{2,0},{4,6},{6,4},{8,10},{10,8},{12,14},{14,12},{16,18},{18,... | collective-permute-start | bytes 393224 | tf_op jit(solution)/shard_map/ppermute | solution.py:59
  217.0 1.4 collective-permute-start.28
  218.4 1.3 collective-permute-start.27
  224.1 5.6 %collective-permute-start.30 = (bf16[128,512]{1,0:T(8,128)(2,1)S(1)}, bf16[128,512]{1,0:T(8,128)(2,1)S(1)}, u32[]{:S(2)}, u32[]{:S(2)}) collective-permute-start(bf16[128,512]{1,0:T(8,128)(2,1)S(1)} %get-tuple-element.59), channel_id=1, source_target_pairs={{0,1},{1,0},{2,3},{3,2},{4,5},{5,4},{6,7},{7,6},{8,9},{9,8},{10,11... | collective-permute-start | bytes 393224 | tf_op jit(solution)/shard_map/ppermute | solution.py:372

commit v12 on v11

--- a/solution.py
+++ b/solution.py
@@ -12,7 +12,7 @@
 MAX_PAGES = 2
 WAVE = 3
 ROW_UNROLL = 4
-EARLY = 4
+EARLY = 2
 VMEM_LIMIT = 20 * 1024 * 1024
 
 
@@ -59,17 +59,17 @@
     return lax.ppermute(array, "group", pairs)
 
 
-def gather_shards(shard, dims):
-    far, near = dims
-    held = {(0, 0): shard}
-    swaps = [1 << i for i in reversed(range(near.bit_length() - 1))]
-    for stage in [[(z, 0) for z in range(1, far)]] + [[(0, n)] for n in swaps]:
-        incoming = {}
-        for step in stage:
-            for offset, array in held.items():
-                moved = send_by(array, uniform(*step, dims), dims)
-                incoming[offset[0] + step[0], offset[1] | step[1]] = moved
-        held.update(incoming)
+def swap(array, mask):
+    groups = lax.axis_size("group")
+    return lax.ppermute(array, "group", [(s, s ^ mask) for s in range(groups)])
+
+
+def gather_shards(shard):
+    held = {0: shard}
+    mask = lax.axis_size("group") // 2
+    while mask:
+        held.update({done | mask: swap(array, mask) for done, array in held.items()})
+        mask //= 2
     return held
 
 
@@ -85,9 +85,9 @@
 
 
 def prepare_kernel(dims, routes, own, table_hbm, pool, *rest):
-    aliased = 0 if own else 1
-    received, *sends = rest[aliased : aliased + 1 + len(routes)]
-    table, held, zero_page, start_of, count_of, table_sem, in_sems, out_sem = rest[aliased + 1 + len(routes) :]
+    table, held, zero_page, start_of, count_of, table_sem, in_sems, out_sem = rest[-8:]
+    received = rest[-8 - len(routes) - own : -8 - len(routes)]
+    sends = rest[-8 - len(routes) : -8]
     me = lax.axis_index("group")
     groups = lax.axis_size("group")
     page_size = pool.shape[1]
@@ -111,7 +111,7 @@
     lax.fori_loop(0, table.shape[0], visit, jnp.int32(0), unroll=8)
     targets = [(routed(me, route, dims), send, 0) for route, send in zip(routes, sends)]
     if own:
-        targets.append((me, received, me * MAX_PAGES))
+        targets.append((me, received[0], me * MAX_PAGES))
 
     def each(do):
         for i, (to, target, base) in enumerate(targets):
@@ -144,15 +144,14 @@
     each(finish)
 
 
-def prepare(dims, routes, table, pool, received=None):
-    own = received is None
+def prepare(dims, routes, table, pool, own, after=()):
     groups = lax.axis_size("group")
     page = pool.shape[1:]
     blocks = len(routes) + (1 if own else 0)
     hbm = pl.BlockSpec(memory_space=pl.ANY)
     block = jax.ShapeDtypeStruct((MAX_PAGES,) + page, pool.dtype)
-    outs = [jax.ShapeDtypeStruct((groups * MAX_PAGES,) + page, pool.dtype)] + [block] * len(routes)
-    operands = [table, pool] + ([] if own else [received])
+    outs = [jax.ShapeDtypeStruct((groups * MAX_PAGES,) + page, pool.dtype)] * own + [block] * len(routes)
+    operands = [table, pool, *after]
     return pl.pallas_call(
         functools.partial(prepare_kernel, dims, routes, own),
         out_shape=outs,
@@ -168,7 +167,6 @@
             pltpu.SemaphoreType.DMA((blocks, MAX_PAGES)),
             pltpu.SemaphoreType.DMA,
         ],
-        input_output_aliases={} if own else {2: 0},
         compiler_params=pltpu.CompilerParams(vmem_limit_bytes=VMEM_LIMIT),
         cost_estimate=pl.CostEstimate(
             flops=0, bytes_accessed=4 * blocks * MAX_PAGES * math.prod(page), transcendentals=0
@@ -296,54 +294,87 @@
     )(table, row_request, queries, rows, received, *blocks)
 
 
-def project_kernel(dims, offsets, out_weight, *rest):
-    shards = rest[: len(offsets)]
-    own, *theirs = rest[len(offsets) : -3]
+def multiply_rows(shards, out_weight, attended, sems):
+    copies = []
+    row_local = shards[0].shape[0]
+    for i, shard in enumerate(shards):
+        copies.append(pltpu.make_async_copy(shard, attended.at[pl.ds(i * row_local, row_local)], sems.at[i]))
+        copies[-1].start()
+    for copy in copies:
+        copy.wait()
+    return jnp.dot(attended[...], out_weight[...], preferred_element_type=jnp.float32)
+
+
+def project_some_kernel(count, out_weight, *rest):
+    out, attended, sems = rest[count:]
+    out[...] = multiply_rows(rest[:count], out_weight, attended, sems)
+
+
+def project_rest_kernel(masks, count, out_weight, some, *rest):
+    own, *theirs = rest[count:-3]
     attended, product, sems = rest[-3:]
     me = lax.axis_index("group")
     heads = lax.axis_size("head")
     my_head = lax.axis_index("head")
-    row_local = shards[0].shape[0]
+    row_local = rest[0].shape[0]
     share = own.shape[0]
-    copies = []
-    for i, offset in enumerate(offsets):
-        place = pl.ds(routed(me, reverse(uniform(*offset, dims)), dims) * row_local, row_local)
-        copies.append(pltpu.make_async_copy(shards[i], attended.at[place], sems.at[i]))
-        copies[-1].start()
-    for copy in copies:
-        copy.wait()
-    product[...] = jnp.dot(attended[...], out_weight[...], preferred_element_type=jnp.float32)
-    own[...] = product[pl.ds(pl.multiple_of(my_head * share, share), share)]
-    for ahead_by, target in enumerate(theirs, 1):
-        start = pl.multiple_of(lax.rem(my_head + ahead_by, heads) * share, share)
-        target[...] = product[pl.ds(start, share)].astype(target.dtype)
-
-
-def project(dims, gathered, out_weight, heads):
-    offsets = list(gathered)
-    shards = [gathered[offset] for offset in offsets]
-    row_local, width = shards[0].shape
-    row_total = row_local * len(shards)
-    share, columns = row_total // heads, out_weight.shape[1]
+    product[...] = multiply_rows(rest[:count], out_weight, attended, sems)
+    for i, mask in enumerate(masks):
+        done = len(masks) - count
+        part = some if i < done else product
+        at = i if i < done else i - done
+        values = part[at * row_local : (at + 1) * row_local]
+        row = (me ^ mask) * row_local
+        ahead = lax.rem(row // share - my_head + heads, heads)
+        place = pl.ds(pl.multiple_of(lax.rem(row, share), row_local), row_local)
+        for k, out in enumerate([own, *theirs]):
+
+            @pl.when(ahead == k)
+            def _():
+                out[place] = values.astype(out.dtype)
+
+
+def project(gathered, out_weight, heads):
+    masks = [mask for mask in gathered if mask % 2 == 0] + [mask for mask in gathered if mask % 2]
+    some = len(masks) // 2
+    row_local, width = gathered[0].shape
+    columns = out_weight.shape[1]
+    share = row_local * len(masks) // heads
     vmem = pl.BlockSpec(memory_space=pltpu.VMEM)
     hbm = pl.BlockSpec(memory_space=pl.ANY)
+
+    def call(kernel, name, outs, blocks, extra, scratch):
+        rows = row_local * len(blocks)
+        return pl.pallas_call(
+            kernel,
+            out_shape=outs,
+            in_specs=[vmem] * (1 + len(extra)) + [hbm] * len(blocks),
+            out_specs=[vmem] * len(outs),
+            scratch_shapes=[
+                pltpu.VMEM((rows, width), jnp.bfloat16),
+                *scratch,
+                pltpu.SemaphoreType.DMA((len(blocks),)),
+            ],
+            compiler_params=pltpu.CompilerParams(vmem_limit_bytes=VMEM_LIMIT),
+            cost_estimate=pl.CostEstimate(
+                flops=2 * rows * width * columns, bytes_accessed=2 * out_weight.size, transcendentals=0
+            ),
+            name=name,
+        )(out_weight, *extra, *blocks)
+
+    out_weight = pltpu.with_memory_space_constraint(out_weight, pltpu.VMEM)
+    first = [gathered[mask] for mask in masks[:some]]
+    last = [gathered[mask] for mask in masks[some:]]
+    (done,) = call(
+        functools.partial(project_some_kernel, some), "project_some_rows",
+        [jax.ShapeDtypeStruct((some * row_local, columns), jnp.float32)], first, [], [],
+    )
     theirs = jax.ShapeDtypeStruct((share, columns), jnp.bfloat16)
-    return pl.pallas_call(
-        functools.partial(project_kernel, dims, offsets),
-        out_shape=[jax.ShapeDtypeStruct((share, columns), jnp.float32)] + [theirs] * (heads - 1),
-        in_specs=[vmem] + [hbm] * len(shards),
-        out_specs=[vmem] * heads,
-        scratch_shapes=[
-            pltpu.VMEM((row_total, width), jnp.bfloat16),
-            pltpu.VMEM((row_total, columns), jnp.float32),
-            pltpu.SemaphoreType.DMA((len(shards),)),
-        ],
-        compiler_params=pltpu.CompilerParams(vmem_limit_bytes=VMEM_LIMIT),
-        cost_estimate=pl.CostEstimate(
-            flops=2 * row_total * width * columns, bytes_accessed=2 * out_weight.size, transcendentals=0
-        ),
-        name="project_rows",
-    )(pltpu.with_memory_space_constraint(out_weight, pltpu.VMEM), *shards)
+    return call(
+        functools.partial(project_rest_kernel, masks, len(last)), "project_rows",
+        [jax.ShapeDtypeStruct((share, columns), jnp.float32)] + [theirs] * (heads - 1), last, [done],
+        [pltpu.VMEM((len(last) * row_local, columns), jnp.float32)],
+    )
 
 
 def local(kv_pool, lengths, prefill_of, decode_of, row_request, queries, out_weight):
@@ -355,9 +386,9 @@
     routes = page_rounds(dims)
     table = packed(lengths, prefill_of, decode_of, math.prod(dims))
     kv_pool = pltpu.with_memory_space_constraint(kv_pool, pltpu.HBM)
-    received, *early = prepare(dims, routes[:EARLY], table, kv_pool)
-    received, *late = prepare(dims, routes[EARLY:], table, kv_pool, received)
-    arrived = [send_by(block, route, dims) for block, route in zip(early + late, routes)]
+    early = prepare(dims, routes[:EARLY], table, kv_pool, False)
+    received, *late = prepare(dims, routes[EARLY:], table, kv_pool, True, early[:1])
+    arrived = [send_by(block, route, dims) for block, route in zip([*early, *late], routes)]
     rows = jnp.zeros(query_heads.shape, jnp.float32)
     for first in range(0, len(routes), WAVE):
         wave = slice(first, first + WAVE)
@@ -366,7 +397,7 @@
             dims, routes[wave], first == 0, last, table, row_request, query_heads, rows, received, arrived[wave]
         )
 
-    own, *theirs = project(dims, gather_shards(rows, dims), out_weight, heads)
+    own, *theirs = project(gather_shards(rows), out_weight, heads)
     for ahead_by, part in enumerate(theirs, 1):
         pairs = [(h, (h + ahead_by) % heads) for h in range(heads)]
         own = own + lax.ppermute(part, "head", pairs).astype(jnp.float32)
@@ -383,5 +414,6 @@
         P("group", "head"),
         P("head", "group"),
     )
+    assert mesh.shape["group"] & (mesh.shape["group"] - 1) == 0
     out_specs = (P("group", None, "head"), P("head", "group"))
     return jax.shard_map(local, mesh=mesh, in_specs=in_specs, out_specs=out_specs, check_vma=False)

time: 231 us -> 228 us (0.987)
  starting transfers between devices: 107 us -> 104 us
    ppermute x0 -> x15, waiting for transfers between devices: none -> 14.8 us  [swap(): return lax.ppermute(array, 'group', [(s, s ^ mask) for s in range(groups)])]
    ppermute x30 -> x15, waiting for transfers between devices: 89.3 us -> 74.5 us  [send_by(): return lax.ppermute(array, 'group', pairs)]
    ppermute x30 -> x15, starting transfers between devices: 105 us -> 95.2 us  [send_by(): return lax.ppermute(array, 'group', pairs)]
    ppermute x0 -> x15, starting transfers between devices: none -> 7.34 us  [swap(): return lax.ppermute(array, 'group', [(s, s ^ mask) for s in range(groups)])]
  transfers between devices with their start and end apart: 31 -> 31, of which waited for: 13 -> 13; matrix products, arithmetic and copies ran while one was open for 0% -> 0% of each run, Pallas kernels for 7% -> 9%
where the time goes in v12:
time: 228 us
  starting transfers between devices  104 us (46%)
  waiting for transfers between devices  93.8 us (41%)
  Pallas kernels  28.2 us (12%)
    ppermute x15, starting transfers between devices, send_by(): return lax.ppermute(array, 'group', pairs)  95.2 us
    ppermute x15, waiting for transfers between devices, send_by(): return lax.ppermute(array, 'group', pairs)  74.5 us
    ppermute x15, waiting for transfers between devices, swap(): return lax.ppermute(array, 'group', [(s, s ^ mask) for s in range(groups)])  14.8 us
    pallas_call x5, Pallas kernels, settle(): pl.pallas_call(functools.partial(settle_kernel, dims, routes, own, last),...  13.4 us
    pallas_call x2, Pallas kernels, prepare(): pl.pallas_call(functools.partial(prepare_kernel, dims, routes, own), out_...  10.2 us
    ppermute x15, starting transfers between devices, swap(): return lax.ppermute(array, 'group', [(s, s ^ mask) for s in range(groups)])  7.34 us
    pallas_call x2, Pallas kernels, call(): pl.pallas_call(kernel, out_shape=outs, in_specs=[vmem] * (1 + len(extra))...  4.6 us
  transfers between devices with their start and end apart: 31, of which 13 were waited for; matrix products, arithmetic and copies ran while one was open for 0% of the time, Pallas kernels for 9%

profile of v12, /device:TPU:0, one launch (start us, length us, event | category | flops | bytes accessed | tf_op | source)
XLA Modules:
  0.0 228.4 jit_solution(12460299964538485744)
XLA Ops:
  0.6 0.7 or_or_fusion.table_hbm.table
  1.4 3.9 %outgoing_pages.2 = (bf16[2,128,1024]{2,1,0:T(8,128)(2,1)S(1)}, bf16[2,128,1024]{2,1,0:T(8,128)(2,1)S(1)}) custom-call(s32[256]{0:T(256)S(1)} %or_or_fusion.table_hbm.table, bf16[32,128,1024]{2,1,0:T(8,128)(2,1)} %pool.3), custom_call_target="tpu_custom_call" | custom-call | bytes 2097152 | tf_op jit(solution)/shard_map/outgoing_pages/pallas_call | solution.py:155
  5.3 2.5 %collective-permute-start.1 = (bf16[2,128,1024]{2,1,0:T(8,128)(2,1)S(1)}, bf16[2,128,1024]{2,1,0:T(8,128)(2,1)S(1)}, u32[]{:S(2)}, u32[]{:S(2)}) collective-permute-start(bf16[2,128,1024]{2,1,0:T(8,128)(2,1)S(1)} %get-tuple-element.32), channel_id=1, source_target_pairs={{0,10},{2,8},{4,14},{6,12},{8,18},{10,16},{12,22},{14,20},{16,26},... | collective-permute-start | bytes 1572872 | tf_op jit(solution)/shard_map/ppermute | solution.py:59
  7.8 1.7 collective-permute-start
  9.4 6.3 %outgoing_pages.3 = (bf16[32,128,1024]{2,1,0:T(8,128)(2,1)}, bf16[2,128,1024]{2,1,0:T(8,128)(2,1)S(1)}, bf16[2,128,1024]{2,1,0:T(8,128)(2,1)S(1)}, bf16[2,128,10...) custom-call(s32[256]{0:T(256)S(1)} %or_or_fusion.table_hbm.table, ...), custom_call_target="tpu_custom_call" | custom-call | bytes 14680064 | tf_op jit(solution)/shard_map/outgoing_pages/pallas_call | solution.py:155
  15.7 0.8 collective-permute-start.2
  16.5 1.0 collective-permute-start.3
  17.6 2.6 %collective-permute-start.4 = (bf16[2,128,1024]{2,1,0:T(8,128)(2,1)S(1)}, bf16[2,128,1024]{2,1,0:T(8,128)(2,1)S(1)}, u32[]{:S(2)}, u32[]{:S(2)}) collective-permute-start(bf16[2,128,1024]{2,1,0:T(8,128)(2,1)S(1)} %get-tuple-element.37), channel_id=1, source_target_pairs={{0,24},{2,26},{4,28},{6,30},{8,0},{10,2},{12,4},{14,6},{16,8},{18,... | collective-permute-start | bytes 1572872 | tf_op jit(solution)/shard_map/ppermute | solution.py:59
  20.2 1.4 collective-permute-done.1.rest_1_
  21.6 2.0 collective-permute-start.5
  23.7 11.0 %collective-permute-done.rest_0_ = bf16[2,128,1024]{2,1,0:T(8,128)(2,1)S(1)} collective-permute-done((bf16[2,128,1024]{2,1,0:T(8,128)(2,1)S(1)}, bf16[2,128,1024]{2,1,0:T(8,128)(2,1)S(1)}, u32[]{:S(2)}, u32[]{:S(2)}) %collective-permute-start) | collective-permute-done | bytes 524320 | tf_op jit(solution)/shard_map/ppermute | solution.py:59
  34.7 1.4 collective-permute-start.6
  36.0 0.0 collective-permute-done.2.rest_2_
  36.0 22.4 %collective-permute-start.7 = (bf16[2,128,1024]{2,1,0:T(8,128)(2,1)S(1)}, bf16[2,128,1024]{2,1,0:T(8,128)(2,1)S(1)}, u32[]{:S(2)}, u32[]{:S(2)}) collective-permute-start(bf16[2,128,1024]{2,1,0:T(8,128)(2,1)S(1)} %get-tuple-element.42), channel_id=1, source_target_pairs={{0,18},{2,16},{4,22},{6,20},{8,26},{10,24},{12,30},{14,28},{16,2},... | collective-permute-start | bytes 1572872 | tf_op jit(solution)/shard_map/ppermute | solution.py:59
  58.4 27.6 %collective-permute-start.8 = (bf16[2,128,1024]{2,1,0:T(8,128)(2,1)S(1)}, bf16[2,128,1024]{2,1,0:T(8,128)(2,1)S(1)}, u32[]{:S(2)}, u32[]{:S(2)}) collective-permute-start(bf16[2,128,1024]{2,1,0:T(8,128)(2,1)S(1)} %get-tuple-element.43), channel_id=1, source_target_pairs={{0,26},{2,24},{4,30},{6,28},{8,2},{10,0},{12,6},{14,4},{16,10},{18... | collective-permute-start | bytes 1572872 | tf_op jit(solution)/shard_map/ppermute | solution.py:59
  86.0 11.1 %collective-permute-start.9 = (bf16[2,128,1024]{2,1,0:T(8,128)(2,1)S(1)}, bf16[2,128,1024]{2,1,0:T(8,128)(2,1)S(1)}, u32[]{:S(2)}, u32[]{:S(2)}) collective-permute-start(bf16[2,128,1024]{2,1,0:T(8,128)(2,1)S(1)} %get-tuple-element.46), channel_id=1, source_target_pairs={{0,14},{2,12},{4,10},{6,8},{8,22},{10,20},{12,18},{14,16},{16,30},... | collective-permute-start | bytes 1572872 | tf_op jit(solution)/shard_map/ppermute | solution.py:59
  97.2 0.1 collective-permute-start.10
  97.3 0.0 collective-permute-done.6.rest_0_
  97.3 7.2 %collective-permute-start.11 = (bf16[2,128,1024]{2,1,0:T(8,128)(2,1)S(1)}, bf16[2,128,1024]{2,1,0:T(8,128)(2,1)S(1)}, u32[]{:S(2)}, u32[]{:S(2)}) collective-permute-start(bf16[2,128,1024]{2,1,0:T(8,128)(2,1)S(1)} %get-tuple-element.48), channel_id=1, source_target_pairs={{0,20},{2,22},{4,16},{6,18},{8,28},{10,30},{12,24},{14,26},{16,4},... | collective-permute-start | bytes 1572872 | tf_op jit(solution)/shard_map/ppermute | solution.py:59
  104.4 19.0 %collective-permute-done.7.rest_1_ = bf16[2,128,1024]{2,1,0:T(8,128)(2,1)S(1)} collective-permute-done((bf16[2,128,1024]{2,1,0:T(8,128)(2,1)S(1)}, bf16[2,128,1024]{2,1,0:T(8,128)(2,1)S(1)}, u32[]{:S(2)}, u32[]{:S(2)}) %collective-permute-start.7) | collective-permute-done | bytes 524320 | tf_op jit(solution)/shard_map/ppermute | solution.py:59
  123.4 0.0 collective-permute-start.12
  123.4 0.0 collective-permute-done.8.rest_2_
  123.4 12.0 %collective-permute-start.13 = (bf16[2,128,1024]{2,1,0:T(8,128)(2,1)S(1)}, bf16[2,128,1024]{2,1,0:T(8,128)(2,1)S(1)}, u32[]{:S(2)}, u32[]{:S(2)}) collective-permute-start(bf16[2,128,1024]{2,1,0:T(8,128)(2,1)S(1)} %get-tuple-element.52), channel_id=1, source_target_pairs={{0,22},{2,20},{4,18},{6,16},{8,30},{10,28},{12,26},{14,24},{16,6},... | collective-permute-start | bytes 1572872 | tf_op jit(solution)/shard_map/ppermute | solution.py:59
  135.5 2.8 %collective-permute-start.14 = (bf16[2,128,1024]{2,1,0:T(8,128)(2,1)S(1)}, bf16[2,128,1024]{2,1,0:T(8,128)(2,1)S(1)}, u32[]{:S(2)}, u32[]{:S(2)}) collective-permute-start(bf16[2,128,1024]{2,1,0:T(8,128)(2,1)S(1)} %get-tuple-element.53), channel_id=1, source_target_pairs={{0,30},{2,28},{4,26},{6,24},{8,6},{10,4},{12,2},{14,0},{16,14},{18... | collective-permute-start | bytes 1572872 | tf_op jit(solution)/shard_map/ppermute | solution.py:59
  138.3 3.1 %settle_pages.5 = (bf16[32,128,1024]{2,1,0:T(8,128)(2,1)}, f32[16,32,128]{2,1,0:T(8,128)S(1)}) custom-call(s32[256]{0:T(256)S(1)} %or_or_fusion.table_hbm.table, s32[256]{0:T(256)S(1)} %copy-done.1, bf16[16,32,128]{2,1,0:T(8,128)(2,1)S(1)} %bitcast.2, f32[16,32,128]{2,1,0:T(8,128)S(1)} %broadcast_in_dim.3.rows_in, ...), custom_call_target="tpu_custom_call", output_to_operand_aliasing={{0}: (4, {})} | custom-call | flops 1073741824 | bytes 3145728 | tf_op jit(solution)/shard_map/settle_pages/pallas_call | solution.py:274
  141.4 2.2 settle_pages.6
  143.6 3.5 %settle_pages.7 = (bf16[32,128,1024]{2,1,0:T(8,128)(2,1)}, f32[16,32,128]{2,1,0:T(8,128)S(1)}) custom-call(s32[256]{0:T(256)S(1)} %or_or_fusion.table_hbm.table, s32[256]{0:T(256)S(1)} %copy-done.1, bf16[16,32,128]{2,1,0:T(8,128)(2,1)S(1)} %bitcast.4, f32[16,32,128]{2,1,0:T(8,128)S(1)} %get-tuple-element.39.rows_in, ...), custom_call_target="tpu_custom_call", output_to_operand_aliasing={{0}: (4, {})} | custom-call | flops 1073741824 | bytes 3145728 | tf_op jit(solution)/shard_map/settle_pages/pallas_call | solution.py:274
  147.2 11.7 %collective-permute-done.11.rest_2_ = bf16[2,128,1024]{2,1,0:T(8,128)(2,1)S(1)} collective-permute-done((bf16[2,128,1024]{2,1,0:T(8,128)(2,1)S(1)}, bf16[2,128,1024]{2,1,0:T(8,128)(2,1)S(1)}, u32[]{:S(2)}, u32[]{:S(2)}) %collective-permute-start.11) | collective-permute-done | bytes 524320 | tf_op jit(solution)/shard_map/ppermute | solution.py:59
  158.9 2.2 settle_pages.8
  161.1 20.2 %collective-permute-done.13.rest_1_ = bf16[2,128,1024]{2,1,0:T(8,128)(2,1)S(1)} collective-permute-done((bf16[2,128,1024]{2,1,0:T(8,128)(2,1)S(1)}, bf16[2,128,1024]{2,1,0:T(8,128)(2,1)S(1)}, u32[]{:S(2)}, u32[]{:S(2)}) %collective-permute-start.13) | collective-permute-done | bytes 524320 | tf_op jit(solution)/shard_map/ppermute | solution.py:59
  181.3 11.2 %collective-permute-done.14.rest_2_ = bf16[2,128,1024]{2,1,0:T(8,128)(2,1)S(1)} collective-permute-done((bf16[2,128,1024]{2,1,0:T(8,128)(2,1)S(1)}, bf16[2,128,1024]{2,1,0:T(8,128)(2,1)S(1)}, u32[]{:S(2)}, u32[]{:S(2)}) %collective-permute-start.14) | collective-permute-done | bytes 524320 | tf_op jit(solution)/shard_map/ppermute | solution.py:59
  192.5 2.4 %settle_pages.9 = (bf16[32,128,1024]{2,1,0:T(8,128)(2,1)}, bf16[16,4096]{1,0:T(8,128)(2,1)S(1)}) custom-call(s32[256]{0:T(256)S(1)} %or_or_fusion.table_hbm.table, s32[256]{0:T(256)S(1)} %copy-done.1, bf16[16,32,128]{2,1,0:T(8,128)(2,1)S(1)} %bitcast.6, f32[16,32,128]{2,1,0:T(8,128)S(1)} %get-tuple-element.49.rows_in, ...), custom_call_target="tpu_custom_call", output_to_operand_aliasing={{0}: (4, {})} | custom-call | flops 1073741824 | bytes 3145728 | tf_op jit(solution)/shard_map/settle_pages/pallas_call | solution.py:274
  194.9 0.1 collective-permute-start.15
  195.0 0.2 collective-permute-start.18
  195.2 4.5 %collective-permute-start.16 = (bf16[16,4096]{1,0:T(8,128)(2,1)S(1)}, bf16[16,4096]{1,0:T(8,128)(2,1)S(1)}, u32[]{:S(2)}, u32[]{:S(2)}) collective-permute-start(bf16[16,4096]{1,0:T(8,128)(2,1)S(1)} %get-tuple-element.55.rest_0_), channel_id=1, source_target_pairs={{0,8},{2,10},{4,12},{6,14},{8,0},{10,2},{12,4},{14,6},{16,24},{18,... | collective-permute-start | bytes 393224 | tf_op jit(solution)/shard_map/ppermute | solution.py:64
  199.7 4.6 %collective-permute-done.15.rest_1_ = bf16[16,4096]{1,0:T(8,128)(2,1)S(1)} collective-permute-done((bf16[16,4096]{1,0:T(8,128)(2,1)S(1)}, bf16[16,4096]{1,0:T(8,128)(2,1)S(1)}, u32[]{:S(2)}, u32[]{:S(2)}) %collective-permute-start.15) | collective-permute-done | bytes 131104 | tf_op jit(solution)/shard_map/ppermute | solution.py:64
  204.3 1.3 collective-permute-done.16.rest_2_
  205.6 2.0 collective-permute-start.19
  207.6 2.1 collective-permute-done.17.rest_3_
  209.7 0.5 collective-permute-start.25
  210.2 1.7 collective-permute-done.20.rest_6_
  211.9 2.8 %collective-permute-done.19.rest_5_ = bf16[16,4096]{1,0:T(8,128)(2,1)S(1)} collective-permute-done((bf16[16,4096]{1,0:T(8,128)(2,1)S(1)}, bf16[16,4096]{1,0:T(8,128)(2,1)S(1)}, u32[]{:S(2)}, u32[]{:S(2)}) %collective-permute-start.19) | collective-permute-done | bytes 131104 | tf_op jit(solution)/shard_map/ppermute | solution.py:64
  214.7 2.4 %collective-permute-done.21.rest_7_ = bf16[16,4096]{1,0:T(8,128)(2,1)S(1)} collective-permute-done((bf16[16,4096]{1,0:T(8,128)(2,1)S(1)}, bf16[16,4096]{1,0:T(8,128)(2,1)S(1)}, u32[]{:S(2)}, u32[]{:S(2)}) %collective-permute-start.21) | collective-permute-done | bytes 131104 | tf_op jit(solution)/shard_map/ppermute | solution.py:64
  217.1 2.1 project_some_rows.1.some
  219.3 2.5 %project_rows.1 = (f32[128,512]{1,0:T(8,128)S(1)}, bf16[128,512]{1,0:T(8,128)(2,1)S(1)}) custom-call(bf16[4096,512]{1,0:T(8,128)(2,1)S(1)} %copy-done, f32[128,512]{1,0:T(8,128)S(1)} %project_some_rows.1.some, bf16[16,4096]{1,0:T(8,128)(2,1)S(1)} %collective-permute-done.22.rest_0_, bf16[16,4096]{1,0:T(8,128)(2,1)S(1)} %collective-permute-done.23.rest_1_, ...), custom_call_target="tpu_custom_call" | custom-call | flops 536870912 | bytes 4194304 | tf_op jit(solution)/shard_map/project_rows/pallas_call | solution.py:348
  221.8 1.6 collective-permute-start.30
  223.4 4.4 %collective-permute-done.30 = bf16[128,512]{1,0:T(8,128)(2,1)S(1)} collective-permute-done((bf16[128,512]{1,0:T(8,128)(2,1)S(1)}, bf16[128,512]{1,0:T(8,128)(2,1)S(1)}, u32[]{:S(2)}, u32[]{:S(2)}) %collective-permute-start.30) | collective-permute-done | bytes 131104 | tf_op jit(solution)/shard_map/ppermute | solution.py:403
  227.8 0.7 add_convert_fusion
  (33 shorter events, 0.1 us)
Async XLA Ops:
  1.3 136.9 %copy-start.2 = (bf16[16,4096]{1,0:T(8,128)(2,1)S(1)}, bf16[16,4096]{1,0:T(8,128)(2,1)}, u32[]{:S(2)}) copy-start(bf16[16,4096]{1,0:T(8,128)(2,1)} %param.12) | copy-start | bytes 393220
  1.3 137.0 %copy-start.1 = (s32[256]{0:T(256)S(1)}, s32[256]{0:T(256)}, u32[]{:S(2)}) copy-start(s32[256]{0:T(256)} %row_request.9) | copy-start | bytes 3076
  5.3 16.4 %collective-permute-start.1 = (bf16[2,128,1024]{2,1,0:T(8,128)(2,1)S(1)}, bf16[2,128,1024]{2,1,0:T(8,128)(2,1)S(1)}, u32[]{:S(2)}, u32[]{:S(2)}) collective-permute-start(bf16[2,128,1024]{2,1,0:T(8,128)(2,1)S(1)} %get-tuple-element.32), channel_id=1, source_target_pairs={{0,10},{2,8},{4,14},{6,12},{8,18},{10,16},{12,22},{14,20},{16,26},... | collective-permute-start | bytes 1572872 | tf_op jit(solution)/shard_map/ppermute | solution.py:59
  7.8 26.9 %collective-permute-start = (bf16[2,128,1024]{2,1,0:T(8,128)(2,1)S(1)}, bf16[2,128,1024]{2,1,0:T(8,128)(2,1)S(1)}, u32[]{:S(2)}, u32[]{:S(2)}) collective-permute-start(bf16[2,128,1024]{2,1,0:T(8,128)(2,1)S(1)} %get-tuple-element.30.rest_0_), channel_id=1, source_target_pairs={{0,8},{2,10},{4,12},{6,14},{8,16},{10,18},{12,20},{14,22},{16,24},... | collective-permute-start | bytes 1572872 | tf_op jit(solution)/shard_map/ppermute | solution.py:59
  15.7 20.3 %collective-permute-start.2 = (bf16[2,128,1024]{2,1,0:T(8,128)(2,1)S(1)}, bf16[2,128,1024]{2,1,0:T(8,128)(2,1)S(1)}, u32[]{:S(2)}, u32[]{:S(2)}) collective-permute-start(bf16[2,128,1024]{2,1,0:T(8,128)(2,1)S(1)} %get-tuple-element.33), channel_id=1, source_target_pairs={{0,2},{2,0},{4,6},{6,4},{8,10},{10,8},{12,14},{14,12},{16,18},{18,... | collective-permute-start | bytes 1572872 | tf_op jit(solution)/shard_map/ppermute | solution.py:59
  16.5 41.9 %collective-permute-start.3 = (bf16[2,128,1024]{2,1,0:T(8,128)(2,1)S(1)}, bf16[2,128,1024]{2,1,0:T(8,128)(2,1)S(1)}, u32[]{:S(2)}, u32[]{:S(2)}) collective-permute-start(bf16[2,128,1024]{2,1,0:T(8,128)(2,1)S(1)} %get-tuple-element.36), channel_id=1, source_target_pairs={{0,16},{2,18},{4,20},{6,22},{8,24},{10,26},{12,28},{14,30},{16,0},... | collective-permute-start | bytes 1572872 | tf_op jit(solution)/shard_map/ppermute | solution.py:59
  17.6 68.5 %collective-permute-start.4 = (bf16[2,128,1024]{2,1,0:T(8,128)(2,1)S(1)}, bf16[2,128,1024]{2,1,0:T(8,128)(2,1)S(1)}, u32[]{:S(2)}, u32[]{:S(2)}) collective-permute-start(bf16[2,128,1024]{2,1,0:T(8,128)(2,1)S(1)} %get-tuple-element.37), channel_id=1, source_target_pairs={{0,24},{2,26},{4,28},{6,30},{8,0},{10,2},{12,4},{14,6},{16,8},{18,... | collective-permute-start | bytes 1572872 | tf_op jit(solution)/shard_map/ppermute | solution.py:59
  21.6 75.5 %collective-permute-start.5 = (bf16[2,128,1024]{2,1,0:T(8,128)(2,1)S(1)}, bf16[2,128,1024]{2,1,0:T(8,128)(2,1)S(1)}, u32[]{:S(2)}, u32[]{:S(2)}) collective-permute-start(bf16[2,128,1024]{2,1,0:T(8,128)(2,1)S(1)} %get-tuple-element.38), channel_id=1, source_target_pairs={{0,12},{2,14},{4,8},{6,10},{8,20},{10,22},{12,16},{14,18},{16,28},... | collective-permute-start | bytes 1572872 | tf_op jit(solution)/shard_map/ppermute | solution.py:59
  34.7 62.6 %collective-permute-start.6 = (bf16[2,128,1024]{2,1,0:T(8,128)(2,1)S(1)}, bf16[2,128,1024]{2,1,0:T(8,128)(2,1)S(1)}, u32[]{:S(2)}, u32[]{:S(2)}) collective-permute-start(bf16[2,128,1024]{2,1,0:T(8,128)(2,1)S(1)} %get-tuple-element.41), channel_id=1, source_target_pairs={{0,4},{2,6},{4,0},{6,2},{8,12},{10,14},{12,8},{14,10},{16,20},{18,... | collective-permute-start | bytes 1572872 | tf_op jit(solution)/shard_map/ppermute | solution.py:59
  36.0 87.4 %collective-permute-start.7 = (bf16[2,128,1024]{2,1,0:T(8,128)(2,1)S(1)}, bf16[2,128,1024]{2,1,0:T(8,128)(2,1)S(1)}, u32[]{:S(2)}, u32[]{:S(2)}) collective-permute-start(bf16[2,128,1024]{2,1,0:T(8,128)(2,1)S(1)} %get-tuple-element.42), channel_id=1, source_target_pairs={{0,18},{2,16},{4,22},{6,20},{8,26},{10,24},{12,30},{14,28},{16,2},... | collective-permute-start | bytes 1572872 | tf_op jit(solution)/shard_map/ppermute | solution.py:59
  58.4 65.0 %collective-permute-start.8 = (bf16[2,128,1024]{2,1,0:T(8,128)(2,1)S(1)}, bf16[2,128,1024]{2,1,0:T(8,128)(2,1)S(1)}, u32[]{:S(2)}, u32[]{:S(2)}) collective-permute-start(bf16[2,128,1024]{2,1,0:T(8,128)(2,1)S(1)} %get-tuple-element.43), channel_id=1, source_target_pairs={{0,26},{2,24},{4,30},{6,28},{8,2},{10,0},{12,6},{14,4},{16,10},{18... | collective-permute-start | bytes 1572872 | tf_op jit(solution)/shard_map/ppermute | solution.py:59
  86.0 49.4 %collective-permute-start.9 = (bf16[2,128,1024]{2,1,0:T(8,128)(2,1)S(1)}, bf16[2,128,1024]{2,1,0:T(8,128)(2,1)S(1)}, u32[]{:S(2)}, u32[]{:S(2)}) collective-permute-start(bf16[2,128,1024]{2,1,0:T(8,128)(2,1)S(1)} %get-tuple-element.46), channel_id=1, source_target_pairs={{0,14},{2,12},{4,10},{6,8},{8,22},{10,20},{12,18},{14,16},{16,30},... | collective-permute-start | bytes 1572872 | tf_op jit(solution)/shard_map/ppermute | solution.py:59
  97.2 50.0 %collective-permute-start.10 = (bf16[2,128,1024]{2,1,0:T(8,128)(2,1)S(1)}, bf16[2,128,1024]{2,1,0:T(8,128)(2,1)S(1)}, u32[]{:S(2)}, u32[]{:S(2)}) collective-permute-start(bf16[2,128,1024]{2,1,0:T(8,128)(2,1)S(1)} %get-tuple-element.47), channel_id=1, source_target_pairs={{0,6},{2,4},{4,2},{6,0},{8,14},{10,12},{12,10},{14,8},{16,22},{18,... | collective-permute-start | bytes 1572872 | tf_op jit(solution)/shard_map/ppermute | solution.py:59
  97.3 61.6 %collective-permute-start.11 = (bf16[2,128,1024]{2,1,0:T(8,128)(2,1)S(1)}, bf16[2,128,1024]{2,1,0:T(8,128)(2,1)S(1)}, u32[]{:S(2)}, u32[]{:S(2)}) collective-permute-start(bf16[2,128,1024]{2,1,0:T(8,128)(2,1)S(1)} %get-tuple-element.48), channel_id=1, source_target_pairs={{0,20},{2,22},{4,16},{6,18},{8,28},{10,30},{12,24},{14,26},{16,4},... | collective-permute-start | bytes 1572872 | tf_op jit(solution)/shard_map/ppermute | solution.py:59
  123.4 37.7 %collective-permute-start.12 = (bf16[2,128,1024]{2,1,0:T(8,128)(2,1)S(1)}, bf16[2,128,1024]{2,1,0:T(8,128)(2,1)S(1)}, u32[]{:S(2)}, u32[]{:S(2)}) collective-permute-start(bf16[2,128,1024]{2,1,0:T(8,128)(2,1)S(1)} %get-tuple-element.51), channel_id=1, source_target_pairs={{0,28},{2,30},{4,24},{6,26},{8,4},{10,6},{12,0},{14,2},{16,12},{18... | collective-permute-start | bytes 1572872 | tf_op jit(solution)/shard_map/ppermute | solution.py:59
  123.4 57.8 %collective-permute-start.13 = (bf16[2,128,1024]{2,1,0:T(8,128)(2,1)S(1)}, bf16[2,128,1024]{2,1,0:T(8,128)(2,1)S(1)}, u32[]{:S(2)}, u32[]{:S(2)}) collective-permute-start(bf16[2,128,1024]{2,1,0:T(8,128)(2,1)S(1)} %get-tuple-element.52), channel_id=1, source_target_pairs={{0,22},{2,20},{4,18},{6,16},{8,30},{10,28},{12,26},{14,24},{16,6},... | collective-permute-start | bytes 1572872 | tf_op jit(solution)/shard_map/ppermute | solution.py:59
  135.5 57.0 %collective-permute-start.14 = (bf16[2,128,1024]{2,1,0:T(8,128)(2,1)S(1)}, bf16[2,128,1024]{2,1,0:T(8,128)(2,1)S(1)}, u32[]{:S(2)}, u32[]{:S(2)}) collective-permute-start(bf16[2,128,1024]{2,1,0:T(8,128)(2,1)S(1)} %get-tuple-element.53), channel_id=1, source_target_pairs={{0,30},{2,28},{4,26},{6,24},{8,6},{10,4},{12,2},{14,0},{16,14},{18... | collective-permute-start | bytes 1572872 | tf_op jit(solution)/shard_map/ppermute | solution.py:59
  158.9 58.2 %copy-start = (bf16[4096,512]{1,0:T(8,128)(2,1)S(1)}, bf16[4096,512]{1,0:T(8,128)(2,1)}, u32[]{:S(2)}) copy-start(bf16[4096,512]{1,0:T(8,128)(2,1)} %out_weight.3) | copy-start | bytes 12582916
  194.9 9.4 %collective-permute-start.15 = (bf16[16,4096]{1,0:T(8,128)(2,1)S(1)}, bf16[16,4096]{1,0:T(8,128)(2,1)S(1)}, u32[]{:S(2)}, u32[]{:S(2)}) collective-permute-start(bf16[16,4096]{1,0:T(8,128)(2,1)S(1)} %get-tuple-element.55.rest_0_), channel_id=1, source_target_pairs={{0,16},{2,18},{4,20},{6,22},{8,24},{10,26},{12,28},{14,30},{16,0},... | collective-permute-start | bytes 393224 | tf_op jit(solution)/shard_map/ppermute | solution.py:64
  195.0 9.3 %collective-permute-start.18 = (bf16[16,4096]{1,0:T(8,128)(2,1)S(1)}, bf16[16,4096]{1,0:T(8,128)(2,1)S(1)}, u32[]{:S(2)}, u32[]{:S(2)}) collective-permute-start(bf16[16,4096]{1,0:T(8,128)(2,1)S(1)} %get-tuple-element.55.rest_0_), channel_id=1, source_target_pairs={{0,4},{2,6},{4,0},{6,2},{8,12},{10,14},{12,8},{14,10},{16,20},{18,... | collective-permute-start | bytes 393224 | tf_op jit(solution)/shard_map/ppermute | solution.py:64
  195.2 10.4 %collective-permute-start.16 = (bf16[16,4096]{1,0:T(8,128)(2,1)S(1)}, bf16[16,4096]{1,0:T(8,128)(2,1)S(1)}, u32[]{:S(2)}, u32[]{:S(2)}) collective-permute-start(bf16[16,4096]{1,0:T(8,128)(2,1)S(1)} %get-tuple-element.55.rest_0_), channel_id=1, source_target_pairs={{0,8},{2,10},{4,12},{6,14},{8,0},{10,2},{12,4},{14,6},{16,24},{18,... | collective-permute-start | bytes 393224 | tf_op jit(solution)/shard_map/ppermute | solution.py:64
  199.7 5.9 %collective-permute-start.22 = (bf16[16,4096]{1,0:T(8,128)(2,1)S(1)}, bf16[16,4096]{1,0:T(8,128)(2,1)S(1)}, u32[]{:S(2)}, u32[]{:S(2)}) collective-permute-start(bf16[16,4096]{1,0:T(8,128)(2,1)S(1)} %get-tuple-element.55.rest_0_), channel_id=1, source_target_pairs={{0,2},{2,0},{4,6},{6,4},{8,10},{10,8},{12,14},{14,12},{16,18},{18,... | collective-permute-start | bytes 393224 | tf_op jit(solution)/shard_map/ppermute | solution.py:64
  204.3 5.4 %collective-permute-start.17 = (bf16[16,4096]{1,0:T(8,128)(2,1)S(1)}, bf16[16,4096]{1,0:T(8,128)(2,1)S(1)}, u32[]{:S(2)}, u32[]{:S(2)}) collective-permute-start(bf16[16,4096]{1,0:T(8,128)(2,1)S(1)} %collective-permute-done.15.rest_1_), channel_id=1, source_target_pairs={{0,8},{2,10},{4,12},{6,14},{8,0},{10,2},{12,4},{14,6},{16,24},{18,... | collective-permute-start | bytes 393224 | tf_op jit(solution)/shard_map/ppermute | solution.py:64
  204.3 5.4 %collective-permute-start.26 = (bf16[16,4096]{1,0:T(8,128)(2,1)S(1)}, bf16[16,4096]{1,0:T(8,128)(2,1)S(1)}, u32[]{:S(2)}, u32[]{:S(2)}) collective-permute-start(bf16[16,4096]{1,0:T(8,128)(2,1)S(1)} %collective-permute-done.18.rest_4_), channel_id=1, source_target_pairs={{0,2},{2,0},{4,6},{6,4},{8,10},{10,8},{12,14},{14,12},{16,18},{18,... | collective-permute-start | bytes 393224 | tf_op jit(solution)/shard_map/ppermute | solution.py:64
  205.6 4.1 %collective-permute-start.24 = (bf16[16,4096]{1,0:T(8,128)(2,1)S(1)}, bf16[16,4096]{1,0:T(8,128)(2,1)S(1)}, u32[]{:S(2)}, u32[]{:S(2)}) collective-permute-start(bf16[16,4096]{1,0:T(8,128)(2,1)S(1)} %collective-permute-done.16.rest_2_), channel_id=1, source_target_pairs={{0,2},{2,0},{4,6},{6,4},{8,10},{10,8},{12,14},{14,12},{16,18},{18,... | collective-permute-start | bytes 393224 | tf_op jit(solution)/shard_map/ppermute | solution.py:64
  205.6 6.3 %collective-permute-start.20 = (bf16[16,4096]{1,0:T(8,128)(2,1)S(1)}, bf16[16,4096]{1,0:T(8,128)(2,1)S(1)}, u32[]{:S(2)}, u32[]{:S(2)}) collective-permute-start(bf16[16,4096]{1,0:T(8,128)(2,1)S(1)} %collective-permute-done.16.rest_2_), channel_id=1, source_target_pairs={{0,4},{2,6},{4,0},{6,2},{8,12},{10,14},{12,8},{14,10},{16,20},{18,... | collective-permute-start | bytes 393224 | tf_op jit(solution)/shard_map/ppermute | solution.py:64
  205.6 9.1 %collective-permute-start.19 = (bf16[16,4096]{1,0:T(8,128)(2,1)S(1)}, bf16[16,4096]{1,0:T(8,128)(2,1)S(1)}, u32[]{:S(2)}, u32[]{:S(2)}) collective-permute-start(bf16[16,4096]{1,0:T(8,128)(2,1)S(1)} %collective-permute-done.15.rest_1_), channel_id=1, source_target_pairs={{0,4},{2,6},{4,0},{6,2},{8,12},{10,14},{12,8},{14,10},{16,20},{18,... | collective-permute-start | bytes 393224 | tf_op jit(solution)/shard_map/ppermute | solution.py:64
  209.7 7.4 %collective-permute-start.21 = (bf16[16,4096]{1,0:T(8,128)(2,1)S(1)}, bf16[16,4096]{1,0:T(8,128)(2,1)S(1)}, u32[]{:S(2)}, u32[]{:S(2)}) collective-permute-start(bf16[16,4096]{1,0:T(8,128)(2,1)S(1)} %collective-permute-done.17.rest_3_), channel_id=1, source_target_pairs={{0,4},{2,6},{4,0},{6,2},{8,12},{10,14},{12,8},{14,10},{16,20},{18,... | collective-permute-start | bytes 393224 | tf_op jit(solution)/shard_map/ppermute | solution.py:64
  209.7 9.6 %collective-permute-start.23 = (bf16[16,4096]{1,0:T(8,128)(2,1)S(1)}, bf16[16,4096]{1,0:T(8,128)(2,1)S(1)}, u32[]{:S(2)}, u32[]{:S(2)}) collective-permute-start(bf16[16,4096]{1,0:T(8,128)(2,1)S(1)} %collective-permute-done.15.rest_1_), channel_id=1, source_target_pairs={{0,2},{2,0},{4,6},{6,4},{8,10},{10,8},{12,14},{14,12},{16,18},{18,... | collective-permute-start | bytes 393224 | tf_op jit(solution)/shard_map/ppermute | solution.py:64
  209.7 9.6 %collective-permute-start.25 = (bf16[16,4096]{1,0:T(8,128)(2,1)S(1)}, bf16[16,4096]{1,0:T(8,128)(2,1)S(1)}, u32[]{:S(2)}, u32[]{:S(2)}) collective-permute-start(bf16[16,4096]{1,0:T(8,128)(2,1)S(1)} %collective-permute-done.17.rest_3_), channel_id=1, source_target_pairs={{0,2},{2,0},{4,6},{6,4},{8,10},{10,8},{12,14},{14,12},{16,18},{18,... | collective-permute-start | bytes 393224 | tf_op jit(solution)/shard_map/ppermute | solution.py:64
  211.9 7.4 %collective-permute-start.28 = (bf16[16,4096]{1,0:T(8,128)(2,1)S(1)}, bf16[16,4096]{1,0:T(8,128)(2,1)S(1)}, u32[]{:S(2)}, u32[]{:S(2)}) collective-permute-start(bf16[16,4096]{1,0:T(8,128)(2,1)S(1)} %collective-permute-done.20.rest_6_), channel_id=1, source_target_pairs={{0,2},{2,0},{4,6},{6,4},{8,10},{10,8},{12,14},{14,12},{16,18},{18,... | collective-permute-start | bytes 393224 | tf_op jit(solution)/shard_map/ppermute | solution.py:64
  214.7 4.6 %collective-permute-start.27 = (bf16[16,4096]{1,0:T(8,128)(2,1)S(1)}, bf16[16,4096]{1,0:T(8,128)(2,1)S(1)}, u32[]{:S(2)}, u32[]{:S(2)}) collective-permute-start(bf16[16,4096]{1,0:T(8,128)(2,1)S(1)} %collective-permute-done.19.rest_5_), channel_id=1, source_target_pairs={{0,2},{2,0},{4,6},{6,4},{8,10},{10,8},{12,14},{14,12},{16,18},{18,... | collective-permute-start | bytes 393224 | tf_op jit(solution)/shard_map/ppermute | solution.py:64
  217.1 2.2 collective-permute-start.29
  221.8 6.0 %collective-permute-start.30 = (bf16[128,512]{1,0:T(8,128)(2,1)S(1)}, bf16[128,512]{1,0:T(8,128)(2,1)S(1)}, u32[]{:S(2)}, u32[]{:S(2)}) collective-permute-start(bf16[128,512]{1,0:T(8,128)(2,1)S(1)} %get-tuple-element.57), channel_id=1, source_target_pairs={{0,1},{1,0},{2,3},{3,2},{4,5},{5,4},{6,7},{7,6},{8,9},{9,8},{10,11... | collective-permute-start | bytes 393224 | tf_op jit(solution)/shard_map/ppermute | solution.py:403

commit v13 on v12

--- a/solution.py
+++ b/solution.py
@@ -27,12 +27,13 @@
 
 def page_rounds(dims):
     far, near = dims
-    single, longer = [(1, n) for n in range(near)], [(z, n) for n in range(near) for z in range(2, far)]
-    order, near_left = single[:2], [(0, n) for n in range(1, near)]
-    single = single[2:]
-    while longer or single or near_left:
-        order += near_left[:1] + longer[: max(far - 2, 1)] + single[:1]
-        near_left, longer, single = near_left[1:], longer[max(far - 2, 1) :], single[1:]
+    half = max(near // 2, 1)
+    order = []
+    for low in range(0, near, half):
+        swaps = range(low, min(low + half, near))
+        opening = [(1, n) for n in swaps] if low == 0 else [(z, n) for n in swaps for z in (1, 0)]
+        rest = [(z, n) for n in swaps for z in range(2, far)]
+        order += opening + ([(0, n) for n in swaps if n] if low == 0 else []) + rest
     return [uniform(z, n, dims) for z, n in order]
 
 

time: 228 us -> 226 us (level)
  starting transfers between devices: 104 us -> 86 us
  waiting for transfers between devices: 93.8 us -> 108 us
    ppermute x15, starting transfers between devices: 95.2 us -> 61.5 us  [send_by(): return lax.ppermute(array, 'group', pairs)]
    ppermute x15, waiting for transfers between devices: 74.5 us -> 96.7 us  [send_by(): return lax.ppermute(array, 'group', pairs)]
    ppermute x15, starting transfers between devices: 7.34 us -> 22.8 us  [swap(): return lax.ppermute(array, 'group', [(s, s ^ mask) for s in range(groups)])]
    ppermute x15, waiting for transfers between devices: 14.8 us -> 7.51 us  [swap(): return lax.ppermute(array, 'group', [(s, s ^ mask) for s in range(groups)])]
  transfers between devices with their start and end apart: 31 -> 31, of which waited for: 13 -> 11; matrix products, arithmetic and copies ran while one was open for 0% -> 0% of each run, Pallas kernels for 9% -> 9%
where the time goes in v13:
time: 226 us
  waiting for transfers between devices  108 us (48%)
  starting transfers between devices  86 us (38%)
  Pallas kernels  29.6 us (13%)
    ppermute x15, waiting for transfers between devices, send_by(): return lax.ppermute(array, 'group', pairs)  96.7 us
    ppermute x15, starting transfers between devices, send_by(): return lax.ppermute(array, 'group', pairs)  61.5 us
    ppermute x15, starting transfers between devices, swap(): return lax.ppermute(array, 'group', [(s, s ^ mask) for s in range(groups)])  22.8 us
    pallas_call x5, Pallas kernels, settle(): pl.pallas_call(functools.partial(settle_kernel, dims, routes, own, last),...  14.5 us
    pallas_call x2, Pallas kernels, prepare(): pl.pallas_call(functools.partial(prepare_kernel, dims, routes, own), out_...  10.5 us
    ppermute x15, waiting for transfers between devices, swap(): return lax.ppermute(array, 'group', [(s, s ^ mask) for s in range(groups)])  7.51 us
    pallas_call x2, Pallas kernels, call(): pl.pallas_call(kernel, out_shape=outs, in_specs=[vmem] * (1 + len(extra))...  4.6 us
  transfers between devices with their start and end apart: 31, of which 11 were waited for; matrix products, arithmetic and copies ran while one was open for 0% of the time, Pallas kernels for 9%

profile of v13, /device:TPU:0, one launch (start us, length us, event | category | flops | bytes accessed | tf_op | source)
XLA Modules:
  0.0 226.3 jit_solution(912476866320894149)
XLA Ops:
  0.6 0.7 or_or_fusion.table_hbm.table
  1.4 4.0 %outgoing_pages.2 = (bf16[2,128,1024]{2,1,0:T(8,128)(2,1)S(1)}, bf16[2,128,1024]{2,1,0:T(8,128)(2,1)S(1)}) custom-call(s32[256]{0:T(256)S(1)} %or_or_fusion.table_hbm.table, bf16[32,128,1024]{2,1,0:T(8,128)(2,1)} %pool.3), custom_call_target="tpu_custom_call" | custom-call | bytes 2097152 | tf_op jit(solution)/shard_map/outgoing_pages/pallas_call | solution.py:156
  5.3 2.4 %collective-permute-start.1 = (bf16[2,128,1024]{2,1,0:T(8,128)(2,1)S(1)}, bf16[2,128,1024]{2,1,0:T(8,128)(2,1)S(1)}, u32[]{:S(2)}, u32[]{:S(2)}) collective-permute-start(bf16[2,128,1024]{2,1,0:T(8,128)(2,1)S(1)} %get-tuple-element.32), channel_id=1, source_target_pairs={{0,10},{2,8},{4,14},{6,12},{8,18},{10,16},{12,22},{14,20},{16,26},... | collective-permute-start | bytes 1572872 | tf_op jit(solution)/shard_map/ppermute | solution.py:60
  7.8 1.7 collective-permute-start
  9.5 6.5 %outgoing_pages.3 = (bf16[32,128,1024]{2,1,0:T(8,128)(2,1)}, bf16[2,128,1024]{2,1,0:T(8,128)(2,1)S(1)}, bf16[2,128,1024]{2,1,0:T(8,128)(2,1)S(1)}, bf16[2,128,10...) custom-call(s32[256]{0:T(256)S(1)} %or_or_fusion.table_hbm.table, ...), custom_call_target="tpu_custom_call" | custom-call | bytes 14680064 | tf_op jit(solution)/shard_map/outgoing_pages/pallas_call | solution.py:156
  16.0 0.2 collective-permute-start.2
  16.2 1.4 collective-permute-start.3
  17.6 2.6 %collective-permute-start.4 = (bf16[2,128,1024]{2,1,0:T(8,128)(2,1)S(1)}, bf16[2,128,1024]{2,1,0:T(8,128)(2,1)S(1)}, u32[]{:S(2)}, u32[]{:S(2)}) collective-permute-start(bf16[2,128,1024]{2,1,0:T(8,128)(2,1)S(1)} %get-tuple-element.37), channel_id=1, source_target_pairs={{0,24},{2,26},{4,28},{6,30},{8,0},{10,2},{12,4},{14,6},{16,8},{18,... | collective-permute-start | bytes 1572872 | tf_op jit(solution)/shard_map/ppermute | solution.py:60
  20.2 1.5 collective-permute-done.1.rest_1_
  21.7 1.6 collective-permute-start.5
  23.3 11.3 %collective-permute-done.rest_0_ = bf16[2,128,1024]{2,1,0:T(8,128)(2,1)S(1)} collective-permute-done((bf16[2,128,1024]{2,1,0:T(8,128)(2,1)S(1)}, bf16[2,128,1024]{2,1,0:T(8,128)(2,1)S(1)}, u32[]{:S(2)}, u32[]{:S(2)}) %collective-permute-start) | collective-permute-done | bytes 524320 | tf_op jit(solution)/shard_map/ppermute | solution.py:60
  34.6 1.0 collective-permute-start.6
  35.6 0.9 collective-permute-start.7
  36.5 20.6 %collective-permute-done.3.rest_0_ = bf16[2,128,1024]{2,1,0:T(8,128)(2,1)S(1)} collective-permute-done((bf16[2,128,1024]{2,1,0:T(8,128)(2,1)S(1)}, bf16[2,128,1024]{2,1,0:T(8,128)(2,1)S(1)}, u32[]{:S(2)}, u32[]{:S(2)}) %collective-permute-start.3) | collective-permute-done | bytes 524320 | tf_op jit(solution)/shard_map/ppermute | solution.py:60
  57.0 1.5 collective-permute-start.8
  58.5 31.5 %collective-permute-start.9 = (bf16[2,128,1024]{2,1,0:T(8,128)(2,1)S(1)}, bf16[2,128,1024]{2,1,0:T(8,128)(2,1)S(1)}, u32[]{:S(2)}, u32[]{:S(2)}) collective-permute-start(bf16[2,128,1024]{2,1,0:T(8,128)(2,1)S(1)} %get-tuple-element.46), channel_id=1, source_target_pairs={{0,14},{2,12},{4,10},{6,8},{8,22},{10,20},{12,18},{14,16},{16,30},... | collective-permute-start | bytes 1572872 | tf_op jit(solution)/shard_map/ppermute | solution.py:60
  90.0 22.3 %collective-permute-done.5.rest_2_ = bf16[2,128,1024]{2,1,0:T(8,128)(2,1)S(1)} collective-permute-done((bf16[2,128,1024]{2,1,0:T(8,128)(2,1)S(1)}, bf16[2,128,1024]{2,1,0:T(8,128)(2,1)S(1)}, u32[]{:S(2)}, u32[]{:S(2)}) %collective-permute-start.5) | collective-permute-done | bytes 524320 | tf_op jit(solution)/shard_map/ppermute | solution.py:60
  112.3 1.6 collective-permute-start.10
  113.9 10.6 %collective-permute-start.11 = (bf16[2,128,1024]{2,1,0:T(8,128)(2,1)S(1)}, bf16[2,128,1024]{2,1,0:T(8,128)(2,1)S(1)}, u32[]{:S(2)}, u32[]{:S(2)}) collective-permute-start(bf16[2,128,1024]{2,1,0:T(8,128)(2,1)S(1)} %get-tuple-element.48), channel_id=1, source_target_pairs={{0,20},{2,22},{4,16},{6,18},{8,28},{10,30},{12,24},{14,26},{16,4},... | collective-permute-start | bytes 1572872 | tf_op jit(solution)/shard_map/ppermute | solution.py:60
  124.5 2.9 %collective-permute-start.12 = (bf16[2,128,1024]{2,1,0:T(8,128)(2,1)S(1)}, bf16[2,128,1024]{2,1,0:T(8,128)(2,1)S(1)}, u32[]{:S(2)}, u32[]{:S(2)}) collective-permute-start(bf16[2,128,1024]{2,1,0:T(8,128)(2,1)S(1)} %get-tuple-element.51), channel_id=1, source_target_pairs={{0,28},{2,30},{4,24},{6,26},{8,4},{10,6},{12,0},{14,2},{16,12},{18... | collective-permute-start | bytes 1572872 | tf_op jit(solution)/shard_map/ppermute | solution.py:60
  127.4 1.7 collective-permute-start.14
  129.1 4.4 %settle_pages.5 = (bf16[32,128,1024]{2,1,0:T(8,128)(2,1)}, f32[16,32,128]{2,1,0:T(8,128)S(1)}) custom-call(s32[256]{0:T(256)S(1)} %or_or_fusion.table_hbm.table, s32[256]{0:T(256)S(1)} %copy-done.1, bf16[16,32,128]{2,1,0:T(8,128)(2,1)S(1)} %bitcast.2, f32[16,32,128]{2,1,0:T(8,128)S(1)} %broadcast_in_dim.3.rows_in, ...), custom_call_target="tpu_custom_call", output_to_operand_aliasing={{0}: (4, {})} | custom-call | flops 1073741824 | bytes 3145728 | tf_op jit(solution)/shard_map/settle_pages/pallas_call | solution.py:275
  133.5 2.2 settle_pages.6
  135.7 2.0 settle_pages.7
  137.7 22.1 %collective-permute-done.10.rest_1_ = bf16[2,128,1024]{2,1,0:T(8,128)(2,1)S(1)} collective-permute-done((bf16[2,128,1024]{2,1,0:T(8,128)(2,1)S(1)}, bf16[2,128,1024]{2,1,0:T(8,128)(2,1)S(1)}, u32[]{:S(2)}, u32[]{:S(2)}) %collective-permute-start.10) | collective-permute-done | bytes 524320 | tf_op jit(solution)/shard_map/ppermute | solution.py:60
  159.8 2.2 settle_pages.8
  162.0 18.9 %collective-permute-done.13.rest_1_ = bf16[2,128,1024]{2,1,0:T(8,128)(2,1)S(1)} collective-permute-done((bf16[2,128,1024]{2,1,0:T(8,128)(2,1)S(1)}, bf16[2,128,1024]{2,1,0:T(8,128)(2,1)S(1)}, u32[]{:S(2)}, u32[]{:S(2)}) %collective-permute-start.13) | collective-permute-done | bytes 524320 | tf_op jit(solution)/shard_map/ppermute | solution.py:60
  181.0 3.7 %settle_pages.9 = (bf16[32,128,1024]{2,1,0:T(8,128)(2,1)}, bf16[16,4096]{1,0:T(8,128)(2,1)S(1)}) custom-call(s32[256]{0:T(256)S(1)} %or_or_fusion.table_hbm.table, s32[256]{0:T(256)S(1)} %copy-done.1, bf16[16,32,128]{2,1,0:T(8,128)(2,1)S(1)} %bitcast.6, f32[16,32,128]{2,1,0:T(8,128)S(1)} %get-tuple-element.49.rows_in, ...), custom_call_target="tpu_custom_call", output_to_operand_aliasing={{0}: (4, {})} | custom-call | flops 1073741824 | bytes 3145728 | tf_op jit(solution)/shard_map/settle_pages/pallas_call | solution.py:275
  184.7 8.9 %collective-permute-start.15 = (bf16[16,4096]{1,0:T(8,128)(2,1)S(1)}, bf16[16,4096]{1,0:T(8,128)(2,1)S(1)}, u32[]{:S(2)}, u32[]{:S(2)}) collective-permute-start(bf16[16,4096]{1,0:T(8,128)(2,1)S(1)} %get-tuple-element.55.rest_0_), channel_id=1, source_target_pairs={{0,16},{2,18},{4,20},{6,22},{8,24},{10,26},{12,28},{14,30},{16,0},... | collective-permute-start | bytes 393224 | tf_op jit(solution)/shard_map/ppermute | solution.py:65
  193.6 1.8 collective-permute-start.18
  195.4 3.5 %collective-permute-start.16 = (bf16[16,4096]{1,0:T(8,128)(2,1)S(1)}, bf16[16,4096]{1,0:T(8,128)(2,1)S(1)}, u32[]{:S(2)}, u32[]{:S(2)}) collective-permute-start(bf16[16,4096]{1,0:T(8,128)(2,1)S(1)} %get-tuple-element.55.rest_0_), channel_id=1, source_target_pairs={{0,8},{2,10},{4,12},{6,14},{8,0},{10,2},{12,4},{14,6},{16,24},{18,... | collective-permute-start | bytes 393224 | tf_op jit(solution)/shard_map/ppermute | solution.py:65
  199.0 0.8 collective-permute-start.22
  199.8 2.8 %collective-permute-start.17 = (bf16[16,4096]{1,0:T(8,128)(2,1)S(1)}, bf16[16,4096]{1,0:T(8,128)(2,1)S(1)}, u32[]{:S(2)}, u32[]{:S(2)}) collective-permute-start(bf16[16,4096]{1,0:T(8,128)(2,1)S(1)} %collective-permute-done.15.rest_1_), channel_id=1, source_target_pairs={{0,8},{2,10},{4,12},{6,14},{8,0},{10,2},{12,4},{14,6},{16,24},{18,... | collective-permute-start | bytes 393224 | tf_op jit(solution)/shard_map/ppermute | solution.py:65
  202.6 0.9 collective-permute-start.26
  203.5 0.1 collective-permute-start.24
  203.5 2.0 collective-permute-start.20
  205.6 0.0 collective-permute-start.19
  205.6 0.9 collective-permute-done.17.rest_3_
  206.5 1.4 collective-permute-start.21
  207.9 0.5 collective-permute-start.25
  208.4 1.4 collective-permute-done.20.rest_6_
  209.9 2.8 %collective-permute-done.19.rest_5_ = bf16[16,4096]{1,0:T(8,128)(2,1)S(1)} collective-permute-done((bf16[16,4096]{1,0:T(8,128)(2,1)S(1)}, bf16[16,4096]{1,0:T(8,128)(2,1)S(1)}, u32[]{:S(2)}, u32[]{:S(2)}) %collective-permute-start.19) | collective-permute-done | bytes 131104 | tf_op jit(solution)/shard_map/ppermute | solution.py:65
  212.7 2.3 %collective-permute-done.21.rest_7_ = bf16[16,4096]{1,0:T(8,128)(2,1)S(1)} collective-permute-done((bf16[16,4096]{1,0:T(8,128)(2,1)S(1)}, bf16[16,4096]{1,0:T(8,128)(2,1)S(1)}, u32[]{:S(2)}, u32[]{:S(2)}) %collective-permute-start.21) | collective-permute-done | bytes 131104 | tf_op jit(solution)/shard_map/ppermute | solution.py:65
  215.0 2.1 project_some_rows.1.some
  217.2 2.5 %project_rows.1 = (f32[128,512]{1,0:T(8,128)S(1)}, bf16[128,512]{1,0:T(8,128)(2,1)S(1)}) custom-call(bf16[4096,512]{1,0:T(8,128)(2,1)S(1)} %copy-done, f32[128,512]{1,0:T(8,128)S(1)} %project_some_rows.1.some, bf16[16,4096]{1,0:T(8,128)(2,1)S(1)} %collective-permute-done.22.rest_0_, bf16[16,4096]{1,0:T(8,128)(2,1)S(1)} %collective-permute-done.23.rest_1_, ...), custom_call_target="tpu_custom_call" | custom-call | flops 536870912 | bytes 4194304 | tf_op jit(solution)/shard_map/project_rows/pallas_call | solution.py:349
  219.7 1.7 collective-permute-start.30
  221.4 4.2 %collective-permute-done.30 = bf16[128,512]{1,0:T(8,128)(2,1)S(1)} collective-permute-done((bf16[128,512]{1,0:T(8,128)(2,1)S(1)}, bf16[128,512]{1,0:T(8,128)(2,1)S(1)}, u32[]{:S(2)}, u32[]{:S(2)}) %collective-permute-start.30) | collective-permute-done | bytes 131104 | tf_op jit(solution)/shard_map/ppermute | solution.py:404
  225.6 0.7 add_convert_fusion
  (33 shorter events, 0.1 us)
Async XLA Ops:
  1.3 127.7 %copy-start.2 = (bf16[16,4096]{1,0:T(8,128)(2,1)S(1)}, bf16[16,4096]{1,0:T(8,128)(2,1)}, u32[]{:S(2)}) copy-start(bf16[16,4096]{1,0:T(8,128)(2,1)} %param.12) | copy-start | bytes 393220
  1.3 127.7 %copy-start.1 = (s32[256]{0:T(256)S(1)}, s32[256]{0:T(256)}, u32[]{:S(2)}) copy-start(s32[256]{0:T(256)} %row_request.9) | copy-start | bytes 3076
  5.3 16.4 %collective-permute-start.1 = (bf16[2,128,1024]{2,1,0:T(8,128)(2,1)S(1)}, bf16[2,128,1024]{2,1,0:T(8,128)(2,1)S(1)}, u32[]{:S(2)}, u32[]{:S(2)}) collective-permute-start(bf16[2,128,1024]{2,1,0:T(8,128)(2,1)S(1)} %get-tuple-element.32), channel_id=1, source_target_pairs={{0,10},{2,8},{4,14},{6,12},{8,18},{10,16},{12,22},{14,20},{16,26},... | collective-permute-start | bytes 1572872 | tf_op jit(solution)/shard_map/ppermute | solution.py:60
  7.8 26.8 %collective-permute-start = (bf16[2,128,1024]{2,1,0:T(8,128)(2,1)S(1)}, bf16[2,128,1024]{2,1,0:T(8,128)(2,1)S(1)}, u32[]{:S(2)}, u32[]{:S(2)}) collective-permute-start(bf16[2,128,1024]{2,1,0:T(8,128)(2,1)S(1)} %get-tuple-element.30.rest_0_), channel_id=1, source_target_pairs={{0,8},{2,10},{4,12},{6,14},{8,16},{10,18},{12,20},{14,22},{16,24},... | collective-permute-start | bytes 1572872 | tf_op jit(solution)/shard_map/ppermute | solution.py:60
  16.0 19.6 %collective-permute-start.2 = (bf16[2,128,1024]{2,1,0:T(8,128)(2,1)S(1)}, bf16[2,128,1024]{2,1,0:T(8,128)(2,1)S(1)}, u32[]{:S(2)}, u32[]{:S(2)}) collective-permute-start(bf16[2,128,1024]{2,1,0:T(8,128)(2,1)S(1)} %get-tuple-element.33), channel_id=1, source_target_pairs={{0,2},{2,0},{4,6},{6,4},{8,10},{10,8},{12,14},{14,12},{16,18},{18,... | collective-permute-start | bytes 1572872 | tf_op jit(solution)/shard_map/ppermute | solution.py:60
  16.2 40.9 %collective-permute-start.3 = (bf16[2,128,1024]{2,1,0:T(8,128)(2,1)S(1)}, bf16[2,128,1024]{2,1,0:T(8,128)(2,1)S(1)}, u32[]{:S(2)}, u32[]{:S(2)}) collective-permute-start(bf16[2,128,1024]{2,1,0:T(8,128)(2,1)S(1)} %get-tuple-element.36), channel_id=1, source_target_pairs={{0,16},{2,18},{4,20},{6,22},{8,24},{10,26},{12,28},{14,30},{16,0},... | collective-permute-start | bytes 1572872 | tf_op jit(solution)/shard_map/ppermute | solution.py:60
  17.6 41.0 %collective-permute-start.4 = (bf16[2,128,1024]{2,1,0:T(8,128)(2,1)S(1)}, bf16[2,128,1024]{2,1,0:T(8,128)(2,1)S(1)}, u32[]{:S(2)}, u32[]{:S(2)}) collective-permute-start(bf16[2,128,1024]{2,1,0:T(8,128)(2,1)S(1)} %get-tuple-element.37), channel_id=1, source_target_pairs={{0,24},{2,26},{4,28},{6,30},{8,0},{10,2},{12,4},{14,6},{16,8},{18,... | collective-permute-start | bytes 1572872 | tf_op jit(solution)/shard_map/ppermute | solution.py:60
  21.7 90.6 %collective-permute-start.5 = (bf16[2,128,1024]{2,1,0:T(8,128)(2,1)S(1)}, bf16[2,128,1024]{2,1,0:T(8,128)(2,1)S(1)}, u32[]{:S(2)}, u32[]{:S(2)}) collective-permute-start(bf16[2,128,1024]{2,1,0:T(8,128)(2,1)S(1)} %get-tuple-element.38), channel_id=1, source_target_pairs={{0,18},{2,16},{4,22},{6,20},{8,26},{10,24},{12,30},{14,28},{16,2},... | collective-permute-start | bytes 1572872 | tf_op jit(solution)/shard_map/ppermute | solution.py:60
  34.6 79.3 %collective-permute-start.6 = (bf16[2,128,1024]{2,1,0:T(8,128)(2,1)S(1)}, bf16[2,128,1024]{2,1,0:T(8,128)(2,1)S(1)}, u32[]{:S(2)}, u32[]{:S(2)}) collective-permute-start(bf16[2,128,1024]{2,1,0:T(8,128)(2,1)S(1)} %get-tuple-element.41), channel_id=1, source_target_pairs={{0,26},{2,24},{4,30},{6,28},{8,2},{10,0},{12,6},{14,4},{16,10},{18... | collective-permute-start | bytes 1572872 | tf_op jit(solution)/shard_map/ppermute | solution.py:60
  35.6 88.9 %collective-permute-start.7 = (bf16[2,128,1024]{2,1,0:T(8,128)(2,1)S(1)}, bf16[2,128,1024]{2,1,0:T(8,128)(2,1)S(1)}, u32[]{:S(2)}, u32[]{:S(2)}) collective-permute-start(bf16[2,128,1024]{2,1,0:T(8,128)(2,1)S(1)} %get-tuple-element.42), channel_id=1, source_target_pairs={{0,12},{2,14},{4,8},{6,10},{8,20},{10,22},{12,16},{14,18},{16,28},... | collective-permute-start | bytes 1572872 | tf_op jit(solution)/shard_map/ppermute | solution.py:60
  57.0 70.3 %collective-permute-start.8 = (bf16[2,128,1024]{2,1,0:T(8,128)(2,1)S(1)}, bf16[2,128,1024]{2,1,0:T(8,128)(2,1)S(1)}, u32[]{:S(2)}, u32[]{:S(2)}) collective-permute-start(bf16[2,128,1024]{2,1,0:T(8,128)(2,1)S(1)} %get-tuple-element.43), channel_id=1, source_target_pairs={{0,4},{2,6},{4,0},{6,2},{8,12},{10,14},{12,8},{14,10},{16,20},{18,... | collective-permute-start | bytes 1572872 | tf_op jit(solution)/shard_map/ppermute | solution.py:60
  58.5 68.8 %collective-permute-start.9 = (bf16[2,128,1024]{2,1,0:T(8,128)(2,1)S(1)}, bf16[2,128,1024]{2,1,0:T(8,128)(2,1)S(1)}, u32[]{:S(2)}, u32[]{:S(2)}) collective-permute-start(bf16[2,128,1024]{2,1,0:T(8,128)(2,1)S(1)} %get-tuple-element.46), channel_id=1, source_target_pairs={{0,14},{2,12},{4,10},{6,8},{8,22},{10,20},{12,18},{14,16},{16,30},... | collective-permute-start | bytes 1572872 | tf_op jit(solution)/shard_map/ppermute | solution.py:60
  112.3 47.6 %collective-permute-start.10 = (bf16[2,128,1024]{2,1,0:T(8,128)(2,1)S(1)}, bf16[2,128,1024]{2,1,0:T(8,128)(2,1)S(1)}, u32[]{:S(2)}, u32[]{:S(2)}) collective-permute-start(bf16[2,128,1024]{2,1,0:T(8,128)(2,1)S(1)} %get-tuple-element.47), channel_id=1, source_target_pairs={{0,6},{2,4},{4,2},{6,0},{8,14},{10,12},{12,10},{14,8},{16,22},{18,... | collective-permute-start | bytes 1572872 | tf_op jit(solution)/shard_map/ppermute | solution.py:60
  113.9 45.9 %collective-permute-start.11 = (bf16[2,128,1024]{2,1,0:T(8,128)(2,1)S(1)}, bf16[2,128,1024]{2,1,0:T(8,128)(2,1)S(1)}, u32[]{:S(2)}, u32[]{:S(2)}) collective-permute-start(bf16[2,128,1024]{2,1,0:T(8,128)(2,1)S(1)} %get-tuple-element.48), channel_id=1, source_target_pairs={{0,20},{2,22},{4,16},{6,18},{8,28},{10,30},{12,24},{14,26},{16,4},... | collective-permute-start | bytes 1572872 | tf_op jit(solution)/shard_map/ppermute | solution.py:60
  124.5 37.5 %collective-permute-start.12 = (bf16[2,128,1024]{2,1,0:T(8,128)(2,1)S(1)}, bf16[2,128,1024]{2,1,0:T(8,128)(2,1)S(1)}, u32[]{:S(2)}, u32[]{:S(2)}) collective-permute-start(bf16[2,128,1024]{2,1,0:T(8,128)(2,1)S(1)} %get-tuple-element.51), channel_id=1, source_target_pairs={{0,28},{2,30},{4,24},{6,26},{8,4},{10,6},{12,0},{14,2},{16,12},{18... | collective-permute-start | bytes 1572872 | tf_op jit(solution)/shard_map/ppermute | solution.py:60
  127.3 53.6 %collective-permute-start.13 = (bf16[2,128,1024]{2,1,0:T(8,128)(2,1)S(1)}, bf16[2,128,1024]{2,1,0:T(8,128)(2,1)S(1)}, u32[]{:S(2)}, u32[]{:S(2)}) collective-permute-start(bf16[2,128,1024]{2,1,0:T(8,128)(2,1)S(1)} %get-tuple-element.52), channel_id=1, source_target_pairs={{0,22},{2,20},{4,18},{6,16},{8,30},{10,28},{12,26},{14,24},{16,6},... | collective-permute-start | bytes 1572872 | tf_op jit(solution)/shard_map/ppermute | solution.py:60
  127.4 53.6 %collective-permute-start.14 = (bf16[2,128,1024]{2,1,0:T(8,128)(2,1)S(1)}, bf16[2,128,1024]{2,1,0:T(8,128)(2,1)S(1)}, u32[]{:S(2)}, u32[]{:S(2)}) collective-permute-start(bf16[2,128,1024]{2,1,0:T(8,128)(2,1)S(1)} %get-tuple-element.53), channel_id=1, source_target_pairs={{0,30},{2,28},{4,26},{6,24},{8,6},{10,4},{12,2},{14,0},{16,14},{18... | collective-permute-start | bytes 1572872 | tf_op jit(solution)/shard_map/ppermute | solution.py:60
  159.8 55.2 %copy-start = (bf16[4096,512]{1,0:T(8,128)(2,1)S(1)}, bf16[4096,512]{1,0:T(8,128)(2,1)}, u32[]{:S(2)}) copy-start(bf16[4096,512]{1,0:T(8,128)(2,1)} %out_weight.3) | copy-start | bytes 12582916
  184.7 15.0 %collective-permute-start.15 = (bf16[16,4096]{1,0:T(8,128)(2,1)S(1)}, bf16[16,4096]{1,0:T(8,128)(2,1)S(1)}, u32[]{:S(2)}, u32[]{:S(2)}) collective-permute-start(bf16[16,4096]{1,0:T(8,128)(2,1)S(1)} %get-tuple-element.55.rest_0_), channel_id=1, source_target_pairs={{0,16},{2,18},{4,20},{6,22},{8,24},{10,26},{12,28},{14,30},{16,0},... | collective-permute-start | bytes 393224 | tf_op jit(solution)/shard_map/ppermute | solution.py:65
  193.6 8.9 %collective-permute-start.18 = (bf16[16,4096]{1,0:T(8,128)(2,1)S(1)}, bf16[16,4096]{1,0:T(8,128)(2,1)S(1)}, u32[]{:S(2)}, u32[]{:S(2)}) collective-permute-start(bf16[16,4096]{1,0:T(8,128)(2,1)S(1)} %get-tuple-element.55.rest_0_), channel_id=1, source_target_pairs={{0,4},{2,6},{4,0},{6,2},{8,12},{10,14},{12,8},{14,10},{16,20},{18,... | collective-permute-start | bytes 393224 | tf_op jit(solution)/shard_map/ppermute | solution.py:65
  195.4 8.0 %collective-permute-start.16 = (bf16[16,4096]{1,0:T(8,128)(2,1)S(1)}, bf16[16,4096]{1,0:T(8,128)(2,1)S(1)}, u32[]{:S(2)}, u32[]{:S(2)}) collective-permute-start(bf16[16,4096]{1,0:T(8,128)(2,1)S(1)} %get-tuple-element.55.rest_0_), channel_id=1, source_target_pairs={{0,8},{2,10},{4,12},{6,14},{8,0},{10,2},{12,4},{14,6},{16,24},{18,... | collective-permute-start | bytes 393224 | tf_op jit(solution)/shard_map/ppermute | solution.py:65
  199.0 6.6 %collective-permute-start.22 = (bf16[16,4096]{1,0:T(8,128)(2,1)S(1)}, bf16[16,4096]{1,0:T(8,128)(2,1)S(1)}, u32[]{:S(2)}, u32[]{:S(2)}) collective-permute-start(bf16[16,4096]{1,0:T(8,128)(2,1)S(1)} %get-tuple-element.55.rest_0_), channel_id=1, source_target_pairs={{0,2},{2,0},{4,6},{6,4},{8,10},{10,8},{12,14},{14,12},{16,18},{18,... | collective-permute-start | bytes 393224 | tf_op jit(solution)/shard_map/ppermute | solution.py:65
  199.8 6.8 %collective-permute-start.17 = (bf16[16,4096]{1,0:T(8,128)(2,1)S(1)}, bf16[16,4096]{1,0:T(8,128)(2,1)S(1)}, u32[]{:S(2)}, u32[]{:S(2)}) collective-permute-start(bf16[16,4096]{1,0:T(8,128)(2,1)S(1)} %collective-permute-done.15.rest_1_), channel_id=1, source_target_pairs={{0,8},{2,10},{4,12},{6,14},{8,0},{10,2},{12,4},{14,6},{16,24},{18,... | collective-permute-start | bytes 393224 | tf_op jit(solution)/shard_map/ppermute | solution.py:65
  202.6 5.3 %collective-permute-start.26 = (bf16[16,4096]{1,0:T(8,128)(2,1)S(1)}, bf16[16,4096]{1,0:T(8,128)(2,1)S(1)}, u32[]{:S(2)}, u32[]{:S(2)}) collective-permute-start(bf16[16,4096]{1,0:T(8,128)(2,1)S(1)} %collective-permute-done.18.rest_4_), channel_id=1, source_target_pairs={{0,2},{2,0},{4,6},{6,4},{8,10},{10,8},{12,14},{14,12},{16,18},{18,... | collective-permute-start | bytes 393224 | tf_op jit(solution)/shard_map/ppermute | solution.py:65
  203.5 4.5 %collective-permute-start.24 = (bf16[16,4096]{1,0:T(8,128)(2,1)S(1)}, bf16[16,4096]{1,0:T(8,128)(2,1)S(1)}, u32[]{:S(2)}, u32[]{:S(2)}) collective-permute-start(bf16[16,4096]{1,0:T(8,128)(2,1)S(1)} %collective-permute-done.16.rest_2_), channel_id=1, source_target_pairs={{0,2},{2,0},{4,6},{6,4},{8,10},{10,8},{12,14},{14,12},{16,18},{18,... | collective-permute-start | bytes 393224 | tf_op jit(solution)/shard_map/ppermute | solution.py:65
  203.5 6.3 %collective-permute-start.20 = (bf16[16,4096]{1,0:T(8,128)(2,1)S(1)}, bf16[16,4096]{1,0:T(8,128)(2,1)S(1)}, u32[]{:S(2)}, u32[]{:S(2)}) collective-permute-start(bf16[16,4096]{1,0:T(8,128)(2,1)S(1)} %collective-permute-done.16.rest_2_), channel_id=1, source_target_pairs={{0,4},{2,6},{4,0},{6,2},{8,12},{10,14},{12,8},{14,10},{16,20},{18,... | collective-permute-start | bytes 393224 | tf_op jit(solution)/shard_map/ppermute | solution.py:65
  205.6 7.1 %collective-permute-start.19 = (bf16[16,4096]{1,0:T(8,128)(2,1)S(1)}, bf16[16,4096]{1,0:T(8,128)(2,1)S(1)}, u32[]{:S(2)}, u32[]{:S(2)}) collective-permute-start(bf16[16,4096]{1,0:T(8,128)(2,1)S(1)} %collective-permute-done.15.rest_1_), channel_id=1, source_target_pairs={{0,4},{2,6},{4,0},{6,2},{8,12},{10,14},{12,8},{14,10},{16,20},{18,... | collective-permute-start | bytes 393224 | tf_op jit(solution)/shard_map/ppermute | solution.py:65
  206.5 8.5 %collective-permute-start.21 = (bf16[16,4096]{1,0:T(8,128)(2,1)S(1)}, bf16[16,4096]{1,0:T(8,128)(2,1)S(1)}, u32[]{:S(2)}, u32[]{:S(2)}) collective-permute-start(bf16[16,4096]{1,0:T(8,128)(2,1)S(1)} %collective-permute-done.17.rest_3_), channel_id=1, source_target_pairs={{0,4},{2,6},{4,0},{6,2},{8,12},{10,14},{12,8},{14,10},{16,20},{18,... | collective-permute-start | bytes 393224 | tf_op jit(solution)/shard_map/ppermute | solution.py:65
  207.9 9.2 %collective-permute-start.23 = (bf16[16,4096]{1,0:T(8,128)(2,1)S(1)}, bf16[16,4096]{1,0:T(8,128)(2,1)S(1)}, u32[]{:S(2)}, u32[]{:S(2)}) collective-permute-start(bf16[16,4096]{1,0:T(8,128)(2,1)S(1)} %collective-permute-done.15.rest_1_), channel_id=1, source_target_pairs={{0,2},{2,0},{4,6},{6,4},{8,10},{10,8},{12,14},{14,12},{16,18},{18,... | collective-permute-start | bytes 393224 | tf_op jit(solution)/shard_map/ppermute | solution.py:65
  207.9 9.3 %collective-permute-start.25 = (bf16[16,4096]{1,0:T(8,128)(2,1)S(1)}, bf16[16,4096]{1,0:T(8,128)(2,1)S(1)}, u32[]{:S(2)}, u32[]{:S(2)}) collective-permute-start(bf16[16,4096]{1,0:T(8,128)(2,1)S(1)} %collective-permute-done.17.rest_3_), channel_id=1, source_target_pairs={{0,2},{2,0},{4,6},{6,4},{8,10},{10,8},{12,14},{14,12},{16,18},{18,... | collective-permute-start | bytes 393224 | tf_op jit(solution)/shard_map/ppermute | solution.py:65
  209.9 7.3 %collective-permute-start.28 = (bf16[16,4096]{1,0:T(8,128)(2,1)S(1)}, bf16[16,4096]{1,0:T(8,128)(2,1)S(1)}, u32[]{:S(2)}, u32[]{:S(2)}) collective-permute-start(bf16[16,4096]{1,0:T(8,128)(2,1)S(1)} %collective-permute-done.20.rest_6_), channel_id=1, source_target_pairs={{0,2},{2,0},{4,6},{6,4},{8,10},{10,8},{12,14},{14,12},{16,18},{18,... | collective-permute-start | bytes 393224 | tf_op jit(solution)/shard_map/ppermute | solution.py:65
  212.7 4.5 %collective-permute-start.27 = (bf16[16,4096]{1,0:T(8,128)(2,1)S(1)}, bf16[16,4096]{1,0:T(8,128)(2,1)S(1)}, u32[]{:S(2)}, u32[]{:S(2)}) collective-permute-start(bf16[16,4096]{1,0:T(8,128)(2,1)S(1)} %collective-permute-done.19.rest_5_), channel_id=1, source_target_pairs={{0,2},{2,0},{4,6},{6,4},{8,10},{10,8},{12,14},{14,12},{16,18},{18,... | collective-permute-start | bytes 393224 | tf_op jit(solution)/shard_map/ppermute | solution.py:65
  215.0 2.2 collective-permute-start.29
  219.7 6.0 %collective-permute-start.30 = (bf16[128,512]{1,0:T(8,128)(2,1)S(1)}, bf16[128,512]{1,0:T(8,128)(2,1)S(1)}, u32[]{:S(2)}, u32[]{:S(2)}) collective-permute-start(bf16[128,512]{1,0:T(8,128)(2,1)S(1)} %get-tuple-element.57), channel_id=1, source_target_pairs={{0,1},{1,0},{2,3},{3,2},{4,5},{5,4},{6,7},{7,6},{8,9},{9,8},{10,11... | collective-permute-start | bytes 393224 | tf_op jit(solution)/shard_map/ppermute | solution.py:404

commit v14 on v13

--- a/solution.py
+++ b/solution.py
@@ -28,13 +28,21 @@
 def page_rounds(dims):
     far, near = dims
     half = max(near // 2, 1)
-    order = []
-    for low in range(0, near, half):
-        swaps = range(low, min(low + half, near))
-        opening = [(1, n) for n in swaps] if low == 0 else [(z, n) for n in swaps for z in (1, 0)]
-        rest = [(z, n) for n in swaps for z in range(2, far)]
-        order += opening + ([(0, n) for n in swaps if n] if low == 0 else []) + rest
-    return [uniform(z, n, dims) for z, n in order]
+    if far != 4:
+        swaps = [range(low, min(low + half, near)) for low in range(0, near, half)]
+        return [uniform(z, n, dims) for part in swaps for z in range(far) for n in part if z or n]
+
+    def outer(swaps):
+        rounds = [((2, n), (0, n), (3, n), (1, n)) for n in swaps]
+        return rounds + [((3, n), (1, n), (2, n), (0, n)) for n in swaps if n]
+
+    def inner(swaps):
+        rounds = [((0, n), (2, n), (1, n), (3, n)) for n in swaps if n]
+        return rounds + [((1, n), (3, n), (0, n), (2, n)) for n in swaps]
+
+    same, other = range(half), range(half, near)
+    across = [((3, 0), (2, 0), (1, 0), (0, 0))]
+    return outer(same) + across + inner(same) + inner(other) + outer(other)
 
 
 def reverse(route):

time: 226 us -> 234 us (1.035)
  waiting for transfers between devices: 108 us -> 121 us
  starting transfers between devices: 86 us -> 80.9 us
    ppermute x15, starting transfers between devices: 22.8 us -> 8.64 us  [swap(): return lax.ppermute(array, 'group', [(s, s ^ mask) for s in range(groups)])]
    ppermute x15, starting transfers between devices: 61.5 us -> 70.7 us  [send_by(): return lax.ppermute(array, 'group', pairs)]
    ppermute x15, waiting for transfers between devices: 96.7 us -> 104 us  [send_by(): return lax.ppermute(array, 'group', pairs)]
    ppermute x15, waiting for transfers between devices: 7.51 us -> 13.2 us  [swap(): return lax.ppermute(array, 'group', [(s, s ^ mask) for s in range(groups)])]
  transfers between devices with their start and end apart: 31 -> 31, of which waited for: 11 -> 14; matrix products, arithmetic and copies ran while one was open for 0% -> 0% of each run, Pallas kernels for 9% -> 8%
where the time goes in v14:
time: 234 us; the launch traced here: 233 us
  waiting for transfers between devices  121 us (52%)
  starting transfers between devices  80.9 us (35%)
  Pallas kernels  28.5 us (12%)
    ppermute x15, waiting for transfers between devices, send_by(): return lax.ppermute(array, 'group', pairs)  104 us
    ppermute x15, starting transfers between devices, send_by(): return lax.ppermute(array, 'group', pairs)  70.7 us
    pallas_call x5, Pallas kernels, settle(): pl.pallas_call(functools.partial(settle_kernel, dims, routes, own, last),...  13.4 us
    ppermute x15, waiting for transfers between devices, swap(): return lax.ppermute(array, 'group', [(s, s ^ mask) for s in range(groups)])  13.2 us
    pallas_call x2, Pallas kernels, prepare(): pl.pallas_call(functools.partial(prepare_kernel, dims, routes, own), out_...  10.5 us
    ppermute x15, starting transfers between devices, swap(): return lax.ppermute(array, 'group', [(s, s ^ mask) for s in range(groups)])  8.64 us
  transfers between devices with their start and end apart: 31, of which 14 were waited for; matrix products, arithmetic and copies ran while one was open for 0% of the time, Pallas kernels for 8%

profile of v14, /device:TPU:0, one launch (start us, length us, event | category | flops | bytes accessed | tf_op | source)
XLA Modules:
  0.0 232.8 jit_solution(6373954725921156036)
XLA Ops:
  0.6 0.7 or_or_fusion.table_hbm.table
  1.4 4.0 %outgoing_pages.2 = (bf16[2,128,1024]{2,1,0:T(8,128)(2,1)S(1)}, bf16[2,128,1024]{2,1,0:T(8,128)(2,1)S(1)}) custom-call(s32[256]{0:T(256)S(1)} %or_or_fusion.table_hbm.table, bf16[32,128,1024]{2,1,0:T(8,128)(2,1)} %pool.3), custom_call_target="tpu_custom_call" | custom-call | bytes 2097152 | tf_op jit(solution)/shard_map/outgoing_pages/pallas_call | solution.py:164
  5.4 3.5 %collective-permute-start.1 = (bf16[2,128,1024]{2,1,0:T(8,128)(2,1)S(1)}, bf16[2,128,1024]{2,1,0:T(8,128)(2,1)S(1)}, u32[]{:S(2)}, u32[]{:S(2)}) collective-permute-start(bf16[2,128,1024]{2,1,0:T(8,128)(2,1)S(1)} %get-tuple-element.32), channel_id=1, source_target_pairs={{0,18},{2,16},{4,22},{6,20},{8,2},{10,0},{12,6},{14,4},{16,26},{18... | collective-permute-start | bytes 1572872 | tf_op jit(solution)/shard_map/ppermute | solution.py:68
  8.9 1.6 collective-permute-start
  10.4 6.4 %outgoing_pages.3 = (bf16[32,128,1024]{2,1,0:T(8,128)(2,1)}, bf16[2,128,1024]{2,1,0:T(8,128)(2,1)S(1)}, bf16[2,128,1024]{2,1,0:T(8,128)(2,1)S(1)}, bf16[2,128,10...) custom-call(s32[256]{0:T(256)S(1)} %or_or_fusion.table_hbm.table, ...), custom_call_target="tpu_custom_call" | custom-call | bytes 14680064 | tf_op jit(solution)/shard_map/outgoing_pages/pallas_call | solution.py:164
  16.9 0.1 collective-permute-start.2
  17.0 3.8 %collective-permute-start.3 = (bf16[2,128,1024]{2,1,0:T(8,128)(2,1)S(1)}, bf16[2,128,1024]{2,1,0:T(8,128)(2,1)S(1)}, u32[]{:S(2)}, u32[]{:S(2)}) collective-permute-start(bf16[2,128,1024]{2,1,0:T(8,128)(2,1)S(1)} %get-tuple-element.36), channel_id=1, source_target_pairs={{0,24},{2,26},{4,28},{6,30},{8,16},{10,18},{12,20},{14,22},{16,8},... | collective-permute-start | bytes 1572872 | tf_op jit(solution)/shard_map/ppermute | solution.py:68
  20.8 0.5 collective-permute-done.1.rest_1_
  21.2 2.2 collective-permute-start.5
  23.4 9.1 %collective-permute-done.rest_0_ = bf16[2,128,1024]{2,1,0:T(8,128)(2,1)S(1)} collective-permute-done((bf16[2,128,1024]{2,1,0:T(8,128)(2,1)S(1)}, bf16[2,128,1024]{2,1,0:T(8,128)(2,1)S(1)}, u32[]{:S(2)}, u32[]{:S(2)}) %collective-permute-start) | collective-permute-done | bytes 524320 | tf_op jit(solution)/shard_map/ppermute | solution.py:68
  32.5 1.8 collective-permute-start.6
  34.3 11.0 %collective-permute-done.2.rest_2_ = bf16[2,128,1024]{2,1,0:T(8,128)(2,1)S(1)} collective-permute-done((bf16[2,128,1024]{2,1,0:T(8,128)(2,1)S(1)}, bf16[2,128,1024]{2,1,0:T(8,128)(2,1)S(1)}, u32[]{:S(2)}, u32[]{:S(2)}) %collective-permute-start.2) | collective-permute-done | bytes 524320 | tf_op jit(solution)/shard_map/ppermute | solution.py:68
  45.3 1.4 collective-permute-start.7
  46.7 10.2 %collective-permute-done.3.rest_0_ = bf16[2,128,1024]{2,1,0:T(8,128)(2,1)S(1)} collective-permute-done((bf16[2,128,1024]{2,1,0:T(8,128)(2,1)S(1)}, bf16[2,128,1024]{2,1,0:T(8,128)(2,1)S(1)}, u32[]{:S(2)}, u32[]{:S(2)}) %collective-permute-start.3) | collective-permute-done | bytes 524320 | tf_op jit(solution)/shard_map/ppermute | solution.py:68
  57.0 0.7 collective-permute-start.8
  57.6 22.9 %collective-permute-start.9 = (bf16[2,128,1024]{2,1,0:T(8,128)(2,1)S(1)}, bf16[2,128,1024]{2,1,0:T(8,128)(2,1)S(1)}, u32[]{:S(2)}, u32[]{:S(2)}) collective-permute-start(bf16[2,128,1024]{2,1,0:T(8,128)(2,1)S(1)} %get-tuple-element.46), channel_id=1, source_target_pairs={{0,12},{2,14},{4,8},{6,10},{8,28},{10,30},{12,24},{14,26},{16,4},{... | collective-permute-start | bytes 1572872 | tf_op jit(solution)/shard_map/ppermute | solution.py:68
  80.5 9.9 %collective-permute-done.5.rest_2_ = bf16[2,128,1024]{2,1,0:T(8,128)(2,1)S(1)} collective-permute-done((bf16[2,128,1024]{2,1,0:T(8,128)(2,1)S(1)}, bf16[2,128,1024]{2,1,0:T(8,128)(2,1)S(1)}, u32[]{:S(2)}, u32[]{:S(2)}) %collective-permute-start.5) | collective-permute-done | bytes 524320 | tf_op jit(solution)/shard_map/ppermute | solution.py:68
  90.4 0.2 collective-permute-start.10
  90.7 10.9 %collective-permute-done.6.rest_0_ = bf16[2,128,1024]{2,1,0:T(8,128)(2,1)S(1)} collective-permute-done((bf16[2,128,1024]{2,1,0:T(8,128)(2,1)S(1)}, bf16[2,128,1024]{2,1,0:T(8,128)(2,1)S(1)}, u32[]{:S(2)}, u32[]{:S(2)}) %collective-permute-start.6) | collective-permute-done | bytes 524320 | tf_op jit(solution)/shard_map/ppermute | solution.py:68
  101.6 0.5 collective-permute-start.11
  102.1 27.7 %collective-permute-start.12 = (bf16[2,128,1024]{2,1,0:T(8,128)(2,1)S(1)}, bf16[2,128,1024]{2,1,0:T(8,128)(2,1)S(1)}, u32[]{:S(2)}, u32[]{:S(2)}) collective-permute-start(bf16[2,128,1024]{2,1,0:T(8,128)(2,1)S(1)} %get-tuple-element.51), channel_id=1, source_target_pairs={{0,22},{2,20},{4,18},{6,16},{8,6},{10,4},{12,2},{14,0},{16,30},{18... | collective-permute-start | bytes 1572872 | tf_op jit(solution)/shard_map/ppermute | solution.py:68
  129.8 1.3 collective-permute-start.13
  131.1 41.5 %collective-permute-done.9.rest_0_ = bf16[2,128,1024]{2,1,0:T(8,128)(2,1)S(1)} collective-permute-done((bf16[2,128,1024]{2,1,0:T(8,128)(2,1)S(1)}, bf16[2,128,1024]{2,1,0:T(8,128)(2,1)S(1)}, u32[]{:S(2)}, u32[]{:S(2)}) %collective-permute-start.9) | collective-permute-done | bytes 524320 | tf_op jit(solution)/shard_map/ppermute | solution.py:68
  172.6 3.0 %collective-permute-start.14 = (bf16[2,128,1024]{2,1,0:T(8,128)(2,1)S(1)}, bf16[2,128,1024]{2,1,0:T(8,128)(2,1)S(1)}, u32[]{:S(2)}, u32[]{:S(2)}) collective-permute-start(bf16[2,128,1024]{2,1,0:T(8,128)(2,1)S(1)} %get-tuple-element.53), channel_id=1, source_target_pairs={{0,30},{2,28},{4,26},{6,24},{8,14},{10,12},{12,10},{14,8},{16,22},... | collective-permute-start | bytes 1572872 | tf_op jit(solution)/shard_map/ppermute | solution.py:68
  175.7 4.4 %settle_pages.5 = (bf16[32,128,1024]{2,1,0:T(8,128)(2,1)}, f32[16,32,128]{2,1,0:T(8,128)S(1)}) custom-call(s32[256]{0:T(256)S(1)} %or_or_fusion.table_hbm.table, s32[256]{0:T(256)S(1)} %copy-done.1, bf16[16,32,128]{2,1,0:T(8,128)(2,1)S(1)} %bitcast.2, f32[16,32,128]{2,1,0:T(8,128)S(1)} %broadcast_in_dim.3.rows_in, ...), custom_call_target="tpu_custom_call", output_to_operand_aliasing={{0}: (4, {})} | custom-call | flops 1073741824 | bytes 3145728 | tf_op jit(solution)/shard_map/settle_pages/pallas_call | solution.py:283
  180.1 2.2 settle_pages.6
  182.3 2.2 settle_pages.7
  184.5 10.4 %collective-permute-done.10.rest_1_ = bf16[2,128,1024]{2,1,0:T(8,128)(2,1)S(1)} collective-permute-done((bf16[2,128,1024]{2,1,0:T(8,128)(2,1)S(1)}, bf16[2,128,1024]{2,1,0:T(8,128)(2,1)S(1)}, u32[]{:S(2)}, u32[]{:S(2)}) %collective-permute-start.10) | collective-permute-done | bytes 524320 | tf_op jit(solution)/shard_map/ppermute | solution.py:68
  195.0 2.2 settle_pages.8
  197.2 2.4 %settle_pages.9 = (bf16[32,128,1024]{2,1,0:T(8,128)(2,1)}, bf16[16,4096]{1,0:T(8,128)(2,1)S(1)}) custom-call(s32[256]{0:T(256)S(1)} %or_or_fusion.table_hbm.table, s32[256]{0:T(256)S(1)} %copy-done.1, bf16[16,32,128]{2,1,0:T(8,128)(2,1)S(1)} %bitcast.6, f32[16,32,128]{2,1,0:T(8,128)S(1)} %get-tuple-element.49.rows_in, ...), custom_call_target="tpu_custom_call", output_to_operand_aliasing={{0}: (4, {})} | custom-call | flops 1073741824 | bytes 3145728 | tf_op jit(solution)/shard_map/settle_pages/pallas_call | solution.py:283
  199.7 1.0 collective-permute-start.15
  200.7 0.6 collective-permute-start.18
  201.3 2.9 %collective-permute-start.16 = (bf16[16,4096]{1,0:T(8,128)(2,1)S(1)}, bf16[16,4096]{1,0:T(8,128)(2,1)S(1)}, u32[]{:S(2)}, u32[]{:S(2)}) collective-permute-start(bf16[16,4096]{1,0:T(8,128)(2,1)S(1)} %get-tuple-element.55.rest_0_), channel_id=1, source_target_pairs={{0,8},{2,10},{4,12},{6,14},{8,0},{10,2},{12,4},{14,6},{16,24},{18,... | collective-permute-start | bytes 393224 | tf_op jit(solution)/shard_map/ppermute | solution.py:73
  204.3 4.8 %collective-permute-done.15.rest_1_ = bf16[16,4096]{1,0:T(8,128)(2,1)S(1)} collective-permute-done((bf16[16,4096]{1,0:T(8,128)(2,1)S(1)}, bf16[16,4096]{1,0:T(8,128)(2,1)S(1)}, u32[]{:S(2)}, u32[]{:S(2)}) %collective-permute-start.15) | collective-permute-done | bytes 131104 | tf_op jit(solution)/shard_map/ppermute | solution.py:73
  209.1 0.8 collective-permute-done.16.rest_2_
  209.9 2.0 collective-permute-start.20
  211.9 0.0 collective-permute-start.19
  211.9 2.2 collective-permute-done.17.rest_3_
  214.1 1.4 collective-permute-start.21
  215.6 0.5 collective-permute-start.25
  216.1 0.0 collective-permute-done.20.rest_6_
  216.2 2.8 %collective-permute-done.19.rest_5_ = bf16[16,4096]{1,0:T(8,128)(2,1)S(1)} collective-permute-done((bf16[16,4096]{1,0:T(8,128)(2,1)S(1)}, bf16[16,4096]{1,0:T(8,128)(2,1)S(1)}, u32[]{:S(2)}, u32[]{:S(2)}) %collective-permute-start.19) | collective-permute-done | bytes 131104 | tf_op jit(solution)/shard_map/ppermute | solution.py:73
  219.0 2.5 %collective-permute-done.21.rest_7_ = bf16[16,4096]{1,0:T(8,128)(2,1)S(1)} collective-permute-done((bf16[16,4096]{1,0:T(8,128)(2,1)S(1)}, bf16[16,4096]{1,0:T(8,128)(2,1)S(1)}, u32[]{:S(2)}, u32[]{:S(2)}) %collective-permute-start.21) | collective-permute-done | bytes 131104 | tf_op jit(solution)/shard_map/ppermute | solution.py:73
  221.5 2.1 project_some_rows.1.some
  223.7 2.5 %project_rows.1 = (f32[128,512]{1,0:T(8,128)S(1)}, bf16[128,512]{1,0:T(8,128)(2,1)S(1)}) custom-call(bf16[4096,512]{1,0:T(8,128)(2,1)S(1)} %copy-done, f32[128,512]{1,0:T(8,128)S(1)} %project_some_rows.1.some, bf16[16,4096]{1,0:T(8,128)(2,1)S(1)} %collective-permute-done.22.rest_0_, bf16[16,4096]{1,0:T(8,128)(2,1)S(1)} %collective-permute-done.23.rest_1_, ...), custom_call_target="tpu_custom_call" | custom-call | flops 536870912 | bytes 4194304 | tf_op jit(solution)/shard_map/project_rows/pallas_call | solution.py:357
  226.2 1.6 collective-permute-start.30
  227.7 4.4 %collective-permute-done.30 = bf16[128,512]{1,0:T(8,128)(2,1)S(1)} collective-permute-done((bf16[128,512]{1,0:T(8,128)(2,1)S(1)}, bf16[128,512]{1,0:T(8,128)(2,1)S(1)}, u32[]{:S(2)}, u32[]{:S(2)}) %collective-permute-start.30) | collective-permute-done | bytes 131104 | tf_op jit(solution)/shard_map/ppermute | solution.py:412
  232.1 0.7 add_convert_fusion
  (33 shorter events, 0.1 us)
Async XLA Ops:
  1.3 174.3 %copy-start.2 = (bf16[16,4096]{1,0:T(8,128)(2,1)S(1)}, bf16[16,4096]{1,0:T(8,128)(2,1)}, u32[]{:S(2)}) copy-start(bf16[16,4096]{1,0:T(8,128)(2,1)} %param.12) | copy-start | bytes 393220
  1.3 174.3 %copy-start.1 = (s32[256]{0:T(256)S(1)}, s32[256]{0:T(256)}, u32[]{:S(2)}) copy-start(s32[256]{0:T(256)} %row_request.9) | copy-start | bytes 3076
  5.4 15.8 %collective-permute-start.1 = (bf16[2,128,1024]{2,1,0:T(8,128)(2,1)S(1)}, bf16[2,128,1024]{2,1,0:T(8,128)(2,1)S(1)}, u32[]{:S(2)}, u32[]{:S(2)}) collective-permute-start(bf16[2,128,1024]{2,1,0:T(8,128)(2,1)S(1)} %get-tuple-element.32), channel_id=1, source_target_pairs={{0,18},{2,16},{4,22},{6,20},{8,2},{10,0},{12,6},{14,4},{16,26},{18... | collective-permute-start | bytes 1572872 | tf_op jit(solution)/shard_map/ppermute | solution.py:68
  8.9 23.6 %collective-permute-start = (bf16[2,128,1024]{2,1,0:T(8,128)(2,1)S(1)}, bf16[2,128,1024]{2,1,0:T(8,128)(2,1)S(1)}, u32[]{:S(2)}, u32[]{:S(2)}) collective-permute-start(bf16[2,128,1024]{2,1,0:T(8,128)(2,1)S(1)} %get-tuple-element.30.rest_0_), channel_id=1, source_target_pairs={{0,16},{2,18},{4,20},{6,22},{8,0},{10,2},{12,4},{14,6},{16,24},{18... | collective-permute-start | bytes 1572872 | tf_op jit(solution)/shard_map/ppermute | solution.py:68
  16.9 28.4 %collective-permute-start.2 = (bf16[2,128,1024]{2,1,0:T(8,128)(2,1)S(1)}, bf16[2,128,1024]{2,1,0:T(8,128)(2,1)S(1)}, u32[]{:S(2)}, u32[]{:S(2)}) collective-permute-start(bf16[2,128,1024]{2,1,0:T(8,128)(2,1)S(1)} %get-tuple-element.33), channel_id=1, source_target_pairs={{0,26},{2,24},{4,30},{6,28},{8,10},{10,8},{12,14},{14,12},{16,18},... | collective-permute-start | bytes 1572872 | tf_op jit(solution)/shard_map/ppermute | solution.py:68
  17.0 40.0 %collective-permute-start.3 = (bf16[2,128,1024]{2,1,0:T(8,128)(2,1)S(1)}, bf16[2,128,1024]{2,1,0:T(8,128)(2,1)S(1)}, u32[]{:S(2)}, u32[]{:S(2)}) collective-permute-start(bf16[2,128,1024]{2,1,0:T(8,128)(2,1)S(1)} %get-tuple-element.36), channel_id=1, source_target_pairs={{0,24},{2,26},{4,28},{6,30},{8,16},{10,18},{12,20},{14,22},{16,8},... | collective-permute-start | bytes 1572872 | tf_op jit(solution)/shard_map/ppermute | solution.py:68
  20.8 36.9 %collective-permute-start.4 = (bf16[2,128,1024]{2,1,0:T(8,128)(2,1)S(1)}, bf16[2,128,1024]{2,1,0:T(8,128)(2,1)S(1)}, u32[]{:S(2)}, u32[]{:S(2)}) collective-permute-start(bf16[2,128,1024]{2,1,0:T(8,128)(2,1)S(1)} %get-tuple-element.37), channel_id=1, source_target_pairs={{0,2},{2,0},{4,6},{6,4},{8,18},{10,16},{12,22},{14,20},{16,10},{18... | collective-permute-start | bytes 1572872 | tf_op jit(solution)/shard_map/ppermute | solution.py:68
  21.2 69.2 %collective-permute-start.5 = (bf16[2,128,1024]{2,1,0:T(8,128)(2,1)S(1)}, bf16[2,128,1024]{2,1,0:T(8,128)(2,1)S(1)}, u32[]{:S(2)}, u32[]{:S(2)}) collective-permute-start(bf16[2,128,1024]{2,1,0:T(8,128)(2,1)S(1)} %get-tuple-element.38), channel_id=1, source_target_pairs={{0,8},{2,10},{4,12},{6,14},{8,24},{10,26},{12,28},{14,30},{16,0},{... | collective-permute-start | bytes 1572872 | tf_op jit(solution)/shard_map/ppermute | solution.py:68
  32.5 69.1 %collective-permute-start.6 = (bf16[2,128,1024]{2,1,0:T(8,128)(2,1)S(1)}, bf16[2,128,1024]{2,1,0:T(8,128)(2,1)S(1)}, u32[]{:S(2)}, u32[]{:S(2)}) collective-permute-start(bf16[2,128,1024]{2,1,0:T(8,128)(2,1)S(1)} %get-tuple-element.41), channel_id=1, source_target_pairs={{0,10},{2,8},{4,14},{6,12},{8,26},{10,24},{12,30},{14,28},{16,2},{... | collective-permute-start | bytes 1572872 | tf_op jit(solution)/shard_map/ppermute | solution.py:68
  45.3 56.8 %collective-permute-start.7 = (bf16[2,128,1024]{2,1,0:T(8,128)(2,1)S(1)}, bf16[2,128,1024]{2,1,0:T(8,128)(2,1)S(1)}, u32[]{:S(2)}, u32[]{:S(2)}) collective-permute-start(bf16[2,128,1024]{2,1,0:T(8,128)(2,1)S(1)} %get-tuple-element.42), channel_id=1, source_target_pairs={{0,4},{2,6},{4,0},{6,2},{8,20},{10,22},{12,16},{14,18},{16,12},{18... | collective-permute-start | bytes 1572872 | tf_op jit(solution)/shard_map/ppermute | solution.py:68
  57.0 72.8 %collective-permute-start.8 = (bf16[2,128,1024]{2,1,0:T(8,128)(2,1)S(1)}, bf16[2,128,1024]{2,1,0:T(8,128)(2,1)S(1)}, u32[]{:S(2)}, u32[]{:S(2)}) collective-permute-start(bf16[2,128,1024]{2,1,0:T(8,128)(2,1)S(1)} %get-tuple-element.43), channel_id=1, source_target_pairs={{0,6},{2,4},{4,2},{6,0},{8,22},{10,20},{12,18},{14,16},{16,14},{18... | collective-permute-start | bytes 1572872 | tf_op jit(solution)/shard_map/ppermute | solution.py:68
  57.6 115.0 %collective-permute-start.9 = (bf16[2,128,1024]{2,1,0:T(8,128)(2,1)S(1)}, bf16[2,128,1024]{2,1,0:T(8,128)(2,1)S(1)}, u32[]{:S(2)}, u32[]{:S(2)}) collective-permute-start(bf16[2,128,1024]{2,1,0:T(8,128)(2,1)S(1)} %get-tuple-element.46), channel_id=1, source_target_pairs={{0,12},{2,14},{4,8},{6,10},{8,28},{10,30},{12,24},{14,26},{16,4},{... | collective-permute-start | bytes 1572872 | tf_op jit(solution)/shard_map/ppermute | solution.py:68
  90.4 104.5 %collective-permute-start.10 = (bf16[2,128,1024]{2,1,0:T(8,128)(2,1)S(1)}, bf16[2,128,1024]{2,1,0:T(8,128)(2,1)S(1)}, u32[]{:S(2)}, u32[]{:S(2)}) collective-permute-start(bf16[2,128,1024]{2,1,0:T(8,128)(2,1)S(1)} %get-tuple-element.47), channel_id=1, source_target_pairs={{0,14},{2,12},{4,10},{6,8},{8,30},{10,28},{12,26},{14,24},{16,6},{... | collective-permute-start | bytes 1572872 | tf_op jit(solution)/shard_map/ppermute | solution.py:68
  101.6 93.4 %collective-permute-start.11 = (bf16[2,128,1024]{2,1,0:T(8,128)(2,1)S(1)}, bf16[2,128,1024]{2,1,0:T(8,128)(2,1)S(1)}, u32[]{:S(2)}, u32[]{:S(2)}) collective-permute-start(bf16[2,128,1024]{2,1,0:T(8,128)(2,1)S(1)} %get-tuple-element.48), channel_id=1, source_target_pairs={{0,20},{2,22},{4,16},{6,18},{8,4},{10,6},{12,0},{14,2},{16,28},{18... | collective-permute-start | bytes 1572872 | tf_op jit(solution)/shard_map/ppermute | solution.py:68
  102.1 95.1 %collective-permute-start.12 = (bf16[2,128,1024]{2,1,0:T(8,128)(2,1)S(1)}, bf16[2,128,1024]{2,1,0:T(8,128)(2,1)S(1)}, u32[]{:S(2)}, u32[]{:S(2)}) collective-permute-start(bf16[2,128,1024]{2,1,0:T(8,128)(2,1)S(1)} %get-tuple-element.51), channel_id=1, source_target_pairs={{0,22},{2,20},{4,18},{6,16},{8,6},{10,4},{12,2},{14,0},{16,30},{18... | collective-permute-start | bytes 1572872 | tf_op jit(solution)/shard_map/ppermute | solution.py:68
  129.8 67.4 %collective-permute-start.13 = (bf16[2,128,1024]{2,1,0:T(8,128)(2,1)S(1)}, bf16[2,128,1024]{2,1,0:T(8,128)(2,1)S(1)}, u32[]{:S(2)}, u32[]{:S(2)}) collective-permute-start(bf16[2,128,1024]{2,1,0:T(8,128)(2,1)S(1)} %get-tuple-element.52), channel_id=1, source_target_pairs={{0,28},{2,30},{4,24},{6,26},{8,12},{10,14},{12,8},{14,10},{16,20},... | collective-permute-start | bytes 1572872 | tf_op jit(solution)/shard_map/ppermute | solution.py:68
  172.6 24.6 %collective-permute-start.14 = (bf16[2,128,1024]{2,1,0:T(8,128)(2,1)S(1)}, bf16[2,128,1024]{2,1,0:T(8,128)(2,1)S(1)}, u32[]{:S(2)}, u32[]{:S(2)}) collective-permute-start(bf16[2,128,1024]{2,1,0:T(8,128)(2,1)S(1)} %get-tuple-element.53), channel_id=1, source_target_pairs={{0,30},{2,28},{4,26},{6,24},{8,14},{10,12},{12,10},{14,8},{16,22},... | collective-permute-start | bytes 1572872 | tf_op jit(solution)/shard_map/ppermute | solution.py:68
  195.0 26.5 %copy-start = (bf16[4096,512]{1,0:T(8,128)(2,1)S(1)}, bf16[4096,512]{1,0:T(8,128)(2,1)}, u32[]{:S(2)}) copy-start(bf16[4096,512]{1,0:T(8,128)(2,1)} %out_weight.3) | copy-start | bytes 12582916
  199.7 9.4 %collective-permute-start.15 = (bf16[16,4096]{1,0:T(8,128)(2,1)S(1)}, bf16[16,4096]{1,0:T(8,128)(2,1)S(1)}, u32[]{:S(2)}, u32[]{:S(2)}) collective-permute-start(bf16[16,4096]{1,0:T(8,128)(2,1)S(1)} %get-tuple-element.55.rest_0_), channel_id=1, source_target_pairs={{0,16},{2,18},{4,20},{6,22},{8,24},{10,26},{12,28},{14,30},{16,0},... | collective-permute-start | bytes 393224 | tf_op jit(solution)/shard_map/ppermute | solution.py:73
  200.7 8.4 %collective-permute-start.18 = (bf16[16,4096]{1,0:T(8,128)(2,1)S(1)}, bf16[16,4096]{1,0:T(8,128)(2,1)S(1)}, u32[]{:S(2)}, u32[]{:S(2)}) collective-permute-start(bf16[16,4096]{1,0:T(8,128)(2,1)S(1)} %get-tuple-element.55.rest_0_), channel_id=1, source_target_pairs={{0,4},{2,6},{4,0},{6,2},{8,12},{10,14},{12,8},{14,10},{16,20},{18,... | collective-permute-start | bytes 393224 | tf_op jit(solution)/shard_map/ppermute | solution.py:73
  201.3 8.5 %collective-permute-start.16 = (bf16[16,4096]{1,0:T(8,128)(2,1)S(1)}, bf16[16,4096]{1,0:T(8,128)(2,1)S(1)}, u32[]{:S(2)}, u32[]{:S(2)}) collective-permute-start(bf16[16,4096]{1,0:T(8,128)(2,1)S(1)} %get-tuple-element.55.rest_0_), channel_id=1, source_target_pairs={{0,8},{2,10},{4,12},{6,14},{8,0},{10,2},{12,4},{14,6},{16,24},{18,... | collective-permute-start | bytes 393224 | tf_op jit(solution)/shard_map/ppermute | solution.py:73
  204.3 7.6 %collective-permute-start.22 = (bf16[16,4096]{1,0:T(8,128)(2,1)S(1)}, bf16[16,4096]{1,0:T(8,128)(2,1)S(1)}, u32[]{:S(2)}, u32[]{:S(2)}) collective-permute-start(bf16[16,4096]{1,0:T(8,128)(2,1)S(1)} %get-tuple-element.55.rest_0_), channel_id=1, source_target_pairs={{0,2},{2,0},{4,6},{6,4},{8,10},{10,8},{12,14},{14,12},{16,18},{18,... | collective-permute-start | bytes 393224 | tf_op jit(solution)/shard_map/ppermute | solution.py:73
  209.1 5.1 %collective-permute-start.17 = (bf16[16,4096]{1,0:T(8,128)(2,1)S(1)}, bf16[16,4096]{1,0:T(8,128)(2,1)S(1)}, u32[]{:S(2)}, u32[]{:S(2)}) collective-permute-start(bf16[16,4096]{1,0:T(8,128)(2,1)S(1)} %collective-permute-done.15.rest_1_), channel_id=1, source_target_pairs={{0,8},{2,10},{4,12},{6,14},{8,0},{10,2},{12,4},{14,6},{16,24},{18,... | collective-permute-start | bytes 393224 | tf_op jit(solution)/shard_map/ppermute | solution.py:73
  209.1 6.5 %collective-permute-start.26 = (bf16[16,4096]{1,0:T(8,128)(2,1)S(1)}, bf16[16,4096]{1,0:T(8,128)(2,1)S(1)}, u32[]{:S(2)}, u32[]{:S(2)}) collective-permute-start(bf16[16,4096]{1,0:T(8,128)(2,1)S(1)} %collective-permute-done.18.rest_4_), channel_id=1, source_target_pairs={{0,2},{2,0},{4,6},{6,4},{8,10},{10,8},{12,14},{14,12},{16,18},{18,... | collective-permute-start | bytes 393224 | tf_op jit(solution)/shard_map/ppermute | solution.py:73
  209.9 5.7 %collective-permute-start.24 = (bf16[16,4096]{1,0:T(8,128)(2,1)S(1)}, bf16[16,4096]{1,0:T(8,128)(2,1)S(1)}, u32[]{:S(2)}, u32[]{:S(2)}) collective-permute-start(bf16[16,4096]{1,0:T(8,128)(2,1)S(1)} %collective-permute-done.16.rest_2_), channel_id=1, source_target_pairs={{0,2},{2,0},{4,6},{6,4},{8,10},{10,8},{12,14},{14,12},{16,18},{18,... | collective-permute-start | bytes 393224 | tf_op jit(solution)/shard_map/ppermute | solution.py:73
  209.9 6.3 %collective-permute-start.20 = (bf16[16,4096]{1,0:T(8,128)(2,1)S(1)}, bf16[16,4096]{1,0:T(8,128)(2,1)S(1)}, u32[]{:S(2)}, u32[]{:S(2)}) collective-permute-start(bf16[16,4096]{1,0:T(8,128)(2,1)S(1)} %collective-permute-done.16.rest_2_), channel_id=1, source_target_pairs={{0,4},{2,6},{4,0},{6,2},{8,12},{10,14},{12,8},{14,10},{16,20},{18,... | collective-permute-start | bytes 393224 | tf_op jit(solution)/shard_map/ppermute | solution.py:73
  211.9 7.1 %collective-permute-start.19 = (bf16[16,4096]{1,0:T(8,128)(2,1)S(1)}, bf16[16,4096]{1,0:T(8,128)(2,1)S(1)}, u32[]{:S(2)}, u32[]{:S(2)}) collective-permute-start(bf16[16,4096]{1,0:T(8,128)(2,1)S(1)} %collective-permute-done.15.rest_1_), channel_id=1, source_target_pairs={{0,4},{2,6},{4,0},{6,2},{8,12},{10,14},{12,8},{14,10},{16,20},{18,... | collective-permute-start | bytes 393224 | tf_op jit(solution)/shard_map/ppermute | solution.py:73
  214.1 7.4 %collective-permute-start.21 = (bf16[16,4096]{1,0:T(8,128)(2,1)S(1)}, bf16[16,4096]{1,0:T(8,128)(2,1)S(1)}, u32[]{:S(2)}, u32[]{:S(2)}) collective-permute-start(bf16[16,4096]{1,0:T(8,128)(2,1)S(1)} %collective-permute-done.17.rest_3_), channel_id=1, source_target_pairs={{0,4},{2,6},{4,0},{6,2},{8,12},{10,14},{12,8},{14,10},{16,20},{18,... | collective-permute-start | bytes 393224 | tf_op jit(solution)/shard_map/ppermute | solution.py:73
  215.6 8.1 %collective-permute-start.23 = (bf16[16,4096]{1,0:T(8,128)(2,1)S(1)}, bf16[16,4096]{1,0:T(8,128)(2,1)S(1)}, u32[]{:S(2)}, u32[]{:S(2)}) collective-permute-start(bf16[16,4096]{1,0:T(8,128)(2,1)S(1)} %collective-permute-done.15.rest_1_), channel_id=1, source_target_pairs={{0,2},{2,0},{4,6},{6,4},{8,10},{10,8},{12,14},{14,12},{16,18},{18,... | collective-permute-start | bytes 393224 | tf_op jit(solution)/shard_map/ppermute | solution.py:73
  215.6 8.1 %collective-permute-start.25 = (bf16[16,4096]{1,0:T(8,128)(2,1)S(1)}, bf16[16,4096]{1,0:T(8,128)(2,1)S(1)}, u32[]{:S(2)}, u32[]{:S(2)}) collective-permute-start(bf16[16,4096]{1,0:T(8,128)(2,1)S(1)} %collective-permute-done.17.rest_3_), channel_id=1, source_target_pairs={{0,2},{2,0},{4,6},{6,4},{8,10},{10,8},{12,14},{14,12},{16,18},{18,... | collective-permute-start | bytes 393224 | tf_op jit(solution)/shard_map/ppermute | solution.py:73
  216.1 7.5 %collective-permute-start.28 = (bf16[16,4096]{1,0:T(8,128)(2,1)S(1)}, bf16[16,4096]{1,0:T(8,128)(2,1)S(1)}, u32[]{:S(2)}, u32[]{:S(2)}) collective-permute-start(bf16[16,4096]{1,0:T(8,128)(2,1)S(1)} %collective-permute-done.20.rest_6_), channel_id=1, source_target_pairs={{0,2},{2,0},{4,6},{6,4},{8,10},{10,8},{12,14},{14,12},{16,18},{18,... | collective-permute-start | bytes 393224 | tf_op jit(solution)/shard_map/ppermute | solution.py:73
  218.9 4.7 %collective-permute-start.27 = (bf16[16,4096]{1,0:T(8,128)(2,1)S(1)}, bf16[16,4096]{1,0:T(8,128)(2,1)S(1)}, u32[]{:S(2)}, u32[]{:S(2)}) collective-permute-start(bf16[16,4096]{1,0:T(8,128)(2,1)S(1)} %collective-permute-done.19.rest_5_), channel_id=1, source_target_pairs={{0,2},{2,0},{4,6},{6,4},{8,10},{10,8},{12,14},{14,12},{16,18},{18,... | collective-permute-start | bytes 393224 | tf_op jit(solution)/shard_map/ppermute | solution.py:73
  221.5 2.2 collective-permute-start.29
  226.2 6.0 %collective-permute-start.30 = (bf16[128,512]{1,0:T(8,128)(2,1)S(1)}, bf16[128,512]{1,0:T(8,128)(2,1)S(1)}, u32[]{:S(2)}, u32[]{:S(2)}) collective-permute-start(bf16[128,512]{1,0:T(8,128)(2,1)S(1)} %get-tuple-element.57), channel_id=1, source_target_pairs={{0,1},{1,0},{2,3},{3,2},{4,5},{5,4},{6,7},{7,6},{8,9},{9,8},{10,11... | collective-permute-start | bytes 393224 | tf_op jit(solution)/shard_map/ppermute | solution.py:412

commit v15 on v14

--- a/solution.py
+++ b/solution.py
@@ -32,17 +32,14 @@
         swaps = [range(low, min(low + half, near)) for low in range(0, near, half)]
         return [uniform(z, n, dims) for part in swaps for z in range(far) for n in part if z or n]
 
-    def outer(swaps):
-        rounds = [((2, n), (0, n), (3, n), (1, n)) for n in swaps]
-        return rounds + [((3, n), (1, n), (2, n), (0, n)) for n in swaps if n]
-
-    def inner(swaps):
-        rounds = [((0, n), (2, n), (1, n), (3, n)) for n in swaps if n]
-        return rounds + [((1, n), (3, n), (0, n), (2, n)) for n in swaps]
-
-    same, other = range(half), range(half, near)
-    across = [((3, 0), (2, 0), (1, 0), (0, 0))]
-    return outer(same) + across + inner(same) + inner(other) + outer(other)
+    def rounds(swaps):
+        outer = [((2, n), (0, n), (3, n), (1, n)) for n in swaps]
+        inner = [((1, n), (3, n), (0, n), (2, n)) for n in swaps]
+        across = [tuple((3 - z, n) for z in range(far)) for n in swaps]
+        here = [uniform(0, n, dims) for n in swaps if n]
+        return outer + inner + [r for pair in zip([[]] * (len(across) - len(here)) + here, across) for r in pair if r]
+
+    return rounds(range(half)) + rounds(range(half, near))
 
 
 def reverse(route):

time: 234 us -> 227 us (0.970)
  waiting for transfers between devices: 121 us -> 113 us
  starting transfers between devices: 80.9 us -> 83.4 us
    ppermute x15, waiting for transfers between devices: 104 us -> 93.1 us  [send_by(): return lax.ppermute(array, 'group', pairs)]
    ppermute x15, starting transfers between devices: 8.64 us -> 14 us  [swap(): return lax.ppermute(array, 'group', [(s, s ^ mask) for s in range(groups)])]
    ppermute x15, starting transfers between devices: 70.7 us -> 67.9 us  [send_by(): return lax.ppermute(array, 'group', pairs)]
  transfers between devices with their start and end apart: 31 -> 31, of which waited for: 14 -> 15; matrix products, arithmetic and copies ran while one was open for 0% -> 0% of each run, Pallas kernels for 8% -> 9%
where the time goes in v15:
time: 227 us
  waiting for transfers between devices  113 us (50%)
  starting transfers between devices  83.4 us (37%)
  Pallas kernels  28.3 us (12%)
    ppermute x15, waiting for transfers between devices, send_by(): return lax.ppermute(array, 'group', pairs)  93.1 us
    ppermute x15, starting transfers between devices, send_by(): return lax.ppermute(array, 'group', pairs)  67.9 us
    ppermute x15, waiting for transfers between devices, swap(): return lax.ppermute(array, 'group', [(s, s ^ mask) for s in range(groups)])  15 us
    ppermute x15, starting transfers between devices, swap(): return lax.ppermute(array, 'group', [(s, s ^ mask) for s in range(groups)])  14 us
    pallas_call x5, Pallas kernels, settle(): pl.pallas_call(functools.partial(settle_kernel, dims, routes, own, last),...  13.2 us
    pallas_call x2, Pallas kernels, prepare(): pl.pallas_call(functools.partial(prepare_kernel, dims, routes, own), out_...  10.5 us
    pallas_call x2, Pallas kernels, call(): pl.pallas_call(kernel, out_shape=outs, in_specs=[vmem] * (1 + len(extra))...  4.61 us
  transfers between devices with their start and end apart: 31, of which 15 were waited for; matrix products, arithmetic and copies ran while one was open for 0% of the time, Pallas kernels for 9%

profile of v15, /device:TPU:0, one launch (start us, length us, event | category | flops | bytes accessed | tf_op | source)
XLA Modules:
  0.0 226.5 jit_solution(12271465449148243043)
XLA Ops:
  0.6 0.7 or_or_fusion.table_hbm.table
  1.4 3.9 %outgoing_pages.2 = (bf16[2,128,1024]{2,1,0:T(8,128)(2,1)S(1)}, bf16[2,128,1024]{2,1,0:T(8,128)(2,1)S(1)}) custom-call(s32[256]{0:T(256)S(1)} %or_or_fusion.table_hbm.table, bf16[32,128,1024]{2,1,0:T(8,128)(2,1)} %pool.3), custom_call_target="tpu_custom_call" | custom-call | bytes 2097152 | tf_op jit(solution)/shard_map/outgoing_pages/pallas_call | solution.py:161
  5.3 3.6 %collective-permute-start.1 = (bf16[2,128,1024]{2,1,0:T(8,128)(2,1)S(1)}, bf16[2,128,1024]{2,1,0:T(8,128)(2,1)S(1)}, u32[]{:S(2)}, u32[]{:S(2)}) collective-permute-start(bf16[2,128,1024]{2,1,0:T(8,128)(2,1)S(1)} %get-tuple-element.32), channel_id=1, source_target_pairs={{0,18},{2,16},{4,22},{6,20},{8,2},{10,0},{12,6},{14,4},{16,26},{18... | collective-permute-start | bytes 1572872 | tf_op jit(solution)/shard_map/ppermute | solution.py:65
  8.9 1.7 collective-permute-start
  10.5 6.6 %outgoing_pages.3 = (bf16[32,128,1024]{2,1,0:T(8,128)(2,1)}, bf16[2,128,1024]{2,1,0:T(8,128)(2,1)S(1)}, bf16[2,128,1024]{2,1,0:T(8,128)(2,1)S(1)}, bf16[2,128,10...) custom-call(s32[256]{0:T(256)S(1)} %or_or_fusion.table_hbm.table, ...), custom_call_target="tpu_custom_call" | custom-call | bytes 14680064 | tf_op jit(solution)/shard_map/outgoing_pages/pallas_call | solution.py:161
  17.1 0.4 collective-permute-start.2
  17.4 0.1 collective-permute-start.3
  17.6 3.7 %collective-permute-start.4 = (bf16[2,128,1024]{2,1,0:T(8,128)(2,1)S(1)}, bf16[2,128,1024]{2,1,0:T(8,128)(2,1)S(1)}, u32[]{:S(2)}, u32[]{:S(2)}) collective-permute-start(bf16[2,128,1024]{2,1,0:T(8,128)(2,1)S(1)} %get-tuple-element.37), channel_id=1, source_target_pairs={{0,24},{2,26},{4,28},{6,30},{8,16},{10,18},{12,20},{14,22},{16,8},... | collective-permute-start | bytes 1572872 | tf_op jit(solution)/shard_map/ppermute | solution.py:65
  21.3 0.0 collective-permute-done.1.rest_1_
  21.3 0.1 collective-permute-start.5
  21.4 11.0 %collective-permute-done.rest_0_ = bf16[2,128,1024]{2,1,0:T(8,128)(2,1)S(1)} collective-permute-done((bf16[2,128,1024]{2,1,0:T(8,128)(2,1)S(1)}, bf16[2,128,1024]{2,1,0:T(8,128)(2,1)S(1)}, u32[]{:S(2)}, u32[]{:S(2)}) %collective-permute-start) | collective-permute-done | bytes 524320 | tf_op jit(solution)/shard_map/ppermute | solution.py:65
  32.4 3.3 %collective-permute-start.6 = (bf16[2,128,1024]{2,1,0:T(8,128)(2,1)S(1)}, bf16[2,128,1024]{2,1,0:T(8,128)(2,1)S(1)}, u32[]{:S(2)}, u32[]{:S(2)}) collective-permute-start(bf16[2,128,1024]{2,1,0:T(8,128)(2,1)S(1)} %get-tuple-element.41), channel_id=1, source_target_pairs={{0,26},{2,24},{4,30},{6,28},{8,18},{10,16},{12,22},{14,20},{16,10}... | collective-permute-start | bytes 1572872 | tf_op jit(solution)/shard_map/ppermute | solution.py:65
  35.7 9.8 %collective-permute-done.2.rest_2_ = bf16[2,128,1024]{2,1,0:T(8,128)(2,1)S(1)} collective-permute-done((bf16[2,128,1024]{2,1,0:T(8,128)(2,1)S(1)}, bf16[2,128,1024]{2,1,0:T(8,128)(2,1)S(1)}, u32[]{:S(2)}, u32[]{:S(2)}) %collective-permute-start.2) | collective-permute-done | bytes 524320 | tf_op jit(solution)/shard_map/ppermute | solution.py:65
  45.4 1.9 collective-permute-start.7
  47.3 9.6 %collective-permute-done.3.rest_0_ = bf16[2,128,1024]{2,1,0:T(8,128)(2,1)S(1)} collective-permute-done((bf16[2,128,1024]{2,1,0:T(8,128)(2,1)S(1)}, bf16[2,128,1024]{2,1,0:T(8,128)(2,1)S(1)}, u32[]{:S(2)}, u32[]{:S(2)}) %collective-permute-start.3) | collective-permute-done | bytes 524320 | tf_op jit(solution)/shard_map/ppermute | solution.py:65
  56.9 1.1 collective-permute-start.8
  58.0 10.3 %collective-permute-done.4.rest_1_ = bf16[2,128,1024]{2,1,0:T(8,128)(2,1)S(1)} collective-permute-done((bf16[2,128,1024]{2,1,0:T(8,128)(2,1)S(1)}, bf16[2,128,1024]{2,1,0:T(8,128)(2,1)S(1)}, u32[]{:S(2)}, u32[]{:S(2)}) %collective-permute-start.4) | collective-permute-done | bytes 524320 | tf_op jit(solution)/shard_map/ppermute | solution.py:65
  68.3 46.2 %collective-permute-start.9 = (bf16[2,128,1024]{2,1,0:T(8,128)(2,1)S(1)}, bf16[2,128,1024]{2,1,0:T(8,128)(2,1)S(1)}, u32[]{:S(2)}, u32[]{:S(2)}) collective-permute-start(bf16[2,128,1024]{2,1,0:T(8,128)(2,1)S(1)} %get-tuple-element.46), channel_id=1, source_target_pairs={{0,12},{2,14},{4,8},{6,10},{8,28},{10,30},{12,24},{14,26},{16,4},{... | collective-permute-start | bytes 1572872 | tf_op jit(solution)/shard_map/ppermute | solution.py:65
  114.5 0.5 collective-permute-start.11
  115.0 3.5 %collective-permute-start.12 = (bf16[2,128,1024]{2,1,0:T(8,128)(2,1)S(1)}, bf16[2,128,1024]{2,1,0:T(8,128)(2,1)S(1)}, u32[]{:S(2)}, u32[]{:S(2)}) collective-permute-start(bf16[2,128,1024]{2,1,0:T(8,128)(2,1)S(1)} %get-tuple-element.51), channel_id=1, source_target_pairs={{0,28},{2,30},{4,24},{6,26},{8,20},{10,22},{12,16},{14,18},{16,12}... | collective-permute-start | bytes 1572872 | tf_op jit(solution)/shard_map/ppermute | solution.py:65
  118.5 18.0 %collective-permute-done.9.rest_0_ = bf16[2,128,1024]{2,1,0:T(8,128)(2,1)S(1)} collective-permute-done((bf16[2,128,1024]{2,1,0:T(8,128)(2,1)S(1)}, bf16[2,128,1024]{2,1,0:T(8,128)(2,1)S(1)}, u32[]{:S(2)}, u32[]{:S(2)}) %collective-permute-start.9) | collective-permute-done | bytes 524320 | tf_op jit(solution)/shard_map/ppermute | solution.py:65
  136.5 1.9 collective-permute-start.14
  138.5 2.9 %settle_pages.5 = (bf16[32,128,1024]{2,1,0:T(8,128)(2,1)}, f32[16,32,128]{2,1,0:T(8,128)S(1)}) custom-call(s32[256]{0:T(256)S(1)} %or_or_fusion.table_hbm.table, s32[256]{0:T(256)S(1)} %copy-done.1, bf16[16,32,128]{2,1,0:T(8,128)(2,1)S(1)} %bitcast.2, f32[16,32,128]{2,1,0:T(8,128)S(1)} %broadcast_in_dim.3.rows_in, ...), custom_call_target="tpu_custom_call", output_to_operand_aliasing={{0}: (4, {})} | custom-call | flops 1073741824 | bytes 3145728 | tf_op jit(solution)/shard_map/settle_pages/pallas_call | solution.py:280
  141.4 2.2 settle_pages.6
  143.6 3.5 %settle_pages.7 = (bf16[32,128,1024]{2,1,0:T(8,128)(2,1)}, f32[16,32,128]{2,1,0:T(8,128)S(1)}) custom-call(s32[256]{0:T(256)S(1)} %or_or_fusion.table_hbm.table, s32[256]{0:T(256)S(1)} %copy-done.1, bf16[16,32,128]{2,1,0:T(8,128)(2,1)S(1)} %bitcast.4, f32[16,32,128]{2,1,0:T(8,128)S(1)} %get-tuple-element.39.rows_in, ...), custom_call_target="tpu_custom_call", output_to_operand_aliasing={{0}: (4, {})} | custom-call | flops 1073741824 | bytes 3145728 | tf_op jit(solution)/shard_map/settle_pages/pallas_call | solution.py:280
  147.1 22.9 %collective-permute-done.10.rest_1_ = bf16[2,128,1024]{2,1,0:T(8,128)(2,1)S(1)} collective-permute-done((bf16[2,128,1024]{2,1,0:T(8,128)(2,1)S(1)}, bf16[2,128,1024]{2,1,0:T(8,128)(2,1)S(1)}, u32[]{:S(2)}, u32[]{:S(2)}) %collective-permute-start.10) | collective-permute-done | bytes 524320 | tf_op jit(solution)/shard_map/ppermute | solution.py:65
  170.0 4.2 %collective-permute-done.11.rest_2_ = bf16[2,128,1024]{2,1,0:T(8,128)(2,1)S(1)} collective-permute-done((bf16[2,128,1024]{2,1,0:T(8,128)(2,1)S(1)}, bf16[2,128,1024]{2,1,0:T(8,128)(2,1)S(1)}, u32[]{:S(2)}, u32[]{:S(2)}) %collective-permute-start.11) | collective-permute-done | bytes 524320 | tf_op jit(solution)/shard_map/ppermute | solution.py:65
  174.3 2.2 settle_pages.8
  176.5 7.3 %collective-permute-done.13.rest_1_ = bf16[2,128,1024]{2,1,0:T(8,128)(2,1)S(1)} collective-permute-done((bf16[2,128,1024]{2,1,0:T(8,128)(2,1)S(1)}, bf16[2,128,1024]{2,1,0:T(8,128)(2,1)S(1)}, u32[]{:S(2)}, u32[]{:S(2)}) %collective-permute-start.13) | collective-permute-done | bytes 524320 | tf_op jit(solution)/shard_map/ppermute | solution.py:65
  183.8 2.4 %settle_pages.9 = (bf16[32,128,1024]{2,1,0:T(8,128)(2,1)}, bf16[16,4096]{1,0:T(8,128)(2,1)S(1)}) custom-call(s32[256]{0:T(256)S(1)} %or_or_fusion.table_hbm.table, s32[256]{0:T(256)S(1)} %copy-done.1, bf16[16,32,128]{2,1,0:T(8,128)(2,1)S(1)} %bitcast.6, f32[16,32,128]{2,1,0:T(8,128)S(1)} %get-tuple-element.49.rows_in, ...), custom_call_target="tpu_custom_call", output_to_operand_aliasing={{0}: (4, {})} | custom-call | flops 1073741824 | bytes 3145728 | tf_op jit(solution)/shard_map/settle_pages/pallas_call | solution.py:280
  186.2 10.3 %collective-permute-start.15 = (bf16[16,4096]{1,0:T(8,128)(2,1)S(1)}, bf16[16,4096]{1,0:T(8,128)(2,1)S(1)}, u32[]{:S(2)}, u32[]{:S(2)}) collective-permute-start(bf16[16,4096]{1,0:T(8,128)(2,1)S(1)} %get-tuple-element.55.rest_0_), channel_id=1, source_target_pairs={{0,16},{2,18},{4,20},{6,22},{8,24},{10,26},{12,28},{14,30},{16,0},... | collective-permute-start | bytes 393224 | tf_op jit(solution)/shard_map/ppermute | solution.py:70
  196.5 0.5 collective-permute-start.18
  197.1 6.2 %collective-permute-done.15.rest_1_ = bf16[16,4096]{1,0:T(8,128)(2,1)S(1)} collective-permute-done((bf16[16,4096]{1,0:T(8,128)(2,1)S(1)}, bf16[16,4096]{1,0:T(8,128)(2,1)S(1)}, u32[]{:S(2)}, u32[]{:S(2)}) %collective-permute-start.15) | collective-permute-done | bytes 131104 | tf_op jit(solution)/shard_map/ppermute | solution.py:70
  203.2 0.5 collective-permute-done.16.rest_2_
  203.7 0.1 collective-permute-start.24
  203.7 1.5 collective-permute-start.20
  205.2 0.5 collective-permute-start.19
  205.8 2.4 %collective-permute-done.17.rest_3_ = bf16[16,4096]{1,0:T(8,128)(2,1)S(1)} collective-permute-done((bf16[16,4096]{1,0:T(8,128)(2,1)S(1)}, bf16[16,4096]{1,0:T(8,128)(2,1)S(1)}, u32[]{:S(2)}, u32[]{:S(2)}) %collective-permute-start.17) | collective-permute-done | bytes 131104 | tf_op jit(solution)/shard_map/ppermute | solution.py:70
  208.2 0.5 collective-permute-start.21
  208.7 0.5 collective-permute-start.25
  209.2 0.8 collective-permute-done.20.rest_6_
  210.0 2.8 %collective-permute-done.19.rest_5_ = bf16[16,4096]{1,0:T(8,128)(2,1)S(1)} collective-permute-done((bf16[16,4096]{1,0:T(8,128)(2,1)S(1)}, bf16[16,4096]{1,0:T(8,128)(2,1)S(1)}, u32[]{:S(2)}, u32[]{:S(2)}) %collective-permute-start.19) | collective-permute-done | bytes 131104 | tf_op jit(solution)/shard_map/ppermute | solution.py:70
  212.8 2.4 %collective-permute-done.21.rest_7_ = bf16[16,4096]{1,0:T(8,128)(2,1)S(1)} collective-permute-done((bf16[16,4096]{1,0:T(8,128)(2,1)S(1)}, bf16[16,4096]{1,0:T(8,128)(2,1)S(1)}, u32[]{:S(2)}, u32[]{:S(2)}) %collective-permute-start.21) | collective-permute-done | bytes 131104 | tf_op jit(solution)/shard_map/ppermute | solution.py:70
  215.2 2.1 project_some_rows.1.some
  217.4 2.5 %project_rows.1 = (f32[128,512]{1,0:T(8,128)S(1)}, bf16[128,512]{1,0:T(8,128)(2,1)S(1)}) custom-call(bf16[4096,512]{1,0:T(8,128)(2,1)S(1)} %copy-done, f32[128,512]{1,0:T(8,128)S(1)} %project_some_rows.1.some, bf16[16,4096]{1,0:T(8,128)(2,1)S(1)} %collective-permute-done.22.rest_0_, bf16[16,4096]{1,0:T(8,128)(2,1)S(1)} %collective-permute-done.23.rest_1_, ...), custom_call_target="tpu_custom_call" | custom-call | flops 536870912 | bytes 4194304 | tf_op jit(solution)/shard_map/project_rows/pallas_call | solution.py:354
  219.9 1.5 collective-permute-start.30
  221.4 4.4 %collective-permute-done.30 = bf16[128,512]{1,0:T(8,128)(2,1)S(1)} collective-permute-done((bf16[128,512]{1,0:T(8,128)(2,1)S(1)}, bf16[128,512]{1,0:T(8,128)(2,1)S(1)}, u32[]{:S(2)}, u32[]{:S(2)}) %collective-permute-start.30) | collective-permute-done | bytes 131104 | tf_op jit(solution)/shard_map/ppermute | solution.py:409
  225.9 0.7 add_convert_fusion
  (33 shorter events, 0.1 us)
Async XLA Ops:
  1.3 137.1 %copy-start.2 = (bf16[16,4096]{1,0:T(8,128)(2,1)S(1)}, bf16[16,4096]{1,0:T(8,128)(2,1)}, u32[]{:S(2)}) copy-start(bf16[16,4096]{1,0:T(8,128)(2,1)} %param.12) | copy-start | bytes 393220
  1.3 137.1 %copy-start.1 = (s32[256]{0:T(256)S(1)}, s32[256]{0:T(256)}, u32[]{:S(2)}) copy-start(s32[256]{0:T(256)} %row_request.9) | copy-start | bytes 3076
  5.3 16.1 %collective-permute-start.1 = (bf16[2,128,1024]{2,1,0:T(8,128)(2,1)S(1)}, bf16[2,128,1024]{2,1,0:T(8,128)(2,1)S(1)}, u32[]{:S(2)}, u32[]{:S(2)}) collective-permute-start(bf16[2,128,1024]{2,1,0:T(8,128)(2,1)S(1)} %get-tuple-element.32), channel_id=1, source_target_pairs={{0,18},{2,16},{4,22},{6,20},{8,2},{10,0},{12,6},{14,4},{16,26},{18... | collective-permute-start | bytes 1572872 | tf_op jit(solution)/shard_map/ppermute | solution.py:65
  8.9 23.5 %collective-permute-start = (bf16[2,128,1024]{2,1,0:T(8,128)(2,1)S(1)}, bf16[2,128,1024]{2,1,0:T(8,128)(2,1)S(1)}, u32[]{:S(2)}, u32[]{:S(2)}) collective-permute-start(bf16[2,128,1024]{2,1,0:T(8,128)(2,1)S(1)} %get-tuple-element.30.rest_0_), channel_id=1, source_target_pairs={{0,16},{2,18},{4,20},{6,22},{8,0},{10,2},{12,4},{14,6},{16,24},{18... | collective-permute-start | bytes 1572872 | tf_op jit(solution)/shard_map/ppermute | solution.py:65
  17.1 28.3 %collective-permute-start.2 = (bf16[2,128,1024]{2,1,0:T(8,128)(2,1)S(1)}, bf16[2,128,1024]{2,1,0:T(8,128)(2,1)S(1)}, u32[]{:S(2)}, u32[]{:S(2)}) collective-permute-start(bf16[2,128,1024]{2,1,0:T(8,128)(2,1)S(1)} %get-tuple-element.33), channel_id=1, source_target_pairs={{0,8},{2,10},{4,12},{6,14},{8,24},{10,26},{12,28},{14,30},{16,0},{... | collective-permute-start | bytes 1572872 | tf_op jit(solution)/shard_map/ppermute | solution.py:65
  17.4 39.5 %collective-permute-start.3 = (bf16[2,128,1024]{2,1,0:T(8,128)(2,1)S(1)}, bf16[2,128,1024]{2,1,0:T(8,128)(2,1)S(1)}, u32[]{:S(2)}, u32[]{:S(2)}) collective-permute-start(bf16[2,128,1024]{2,1,0:T(8,128)(2,1)S(1)} %get-tuple-element.36), channel_id=1, source_target_pairs={{0,10},{2,8},{4,14},{6,12},{8,26},{10,24},{12,30},{14,28},{16,2},{... | collective-permute-start | bytes 1572872 | tf_op jit(solution)/shard_map/ppermute | solution.py:65
  17.6 50.7 %collective-permute-start.4 = (bf16[2,128,1024]{2,1,0:T(8,128)(2,1)S(1)}, bf16[2,128,1024]{2,1,0:T(8,128)(2,1)S(1)}, u32[]{:S(2)}, u32[]{:S(2)}) collective-permute-start(bf16[2,128,1024]{2,1,0:T(8,128)(2,1)S(1)} %get-tuple-element.37), channel_id=1, source_target_pairs={{0,24},{2,26},{4,28},{6,30},{8,16},{10,18},{12,20},{14,22},{16,8},... | collective-permute-start | bytes 1572872 | tf_op jit(solution)/shard_map/ppermute | solution.py:65
  21.3 93.2 %collective-permute-start.5 = (bf16[2,128,1024]{2,1,0:T(8,128)(2,1)S(1)}, bf16[2,128,1024]{2,1,0:T(8,128)(2,1)S(1)}, u32[]{:S(2)}, u32[]{:S(2)}) collective-permute-start(bf16[2,128,1024]{2,1,0:T(8,128)(2,1)S(1)} %get-tuple-element.38), channel_id=1, source_target_pairs={{0,2},{2,0},{4,6},{6,4},{8,10},{10,8},{12,14},{14,12},{16,18},{18,... | collective-permute-start | bytes 1572872 | tf_op jit(solution)/shard_map/ppermute | solution.py:65
  32.4 82.1 %collective-permute-start.6 = (bf16[2,128,1024]{2,1,0:T(8,128)(2,1)S(1)}, bf16[2,128,1024]{2,1,0:T(8,128)(2,1)S(1)}, u32[]{:S(2)}, u32[]{:S(2)}) collective-permute-start(bf16[2,128,1024]{2,1,0:T(8,128)(2,1)S(1)} %get-tuple-element.41), channel_id=1, source_target_pairs={{0,26},{2,24},{4,30},{6,28},{8,18},{10,16},{12,22},{14,20},{16,10}... | collective-permute-start | bytes 1572872 | tf_op jit(solution)/shard_map/ppermute | solution.py:65
  45.4 69.6 %collective-permute-start.7 = (bf16[2,128,1024]{2,1,0:T(8,128)(2,1)S(1)}, bf16[2,128,1024]{2,1,0:T(8,128)(2,1)S(1)}, u32[]{:S(2)}, u32[]{:S(2)}) collective-permute-start(bf16[2,128,1024]{2,1,0:T(8,128)(2,1)S(1)} %get-tuple-element.42), channel_id=1, source_target_pairs={{0,20},{2,22},{4,16},{6,18},{8,4},{10,6},{12,0},{14,2},{16,28},{18... | collective-permute-start | bytes 1572872 | tf_op jit(solution)/shard_map/ppermute | solution.py:65
  56.9 61.6 %collective-permute-start.8 = (bf16[2,128,1024]{2,1,0:T(8,128)(2,1)S(1)}, bf16[2,128,1024]{2,1,0:T(8,128)(2,1)S(1)}, u32[]{:S(2)}, u32[]{:S(2)}) collective-permute-start(bf16[2,128,1024]{2,1,0:T(8,128)(2,1)S(1)} %get-tuple-element.43), channel_id=1, source_target_pairs={{0,22},{2,20},{4,18},{6,16},{8,6},{10,4},{12,2},{14,0},{16,30},{18... | collective-permute-start | bytes 1572872 | tf_op jit(solution)/shard_map/ppermute | solution.py:65
  68.3 68.2 %collective-permute-start.9 = (bf16[2,128,1024]{2,1,0:T(8,128)(2,1)S(1)}, bf16[2,128,1024]{2,1,0:T(8,128)(2,1)S(1)}, u32[]{:S(2)}, u32[]{:S(2)}) collective-permute-start(bf16[2,128,1024]{2,1,0:T(8,128)(2,1)S(1)} %get-tuple-element.46), channel_id=1, source_target_pairs={{0,12},{2,14},{4,8},{6,10},{8,28},{10,30},{12,24},{14,26},{16,4},{... | collective-permute-start | bytes 1572872 | tf_op jit(solution)/shard_map/ppermute | solution.py:65
  114.5 55.6 %collective-permute-start.10 = (bf16[2,128,1024]{2,1,0:T(8,128)(2,1)S(1)}, bf16[2,128,1024]{2,1,0:T(8,128)(2,1)S(1)}, u32[]{:S(2)}, u32[]{:S(2)}) collective-permute-start(bf16[2,128,1024]{2,1,0:T(8,128)(2,1)S(1)} %get-tuple-element.47), channel_id=1, source_target_pairs={{0,14},{2,12},{4,10},{6,8},{8,30},{10,28},{12,26},{14,24},{16,6},{... | collective-permute-start | bytes 1572872 | tf_op jit(solution)/shard_map/ppermute | solution.py:65
  114.5 59.8 %collective-permute-start.11 = (bf16[2,128,1024]{2,1,0:T(8,128)(2,1)S(1)}, bf16[2,128,1024]{2,1,0:T(8,128)(2,1)S(1)}, u32[]{:S(2)}, u32[]{:S(2)}) collective-permute-start(bf16[2,128,1024]{2,1,0:T(8,128)(2,1)S(1)} %get-tuple-element.48), channel_id=1, source_target_pairs={{0,4},{2,6},{4,0},{6,2},{8,12},{10,14},{12,8},{14,10},{16,20},{18,... | collective-permute-start | bytes 1572872 | tf_op jit(solution)/shard_map/ppermute | solution.py:65
  115.0 61.5 %collective-permute-start.12 = (bf16[2,128,1024]{2,1,0:T(8,128)(2,1)S(1)}, bf16[2,128,1024]{2,1,0:T(8,128)(2,1)S(1)}, u32[]{:S(2)}, u32[]{:S(2)}) collective-permute-start(bf16[2,128,1024]{2,1,0:T(8,128)(2,1)S(1)} %get-tuple-element.51), channel_id=1, source_target_pairs={{0,28},{2,30},{4,24},{6,26},{8,20},{10,22},{12,16},{14,18},{16,12}... | collective-permute-start | bytes 1572872 | tf_op jit(solution)/shard_map/ppermute | solution.py:65
  118.5 65.3 %collective-permute-start.13 = (bf16[2,128,1024]{2,1,0:T(8,128)(2,1)S(1)}, bf16[2,128,1024]{2,1,0:T(8,128)(2,1)S(1)}, u32[]{:S(2)}, u32[]{:S(2)}) collective-permute-start(bf16[2,128,1024]{2,1,0:T(8,128)(2,1)S(1)} %get-tuple-element.52), channel_id=1, source_target_pairs={{0,6},{2,4},{4,2},{6,0},{8,14},{10,12},{12,10},{14,8},{16,22},{18,... | collective-permute-start | bytes 1572872 | tf_op jit(solution)/shard_map/ppermute | solution.py:65
  136.5 47.3 %collective-permute-start.14 = (bf16[2,128,1024]{2,1,0:T(8,128)(2,1)S(1)}, bf16[2,128,1024]{2,1,0:T(8,128)(2,1)S(1)}, u32[]{:S(2)}, u32[]{:S(2)}) collective-permute-start(bf16[2,128,1024]{2,1,0:T(8,128)(2,1)S(1)} %get-tuple-element.53), channel_id=1, source_target_pairs={{0,30},{2,28},{4,26},{6,24},{8,22},{10,20},{12,18},{14,16},{16,14}... | collective-permute-start | bytes 1572872 | tf_op jit(solution)/shard_map/ppermute | solution.py:65
  174.3 40.9 %copy-start = (bf16[4096,512]{1,0:T(8,128)(2,1)S(1)}, bf16[4096,512]{1,0:T(8,128)(2,1)}, u32[]{:S(2)}) copy-start(bf16[4096,512]{1,0:T(8,128)(2,1)} %out_weight.3) | copy-start | bytes 12582916
  186.2 17.0 %collective-permute-start.15 = (bf16[16,4096]{1,0:T(8,128)(2,1)S(1)}, bf16[16,4096]{1,0:T(8,128)(2,1)S(1)}, u32[]{:S(2)}, u32[]{:S(2)}) collective-permute-start(bf16[16,4096]{1,0:T(8,128)(2,1)S(1)} %get-tuple-element.55.rest_0_), channel_id=1, source_target_pairs={{0,16},{2,18},{4,20},{6,22},{8,24},{10,26},{12,28},{14,30},{16,0},... | collective-permute-start | bytes 393224 | tf_op jit(solution)/shard_map/ppermute | solution.py:70
  196.5 6.7 %collective-permute-start.18 = (bf16[16,4096]{1,0:T(8,128)(2,1)S(1)}, bf16[16,4096]{1,0:T(8,128)(2,1)S(1)}, u32[]{:S(2)}, u32[]{:S(2)}) collective-permute-start(bf16[16,4096]{1,0:T(8,128)(2,1)S(1)} %get-tuple-element.55.rest_0_), channel_id=1, source_target_pairs={{0,4},{2,6},{4,0},{6,2},{8,12},{10,14},{12,8},{14,10},{16,20},{18,... | collective-permute-start | bytes 393224 | tf_op jit(solution)/shard_map/ppermute | solution.py:70
  197.1 6.6 %collective-permute-start.16 = (bf16[16,4096]{1,0:T(8,128)(2,1)S(1)}, bf16[16,4096]{1,0:T(8,128)(2,1)S(1)}, u32[]{:S(2)}, u32[]{:S(2)}) collective-permute-start(bf16[16,4096]{1,0:T(8,128)(2,1)S(1)} %get-tuple-element.55.rest_0_), channel_id=1, source_target_pairs={{0,8},{2,10},{4,12},{6,14},{8,0},{10,2},{12,4},{14,6},{16,24},{18,... | collective-permute-start | bytes 393224 | tf_op jit(solution)/shard_map/ppermute | solution.py:70
  197.1 8.2 %collective-permute-start.22 = (bf16[16,4096]{1,0:T(8,128)(2,1)S(1)}, bf16[16,4096]{1,0:T(8,128)(2,1)S(1)}, u32[]{:S(2)}, u32[]{:S(2)}) collective-permute-start(bf16[16,4096]{1,0:T(8,128)(2,1)S(1)} %get-tuple-element.55.rest_0_), channel_id=1, source_target_pairs={{0,2},{2,0},{4,6},{6,4},{8,10},{10,8},{12,14},{14,12},{16,18},{18,... | collective-permute-start | bytes 393224 | tf_op jit(solution)/shard_map/ppermute | solution.py:70
  203.2 5.0 %collective-permute-start.17 = (bf16[16,4096]{1,0:T(8,128)(2,1)S(1)}, bf16[16,4096]{1,0:T(8,128)(2,1)S(1)}, u32[]{:S(2)}, u32[]{:S(2)}) collective-permute-start(bf16[16,4096]{1,0:T(8,128)(2,1)S(1)} %collective-permute-done.15.rest_1_), channel_id=1, source_target_pairs={{0,8},{2,10},{4,12},{6,14},{8,0},{10,2},{12,4},{14,6},{16,24},{18,... | collective-permute-start | bytes 393224 | tf_op jit(solution)/shard_map/ppermute | solution.py:70
  203.2 5.5 %collective-permute-start.26 = (bf16[16,4096]{1,0:T(8,128)(2,1)S(1)}, bf16[16,4096]{1,0:T(8,128)(2,1)S(1)}, u32[]{:S(2)}, u32[]{:S(2)}) collective-permute-start(bf16[16,4096]{1,0:T(8,128)(2,1)S(1)} %collective-permute-done.18.rest_4_), channel_id=1, source_target_pairs={{0,2},{2,0},{4,6},{6,4},{8,10},{10,8},{12,14},{14,12},{16,18},{18,... | collective-permute-start | bytes 393224 | tf_op jit(solution)/shard_map/ppermute | solution.py:70
  203.7 5.0 %collective-permute-start.24 = (bf16[16,4096]{1,0:T(8,128)(2,1)S(1)}, bf16[16,4096]{1,0:T(8,128)(2,1)S(1)}, u32[]{:S(2)}, u32[]{:S(2)}) collective-permute-start(bf16[16,4096]{1,0:T(8,128)(2,1)S(1)} %collective-permute-done.16.rest_2_), channel_id=1, source_target_pairs={{0,2},{2,0},{4,6},{6,4},{8,10},{10,8},{12,14},{14,12},{16,18},{18,... | collective-permute-start | bytes 393224 | tf_op jit(solution)/shard_map/ppermute | solution.py:70
  203.7 6.3 %collective-permute-start.20 = (bf16[16,4096]{1,0:T(8,128)(2,1)S(1)}, bf16[16,4096]{1,0:T(8,128)(2,1)S(1)}, u32[]{:S(2)}, u32[]{:S(2)}) collective-permute-start(bf16[16,4096]{1,0:T(8,128)(2,1)S(1)} %collective-permute-done.16.rest_2_), channel_id=1, source_target_pairs={{0,4},{2,6},{4,0},{6,2},{8,12},{10,14},{12,8},{14,10},{16,20},{18,... | collective-permute-start | bytes 393224 | tf_op jit(solution)/shard_map/ppermute | solution.py:70
  205.2 7.6 %collective-permute-start.19 = (bf16[16,4096]{1,0:T(8,128)(2,1)S(1)}, bf16[16,4096]{1,0:T(8,128)(2,1)S(1)}, u32[]{:S(2)}, u32[]{:S(2)}) collective-permute-start(bf16[16,4096]{1,0:T(8,128)(2,1)S(1)} %collective-permute-done.15.rest_1_), channel_id=1, source_target_pairs={{0,4},{2,6},{4,0},{6,2},{8,12},{10,14},{12,8},{14,10},{16,20},{18,... | collective-permute-start | bytes 393224 | tf_op jit(solution)/shard_map/ppermute | solution.py:70
  208.2 7.0 %collective-permute-start.21 = (bf16[16,4096]{1,0:T(8,128)(2,1)S(1)}, bf16[16,4096]{1,0:T(8,128)(2,1)S(1)}, u32[]{:S(2)}, u32[]{:S(2)}) collective-permute-start(bf16[16,4096]{1,0:T(8,128)(2,1)S(1)} %collective-permute-done.17.rest_3_), channel_id=1, source_target_pairs={{0,4},{2,6},{4,0},{6,2},{8,12},{10,14},{12,8},{14,10},{16,20},{18,... | collective-permute-start | bytes 393224 | tf_op jit(solution)/shard_map/ppermute | solution.py:70
  208.7 8.7 %collective-permute-start.23 = (bf16[16,4096]{1,0:T(8,128)(2,1)S(1)}, bf16[16,4096]{1,0:T(8,128)(2,1)S(1)}, u32[]{:S(2)}, u32[]{:S(2)}) collective-permute-start(bf16[16,4096]{1,0:T(8,128)(2,1)S(1)} %collective-permute-done.15.rest_1_), channel_id=1, source_target_pairs={{0,2},{2,0},{4,6},{6,4},{8,10},{10,8},{12,14},{14,12},{16,18},{18,... | collective-permute-start | bytes 393224 | tf_op jit(solution)/shard_map/ppermute | solution.py:70
  208.7 8.7 %collective-permute-start.25 = (bf16[16,4096]{1,0:T(8,128)(2,1)S(1)}, bf16[16,4096]{1,0:T(8,128)(2,1)S(1)}, u32[]{:S(2)}, u32[]{:S(2)}) collective-permute-start(bf16[16,4096]{1,0:T(8,128)(2,1)S(1)} %collective-permute-done.17.rest_3_), channel_id=1, source_target_pairs={{0,2},{2,0},{4,6},{6,4},{8,10},{10,8},{12,14},{14,12},{16,18},{18,... | collective-permute-start | bytes 393224 | tf_op jit(solution)/shard_map/ppermute | solution.py:70
  210.0 7.3 %collective-permute-start.28 = (bf16[16,4096]{1,0:T(8,128)(2,1)S(1)}, bf16[16,4096]{1,0:T(8,128)(2,1)S(1)}, u32[]{:S(2)}, u32[]{:S(2)}) collective-permute-start(bf16[16,4096]{1,0:T(8,128)(2,1)S(1)} %collective-permute-done.20.rest_6_), channel_id=1, source_target_pairs={{0,2},{2,0},{4,6},{6,4},{8,10},{10,8},{12,14},{14,12},{16,18},{18,... | collective-permute-start | bytes 393224 | tf_op jit(solution)/shard_map/ppermute | solution.py:70
  212.8 4.5 %collective-permute-start.27 = (bf16[16,4096]{1,0:T(8,128)(2,1)S(1)}, bf16[16,4096]{1,0:T(8,128)(2,1)S(1)}, u32[]{:S(2)}, u32[]{:S(2)}) collective-permute-start(bf16[16,4096]{1,0:T(8,128)(2,1)S(1)} %collective-permute-done.19.rest_5_), channel_id=1, source_target_pairs={{0,2},{2,0},{4,6},{6,4},{8,10},{10,8},{12,14},{14,12},{16,18},{18,... | collective-permute-start | bytes 393224 | tf_op jit(solution)/shard_map/ppermute | solution.py:70
  215.2 2.2 collective-permute-start.29
  219.9 6.0 %collective-permute-start.30 = (bf16[128,512]{1,0:T(8,128)(2,1)S(1)}, bf16[128,512]{1,0:T(8,128)(2,1)S(1)}, u32[]{:S(2)}, u32[]{:S(2)}) collective-permute-start(bf16[128,512]{1,0:T(8,128)(2,1)S(1)} %get-tuple-element.57), channel_id=1, source_target_pairs={{0,1},{1,0},{2,3},{3,2},{4,5},{5,4},{6,7},{7,6},{8,9},{9,8},{10,11... | collective-permute-start | bytes 393224 | tf_op jit(solution)/shard_map/ppermute | solution.py:409

commit v16 on v13

--- a/solution.py
+++ b/solution.py
@@ -31,9 +31,11 @@
     order = []
     for low in range(0, near, half):
         swaps = range(low, min(low + half, near))
-        opening = [(1, n) for n in swaps] if low == 0 else [(z, n) for n in swaps for z in (1, 0)]
-        rest = [(z, n) for n in swaps for z in range(2, far)]
-        order += opening + ([(0, n) for n in swaps if n] if low == 0 else []) + rest
+        steps = [z if low == 0 else far - z for z in range(1, far)]
+        opening = [(steps[0], n) for n in swaps] + [(0, n) for n in swaps if n]
+        if low:
+            opening = [(z, n) for n in swaps for z in (steps[0], 0)]
+        order += opening + [(z, n) for n in swaps for z in steps[1:]]
     return [uniform(z, n, dims) for z, n in order]
 
 
@@ -65,13 +67,22 @@
     return lax.ppermute(array, "group", [(s, s ^ mask) for s in range(groups)])
 
 
+def tied(array, after):
+    return lax.optimization_barrier((array, after))[0]
+
+
 def gather_shards(shard):
-    held = {0: shard}
-    mask = lax.axis_size("group") // 2
-    while mask:
-        held.update({done | mask: swap(array, mask) for done, array in held.items()})
-        mask //= 2
-    return held
+    groups = lax.axis_size("group")
+    across, halves = swap(shard, groups // 2), []
+    for start in (0, groups // 2):
+        held, mask = {start: across if start else shard}, groups // 4
+        while mask > 1:
+            held.update({done | mask: swap(array, mask) for done, array in held.items()})
+            mask //= 2
+        halves.append(held)
+        across = tied(across, held[max(held)])
+    held = halves[0] | halves[1]
+    return held | {done | 1: swap(array, 1) for done, array in held.items()}
 
 
 def packed(lengths, prefill_of, decode_of, groups):

time: 226 us -> 236 us (1.044)
  starting transfers between devices: 86 us -> 102 us
  waiting for transfers between devices: 108 us -> 103 us
    ppermute x15, starting transfers between devices: 61.5 us -> 94.9 us  [send_by(): return lax.ppermute(array, 'group', pairs)]
    ppermute x15, waiting for transfers between devices: 96.7 us -> 78.8 us  [send_by(): return lax.ppermute(array, 'group', pairs)]
    ppermute x15, starting transfers between devices: 22.8 us -> 5.74 us  [swap(): return lax.ppermute(array, 'group', [(s, s ^ mask) for s in range(groups)])]
    ppermute x15, waiting for transfers between devices: 7.51 us -> 19.6 us  [swap(): return lax.ppermute(array, 'group', [(s, s ^ mask) for s in range(groups)])]
  transfers between devices with their start and end apart: 31 -> 31, of which waited for: 11 -> 12; matrix products, arithmetic and copies ran while one was open for 0% -> 0% of each run, Pallas kernels for 9% -> 8%
where the time goes in v16:
time: 236 us; the launch traced here: 235 us
  waiting for transfers between devices  103 us (44%)
  starting transfers between devices  102 us (43%)
  Pallas kernels  28.1 us (12%)
    ppermute x15, starting transfers between devices, send_by(): return lax.ppermute(array, 'group', pairs)  94.9 us
    ppermute x15, waiting for transfers between devices, send_by(): return lax.ppermute(array, 'group', pairs)  78.8 us
    ppermute x15, waiting for transfers between devices, swap(): return lax.ppermute(array, 'group', [(s, s ^ mask) for s in range(groups)])  19.6 us
    pallas_call x5, Pallas kernels, settle(): pl.pallas_call(functools.partial(settle_kernel, dims, routes, own, last),...  13 us
    pallas_call x2, Pallas kernels, prepare(): pl.pallas_call(functools.partial(prepare_kernel, dims, routes, own), out_...  10.5 us
    ppermute x15, starting transfers between devices, swap(): return lax.ppermute(array, 'group', [(s, s ^ mask) for s in range(groups)])  5.74 us
  transfers between devices with their start and end apart: 31, of which 12 were waited for; matrix products, arithmetic and copies ran while one was open for 0% of the time, Pallas kernels for 8%

profile of v16, /device:TPU:0, one launch (start us, length us, event | category | flops | bytes accessed | tf_op | source)
XLA Modules:
  0.0 235.3 jit_solution(10932496819719477641)
XLA Ops:
  0.6 0.7 or_or_fusion.table_hbm.table
  1.4 4.0 %outgoing_pages.2 = (bf16[2,128,1024]{2,1,0:T(8,128)(2,1)S(1)}, bf16[2,128,1024]{2,1,0:T(8,128)(2,1)S(1)}) custom-call(s32[256]{0:T(256)S(1)} %or_or_fusion.table_hbm.table, bf16[32,128,1024]{2,1,0:T(8,128)(2,1)} %pool.3), custom_call_target="tpu_custom_call" | custom-call | bytes 2097152 | tf_op jit(solution)/shard_map/outgoing_pages/pallas_call | solution.py:167
  5.3 2.4 %collective-permute-start.1 = (bf16[2,128,1024]{2,1,0:T(8,128)(2,1)S(1)}, bf16[2,128,1024]{2,1,0:T(8,128)(2,1)S(1)}, u32[]{:S(2)}, u32[]{:S(2)}) collective-permute-start(bf16[2,128,1024]{2,1,0:T(8,128)(2,1)S(1)} %get-tuple-element.33), channel_id=1, source_target_pairs={{0,10},{2,8},{4,14},{6,12},{8,18},{10,16},{12,22},{14,20},{16,26},... | collective-permute-start | bytes 1572872 | tf_op jit(solution)/shard_map/ppermute | solution.py:62
  7.8 1.7 collective-permute-start
  9.5 6.5 %outgoing_pages.3 = (bf16[32,128,1024]{2,1,0:T(8,128)(2,1)}, bf16[2,128,1024]{2,1,0:T(8,128)(2,1)S(1)}, bf16[2,128,1024]{2,1,0:T(8,128)(2,1)S(1)}, bf16[2,128,10...) custom-call(s32[256]{0:T(256)S(1)} %or_or_fusion.table_hbm.table, ...), custom_call_target="tpu_custom_call" | custom-call | bytes 14680064 | tf_op jit(solution)/shard_map/outgoing_pages/pallas_call | solution.py:167
  16.0 0.2 collective-permute-start.2
  16.2 1.5 collective-permute-start.3
  17.7 2.2 collective-permute-start.4
  19.9 1.9 collective-permute-done.1.rest_1_
  21.8 1.5 collective-permute-start.5
  23.3 11.2 %collective-permute-done.rest_0_ = bf16[2,128,1024]{2,1,0:T(8,128)(2,1)S(1)} collective-permute-done((bf16[2,128,1024]{2,1,0:T(8,128)(2,1)S(1)}, bf16[2,128,1024]{2,1,0:T(8,128)(2,1)S(1)}, u32[]{:S(2)}, u32[]{:S(2)}) %collective-permute-start) | collective-permute-done | bytes 524320 | tf_op jit(solution)/shard_map/ppermute | solution.py:62
  34.5 1.0 collective-permute-start.6
  35.4 1.6 collective-permute-start.7
  37.1 19.9 %collective-permute-done.3.rest_0_ = bf16[2,128,1024]{2,1,0:T(8,128)(2,1)S(1)} collective-permute-done((bf16[2,128,1024]{2,1,0:T(8,128)(2,1)S(1)}, bf16[2,128,1024]{2,1,0:T(8,128)(2,1)S(1)}, u32[]{:S(2)}, u32[]{:S(2)}) %collective-permute-start.3) | collective-permute-done | bytes 524320 | tf_op jit(solution)/shard_map/ppermute | solution.py:62
  57.0 1.6 collective-permute-start.8
  58.6 0.0 collective-permute-done.4.rest_1_
  58.6 45.4 %collective-permute-start.9 = (bf16[2,128,1024]{2,1,0:T(8,128)(2,1)S(1)}, bf16[2,128,1024]{2,1,0:T(8,128)(2,1)S(1)}, u32[]{:S(2)}, u32[]{:S(2)}) collective-permute-start(bf16[2,128,1024]{2,1,0:T(8,128)(2,1)S(1)} %get-tuple-element.47), channel_id=1, source_target_pairs={{0,30},{2,28},{4,26},{6,24},{8,6},{10,4},{12,2},{14,0},{16,14},{18... | collective-permute-start | bytes 1572872 | tf_op jit(solution)/shard_map/ppermute | solution.py:62
  104.0 1.9 collective-permute-start.10
  105.9 0.0 collective-permute-done.7.rest_1_
  105.9 33.7 %collective-permute-start.12 = (bf16[2,128,1024]{2,1,0:T(8,128)(2,1)S(1)}, bf16[2,128,1024]{2,1,0:T(8,128)(2,1)S(1)}, u32[]{:S(2)}, u32[]{:S(2)}) collective-permute-start(bf16[2,128,1024]{2,1,0:T(8,128)(2,1)S(1)} %get-tuple-element.52), channel_id=1, source_target_pairs={{0,12},{2,14},{4,8},{6,10},{8,20},{10,22},{12,16},{14,18},{16,28},... | collective-permute-start | bytes 1572872 | tf_op jit(solution)/shard_map/ppermute | solution.py:62
  139.6 0.0 collective-permute-done.8.rest_2_
  139.6 0.1 collective-permute-start.14
  139.7 4.4 %settle_pages.5 = (bf16[32,128,1024]{2,1,0:T(8,128)(2,1)}, f32[16,32,128]{2,1,0:T(8,128)S(1)}) custom-call(s32[256]{0:T(256)S(1)} %or_or_fusion.table_hbm.table, s32[256]{0:T(256)S(1)} %copy-done.1, bf16[16,32,128]{2,1,0:T(8,128)(2,1)S(1)} %bitcast.2, f32[16,32,128]{2,1,0:T(8,128)S(1)} %broadcast_in_dim.3.rows_in, ...), custom_call_target="tpu_custom_call", output_to_operand_aliasing={{0}: (4, {})} | custom-call | flops 1073741824 | bytes 3145728 | tf_op jit(solution)/shard_map/settle_pages/pallas_call | solution.py:286
  144.2 2.2 settle_pages.6
  146.4 2.2 settle_pages.7
  148.6 0.0 copy-start
  148.6 2.2 settle_pages.8
  150.8 18.2 %collective-permute-done.12.rest_0_ = bf16[2,128,1024]{2,1,0:T(8,128)(2,1)S(1)} collective-permute-done((bf16[2,128,1024]{2,1,0:T(8,128)(2,1)S(1)}, bf16[2,128,1024]{2,1,0:T(8,128)(2,1)S(1)}, u32[]{:S(2)}, u32[]{:S(2)}) %collective-permute-start.12) | collective-permute-done | bytes 524320 | tf_op jit(solution)/shard_map/ppermute | solution.py:62
  169.0 27.7 %collective-permute-done.13.rest_1_ = bf16[2,128,1024]{2,1,0:T(8,128)(2,1)S(1)} collective-permute-done((bf16[2,128,1024]{2,1,0:T(8,128)(2,1)S(1)}, bf16[2,128,1024]{2,1,0:T(8,128)(2,1)S(1)}, u32[]{:S(2)}, u32[]{:S(2)}) %collective-permute-start.13) | collective-permute-done | bytes 524320 | tf_op jit(solution)/shard_map/ppermute | solution.py:62
  196.7 2.0 settle_pages.9
  198.7 0.1 collective-permute-start.15
  198.7 2.3 collective-permute-start.18
  201.0 6.3 %collective-permute-done.15.rest_1_ = bf16[16,4096]{1,0:T(8,128)(2,1)S(1)} collective-permute-done((bf16[16,4096]{1,0:T(8,128)(2,1)S(1)}, bf16[16,4096]{1,0:T(8,128)(2,1)S(1)}, u32[]{:S(2)}, u32[]{:S(2)}) %collective-permute-start.15) | collective-permute-done | bytes 131104 | tf_op jit(solution)/shard_map/ppermute | solution.py:67
  207.3 2.0 collective-permute-start.16
  209.3 4.4 %collective-permute-done.17.rest_3_ = bf16[16,4096]{1,0:T(8,128)(2,1)S(1)} collective-permute-done((bf16[16,4096]{1,0:T(8,128)(2,1)S(1)}, bf16[16,4096]{1,0:T(8,128)(2,1)S(1)}, u32[]{:S(2)}, u32[]{:S(2)}) %collective-permute-start.17) | collective-permute-done | bytes 131104 | tf_op jit(solution)/shard_map/ppermute | solution.py:67
  213.7 1.6 collective-permute-done.16.rest_2_
  215.3 0.5 collective-permute-start.23
  215.8 0.3 collective-permute-start.20
  216.1 2.6 %collective-permute-done.19.rest_5_ = bf16[16,4096]{1,0:T(8,128)(2,1)S(1)} collective-permute-done((bf16[16,4096]{1,0:T(8,128)(2,1)S(1)}, bf16[16,4096]{1,0:T(8,128)(2,1)S(1)}, u32[]{:S(2)}, u32[]{:S(2)}) %collective-permute-start.19) | collective-permute-done | bytes 131104 | tf_op jit(solution)/shard_map/ppermute | solution.py:67
  218.7 0.5 collective-permute-start.25
  219.2 0.1 collective-permute-start.27
  219.2 2.9 %collective-permute-done.20.rest_6_ = bf16[16,4096]{1,0:T(8,128)(2,1)S(1)} collective-permute-done((bf16[16,4096]{1,0:T(8,128)(2,1)S(1)}, bf16[16,4096]{1,0:T(8,128)(2,1)S(1)}, u32[]{:S(2)}, u32[]{:S(2)}) %collective-permute-start.20) | collective-permute-done | bytes 131104 | tf_op jit(solution)/shard_map/ppermute | solution.py:67
  222.2 1.8 collective-permute-done.21.rest_7_
  224.0 2.1 project_some_rows.1.some
  226.2 2.5 %project_rows.1 = (f32[128,512]{1,0:T(8,128)S(1)}, bf16[128,512]{1,0:T(8,128)(2,1)S(1)}) custom-call(bf16[4096,512]{1,0:T(8,128)(2,1)S(1)} %copy-done, f32[128,512]{1,0:T(8,128)S(1)} %project_some_rows.1.some, bf16[16,4096]{1,0:T(8,128)(2,1)S(1)} %collective-permute-done.22.rest_0_, bf16[16,4096]{1,0:T(8,128)(2,1)S(1)} %collective-permute-done.23.rest_1_, ...), custom_call_target="tpu_custom_call" | custom-call | flops 536870912 | bytes 4194304 | tf_op jit(solution)/shard_map/project_rows/pallas_call | solution.py:360
  228.7 1.5 collective-permute-start.30
  230.2 4.4 %collective-permute-done.30 = bf16[128,512]{1,0:T(8,128)(2,1)S(1)} collective-permute-done((bf16[128,512]{1,0:T(8,128)(2,1)S(1)}, bf16[128,512]{1,0:T(8,128)(2,1)S(1)}, u32[]{:S(2)}, u32[]{:S(2)}) %collective-permute-start.30) | collective-permute-done | bytes 131104 | tf_op jit(solution)/shard_map/ppermute | solution.py:415
  234.7 0.7 add_convert_fusion
  (33 shorter events, 0.1 us)
Async XLA Ops:
  1.3 138.3 %copy-start.2 = (bf16[16,4096]{1,0:T(8,128)(2,1)S(1)}, bf16[16,4096]{1,0:T(8,128)(2,1)}, u32[]{:S(2)}) copy-start(bf16[16,4096]{1,0:T(8,128)(2,1)} %param.12) | copy-start | bytes 393220
  1.3 138.4 %copy-start.1 = (s32[256]{0:T(256)S(1)}, s32[256]{0:T(256)}, u32[]{:S(2)}) copy-start(s32[256]{0:T(256)} %row_request.9) | copy-start | bytes 3076
  5.3 16.5 %collective-permute-start.1 = (bf16[2,128,1024]{2,1,0:T(8,128)(2,1)S(1)}, bf16[2,128,1024]{2,1,0:T(8,128)(2,1)S(1)}, u32[]{:S(2)}, u32[]{:S(2)}) collective-permute-start(bf16[2,128,1024]{2,1,0:T(8,128)(2,1)S(1)} %get-tuple-element.33), channel_id=1, source_target_pairs={{0,10},{2,8},{4,14},{6,12},{8,18},{10,16},{12,22},{14,20},{16,26},... | collective-permute-start | bytes 1572872 | tf_op jit(solution)/shard_map/ppermute | solution.py:62
  7.8 26.7 %collective-permute-start = (bf16[2,128,1024]{2,1,0:T(8,128)(2,1)S(1)}, bf16[2,128,1024]{2,1,0:T(8,128)(2,1)S(1)}, u32[]{:S(2)}, u32[]{:S(2)}) collective-permute-start(bf16[2,128,1024]{2,1,0:T(8,128)(2,1)S(1)} %get-tuple-element.31.rest_0_), channel_id=1, source_target_pairs={{0,8},{2,10},{4,12},{6,14},{8,16},{10,18},{12,20},{14,22},{16,24},... | collective-permute-start | bytes 1572872 | tf_op jit(solution)/shard_map/ppermute | solution.py:62
  16.0 19.5 %collective-permute-start.2 = (bf16[2,128,1024]{2,1,0:T(8,128)(2,1)S(1)}, bf16[2,128,1024]{2,1,0:T(8,128)(2,1)S(1)}, u32[]{:S(2)}, u32[]{:S(2)}) collective-permute-start(bf16[2,128,1024]{2,1,0:T(8,128)(2,1)S(1)} %get-tuple-element.34), channel_id=1, source_target_pairs={{0,2},{2,0},{4,6},{6,4},{8,10},{10,8},{12,14},{14,12},{16,18},{18,... | collective-permute-start | bytes 1572872 | tf_op jit(solution)/shard_map/ppermute | solution.py:62
  16.2 40.8 %collective-permute-start.3 = (bf16[2,128,1024]{2,1,0:T(8,128)(2,1)S(1)}, bf16[2,128,1024]{2,1,0:T(8,128)(2,1)S(1)}, u32[]{:S(2)}, u32[]{:S(2)}) collective-permute-start(bf16[2,128,1024]{2,1,0:T(8,128)(2,1)S(1)} %get-tuple-element.37), channel_id=1, source_target_pairs={{0,16},{2,18},{4,20},{6,22},{8,24},{10,26},{12,28},{14,30},{16,0},... | collective-permute-start | bytes 1572872 | tf_op jit(solution)/shard_map/ppermute | solution.py:62
  17.7 40.9 %collective-permute-start.4 = (bf16[2,128,1024]{2,1,0:T(8,128)(2,1)S(1)}, bf16[2,128,1024]{2,1,0:T(8,128)(2,1)S(1)}, u32[]{:S(2)}, u32[]{:S(2)}) collective-permute-start(bf16[2,128,1024]{2,1,0:T(8,128)(2,1)S(1)} %get-tuple-element.38), channel_id=1, source_target_pairs={{0,24},{2,26},{4,28},{6,30},{8,0},{10,2},{12,4},{14,6},{16,8},{18,... | collective-permute-start | bytes 1572872 | tf_op jit(solution)/shard_map/ppermute | solution.py:62
  21.8 82.2 %collective-permute-start.5 = (bf16[2,128,1024]{2,1,0:T(8,128)(2,1)S(1)}, bf16[2,128,1024]{2,1,0:T(8,128)(2,1)S(1)}, u32[]{:S(2)}, u32[]{:S(2)}) collective-permute-start(bf16[2,128,1024]{2,1,0:T(8,128)(2,1)S(1)} %get-tuple-element.39), channel_id=1, source_target_pairs={{0,18},{2,16},{4,22},{6,20},{8,26},{10,24},{12,30},{14,28},{16,2},... | collective-permute-start | bytes 1572872 | tf_op jit(solution)/shard_map/ppermute | solution.py:62
  34.5 71.4 %collective-permute-start.6 = (bf16[2,128,1024]{2,1,0:T(8,128)(2,1)S(1)}, bf16[2,128,1024]{2,1,0:T(8,128)(2,1)S(1)}, u32[]{:S(2)}, u32[]{:S(2)}) collective-permute-start(bf16[2,128,1024]{2,1,0:T(8,128)(2,1)S(1)} %get-tuple-element.42), channel_id=1, source_target_pairs={{0,26},{2,24},{4,30},{6,28},{8,2},{10,0},{12,6},{14,4},{16,10},{18... | collective-permute-start | bytes 1572872 | tf_op jit(solution)/shard_map/ppermute | solution.py:62
  35.4 70.5 %collective-permute-start.7 = (bf16[2,128,1024]{2,1,0:T(8,128)(2,1)S(1)}, bf16[2,128,1024]{2,1,0:T(8,128)(2,1)S(1)}, u32[]{:S(2)}, u32[]{:S(2)}) collective-permute-start(bf16[2,128,1024]{2,1,0:T(8,128)(2,1)S(1)} %get-tuple-element.43), channel_id=1, source_target_pairs={{0,28},{2,30},{4,24},{6,26},{8,4},{10,6},{12,0},{14,2},{16,12},{18... | collective-permute-start | bytes 1572872 | tf_op jit(solution)/shard_map/ppermute | solution.py:62
  57.0 82.6 %collective-permute-start.8 = (bf16[2,128,1024]{2,1,0:T(8,128)(2,1)S(1)}, bf16[2,128,1024]{2,1,0:T(8,128)(2,1)S(1)}, u32[]{:S(2)}, u32[]{:S(2)}) collective-permute-start(bf16[2,128,1024]{2,1,0:T(8,128)(2,1)S(1)} %get-tuple-element.44), channel_id=1, source_target_pairs={{0,4},{2,6},{4,0},{6,2},{8,12},{10,14},{12,8},{14,10},{16,20},{18,... | collective-permute-start | bytes 1572872 | tf_op jit(solution)/shard_map/ppermute | solution.py:62
  58.6 81.0 %collective-permute-start.9 = (bf16[2,128,1024]{2,1,0:T(8,128)(2,1)S(1)}, bf16[2,128,1024]{2,1,0:T(8,128)(2,1)S(1)}, u32[]{:S(2)}, u32[]{:S(2)}) collective-permute-start(bf16[2,128,1024]{2,1,0:T(8,128)(2,1)S(1)} %get-tuple-element.47), channel_id=1, source_target_pairs={{0,30},{2,28},{4,26},{6,24},{8,6},{10,4},{12,2},{14,0},{16,14},{18... | collective-permute-start | bytes 1572872 | tf_op jit(solution)/shard_map/ppermute | solution.py:62
  104.0 44.6 %collective-permute-start.10 = (bf16[2,128,1024]{2,1,0:T(8,128)(2,1)S(1)}, bf16[2,128,1024]{2,1,0:T(8,128)(2,1)S(1)}, u32[]{:S(2)}, u32[]{:S(2)}) collective-permute-start(bf16[2,128,1024]{2,1,0:T(8,128)(2,1)S(1)} %get-tuple-element.48), channel_id=1, source_target_pairs={{0,6},{2,4},{4,2},{6,0},{8,14},{10,12},{12,10},{14,8},{16,22},{18,... | collective-permute-start | bytes 1572872 | tf_op jit(solution)/shard_map/ppermute | solution.py:62
  105.9 42.7 %collective-permute-start.11 = (bf16[2,128,1024]{2,1,0:T(8,128)(2,1)S(1)}, bf16[2,128,1024]{2,1,0:T(8,128)(2,1)S(1)}, u32[]{:S(2)}, u32[]{:S(2)}) collective-permute-start(bf16[2,128,1024]{2,1,0:T(8,128)(2,1)S(1)} %get-tuple-element.49), channel_id=1, source_target_pairs={{0,20},{2,22},{4,16},{6,18},{8,28},{10,30},{12,24},{14,26},{16,4},... | collective-permute-start | bytes 1572872 | tf_op jit(solution)/shard_map/ppermute | solution.py:62
  105.9 63.0 %collective-permute-start.12 = (bf16[2,128,1024]{2,1,0:T(8,128)(2,1)S(1)}, bf16[2,128,1024]{2,1,0:T(8,128)(2,1)S(1)}, u32[]{:S(2)}, u32[]{:S(2)}) collective-permute-start(bf16[2,128,1024]{2,1,0:T(8,128)(2,1)S(1)} %get-tuple-element.52), channel_id=1, source_target_pairs={{0,12},{2,14},{4,8},{6,10},{8,20},{10,22},{12,16},{14,18},{16,28},... | collective-permute-start | bytes 1572872 | tf_op jit(solution)/shard_map/ppermute | solution.py:62
  139.6 57.1 %collective-permute-start.13 = (bf16[2,128,1024]{2,1,0:T(8,128)(2,1)S(1)}, bf16[2,128,1024]{2,1,0:T(8,128)(2,1)S(1)}, u32[]{:S(2)}, u32[]{:S(2)}) collective-permute-start(bf16[2,128,1024]{2,1,0:T(8,128)(2,1)S(1)} %get-tuple-element.53), channel_id=1, source_target_pairs={{0,22},{2,20},{4,18},{6,16},{8,30},{10,28},{12,26},{14,24},{16,6},... | collective-permute-start | bytes 1572872 | tf_op jit(solution)/shard_map/ppermute | solution.py:62
  139.6 57.1 %collective-permute-start.14 = (bf16[2,128,1024]{2,1,0:T(8,128)(2,1)S(1)}, bf16[2,128,1024]{2,1,0:T(8,128)(2,1)S(1)}, u32[]{:S(2)}, u32[]{:S(2)}) collective-permute-start(bf16[2,128,1024]{2,1,0:T(8,128)(2,1)S(1)} %get-tuple-element.54), channel_id=1, source_target_pairs={{0,14},{2,12},{4,10},{6,8},{8,22},{10,20},{12,18},{14,16},{16,30},... | collective-permute-start | bytes 1572872 | tf_op jit(solution)/shard_map/ppermute | solution.py:62
  148.6 75.4 %copy-start = (bf16[4096,512]{1,0:T(8,128)(2,1)S(1)}, bf16[4096,512]{1,0:T(8,128)(2,1)}, u32[]{:S(2)}) copy-start(bf16[4096,512]{1,0:T(8,128)(2,1)} %out_weight.3) | copy-start | bytes 12582916
  198.7 8.6 %collective-permute-start.15 = (bf16[16,4096]{1,0:T(8,128)(2,1)S(1)}, bf16[16,4096]{1,0:T(8,128)(2,1)S(1)}, u32[]{:S(2)}, u32[]{:S(2)}) collective-permute-start(bf16[16,4096]{1,0:T(8,128)(2,1)S(1)} %get-tuple-element.56.rest_0_), channel_id=1, source_target_pairs={{0,8},{2,10},{4,12},{6,14},{8,0},{10,2},{12,4},{14,6},{16,24},{18,... | collective-permute-start | bytes 393224 | tf_op jit(solution)/shard_map/ppermute | solution.py:67
  198.7 10.6 %collective-permute-start.18 = (bf16[16,4096]{1,0:T(8,128)(2,1)S(1)}, bf16[16,4096]{1,0:T(8,128)(2,1)S(1)}, u32[]{:S(2)}, u32[]{:S(2)}) collective-permute-start(bf16[16,4096]{1,0:T(8,128)(2,1)S(1)} %get-tuple-element.56.rest_0_), channel_id=1, source_target_pairs={{0,16},{2,18},{4,20},{6,22},{8,24},{10,26},{12,28},{14,30},{16,0},... | collective-permute-start | bytes 393224 | tf_op jit(solution)/shard_map/ppermute | solution.py:67
  207.3 6.4 %collective-permute-start.17 = (bf16[16,4096]{1,0:T(8,128)(2,1)S(1)}, bf16[16,4096]{1,0:T(8,128)(2,1)S(1)}, u32[]{:S(2)}, u32[]{:S(2)}) collective-permute-start(bf16[16,4096]{1,0:T(8,128)(2,1)S(1)} %collective-permute-done.15.rest_1_), channel_id=1, source_target_pairs={{0,4},{2,6},{4,0},{6,2},{8,12},{10,14},{12,8},{14,10},{16,20},{18,... | collective-permute-start | bytes 393224 | tf_op jit(solution)/shard_map/ppermute | solution.py:67
  207.3 8.0 %collective-permute-start.16 = (bf16[16,4096]{1,0:T(8,128)(2,1)S(1)}, bf16[16,4096]{1,0:T(8,128)(2,1)S(1)}, u32[]{:S(2)}, u32[]{:S(2)}) collective-permute-start(bf16[16,4096]{1,0:T(8,128)(2,1)S(1)} %get-tuple-element.56.rest_0_), channel_id=1, source_target_pairs={{0,4},{2,6},{4,0},{6,2},{8,12},{10,14},{12,8},{14,10},{16,20},{18,... | collective-permute-start | bytes 393224 | tf_op jit(solution)/shard_map/ppermute | solution.py:67
  213.7 5.0 %collective-permute-start.19 = (bf16[16,4096]{1,0:T(8,128)(2,1)S(1)}, bf16[16,4096]{1,0:T(8,128)(2,1)S(1)}, u32[]{:S(2)}, u32[]{:S(2)}) collective-permute-start(bf16[16,4096]{1,0:T(8,128)(2,1)S(1)} %collective-permute-done.18.rest_4_), channel_id=1, source_target_pairs={{0,8},{2,10},{4,12},{6,14},{8,0},{10,2},{12,4},{14,6},{16,24},{18,... | collective-permute-start | bytes 393224 | tf_op jit(solution)/shard_map/ppermute | solution.py:67
  213.7 5.0 %collective-permute-start.22 = (bf16[16,4096]{1,0:T(8,128)(2,1)S(1)}, bf16[16,4096]{1,0:T(8,128)(2,1)S(1)}, u32[]{:S(2)}, u32[]{:S(2)}) collective-permute-start(bf16[16,4096]{1,0:T(8,128)(2,1)S(1)} %get-tuple-element.56.rest_0_), channel_id=1, source_target_pairs={{0,2},{2,0},{4,6},{6,4},{8,10},{10,8},{12,14},{14,12},{16,18},{18,... | collective-permute-start | bytes 393224 | tf_op jit(solution)/shard_map/ppermute | solution.py:67
  215.3 3.4 %collective-permute-start.24 = (bf16[16,4096]{1,0:T(8,128)(2,1)S(1)}, bf16[16,4096]{1,0:T(8,128)(2,1)S(1)}, u32[]{:S(2)}, u32[]{:S(2)}) collective-permute-start(bf16[16,4096]{1,0:T(8,128)(2,1)S(1)} %collective-permute-done.16.rest_2_), channel_id=1, source_target_pairs={{0,2},{2,0},{4,6},{6,4},{8,10},{10,8},{12,14},{14,12},{16,18},{18,... | collective-permute-start | bytes 393224 | tf_op jit(solution)/shard_map/ppermute | solution.py:67
  215.3 3.9 %collective-permute-start.23 = (bf16[16,4096]{1,0:T(8,128)(2,1)S(1)}, bf16[16,4096]{1,0:T(8,128)(2,1)S(1)}, u32[]{:S(2)}, u32[]{:S(2)}) collective-permute-start(bf16[16,4096]{1,0:T(8,128)(2,1)S(1)} %collective-permute-done.15.rest_1_), channel_id=1, source_target_pairs={{0,2},{2,0},{4,6},{6,4},{8,10},{10,8},{12,14},{14,12},{16,18},{18,... | collective-permute-start | bytes 393224 | tf_op jit(solution)/shard_map/ppermute | solution.py:67
  215.8 6.4 %collective-permute-start.20 = (bf16[16,4096]{1,0:T(8,128)(2,1)S(1)}, bf16[16,4096]{1,0:T(8,128)(2,1)S(1)}, u32[]{:S(2)}, u32[]{:S(2)}) collective-permute-start(bf16[16,4096]{1,0:T(8,128)(2,1)S(1)} %collective-permute-done.18.rest_4_), channel_id=1, source_target_pairs={{0,4},{2,6},{4,0},{6,2},{8,12},{10,14},{12,8},{14,10},{16,20},{18,... | collective-permute-start | bytes 393224 | tf_op jit(solution)/shard_map/ppermute | solution.py:67
  218.6 5.4 %collective-permute-start.21 = (bf16[16,4096]{1,0:T(8,128)(2,1)S(1)}, bf16[16,4096]{1,0:T(8,128)(2,1)S(1)}, u32[]{:S(2)}, u32[]{:S(2)}) collective-permute-start(bf16[16,4096]{1,0:T(8,128)(2,1)S(1)} %collective-permute-done.19.rest_5_), channel_id=1, source_target_pairs={{0,4},{2,6},{4,0},{6,2},{8,12},{10,14},{12,8},{14,10},{16,20},{18,... | collective-permute-start | bytes 393224 | tf_op jit(solution)/shard_map/ppermute | solution.py:67
  218.6 7.5 %collective-permute-start.26 = (bf16[16,4096]{1,0:T(8,128)(2,1)S(1)}, bf16[16,4096]{1,0:T(8,128)(2,1)S(1)}, u32[]{:S(2)}, u32[]{:S(2)}) collective-permute-start(bf16[16,4096]{1,0:T(8,128)(2,1)S(1)} %collective-permute-done.18.rest_4_), channel_id=1, source_target_pairs={{0,2},{2,0},{4,6},{6,4},{8,10},{10,8},{12,14},{14,12},{16,18},{18,... | collective-permute-start | bytes 393224 | tf_op jit(solution)/shard_map/ppermute | solution.py:67
  218.7 7.5 %collective-permute-start.25 = (bf16[16,4096]{1,0:T(8,128)(2,1)S(1)}, bf16[16,4096]{1,0:T(8,128)(2,1)S(1)}, u32[]{:S(2)}, u32[]{:S(2)}) collective-permute-start(bf16[16,4096]{1,0:T(8,128)(2,1)S(1)} %collective-permute-done.17.rest_3_), channel_id=1, source_target_pairs={{0,2},{2,0},{4,6},{6,4},{8,10},{10,8},{12,14},{14,12},{16,18},{18,... | collective-permute-start | bytes 393224 | tf_op jit(solution)/shard_map/ppermute | solution.py:67
  219.2 7.0 %collective-permute-start.27 = (bf16[16,4096]{1,0:T(8,128)(2,1)S(1)}, bf16[16,4096]{1,0:T(8,128)(2,1)S(1)}, u32[]{:S(2)}, u32[]{:S(2)}) collective-permute-start(bf16[16,4096]{1,0:T(8,128)(2,1)S(1)} %collective-permute-done.19.rest_5_), channel_id=1, source_target_pairs={{0,2},{2,0},{4,6},{6,4},{8,10},{10,8},{12,14},{14,12},{16,18},{18,... | collective-permute-start | bytes 393224 | tf_op jit(solution)/shard_map/ppermute | solution.py:67
  222.2 4.0 %collective-permute-start.28 = (bf16[16,4096]{1,0:T(8,128)(2,1)S(1)}, bf16[16,4096]{1,0:T(8,128)(2,1)S(1)}, u32[]{:S(2)}, u32[]{:S(2)}) collective-permute-start(bf16[16,4096]{1,0:T(8,128)(2,1)S(1)} %collective-permute-done.20.rest_6_), channel_id=1, source_target_pairs={{0,2},{2,0},{4,6},{6,4},{8,10},{10,8},{12,14},{14,12},{16,18},{18,... | collective-permute-start | bytes 393224 | tf_op jit(solution)/shard_map/ppermute | solution.py:67
  224.0 2.2 collective-permute-start.29
  228.7 6.0 %collective-permute-start.30 = (bf16[128,512]{1,0:T(8,128)(2,1)S(1)}, bf16[128,512]{1,0:T(8,128)(2,1)S(1)}, u32[]{:S(2)}, u32[]{:S(2)}) collective-permute-start(bf16[128,512]{1,0:T(8,128)(2,1)S(1)} %get-tuple-element.59), channel_id=1, source_target_pairs={{0,1},{1,0},{2,3},{3,2},{4,5},{5,4},{6,7},{7,6},{8,9},{9,8},{10,11... | collective-permute-start | bytes 393224 | tf_op jit(solution)/shard_map/ppermute | solution.py:415

commit v17 on v13

--- a/solution.py
+++ b/solution.py
@@ -28,13 +28,17 @@
 def page_rounds(dims):
     far, near = dims
     half = max(near // 2, 1)
-    order = []
-    for low in range(0, near, half):
-        swaps = range(low, min(low + half, near))
-        opening = [(1, n) for n in swaps] if low == 0 else [(z, n) for n in swaps for z in (1, 0)]
-        rest = [(z, n) for n in swaps for z in range(2, far)]
-        order += opening + ([(0, n) for n in swaps if n] if low == 0 else []) + rest
-    return [uniform(z, n, dims) for z, n in order]
+    same, other = range(half), range(half, near)
+    if far == 4:
+        rounds = [((2, n), (0, n), (3, n), (1, n)) for n in same]
+        rounds += [((3, n), (1, n), (2, n), (0, n)) for n in same if n]
+        rounds += [((3, 0), (2, 0), (1, 0), (0, 0))]
+        rounds += [((0, n), (2, n), (1, n), (3, n)) for n in same if n]
+        rounds += [((1, n), (3, n), (0, n), (2, n)) for n in same]
+    else:
+        rounds = [uniform(z, n, dims) for z in range(far) for n in same if z or n]
+    rounds += [uniform(z, n, dims) for n in other for z in (1, 0)]
+    return rounds + [uniform(z, n, dims) for n in other for z in range(2, far)]
 
 
 def reverse(route):
@@ -86,7 +90,7 @@
 
 
 def prepare_kernel(dims, routes, own, table_hbm, pool, *rest):
-    table, held, zero_page, start_of, count_of, table_sem, in_sems, out_sem = rest[-8:]
+    table, held, zero_page, start_of, count_of, table_sem, in_sems, out_sems = rest[-8:]
     received = rest[-8 - len(routes) - own : -8 - len(routes)]
     sends = rest[-8 - len(routes) : -8]
     me = lax.axis_index("group")
@@ -120,7 +124,8 @@
                 there = page < count_of[to]
                 source = pool.at[jnp.where(there, start_of[to] + page, 0)]
                 buffer, place = held.at[i, page], target.at[base + page]
-                do(there, (source, buffer, in_sems.at[i, page]), (buffer, place, out_sem), (zero_page, place, out_sem))
+                sem = out_sems.at[i, page]
+                do(there, (source, buffer, in_sems.at[i, page]), (buffer, place, sem), (zero_page, place, sem))
 
     def fetch(there, load, store, blank):
         @pl.when(there)
@@ -166,7 +171,7 @@
             pltpu.SMEM((groups + 1,), jnp.int32),
             pltpu.SemaphoreType.DMA,
             pltpu.SemaphoreType.DMA((blocks, MAX_PAGES)),
-            pltpu.SemaphoreType.DMA,
+            pltpu.SemaphoreType.DMA((blocks, MAX_PAGES)),
         ],
         compiler_params=pltpu.CompilerParams(vmem_limit_bytes=VMEM_LIMIT),
         cost_estimate=pl.CostEstimate(

time: 226 us -> 230 us (1.018)
  waiting for transfers between devices: 108 us -> 135 us
  starting transfers between devices: 86 us -> 63.2 us
    ppermute x15, waiting for transfers between devices: 96.7 us -> 123 us  [send_by(): return lax.ppermute(array, 'group', pairs)]
    ppermute x15, starting transfers between devices: 61.5 us -> 43.9 us  [send_by(): return lax.ppermute(array, 'group', pairs)]
    ppermute x15, starting transfers between devices: 22.8 us -> 17.8 us  [swap(): return lax.ppermute(array, 'group', [(s, s ^ mask) for s in range(groups)])]
  transfers between devices with their start and end apart: 31 -> 31, of which waited for: 11 -> 15; matrix products, arithmetic and copies ran while one was open for 0% -> 0% of each run, Pallas kernels for 9% -> 9%
where the time goes in v17:
time: 230 us; the launch traced here: 229 us
  waiting for transfers between devices  135 us (59%)
  starting transfers between devices  63.2 us (27%)
  Pallas kernels  28.9 us (13%)
    ppermute x15, waiting for transfers between devices, send_by(): return lax.ppermute(array, 'group', pairs)  123 us
    ppermute x15, starting transfers between devices, send_by(): return lax.ppermute(array, 'group', pairs)  43.9 us
    ppermute x15, starting transfers between devices, swap(): return lax.ppermute(array, 'group', [(s, s ^ mask) for s in range(groups)])  17.8 us
    pallas_call x5, Pallas kernels, settle(): pl.pallas_call(functools.partial(settle_kernel, dims, routes, own, last),...  13.4 us
    pallas_call x2, Pallas kernels, prepare(): pl.pallas_call(functools.partial(prepare_kernel, dims, routes, own), out_...  10.8 us
    ppermute x15, waiting for transfers between devices, swap(): return lax.ppermute(array, 'group', [(s, s ^ mask) for s in range(groups)])  7.27 us
  transfers between devices with their start and end apart: 31, of which 15 were waited for; matrix products, arithmetic and copies ran while one was open for 0% of the time, Pallas kernels for 9%

profile of v17, /device:TPU:0, one launch (start us, length us, event | category | flops | bytes accessed | tf_op | source)
XLA Modules:
  0.0 229.2 jit_solution(9452775499195199772)
XLA Ops:
  0.6 0.7 or_or_fusion.table_hbm.table
  1.4 4.0 %outgoing_pages.2 = (bf16[2,128,1024]{2,1,0:T(8,128)(2,1)S(1)}, bf16[2,128,1024]{2,1,0:T(8,128)(2,1)S(1)}) custom-call(s32[256]{0:T(256)S(1)} %or_or_fusion.table_hbm.table, bf16[32,128,1024]{2,1,0:T(8,128)(2,1)} %pool.3), custom_call_target="tpu_custom_call" | custom-call | bytes 2097152 | tf_op jit(solution)/shard_map/outgoing_pages/pallas_call | solution.py:161
  5.4 3.5 %collective-permute-start.1 = (bf16[2,128,1024]{2,1,0:T(8,128)(2,1)S(1)}, bf16[2,128,1024]{2,1,0:T(8,128)(2,1)S(1)}, u32[]{:S(2)}, u32[]{:S(2)}) collective-permute-start(bf16[2,128,1024]{2,1,0:T(8,128)(2,1)S(1)} %get-tuple-element.32), channel_id=1, source_target_pairs={{0,18},{2,16},{4,22},{6,20},{8,2},{10,0},{12,6},{14,4},{16,26},{18... | collective-permute-start | bytes 1572872 | tf_op jit(solution)/shard_map/ppermute | solution.py:64
  8.8 1.6 collective-permute-start
  10.4 6.8 %outgoing_pages.3 = (bf16[32,128,1024]{2,1,0:T(8,128)(2,1)}, bf16[2,128,1024]{2,1,0:T(8,128)(2,1)S(1)}, bf16[2,128,1024]{2,1,0:T(8,128)(2,1)S(1)}, bf16[2,128,10...) custom-call(s32[256]{0:T(256)S(1)} %or_or_fusion.table_hbm.table, ...), custom_call_target="tpu_custom_call" | custom-call | bytes 14680064 | tf_op jit(solution)/shard_map/outgoing_pages/pallas_call | solution.py:161
  17.3 3.5 %collective-permute-start.3 = (bf16[2,128,1024]{2,1,0:T(8,128)(2,1)S(1)}, bf16[2,128,1024]{2,1,0:T(8,128)(2,1)S(1)}, u32[]{:S(2)}, u32[]{:S(2)}) collective-permute-start(bf16[2,128,1024]{2,1,0:T(8,128)(2,1)S(1)} %get-tuple-element.36), channel_id=1, source_target_pairs={{0,24},{2,26},{4,28},{6,30},{8,16},{10,18},{12,20},{14,22},{16,8},... | collective-permute-start | bytes 1572872 | tf_op jit(solution)/shard_map/ppermute | solution.py:64
  20.9 0.2 collective-permute-done.1.rest_1_
  21.1 2.3 %collective-permute-start.5 = (bf16[2,128,1024]{2,1,0:T(8,128)(2,1)S(1)}, bf16[2,128,1024]{2,1,0:T(8,128)(2,1)S(1)}, u32[]{:S(2)}, u32[]{:S(2)}) collective-permute-start(bf16[2,128,1024]{2,1,0:T(8,128)(2,1)S(1)} %get-tuple-element.38), channel_id=1, source_target_pairs={{0,8},{2,10},{4,12},{6,14},{8,24},{10,26},{12,28},{14,30},{16,0},{... | collective-permute-start | bytes 1572872 | tf_op jit(solution)/shard_map/ppermute | solution.py:64
  23.4 8.9 %collective-permute-done.rest_0_ = bf16[2,128,1024]{2,1,0:T(8,128)(2,1)S(1)} collective-permute-done((bf16[2,128,1024]{2,1,0:T(8,128)(2,1)S(1)}, bf16[2,128,1024]{2,1,0:T(8,128)(2,1)S(1)}, u32[]{:S(2)}, u32[]{:S(2)}) %collective-permute-start) | collective-permute-done | bytes 524320 | tf_op jit(solution)/shard_map/ppermute | solution.py:64
  32.3 2.0 collective-permute-start.6
  34.3 11.0 %collective-permute-done.2.rest_2_ = bf16[2,128,1024]{2,1,0:T(8,128)(2,1)S(1)} collective-permute-done((bf16[2,128,1024]{2,1,0:T(8,128)(2,1)S(1)}, bf16[2,128,1024]{2,1,0:T(8,128)(2,1)S(1)}, u32[]{:S(2)}, u32[]{:S(2)}) %collective-permute-start.2) | collective-permute-done | bytes 524320 | tf_op jit(solution)/shard_map/ppermute | solution.py:64
  45.3 11.7 %collective-permute-done.3.rest_0_ = bf16[2,128,1024]{2,1,0:T(8,128)(2,1)S(1)} collective-permute-done((bf16[2,128,1024]{2,1,0:T(8,128)(2,1)S(1)}, bf16[2,128,1024]{2,1,0:T(8,128)(2,1)S(1)}, u32[]{:S(2)}, u32[]{:S(2)}) %collective-permute-start.3) | collective-permute-done | bytes 524320 | tf_op jit(solution)/shard_map/ppermute | solution.py:64
  57.0 1.6 collective-permute-start.8
  58.6 22.3 %collective-permute-start.9 = (bf16[2,128,1024]{2,1,0:T(8,128)(2,1)S(1)}, bf16[2,128,1024]{2,1,0:T(8,128)(2,1)S(1)}, u32[]{:S(2)}, u32[]{:S(2)}) collective-permute-start(bf16[2,128,1024]{2,1,0:T(8,128)(2,1)S(1)} %get-tuple-element.46), channel_id=1, source_target_pairs={{0,14},{2,12},{4,10},{6,8},{8,22},{10,20},{12,18},{14,16},{16,30},... | collective-permute-start | bytes 1572872 | tf_op jit(solution)/shard_map/ppermute | solution.py:64
  80.8 43.3 %collective-permute-done.5.rest_2_ = bf16[2,128,1024]{2,1,0:T(8,128)(2,1)S(1)} collective-permute-done((bf16[2,128,1024]{2,1,0:T(8,128)(2,1)S(1)}, bf16[2,128,1024]{2,1,0:T(8,128)(2,1)S(1)}, u32[]{:S(2)}, u32[]{:S(2)}) %collective-permute-start.5) | collective-permute-done | bytes 524320 | tf_op jit(solution)/shard_map/ppermute | solution.py:64
  124.2 1.1 collective-permute-start.10
  125.3 10.0 %collective-permute-done.6.rest_0_ = bf16[2,128,1024]{2,1,0:T(8,128)(2,1)S(1)} collective-permute-done((bf16[2,128,1024]{2,1,0:T(8,128)(2,1)S(1)}, bf16[2,128,1024]{2,1,0:T(8,128)(2,1)S(1)}, u32[]{:S(2)}, u32[]{:S(2)}) %collective-permute-start.6) | collective-permute-done | bytes 524320 | tf_op jit(solution)/shard_map/ppermute | solution.py:64
  135.3 0.6 collective-permute-start.11
  135.9 2.8 %collective-permute-start.13 = (bf16[2,128,1024]{2,1,0:T(8,128)(2,1)S(1)}, bf16[2,128,1024]{2,1,0:T(8,128)(2,1)S(1)}, u32[]{:S(2)}, u32[]{:S(2)}) collective-permute-start(bf16[2,128,1024]{2,1,0:T(8,128)(2,1)S(1)} %get-tuple-element.52), channel_id=1, source_target_pairs={{0,22},{2,20},{4,18},{6,16},{8,30},{10,28},{12,26},{14,24},{16,6},... | collective-permute-start | bytes 1572872 | tf_op jit(solution)/shard_map/ppermute | solution.py:64
  138.6 2.6 %collective-permute-start.14 = (bf16[2,128,1024]{2,1,0:T(8,128)(2,1)S(1)}, bf16[2,128,1024]{2,1,0:T(8,128)(2,1)S(1)}, u32[]{:S(2)}, u32[]{:S(2)}) collective-permute-start(bf16[2,128,1024]{2,1,0:T(8,128)(2,1)S(1)} %get-tuple-element.53), channel_id=1, source_target_pairs={{0,30},{2,28},{4,26},{6,24},{8,6},{10,4},{12,2},{14,0},{16,14},{18... | collective-permute-start | bytes 1572872 | tf_op jit(solution)/shard_map/ppermute | solution.py:64
  141.3 3.1 %settle_pages.5 = (bf16[32,128,1024]{2,1,0:T(8,128)(2,1)}, f32[16,32,128]{2,1,0:T(8,128)S(1)}) custom-call(s32[256]{0:T(256)S(1)} %or_or_fusion.table_hbm.table, s32[256]{0:T(256)S(1)} %copy-done.1, bf16[16,32,128]{2,1,0:T(8,128)(2,1)S(1)} %bitcast.2, f32[16,32,128]{2,1,0:T(8,128)S(1)} %broadcast_in_dim.3.rows_in, ...), custom_call_target="tpu_custom_call", output_to_operand_aliasing={{0}: (4, {})} | custom-call | flops 1073741824 | bytes 3145728 | tf_op jit(solution)/shard_map/settle_pages/pallas_call | solution.py:280
  144.4 2.2 settle_pages.6
  146.6 3.5 %settle_pages.7 = (bf16[32,128,1024]{2,1,0:T(8,128)(2,1)}, f32[16,32,128]{2,1,0:T(8,128)S(1)}) custom-call(s32[256]{0:T(256)S(1)} %or_or_fusion.table_hbm.table, s32[256]{0:T(256)S(1)} %copy-done.1, bf16[16,32,128]{2,1,0:T(8,128)(2,1)S(1)} %bitcast.4, f32[16,32,128]{2,1,0:T(8,128)S(1)} %get-tuple-element.39.rows_in, ...), custom_call_target="tpu_custom_call", output_to_operand_aliasing={{0}: (4, {})} | custom-call | flops 1073741824 | bytes 3145728 | tf_op jit(solution)/shard_map/settle_pages/pallas_call | solution.py:280
  150.2 3.8 %collective-permute-done.11.rest_2_ = bf16[2,128,1024]{2,1,0:T(8,128)(2,1)S(1)} collective-permute-done((bf16[2,128,1024]{2,1,0:T(8,128)(2,1)S(1)}, bf16[2,128,1024]{2,1,0:T(8,128)(2,1)S(1)}, u32[]{:S(2)}, u32[]{:S(2)}) %collective-permute-start.11) | collective-permute-done | bytes 524320 | tf_op jit(solution)/shard_map/ppermute | solution.py:64
  154.0 2.2 settle_pages.8
  156.2 9.0 %collective-permute-done.12.rest_0_ = bf16[2,128,1024]{2,1,0:T(8,128)(2,1)S(1)} collective-permute-done((bf16[2,128,1024]{2,1,0:T(8,128)(2,1)S(1)}, bf16[2,128,1024]{2,1,0:T(8,128)(2,1)S(1)}, u32[]{:S(2)}, u32[]{:S(2)}) %collective-permute-start.12) | collective-permute-done | bytes 524320 | tf_op jit(solution)/shard_map/ppermute | solution.py:64
  165.2 18.7 %collective-permute-done.13.rest_1_ = bf16[2,128,1024]{2,1,0:T(8,128)(2,1)S(1)} collective-permute-done((bf16[2,128,1024]{2,1,0:T(8,128)(2,1)S(1)}, bf16[2,128,1024]{2,1,0:T(8,128)(2,1)S(1)}, u32[]{:S(2)}, u32[]{:S(2)}) %collective-permute-start.13) | collective-permute-done | bytes 524320 | tf_op jit(solution)/shard_map/ppermute | solution.py:64
  183.9 6.5 %collective-permute-done.14.rest_2_ = bf16[2,128,1024]{2,1,0:T(8,128)(2,1)S(1)} collective-permute-done((bf16[2,128,1024]{2,1,0:T(8,128)(2,1)S(1)}, bf16[2,128,1024]{2,1,0:T(8,128)(2,1)S(1)}, u32[]{:S(2)}, u32[]{:S(2)}) %collective-permute-start.14) | collective-permute-done | bytes 524320 | tf_op jit(solution)/shard_map/ppermute | solution.py:64
  190.4 2.4 %settle_pages.9 = (bf16[32,128,1024]{2,1,0:T(8,128)(2,1)}, bf16[16,4096]{1,0:T(8,128)(2,1)S(1)}) custom-call(s32[256]{0:T(256)S(1)} %or_or_fusion.table_hbm.table, s32[256]{0:T(256)S(1)} %copy-done.1, bf16[16,32,128]{2,1,0:T(8,128)(2,1)S(1)} %bitcast.6, f32[16,32,128]{2,1,0:T(8,128)S(1)} %get-tuple-element.49.rows_in, ...), custom_call_target="tpu_custom_call", output_to_operand_aliasing={{0}: (4, {})} | custom-call | flops 1073741824 | bytes 3145728 | tf_op jit(solution)/shard_map/settle_pages/pallas_call | solution.py:280
  192.9 5.2 %collective-permute-start.15 = (bf16[16,4096]{1,0:T(8,128)(2,1)S(1)}, bf16[16,4096]{1,0:T(8,128)(2,1)S(1)}, u32[]{:S(2)}, u32[]{:S(2)}) collective-permute-start(bf16[16,4096]{1,0:T(8,128)(2,1)S(1)} %get-tuple-element.55.rest_0_), channel_id=1, source_target_pairs={{0,16},{2,18},{4,20},{6,22},{8,24},{10,26},{12,28},{14,30},{16,0},... | collective-permute-start | bytes 393224 | tf_op jit(solution)/shard_map/ppermute | solution.py:69
  198.1 1.8 collective-permute-start.18
  199.9 2.0 collective-permute-start.16
  201.9 0.3 collective-permute-start.22
  202.3 4.0 %collective-permute-start.17 = (bf16[16,4096]{1,0:T(8,128)(2,1)S(1)}, bf16[16,4096]{1,0:T(8,128)(2,1)S(1)}, u32[]{:S(2)}, u32[]{:S(2)}) collective-permute-start(bf16[16,4096]{1,0:T(8,128)(2,1)S(1)} %collective-permute-done.15.rest_1_), channel_id=1, source_target_pairs={{0,8},{2,10},{4,12},{6,14},{8,0},{10,2},{12,4},{14,6},{16,24},{18,... | collective-permute-start | bytes 393224 | tf_op jit(solution)/shard_map/ppermute | solution.py:69
  206.3 0.5 collective-permute-start.24
  206.8 0.7 collective-permute-start.20
  207.5 1.3 collective-permute-start.19
  208.8 0.4 collective-permute-done.17.rest_3_
  209.2 1.3 collective-permute-start.21
  210.6 0.5 collective-permute-start.25
  211.1 2.1 collective-permute-done.20.rest_6_
  213.2 2.8 %collective-permute-done.19.rest_5_ = bf16[16,4096]{1,0:T(8,128)(2,1)S(1)} collective-permute-done((bf16[16,4096]{1,0:T(8,128)(2,1)S(1)}, bf16[16,4096]{1,0:T(8,128)(2,1)S(1)}, u32[]{:S(2)}, u32[]{:S(2)}) %collective-permute-start.19) | collective-permute-done | bytes 131104 | tf_op jit(solution)/shard_map/ppermute | solution.py:69
  216.0 1.9 collective-permute-done.21.rest_7_
  217.9 2.1 project_some_rows.1.some
  220.1 2.5 %project_rows.1 = (f32[128,512]{1,0:T(8,128)S(1)}, bf16[128,512]{1,0:T(8,128)(2,1)S(1)}) custom-call(bf16[4096,512]{1,0:T(8,128)(2,1)S(1)} %copy-done, f32[128,512]{1,0:T(8,128)S(1)} %project_some_rows.1.some, bf16[16,4096]{1,0:T(8,128)(2,1)S(1)} %collective-permute-done.22.rest_0_, bf16[16,4096]{1,0:T(8,128)(2,1)S(1)} %collective-permute-done.23.rest_1_, ...), custom_call_target="tpu_custom_call" | custom-call | flops 536870912 | bytes 4194304 | tf_op jit(solution)/shard_map/project_rows/pallas_call | solution.py:354
  222.6 1.6 collective-permute-start.30
  224.1 4.4 %collective-permute-done.30 = bf16[128,512]{1,0:T(8,128)(2,1)S(1)} collective-permute-done((bf16[128,512]{1,0:T(8,128)(2,1)S(1)}, bf16[128,512]{1,0:T(8,128)(2,1)S(1)}, u32[]{:S(2)}, u32[]{:S(2)}) %collective-permute-start.30) | collective-permute-done | bytes 131104 | tf_op jit(solution)/shard_map/ppermute | solution.py:409
  228.5 0.7 add_convert_fusion
  (33 shorter events, 0.3 us)
Async XLA Ops:
  1.3 139.9 %copy-start.2 = (bf16[16,4096]{1,0:T(8,128)(2,1)S(1)}, bf16[16,4096]{1,0:T(8,128)(2,1)}, u32[]{:S(2)}) copy-start(bf16[16,4096]{1,0:T(8,128)(2,1)} %param.12) | copy-start | bytes 393220
  1.3 139.9 %copy-start.1 = (s32[256]{0:T(256)S(1)}, s32[256]{0:T(256)}, u32[]{:S(2)}) copy-start(s32[256]{0:T(256)} %row_request.9) | copy-start | bytes 3076
  5.4 15.7 %collective-permute-start.1 = (bf16[2,128,1024]{2,1,0:T(8,128)(2,1)S(1)}, bf16[2,128,1024]{2,1,0:T(8,128)(2,1)S(1)}, u32[]{:S(2)}, u32[]{:S(2)}) collective-permute-start(bf16[2,128,1024]{2,1,0:T(8,128)(2,1)S(1)} %get-tuple-element.32), channel_id=1, source_target_pairs={{0,18},{2,16},{4,22},{6,20},{8,2},{10,0},{12,6},{14,4},{16,26},{18... | collective-permute-start | bytes 1572872 | tf_op jit(solution)/shard_map/ppermute | solution.py:64
  8.8 23.5 %collective-permute-start = (bf16[2,128,1024]{2,1,0:T(8,128)(2,1)S(1)}, bf16[2,128,1024]{2,1,0:T(8,128)(2,1)S(1)}, u32[]{:S(2)}, u32[]{:S(2)}) collective-permute-start(bf16[2,128,1024]{2,1,0:T(8,128)(2,1)S(1)} %get-tuple-element.30.rest_0_), channel_id=1, source_target_pairs={{0,16},{2,18},{4,20},{6,22},{8,0},{10,2},{12,4},{14,6},{16,24},{18... | collective-permute-start | bytes 1572872 | tf_op jit(solution)/shard_map/ppermute | solution.py:64
  17.2 28.1 %collective-permute-start.2 = (bf16[2,128,1024]{2,1,0:T(8,128)(2,1)S(1)}, bf16[2,128,1024]{2,1,0:T(8,128)(2,1)S(1)}, u32[]{:S(2)}, u32[]{:S(2)}) collective-permute-start(bf16[2,128,1024]{2,1,0:T(8,128)(2,1)S(1)} %get-tuple-element.33), channel_id=1, source_target_pairs={{0,26},{2,24},{4,30},{6,28},{8,10},{10,8},{12,14},{14,12},{16,18},... | collective-permute-start | bytes 1572872 | tf_op jit(solution)/shard_map/ppermute | solution.py:64
  17.3 39.6 %collective-permute-start.3 = (bf16[2,128,1024]{2,1,0:T(8,128)(2,1)S(1)}, bf16[2,128,1024]{2,1,0:T(8,128)(2,1)S(1)}, u32[]{:S(2)}, u32[]{:S(2)}) collective-permute-start(bf16[2,128,1024]{2,1,0:T(8,128)(2,1)S(1)} %get-tuple-element.36), channel_id=1, source_target_pairs={{0,24},{2,26},{4,28},{6,30},{8,16},{10,18},{12,20},{14,22},{16,8},... | collective-permute-start | bytes 1572872 | tf_op jit(solution)/shard_map/ppermute | solution.py:64
  20.9 37.7 %collective-permute-start.4 = (bf16[2,128,1024]{2,1,0:T(8,128)(2,1)S(1)}, bf16[2,128,1024]{2,1,0:T(8,128)(2,1)S(1)}, u32[]{:S(2)}, u32[]{:S(2)}) collective-permute-start(bf16[2,128,1024]{2,1,0:T(8,128)(2,1)S(1)} %get-tuple-element.37), channel_id=1, source_target_pairs={{0,2},{2,0},{4,6},{6,4},{8,18},{10,16},{12,22},{14,20},{16,10},{18... | collective-permute-start | bytes 1572872 | tf_op jit(solution)/shard_map/ppermute | solution.py:64
  21.1 103.1 %collective-permute-start.5 = (bf16[2,128,1024]{2,1,0:T(8,128)(2,1)S(1)}, bf16[2,128,1024]{2,1,0:T(8,128)(2,1)S(1)}, u32[]{:S(2)}, u32[]{:S(2)}) collective-permute-start(bf16[2,128,1024]{2,1,0:T(8,128)(2,1)S(1)} %get-tuple-element.38), channel_id=1, source_target_pairs={{0,8},{2,10},{4,12},{6,14},{8,24},{10,26},{12,28},{14,30},{16,0},{... | collective-permute-start | bytes 1572872 | tf_op jit(solution)/shard_map/ppermute | solution.py:64
  32.3 102.9 %collective-permute-start.6 = (bf16[2,128,1024]{2,1,0:T(8,128)(2,1)S(1)}, bf16[2,128,1024]{2,1,0:T(8,128)(2,1)S(1)}, u32[]{:S(2)}, u32[]{:S(2)}) collective-permute-start(bf16[2,128,1024]{2,1,0:T(8,128)(2,1)S(1)} %get-tuple-element.41), channel_id=1, source_target_pairs={{0,10},{2,8},{4,14},{6,12},{8,26},{10,24},{12,30},{14,28},{16,2},{... | collective-permute-start | bytes 1572872 | tf_op jit(solution)/shard_map/ppermute | solution.py:64
  45.3 90.5 %collective-permute-start.7 = (bf16[2,128,1024]{2,1,0:T(8,128)(2,1)S(1)}, bf16[2,128,1024]{2,1,0:T(8,128)(2,1)S(1)}, u32[]{:S(2)}, u32[]{:S(2)}) collective-permute-start(bf16[2,128,1024]{2,1,0:T(8,128)(2,1)S(1)} %get-tuple-element.42), channel_id=1, source_target_pairs={{0,12},{2,14},{4,8},{6,10},{8,20},{10,22},{12,16},{14,18},{16,28},... | collective-permute-start | bytes 1572872 | tf_op jit(solution)/shard_map/ppermute | solution.py:64
  57.0 78.9 %collective-permute-start.8 = (bf16[2,128,1024]{2,1,0:T(8,128)(2,1)S(1)}, bf16[2,128,1024]{2,1,0:T(8,128)(2,1)S(1)}, u32[]{:S(2)}, u32[]{:S(2)}) collective-permute-start(bf16[2,128,1024]{2,1,0:T(8,128)(2,1)S(1)} %get-tuple-element.43), channel_id=1, source_target_pairs={{0,4},{2,6},{4,0},{6,2},{8,12},{10,14},{12,8},{14,10},{16,20},{18,... | collective-permute-start | bytes 1572872 | tf_op jit(solution)/shard_map/ppermute | solution.py:64
  58.6 80.0 %collective-permute-start.9 = (bf16[2,128,1024]{2,1,0:T(8,128)(2,1)S(1)}, bf16[2,128,1024]{2,1,0:T(8,128)(2,1)S(1)}, u32[]{:S(2)}, u32[]{:S(2)}) collective-permute-start(bf16[2,128,1024]{2,1,0:T(8,128)(2,1)S(1)} %get-tuple-element.46), channel_id=1, source_target_pairs={{0,14},{2,12},{4,10},{6,8},{8,22},{10,20},{12,18},{14,16},{16,30},... | collective-permute-start | bytes 1572872 | tf_op jit(solution)/shard_map/ppermute | solution.py:64
  124.2 26.0 %collective-permute-start.10 = (bf16[2,128,1024]{2,1,0:T(8,128)(2,1)S(1)}, bf16[2,128,1024]{2,1,0:T(8,128)(2,1)S(1)}, u32[]{:S(2)}, u32[]{:S(2)}) collective-permute-start(bf16[2,128,1024]{2,1,0:T(8,128)(2,1)S(1)} %get-tuple-element.47), channel_id=1, source_target_pairs={{0,6},{2,4},{4,2},{6,0},{8,14},{10,12},{12,10},{14,8},{16,22},{18,... | collective-permute-start | bytes 1572872 | tf_op jit(solution)/shard_map/ppermute | solution.py:64
  135.3 18.7 %collective-permute-start.11 = (bf16[2,128,1024]{2,1,0:T(8,128)(2,1)S(1)}, bf16[2,128,1024]{2,1,0:T(8,128)(2,1)S(1)}, u32[]{:S(2)}, u32[]{:S(2)}) collective-permute-start(bf16[2,128,1024]{2,1,0:T(8,128)(2,1)S(1)} %get-tuple-element.48), channel_id=1, source_target_pairs={{0,20},{2,22},{4,16},{6,18},{8,28},{10,30},{12,24},{14,26},{16,4},... | collective-permute-start | bytes 1572872 | tf_op jit(solution)/shard_map/ppermute | solution.py:64
  135.9 29.4 %collective-permute-start.12 = (bf16[2,128,1024]{2,1,0:T(8,128)(2,1)S(1)}, bf16[2,128,1024]{2,1,0:T(8,128)(2,1)S(1)}, u32[]{:S(2)}, u32[]{:S(2)}) collective-permute-start(bf16[2,128,1024]{2,1,0:T(8,128)(2,1)S(1)} %get-tuple-element.51), channel_id=1, source_target_pairs={{0,28},{2,30},{4,24},{6,26},{8,4},{10,6},{12,0},{14,2},{16,12},{18... | collective-permute-start | bytes 1572872 | tf_op jit(solution)/shard_map/ppermute | solution.py:64
  135.9 48.1 %collective-permute-start.13 = (bf16[2,128,1024]{2,1,0:T(8,128)(2,1)S(1)}, bf16[2,128,1024]{2,1,0:T(8,128)(2,1)S(1)}, u32[]{:S(2)}, u32[]{:S(2)}) collective-permute-start(bf16[2,128,1024]{2,1,0:T(8,128)(2,1)S(1)} %get-tuple-element.52), channel_id=1, source_target_pairs={{0,22},{2,20},{4,18},{6,16},{8,30},{10,28},{12,26},{14,24},{16,6},... | collective-permute-start | bytes 1572872 | tf_op jit(solution)/shard_map/ppermute | solution.py:64
  138.6 51.8 %collective-permute-start.14 = (bf16[2,128,1024]{2,1,0:T(8,128)(2,1)S(1)}, bf16[2,128,1024]{2,1,0:T(8,128)(2,1)S(1)}, u32[]{:S(2)}, u32[]{:S(2)}) collective-permute-start(bf16[2,128,1024]{2,1,0:T(8,128)(2,1)S(1)} %get-tuple-element.53), channel_id=1, source_target_pairs={{0,30},{2,28},{4,26},{6,24},{8,6},{10,4},{12,2},{14,0},{16,14},{18... | collective-permute-start | bytes 1572872 | tf_op jit(solution)/shard_map/ppermute | solution.py:64
  154.0 63.9 %copy-start = (bf16[4096,512]{1,0:T(8,128)(2,1)S(1)}, bf16[4096,512]{1,0:T(8,128)(2,1)}, u32[]{:S(2)}) copy-start(bf16[4096,512]{1,0:T(8,128)(2,1)} %out_weight.3) | copy-start | bytes 12582916
  192.9 9.4 %collective-permute-start.15 = (bf16[16,4096]{1,0:T(8,128)(2,1)S(1)}, bf16[16,4096]{1,0:T(8,128)(2,1)S(1)}, u32[]{:S(2)}, u32[]{:S(2)}) collective-permute-start(bf16[16,4096]{1,0:T(8,128)(2,1)S(1)} %get-tuple-element.55.rest_0_), channel_id=1, source_target_pairs={{0,16},{2,18},{4,20},{6,22},{8,24},{10,26},{12,28},{14,30},{16,0},... | collective-permute-start | bytes 393224 | tf_op jit(solution)/shard_map/ppermute | solution.py:69
  198.1 8.2 %collective-permute-start.18 = (bf16[16,4096]{1,0:T(8,128)(2,1)S(1)}, bf16[16,4096]{1,0:T(8,128)(2,1)S(1)}, u32[]{:S(2)}, u32[]{:S(2)}) collective-permute-start(bf16[16,4096]{1,0:T(8,128)(2,1)S(1)} %get-tuple-element.55.rest_0_), channel_id=1, source_target_pairs={{0,4},{2,6},{4,0},{6,2},{8,12},{10,14},{12,8},{14,10},{16,20},{18,... | collective-permute-start | bytes 393224 | tf_op jit(solution)/shard_map/ppermute | solution.py:69
  199.9 6.4 %collective-permute-start.16 = (bf16[16,4096]{1,0:T(8,128)(2,1)S(1)}, bf16[16,4096]{1,0:T(8,128)(2,1)S(1)}, u32[]{:S(2)}, u32[]{:S(2)}) collective-permute-start(bf16[16,4096]{1,0:T(8,128)(2,1)S(1)} %get-tuple-element.55.rest_0_), channel_id=1, source_target_pairs={{0,8},{2,10},{4,12},{6,14},{8,0},{10,2},{12,4},{14,6},{16,24},{18,... | collective-permute-start | bytes 393224 | tf_op jit(solution)/shard_map/ppermute | solution.py:69
  201.9 5.6 %collective-permute-start.22 = (bf16[16,4096]{1,0:T(8,128)(2,1)S(1)}, bf16[16,4096]{1,0:T(8,128)(2,1)S(1)}, u32[]{:S(2)}, u32[]{:S(2)}) collective-permute-start(bf16[16,4096]{1,0:T(8,128)(2,1)S(1)} %get-tuple-element.55.rest_0_), channel_id=1, source_target_pairs={{0,2},{2,0},{4,6},{6,4},{8,10},{10,8},{12,14},{14,12},{16,18},{18,... | collective-permute-start | bytes 393224 | tf_op jit(solution)/shard_map/ppermute | solution.py:69
  202.3 7.0 %collective-permute-start.17 = (bf16[16,4096]{1,0:T(8,128)(2,1)S(1)}, bf16[16,4096]{1,0:T(8,128)(2,1)S(1)}, u32[]{:S(2)}, u32[]{:S(2)}) collective-permute-start(bf16[16,4096]{1,0:T(8,128)(2,1)S(1)} %collective-permute-done.15.rest_1_), channel_id=1, source_target_pairs={{0,8},{2,10},{4,12},{6,14},{8,0},{10,2},{12,4},{14,6},{16,24},{18,... | collective-permute-start | bytes 393224 | tf_op jit(solution)/shard_map/ppermute | solution.py:69
  206.3 4.3 %collective-permute-start.26 = (bf16[16,4096]{1,0:T(8,128)(2,1)S(1)}, bf16[16,4096]{1,0:T(8,128)(2,1)S(1)}, u32[]{:S(2)}, u32[]{:S(2)}) collective-permute-start(bf16[16,4096]{1,0:T(8,128)(2,1)S(1)} %collective-permute-done.18.rest_4_), channel_id=1, source_target_pairs={{0,2},{2,0},{4,6},{6,4},{8,10},{10,8},{12,14},{14,12},{16,18},{18,... | collective-permute-start | bytes 393224 | tf_op jit(solution)/shard_map/ppermute | solution.py:69
  206.3 4.2 %collective-permute-start.24 = (bf16[16,4096]{1,0:T(8,128)(2,1)S(1)}, bf16[16,4096]{1,0:T(8,128)(2,1)S(1)}, u32[]{:S(2)}, u32[]{:S(2)}) collective-permute-start(bf16[16,4096]{1,0:T(8,128)(2,1)S(1)} %collective-permute-done.16.rest_2_), channel_id=1, source_target_pairs={{0,2},{2,0},{4,6},{6,4},{8,10},{10,8},{12,14},{14,12},{16,18},{18,... | collective-permute-start | bytes 393224 | tf_op jit(solution)/shard_map/ppermute | solution.py:69
  206.8 6.4 %collective-permute-start.20 = (bf16[16,4096]{1,0:T(8,128)(2,1)S(1)}, bf16[16,4096]{1,0:T(8,128)(2,1)S(1)}, u32[]{:S(2)}, u32[]{:S(2)}) collective-permute-start(bf16[16,4096]{1,0:T(8,128)(2,1)S(1)} %collective-permute-done.16.rest_2_), channel_id=1, source_target_pairs={{0,4},{2,6},{4,0},{6,2},{8,12},{10,14},{12,8},{14,10},{16,20},{18,... | collective-permute-start | bytes 393224 | tf_op jit(solution)/shard_map/ppermute | solution.py:69
  207.5 8.4 %collective-permute-start.19 = (bf16[16,4096]{1,0:T(8,128)(2,1)S(1)}, bf16[16,4096]{1,0:T(8,128)(2,1)S(1)}, u32[]{:S(2)}, u32[]{:S(2)}) collective-permute-start(bf16[16,4096]{1,0:T(8,128)(2,1)S(1)} %collective-permute-done.15.rest_1_), channel_id=1, source_target_pairs={{0,4},{2,6},{4,0},{6,2},{8,12},{10,14},{12,8},{14,10},{16,20},{18,... | collective-permute-start | bytes 393224 | tf_op jit(solution)/shard_map/ppermute | solution.py:69
  209.2 8.7 %collective-permute-start.21 = (bf16[16,4096]{1,0:T(8,128)(2,1)S(1)}, bf16[16,4096]{1,0:T(8,128)(2,1)S(1)}, u32[]{:S(2)}, u32[]{:S(2)}) collective-permute-start(bf16[16,4096]{1,0:T(8,128)(2,1)S(1)} %collective-permute-done.17.rest_3_), channel_id=1, source_target_pairs={{0,4},{2,6},{4,0},{6,2},{8,12},{10,14},{12,8},{14,10},{16,20},{18,... | collective-permute-start | bytes 393224 | tf_op jit(solution)/shard_map/ppermute | solution.py:69
  210.5 9.5 %collective-permute-start.23 = (bf16[16,4096]{1,0:T(8,128)(2,1)S(1)}, bf16[16,4096]{1,0:T(8,128)(2,1)S(1)}, u32[]{:S(2)}, u32[]{:S(2)}) collective-permute-start(bf16[16,4096]{1,0:T(8,128)(2,1)S(1)} %collective-permute-done.15.rest_1_), channel_id=1, source_target_pairs={{0,2},{2,0},{4,6},{6,4},{8,10},{10,8},{12,14},{14,12},{16,18},{18,... | collective-permute-start | bytes 393224 | tf_op jit(solution)/shard_map/ppermute | solution.py:69
  210.6 9.5 %collective-permute-start.25 = (bf16[16,4096]{1,0:T(8,128)(2,1)S(1)}, bf16[16,4096]{1,0:T(8,128)(2,1)S(1)}, u32[]{:S(2)}, u32[]{:S(2)}) collective-permute-start(bf16[16,4096]{1,0:T(8,128)(2,1)S(1)} %collective-permute-done.17.rest_3_), channel_id=1, source_target_pairs={{0,2},{2,0},{4,6},{6,4},{8,10},{10,8},{12,14},{14,12},{16,18},{18,... | collective-permute-start | bytes 393224 | tf_op jit(solution)/shard_map/ppermute | solution.py:69
  213.2 6.9 %collective-permute-start.28 = (bf16[16,4096]{1,0:T(8,128)(2,1)S(1)}, bf16[16,4096]{1,0:T(8,128)(2,1)S(1)}, u32[]{:S(2)}, u32[]{:S(2)}) collective-permute-start(bf16[16,4096]{1,0:T(8,128)(2,1)S(1)} %collective-permute-done.20.rest_6_), channel_id=1, source_target_pairs={{0,2},{2,0},{4,6},{6,4},{8,10},{10,8},{12,14},{14,12},{16,18},{18,... | collective-permute-start | bytes 393224 | tf_op jit(solution)/shard_map/ppermute | solution.py:69
  216.0 4.1 %collective-permute-start.27 = (bf16[16,4096]{1,0:T(8,128)(2,1)S(1)}, bf16[16,4096]{1,0:T(8,128)(2,1)S(1)}, u32[]{:S(2)}, u32[]{:S(2)}) collective-permute-start(bf16[16,4096]{1,0:T(8,128)(2,1)S(1)} %collective-permute-done.19.rest_5_), channel_id=1, source_target_pairs={{0,2},{2,0},{4,6},{6,4},{8,10},{10,8},{12,14},{14,12},{16,18},{18,... | collective-permute-start | bytes 393224 | tf_op jit(solution)/shard_map/ppermute | solution.py:69
  217.9 2.2 collective-permute-start.29
  222.6 6.0 %collective-permute-start.30 = (bf16[128,512]{1,0:T(8,128)(2,1)S(1)}, bf16[128,512]{1,0:T(8,128)(2,1)S(1)}, u32[]{:S(2)}, u32[]{:S(2)}) collective-permute-start(bf16[128,512]{1,0:T(8,128)(2,1)S(1)} %get-tuple-element.57), channel_id=1, source_target_pairs={{0,1},{1,0},{2,3},{3,2},{4,5},{5,4},{6,7},{7,6},{8,9},{9,8},{10,11... | collective-permute-start | bytes 393224 | tf_op jit(solution)/shard_map/ppermute | solution.py:409

commit v18 on v13

--- a/solution.py
+++ b/solution.py
@@ -32,7 +32,7 @@
     for low in range(0, near, half):
         swaps = range(low, min(low + half, near))
         opening = [(1, n) for n in swaps] if low == 0 else [(z, n) for n in swaps for z in (1, 0)]
-        rest = [(z, n) for n in swaps for z in range(2, far)]
+        rest = [(z, n) for n in swaps for z in range(far - 1, 1, -1)]
         order += opening + ([(0, n) for n in swaps if n] if low == 0 else []) + rest
     return [uniform(z, n, dims) for z, n in order]
 
@@ -86,7 +86,7 @@
 
 
 def prepare_kernel(dims, routes, own, table_hbm, pool, *rest):
-    table, held, zero_page, start_of, count_of, table_sem, in_sems, out_sem = rest[-8:]
+    table, held, zero_page, start_of, count_of, table_sem, in_sems, out_sems = rest[-8:]
     received = rest[-8 - len(routes) - own : -8 - len(routes)]
     sends = rest[-8 - len(routes) : -8]
     me = lax.axis_index("group")
@@ -120,7 +120,8 @@
                 there = page < count_of[to]
                 source = pool.at[jnp.where(there, start_of[to] + page, 0)]
                 buffer, place = held.at[i, page], target.at[base + page]
-                do(there, (source, buffer, in_sems.at[i, page]), (buffer, place, out_sem), (zero_page, place, out_sem))
+                sem = out_sems.at[i, page]
+                do(there, (source, buffer, in_sems.at[i, page]), (buffer, place, sem), (zero_page, place, sem))
 
     def fetch(there, load, store, blank):
         @pl.when(there)
@@ -166,7 +167,7 @@
             pltpu.SMEM((groups + 1,), jnp.int32),
             pltpu.SemaphoreType.DMA,
             pltpu.SemaphoreType.DMA((blocks, MAX_PAGES)),
-            pltpu.SemaphoreType.DMA,
+            pltpu.SemaphoreType.DMA((blocks, MAX_PAGES)),
         ],
         compiler_params=pltpu.CompilerParams(vmem_limit_bytes=VMEM_LIMIT),
         cost_estimate=pl.CostEstimate(

time: 226 us -> 229 us (1.013)
  waiting for transfers between devices: 108 us -> 114 us
    ppermute x15, starting transfers between devices: 22.8 us -> 9.32 us  [swap(): return lax.ppermute(array, 'group', [(s, s ^ mask) for s in range(groups)])]
    ppermute x15, starting transfers between devices: 61.5 us -> 72.5 us  [send_by(): return lax.ppermute(array, 'group', pairs)]
    ppermute x15, waiting for transfers between devices: 7.51 us -> 12.7 us  [swap(): return lax.ppermute(array, 'group', [(s, s ^ mask) for s in range(groups)])]
  transfers between devices with their start and end apart: 31 -> 31, of which waited for: 11 -> 14; matrix products, arithmetic and copies ran while one was open for 0% -> 0% of each run, Pallas kernels for 9% -> 9%
where the time goes in v18:
time: 229 us; the launch traced here: 228 us
  waiting for transfers between devices  114 us (50%)
  starting transfers between devices  83.8 us (37%)
  Pallas kernels  28.4 us (12%)
    ppermute x15, waiting for transfers between devices, send_by(): return lax.ppermute(array, 'group', pairs)  96.9 us
    ppermute x15, starting transfers between devices, send_by(): return lax.ppermute(array, 'group', pairs)  72.5 us
    pallas_call x5, Pallas kernels, settle(): pl.pallas_call(functools.partial(settle_kernel, dims, routes, own, last),...  13.4 us
    ppermute x15, waiting for transfers between devices, swap(): return lax.ppermute(array, 'group', [(s, s ^ mask) for s in range(groups)])  12.7 us
    pallas_call x2, Pallas kernels, prepare(): pl.pallas_call(functools.partial(prepare_kernel, dims, routes, own), out_...  10.4 us
    ppermute x15, starting transfers between devices, swap(): return lax.ppermute(array, 'group', [(s, s ^ mask) for s in range(groups)])  9.32 us
    pallas_call x2, Pallas kernels, call(): pl.pallas_call(kernel, out_shape=outs, in_specs=[vmem] * (1 + len(extra))...  4.6 us
  transfers between devices with their start and end apart: 31, of which 14 were waited for; matrix products, arithmetic and copies ran while one was open for 0% of the time, Pallas kernels for 9%

profile of v18, /device:TPU:0, one launch (start us, length us, event | category | flops | bytes accessed | tf_op | source)
XLA Modules:
  0.0 228.2 jit_solution(3006291554602563520)
XLA Ops:
  0.6 0.7 or_or_fusion.table_hbm.table
  1.4 3.9 %outgoing_pages.2 = (bf16[2,128,1024]{2,1,0:T(8,128)(2,1)S(1)}, bf16[2,128,1024]{2,1,0:T(8,128)(2,1)S(1)}) custom-call(s32[256]{0:T(256)S(1)} %or_or_fusion.table_hbm.table, bf16[32,128,1024]{2,1,0:T(8,128)(2,1)} %pool.3), custom_call_target="tpu_custom_call" | custom-call | bytes 2097152 | tf_op jit(solution)/shard_map/outgoing_pages/pallas_call | solution.py:157
  5.3 2.6 %collective-permute-start.1 = (bf16[2,128,1024]{2,1,0:T(8,128)(2,1)S(1)}, bf16[2,128,1024]{2,1,0:T(8,128)(2,1)S(1)}, u32[]{:S(2)}, u32[]{:S(2)}) collective-permute-start(bf16[2,128,1024]{2,1,0:T(8,128)(2,1)S(1)} %get-tuple-element.32), channel_id=1, source_target_pairs={{0,10},{2,8},{4,14},{6,12},{8,18},{10,16},{12,22},{14,20},{16,26},... | collective-permute-start | bytes 1572872 | tf_op jit(solution)/shard_map/ppermute | solution.py:60
  7.9 1.6 collective-permute-start
  9.5 6.4 %outgoing_pages.3 = (bf16[32,128,1024]{2,1,0:T(8,128)(2,1)}, bf16[2,128,1024]{2,1,0:T(8,128)(2,1)S(1)}, bf16[2,128,1024]{2,1,0:T(8,128)(2,1)S(1)}, bf16[2,128,10...) custom-call(s32[256]{0:T(256)S(1)} %or_or_fusion.table_hbm.table, ...), custom_call_target="tpu_custom_call" | custom-call | bytes 14680064 | tf_op jit(solution)/shard_map/outgoing_pages/pallas_call | solution.py:157
  15.9 0.8 collective-permute-start.2
  16.7 2.3 %collective-permute-start.3 = (bf16[2,128,1024]{2,1,0:T(8,128)(2,1)S(1)}, bf16[2,128,1024]{2,1,0:T(8,128)(2,1)S(1)}, u32[]{:S(2)}, u32[]{:S(2)}) collective-permute-start(bf16[2,128,1024]{2,1,0:T(8,128)(2,1)S(1)} %get-tuple-element.36), channel_id=1, source_target_pairs={{0,24},{2,26},{4,28},{6,30},{8,0},{10,2},{12,4},{14,6},{16,8},{18,... | collective-permute-start | bytes 1572872 | tf_op jit(solution)/shard_map/ppermute | solution.py:60
  19.0 0.9 collective-permute-start.4
  19.9 1.8 collective-permute-done.1.rest_1_
  21.6 2.7 %collective-permute-start.5 = (bf16[2,128,1024]{2,1,0:T(8,128)(2,1)S(1)}, bf16[2,128,1024]{2,1,0:T(8,128)(2,1)S(1)}, u32[]{:S(2)}, u32[]{:S(2)}) collective-permute-start(bf16[2,128,1024]{2,1,0:T(8,128)(2,1)S(1)} %get-tuple-element.38), channel_id=1, source_target_pairs={{0,26},{2,24},{4,30},{6,28},{8,2},{10,0},{12,6},{14,4},{16,10},{18... | collective-permute-start | bytes 1572872 | tf_op jit(solution)/shard_map/ppermute | solution.py:60
  24.4 10.2 %collective-permute-done.rest_0_ = bf16[2,128,1024]{2,1,0:T(8,128)(2,1)S(1)} collective-permute-done((bf16[2,128,1024]{2,1,0:T(8,128)(2,1)S(1)}, bf16[2,128,1024]{2,1,0:T(8,128)(2,1)S(1)}, u32[]{:S(2)}, u32[]{:S(2)}) %collective-permute-start) | collective-permute-done | bytes 524320 | tf_op jit(solution)/shard_map/ppermute | solution.py:60
  34.6 39.3 %collective-permute-start.6 = (bf16[2,128,1024]{2,1,0:T(8,128)(2,1)S(1)}, bf16[2,128,1024]{2,1,0:T(8,128)(2,1)S(1)}, u32[]{:S(2)}, u32[]{:S(2)}) collective-permute-start(bf16[2,128,1024]{2,1,0:T(8,128)(2,1)S(1)} %get-tuple-element.41), channel_id=1, source_target_pairs={{0,18},{2,16},{4,22},{6,20},{8,26},{10,24},{12,30},{14,28},{16,2},... | collective-permute-start | bytes 1572872 | tf_op jit(solution)/shard_map/ppermute | solution.py:60
  73.9 0.0 collective-permute-done.2.rest_2_
  73.9 1.5 collective-permute-start.8
  75.4 14.5 %collective-permute-start.9 = (bf16[2,128,1024]{2,1,0:T(8,128)(2,1)S(1)}, bf16[2,128,1024]{2,1,0:T(8,128)(2,1)S(1)}, u32[]{:S(2)}, u32[]{:S(2)}) collective-permute-start(bf16[2,128,1024]{2,1,0:T(8,128)(2,1)S(1)} %get-tuple-element.46), channel_id=1, source_target_pairs={{0,14},{2,12},{4,10},{6,8},{8,22},{10,20},{12,18},{14,16},{16,30},... | collective-permute-start | bytes 1572872 | tf_op jit(solution)/shard_map/ppermute | solution.py:60
  90.0 0.4 collective-permute-start.10
  90.4 33.1 %collective-permute-done.6.rest_0_ = bf16[2,128,1024]{2,1,0:T(8,128)(2,1)S(1)} collective-permute-done((bf16[2,128,1024]{2,1,0:T(8,128)(2,1)S(1)}, bf16[2,128,1024]{2,1,0:T(8,128)(2,1)S(1)}, u32[]{:S(2)}, u32[]{:S(2)}) %collective-permute-start.6) | collective-permute-done | bytes 524320 | tf_op jit(solution)/shard_map/ppermute | solution.py:60
  123.4 1.1 collective-permute-start.12
  124.5 4.8 %collective-permute-start.13 = (bf16[2,128,1024]{2,1,0:T(8,128)(2,1)S(1)}, bf16[2,128,1024]{2,1,0:T(8,128)(2,1)S(1)}, u32[]{:S(2)}, u32[]{:S(2)}) collective-permute-start(bf16[2,128,1024]{2,1,0:T(8,128)(2,1)S(1)} %get-tuple-element.52), channel_id=1, source_target_pairs={{0,30},{2,28},{4,26},{6,24},{8,6},{10,4},{12,2},{14,0},{16,14},{18... | collective-permute-start | bytes 1572872 | tf_op jit(solution)/shard_map/ppermute | solution.py:60
  129.4 3.1 %settle_pages.5 = (bf16[32,128,1024]{2,1,0:T(8,128)(2,1)}, f32[16,32,128]{2,1,0:T(8,128)S(1)}) custom-call(s32[256]{0:T(256)S(1)} %or_or_fusion.table_hbm.table, s32[256]{0:T(256)S(1)} %copy-done.1, bf16[16,32,128]{2,1,0:T(8,128)(2,1)S(1)} %bitcast.2, f32[16,32,128]{2,1,0:T(8,128)S(1)} %broadcast_in_dim.3.rows_in, ...), custom_call_target="tpu_custom_call", output_to_operand_aliasing={{0}: (4, {})} | custom-call | flops 1073741824 | bytes 3145728 | tf_op jit(solution)/shard_map/settle_pages/pallas_call | solution.py:276
  132.5 2.2 settle_pages.6
  134.7 3.5 %settle_pages.7 = (bf16[32,128,1024]{2,1,0:T(8,128)(2,1)}, f32[16,32,128]{2,1,0:T(8,128)S(1)}) custom-call(s32[256]{0:T(256)S(1)} %or_or_fusion.table_hbm.table, s32[256]{0:T(256)S(1)} %copy-done.1, bf16[16,32,128]{2,1,0:T(8,128)(2,1)S(1)} %bitcast.4, f32[16,32,128]{2,1,0:T(8,128)S(1)} %get-tuple-element.39.rows_in, ...), custom_call_target="tpu_custom_call", output_to_operand_aliasing={{0}: (4, {})} | custom-call | flops 1073741824 | bytes 3145728 | tf_op jit(solution)/shard_map/settle_pages/pallas_call | solution.py:276
  138.3 1.6 collective-permute-done.11.rest_2_
  139.8 2.2 settle_pages.8
  142.0 17.8 %collective-permute-done.12.rest_0_ = bf16[2,128,1024]{2,1,0:T(8,128)(2,1)S(1)} collective-permute-done((bf16[2,128,1024]{2,1,0:T(8,128)(2,1)S(1)}, bf16[2,128,1024]{2,1,0:T(8,128)(2,1)S(1)}, u32[]{:S(2)}, u32[]{:S(2)}) %collective-permute-start.12) | collective-permute-done | bytes 524320 | tf_op jit(solution)/shard_map/ppermute | solution.py:60
  159.8 0.1 collective-permute-done.13.rest_1_
  159.9 32.4 %collective-permute-done.14.rest_2_ = bf16[2,128,1024]{2,1,0:T(8,128)(2,1)S(1)} collective-permute-done((bf16[2,128,1024]{2,1,0:T(8,128)(2,1)S(1)}, bf16[2,128,1024]{2,1,0:T(8,128)(2,1)S(1)}, u32[]{:S(2)}, u32[]{:S(2)}) %collective-permute-start.14) | collective-permute-done | bytes 524320 | tf_op jit(solution)/shard_map/ppermute | solution.py:60
  192.3 2.4 %settle_pages.9 = (bf16[32,128,1024]{2,1,0:T(8,128)(2,1)}, bf16[16,4096]{1,0:T(8,128)(2,1)S(1)}) custom-call(s32[256]{0:T(256)S(1)} %or_or_fusion.table_hbm.table, s32[256]{0:T(256)S(1)} %copy-done.1, bf16[16,32,128]{2,1,0:T(8,128)(2,1)S(1)} %bitcast.6, f32[16,32,128]{2,1,0:T(8,128)S(1)} %get-tuple-element.49.rows_in, ...), custom_call_target="tpu_custom_call", output_to_operand_aliasing={{0}: (4, {})} | custom-call | flops 1073741824 | bytes 3145728 | tf_op jit(solution)/shard_map/settle_pages/pallas_call | solution.py:276
  194.7 0.1 collective-permute-start.15
  194.8 0.7 collective-permute-start.18
  195.5 4.6 %collective-permute-start.16 = (bf16[16,4096]{1,0:T(8,128)(2,1)S(1)}, bf16[16,4096]{1,0:T(8,128)(2,1)S(1)}, u32[]{:S(2)}, u32[]{:S(2)}) collective-permute-start(bf16[16,4096]{1,0:T(8,128)(2,1)S(1)} %get-tuple-element.55.rest_0_), channel_id=1, source_target_pairs={{0,8},{2,10},{4,12},{6,14},{8,0},{10,2},{12,4},{14,6},{16,24},{18,... | collective-permute-start | bytes 393224 | tf_op jit(solution)/shard_map/ppermute | solution.py:65
  200.1 0.6 collective-permute-start.22
  200.6 3.8 %collective-permute-done.15.rest_1_ = bf16[16,4096]{1,0:T(8,128)(2,1)S(1)} collective-permute-done((bf16[16,4096]{1,0:T(8,128)(2,1)S(1)}, bf16[16,4096]{1,0:T(8,128)(2,1)S(1)}, u32[]{:S(2)}, u32[]{:S(2)}) %collective-permute-start.15) | collective-permute-done | bytes 131104 | tf_op jit(solution)/shard_map/ppermute | solution.py:65
  204.5 0.8 collective-permute-done.16.rest_2_
  205.2 0.1 collective-permute-start.24
  205.4 0.7 collective-permute-start.20
  206.1 1.4 collective-permute-start.19
  207.4 2.0 collective-permute-done.17.rest_3_
  209.4 0.7 collective-permute-start.21
  210.1 0.5 collective-permute-start.25
  210.7 1.1 collective-permute-done.20.rest_6_
  211.7 2.8 %collective-permute-done.19.rest_5_ = bf16[16,4096]{1,0:T(8,128)(2,1)S(1)} collective-permute-done((bf16[16,4096]{1,0:T(8,128)(2,1)S(1)}, bf16[16,4096]{1,0:T(8,128)(2,1)S(1)}, u32[]{:S(2)}, u32[]{:S(2)}) %collective-permute-start.19) | collective-permute-done | bytes 131104 | tf_op jit(solution)/shard_map/ppermute | solution.py:65
  214.5 2.3 collective-permute-done.21.rest_7_
  216.8 2.1 project_some_rows.1.some
  219.0 2.5 %project_rows.1 = (f32[128,512]{1,0:T(8,128)S(1)}, bf16[128,512]{1,0:T(8,128)(2,1)S(1)}) custom-call(bf16[4096,512]{1,0:T(8,128)(2,1)S(1)} %copy-done, f32[128,512]{1,0:T(8,128)S(1)} %project_some_rows.1.some, bf16[16,4096]{1,0:T(8,128)(2,1)S(1)} %collective-permute-done.22.rest_0_, bf16[16,4096]{1,0:T(8,128)(2,1)S(1)} %collective-permute-done.23.rest_1_, ...), custom_call_target="tpu_custom_call" | custom-call | flops 536870912 | bytes 4194304 | tf_op jit(solution)/shard_map/project_rows/pallas_call | solution.py:350
  221.5 2.0 collective-permute-start.30
  223.4 4.1 %collective-permute-done.30 = bf16[128,512]{1,0:T(8,128)(2,1)S(1)} collective-permute-done((bf16[128,512]{1,0:T(8,128)(2,1)S(1)}, bf16[128,512]{1,0:T(8,128)(2,1)S(1)}, u32[]{:S(2)}, u32[]{:S(2)}) %collective-permute-start.30) | collective-permute-done | bytes 131104 | tf_op jit(solution)/shard_map/ppermute | solution.py:405
  227.6 0.7 add_convert_fusion
  (33 shorter events, 0.1 us)
Async XLA Ops:
  1.3 128.0 %copy-start.2 = (bf16[16,4096]{1,0:T(8,128)(2,1)S(1)}, bf16[16,4096]{1,0:T(8,128)(2,1)}, u32[]{:S(2)}) copy-start(bf16[16,4096]{1,0:T(8,128)(2,1)} %param.12) | copy-start | bytes 393220
  1.3 128.0 %copy-start.1 = (s32[256]{0:T(256)S(1)}, s32[256]{0:T(256)}, u32[]{:S(2)}) copy-start(s32[256]{0:T(256)} %row_request.9) | copy-start | bytes 3076
  5.3 16.3 %collective-permute-start.1 = (bf16[2,128,1024]{2,1,0:T(8,128)(2,1)S(1)}, bf16[2,128,1024]{2,1,0:T(8,128)(2,1)S(1)}, u32[]{:S(2)}, u32[]{:S(2)}) collective-permute-start(bf16[2,128,1024]{2,1,0:T(8,128)(2,1)S(1)} %get-tuple-element.32), channel_id=1, source_target_pairs={{0,10},{2,8},{4,14},{6,12},{8,18},{10,16},{12,22},{14,20},{16,26},... | collective-permute-start | bytes 1572872 | tf_op jit(solution)/shard_map/ppermute | solution.py:60
  7.9 26.7 %collective-permute-start = (bf16[2,128,1024]{2,1,0:T(8,128)(2,1)S(1)}, bf16[2,128,1024]{2,1,0:T(8,128)(2,1)S(1)}, u32[]{:S(2)}, u32[]{:S(2)}) collective-permute-start(bf16[2,128,1024]{2,1,0:T(8,128)(2,1)S(1)} %get-tuple-element.30.rest_0_), channel_id=1, source_target_pairs={{0,8},{2,10},{4,12},{6,14},{8,16},{10,18},{12,20},{14,22},{16,24},... | collective-permute-start | bytes 1572872 | tf_op jit(solution)/shard_map/ppermute | solution.py:60
  15.9 58.0 %collective-permute-start.2 = (bf16[2,128,1024]{2,1,0:T(8,128)(2,1)S(1)}, bf16[2,128,1024]{2,1,0:T(8,128)(2,1)S(1)}, u32[]{:S(2)}, u32[]{:S(2)}) collective-permute-start(bf16[2,128,1024]{2,1,0:T(8,128)(2,1)S(1)} %get-tuple-element.33), channel_id=1, source_target_pairs={{0,2},{2,0},{4,6},{6,4},{8,10},{10,8},{12,14},{14,12},{16,18},{18,... | collective-permute-start | bytes 1572872 | tf_op jit(solution)/shard_map/ppermute | solution.py:60
  16.7 57.2 %collective-permute-start.3 = (bf16[2,128,1024]{2,1,0:T(8,128)(2,1)S(1)}, bf16[2,128,1024]{2,1,0:T(8,128)(2,1)S(1)}, u32[]{:S(2)}, u32[]{:S(2)}) collective-permute-start(bf16[2,128,1024]{2,1,0:T(8,128)(2,1)S(1)} %get-tuple-element.36), channel_id=1, source_target_pairs={{0,24},{2,26},{4,28},{6,30},{8,0},{10,2},{12,4},{14,6},{16,8},{18,... | collective-permute-start | bytes 1572872 | tf_op jit(solution)/shard_map/ppermute | solution.py:60
  19.0 56.5 %collective-permute-start.4 = (bf16[2,128,1024]{2,1,0:T(8,128)(2,1)S(1)}, bf16[2,128,1024]{2,1,0:T(8,128)(2,1)S(1)}, u32[]{:S(2)}, u32[]{:S(2)}) collective-permute-start(bf16[2,128,1024]{2,1,0:T(8,128)(2,1)S(1)} %get-tuple-element.37), channel_id=1, source_target_pairs={{0,16},{2,18},{4,20},{6,22},{8,24},{10,26},{12,28},{14,30},{16,0},... | collective-permute-start | bytes 1572872 | tf_op jit(solution)/shard_map/ppermute | solution.py:60
  21.6 68.3 %collective-permute-start.5 = (bf16[2,128,1024]{2,1,0:T(8,128)(2,1)S(1)}, bf16[2,128,1024]{2,1,0:T(8,128)(2,1)S(1)}, u32[]{:S(2)}, u32[]{:S(2)}) collective-permute-start(bf16[2,128,1024]{2,1,0:T(8,128)(2,1)S(1)} %get-tuple-element.38), channel_id=1, source_target_pairs={{0,26},{2,24},{4,30},{6,28},{8,2},{10,0},{12,6},{14,4},{16,10},{18... | collective-permute-start | bytes 1572872 | tf_op jit(solution)/shard_map/ppermute | solution.py:60
  34.6 88.8 %collective-permute-start.6 = (bf16[2,128,1024]{2,1,0:T(8,128)(2,1)S(1)}, bf16[2,128,1024]{2,1,0:T(8,128)(2,1)S(1)}, u32[]{:S(2)}, u32[]{:S(2)}) collective-permute-start(bf16[2,128,1024]{2,1,0:T(8,128)(2,1)S(1)} %get-tuple-element.41), channel_id=1, source_target_pairs={{0,18},{2,16},{4,22},{6,20},{8,26},{10,24},{12,30},{14,28},{16,2},... | collective-permute-start | bytes 1572872 | tf_op jit(solution)/shard_map/ppermute | solution.py:60
  73.9 49.5 %collective-permute-start.7 = (bf16[2,128,1024]{2,1,0:T(8,128)(2,1)S(1)}, bf16[2,128,1024]{2,1,0:T(8,128)(2,1)S(1)}, u32[]{:S(2)}, u32[]{:S(2)}) collective-permute-start(bf16[2,128,1024]{2,1,0:T(8,128)(2,1)S(1)} %get-tuple-element.42), channel_id=1, source_target_pairs={{0,12},{2,14},{4,8},{6,10},{8,20},{10,22},{12,16},{14,18},{16,28},... | collective-permute-start | bytes 1572872 | tf_op jit(solution)/shard_map/ppermute | solution.py:60
  73.9 50.6 %collective-permute-start.8 = (bf16[2,128,1024]{2,1,0:T(8,128)(2,1)S(1)}, bf16[2,128,1024]{2,1,0:T(8,128)(2,1)S(1)}, u32[]{:S(2)}, u32[]{:S(2)}) collective-permute-start(bf16[2,128,1024]{2,1,0:T(8,128)(2,1)S(1)} %get-tuple-element.43), channel_id=1, source_target_pairs={{0,4},{2,6},{4,0},{6,2},{8,12},{10,14},{12,8},{14,10},{16,20},{18,... | collective-permute-start | bytes 1572872 | tf_op jit(solution)/shard_map/ppermute | solution.py:60
  75.4 53.9 %collective-permute-start.9 = (bf16[2,128,1024]{2,1,0:T(8,128)(2,1)S(1)}, bf16[2,128,1024]{2,1,0:T(8,128)(2,1)S(1)}, u32[]{:S(2)}, u32[]{:S(2)}) collective-permute-start(bf16[2,128,1024]{2,1,0:T(8,128)(2,1)S(1)} %get-tuple-element.46), channel_id=1, source_target_pairs={{0,14},{2,12},{4,10},{6,8},{8,22},{10,20},{12,18},{14,16},{16,30},... | collective-permute-start | bytes 1572872 | tf_op jit(solution)/shard_map/ppermute | solution.py:60
  90.0 48.3 %collective-permute-start.10 = (bf16[2,128,1024]{2,1,0:T(8,128)(2,1)S(1)}, bf16[2,128,1024]{2,1,0:T(8,128)(2,1)S(1)}, u32[]{:S(2)}, u32[]{:S(2)}) collective-permute-start(bf16[2,128,1024]{2,1,0:T(8,128)(2,1)S(1)} %get-tuple-element.47), channel_id=1, source_target_pairs={{0,6},{2,4},{4,2},{6,0},{8,14},{10,12},{12,10},{14,8},{16,22},{18,... | collective-permute-start | bytes 1572872 | tf_op jit(solution)/shard_map/ppermute | solution.py:60
  123.4 16.4 %collective-permute-start.11 = (bf16[2,128,1024]{2,1,0:T(8,128)(2,1)S(1)}, bf16[2,128,1024]{2,1,0:T(8,128)(2,1)S(1)}, u32[]{:S(2)}, u32[]{:S(2)}) collective-permute-start(bf16[2,128,1024]{2,1,0:T(8,128)(2,1)S(1)} %get-tuple-element.48), channel_id=1, source_target_pairs={{0,28},{2,30},{4,24},{6,26},{8,4},{10,6},{12,0},{14,2},{16,12},{18... | collective-permute-start | bytes 1572872 | tf_op jit(solution)/shard_map/ppermute | solution.py:60
  123.4 36.4 %collective-permute-start.12 = (bf16[2,128,1024]{2,1,0:T(8,128)(2,1)S(1)}, bf16[2,128,1024]{2,1,0:T(8,128)(2,1)S(1)}, u32[]{:S(2)}, u32[]{:S(2)}) collective-permute-start(bf16[2,128,1024]{2,1,0:T(8,128)(2,1)S(1)} %get-tuple-element.51), channel_id=1, source_target_pairs={{0,20},{2,22},{4,16},{6,18},{8,28},{10,30},{12,24},{14,26},{16,4},... | collective-permute-start | bytes 1572872 | tf_op jit(solution)/shard_map/ppermute | solution.py:60
  124.5 35.4 %collective-permute-start.13 = (bf16[2,128,1024]{2,1,0:T(8,128)(2,1)S(1)}, bf16[2,128,1024]{2,1,0:T(8,128)(2,1)S(1)}, u32[]{:S(2)}, u32[]{:S(2)}) collective-permute-start(bf16[2,128,1024]{2,1,0:T(8,128)(2,1)S(1)} %get-tuple-element.52), channel_id=1, source_target_pairs={{0,30},{2,28},{4,26},{6,24},{8,6},{10,4},{12,2},{14,0},{16,14},{18... | collective-permute-start | bytes 1572872 | tf_op jit(solution)/shard_map/ppermute | solution.py:60
  129.3 62.9 %collective-permute-start.14 = (bf16[2,128,1024]{2,1,0:T(8,128)(2,1)S(1)}, bf16[2,128,1024]{2,1,0:T(8,128)(2,1)S(1)}, u32[]{:S(2)}, u32[]{:S(2)}) collective-permute-start(bf16[2,128,1024]{2,1,0:T(8,128)(2,1)S(1)} %get-tuple-element.53), channel_id=1, source_target_pairs={{0,22},{2,20},{4,18},{6,16},{8,30},{10,28},{12,26},{14,24},{16,6},... | collective-permute-start | bytes 1572872 | tf_op jit(solution)/shard_map/ppermute | solution.py:60
  139.8 77.0 %copy-start = (bf16[4096,512]{1,0:T(8,128)(2,1)S(1)}, bf16[4096,512]{1,0:T(8,128)(2,1)}, u32[]{:S(2)}) copy-start(bf16[4096,512]{1,0:T(8,128)(2,1)} %out_weight.3) | copy-start | bytes 12582916
  194.7 9.7 %collective-permute-start.15 = (bf16[16,4096]{1,0:T(8,128)(2,1)S(1)}, bf16[16,4096]{1,0:T(8,128)(2,1)S(1)}, u32[]{:S(2)}, u32[]{:S(2)}) collective-permute-start(bf16[16,4096]{1,0:T(8,128)(2,1)S(1)} %get-tuple-element.55.rest_0_), channel_id=1, source_target_pairs={{0,16},{2,18},{4,20},{6,22},{8,24},{10,26},{12,28},{14,30},{16,0},... | collective-permute-start | bytes 393224 | tf_op jit(solution)/shard_map/ppermute | solution.py:65
  194.8 9.6 %collective-permute-start.18 = (bf16[16,4096]{1,0:T(8,128)(2,1)S(1)}, bf16[16,4096]{1,0:T(8,128)(2,1)S(1)}, u32[]{:S(2)}, u32[]{:S(2)}) collective-permute-start(bf16[16,4096]{1,0:T(8,128)(2,1)S(1)} %get-tuple-element.55.rest_0_), channel_id=1, source_target_pairs={{0,4},{2,6},{4,0},{6,2},{8,12},{10,14},{12,8},{14,10},{16,20},{18,... | collective-permute-start | bytes 393224 | tf_op jit(solution)/shard_map/ppermute | solution.py:65
  195.5 9.7 %collective-permute-start.16 = (bf16[16,4096]{1,0:T(8,128)(2,1)S(1)}, bf16[16,4096]{1,0:T(8,128)(2,1)S(1)}, u32[]{:S(2)}, u32[]{:S(2)}) collective-permute-start(bf16[16,4096]{1,0:T(8,128)(2,1)S(1)} %get-tuple-element.55.rest_0_), channel_id=1, source_target_pairs={{0,8},{2,10},{4,12},{6,14},{8,0},{10,2},{12,4},{14,6},{16,24},{18,... | collective-permute-start | bytes 393224 | tf_op jit(solution)/shard_map/ppermute | solution.py:65
  200.1 6.0 %collective-permute-start.22 = (bf16[16,4096]{1,0:T(8,128)(2,1)S(1)}, bf16[16,4096]{1,0:T(8,128)(2,1)S(1)}, u32[]{:S(2)}, u32[]{:S(2)}) collective-permute-start(bf16[16,4096]{1,0:T(8,128)(2,1)S(1)} %get-tuple-element.55.rest_0_), channel_id=1, source_target_pairs={{0,2},{2,0},{4,6},{6,4},{8,10},{10,8},{12,14},{14,12},{16,18},{18,... | collective-permute-start | bytes 393224 | tf_op jit(solution)/shard_map/ppermute | solution.py:65
  204.5 5.0 %collective-permute-start.17 = (bf16[16,4096]{1,0:T(8,128)(2,1)S(1)}, bf16[16,4096]{1,0:T(8,128)(2,1)S(1)}, u32[]{:S(2)}, u32[]{:S(2)}) collective-permute-start(bf16[16,4096]{1,0:T(8,128)(2,1)S(1)} %collective-permute-done.15.rest_1_), channel_id=1, source_target_pairs={{0,8},{2,10},{4,12},{6,14},{8,0},{10,2},{12,4},{14,6},{16,24},{18,... | collective-permute-start | bytes 393224 | tf_op jit(solution)/shard_map/ppermute | solution.py:65
  204.5 5.7 %collective-permute-start.26 = (bf16[16,4096]{1,0:T(8,128)(2,1)S(1)}, bf16[16,4096]{1,0:T(8,128)(2,1)S(1)}, u32[]{:S(2)}, u32[]{:S(2)}) collective-permute-start(bf16[16,4096]{1,0:T(8,128)(2,1)S(1)} %collective-permute-done.18.rest_4_), channel_id=1, source_target_pairs={{0,2},{2,0},{4,6},{6,4},{8,10},{10,8},{12,14},{14,12},{16,18},{18,... | collective-permute-start | bytes 393224 | tf_op jit(solution)/shard_map/ppermute | solution.py:65
  205.2 4.9 %collective-permute-start.24 = (bf16[16,4096]{1,0:T(8,128)(2,1)S(1)}, bf16[16,4096]{1,0:T(8,128)(2,1)S(1)}, u32[]{:S(2)}, u32[]{:S(2)}) collective-permute-start(bf16[16,4096]{1,0:T(8,128)(2,1)S(1)} %collective-permute-done.16.rest_2_), channel_id=1, source_target_pairs={{0,2},{2,0},{4,6},{6,4},{8,10},{10,8},{12,14},{14,12},{16,18},{18,... | collective-permute-start | bytes 393224 | tf_op jit(solution)/shard_map/ppermute | solution.py:65
  205.4 6.3 %collective-permute-start.20 = (bf16[16,4096]{1,0:T(8,128)(2,1)S(1)}, bf16[16,4096]{1,0:T(8,128)(2,1)S(1)}, u32[]{:S(2)}, u32[]{:S(2)}) collective-permute-start(bf16[16,4096]{1,0:T(8,128)(2,1)S(1)} %collective-permute-done.16.rest_2_), channel_id=1, source_target_pairs={{0,4},{2,6},{4,0},{6,2},{8,12},{10,14},{12,8},{14,10},{16,20},{18,... | collective-permute-start | bytes 393224 | tf_op jit(solution)/shard_map/ppermute | solution.py:65
  206.1 8.4 %collective-permute-start.19 = (bf16[16,4096]{1,0:T(8,128)(2,1)S(1)}, bf16[16,4096]{1,0:T(8,128)(2,1)S(1)}, u32[]{:S(2)}, u32[]{:S(2)}) collective-permute-start(bf16[16,4096]{1,0:T(8,128)(2,1)S(1)} %collective-permute-done.15.rest_1_), channel_id=1, source_target_pairs={{0,4},{2,6},{4,0},{6,2},{8,12},{10,14},{12,8},{14,10},{16,20},{18,... | collective-permute-start | bytes 393224 | tf_op jit(solution)/shard_map/ppermute | solution.py:65
  209.4 7.4 %collective-permute-start.21 = (bf16[16,4096]{1,0:T(8,128)(2,1)S(1)}, bf16[16,4096]{1,0:T(8,128)(2,1)S(1)}, u32[]{:S(2)}, u32[]{:S(2)}) collective-permute-start(bf16[16,4096]{1,0:T(8,128)(2,1)S(1)} %collective-permute-done.17.rest_3_), channel_id=1, source_target_pairs={{0,4},{2,6},{4,0},{6,2},{8,12},{10,14},{12,8},{14,10},{16,20},{18,... | collective-permute-start | bytes 393224 | tf_op jit(solution)/shard_map/ppermute | solution.py:65
  210.1 8.8 %collective-permute-start.23 = (bf16[16,4096]{1,0:T(8,128)(2,1)S(1)}, bf16[16,4096]{1,0:T(8,128)(2,1)S(1)}, u32[]{:S(2)}, u32[]{:S(2)}) collective-permute-start(bf16[16,4096]{1,0:T(8,128)(2,1)S(1)} %collective-permute-done.15.rest_1_), channel_id=1, source_target_pairs={{0,2},{2,0},{4,6},{6,4},{8,10},{10,8},{12,14},{14,12},{16,18},{18,... | collective-permute-start | bytes 393224 | tf_op jit(solution)/shard_map/ppermute | solution.py:65
  210.1 8.8 %collective-permute-start.25 = (bf16[16,4096]{1,0:T(8,128)(2,1)S(1)}, bf16[16,4096]{1,0:T(8,128)(2,1)S(1)}, u32[]{:S(2)}, u32[]{:S(2)}) collective-permute-start(bf16[16,4096]{1,0:T(8,128)(2,1)S(1)} %collective-permute-done.17.rest_3_), channel_id=1, source_target_pairs={{0,2},{2,0},{4,6},{6,4},{8,10},{10,8},{12,14},{14,12},{16,18},{18,... | collective-permute-start | bytes 393224 | tf_op jit(solution)/shard_map/ppermute | solution.py:65
  211.7 7.2 %collective-permute-start.28 = (bf16[16,4096]{1,0:T(8,128)(2,1)S(1)}, bf16[16,4096]{1,0:T(8,128)(2,1)S(1)}, u32[]{:S(2)}, u32[]{:S(2)}) collective-permute-start(bf16[16,4096]{1,0:T(8,128)(2,1)S(1)} %collective-permute-done.20.rest_6_), channel_id=1, source_target_pairs={{0,2},{2,0},{4,6},{6,4},{8,10},{10,8},{12,14},{14,12},{16,18},{18,... | collective-permute-start | bytes 393224 | tf_op jit(solution)/shard_map/ppermute | solution.py:65
  214.5 4.4 %collective-permute-start.27 = (bf16[16,4096]{1,0:T(8,128)(2,1)S(1)}, bf16[16,4096]{1,0:T(8,128)(2,1)S(1)}, u32[]{:S(2)}, u32[]{:S(2)}) collective-permute-start(bf16[16,4096]{1,0:T(8,128)(2,1)S(1)} %collective-permute-done.19.rest_5_), channel_id=1, source_target_pairs={{0,2},{2,0},{4,6},{6,4},{8,10},{10,8},{12,14},{14,12},{16,18},{18,... | collective-permute-start | bytes 393224 | tf_op jit(solution)/shard_map/ppermute | solution.py:65
  216.8 2.2 collective-permute-start.29
  221.5 6.1 %collective-permute-start.30 = (bf16[128,512]{1,0:T(8,128)(2,1)S(1)}, bf16[128,512]{1,0:T(8,128)(2,1)S(1)}, u32[]{:S(2)}, u32[]{:S(2)}) collective-permute-start(bf16[128,512]{1,0:T(8,128)(2,1)S(1)} %get-tuple-element.57), channel_id=1, source_target_pairs={{0,1},{1,0},{2,3},{3,2},{4,5},{5,4},{6,7},{7,6},{8,9},{9,8},{10,11... | collective-permute-start | bytes 393224 | tf_op jit(solution)/shard_map/ppermute | solution.py:405

commit v19 on v18

--- a/solution.py
+++ b/solution.py
@@ -12,7 +12,7 @@
 MAX_PAGES = 2
 WAVE = 3
 ROW_UNROLL = 4
-EARLY = 2
+EARLY = 1
 VMEM_LIMIT = 20 * 1024 * 1024
 
 
@@ -25,16 +25,16 @@
     return tuple(((z + step) % dims[0], swap) for z in range(dims[0]))
 
 
-def page_rounds(dims):
+def page_sendings(dims):
     far, near = dims
     half = max(near // 2, 1)
-    order = []
+    steps, sendings = range(1, far), []
     for low in range(0, near, half):
-        swaps = range(low, min(low + half, near))
-        opening = [(1, n) for n in swaps] if low == 0 else [(z, n) for n in swaps for z in (1, 0)]
-        rest = [(z, n) for n in swaps for z in range(far - 1, 1, -1)]
-        order += opening + ([(0, n) for n in swaps if n] if low == 0 else []) + rest
-    return [uniform(z, n, dims) for z, n in order]
+        here = [[(0, n)] for n in range(low, min(low + half, near)) if n]
+        pairs = [[(z, n) for n in range(low, min(low + half, near))] for z in steps]
+        sendings += pairs[:1] + here + pairs[1:]
+    sendings[-1:] = [[round_] for round_ in sendings[-1]]
+    return [[uniform(z, n, dims) for z, n in several] for several in sendings]
 
 
 def reverse(route):
@@ -85,10 +85,10 @@
     return entry >> 2 * bits, (entry >> bits) & mask, entry & mask
 
 
-def prepare_kernel(dims, routes, own, table_hbm, pool, *rest):
+def prepare_kernel(dims, sendings, own, table_hbm, pool, *rest):
     table, held, zero_page, start_of, count_of, table_sem, in_sems, out_sems = rest[-8:]
-    received = rest[-8 - len(routes) - own : -8 - len(routes)]
-    sends = rest[-8 - len(routes) : -8]
+    received = rest[-8 - len(sendings) - own : -8 - len(sendings)]
+    sends = rest[-8 - len(sendings) : -8]
     me = lax.axis_index("group")
     groups = lax.axis_size("group")
     page_size = pool.shape[1]
@@ -110,7 +110,11 @@
         return running + jnp.where(mine, count, 0)
 
     lax.fori_loop(0, table.shape[0], visit, jnp.int32(0), unroll=8)
-    targets = [(routed(me, route, dims), send, 0) for route, send in zip(routes, sends)]
+    targets = [
+        (routed(me, route, dims), send, i * MAX_PAGES)
+        for several, send in zip(sendings, sends)
+        for i, route in enumerate(several)
+    ]
     if own:
         targets.append((me, received[0], me * MAX_PAGES))
 
@@ -146,16 +150,16 @@
     each(finish)
 
 
-def prepare(dims, routes, table, pool, own, after=()):
-    groups = lax.axis_size("group")
+def prepare(dims, sendings, table, pool, own, after=()):
+    groups = math.prod(dims)
     page = pool.shape[1:]
-    blocks = len(routes) + (1 if own else 0)
+    blocks = sum(len(several) for several in sendings) + (1 if own else 0)
     hbm = pl.BlockSpec(memory_space=pl.ANY)
-    block = jax.ShapeDtypeStruct((MAX_PAGES,) + page, pool.dtype)
-    outs = [jax.ShapeDtypeStruct((groups * MAX_PAGES,) + page, pool.dtype)] * own + [block] * len(routes)
+    outs = [jax.ShapeDtypeStruct((groups * MAX_PAGES,) + page, pool.dtype)] * own
+    outs += [jax.ShapeDtypeStruct((len(several) * MAX_PAGES,) + page, pool.dtype) for several in sendings]
     operands = [table, pool, *after]
     return pl.pallas_call(
-        functools.partial(prepare_kernel, dims, routes, own),
+        functools.partial(prepare_kernel, dims, sendings, own),
         out_shape=outs,
         in_specs=[hbm] * len(operands),
         out_specs=[hbm] * len(outs),
@@ -385,12 +389,18 @@
     heads = lax.axis_size("head")
 
     dims = factors(lax.axis_size("group"))
-    routes = page_rounds(dims)
+    sendings = page_sendings(dims)
+    routes = [route for several in sendings for route in several]
     table = packed(lengths, prefill_of, decode_of, math.prod(dims))
     kv_pool = pltpu.with_memory_space_constraint(kv_pool, pltpu.HBM)
-    early = prepare(dims, routes[:EARLY], table, kv_pool, False)
-    received, *late = prepare(dims, routes[EARLY:], table, kv_pool, True, early[:1])
-    arrived = [send_by(block, route, dims) for block, route in zip([*early, *late], routes)]
+    early = prepare(dims, sendings[:EARLY], table, kv_pool, False)
+    received, *late = prepare(dims, sendings[EARLY:], table, kv_pool, True, early[:1])
+    arrived = []
+    for carried, several in zip([*early, *late], sendings):
+        landed = send_by(carried, several[0], dims)
+        arrived.append(landed[:MAX_PAGES])
+        if len(several) > 1:
+            arrived.append(swap(landed[MAX_PAGES:], 1))
     rows = jnp.zeros(query_heads.shape, jnp.float32)
     for first in range(0, len(routes), WAVE):
         wave = slice(first, first + WAVE)

time: 229 us -> 253 us (1.10)
  waiting for transfers between devices: 114 us -> 154 us
  starting transfers between devices: 83.8 us -> 68.1 us
    ppermute x15 -> x10, waiting for transfers between devices: 96.9 us -> 134 us  [send_by(): return lax.ppermute(array, 'group', pairs)]
    ppermute x15 -> x10, starting transfers between devices: 72.5 us -> 59.5 us  [send_by(): return lax.ppermute(array, 'group', pairs)]
    ppermute x15 -> x20, waiting for transfers between devices: 12.7 us -> 15.3 us  [swap(): return lax.ppermute(array, 'group', [(s, s ^ mask) for s in range(groups)])]
    ppermute x15 -> x20, starting transfers between devices: 9.32 us -> 7.06 us  [swap(): return lax.ppermute(array, 'group', [(s, s ^ mask) for s in range(groups)])]
  transfers between devices with their start and end apart: 31 -> 31, of which waited for: 14 -> 12; matrix products, arithmetic and copies ran while one was open for 0% -> 0% of each run, Pallas kernels for 9% -> 8%
where the time goes in v19:
time: 253 us
  waiting for transfers between devices  154 us (61%)
  starting transfers between devices  68.1 us (27%)
  Pallas kernels  28.3 us (11%)
    ppermute x10, waiting for transfers between devices, send_by(): return lax.ppermute(array, 'group', pairs)  134 us
    ppermute x10, starting transfers between devices, send_by(): return lax.ppermute(array, 'group', pairs)  59.5 us
    ppermute x20, waiting for transfers between devices, swap(): return lax.ppermute(array, 'group', [(s, s ^ mask) for s in range(groups)])  15.3 us
    pallas_call x5, Pallas kernels, settle(): pl.pallas_call(functools.partial(settle_kernel, dims, routes, own, last),...  13.2 us
    pallas_call x2, Pallas kernels, prepare(): pl.pallas_call(functools.partial(prepare_kernel, dims, sendings, own), ou...  10.5 us
    ppermute x20, starting transfers between devices, swap(): return lax.ppermute(array, 'group', [(s, s ^ mask) for s in range(groups)])  7.06 us
  transfers between devices with their start and end apart: 31, of which 12 were waited for; matrix products, arithmetic and copies ran while one was open for 0% of the time, Pallas kernels for 8%

profile of v19, /device:TPU:0, one launch (start us, length us, event | category | flops | bytes accessed | tf_op | source)
XLA Modules:
  0.0 253.0 jit_solution(13877001524765278344)
XLA Ops:
  0.6 0.7 or_or_fusion.table_hbm.table
  1.3 3.9 %outgoing_pages.2.rest_0_ = bf16[4,128,1024]{2,1,0:T(8,128)(2,1)S(1)} custom-call(s32[256]{0:T(256)S(1)} %or_or_fusion.table_hbm.table, bf16[32,128,1024]{2,1,0:T(8,128)(2,1)} %pool.3), custom_call_target="tpu_custom_call" | custom-call | bytes 2097152 | tf_op jit(solution)/shard_map/outgoing_pages/pallas_call | solution.py:161
  5.3 3.2 %collective-permute-start = (bf16[4,128,1024]{2,1,0:T(8,128)(2,1)S(1)}, bf16[4,128,1024]{2,1,0:T(8,128)(2,1)S(1)}, u32[]{:S(2)}, u32[]{:S(2)}) collective-permute-start(bf16[4,128,1024]{2,1,0:T(8,128)(2,1)S(1)} %outgoing_pages.2.rest_0_), channel_id=1, source_target_pairs={{0,8},{2,10},{4,12},{6,14},{8,16},{10,18},{12,20},{14,22},{16,24},... | collective-permute-start | bytes 3145736 | tf_op jit(solution)/shard_map/ppermute | solution.py:60
  8.5 6.6 %outgoing_pages.3 = (bf16[32,128,1024]{2,1,0:T(8,128)(2,1)}, bf16[2,128,1024]{2,1,0:T(8,128)(2,1)S(1)}, bf16[4,128,1024]{2,1,0:T(8,128)(2,1)S(1)}, bf16[4,128,10...) custom-call(s32[256]{0:T(256)S(1)} %or_or_fusion.table_hbm.table, ...), custom_call_target="tpu_custom_call" | custom-call | bytes 14680064 | tf_op jit(solution)/shard_map/outgoing_pages/pallas_call | solution.py:161
  15.1 2.4 collective-permute-start.3
  17.6 1.6 collective-permute-start.5
  19.1 1.8 collective-permute-start.7
  20.9 13.6 %collective-permute-done = bf16[4,128,1024]{2,1,0:T(8,128)(2,1)S(1)} collective-permute-done((bf16[4,128,1024]{2,1,0:T(8,128)(2,1)S(1)}, bf16[4,128,1024]{2,1,0:T(8,128)(2,1)S(1)}, u32[]{:S(2)}, u32[]{:S(2)}) %collective-permute-start) | collective-permute-done | bytes 1048608 | tf_op jit(solution)/shard_map/ppermute | solution.py:60
  34.5 47.0 %collective-permute-start.11 = (bf16[4,128,1024]{2,1,0:T(8,128)(2,1)S(1)}, bf16[4,128,1024]{2,1,0:T(8,128)(2,1)S(1)}, u32[]{:S(2)}, u32[]{:S(2)}) collective-permute-start(bf16[4,128,1024]{2,1,0:T(8,128)(2,1)S(1)} %get-tuple-element.37), channel_id=1, source_target_pairs={{0,20},{2,22},{4,16},{6,18},{8,28},{10,30},{12,24},{14,26},{16,4},... | collective-permute-start | bytes 3145736 | tf_op jit(solution)/shard_map/ppermute | solution.py:60
  81.5 0.1 fusion.4
  81.6 0.1 collective-permute-start.1
  81.7 0.1 fusion.3
  81.8 0.6 collective-permute-start.4
  82.4 20.9 %collective-permute-done.7 = bf16[4,128,1024]{2,1,0:T(8,128)(2,1)S(1)} collective-permute-done((bf16[4,128,1024]{2,1,0:T(8,128)(2,1)S(1)}, bf16[4,128,1024]{2,1,0:T(8,128)(2,1)S(1)}, u32[]{:S(2)}, u32[]{:S(2)}) %collective-permute-start.7) | collective-permute-done | bytes 1048608 | tf_op jit(solution)/shard_map/ppermute | solution.py:60
  103.4 0.1 fusion.1
  103.4 0.6 collective-permute-start.8
  104.0 65.5 %collective-permute-done.11 = bf16[4,128,1024]{2,1,0:T(8,128)(2,1)S(1)} collective-permute-done((bf16[4,128,1024]{2,1,0:T(8,128)(2,1)S(1)}, bf16[4,128,1024]{2,1,0:T(8,128)(2,1)S(1)}, u32[]{:S(2)}, u32[]{:S(2)}) %collective-permute-start.11) | collective-permute-done | bytes 1048608 | tf_op jit(solution)/shard_map/ppermute | solution.py:60
  169.5 0.5 collective-permute-start.9
  170.0 0.9 collective-permute-start.10
  170.9 0.1 fusion
  170.9 1.8 collective-permute-start.13
  172.8 0.3 collective-permute-start.14
  173.1 0.1 collective-permute-start.12
  173.3 4.4 %settle_pages.5 = (bf16[32,128,1024]{2,1,0:T(8,128)(2,1)}, f32[16,32,128]{2,1,0:T(8,128)S(1)}) custom-call(s32[256]{0:T(256)S(1)} %or_or_fusion.table_hbm.table, s32[256]{0:T(256)S(1)} %copy-done.1, bf16[16,32,128]{2,1,0:T(8,128)(2,1)S(1)} %bitcast.2, f32[16,32,128]{2,1,0:T(8,128)S(1)} %broadcast_in_dim.3.rows_in, ...), custom_call_target="tpu_custom_call", output_to_operand_aliasing={{0}: (4, {})} | custom-call | flops 1073741824 | bytes 3145728 | tf_op jit(solution)/shard_map/settle_pages/pallas_call | solution.py:280
  177.7 2.2 settle_pages.6
  179.9 2.2 settle_pages.7
  182.1 24.7 %collective-permute-done.9.rest_0_ = bf16[2,128,1024]{2,1,0:T(8,128)(2,1)S(1)} collective-permute-done((bf16[2,128,1024]{2,1,0:T(8,128)(2,1)S(1)}, bf16[2,128,1024]{2,1,0:T(8,128)(2,1)S(1)}, u32[]{:S(2)}, u32[]{:S(2)}) %collective-permute-start.9) | collective-permute-done | bytes 524320 | tf_op jit(solution)/shard_map/ppermute | solution.py:60
  206.7 9.4 %collective-permute-done.10.rest_1_ = bf16[2,128,1024]{2,1,0:T(8,128)(2,1)S(1)} collective-permute-done((bf16[2,128,1024]{2,1,0:T(8,128)(2,1)S(1)}, bf16[2,128,1024]{2,1,0:T(8,128)(2,1)S(1)}, u32[]{:S(2)}, u32[]{:S(2)}) %collective-permute-start.10) | collective-permute-done | bytes 524320 | tf_op jit(solution)/shard_map/ppermute | solution.py:60
  216.1 2.0 settle_pages.8
  218.1 2.4 settle_pages.9
  220.6 0.1 collective-permute-start.15
  220.7 1.6 collective-permute-start.18
  222.2 0.3 collective-permute-start.16
  222.5 5.5 %collective-permute-done.15.rest_1_ = bf16[16,4096]{1,0:T(8,128)(2,1)S(1)} collective-permute-done((bf16[16,4096]{1,0:T(8,128)(2,1)S(1)}, bf16[16,4096]{1,0:T(8,128)(2,1)S(1)}, u32[]{:S(2)}, u32[]{:S(2)}) %collective-permute-start.15) | collective-permute-done | bytes 131104 | tf_op jit(solution)/shard_map/ppermute | solution.py:65
  228.1 2.1 collective-permute-done.16.rest_2_
  230.1 1.5 collective-permute-start.20
  231.6 0.5 collective-permute-start.19
  232.1 1.3 collective-permute-done.17.rest_3_
  233.4 1.2 collective-permute-start.21
  234.7 0.5 collective-permute-start.25
  235.2 1.2 collective-permute-done.20.rest_6_
  236.4 2.8 %collective-permute-done.19.rest_5_ = bf16[16,4096]{1,0:T(8,128)(2,1)S(1)} collective-permute-done((bf16[16,4096]{1,0:T(8,128)(2,1)S(1)}, bf16[16,4096]{1,0:T(8,128)(2,1)S(1)}, u32[]{:S(2)}, u32[]{:S(2)}) %collective-permute-start.19) | collective-permute-done | bytes 131104 | tf_op jit(solution)/shard_map/ppermute | solution.py:65
  239.2 2.4 collective-permute-done.21.rest_7_
  241.6 2.1 project_some_rows.1.some
  243.8 2.5 project_rows.1
  246.3 1.6 collective-permute-start.30
  247.9 4.4 %collective-permute-done.30 = bf16[128,512]{1,0:T(8,128)(2,1)S(1)} collective-permute-done((bf16[128,512]{1,0:T(8,128)(2,1)S(1)}, bf16[128,512]{1,0:T(8,128)(2,1)S(1)}, u32[]{:S(2)}, u32[]{:S(2)}) %collective-permute-start.30) | collective-permute-done | bytes 131104 | tf_op jit(solution)/shard_map/ppermute | solution.py:415
  252.3 0.7 add_convert_fusion
  (38 shorter events, 0.2 us)
Async XLA Ops:
  5.3 167.9 %copy-start.2 = (bf16[16,4096]{1,0:T(8,128)(2,1)S(1)}, bf16[16,4096]{1,0:T(8,128)(2,1)}, u32[]{:S(2)}) copy-start(bf16[16,4096]{1,0:T(8,128)(2,1)} %param.12) | copy-start | bytes 393220
  5.3 167.9 %copy-start.1 = (s32[256]{0:T(256)S(1)}, s32[256]{0:T(256)}, u32[]{:S(2)}) copy-start(s32[256]{0:T(256)} %row_request.9) | copy-start | bytes 3076
  5.3 29.2 %collective-permute-start = (bf16[4,128,1024]{2,1,0:T(8,128)(2,1)S(1)}, bf16[4,128,1024]{2,1,0:T(8,128)(2,1)S(1)}, u32[]{:S(2)}, u32[]{:S(2)}) collective-permute-start(bf16[4,128,1024]{2,1,0:T(8,128)(2,1)S(1)} %outgoing_pages.2.rest_0_), channel_id=1, source_target_pairs={{0,8},{2,10},{4,12},{6,14},{8,16},{10,18},{12,20},{14,22},{16,24},... | collective-permute-start | bytes 3145736 | tf_op jit(solution)/shard_map/ppermute | solution.py:60
  15.1 66.5 %collective-permute-start.3 = (bf16[4,128,1024]{2,1,0:T(8,128)(2,1)S(1)}, bf16[4,128,1024]{2,1,0:T(8,128)(2,1)S(1)}, u32[]{:S(2)}, u32[]{:S(2)}) collective-permute-start(bf16[4,128,1024]{2,1,0:T(8,128)(2,1)S(1)} %get-tuple-element.28), channel_id=1, source_target_pairs={{0,16},{2,18},{4,20},{6,22},{8,24},{10,26},{12,28},{14,30},{16,0},... | collective-permute-start | bytes 3145736 | tf_op jit(solution)/shard_map/ppermute | solution.py:60
  17.6 64.2 %collective-permute-start.5 = (bf16[4,128,1024]{2,1,0:T(8,128)(2,1)S(1)}, bf16[4,128,1024]{2,1,0:T(8,128)(2,1)S(1)}, u32[]{:S(2)}, u32[]{:S(2)}) collective-permute-start(bf16[4,128,1024]{2,1,0:T(8,128)(2,1)S(1)} %get-tuple-element.29), channel_id=1, source_target_pairs={{0,24},{2,26},{4,28},{6,30},{8,0},{10,2},{12,4},{14,6},{16,8},{18,... | collective-permute-start | bytes 3145736 | tf_op jit(solution)/shard_map/ppermute | solution.py:60
  19.1 84.2 %collective-permute-start.7 = (bf16[4,128,1024]{2,1,0:T(8,128)(2,1)S(1)}, bf16[4,128,1024]{2,1,0:T(8,128)(2,1)S(1)}, u32[]{:S(2)}, u32[]{:S(2)}) collective-permute-start(bf16[4,128,1024]{2,1,0:T(8,128)(2,1)S(1)} %get-tuple-element.32), channel_id=1, source_target_pairs={{0,12},{2,14},{4,8},{6,10},{8,20},{10,22},{12,16},{14,18},{16,28},... | collective-permute-start | bytes 3145736 | tf_op jit(solution)/shard_map/ppermute | solution.py:60
  20.9 82.5 %collective-permute-start.2 = (bf16[2,128,1024]{2,1,0:T(8,128)(2,1)S(1)}, bf16[2,128,1024]{2,1,0:T(8,128)(2,1)S(1)}, u32[]{:S(2)}, u32[]{:S(2)}) collective-permute-start(bf16[2,128,1024]{2,1,0:T(8,128)(2,1)S(1)} %get-tuple-element.25), channel_id=1, source_target_pairs={{0,2},{2,0},{4,6},{6,4},{8,10},{10,8},{12,14},{14,12},{16,18},{18,... | collective-permute-start | bytes 1572872 | tf_op jit(solution)/shard_map/ppermute | solution.py:60
  34.5 135.0 %collective-permute-start.11 = (bf16[4,128,1024]{2,1,0:T(8,128)(2,1)S(1)}, bf16[4,128,1024]{2,1,0:T(8,128)(2,1)S(1)}, u32[]{:S(2)}, u32[]{:S(2)}) collective-permute-start(bf16[4,128,1024]{2,1,0:T(8,128)(2,1)S(1)} %get-tuple-element.37), channel_id=1, source_target_pairs={{0,20},{2,22},{4,16},{6,18},{8,28},{10,30},{12,24},{14,26},{16,4},... | collective-permute-start | bytes 3145736 | tf_op jit(solution)/shard_map/ppermute | solution.py:60
  81.6 88.4 %collective-permute-start.1 = (bf16[2,128,1024]{2,1,0:T(8,128)(2,1)S(1)}, bf16[2,128,1024]{2,1,0:T(8,128)(2,1)S(1)}, u32[]{:S(2)}, u32[]{:S(2)}) collective-permute-start(bf16[2,128,1024]{2,1,0:T(8,128)(2,1)S(1)} %get-tuple-element.54), channel_id=1, source_target_pairs={{0,2},{2,0},{4,6},{6,4},{8,10},{10,8},{12,14},{14,12},{16,18},{18,... | collective-permute-start | bytes 1572872 | tf_op jit(solution)/shard_map/ppermute | solution.py:65
  81.8 89.1 %collective-permute-start.4 = (bf16[2,128,1024]{2,1,0:T(8,128)(2,1)S(1)}, bf16[2,128,1024]{2,1,0:T(8,128)(2,1)S(1)}, u32[]{:S(2)}, u32[]{:S(2)}) collective-permute-start(bf16[2,128,1024]{2,1,0:T(8,128)(2,1)S(1)} %get-tuple-element.52), channel_id=1, source_target_pairs={{0,2},{2,0},{4,6},{6,4},{8,10},{10,8},{12,14},{14,12},{16,18},{18,... | collective-permute-start | bytes 1572872 | tf_op jit(solution)/shard_map/ppermute | solution.py:65
  103.4 69.4 %collective-permute-start.6 = (bf16[2,128,1024]{2,1,0:T(8,128)(2,1)S(1)}, bf16[2,128,1024]{2,1,0:T(8,128)(2,1)S(1)}, u32[]{:S(2)}, u32[]{:S(2)}) collective-permute-start(bf16[2,128,1024]{2,1,0:T(8,128)(2,1)S(1)} %get-tuple-element.50), channel_id=1, source_target_pairs={{0,2},{2,0},{4,6},{6,4},{8,10},{10,8},{12,14},{14,12},{16,18},{18,... | collective-permute-start | bytes 1572872 | tf_op jit(solution)/shard_map/ppermute | solution.py:65
  103.4 69.6 %collective-permute-start.8 = (bf16[2,128,1024]{2,1,0:T(8,128)(2,1)S(1)}, bf16[2,128,1024]{2,1,0:T(8,128)(2,1)S(1)}, u32[]{:S(2)}, u32[]{:S(2)}) collective-permute-start(bf16[2,128,1024]{2,1,0:T(8,128)(2,1)S(1)} %get-tuple-element.48), channel_id=1, source_target_pairs={{0,2},{2,0},{4,6},{6,4},{8,10},{10,8},{12,14},{14,12},{16,18},{18,... | collective-permute-start | bytes 1572872 | tf_op jit(solution)/shard_map/ppermute | solution.py:65
  169.5 37.3 %collective-permute-start.9 = (bf16[2,128,1024]{2,1,0:T(8,128)(2,1)S(1)}, bf16[2,128,1024]{2,1,0:T(8,128)(2,1)S(1)}, u32[]{:S(2)}, u32[]{:S(2)}) collective-permute-start(bf16[2,128,1024]{2,1,0:T(8,128)(2,1)S(1)} %get-tuple-element.35), channel_id=1, source_target_pairs={{0,4},{2,6},{4,0},{6,2},{8,12},{10,14},{12,8},{14,10},{16,20},{18,... | collective-permute-start | bytes 1572872 | tf_op jit(solution)/shard_map/ppermute | solution.py:60
  170.0 46.1 %collective-permute-start.10 = (bf16[2,128,1024]{2,1,0:T(8,128)(2,1)S(1)}, bf16[2,128,1024]{2,1,0:T(8,128)(2,1)S(1)}, u32[]{:S(2)}, u32[]{:S(2)}) collective-permute-start(bf16[2,128,1024]{2,1,0:T(8,128)(2,1)S(1)} %get-tuple-element.36), channel_id=1, source_target_pairs={{0,6},{2,4},{4,2},{6,0},{8,14},{10,12},{12,10},{14,8},{16,22},{18,... | collective-permute-start | bytes 1572872 | tf_op jit(solution)/shard_map/ppermute | solution.py:60
  170.9 47.2 %collective-permute-start.13 = (bf16[2,128,1024]{2,1,0:T(8,128)(2,1)S(1)}, bf16[2,128,1024]{2,1,0:T(8,128)(2,1)S(1)}, u32[]{:S(2)}, u32[]{:S(2)}) collective-permute-start(bf16[2,128,1024]{2,1,0:T(8,128)(2,1)S(1)} %get-tuple-element.40), channel_id=1, source_target_pairs={{0,28},{2,30},{4,24},{6,26},{8,4},{10,6},{12,0},{14,2},{16,12},{18... | collective-permute-start | bytes 1572872 | tf_op jit(solution)/shard_map/ppermute | solution.py:60
  172.8 45.3 %collective-permute-start.14 = (bf16[2,128,1024]{2,1,0:T(8,128)(2,1)S(1)}, bf16[2,128,1024]{2,1,0:T(8,128)(2,1)S(1)}, u32[]{:S(2)}, u32[]{:S(2)}) collective-permute-start(bf16[2,128,1024]{2,1,0:T(8,128)(2,1)S(1)} %get-tuple-element.41), channel_id=1, source_target_pairs={{0,30},{2,28},{4,26},{6,24},{8,6},{10,4},{12,2},{14,0},{16,14},{18... | collective-permute-start | bytes 1572872 | tf_op jit(solution)/shard_map/ppermute | solution.py:60
  173.1 45.0 %collective-permute-start.12 = (bf16[2,128,1024]{2,1,0:T(8,128)(2,1)S(1)}, bf16[2,128,1024]{2,1,0:T(8,128)(2,1)S(1)}, u32[]{:S(2)}, u32[]{:S(2)}) collective-permute-start(bf16[2,128,1024]{2,1,0:T(8,128)(2,1)S(1)} %get-tuple-element.46), channel_id=1, source_target_pairs={{0,2},{2,0},{4,6},{6,4},{8,10},{10,8},{12,14},{14,12},{16,18},{18,... | collective-permute-start | bytes 1572872 | tf_op jit(solution)/shard_map/ppermute | solution.py:65
  216.1 25.6 %copy-start = (bf16[4096,512]{1,0:T(8,128)(2,1)S(1)}, bf16[4096,512]{1,0:T(8,128)(2,1)}, u32[]{:S(2)}) copy-start(bf16[4096,512]{1,0:T(8,128)(2,1)} %out_weight.3) | copy-start | bytes 12582916
  220.6 7.4 %collective-permute-start.15 = (bf16[16,4096]{1,0:T(8,128)(2,1)S(1)}, bf16[16,4096]{1,0:T(8,128)(2,1)S(1)}, u32[]{:S(2)}, u32[]{:S(2)}) collective-permute-start(bf16[16,4096]{1,0:T(8,128)(2,1)S(1)} %get-tuple-element.43.rest_0_), channel_id=1, source_target_pairs={{0,16},{2,18},{4,20},{6,22},{8,24},{10,26},{12,28},{14,30},{16,0},... | collective-permute-start | bytes 393224 | tf_op jit(solution)/shard_map/ppermute | solution.py:65
  220.7 7.4 %collective-permute-start.18 = (bf16[16,4096]{1,0:T(8,128)(2,1)S(1)}, bf16[16,4096]{1,0:T(8,128)(2,1)S(1)}, u32[]{:S(2)}, u32[]{:S(2)}) collective-permute-start(bf16[16,4096]{1,0:T(8,128)(2,1)S(1)} %get-tuple-element.43.rest_0_), channel_id=1, source_target_pairs={{0,4},{2,6},{4,0},{6,2},{8,12},{10,14},{12,8},{14,10},{16,20},{18,... | collective-permute-start | bytes 393224 | tf_op jit(solution)/shard_map/ppermute | solution.py:65
  222.2 7.9 %collective-permute-start.16 = (bf16[16,4096]{1,0:T(8,128)(2,1)S(1)}, bf16[16,4096]{1,0:T(8,128)(2,1)S(1)}, u32[]{:S(2)}, u32[]{:S(2)}) collective-permute-start(bf16[16,4096]{1,0:T(8,128)(2,1)S(1)} %get-tuple-element.43.rest_0_), channel_id=1, source_target_pairs={{0,8},{2,10},{4,12},{6,14},{8,0},{10,2},{12,4},{14,6},{16,24},{18,... | collective-permute-start | bytes 393224 | tf_op jit(solution)/shard_map/ppermute | solution.py:65
  222.5 9.1 %collective-permute-start.22 = (bf16[16,4096]{1,0:T(8,128)(2,1)S(1)}, bf16[16,4096]{1,0:T(8,128)(2,1)S(1)}, u32[]{:S(2)}, u32[]{:S(2)}) collective-permute-start(bf16[16,4096]{1,0:T(8,128)(2,1)S(1)} %get-tuple-element.43.rest_0_), channel_id=1, source_target_pairs={{0,2},{2,0},{4,6},{6,4},{8,10},{10,8},{12,14},{14,12},{16,18},{18,... | collective-permute-start | bytes 393224 | tf_op jit(solution)/shard_map/ppermute | solution.py:65
  228.0 5.4 %collective-permute-start.17 = (bf16[16,4096]{1,0:T(8,128)(2,1)S(1)}, bf16[16,4096]{1,0:T(8,128)(2,1)S(1)}, u32[]{:S(2)}, u32[]{:S(2)}) collective-permute-start(bf16[16,4096]{1,0:T(8,128)(2,1)S(1)} %collective-permute-done.15.rest_1_), channel_id=1, source_target_pairs={{0,8},{2,10},{4,12},{6,14},{8,0},{10,2},{12,4},{14,6},{16,24},{18,... | collective-permute-start | bytes 393224 | tf_op jit(solution)/shard_map/ppermute | solution.py:65
  228.0 6.7 %collective-permute-start.26 = (bf16[16,4096]{1,0:T(8,128)(2,1)S(1)}, bf16[16,4096]{1,0:T(8,128)(2,1)S(1)}, u32[]{:S(2)}, u32[]{:S(2)}) collective-permute-start(bf16[16,4096]{1,0:T(8,128)(2,1)S(1)} %collective-permute-done.18.rest_4_), channel_id=1, source_target_pairs={{0,2},{2,0},{4,6},{6,4},{8,10},{10,8},{12,14},{14,12},{16,18},{18,... | collective-permute-start | bytes 393224 | tf_op jit(solution)/shard_map/ppermute | solution.py:65
  230.1 4.6 %collective-permute-start.24 = (bf16[16,4096]{1,0:T(8,128)(2,1)S(1)}, bf16[16,4096]{1,0:T(8,128)(2,1)S(1)}, u32[]{:S(2)}, u32[]{:S(2)}) collective-permute-start(bf16[16,4096]{1,0:T(8,128)(2,1)S(1)} %collective-permute-done.16.rest_2_), channel_id=1, source_target_pairs={{0,2},{2,0},{4,6},{6,4},{8,10},{10,8},{12,14},{14,12},{16,18},{18,... | collective-permute-start | bytes 393224 | tf_op jit(solution)/shard_map/ppermute | solution.py:65
  230.1 6.3 %collective-permute-start.20 = (bf16[16,4096]{1,0:T(8,128)(2,1)S(1)}, bf16[16,4096]{1,0:T(8,128)(2,1)S(1)}, u32[]{:S(2)}, u32[]{:S(2)}) collective-permute-start(bf16[16,4096]{1,0:T(8,128)(2,1)S(1)} %collective-permute-done.16.rest_2_), channel_id=1, source_target_pairs={{0,4},{2,6},{4,0},{6,2},{8,12},{10,14},{12,8},{14,10},{16,20},{18,... | collective-permute-start | bytes 393224 | tf_op jit(solution)/shard_map/ppermute | solution.py:65
  231.6 7.6 %collective-permute-start.19 = (bf16[16,4096]{1,0:T(8,128)(2,1)S(1)}, bf16[16,4096]{1,0:T(8,128)(2,1)S(1)}, u32[]{:S(2)}, u32[]{:S(2)}) collective-permute-start(bf16[16,4096]{1,0:T(8,128)(2,1)S(1)} %collective-permute-done.15.rest_1_), channel_id=1, source_target_pairs={{0,4},{2,6},{4,0},{6,2},{8,12},{10,14},{12,8},{14,10},{16,20},{18,... | collective-permute-start | bytes 393224 | tf_op jit(solution)/shard_map/ppermute | solution.py:65
  233.4 8.2 %collective-permute-start.21 = (bf16[16,4096]{1,0:T(8,128)(2,1)S(1)}, bf16[16,4096]{1,0:T(8,128)(2,1)S(1)}, u32[]{:S(2)}, u32[]{:S(2)}) collective-permute-start(bf16[16,4096]{1,0:T(8,128)(2,1)S(1)} %collective-permute-done.17.rest_3_), channel_id=1, source_target_pairs={{0,4},{2,6},{4,0},{6,2},{8,12},{10,14},{12,8},{14,10},{16,20},{18,... | collective-permute-start | bytes 393224 | tf_op jit(solution)/shard_map/ppermute | solution.py:65
  234.7 9.1 %collective-permute-start.23 = (bf16[16,4096]{1,0:T(8,128)(2,1)S(1)}, bf16[16,4096]{1,0:T(8,128)(2,1)S(1)}, u32[]{:S(2)}, u32[]{:S(2)}) collective-permute-start(bf16[16,4096]{1,0:T(8,128)(2,1)S(1)} %collective-permute-done.15.rest_1_), channel_id=1, source_target_pairs={{0,2},{2,0},{4,6},{6,4},{8,10},{10,8},{12,14},{14,12},{16,18},{18,... | collective-permute-start | bytes 393224 | tf_op jit(solution)/shard_map/ppermute | solution.py:65
  234.7 9.1 %collective-permute-start.25 = (bf16[16,4096]{1,0:T(8,128)(2,1)S(1)}, bf16[16,4096]{1,0:T(8,128)(2,1)S(1)}, u32[]{:S(2)}, u32[]{:S(2)}) collective-permute-start(bf16[16,4096]{1,0:T(8,128)(2,1)S(1)} %collective-permute-done.17.rest_3_), channel_id=1, source_target_pairs={{0,2},{2,0},{4,6},{6,4},{8,10},{10,8},{12,14},{14,12},{16,18},{18,... | collective-permute-start | bytes 393224 | tf_op jit(solution)/shard_map/ppermute | solution.py:65
  236.4 7.4 %collective-permute-start.28 = (bf16[16,4096]{1,0:T(8,128)(2,1)S(1)}, bf16[16,4096]{1,0:T(8,128)(2,1)S(1)}, u32[]{:S(2)}, u32[]{:S(2)}) collective-permute-start(bf16[16,4096]{1,0:T(8,128)(2,1)S(1)} %collective-permute-done.20.rest_6_), channel_id=1, source_target_pairs={{0,2},{2,0},{4,6},{6,4},{8,10},{10,8},{12,14},{14,12},{16,18},{18,... | collective-permute-start | bytes 393224 | tf_op jit(solution)/shard_map/ppermute | solution.py:65
  239.2 4.6 %collective-permute-start.27 = (bf16[16,4096]{1,0:T(8,128)(2,1)S(1)}, bf16[16,4096]{1,0:T(8,128)(2,1)S(1)}, u32[]{:S(2)}, u32[]{:S(2)}) collective-permute-start(bf16[16,4096]{1,0:T(8,128)(2,1)S(1)} %collective-permute-done.19.rest_5_), channel_id=1, source_target_pairs={{0,2},{2,0},{4,6},{6,4},{8,10},{10,8},{12,14},{14,12},{16,18},{18,... | collective-permute-start | bytes 393224 | tf_op jit(solution)/shard_map/ppermute | solution.py:65
  241.6 2.2 collective-permute-start.29
  246.3 6.0 %collective-permute-start.30 = (bf16[128,512]{1,0:T(8,128)(2,1)S(1)}, bf16[128,512]{1,0:T(8,128)(2,1)S(1)}, u32[]{:S(2)}, u32[]{:S(2)}) collective-permute-start(bf16[128,512]{1,0:T(8,128)(2,1)S(1)} %get-tuple-element.45), channel_id=1, source_target_pairs={{0,1},{1,0},{2,3},{3,2},{4,5},{5,4},{6,7},{7,6},{8,9},{9,8},{10,11... | collective-permute-start | bytes 393224 | tf_op jit(solution)/shard_map/ppermute | solution.py:415

commit v20 on v18

--- a/solution.py
+++ b/solution.py
@@ -32,7 +32,7 @@
     for low in range(0, near, half):
         swaps = range(low, min(low + half, near))
         opening = [(1, n) for n in swaps] if low == 0 else [(z, n) for n in swaps for z in (1, 0)]
-        rest = [(z, n) for n in swaps for z in range(far - 1, 1, -1)]
+        rest = [(z, n) for n in swaps for z in range(2, far)]
         order += opening + ([(0, n) for n in swaps if n] if low == 0 else []) + rest
     return [uniform(z, n, dims) for z, n in order]
 
@@ -65,12 +65,24 @@
     return lax.ppermute(array, "group", [(s, s ^ mask) for s in range(groups)])
 
 
+def tied(array, after):
+    return lax.optimization_barrier((array, after))[0]
+
+
 def gather_shards(shard):
-    held = {0: shard}
-    mask = lax.axis_size("group") // 2
-    while mask:
-        held.update({done | mask: swap(array, mask) for done, array in held.items()})
-        mask //= 2
+    groups = lax.axis_size("group")
+    swaps = [1 << i for i in reversed(range(groups.bit_length() - 1))]
+    own = {mask: swap(shard, mask) for mask in swaps}
+    held = {0: shard, **own}
+    if len(swaps) > 3:
+        far, near, side = swaps[0], swaps[-3], swaps[-2]
+        held[near] = tied(held[near], held[side])
+        held[near | side] = swap(held[near], side)
+        held[far] = tied(held[far], held[near | side])
+    for mask in swaps[1:]:
+        for done, array in list(held.items()):
+            if done & -done > mask and done | mask not in held:
+                held[done | mask] = swap(array, mask)
     return held
 
 

time: 229 us -> 230 us (level)
    ppermute x15, starting transfers between devices: 9.32 us -> 21.3 us  [swap(): return lax.ppermute(array, 'group', [(s, s ^ mask) for s in range(groups)])]
    ppermute x15, starting transfers between devices: 72.5 us -> 61.9 us  [send_by(): return lax.ppermute(array, 'group', pairs)]
    ppermute x15, waiting for transfers between devices: 12.7 us -> 10.2 us  [swap(): return lax.ppermute(array, 'group', [(s, s ^ mask) for s in range(groups)])]
  transfers between devices with their start and end apart: 31 -> 31, of which waited for: 14 -> 11; matrix products, arithmetic and copies ran while one was open for 0% -> 0% of each run, Pallas kernels for 9% -> 8%
where the time goes in v20:
time: 230 us; the launch traced here: 228 us
  waiting for transfers between devices  112 us (49%)
  starting transfers between devices  85.3 us (37%)
  Pallas kernels  28.7 us (12%)
    ppermute x15, waiting for transfers between devices, send_by(): return lax.ppermute(array, 'group', pairs)  97.3 us
    ppermute x15, starting transfers between devices, send_by(): return lax.ppermute(array, 'group', pairs)  61.9 us
    ppermute x15, starting transfers between devices, swap(): return lax.ppermute(array, 'group', [(s, s ^ mask) for s in range(groups)])  21.3 us
    pallas_call x5, Pallas kernels, settle(): pl.pallas_call(functools.partial(settle_kernel, dims, routes, own, last),...  13.4 us
    pallas_call x2, Pallas kernels, prepare(): pl.pallas_call(functools.partial(prepare_kernel, dims, routes, own), out_...  10.7 us
    ppermute x15, waiting for transfers between devices, swap(): return lax.ppermute(array, 'group', [(s, s ^ mask) for s in range(groups)])  10.2 us
    pallas_call x2, Pallas kernels, call(): pl.pallas_call(kernel, out_shape=outs, in_specs=[vmem] * (1 + len(extra))...  4.61 us
  transfers between devices with their start and end apart: 31, of which 11 were waited for; matrix products, arithmetic and copies ran while one was open for 0% of the time, Pallas kernels for 8%

profile of v20, /device:TPU:0, one launch (start us, length us, event | category | flops | bytes accessed | tf_op | source)
XLA Modules:
  0.0 228.0 jit_solution(12569589985719086567)
XLA Ops:
  0.6 0.7 or_or_fusion.table_hbm.table
  1.4 4.0 %outgoing_pages.2 = (bf16[2,128,1024]{2,1,0:T(8,128)(2,1)S(1)}, bf16[2,128,1024]{2,1,0:T(8,128)(2,1)S(1)}) custom-call(s32[256]{0:T(256)S(1)} %or_or_fusion.table_hbm.table, bf16[32,128,1024]{2,1,0:T(8,128)(2,1)} %pool.3), custom_call_target="tpu_custom_call" | custom-call | bytes 2097152 | tf_op jit(solution)/shard_map/outgoing_pages/pallas_call | solution.py:169
  5.4 2.5 %collective-permute-start.1 = (bf16[2,128,1024]{2,1,0:T(8,128)(2,1)S(1)}, bf16[2,128,1024]{2,1,0:T(8,128)(2,1)S(1)}, u32[]{:S(2)}, u32[]{:S(2)}) collective-permute-start(bf16[2,128,1024]{2,1,0:T(8,128)(2,1)S(1)} %get-tuple-element.34), channel_id=1, source_target_pairs={{0,10},{2,8},{4,14},{6,12},{8,18},{10,16},{12,22},{14,20},{16,26},... | collective-permute-start | bytes 1572872 | tf_op jit(solution)/shard_map/ppermute | solution.py:60
  7.9 1.5 collective-permute-start
  9.4 6.7 %outgoing_pages.3 = (bf16[32,128,1024]{2,1,0:T(8,128)(2,1)}, bf16[2,128,1024]{2,1,0:T(8,128)(2,1)S(1)}, bf16[2,128,1024]{2,1,0:T(8,128)(2,1)S(1)}, bf16[2,128,10...) custom-call(s32[256]{0:T(256)S(1)} %or_or_fusion.table_hbm.table, ...), custom_call_target="tpu_custom_call" | custom-call | bytes 14680064 | tf_op jit(solution)/shard_map/outgoing_pages/pallas_call | solution.py:169
  16.1 0.5 collective-permute-start.2
  16.6 1.3 collective-permute-start.3
  17.9 2.5 %collective-permute-start.4 = (bf16[2,128,1024]{2,1,0:T(8,128)(2,1)S(1)}, bf16[2,128,1024]{2,1,0:T(8,128)(2,1)S(1)}, u32[]{:S(2)}, u32[]{:S(2)}) collective-permute-start(bf16[2,128,1024]{2,1,0:T(8,128)(2,1)S(1)} %get-tuple-element.39), channel_id=1, source_target_pairs={{0,24},{2,26},{4,28},{6,30},{8,0},{10,2},{12,4},{14,6},{16,8},{18,... | collective-permute-start | bytes 1572872 | tf_op jit(solution)/shard_map/ppermute | solution.py:60
  20.5 1.1 collective-permute-done.1.rest_1_
  21.6 1.6 collective-permute-start.5
  23.2 11.4 %collective-permute-done.rest_0_ = bf16[2,128,1024]{2,1,0:T(8,128)(2,1)S(1)} collective-permute-done((bf16[2,128,1024]{2,1,0:T(8,128)(2,1)S(1)}, bf16[2,128,1024]{2,1,0:T(8,128)(2,1)S(1)}, u32[]{:S(2)}, u32[]{:S(2)}) %collective-permute-start) | collective-permute-done | bytes 524320 | tf_op jit(solution)/shard_map/ppermute | solution.py:60
  34.6 1.1 collective-permute-start.6
  35.7 1.0 collective-permute-start.7
  36.6 20.5 %collective-permute-done.3.rest_0_ = bf16[2,128,1024]{2,1,0:T(8,128)(2,1)S(1)} collective-permute-done((bf16[2,128,1024]{2,1,0:T(8,128)(2,1)S(1)}, bf16[2,128,1024]{2,1,0:T(8,128)(2,1)S(1)}, u32[]{:S(2)}, u32[]{:S(2)}) %collective-permute-start.3) | collective-permute-done | bytes 524320 | tf_op jit(solution)/shard_map/ppermute | solution.py:60
  57.1 1.4 collective-permute-start.8
  58.5 31.7 %collective-permute-start.9 = (bf16[2,128,1024]{2,1,0:T(8,128)(2,1)S(1)}, bf16[2,128,1024]{2,1,0:T(8,128)(2,1)S(1)}, u32[]{:S(2)}, u32[]{:S(2)}) collective-permute-start(bf16[2,128,1024]{2,1,0:T(8,128)(2,1)S(1)} %get-tuple-element.48), channel_id=1, source_target_pairs={{0,14},{2,12},{4,10},{6,8},{8,22},{10,20},{12,18},{14,16},{16,30},... | collective-permute-start | bytes 1572872 | tf_op jit(solution)/shard_map/ppermute | solution.py:60
  90.2 22.0 %collective-permute-done.5.rest_2_ = bf16[2,128,1024]{2,1,0:T(8,128)(2,1)S(1)} collective-permute-done((bf16[2,128,1024]{2,1,0:T(8,128)(2,1)S(1)}, bf16[2,128,1024]{2,1,0:T(8,128)(2,1)S(1)}, u32[]{:S(2)}, u32[]{:S(2)}) %collective-permute-start.5) | collective-permute-done | bytes 524320 | tf_op jit(solution)/shard_map/ppermute | solution.py:60
  112.2 1.8 collective-permute-start.10
  114.0 10.6 %collective-permute-start.11 = (bf16[2,128,1024]{2,1,0:T(8,128)(2,1)S(1)}, bf16[2,128,1024]{2,1,0:T(8,128)(2,1)S(1)}, u32[]{:S(2)}, u32[]{:S(2)}) collective-permute-start(bf16[2,128,1024]{2,1,0:T(8,128)(2,1)S(1)} %get-tuple-element.50), channel_id=1, source_target_pairs={{0,20},{2,22},{4,16},{6,18},{8,28},{10,30},{12,24},{14,26},{16,4},... | collective-permute-start | bytes 1572872 | tf_op jit(solution)/shard_map/ppermute | solution.py:60
  124.6 2.7 %collective-permute-start.12 = (bf16[2,128,1024]{2,1,0:T(8,128)(2,1)S(1)}, bf16[2,128,1024]{2,1,0:T(8,128)(2,1)S(1)}, u32[]{:S(2)}, u32[]{:S(2)}) collective-permute-start(bf16[2,128,1024]{2,1,0:T(8,128)(2,1)S(1)} %get-tuple-element.53), channel_id=1, source_target_pairs={{0,28},{2,30},{4,24},{6,26},{8,4},{10,6},{12,0},{14,2},{16,12},{18... | collective-permute-start | bytes 1572872 | tf_op jit(solution)/shard_map/ppermute | solution.py:60
  127.3 1.7 collective-permute-start.14
  129.0 3.1 %settle_pages.5 = (bf16[32,128,1024]{2,1,0:T(8,128)(2,1)}, f32[16,32,128]{2,1,0:T(8,128)S(1)}) custom-call(s32[256]{0:T(256)S(1)} %or_or_fusion.table_hbm.table, s32[256]{0:T(256)S(1)} %copy-done.1, bf16[16,32,128]{2,1,0:T(8,128)(2,1)S(1)} %bitcast.2, f32[16,32,128]{2,1,0:T(8,128)S(1)} %broadcast_in_dim.3.rows_in, ...), custom_call_target="tpu_custom_call", output_to_operand_aliasing={{0}: (4, {})} | custom-call | flops 1073741824 | bytes 3145728 | tf_op jit(solution)/shard_map/settle_pages/pallas_call | solution.py:288
  132.2 2.2 settle_pages.6
  134.4 2.2 settle_pages.7
  136.6 23.2 %collective-permute-done.10.rest_1_ = bf16[2,128,1024]{2,1,0:T(8,128)(2,1)S(1)} collective-permute-done((bf16[2,128,1024]{2,1,0:T(8,128)(2,1)S(1)}, bf16[2,128,1024]{2,1,0:T(8,128)(2,1)S(1)}, u32[]{:S(2)}, u32[]{:S(2)}) %collective-permute-start.10) | collective-permute-done | bytes 524320 | tf_op jit(solution)/shard_map/ppermute | solution.py:60
  159.8 2.2 settle_pages.8
  162.0 19.1 %collective-permute-done.13.rest_1_ = bf16[2,128,1024]{2,1,0:T(8,128)(2,1)S(1)} collective-permute-done((bf16[2,128,1024]{2,1,0:T(8,128)(2,1)S(1)}, bf16[2,128,1024]{2,1,0:T(8,128)(2,1)S(1)}, u32[]{:S(2)}, u32[]{:S(2)}) %collective-permute-start.13) | collective-permute-done | bytes 524320 | tf_op jit(solution)/shard_map/ppermute | solution.py:60
  181.1 3.7 %settle_pages.9 = (bf16[32,128,1024]{2,1,0:T(8,128)(2,1)}, bf16[16,4096]{1,0:T(8,128)(2,1)S(1)}) custom-call(s32[256]{0:T(256)S(1)} %or_or_fusion.table_hbm.table, s32[256]{0:T(256)S(1)} %copy-done.1, bf16[16,32,128]{2,1,0:T(8,128)(2,1)S(1)} %bitcast.6, f32[16,32,128]{2,1,0:T(8,128)S(1)} %get-tuple-element.51.rows_in, ...), custom_call_target="tpu_custom_call", output_to_operand_aliasing={{0}: (4, {})} | custom-call | flops 1073741824 | bytes 3145728 | tf_op jit(solution)/shard_map/settle_pages/pallas_call | solution.py:288
  184.9 0.1 collective-permute-start.17
  184.9 11.1 %collective-permute-start.16 = (bf16[16,4096]{1,0:T(8,128)(2,1)S(1)}, bf16[16,4096]{1,0:T(8,128)(2,1)S(1)}, u32[]{:S(2)}, u32[]{:S(2)}) collective-permute-start(bf16[16,4096]{1,0:T(8,128)(2,1)S(1)} %get-tuple-element.57.rest_0_), channel_id=1, source_target_pairs={{0,8},{2,10},{4,12},{6,14},{8,0},{10,2},{12,4},{14,6},{16,24},{18,... | collective-permute-start | bytes 393224 | tf_op jit(solution)/shard_map/ppermute | solution.py:65
  196.1 2.9 %collective-permute-start.15 = (bf16[16,4096]{1,0:T(8,128)(2,1)S(1)}, bf16[16,4096]{1,0:T(8,128)(2,1)S(1)}, u32[]{:S(2)}, u32[]{:S(2)}) collective-permute-start(bf16[16,4096]{1,0:T(8,128)(2,1)S(1)} %get-tuple-element.57.rest_0_), channel_id=1, source_target_pairs={{0,16},{2,18},{4,20},{6,22},{8,24},{10,26},{12,28},{14,30},{16,0},... | collective-permute-start | bytes 393224 | tf_op jit(solution)/shard_map/ppermute | solution.py:65
  199.0 0.6 collective-permute-done.16.rest_2_
  199.6 1.7 collective-permute-start.18
  201.3 4.6 %collective-permute-done.15.rest_1_ = bf16[16,4096]{1,0:T(8,128)(2,1)S(1)} collective-permute-done((bf16[16,4096]{1,0:T(8,128)(2,1)S(1)}, bf16[16,4096]{1,0:T(8,128)(2,1)S(1)}, u32[]{:S(2)}, u32[]{:S(2)}) %collective-permute-start.15) | collective-permute-done | bytes 131104 | tf_op jit(solution)/shard_map/ppermute | solution.py:65
  205.9 0.4 collective-permute-start.19
  206.3 0.5 collective-permute-start.25
  206.8 1.7 collective-permute-start.20
  208.5 2.9 %collective-permute-done.19.rest_5_ = bf16[16,4096]{1,0:T(8,128)(2,1)S(1)} collective-permute-done((bf16[16,4096]{1,0:T(8,128)(2,1)S(1)}, bf16[16,4096]{1,0:T(8,128)(2,1)S(1)}, u32[]{:S(2)}, u32[]{:S(2)}) %collective-permute-start.19) | collective-permute-done | bytes 131104 | tf_op jit(solution)/shard_map/ppermute | solution.py:65
  211.4 2.0 collective-permute-start.21
  213.4 0.5 collective-permute-start.26
  213.9 0.1 collective-permute-start.27
  214.0 0.4 collective-permute-start.28
  214.4 2.0 collective-permute-done.21.rest_7_
  216.4 2.1 project_some_rows.1.some
  218.6 2.5 %project_rows.1 = (f32[128,512]{1,0:T(8,128)S(1)}, bf16[128,512]{1,0:T(8,128)(2,1)S(1)}) custom-call(bf16[4096,512]{1,0:T(8,128)(2,1)S(1)} %copy-done, f32[128,512]{1,0:T(8,128)S(1)} %project_some_rows.1.some, bf16[16,4096]{1,0:T(8,128)(2,1)S(1)} %collective-permute-done.22.rest_0_, bf16[16,4096]{1,0:T(8,128)(2,1)S(1)} %collective-permute-done.23.rest_1_, ...), custom_call_target="tpu_custom_call" | custom-call | flops 536870912 | bytes 4194304 | tf_op jit(solution)/shard_map/project_rows/pallas_call | solution.py:362
  221.1 2.1 collective-permute-start.30
  223.1 4.2 %collective-permute-done.30 = bf16[128,512]{1,0:T(8,128)(2,1)S(1)} collective-permute-done((bf16[128,512]{1,0:T(8,128)(2,1)S(1)}, bf16[128,512]{1,0:T(8,128)(2,1)S(1)}, u32[]{:S(2)}, u32[]{:S(2)}) %collective-permute-start.30) | collective-permute-done | bytes 131104 | tf_op jit(solution)/shard_map/ppermute | solution.py:417
  227.3 0.7 add_convert_fusion
  (33 shorter events, 0.1 us)
Async XLA Ops:
  1.3 127.6 %copy-start.2 = (bf16[16,4096]{1,0:T(8,128)(2,1)S(1)}, bf16[16,4096]{1,0:T(8,128)(2,1)}, u32[]{:S(2)}) copy-start(bf16[16,4096]{1,0:T(8,128)(2,1)} %param.12) | copy-start | bytes 393220
  1.3 127.7 %copy-start.1 = (s32[256]{0:T(256)S(1)}, s32[256]{0:T(256)}, u32[]{:S(2)}) copy-start(s32[256]{0:T(256)} %row_request.9) | copy-start | bytes 3076
  5.4 16.2 %collective-permute-start.1 = (bf16[2,128,1024]{2,1,0:T(8,128)(2,1)S(1)}, bf16[2,128,1024]{2,1,0:T(8,128)(2,1)S(1)}, u32[]{:S(2)}, u32[]{:S(2)}) collective-permute-start(bf16[2,128,1024]{2,1,0:T(8,128)(2,1)S(1)} %get-tuple-element.34), channel_id=1, source_target_pairs={{0,10},{2,8},{4,14},{6,12},{8,18},{10,16},{12,22},{14,20},{16,26},... | collective-permute-start | bytes 1572872 | tf_op jit(solution)/shard_map/ppermute | solution.py:60
  7.9 26.7 %collective-permute-start = (bf16[2,128,1024]{2,1,0:T(8,128)(2,1)S(1)}, bf16[2,128,1024]{2,1,0:T(8,128)(2,1)S(1)}, u32[]{:S(2)}, u32[]{:S(2)}) collective-permute-start(bf16[2,128,1024]{2,1,0:T(8,128)(2,1)S(1)} %get-tuple-element.32.rest_0_), channel_id=1, source_target_pairs={{0,8},{2,10},{4,12},{6,14},{8,16},{10,18},{12,20},{14,22},{16,24},... | collective-permute-start | bytes 1572872 | tf_op jit(solution)/shard_map/ppermute | solution.py:60
  16.1 19.6 %collective-permute-start.2 = (bf16[2,128,1024]{2,1,0:T(8,128)(2,1)S(1)}, bf16[2,128,1024]{2,1,0:T(8,128)(2,1)S(1)}, u32[]{:S(2)}, u32[]{:S(2)}) collective-permute-start(bf16[2,128,1024]{2,1,0:T(8,128)(2,1)S(1)} %get-tuple-element.35), channel_id=1, source_target_pairs={{0,2},{2,0},{4,6},{6,4},{8,10},{10,8},{12,14},{14,12},{16,18},{18,... | collective-permute-start | bytes 1572872 | tf_op jit(solution)/shard_map/ppermute | solution.py:60
  16.6 40.5 %collective-permute-start.3 = (bf16[2,128,1024]{2,1,0:T(8,128)(2,1)S(1)}, bf16[2,128,1024]{2,1,0:T(8,128)(2,1)S(1)}, u32[]{:S(2)}, u32[]{:S(2)}) collective-permute-start(bf16[2,128,1024]{2,1,0:T(8,128)(2,1)S(1)} %get-tuple-element.38), channel_id=1, source_target_pairs={{0,16},{2,18},{4,20},{6,22},{8,24},{10,26},{12,28},{14,30},{16,0},... | collective-permute-start | bytes 1572872 | tf_op jit(solution)/shard_map/ppermute | solution.py:60
  17.9 40.6 %collective-permute-start.4 = (bf16[2,128,1024]{2,1,0:T(8,128)(2,1)S(1)}, bf16[2,128,1024]{2,1,0:T(8,128)(2,1)S(1)}, u32[]{:S(2)}, u32[]{:S(2)}) collective-permute-start(bf16[2,128,1024]{2,1,0:T(8,128)(2,1)S(1)} %get-tuple-element.39), channel_id=1, source_target_pairs={{0,24},{2,26},{4,28},{6,30},{8,0},{10,2},{12,4},{14,6},{16,8},{18,... | collective-permute-start | bytes 1572872 | tf_op jit(solution)/shard_map/ppermute | solution.py:60
  21.6 90.6 %collective-permute-start.5 = (bf16[2,128,1024]{2,1,0:T(8,128)(2,1)S(1)}, bf16[2,128,1024]{2,1,0:T(8,128)(2,1)S(1)}, u32[]{:S(2)}, u32[]{:S(2)}) collective-permute-start(bf16[2,128,1024]{2,1,0:T(8,128)(2,1)S(1)} %get-tuple-element.40), channel_id=1, source_target_pairs={{0,18},{2,16},{4,22},{6,20},{8,26},{10,24},{12,30},{14,28},{16,2},... | collective-permute-start | bytes 1572872 | tf_op jit(solution)/shard_map/ppermute | solution.py:60
  34.6 79.4 %collective-permute-start.6 = (bf16[2,128,1024]{2,1,0:T(8,128)(2,1)S(1)}, bf16[2,128,1024]{2,1,0:T(8,128)(2,1)S(1)}, u32[]{:S(2)}, u32[]{:S(2)}) collective-permute-start(bf16[2,128,1024]{2,1,0:T(8,128)(2,1)S(1)} %get-tuple-element.43), channel_id=1, source_target_pairs={{0,26},{2,24},{4,30},{6,28},{8,2},{10,0},{12,6},{14,4},{16,10},{18... | collective-permute-start | bytes 1572872 | tf_op jit(solution)/shard_map/ppermute | solution.py:60
  35.7 88.9 %collective-permute-start.7 = (bf16[2,128,1024]{2,1,0:T(8,128)(2,1)S(1)}, bf16[2,128,1024]{2,1,0:T(8,128)(2,1)S(1)}, u32[]{:S(2)}, u32[]{:S(2)}) collective-permute-start(bf16[2,128,1024]{2,1,0:T(8,128)(2,1)S(1)} %get-tuple-element.44), channel_id=1, source_target_pairs={{0,12},{2,14},{4,8},{6,10},{8,20},{10,22},{12,16},{14,18},{16,28},... | collective-permute-start | bytes 1572872 | tf_op jit(solution)/shard_map/ppermute | solution.py:60
  57.1 70.1 %collective-permute-start.8 = (bf16[2,128,1024]{2,1,0:T(8,128)(2,1)S(1)}, bf16[2,128,1024]{2,1,0:T(8,128)(2,1)S(1)}, u32[]{:S(2)}, u32[]{:S(2)}) collective-permute-start(bf16[2,128,1024]{2,1,0:T(8,128)(2,1)S(1)} %get-tuple-element.45), channel_id=1, source_target_pairs={{0,4},{2,6},{4,0},{6,2},{8,12},{10,14},{12,8},{14,10},{16,20},{18,... | collective-permute-start | bytes 1572872 | tf_op jit(solution)/shard_map/ppermute | solution.py:60
  58.5 68.7 %collective-permute-start.9 = (bf16[2,128,1024]{2,1,0:T(8,128)(2,1)S(1)}, bf16[2,128,1024]{2,1,0:T(8,128)(2,1)S(1)}, u32[]{:S(2)}, u32[]{:S(2)}) collective-permute-start(bf16[2,128,1024]{2,1,0:T(8,128)(2,1)S(1)} %get-tuple-element.48), channel_id=1, source_target_pairs={{0,14},{2,12},{4,10},{6,8},{8,22},{10,20},{12,18},{14,16},{16,30},... | collective-permute-start | bytes 1572872 | tf_op jit(solution)/shard_map/ppermute | solution.py:60
  112.2 47.6 %collective-permute-start.10 = (bf16[2,128,1024]{2,1,0:T(8,128)(2,1)S(1)}, bf16[2,128,1024]{2,1,0:T(8,128)(2,1)S(1)}, u32[]{:S(2)}, u32[]{:S(2)}) collective-permute-start(bf16[2,128,1024]{2,1,0:T(8,128)(2,1)S(1)} %get-tuple-element.49), channel_id=1, source_target_pairs={{0,6},{2,4},{4,2},{6,0},{8,14},{10,12},{12,10},{14,8},{16,22},{18,... | collective-permute-start | bytes 1572872 | tf_op jit(solution)/shard_map/ppermute | solution.py:60
  114.0 45.7 %collective-permute-start.11 = (bf16[2,128,1024]{2,1,0:T(8,128)(2,1)S(1)}, bf16[2,128,1024]{2,1,0:T(8,128)(2,1)S(1)}, u32[]{:S(2)}, u32[]{:S(2)}) collective-permute-start(bf16[2,128,1024]{2,1,0:T(8,128)(2,1)S(1)} %get-tuple-element.50), channel_id=1, source_target_pairs={{0,20},{2,22},{4,16},{6,18},{8,28},{10,30},{12,24},{14,26},{16,4},... | collective-permute-start | bytes 1572872 | tf_op jit(solution)/shard_map/ppermute | solution.py:60
  124.6 37.4 %collective-permute-start.12 = (bf16[2,128,1024]{2,1,0:T(8,128)(2,1)S(1)}, bf16[2,128,1024]{2,1,0:T(8,128)(2,1)S(1)}, u32[]{:S(2)}, u32[]{:S(2)}) collective-permute-start(bf16[2,128,1024]{2,1,0:T(8,128)(2,1)S(1)} %get-tuple-element.53), channel_id=1, source_target_pairs={{0,28},{2,30},{4,24},{6,26},{8,4},{10,6},{12,0},{14,2},{16,12},{18... | collective-permute-start | bytes 1572872 | tf_op jit(solution)/shard_map/ppermute | solution.py:60
  127.3 53.8 %collective-permute-start.13 = (bf16[2,128,1024]{2,1,0:T(8,128)(2,1)S(1)}, bf16[2,128,1024]{2,1,0:T(8,128)(2,1)S(1)}, u32[]{:S(2)}, u32[]{:S(2)}) collective-permute-start(bf16[2,128,1024]{2,1,0:T(8,128)(2,1)S(1)} %get-tuple-element.54), channel_id=1, source_target_pairs={{0,22},{2,20},{4,18},{6,16},{8,30},{10,28},{12,26},{14,24},{16,6},... | collective-permute-start | bytes 1572872 | tf_op jit(solution)/shard_map/ppermute | solution.py:60
  127.3 53.8 %collective-permute-start.14 = (bf16[2,128,1024]{2,1,0:T(8,128)(2,1)S(1)}, bf16[2,128,1024]{2,1,0:T(8,128)(2,1)S(1)}, u32[]{:S(2)}, u32[]{:S(2)}) collective-permute-start(bf16[2,128,1024]{2,1,0:T(8,128)(2,1)S(1)} %get-tuple-element.55), channel_id=1, source_target_pairs={{0,30},{2,28},{4,26},{6,24},{8,6},{10,4},{12,2},{14,0},{16,14},{18... | collective-permute-start | bytes 1572872 | tf_op jit(solution)/shard_map/ppermute | solution.py:60
  159.8 56.6 %copy-start = (bf16[4096,512]{1,0:T(8,128)(2,1)S(1)}, bf16[4096,512]{1,0:T(8,128)(2,1)}, u32[]{:S(2)}) copy-start(bf16[4096,512]{1,0:T(8,128)(2,1)} %out_weight.3) | copy-start | bytes 12582916
  184.9 14.1 %collective-permute-start.17 = (bf16[16,4096]{1,0:T(8,128)(2,1)S(1)}, bf16[16,4096]{1,0:T(8,128)(2,1)S(1)}, u32[]{:S(2)}, u32[]{:S(2)}) collective-permute-start(bf16[16,4096]{1,0:T(8,128)(2,1)S(1)} %get-tuple-element.57.rest_0_), channel_id=1, source_target_pairs={{0,4},{2,6},{4,0},{6,2},{8,12},{10,14},{12,8},{14,10},{16,20},{18,... | collective-permute-start | bytes 393224 | tf_op jit(solution)/shard_map/ppermute | solution.py:65
  184.9 14.6 %collective-permute-start.16 = (bf16[16,4096]{1,0:T(8,128)(2,1)S(1)}, bf16[16,4096]{1,0:T(8,128)(2,1)S(1)}, u32[]{:S(2)}, u32[]{:S(2)}) collective-permute-start(bf16[16,4096]{1,0:T(8,128)(2,1)S(1)} %get-tuple-element.57.rest_0_), channel_id=1, source_target_pairs={{0,8},{2,10},{4,12},{6,14},{8,0},{10,2},{12,4},{14,6},{16,24},{18,... | collective-permute-start | bytes 393224 | tf_op jit(solution)/shard_map/ppermute | solution.py:65
  196.1 9.8 %collective-permute-start.15 = (bf16[16,4096]{1,0:T(8,128)(2,1)S(1)}, bf16[16,4096]{1,0:T(8,128)(2,1)S(1)}, u32[]{:S(2)}, u32[]{:S(2)}) collective-permute-start(bf16[16,4096]{1,0:T(8,128)(2,1)S(1)} %get-tuple-element.57.rest_0_), channel_id=1, source_target_pairs={{0,16},{2,18},{4,20},{6,22},{8,24},{10,26},{12,28},{14,30},{16,0},... | collective-permute-start | bytes 393224 | tf_op jit(solution)/shard_map/ppermute | solution.py:65
  199.6 6.3 %collective-permute-start.18 = (bf16[16,4096]{1,0:T(8,128)(2,1)S(1)}, bf16[16,4096]{1,0:T(8,128)(2,1)S(1)}, u32[]{:S(2)}, u32[]{:S(2)}) collective-permute-start(bf16[16,4096]{1,0:T(8,128)(2,1)S(1)} %collective-permute-done.16.rest_2_), channel_id=1, source_target_pairs={{0,4},{2,6},{4,0},{6,2},{8,12},{10,14},{12,8},{14,10},{16,20},{18,... | collective-permute-start | bytes 393224 | tf_op jit(solution)/shard_map/ppermute | solution.py:65
  205.9 5.5 %collective-permute-start.19 = (bf16[16,4096]{1,0:T(8,128)(2,1)S(1)}, bf16[16,4096]{1,0:T(8,128)(2,1)S(1)}, u32[]{:S(2)}, u32[]{:S(2)}) collective-permute-start(bf16[16,4096]{1,0:T(8,128)(2,1)S(1)} %collective-permute-done.15.rest_1_), channel_id=1, source_target_pairs={{0,8},{2,10},{4,12},{6,14},{8,0},{10,2},{12,4},{14,6},{16,24},{18,... | collective-permute-start | bytes 393224 | tf_op jit(solution)/shard_map/ppermute | solution.py:65
  206.3 7.1 %collective-permute-start.22 = (bf16[16,4096]{1,0:T(8,128)(2,1)S(1)}, bf16[16,4096]{1,0:T(8,128)(2,1)S(1)}, u32[]{:S(2)}, u32[]{:S(2)}) collective-permute-start(bf16[16,4096]{1,0:T(8,128)(2,1)S(1)} %get-tuple-element.57.rest_0_), channel_id=1, source_target_pairs={{0,2},{2,0},{4,6},{6,4},{8,10},{10,8},{12,14},{14,12},{16,18},{18,... | collective-permute-start | bytes 393224 | tf_op jit(solution)/shard_map/ppermute | solution.py:65
  206.3 7.1 %collective-permute-start.25 = (bf16[16,4096]{1,0:T(8,128)(2,1)S(1)}, bf16[16,4096]{1,0:T(8,128)(2,1)S(1)}, u32[]{:S(2)}, u32[]{:S(2)}) collective-permute-start(bf16[16,4096]{1,0:T(8,128)(2,1)S(1)} %collective-permute-done.17.rest_3_), channel_id=1, source_target_pairs={{0,2},{2,0},{4,6},{6,4},{8,10},{10,8},{12,14},{14,12},{16,18},{18,... | collective-permute-start | bytes 393224 | tf_op jit(solution)/shard_map/ppermute | solution.py:65
  206.8 7.1 %collective-permute-start.24 = (bf16[16,4096]{1,0:T(8,128)(2,1)S(1)}, bf16[16,4096]{1,0:T(8,128)(2,1)S(1)}, u32[]{:S(2)}, u32[]{:S(2)}) collective-permute-start(bf16[16,4096]{1,0:T(8,128)(2,1)S(1)} %collective-permute-done.16.rest_2_), channel_id=1, source_target_pairs={{0,2},{2,0},{4,6},{6,4},{8,10},{10,8},{12,14},{14,12},{16,18},{18,... | collective-permute-start | bytes 393224 | tf_op jit(solution)/shard_map/ppermute | solution.py:65
  206.8 7.1 %collective-permute-start.20 = (bf16[16,4096]{1,0:T(8,128)(2,1)S(1)}, bf16[16,4096]{1,0:T(8,128)(2,1)S(1)}, u32[]{:S(2)}, u32[]{:S(2)}) collective-permute-start(bf16[16,4096]{1,0:T(8,128)(2,1)S(1)} %collective-permute-done.15.rest_1_), channel_id=1, source_target_pairs={{0,4},{2,6},{4,0},{6,2},{8,12},{10,14},{12,8},{14,10},{16,20},{18,... | collective-permute-start | bytes 393224 | tf_op jit(solution)/shard_map/ppermute | solution.py:65
  211.4 5.0 %collective-permute-start.21 = (bf16[16,4096]{1,0:T(8,128)(2,1)S(1)}, bf16[16,4096]{1,0:T(8,128)(2,1)S(1)}, u32[]{:S(2)}, u32[]{:S(2)}) collective-permute-start(bf16[16,4096]{1,0:T(8,128)(2,1)S(1)} %collective-permute-done.19.rest_5_), channel_id=1, source_target_pairs={{0,4},{2,6},{4,0},{6,2},{8,12},{10,14},{12,8},{14,10},{16,20},{18,... | collective-permute-start | bytes 393224 | tf_op jit(solution)/shard_map/ppermute | solution.py:65
  213.4 5.2 %collective-permute-start.23 = (bf16[16,4096]{1,0:T(8,128)(2,1)S(1)}, bf16[16,4096]{1,0:T(8,128)(2,1)S(1)}, u32[]{:S(2)}, u32[]{:S(2)}) collective-permute-start(bf16[16,4096]{1,0:T(8,128)(2,1)S(1)} %collective-permute-done.15.rest_1_), channel_id=1, source_target_pairs={{0,2},{2,0},{4,6},{6,4},{8,10},{10,8},{12,14},{14,12},{16,18},{18,... | collective-permute-start | bytes 393224 | tf_op jit(solution)/shard_map/ppermute | solution.py:65
  213.4 5.2 %collective-permute-start.26 = (bf16[16,4096]{1,0:T(8,128)(2,1)S(1)}, bf16[16,4096]{1,0:T(8,128)(2,1)S(1)}, u32[]{:S(2)}, u32[]{:S(2)}) collective-permute-start(bf16[16,4096]{1,0:T(8,128)(2,1)S(1)} %collective-permute-done.18.rest_4_), channel_id=1, source_target_pairs={{0,2},{2,0},{4,6},{6,4},{8,10},{10,8},{12,14},{14,12},{16,18},{18,... | collective-permute-start | bytes 393224 | tf_op jit(solution)/shard_map/ppermute | solution.py:65
  213.9 4.7 %collective-permute-start.27 = (bf16[16,4096]{1,0:T(8,128)(2,1)S(1)}, bf16[16,4096]{1,0:T(8,128)(2,1)S(1)}, u32[]{:S(2)}, u32[]{:S(2)}) collective-permute-start(bf16[16,4096]{1,0:T(8,128)(2,1)S(1)} %collective-permute-done.19.rest_5_), channel_id=1, source_target_pairs={{0,2},{2,0},{4,6},{6,4},{8,10},{10,8},{12,14},{14,12},{16,18},{18,... | collective-permute-start | bytes 393224 | tf_op jit(solution)/shard_map/ppermute | solution.py:65
  214.0 4.6 %collective-permute-start.28 = (bf16[16,4096]{1,0:T(8,128)(2,1)S(1)}, bf16[16,4096]{1,0:T(8,128)(2,1)S(1)}, u32[]{:S(2)}, u32[]{:S(2)}) collective-permute-start(bf16[16,4096]{1,0:T(8,128)(2,1)S(1)} %collective-permute-done.20.rest_6_), channel_id=1, source_target_pairs={{0,2},{2,0},{4,6},{6,4},{8,10},{10,8},{12,14},{14,12},{16,18},{18,... | collective-permute-start | bytes 393224 | tf_op jit(solution)/shard_map/ppermute | solution.py:65
  216.4 2.2 collective-permute-start.29
  221.1 6.2 %collective-permute-start.30 = (bf16[128,512]{1,0:T(8,128)(2,1)S(1)}, bf16[128,512]{1,0:T(8,128)(2,1)S(1)}, u32[]{:S(2)}, u32[]{:S(2)}) collective-permute-start(bf16[128,512]{1,0:T(8,128)(2,1)S(1)} %get-tuple-element.61), channel_id=1, source_target_pairs={{0,1},{1,0},{2,3},{3,2},{4,5},{5,4},{6,7},{7,6},{8,9},{9,8},{10,11... | collective-permute-start | bytes 393224 | tf_op jit(solution)/shard_map/ppermute | solution.py:417

commit v21 on v13

--- a/solution.py
+++ b/solution.py
@@ -32,7 +32,7 @@
     for low in range(0, near, half):
         swaps = range(low, min(low + half, near))
         opening = [(1, n) for n in swaps] if low == 0 else [(z, n) for n in swaps for z in (1, 0)]
-        rest = [(z, n) for n in swaps for z in range(2, far)]
+        rest = [(z, n) for z in range(2, far) for n in swaps]
         order += opening + ([(0, n) for n in swaps if n] if low == 0 else []) + rest
     return [uniform(z, n, dims) for z, n in order]
 

time: 226 us -> 227 us (level)
  starting transfers between devices: 86 us -> 92.1 us
  waiting for transfers between devices: 108 us -> 103 us
    ppermute x15, starting transfers between devices: 22.8 us -> 32 us  [swap(): return lax.ppermute(array, 'group', [(s, s ^ mask) for s in range(groups)])]
    ppermute x15, waiting for transfers between devices: 96.7 us -> 90.2 us  [send_by(): return lax.ppermute(array, 'group', pairs)]
    ppermute x15, starting transfers between devices: 61.5 us -> 58.7 us  [send_by(): return lax.ppermute(array, 'group', pairs)]
  transfers between devices with their start and end apart: 31 -> 31, of which waited for: 11 -> 10; matrix products, arithmetic and copies ran while one was open for 0% -> 0% of each run, Pallas kernels for 9% -> 9%
where the time goes in v21:
time: 227 us
  waiting for transfers between devices  103 us (45%)
  starting transfers between devices  92.1 us (41%)
  Pallas kernels  29.6 us (13%)
    ppermute x15, waiting for transfers between devices, send_by(): return lax.ppermute(array, 'group', pairs)  90.2 us
    ppermute x15, starting transfers between devices, send_by(): return lax.ppermute(array, 'group', pairs)  58.7 us
    ppermute x15, starting transfers between devices, swap(): return lax.ppermute(array, 'group', [(s, s ^ mask) for s in range(groups)])  32 us
    pallas_call x5, Pallas kernels, settle(): pl.pallas_call(functools.partial(settle_kernel, dims, routes, own, last),...  14.7 us
    pallas_call x2, Pallas kernels, prepare(): pl.pallas_call(functools.partial(prepare_kernel, dims, routes, own), out_...  10.3 us
    ppermute x15, waiting for transfers between devices, swap(): return lax.ppermute(array, 'group', [(s, s ^ mask) for s in range(groups)])  8.02 us
    pallas_call x2, Pallas kernels, call(): pl.pallas_call(kernel, out_shape=outs, in_specs=[vmem] * (1 + len(extra))...  4.6 us
    ppermute x1, waiting for transfers between devices, local(): own = own + lax.ppermute(part, 'head', pairs).astype(jnp.float32)  4.56 us
  transfers between devices with their start and end apart: 31, of which 10 were waited for; matrix products, arithmetic and copies ran while one was open for 0% of the time, Pallas kernels for 9%

profile of v21, /device:TPU:0, one launch (start us, length us, event | category | flops | bytes accessed | tf_op | source)
XLA Modules:
  0.0 226.8 jit_solution(16169115831211630194)
XLA Ops:
  0.6 0.7 or_or_fusion.table_hbm.table
  1.4 4.0 %outgoing_pages.2 = (bf16[2,128,1024]{2,1,0:T(8,128)(2,1)S(1)}, bf16[2,128,1024]{2,1,0:T(8,128)(2,1)S(1)}) custom-call(s32[256]{0:T(256)S(1)} %or_or_fusion.table_hbm.table, bf16[32,128,1024]{2,1,0:T(8,128)(2,1)} %pool.3), custom_call_target="tpu_custom_call" | custom-call | bytes 2097152 | tf_op jit(solution)/shard_map/outgoing_pages/pallas_call | solution.py:156
  5.3 2.5 %collective-permute-start.1 = (bf16[2,128,1024]{2,1,0:T(8,128)(2,1)S(1)}, bf16[2,128,1024]{2,1,0:T(8,128)(2,1)S(1)}, u32[]{:S(2)}, u32[]{:S(2)}) collective-permute-start(bf16[2,128,1024]{2,1,0:T(8,128)(2,1)S(1)} %get-tuple-element.32), channel_id=1, source_target_pairs={{0,10},{2,8},{4,14},{6,12},{8,18},{10,16},{12,22},{14,20},{16,26},... | collective-permute-start | bytes 1572872 | tf_op jit(solution)/shard_map/ppermute | solution.py:60
  7.8 1.7 collective-permute-start
  9.5 6.3 %outgoing_pages.3 = (bf16[32,128,1024]{2,1,0:T(8,128)(2,1)}, bf16[2,128,1024]{2,1,0:T(8,128)(2,1)S(1)}, bf16[2,128,1024]{2,1,0:T(8,128)(2,1)S(1)}, bf16[2,128,10...) custom-call(s32[256]{0:T(256)S(1)} %or_or_fusion.table_hbm.table, ...), custom_call_target="tpu_custom_call" | custom-call | bytes 14680064 | tf_op jit(solution)/shard_map/outgoing_pages/pallas_call | solution.py:156
  15.8 0.7 collective-permute-start.2
  16.5 1.3 collective-permute-start.3
  17.8 1.1 collective-permute-start.4
  18.9 2.8 %collective-permute-done.1.rest_1_ = bf16[2,128,1024]{2,1,0:T(8,128)(2,1)S(1)} collective-permute-done((bf16[2,128,1024]{2,1,0:T(8,128)(2,1)S(1)}, bf16[2,128,1024]{2,1,0:T(8,128)(2,1)S(1)}, u32[]{:S(2)}, u32[]{:S(2)}) %collective-permute-start.1) | collective-permute-done | bytes 524320 | tf_op jit(solution)/shard_map/ppermute | solution.py:60
  21.7 3.0 %collective-permute-start.5 = (bf16[2,128,1024]{2,1,0:T(8,128)(2,1)S(1)}, bf16[2,128,1024]{2,1,0:T(8,128)(2,1)S(1)}, u32[]{:S(2)}, u32[]{:S(2)}) collective-permute-start(bf16[2,128,1024]{2,1,0:T(8,128)(2,1)S(1)} %get-tuple-element.38), channel_id=1, source_target_pairs={{0,24},{2,26},{4,28},{6,30},{8,0},{10,2},{12,4},{14,6},{16,8},{18,... | collective-permute-start | bytes 1572872 | tf_op jit(solution)/shard_map/ppermute | solution.py:60
  24.7 9.9 %collective-permute-done.rest_0_ = bf16[2,128,1024]{2,1,0:T(8,128)(2,1)S(1)} collective-permute-done((bf16[2,128,1024]{2,1,0:T(8,128)(2,1)S(1)}, bf16[2,128,1024]{2,1,0:T(8,128)(2,1)S(1)}, u32[]{:S(2)}, u32[]{:S(2)}) %collective-permute-start) | collective-permute-done | bytes 524320 | tf_op jit(solution)/shard_map/ppermute | solution.py:60
  34.6 1.1 collective-permute-start.6
  35.7 0.9 collective-permute-start.7
  36.6 30.9 %collective-permute-done.3.rest_0_ = bf16[2,128,1024]{2,1,0:T(8,128)(2,1)S(1)} collective-permute-done((bf16[2,128,1024]{2,1,0:T(8,128)(2,1)S(1)}, bf16[2,128,1024]{2,1,0:T(8,128)(2,1)S(1)}, u32[]{:S(2)}, u32[]{:S(2)}) %collective-permute-start.3) | collective-permute-done | bytes 524320 | tf_op jit(solution)/shard_map/ppermute | solution.py:60
  67.5 1.9 collective-permute-start.8
  69.4 14.8 %collective-permute-done.4.rest_1_ = bf16[2,128,1024]{2,1,0:T(8,128)(2,1)S(1)} collective-permute-done((bf16[2,128,1024]{2,1,0:T(8,128)(2,1)S(1)}, bf16[2,128,1024]{2,1,0:T(8,128)(2,1)S(1)}, u32[]{:S(2)}, u32[]{:S(2)}) %collective-permute-start.4) | collective-permute-done | bytes 524320 | tf_op jit(solution)/shard_map/ppermute | solution.py:60
  84.2 16.9 %collective-permute-start.9 = (bf16[2,128,1024]{2,1,0:T(8,128)(2,1)S(1)}, bf16[2,128,1024]{2,1,0:T(8,128)(2,1)S(1)}, u32[]{:S(2)}, u32[]{:S(2)}) collective-permute-start(bf16[2,128,1024]{2,1,0:T(8,128)(2,1)S(1)} %get-tuple-element.46), channel_id=1, source_target_pairs={{0,14},{2,12},{4,10},{6,8},{8,22},{10,20},{12,18},{14,16},{16,30},... | collective-permute-start | bytes 1572872 | tf_op jit(solution)/shard_map/ppermute | solution.py:60
  101.1 0.0 collective-permute-done.5.rest_2_
  101.1 0.6 collective-permute-start.10
  101.7 22.8 %collective-permute-start.11 = (bf16[2,128,1024]{2,1,0:T(8,128)(2,1)S(1)}, bf16[2,128,1024]{2,1,0:T(8,128)(2,1)S(1)}, u32[]{:S(2)}, u32[]{:S(2)}) collective-permute-start(bf16[2,128,1024]{2,1,0:T(8,128)(2,1)S(1)} %get-tuple-element.48), channel_id=1, source_target_pairs={{0,20},{2,22},{4,16},{6,18},{8,28},{10,30},{12,24},{14,26},{16,4},... | collective-permute-start | bytes 1572872 | tf_op jit(solution)/shard_map/ppermute | solution.py:60
  124.5 0.0 collective-permute-done.7.rest_1_
  124.5 2.9 %collective-permute-start.13 = (bf16[2,128,1024]{2,1,0:T(8,128)(2,1)S(1)}, bf16[2,128,1024]{2,1,0:T(8,128)(2,1)S(1)}, u32[]{:S(2)}, u32[]{:S(2)}) collective-permute-start(bf16[2,128,1024]{2,1,0:T(8,128)(2,1)S(1)} %get-tuple-element.52), channel_id=1, source_target_pairs={{0,28},{2,30},{4,24},{6,26},{8,4},{10,6},{12,0},{14,2},{16,12},{18... | collective-permute-start | bytes 1572872 | tf_op jit(solution)/shard_map/ppermute | solution.py:60
  127.4 1.4 collective-permute-start.14
  128.8 4.4 %settle_pages.5 = (bf16[32,128,1024]{2,1,0:T(8,128)(2,1)}, f32[16,32,128]{2,1,0:T(8,128)S(1)}) custom-call(s32[256]{0:T(256)S(1)} %or_or_fusion.table_hbm.table, s32[256]{0:T(256)S(1)} %copy-done.1, bf16[16,32,128]{2,1,0:T(8,128)(2,1)S(1)} %bitcast.2, f32[16,32,128]{2,1,0:T(8,128)S(1)} %broadcast_in_dim.3.rows_in, ...), custom_call_target="tpu_custom_call", output_to_operand_aliasing={{0}: (4, {})} | custom-call | flops 1073741824 | bytes 3145728 | tf_op jit(solution)/shard_map/settle_pages/pallas_call | solution.py:275
  133.3 2.2 settle_pages.6
  135.5 2.2 settle_pages.7
  137.7 31.7 %collective-permute-done.10.rest_1_ = bf16[2,128,1024]{2,1,0:T(8,128)(2,1)S(1)} collective-permute-done((bf16[2,128,1024]{2,1,0:T(8,128)(2,1)S(1)}, bf16[2,128,1024]{2,1,0:T(8,128)(2,1)S(1)}, u32[]{:S(2)}, u32[]{:S(2)}) %collective-permute-start.10) | collective-permute-done | bytes 524320 | tf_op jit(solution)/shard_map/ppermute | solution.py:60
  169.4 3.5 %settle_pages.8 = (bf16[32,128,1024]{2,1,0:T(8,128)(2,1)}, f32[16,32,128]{2,1,0:T(8,128)S(1)}) custom-call(s32[256]{0:T(256)S(1)} %or_or_fusion.table_hbm.table, s32[256]{0:T(256)S(1)} %copy-done.1, bf16[16,32,128]{2,1,0:T(8,128)(2,1)S(1)} %bitcast.5, f32[16,32,128]{2,1,0:T(8,128)S(1)} %get-tuple-element.44.rows_in, ...), custom_call_target="tpu_custom_call", output_to_operand_aliasing={{0}: (4, {})} | custom-call | flops 1073741824 | bytes 3145728 | tf_op jit(solution)/shard_map/settle_pages/pallas_call | solution.py:275
  173.0 2.4 %settle_pages.9 = (bf16[32,128,1024]{2,1,0:T(8,128)(2,1)}, bf16[16,4096]{1,0:T(8,128)(2,1)S(1)}) custom-call(s32[256]{0:T(256)S(1)} %or_or_fusion.table_hbm.table, s32[256]{0:T(256)S(1)} %copy-done.1, bf16[16,32,128]{2,1,0:T(8,128)(2,1)S(1)} %bitcast.6, f32[16,32,128]{2,1,0:T(8,128)S(1)} %get-tuple-element.49.rows_in, ...), custom_call_target="tpu_custom_call", output_to_operand_aliasing={{0}: (4, {})} | custom-call | flops 1073741824 | bytes 3145728 | tf_op jit(solution)/shard_map/settle_pages/pallas_call | solution.py:275
  175.4 19.4 %collective-permute-start.15 = (bf16[16,4096]{1,0:T(8,128)(2,1)S(1)}, bf16[16,4096]{1,0:T(8,128)(2,1)S(1)}, u32[]{:S(2)}, u32[]{:S(2)}) collective-permute-start(bf16[16,4096]{1,0:T(8,128)(2,1)S(1)} %get-tuple-element.55.rest_0_), channel_id=1, source_target_pairs={{0,16},{2,18},{4,20},{6,22},{8,24},{10,26},{12,28},{14,30},{16,0},... | collective-permute-start | bytes 393224 | tf_op jit(solution)/shard_map/ppermute | solution.py:65
  194.8 2.0 collective-permute-start.18
  196.8 2.2 collective-permute-start.16
  199.0 0.7 collective-permute-start.22
  199.8 4.1 %collective-permute-start.17 = (bf16[16,4096]{1,0:T(8,128)(2,1)S(1)}, bf16[16,4096]{1,0:T(8,128)(2,1)S(1)}, u32[]{:S(2)}, u32[]{:S(2)}) collective-permute-start(bf16[16,4096]{1,0:T(8,128)(2,1)S(1)} %collective-permute-done.15.rest_1_), channel_id=1, source_target_pairs={{0,8},{2,10},{4,12},{6,14},{8,0},{10,2},{12,4},{14,6},{16,24},{18,... | collective-permute-start | bytes 393224 | tf_op jit(solution)/shard_map/ppermute | solution.py:65
  203.9 0.5 collective-permute-start.24
  204.4 1.1 collective-permute-start.20
  205.4 1.0 collective-permute-start.19
  206.4 1.2 collective-permute-done.17.rest_3_
  207.6 0.5 collective-permute-start.21
  208.2 0.5 collective-permute-start.25
  208.7 2.0 collective-permute-done.20.rest_6_
  210.7 2.8 %collective-permute-done.19.rest_5_ = bf16[16,4096]{1,0:T(8,128)(2,1)S(1)} collective-permute-done((bf16[16,4096]{1,0:T(8,128)(2,1)S(1)}, bf16[16,4096]{1,0:T(8,128)(2,1)S(1)}, u32[]{:S(2)}, u32[]{:S(2)}) %collective-permute-start.19) | collective-permute-done | bytes 131104 | tf_op jit(solution)/shard_map/ppermute | solution.py:65
  213.5 1.9 collective-permute-done.21.rest_7_
  215.5 2.1 project_some_rows.1.some
  217.7 2.5 %project_rows.1 = (f32[128,512]{1,0:T(8,128)S(1)}, bf16[128,512]{1,0:T(8,128)(2,1)S(1)}) custom-call(bf16[4096,512]{1,0:T(8,128)(2,1)S(1)} %copy-done, f32[128,512]{1,0:T(8,128)S(1)} %project_some_rows.1.some, bf16[16,4096]{1,0:T(8,128)(2,1)S(1)} %collective-permute-done.22.rest_0_, bf16[16,4096]{1,0:T(8,128)(2,1)S(1)} %collective-permute-done.23.rest_1_, ...), custom_call_target="tpu_custom_call" | custom-call | flops 536870912 | bytes 4194304 | tf_op jit(solution)/shard_map/project_rows/pallas_call | solution.py:349
  220.1 1.4 collective-permute-start.30
  221.5 4.6 %collective-permute-done.30 = bf16[128,512]{1,0:T(8,128)(2,1)S(1)} collective-permute-done((bf16[128,512]{1,0:T(8,128)(2,1)S(1)}, bf16[128,512]{1,0:T(8,128)(2,1)S(1)}, u32[]{:S(2)}, u32[]{:S(2)}) %collective-permute-start.30) | collective-permute-done | bytes 131104 | tf_op jit(solution)/shard_map/ppermute | solution.py:404
  226.1 0.7 add_convert_fusion
  (33 shorter events, 0.1 us)
Async XLA Ops:
  1.3 127.4 %copy-start.2 = (bf16[16,4096]{1,0:T(8,128)(2,1)S(1)}, bf16[16,4096]{1,0:T(8,128)(2,1)}, u32[]{:S(2)}) copy-start(bf16[16,4096]{1,0:T(8,128)(2,1)} %param.12) | copy-start | bytes 393220
  1.3 127.5 %copy-start.1 = (s32[256]{0:T(256)S(1)}, s32[256]{0:T(256)}, u32[]{:S(2)}) copy-start(s32[256]{0:T(256)} %row_request.9) | copy-start | bytes 3076
  5.3 16.4 %collective-permute-start.1 = (bf16[2,128,1024]{2,1,0:T(8,128)(2,1)S(1)}, bf16[2,128,1024]{2,1,0:T(8,128)(2,1)S(1)}, u32[]{:S(2)}, u32[]{:S(2)}) collective-permute-start(bf16[2,128,1024]{2,1,0:T(8,128)(2,1)S(1)} %get-tuple-element.32), channel_id=1, source_target_pairs={{0,10},{2,8},{4,14},{6,12},{8,18},{10,16},{12,22},{14,20},{16,26},... | collective-permute-start | bytes 1572872 | tf_op jit(solution)/shard_map/ppermute | solution.py:60
  7.8 26.8 %collective-permute-start = (bf16[2,128,1024]{2,1,0:T(8,128)(2,1)S(1)}, bf16[2,128,1024]{2,1,0:T(8,128)(2,1)S(1)}, u32[]{:S(2)}, u32[]{:S(2)}) collective-permute-start(bf16[2,128,1024]{2,1,0:T(8,128)(2,1)S(1)} %get-tuple-element.30.rest_0_), channel_id=1, source_target_pairs={{0,8},{2,10},{4,12},{6,14},{8,16},{10,18},{12,20},{14,22},{16,24},... | collective-permute-start | bytes 1572872 | tf_op jit(solution)/shard_map/ppermute | solution.py:60
  15.8 19.9 %collective-permute-start.2 = (bf16[2,128,1024]{2,1,0:T(8,128)(2,1)S(1)}, bf16[2,128,1024]{2,1,0:T(8,128)(2,1)S(1)}, u32[]{:S(2)}, u32[]{:S(2)}) collective-permute-start(bf16[2,128,1024]{2,1,0:T(8,128)(2,1)S(1)} %get-tuple-element.33), channel_id=1, source_target_pairs={{0,2},{2,0},{4,6},{6,4},{8,10},{10,8},{12,14},{14,12},{16,18},{18,... | collective-permute-start | bytes 1572872 | tf_op jit(solution)/shard_map/ppermute | solution.py:60
  16.5 51.0 %collective-permute-start.3 = (bf16[2,128,1024]{2,1,0:T(8,128)(2,1)S(1)}, bf16[2,128,1024]{2,1,0:T(8,128)(2,1)S(1)}, u32[]{:S(2)}, u32[]{:S(2)}) collective-permute-start(bf16[2,128,1024]{2,1,0:T(8,128)(2,1)S(1)} %get-tuple-element.36), channel_id=1, source_target_pairs={{0,16},{2,18},{4,20},{6,22},{8,24},{10,26},{12,28},{14,30},{16,0},... | collective-permute-start | bytes 1572872 | tf_op jit(solution)/shard_map/ppermute | solution.py:60
  17.8 66.4 %collective-permute-start.4 = (bf16[2,128,1024]{2,1,0:T(8,128)(2,1)S(1)}, bf16[2,128,1024]{2,1,0:T(8,128)(2,1)S(1)}, u32[]{:S(2)}, u32[]{:S(2)}) collective-permute-start(bf16[2,128,1024]{2,1,0:T(8,128)(2,1)S(1)} %get-tuple-element.37), channel_id=1, source_target_pairs={{0,18},{2,16},{4,22},{6,20},{8,26},{10,24},{12,30},{14,28},{16,2},... | collective-permute-start | bytes 1572872 | tf_op jit(solution)/shard_map/ppermute | solution.py:60
  21.7 79.4 %collective-permute-start.5 = (bf16[2,128,1024]{2,1,0:T(8,128)(2,1)S(1)}, bf16[2,128,1024]{2,1,0:T(8,128)(2,1)S(1)}, u32[]{:S(2)}, u32[]{:S(2)}) collective-permute-start(bf16[2,128,1024]{2,1,0:T(8,128)(2,1)S(1)} %get-tuple-element.38), channel_id=1, source_target_pairs={{0,24},{2,26},{4,28},{6,30},{8,0},{10,2},{12,4},{14,6},{16,8},{18,... | collective-permute-start | bytes 1572872 | tf_op jit(solution)/shard_map/ppermute | solution.py:60
  34.6 67.1 %collective-permute-start.6 = (bf16[2,128,1024]{2,1,0:T(8,128)(2,1)S(1)}, bf16[2,128,1024]{2,1,0:T(8,128)(2,1)S(1)}, u32[]{:S(2)}, u32[]{:S(2)}) collective-permute-start(bf16[2,128,1024]{2,1,0:T(8,128)(2,1)S(1)} %get-tuple-element.41), channel_id=1, source_target_pairs={{0,26},{2,24},{4,30},{6,28},{8,2},{10,0},{12,6},{14,4},{16,10},{18... | collective-permute-start | bytes 1572872 | tf_op jit(solution)/shard_map/ppermute | solution.py:60
  35.7 88.8 %collective-permute-start.7 = (bf16[2,128,1024]{2,1,0:T(8,128)(2,1)S(1)}, bf16[2,128,1024]{2,1,0:T(8,128)(2,1)S(1)}, u32[]{:S(2)}, u32[]{:S(2)}) collective-permute-start(bf16[2,128,1024]{2,1,0:T(8,128)(2,1)S(1)} %get-tuple-element.42), channel_id=1, source_target_pairs={{0,12},{2,14},{4,8},{6,10},{8,20},{10,22},{12,16},{14,18},{16,28},... | collective-permute-start | bytes 1572872 | tf_op jit(solution)/shard_map/ppermute | solution.py:60
  67.5 57.0 %collective-permute-start.8 = (bf16[2,128,1024]{2,1,0:T(8,128)(2,1)S(1)}, bf16[2,128,1024]{2,1,0:T(8,128)(2,1)S(1)}, u32[]{:S(2)}, u32[]{:S(2)}) collective-permute-start(bf16[2,128,1024]{2,1,0:T(8,128)(2,1)S(1)} %get-tuple-element.43), channel_id=1, source_target_pairs={{0,4},{2,6},{4,0},{6,2},{8,12},{10,14},{12,8},{14,10},{16,20},{18,... | collective-permute-start | bytes 1572872 | tf_op jit(solution)/shard_map/ppermute | solution.py:60
  84.2 43.2 %collective-permute-start.9 = (bf16[2,128,1024]{2,1,0:T(8,128)(2,1)S(1)}, bf16[2,128,1024]{2,1,0:T(8,128)(2,1)S(1)}, u32[]{:S(2)}, u32[]{:S(2)}) collective-permute-start(bf16[2,128,1024]{2,1,0:T(8,128)(2,1)S(1)} %get-tuple-element.46), channel_id=1, source_target_pairs={{0,14},{2,12},{4,10},{6,8},{8,22},{10,20},{12,18},{14,16},{16,30},... | collective-permute-start | bytes 1572872 | tf_op jit(solution)/shard_map/ppermute | solution.py:60
  101.1 68.3 %collective-permute-start.10 = (bf16[2,128,1024]{2,1,0:T(8,128)(2,1)S(1)}, bf16[2,128,1024]{2,1,0:T(8,128)(2,1)S(1)}, u32[]{:S(2)}, u32[]{:S(2)}) collective-permute-start(bf16[2,128,1024]{2,1,0:T(8,128)(2,1)S(1)} %get-tuple-element.47), channel_id=1, source_target_pairs={{0,6},{2,4},{4,2},{6,0},{8,14},{10,12},{12,10},{14,8},{16,22},{18,... | collective-permute-start | bytes 1572872 | tf_op jit(solution)/shard_map/ppermute | solution.py:60
  101.7 67.7 %collective-permute-start.11 = (bf16[2,128,1024]{2,1,0:T(8,128)(2,1)S(1)}, bf16[2,128,1024]{2,1,0:T(8,128)(2,1)S(1)}, u32[]{:S(2)}, u32[]{:S(2)}) collective-permute-start(bf16[2,128,1024]{2,1,0:T(8,128)(2,1)S(1)} %get-tuple-element.48), channel_id=1, source_target_pairs={{0,20},{2,22},{4,16},{6,18},{8,28},{10,30},{12,24},{14,26},{16,4},... | collective-permute-start | bytes 1572872 | tf_op jit(solution)/shard_map/ppermute | solution.py:60
  124.5 48.4 %collective-permute-start.12 = (bf16[2,128,1024]{2,1,0:T(8,128)(2,1)S(1)}, bf16[2,128,1024]{2,1,0:T(8,128)(2,1)S(1)}, u32[]{:S(2)}, u32[]{:S(2)}) collective-permute-start(bf16[2,128,1024]{2,1,0:T(8,128)(2,1)S(1)} %get-tuple-element.51), channel_id=1, source_target_pairs={{0,22},{2,20},{4,18},{6,16},{8,30},{10,28},{12,26},{14,24},{16,6},... | collective-permute-start | bytes 1572872 | tf_op jit(solution)/shard_map/ppermute | solution.py:60
  124.5 48.4 %collective-permute-start.13 = (bf16[2,128,1024]{2,1,0:T(8,128)(2,1)S(1)}, bf16[2,128,1024]{2,1,0:T(8,128)(2,1)S(1)}, u32[]{:S(2)}, u32[]{:S(2)}) collective-permute-start(bf16[2,128,1024]{2,1,0:T(8,128)(2,1)S(1)} %get-tuple-element.52), channel_id=1, source_target_pairs={{0,28},{2,30},{4,24},{6,26},{8,4},{10,6},{12,0},{14,2},{16,12},{18... | collective-permute-start | bytes 1572872 | tf_op jit(solution)/shard_map/ppermute | solution.py:60
  127.4 45.6 %collective-permute-start.14 = (bf16[2,128,1024]{2,1,0:T(8,128)(2,1)S(1)}, bf16[2,128,1024]{2,1,0:T(8,128)(2,1)S(1)}, u32[]{:S(2)}, u32[]{:S(2)}) collective-permute-start(bf16[2,128,1024]{2,1,0:T(8,128)(2,1)S(1)} %get-tuple-element.53), channel_id=1, source_target_pairs={{0,30},{2,28},{4,26},{6,24},{8,6},{10,4},{12,2},{14,0},{16,14},{18... | collective-permute-start | bytes 1572872 | tf_op jit(solution)/shard_map/ppermute | solution.py:60
  169.4 46.0 %copy-start = (bf16[4096,512]{1,0:T(8,128)(2,1)S(1)}, bf16[4096,512]{1,0:T(8,128)(2,1)}, u32[]{:S(2)}) copy-start(bf16[4096,512]{1,0:T(8,128)(2,1)} %out_weight.3) | copy-start | bytes 12582916
  175.4 24.4 %collective-permute-start.15 = (bf16[16,4096]{1,0:T(8,128)(2,1)S(1)}, bf16[16,4096]{1,0:T(8,128)(2,1)S(1)}, u32[]{:S(2)}, u32[]{:S(2)}) collective-permute-start(bf16[16,4096]{1,0:T(8,128)(2,1)S(1)} %get-tuple-element.55.rest_0_), channel_id=1, source_target_pairs={{0,16},{2,18},{4,20},{6,22},{8,24},{10,26},{12,28},{14,30},{16,0},... | collective-permute-start | bytes 393224 | tf_op jit(solution)/shard_map/ppermute | solution.py:65
  194.8 9.0 %collective-permute-start.18 = (bf16[16,4096]{1,0:T(8,128)(2,1)S(1)}, bf16[16,4096]{1,0:T(8,128)(2,1)S(1)}, u32[]{:S(2)}, u32[]{:S(2)}) collective-permute-start(bf16[16,4096]{1,0:T(8,128)(2,1)S(1)} %get-tuple-element.55.rest_0_), channel_id=1, source_target_pairs={{0,4},{2,6},{4,0},{6,2},{8,12},{10,14},{12,8},{14,10},{16,20},{18,... | collective-permute-start | bytes 393224 | tf_op jit(solution)/shard_map/ppermute | solution.py:65
  196.8 7.1 %collective-permute-start.16 = (bf16[16,4096]{1,0:T(8,128)(2,1)S(1)}, bf16[16,4096]{1,0:T(8,128)(2,1)S(1)}, u32[]{:S(2)}, u32[]{:S(2)}) collective-permute-start(bf16[16,4096]{1,0:T(8,128)(2,1)S(1)} %get-tuple-element.55.rest_0_), channel_id=1, source_target_pairs={{0,8},{2,10},{4,12},{6,14},{8,0},{10,2},{12,4},{14,6},{16,24},{18,... | collective-permute-start | bytes 393224 | tf_op jit(solution)/shard_map/ppermute | solution.py:65
  199.0 6.4 %collective-permute-start.22 = (bf16[16,4096]{1,0:T(8,128)(2,1)S(1)}, bf16[16,4096]{1,0:T(8,128)(2,1)S(1)}, u32[]{:S(2)}, u32[]{:S(2)}) collective-permute-start(bf16[16,4096]{1,0:T(8,128)(2,1)S(1)} %get-tuple-element.55.rest_0_), channel_id=1, source_target_pairs={{0,2},{2,0},{4,6},{6,4},{8,10},{10,8},{12,14},{14,12},{16,18},{18,... | collective-permute-start | bytes 393224 | tf_op jit(solution)/shard_map/ppermute | solution.py:65
  199.8 7.9 %collective-permute-start.17 = (bf16[16,4096]{1,0:T(8,128)(2,1)S(1)}, bf16[16,4096]{1,0:T(8,128)(2,1)S(1)}, u32[]{:S(2)}, u32[]{:S(2)}) collective-permute-start(bf16[16,4096]{1,0:T(8,128)(2,1)S(1)} %collective-permute-done.15.rest_1_), channel_id=1, source_target_pairs={{0,8},{2,10},{4,12},{6,14},{8,0},{10,2},{12,4},{14,6},{16,24},{18,... | collective-permute-start | bytes 393224 | tf_op jit(solution)/shard_map/ppermute | solution.py:65
  203.8 4.3 %collective-permute-start.26 = (bf16[16,4096]{1,0:T(8,128)(2,1)S(1)}, bf16[16,4096]{1,0:T(8,128)(2,1)S(1)}, u32[]{:S(2)}, u32[]{:S(2)}) collective-permute-start(bf16[16,4096]{1,0:T(8,128)(2,1)S(1)} %collective-permute-done.18.rest_4_), channel_id=1, source_target_pairs={{0,2},{2,0},{4,6},{6,4},{8,10},{10,8},{12,14},{14,12},{16,18},{18,... | collective-permute-start | bytes 393224 | tf_op jit(solution)/shard_map/ppermute | solution.py:65
  203.9 4.3 %collective-permute-start.24 = (bf16[16,4096]{1,0:T(8,128)(2,1)S(1)}, bf16[16,4096]{1,0:T(8,128)(2,1)S(1)}, u32[]{:S(2)}, u32[]{:S(2)}) collective-permute-start(bf16[16,4096]{1,0:T(8,128)(2,1)S(1)} %collective-permute-done.16.rest_2_), channel_id=1, source_target_pairs={{0,2},{2,0},{4,6},{6,4},{8,10},{10,8},{12,14},{14,12},{16,18},{18,... | collective-permute-start | bytes 393224 | tf_op jit(solution)/shard_map/ppermute | solution.py:65
  204.4 6.4 %collective-permute-start.20 = (bf16[16,4096]{1,0:T(8,128)(2,1)S(1)}, bf16[16,4096]{1,0:T(8,128)(2,1)S(1)}, u32[]{:S(2)}, u32[]{:S(2)}) collective-permute-start(bf16[16,4096]{1,0:T(8,128)(2,1)S(1)} %collective-permute-done.16.rest_2_), channel_id=1, source_target_pairs={{0,4},{2,6},{4,0},{6,2},{8,12},{10,14},{12,8},{14,10},{16,20},{18,... | collective-permute-start | bytes 393224 | tf_op jit(solution)/shard_map/ppermute | solution.py:65
  205.4 8.1 %collective-permute-start.19 = (bf16[16,4096]{1,0:T(8,128)(2,1)S(1)}, bf16[16,4096]{1,0:T(8,128)(2,1)S(1)}, u32[]{:S(2)}, u32[]{:S(2)}) collective-permute-start(bf16[16,4096]{1,0:T(8,128)(2,1)S(1)} %collective-permute-done.15.rest_1_), channel_id=1, source_target_pairs={{0,4},{2,6},{4,0},{6,2},{8,12},{10,14},{12,8},{14,10},{16,20},{18,... | collective-permute-start | bytes 393224 | tf_op jit(solution)/shard_map/ppermute | solution.py:65
  207.6 7.8 %collective-permute-start.21 = (bf16[16,4096]{1,0:T(8,128)(2,1)S(1)}, bf16[16,4096]{1,0:T(8,128)(2,1)S(1)}, u32[]{:S(2)}, u32[]{:S(2)}) collective-permute-start(bf16[16,4096]{1,0:T(8,128)(2,1)S(1)} %collective-permute-done.17.rest_3_), channel_id=1, source_target_pairs={{0,4},{2,6},{4,0},{6,2},{8,12},{10,14},{12,8},{14,10},{16,20},{18,... | collective-permute-start | bytes 393224 | tf_op jit(solution)/shard_map/ppermute | solution.py:65
  208.2 9.4 %collective-permute-start.23 = (bf16[16,4096]{1,0:T(8,128)(2,1)S(1)}, bf16[16,4096]{1,0:T(8,128)(2,1)S(1)}, u32[]{:S(2)}, u32[]{:S(2)}) collective-permute-start(bf16[16,4096]{1,0:T(8,128)(2,1)S(1)} %collective-permute-done.15.rest_1_), channel_id=1, source_target_pairs={{0,2},{2,0},{4,6},{6,4},{8,10},{10,8},{12,14},{14,12},{16,18},{18,... | collective-permute-start | bytes 393224 | tf_op jit(solution)/shard_map/ppermute | solution.py:65
  208.2 9.5 %collective-permute-start.25 = (bf16[16,4096]{1,0:T(8,128)(2,1)S(1)}, bf16[16,4096]{1,0:T(8,128)(2,1)S(1)}, u32[]{:S(2)}, u32[]{:S(2)}) collective-permute-start(bf16[16,4096]{1,0:T(8,128)(2,1)S(1)} %collective-permute-done.17.rest_3_), channel_id=1, source_target_pairs={{0,2},{2,0},{4,6},{6,4},{8,10},{10,8},{12,14},{14,12},{16,18},{18,... | collective-permute-start | bytes 393224 | tf_op jit(solution)/shard_map/ppermute | solution.py:65
  210.7 6.9 %collective-permute-start.28 = (bf16[16,4096]{1,0:T(8,128)(2,1)S(1)}, bf16[16,4096]{1,0:T(8,128)(2,1)S(1)}, u32[]{:S(2)}, u32[]{:S(2)}) collective-permute-start(bf16[16,4096]{1,0:T(8,128)(2,1)S(1)} %collective-permute-done.20.rest_6_), channel_id=1, source_target_pairs={{0,2},{2,0},{4,6},{6,4},{8,10},{10,8},{12,14},{14,12},{16,18},{18,... | collective-permute-start | bytes 393224 | tf_op jit(solution)/shard_map/ppermute | solution.py:65
  213.5 4.1 %collective-permute-start.27 = (bf16[16,4096]{1,0:T(8,128)(2,1)S(1)}, bf16[16,4096]{1,0:T(8,128)(2,1)S(1)}, u32[]{:S(2)}, u32[]{:S(2)}) collective-permute-start(bf16[16,4096]{1,0:T(8,128)(2,1)S(1)} %collective-permute-done.19.rest_5_), channel_id=1, source_target_pairs={{0,2},{2,0},{4,6},{6,4},{8,10},{10,8},{12,14},{14,12},{16,18},{18,... | collective-permute-start | bytes 393224 | tf_op jit(solution)/shard_map/ppermute | solution.py:65
  215.5 2.2 collective-permute-start.29
  220.1 6.0 %collective-permute-start.30 = (bf16[128,512]{1,0:T(8,128)(2,1)S(1)}, bf16[128,512]{1,0:T(8,128)(2,1)S(1)}, u32[]{:S(2)}, u32[]{:S(2)}) collective-permute-start(bf16[128,512]{1,0:T(8,128)(2,1)S(1)} %get-tuple-element.57), channel_id=1, source_target_pairs={{0,1},{1,0},{2,3},{3,2},{4,5},{5,4},{6,7},{7,6},{8,9},{9,8},{10,11... | collective-permute-start | bytes 393224 | tf_op jit(solution)/shard_map/ppermute | solution.py:404

commit v22 on v21

--- a/solution.py
+++ b/solution.py
@@ -31,7 +31,7 @@
     order = []
     for low in range(0, near, half):
         swaps = range(low, min(low + half, near))
-        opening = [(1, n) for n in swaps] if low == 0 else [(z, n) for n in swaps for z in (1, 0)]
+        opening = [(1, n) for n in swaps] if low == 0 else [(z, n) for z in (1, 0) for n in swaps]
         rest = [(z, n) for z in range(2, far) for n in swaps]
         order += opening + ([(0, n) for n in swaps if n] if low == 0 else []) + rest
     return [uniform(z, n, dims) for z, n in order]

time: 227 us -> 227 us (level)
  starting transfers between devices: 92.1 us -> 96 us
  Pallas kernels: 29.6 us -> 27 us
    ppermute x15, starting transfers between devices: 58.7 us -> 71.8 us  [send_by(): return lax.ppermute(array, 'group', pairs)]
    ppermute x15, starting transfers between devices: 32 us -> 21.9 us  [swap(): return lax.ppermute(array, 'group', [(s, s ^ mask) for s in range(groups)])]
    pallas_call x5, Pallas kernels: 14.7 us -> 12.1 us  [settle(): pl.pallas_call(functools.partial(settle_kernel, dims, routes, own, last),...]
  transfers between devices with their start and end apart: 31 -> 31, of which waited for: 10 -> 11; matrix products, arithmetic and copies ran while one was open for 0% -> 0% of each run, Pallas kernels for 9% -> 8%
where the time goes in v22:
time: 227 us
  waiting for transfers between devices  101 us (44%)
  starting transfers between devices  96 us (42%)
  Pallas kernels  27 us (12%)
    ppermute x15, waiting for transfers between devices, send_by(): return lax.ppermute(array, 'group', pairs)  89.8 us
    ppermute x15, starting transfers between devices, send_by(): return lax.ppermute(array, 'group', pairs)  71.8 us
    ppermute x15, starting transfers between devices, swap(): return lax.ppermute(array, 'group', [(s, s ^ mask) for s in range(groups)])  21.9 us
    pallas_call x5, Pallas kernels, settle(): pl.pallas_call(functools.partial(settle_kernel, dims, routes, own, last),...  12.1 us
    pallas_call x2, Pallas kernels, prepare(): pl.pallas_call(functools.partial(prepare_kernel, dims, routes, own), out_...  10.2 us
    ppermute x15, waiting for transfers between devices, swap(): return lax.ppermute(array, 'group', [(s, s ^ mask) for s in range(groups)])  7.38 us
    pallas_call x2, Pallas kernels, call(): pl.pallas_call(kernel, out_shape=outs, in_specs=[vmem] * (1 + len(extra))...  4.6 us
  transfers between devices with their start and end apart: 31, of which 11 were waited for; matrix products, arithmetic and copies ran while one was open for 0% of the time, Pallas kernels for 8%

profile of v22, /device:TPU:0, one launch (start us, length us, event | category | flops | bytes accessed | tf_op | source)
XLA Modules:
  0.0 226.6 jit_solution(3672509388945677621)
XLA Ops:
  0.6 0.7 or_or_fusion.table_hbm.table
  1.4 4.0 %outgoing_pages.2 = (bf16[2,128,1024]{2,1,0:T(8,128)(2,1)S(1)}, bf16[2,128,1024]{2,1,0:T(8,128)(2,1)S(1)}) custom-call(s32[256]{0:T(256)S(1)} %or_or_fusion.table_hbm.table, bf16[32,128,1024]{2,1,0:T(8,128)(2,1)} %pool.3), custom_call_target="tpu_custom_call" | custom-call | bytes 2097152 | tf_op jit(solution)/shard_map/outgoing_pages/pallas_call | solution.py:156
  5.4 2.4 %collective-permute-start.1 = (bf16[2,128,1024]{2,1,0:T(8,128)(2,1)S(1)}, bf16[2,128,1024]{2,1,0:T(8,128)(2,1)S(1)}, u32[]{:S(2)}, u32[]{:S(2)}) collective-permute-start(bf16[2,128,1024]{2,1,0:T(8,128)(2,1)S(1)} %get-tuple-element.32), channel_id=1, source_target_pairs={{0,10},{2,8},{4,14},{6,12},{8,18},{10,16},{12,22},{14,20},{16,26},... | collective-permute-start | bytes 1572872 | tf_op jit(solution)/shard_map/ppermute | solution.py:60
  7.8 1.7 collective-permute-start
  9.4 6.2 %outgoing_pages.3 = (bf16[32,128,1024]{2,1,0:T(8,128)(2,1)}, bf16[2,128,1024]{2,1,0:T(8,128)(2,1)S(1)}, bf16[2,128,1024]{2,1,0:T(8,128)(2,1)S(1)}, bf16[2,128,10...) custom-call(s32[256]{0:T(256)S(1)} %or_or_fusion.table_hbm.table, ...), custom_call_target="tpu_custom_call" | custom-call | bytes 14680064 | tf_op jit(solution)/shard_map/outgoing_pages/pallas_call | solution.py:156
  15.6 0.4 collective-permute-start.2
  16.0 1.8 collective-permute-start.3
  17.9 0.6 collective-permute-start.4
  18.5 3.1 %collective-permute-done.1.rest_1_ = bf16[2,128,1024]{2,1,0:T(8,128)(2,1)S(1)} collective-permute-done((bf16[2,128,1024]{2,1,0:T(8,128)(2,1)S(1)}, bf16[2,128,1024]{2,1,0:T(8,128)(2,1)S(1)}, u32[]{:S(2)}, u32[]{:S(2)}) %collective-permute-start.1) | collective-permute-done | bytes 524320 | tf_op jit(solution)/shard_map/ppermute | solution.py:60
  21.5 3.2 %collective-permute-start.5 = (bf16[2,128,1024]{2,1,0:T(8,128)(2,1)S(1)}, bf16[2,128,1024]{2,1,0:T(8,128)(2,1)S(1)}, u32[]{:S(2)}, u32[]{:S(2)}) collective-permute-start(bf16[2,128,1024]{2,1,0:T(8,128)(2,1)S(1)} %get-tuple-element.38), channel_id=1, source_target_pairs={{0,24},{2,26},{4,28},{6,30},{8,0},{10,2},{12,4},{14,6},{16,8},{18,... | collective-permute-start | bytes 1572872 | tf_op jit(solution)/shard_map/ppermute | solution.py:60
  24.7 9.9 %collective-permute-done.rest_0_ = bf16[2,128,1024]{2,1,0:T(8,128)(2,1)S(1)} collective-permute-done((bf16[2,128,1024]{2,1,0:T(8,128)(2,1)S(1)}, bf16[2,128,1024]{2,1,0:T(8,128)(2,1)S(1)}, u32[]{:S(2)}, u32[]{:S(2)}) %collective-permute-start) | collective-permute-done | bytes 524320 | tf_op jit(solution)/shard_map/ppermute | solution.py:60
  34.7 0.9 collective-permute-start.6
  35.6 0.0 collective-permute-done.2.rest_2_
  35.6 1.0 collective-permute-start.7
  36.5 30.9 %collective-permute-done.3.rest_0_ = bf16[2,128,1024]{2,1,0:T(8,128)(2,1)S(1)} collective-permute-done((bf16[2,128,1024]{2,1,0:T(8,128)(2,1)S(1)}, bf16[2,128,1024]{2,1,0:T(8,128)(2,1)S(1)}, u32[]{:S(2)}, u32[]{:S(2)}) %collective-permute-start.3) | collective-permute-done | bytes 524320 | tf_op jit(solution)/shard_map/ppermute | solution.py:60
  67.4 22.4 %collective-permute-start.8 = (bf16[2,128,1024]{2,1,0:T(8,128)(2,1)S(1)}, bf16[2,128,1024]{2,1,0:T(8,128)(2,1)S(1)}, u32[]{:S(2)}, u32[]{:S(2)}) collective-permute-start(bf16[2,128,1024]{2,1,0:T(8,128)(2,1)S(1)} %get-tuple-element.43), channel_id=1, source_target_pairs={{0,14},{2,12},{4,10},{6,8},{8,22},{10,20},{12,18},{14,16},{16,30},... | collective-permute-start | bytes 1572872 | tf_op jit(solution)/shard_map/ppermute | solution.py:60
  89.8 0.0 collective-permute-done.4.rest_1_
  89.8 0.6 collective-permute-start.9
  90.4 1.3 collective-permute-start.10
  91.7 32.8 %collective-permute-start.11 = (bf16[2,128,1024]{2,1,0:T(8,128)(2,1)S(1)}, bf16[2,128,1024]{2,1,0:T(8,128)(2,1)S(1)}, u32[]{:S(2)}, u32[]{:S(2)}) collective-permute-start(bf16[2,128,1024]{2,1,0:T(8,128)(2,1)S(1)} %get-tuple-element.48), channel_id=1, source_target_pairs={{0,20},{2,22},{4,16},{6,18},{8,28},{10,30},{12,24},{14,26},{16,4},... | collective-permute-start | bytes 1572872 | tf_op jit(solution)/shard_map/ppermute | solution.py:60
  124.5 0.0 collective-permute-done.7.rest_1_
  124.5 2.8 %collective-permute-start.13 = (bf16[2,128,1024]{2,1,0:T(8,128)(2,1)S(1)}, bf16[2,128,1024]{2,1,0:T(8,128)(2,1)S(1)}, u32[]{:S(2)}, u32[]{:S(2)}) collective-permute-start(bf16[2,128,1024]{2,1,0:T(8,128)(2,1)S(1)} %get-tuple-element.52), channel_id=1, source_target_pairs={{0,28},{2,30},{4,24},{6,26},{8,4},{10,6},{12,0},{14,2},{16,12},{18... | collective-permute-start | bytes 1572872 | tf_op jit(solution)/shard_map/ppermute | solution.py:60
  127.3 13.7 %collective-permute-done.9.rest_0_ = bf16[2,128,1024]{2,1,0:T(8,128)(2,1)S(1)} collective-permute-done((bf16[2,128,1024]{2,1,0:T(8,128)(2,1)S(1)}, bf16[2,128,1024]{2,1,0:T(8,128)(2,1)S(1)}, u32[]{:S(2)}, u32[]{:S(2)}) %collective-permute-start.9) | collective-permute-done | bytes 524320 | tf_op jit(solution)/shard_map/ppermute | solution.py:60
  141.1 3.1 %settle_pages.5 = (bf16[32,128,1024]{2,1,0:T(8,128)(2,1)}, f32[16,32,128]{2,1,0:T(8,128)S(1)}) custom-call(s32[256]{0:T(256)S(1)} %or_or_fusion.table_hbm.table, s32[256]{0:T(256)S(1)} %copy-done.1, bf16[16,32,128]{2,1,0:T(8,128)(2,1)S(1)} %bitcast.2, f32[16,32,128]{2,1,0:T(8,128)S(1)} %broadcast_in_dim.3.rows_in, ...), custom_call_target="tpu_custom_call", output_to_operand_aliasing={{0}: (4, {})} | custom-call | flops 1073741824 | bytes 3145728 | tf_op jit(solution)/shard_map/settle_pages/pallas_call | solution.py:275
  144.2 2.2 settle_pages.6
  146.4 2.2 settle_pages.7
  148.6 32.1 %collective-permute-done.10.rest_1_ = bf16[2,128,1024]{2,1,0:T(8,128)(2,1)S(1)} collective-permute-done((bf16[2,128,1024]{2,1,0:T(8,128)(2,1)S(1)}, bf16[2,128,1024]{2,1,0:T(8,128)(2,1)S(1)}, u32[]{:S(2)}, u32[]{:S(2)}) %collective-permute-start.10) | collective-permute-done | bytes 524320 | tf_op jit(solution)/shard_map/ppermute | solution.py:60
  180.8 2.2 settle_pages.8
  183.0 2.4 %settle_pages.9 = (bf16[32,128,1024]{2,1,0:T(8,128)(2,1)}, bf16[16,4096]{1,0:T(8,128)(2,1)S(1)}) custom-call(s32[256]{0:T(256)S(1)} %or_or_fusion.table_hbm.table, s32[256]{0:T(256)S(1)} %copy-done.1, bf16[16,32,128]{2,1,0:T(8,128)(2,1)S(1)} %bitcast.6, f32[16,32,128]{2,1,0:T(8,128)S(1)} %get-tuple-element.49.rows_in, ...), custom_call_target="tpu_custom_call", output_to_operand_aliasing={{0}: (4, {})} | custom-call | flops 1073741824 | bytes 3145728 | tf_op jit(solution)/shard_map/settle_pages/pallas_call | solution.py:275
  185.5 8.0 %collective-permute-start.15 = (bf16[16,4096]{1,0:T(8,128)(2,1)S(1)}, bf16[16,4096]{1,0:T(8,128)(2,1)S(1)}, u32[]{:S(2)}, u32[]{:S(2)}) collective-permute-start(bf16[16,4096]{1,0:T(8,128)(2,1)S(1)} %get-tuple-element.55.rest_0_), channel_id=1, source_target_pairs={{0,16},{2,18},{4,20},{6,22},{8,24},{10,26},{12,28},{14,30},{16,0},... | collective-permute-start | bytes 393224 | tf_op jit(solution)/shard_map/ppermute | solution.py:65
  193.5 2.0 collective-permute-start.18
  195.5 4.8 %collective-permute-start.16 = (bf16[16,4096]{1,0:T(8,128)(2,1)S(1)}, bf16[16,4096]{1,0:T(8,128)(2,1)S(1)}, u32[]{:S(2)}, u32[]{:S(2)}) collective-permute-start(bf16[16,4096]{1,0:T(8,128)(2,1)S(1)} %get-tuple-element.55.rest_0_), channel_id=1, source_target_pairs={{0,8},{2,10},{4,12},{6,14},{8,0},{10,2},{12,4},{14,6},{16,24},{18,... | collective-permute-start | bytes 393224 | tf_op jit(solution)/shard_map/ppermute | solution.py:65
  200.2 2.9 %collective-permute-start.17 = (bf16[16,4096]{1,0:T(8,128)(2,1)S(1)}, bf16[16,4096]{1,0:T(8,128)(2,1)S(1)}, u32[]{:S(2)}, u32[]{:S(2)}) collective-permute-start(bf16[16,4096]{1,0:T(8,128)(2,1)S(1)} %collective-permute-done.15.rest_1_), channel_id=1, source_target_pairs={{0,8},{2,10},{4,12},{6,14},{8,0},{10,2},{12,4},{14,6},{16,24},{18,... | collective-permute-start | bytes 393224 | tf_op jit(solution)/shard_map/ppermute | solution.py:65
  203.1 0.1 collective-permute-done.16.rest_2_
  203.2 0.5 collective-permute-start.24
  203.6 1.3 collective-permute-start.20
  205.0 0.7 collective-permute-start.19
  205.7 0.5 collective-permute-done.17.rest_3_
  206.2 1.2 collective-permute-start.21
  207.4 0.5 collective-permute-start.25
  207.9 2.1 collective-permute-done.20.rest_6_
  210.0 2.8 %collective-permute-done.19.rest_5_ = bf16[16,4096]{1,0:T(8,128)(2,1)S(1)} collective-permute-done((bf16[16,4096]{1,0:T(8,128)(2,1)S(1)}, bf16[16,4096]{1,0:T(8,128)(2,1)S(1)}, u32[]{:S(2)}, u32[]{:S(2)}) %collective-permute-start.19) | collective-permute-done | bytes 131104 | tf_op jit(solution)/shard_map/ppermute | solution.py:65
  212.8 1.9 collective-permute-done.21.rest_7_
  214.7 2.1 project_some_rows.1.some
  216.9 2.5 %project_rows.1 = (f32[128,512]{1,0:T(8,128)S(1)}, bf16[128,512]{1,0:T(8,128)(2,1)S(1)}) custom-call(bf16[4096,512]{1,0:T(8,128)(2,1)S(1)} %copy-done, f32[128,512]{1,0:T(8,128)S(1)} %project_some_rows.1.some, bf16[16,4096]{1,0:T(8,128)(2,1)S(1)} %collective-permute-done.22.rest_0_, bf16[16,4096]{1,0:T(8,128)(2,1)S(1)} %collective-permute-done.23.rest_1_, ...), custom_call_target="tpu_custom_call" | custom-call | flops 536870912 | bytes 4194304 | tf_op jit(solution)/shard_map/project_rows/pallas_call | solution.py:349
  219.4 2.3 %collective-permute-start.30 = (bf16[128,512]{1,0:T(8,128)(2,1)S(1)}, bf16[128,512]{1,0:T(8,128)(2,1)S(1)}, u32[]{:S(2)}, u32[]{:S(2)}) collective-permute-start(bf16[128,512]{1,0:T(8,128)(2,1)S(1)} %get-tuple-element.57), channel_id=1, source_target_pairs={{0,1},{1,0},{2,3},{3,2},{4,5},{5,4},{6,7},{7,6},{8,9},{9,8},{10,11... | collective-permute-start | bytes 393224 | tf_op jit(solution)/shard_map/ppermute | solution.py:404
  221.8 4.2 %collective-permute-done.30 = bf16[128,512]{1,0:T(8,128)(2,1)S(1)} collective-permute-done((bf16[128,512]{1,0:T(8,128)(2,1)S(1)}, bf16[128,512]{1,0:T(8,128)(2,1)S(1)}, u32[]{:S(2)}, u32[]{:S(2)}) %collective-permute-start.30) | collective-permute-done | bytes 131104 | tf_op jit(solution)/shard_map/ppermute | solution.py:404
  225.9 0.7 add_convert_fusion
  (33 shorter events, 0.1 us)
Async XLA Ops:
  1.3 139.7 %copy-start.2 = (bf16[16,4096]{1,0:T(8,128)(2,1)S(1)}, bf16[16,4096]{1,0:T(8,128)(2,1)}, u32[]{:S(2)}) copy-start(bf16[16,4096]{1,0:T(8,128)(2,1)} %param.12) | copy-start | bytes 393220
  1.3 139.8 %copy-start.1 = (s32[256]{0:T(256)S(1)}, s32[256]{0:T(256)}, u32[]{:S(2)}) copy-start(s32[256]{0:T(256)} %row_request.9) | copy-start | bytes 3076
  5.4 16.1 %collective-permute-start.1 = (bf16[2,128,1024]{2,1,0:T(8,128)(2,1)S(1)}, bf16[2,128,1024]{2,1,0:T(8,128)(2,1)S(1)}, u32[]{:S(2)}, u32[]{:S(2)}) collective-permute-start(bf16[2,128,1024]{2,1,0:T(8,128)(2,1)S(1)} %get-tuple-element.32), channel_id=1, source_target_pairs={{0,10},{2,8},{4,14},{6,12},{8,18},{10,16},{12,22},{14,20},{16,26},... | collective-permute-start | bytes 1572872 | tf_op jit(solution)/shard_map/ppermute | solution.py:60
  7.8 26.9 %collective-permute-start = (bf16[2,128,1024]{2,1,0:T(8,128)(2,1)S(1)}, bf16[2,128,1024]{2,1,0:T(8,128)(2,1)S(1)}, u32[]{:S(2)}, u32[]{:S(2)}) collective-permute-start(bf16[2,128,1024]{2,1,0:T(8,128)(2,1)S(1)} %get-tuple-element.30.rest_0_), channel_id=1, source_target_pairs={{0,8},{2,10},{4,12},{6,14},{8,16},{10,18},{12,20},{14,22},{16,24},... | collective-permute-start | bytes 1572872 | tf_op jit(solution)/shard_map/ppermute | solution.py:60
  15.6 19.9 %collective-permute-start.2 = (bf16[2,128,1024]{2,1,0:T(8,128)(2,1)S(1)}, bf16[2,128,1024]{2,1,0:T(8,128)(2,1)S(1)}, u32[]{:S(2)}, u32[]{:S(2)}) collective-permute-start(bf16[2,128,1024]{2,1,0:T(8,128)(2,1)S(1)} %get-tuple-element.33), channel_id=1, source_target_pairs={{0,2},{2,0},{4,6},{6,4},{8,10},{10,8},{12,14},{14,12},{16,18},{18,... | collective-permute-start | bytes 1572872 | tf_op jit(solution)/shard_map/ppermute | solution.py:60
  16.0 51.4 %collective-permute-start.3 = (bf16[2,128,1024]{2,1,0:T(8,128)(2,1)S(1)}, bf16[2,128,1024]{2,1,0:T(8,128)(2,1)S(1)}, u32[]{:S(2)}, u32[]{:S(2)}) collective-permute-start(bf16[2,128,1024]{2,1,0:T(8,128)(2,1)S(1)} %get-tuple-element.36), channel_id=1, source_target_pairs={{0,16},{2,18},{4,20},{6,22},{8,24},{10,26},{12,28},{14,30},{16,0},... | collective-permute-start | bytes 1572872 | tf_op jit(solution)/shard_map/ppermute | solution.py:60
  17.9 71.9 %collective-permute-start.4 = (bf16[2,128,1024]{2,1,0:T(8,128)(2,1)S(1)}, bf16[2,128,1024]{2,1,0:T(8,128)(2,1)S(1)}, u32[]{:S(2)}, u32[]{:S(2)}) collective-permute-start(bf16[2,128,1024]{2,1,0:T(8,128)(2,1)S(1)} %get-tuple-element.37), channel_id=1, source_target_pairs={{0,18},{2,16},{4,22},{6,20},{8,26},{10,24},{12,30},{14,28},{16,2},... | collective-permute-start | bytes 1572872 | tf_op jit(solution)/shard_map/ppermute | solution.py:60
  21.5 68.8 %collective-permute-start.5 = (bf16[2,128,1024]{2,1,0:T(8,128)(2,1)S(1)}, bf16[2,128,1024]{2,1,0:T(8,128)(2,1)S(1)}, u32[]{:S(2)}, u32[]{:S(2)}) collective-permute-start(bf16[2,128,1024]{2,1,0:T(8,128)(2,1)S(1)} %get-tuple-element.38), channel_id=1, source_target_pairs={{0,24},{2,26},{4,28},{6,30},{8,0},{10,2},{12,4},{14,6},{16,8},{18,... | collective-permute-start | bytes 1572872 | tf_op jit(solution)/shard_map/ppermute | solution.py:60
  34.7 57.1 %collective-permute-start.6 = (bf16[2,128,1024]{2,1,0:T(8,128)(2,1)S(1)}, bf16[2,128,1024]{2,1,0:T(8,128)(2,1)S(1)}, u32[]{:S(2)}, u32[]{:S(2)}) collective-permute-start(bf16[2,128,1024]{2,1,0:T(8,128)(2,1)S(1)} %get-tuple-element.41), channel_id=1, source_target_pairs={{0,26},{2,24},{4,30},{6,28},{8,2},{10,0},{12,6},{14,4},{16,10},{18... | collective-permute-start | bytes 1572872 | tf_op jit(solution)/shard_map/ppermute | solution.py:60
  35.6 89.0 %collective-permute-start.7 = (bf16[2,128,1024]{2,1,0:T(8,128)(2,1)S(1)}, bf16[2,128,1024]{2,1,0:T(8,128)(2,1)S(1)}, u32[]{:S(2)}, u32[]{:S(2)}) collective-permute-start(bf16[2,128,1024]{2,1,0:T(8,128)(2,1)S(1)} %get-tuple-element.42), channel_id=1, source_target_pairs={{0,12},{2,14},{4,8},{6,10},{8,20},{10,22},{12,16},{14,18},{16,28},... | collective-permute-start | bytes 1572872 | tf_op jit(solution)/shard_map/ppermute | solution.py:60
  67.4 57.1 %collective-permute-start.8 = (bf16[2,128,1024]{2,1,0:T(8,128)(2,1)S(1)}, bf16[2,128,1024]{2,1,0:T(8,128)(2,1)S(1)}, u32[]{:S(2)}, u32[]{:S(2)}) collective-permute-start(bf16[2,128,1024]{2,1,0:T(8,128)(2,1)S(1)} %get-tuple-element.43), channel_id=1, source_target_pairs={{0,14},{2,12},{4,10},{6,8},{8,22},{10,20},{12,18},{14,16},{16,30},... | collective-permute-start | bytes 1572872 | tf_op jit(solution)/shard_map/ppermute | solution.py:60
  89.8 51.3 %collective-permute-start.9 = (bf16[2,128,1024]{2,1,0:T(8,128)(2,1)S(1)}, bf16[2,128,1024]{2,1,0:T(8,128)(2,1)S(1)}, u32[]{:S(2)}, u32[]{:S(2)}) collective-permute-start(bf16[2,128,1024]{2,1,0:T(8,128)(2,1)S(1)} %get-tuple-element.46), channel_id=1, source_target_pairs={{0,4},{2,6},{4,0},{6,2},{8,12},{10,14},{12,8},{14,10},{16,20},{18,... | collective-permute-start | bytes 1572872 | tf_op jit(solution)/shard_map/ppermute | solution.py:60
  90.4 90.4 %collective-permute-start.10 = (bf16[2,128,1024]{2,1,0:T(8,128)(2,1)S(1)}, bf16[2,128,1024]{2,1,0:T(8,128)(2,1)S(1)}, u32[]{:S(2)}, u32[]{:S(2)}) collective-permute-start(bf16[2,128,1024]{2,1,0:T(8,128)(2,1)S(1)} %get-tuple-element.47), channel_id=1, source_target_pairs={{0,6},{2,4},{4,2},{6,0},{8,14},{10,12},{12,10},{14,8},{16,22},{18,... | collective-permute-start | bytes 1572872 | tf_op jit(solution)/shard_map/ppermute | solution.py:60
  91.7 89.1 %collective-permute-start.11 = (bf16[2,128,1024]{2,1,0:T(8,128)(2,1)S(1)}, bf16[2,128,1024]{2,1,0:T(8,128)(2,1)S(1)}, u32[]{:S(2)}, u32[]{:S(2)}) collective-permute-start(bf16[2,128,1024]{2,1,0:T(8,128)(2,1)S(1)} %get-tuple-element.48), channel_id=1, source_target_pairs={{0,20},{2,22},{4,16},{6,18},{8,28},{10,30},{12,24},{14,26},{16,4},... | collective-permute-start | bytes 1572872 | tf_op jit(solution)/shard_map/ppermute | solution.py:60
  124.5 58.5 %collective-permute-start.12 = (bf16[2,128,1024]{2,1,0:T(8,128)(2,1)S(1)}, bf16[2,128,1024]{2,1,0:T(8,128)(2,1)S(1)}, u32[]{:S(2)}, u32[]{:S(2)}) collective-permute-start(bf16[2,128,1024]{2,1,0:T(8,128)(2,1)S(1)} %get-tuple-element.51), channel_id=1, source_target_pairs={{0,22},{2,20},{4,18},{6,16},{8,30},{10,28},{12,26},{14,24},{16,6},... | collective-permute-start | bytes 1572872 | tf_op jit(solution)/shard_map/ppermute | solution.py:60
  124.5 58.5 %collective-permute-start.13 = (bf16[2,128,1024]{2,1,0:T(8,128)(2,1)S(1)}, bf16[2,128,1024]{2,1,0:T(8,128)(2,1)S(1)}, u32[]{:S(2)}, u32[]{:S(2)}) collective-permute-start(bf16[2,128,1024]{2,1,0:T(8,128)(2,1)S(1)} %get-tuple-element.52), channel_id=1, source_target_pairs={{0,28},{2,30},{4,24},{6,26},{8,4},{10,6},{12,0},{14,2},{16,12},{18... | collective-permute-start | bytes 1572872 | tf_op jit(solution)/shard_map/ppermute | solution.py:60
  141.0 42.0 %collective-permute-start.14 = (bf16[2,128,1024]{2,1,0:T(8,128)(2,1)S(1)}, bf16[2,128,1024]{2,1,0:T(8,128)(2,1)S(1)}, u32[]{:S(2)}, u32[]{:S(2)}) collective-permute-start(bf16[2,128,1024]{2,1,0:T(8,128)(2,1)S(1)} %get-tuple-element.53), channel_id=1, source_target_pairs={{0,30},{2,28},{4,26},{6,24},{8,6},{10,4},{12,2},{14,0},{16,14},{18... | collective-permute-start | bytes 1572872 | tf_op jit(solution)/shard_map/ppermute | solution.py:60
  180.8 33.9 %copy-start = (bf16[4096,512]{1,0:T(8,128)(2,1)S(1)}, bf16[4096,512]{1,0:T(8,128)(2,1)}, u32[]{:S(2)}) copy-start(bf16[4096,512]{1,0:T(8,128)(2,1)} %out_weight.3) | copy-start | bytes 12582916
  185.5 14.8 %collective-permute-start.15 = (bf16[16,4096]{1,0:T(8,128)(2,1)S(1)}, bf16[16,4096]{1,0:T(8,128)(2,1)S(1)}, u32[]{:S(2)}, u32[]{:S(2)}) collective-permute-start(bf16[16,4096]{1,0:T(8,128)(2,1)S(1)} %get-tuple-element.55.rest_0_), channel_id=1, source_target_pairs={{0,16},{2,18},{4,20},{6,22},{8,24},{10,26},{12,28},{14,30},{16,0},... | collective-permute-start | bytes 393224 | tf_op jit(solution)/shard_map/ppermute | solution.py:65
  193.5 9.7 %collective-permute-start.18 = (bf16[16,4096]{1,0:T(8,128)(2,1)S(1)}, bf16[16,4096]{1,0:T(8,128)(2,1)S(1)}, u32[]{:S(2)}, u32[]{:S(2)}) collective-permute-start(bf16[16,4096]{1,0:T(8,128)(2,1)S(1)} %get-tuple-element.55.rest_0_), channel_id=1, source_target_pairs={{0,4},{2,6},{4,0},{6,2},{8,12},{10,14},{12,8},{14,10},{16,20},{18,... | collective-permute-start | bytes 393224 | tf_op jit(solution)/shard_map/ppermute | solution.py:65
  195.5 7.7 %collective-permute-start.16 = (bf16[16,4096]{1,0:T(8,128)(2,1)S(1)}, bf16[16,4096]{1,0:T(8,128)(2,1)S(1)}, u32[]{:S(2)}, u32[]{:S(2)}) collective-permute-start(bf16[16,4096]{1,0:T(8,128)(2,1)S(1)} %get-tuple-element.55.rest_0_), channel_id=1, source_target_pairs={{0,8},{2,10},{4,12},{6,14},{8,0},{10,2},{12,4},{14,6},{16,24},{18,... | collective-permute-start | bytes 393224 | tf_op jit(solution)/shard_map/ppermute | solution.py:65
  200.2 4.7 %collective-permute-start.22 = (bf16[16,4096]{1,0:T(8,128)(2,1)S(1)}, bf16[16,4096]{1,0:T(8,128)(2,1)S(1)}, u32[]{:S(2)}, u32[]{:S(2)}) collective-permute-start(bf16[16,4096]{1,0:T(8,128)(2,1)S(1)} %get-tuple-element.55.rest_0_), channel_id=1, source_target_pairs={{0,2},{2,0},{4,6},{6,4},{8,10},{10,8},{12,14},{14,12},{16,18},{18,... | collective-permute-start | bytes 393224 | tf_op jit(solution)/shard_map/ppermute | solution.py:65
  200.2 5.9 %collective-permute-start.17 = (bf16[16,4096]{1,0:T(8,128)(2,1)S(1)}, bf16[16,4096]{1,0:T(8,128)(2,1)S(1)}, u32[]{:S(2)}, u32[]{:S(2)}) collective-permute-start(bf16[16,4096]{1,0:T(8,128)(2,1)S(1)} %collective-permute-done.15.rest_1_), channel_id=1, source_target_pairs={{0,8},{2,10},{4,12},{6,14},{8,0},{10,2},{12,4},{14,6},{16,24},{18,... | collective-permute-start | bytes 393224 | tf_op jit(solution)/shard_map/ppermute | solution.py:65
  203.1 4.3 %collective-permute-start.26 = (bf16[16,4096]{1,0:T(8,128)(2,1)S(1)}, bf16[16,4096]{1,0:T(8,128)(2,1)S(1)}, u32[]{:S(2)}, u32[]{:S(2)}) collective-permute-start(bf16[16,4096]{1,0:T(8,128)(2,1)S(1)} %collective-permute-done.18.rest_4_), channel_id=1, source_target_pairs={{0,2},{2,0},{4,6},{6,4},{8,10},{10,8},{12,14},{14,12},{16,18},{18,... | collective-permute-start | bytes 393224 | tf_op jit(solution)/shard_map/ppermute | solution.py:65
  203.2 4.2 %collective-permute-start.24 = (bf16[16,4096]{1,0:T(8,128)(2,1)S(1)}, bf16[16,4096]{1,0:T(8,128)(2,1)S(1)}, u32[]{:S(2)}, u32[]{:S(2)}) collective-permute-start(bf16[16,4096]{1,0:T(8,128)(2,1)S(1)} %collective-permute-done.16.rest_2_), channel_id=1, source_target_pairs={{0,2},{2,0},{4,6},{6,4},{8,10},{10,8},{12,14},{14,12},{16,18},{18,... | collective-permute-start | bytes 393224 | tf_op jit(solution)/shard_map/ppermute | solution.py:65
  203.6 6.4 %collective-permute-start.20 = (bf16[16,4096]{1,0:T(8,128)(2,1)S(1)}, bf16[16,4096]{1,0:T(8,128)(2,1)S(1)}, u32[]{:S(2)}, u32[]{:S(2)}) collective-permute-start(bf16[16,4096]{1,0:T(8,128)(2,1)S(1)} %collective-permute-done.16.rest_2_), channel_id=1, source_target_pairs={{0,4},{2,6},{4,0},{6,2},{8,12},{10,14},{12,8},{14,10},{16,20},{18,... | collective-permute-start | bytes 393224 | tf_op jit(solution)/shard_map/ppermute | solution.py:65
  205.0 7.8 %collective-permute-start.19 = (bf16[16,4096]{1,0:T(8,128)(2,1)S(1)}, bf16[16,4096]{1,0:T(8,128)(2,1)S(1)}, u32[]{:S(2)}, u32[]{:S(2)}) collective-permute-start(bf16[16,4096]{1,0:T(8,128)(2,1)S(1)} %collective-permute-done.15.rest_1_), channel_id=1, source_target_pairs={{0,4},{2,6},{4,0},{6,2},{8,12},{10,14},{12,8},{14,10},{16,20},{18,... | collective-permute-start | bytes 393224 | tf_op jit(solution)/shard_map/ppermute | solution.py:65
  206.2 8.6 %collective-permute-start.21 = (bf16[16,4096]{1,0:T(8,128)(2,1)S(1)}, bf16[16,4096]{1,0:T(8,128)(2,1)S(1)}, u32[]{:S(2)}, u32[]{:S(2)}) collective-permute-start(bf16[16,4096]{1,0:T(8,128)(2,1)S(1)} %collective-permute-done.17.rest_3_), channel_id=1, source_target_pairs={{0,4},{2,6},{4,0},{6,2},{8,12},{10,14},{12,8},{14,10},{16,20},{18,... | collective-permute-start | bytes 393224 | tf_op jit(solution)/shard_map/ppermute | solution.py:65
  207.4 9.5 %collective-permute-start.23 = (bf16[16,4096]{1,0:T(8,128)(2,1)S(1)}, bf16[16,4096]{1,0:T(8,128)(2,1)S(1)}, u32[]{:S(2)}, u32[]{:S(2)}) collective-permute-start(bf16[16,4096]{1,0:T(8,128)(2,1)S(1)} %collective-permute-done.15.rest_1_), channel_id=1, source_target_pairs={{0,2},{2,0},{4,6},{6,4},{8,10},{10,8},{12,14},{14,12},{16,18},{18,... | collective-permute-start | bytes 393224 | tf_op jit(solution)/shard_map/ppermute | solution.py:65
  207.4 9.5 %collective-permute-start.25 = (bf16[16,4096]{1,0:T(8,128)(2,1)S(1)}, bf16[16,4096]{1,0:T(8,128)(2,1)S(1)}, u32[]{:S(2)}, u32[]{:S(2)}) collective-permute-start(bf16[16,4096]{1,0:T(8,128)(2,1)S(1)} %collective-permute-done.17.rest_3_), channel_id=1, source_target_pairs={{0,2},{2,0},{4,6},{6,4},{8,10},{10,8},{12,14},{14,12},{16,18},{18,... | collective-permute-start | bytes 393224 | tf_op jit(solution)/shard_map/ppermute | solution.py:65
  210.0 6.9 %collective-permute-start.28 = (bf16[16,4096]{1,0:T(8,128)(2,1)S(1)}, bf16[16,4096]{1,0:T(8,128)(2,1)S(1)}, u32[]{:S(2)}, u32[]{:S(2)}) collective-permute-start(bf16[16,4096]{1,0:T(8,128)(2,1)S(1)} %collective-permute-done.20.rest_6_), channel_id=1, source_target_pairs={{0,2},{2,0},{4,6},{6,4},{8,10},{10,8},{12,14},{14,12},{16,18},{18,... | collective-permute-start | bytes 393224 | tf_op jit(solution)/shard_map/ppermute | solution.py:65
  212.8 4.1 %collective-permute-start.27 = (bf16[16,4096]{1,0:T(8,128)(2,1)S(1)}, bf16[16,4096]{1,0:T(8,128)(2,1)S(1)}, u32[]{:S(2)}, u32[]{:S(2)}) collective-permute-start(bf16[16,4096]{1,0:T(8,128)(2,1)S(1)} %collective-permute-done.19.rest_5_), channel_id=1, source_target_pairs={{0,2},{2,0},{4,6},{6,4},{8,10},{10,8},{12,14},{14,12},{16,18},{18,... | collective-permute-start | bytes 393224 | tf_op jit(solution)/shard_map/ppermute | solution.py:65
  214.7 2.2 collective-permute-start.29
  219.4 6.5 %collective-permute-start.30 = (bf16[128,512]{1,0:T(8,128)(2,1)S(1)}, bf16[128,512]{1,0:T(8,128)(2,1)S(1)}, u32[]{:S(2)}, u32[]{:S(2)}) collective-permute-start(bf16[128,512]{1,0:T(8,128)(2,1)S(1)} %get-tuple-element.57), channel_id=1, source_target_pairs={{0,1},{1,0},{2,3},{3,2},{4,5},{5,4},{6,7},{7,6},{8,9},{9,8},{10,11... | collective-permute-start | bytes 393224 | tf_op jit(solution)/shard_map/ppermute | solution.py:404
